TPU v7x, 32 devices: a whole 2x2x4 slice. The times are simulated.
32 devices in a mesh: dp: 8 (over y, x, core), expert: 4 (over z).
Axes of the slice: x: 2, y: 2, z: 4, core: 2. Of those that a mesh axis runs over, the one named last changes fastest.
Arguments:
- tokens: bfloat16 [2, 2048, 2048], P(None, ('dp', 'expert')), may hold values from -6 to 6
- cotangent: bfloat16 [2, 2048, 2048], P(None, ('dp', 'expert')), may hold values from -6 to 6
- seq_lengths: int32 [2, 8, 2], replicated, may hold values from 16 to 240, as said below
- dealing: int32 [2, 2048], P(None, ('dp', 'expert')), may hold values from 0 to 63, as said below
- attn_routes: int32 [2, 2048, 2], P(None, 'dp'), may hold values from 0 to 3, all different within a row; in each aligned block of 64 rows (0 to 63, 64 to 127, ..., all dimensions but the last counted through in order) at most 48 rows name the same one
- ffn_routes: int32 [2, 2048, 2], P(None, 'dp'), may hold values from 0 to 3, all different within a row; in each aligned block of 64 rows (0 to 63, 64 to 127, ..., all dimensions but the last counted through in order) at most 48 rows name the same one
- expert_table: int32 [4], replicated, may hold values from 0 to 3, each once
- clip_limit: int32 [1], replicated, may hold values from 5 to 10
- attn_gain: bfloat16 [2048], replicated, may hold values from 0.5 to 1.5
- ffn_gain: bfloat16 [2048], replicated, may hold values from 0.5 to 1.5
- attn_router: bfloat16 [2048, 4], replicated, may hold values from -0.125 to 0.125
- ffn_router: bfloat16 [2048, 4], replicated, may hold values from -0.125 to 0.125
- query_weight: bfloat16 [4, 2048, 2048], P('expert', 'dp')
- attn_out_weight: bfloat16 [4, 2048, 2048], P('expert', 'dp'), may hold values from -0.375 to 0.375
- kv_weight: bfloat16 [2048, 4096], P('dp', 'expert'), may hold values from -0.125 to 0.125
- gate_up_weight: bfloat16 [4, 2048, 11264], P('expert', 'dp'), may hold values from -0.125 to 0.125
- down_weight: bfloat16 [4, 2048, 5632], P('expert', 'dp'), may hold values from -0.078125 to 0.078125
Outputs:
- block_output: bfloat16 [2, 2048, 2048], P(None, ('dp', 'expert'))
- tokens_grad: bfloat16 [2, 2048, 2048], P(None, ('dp', 'expert'))
- attn_gain_grad: float32 [2048], replicated
- ffn_gain_grad: float32 [2048], replicated
- attn_router_grad: float32 [2048, 4], replicated
- ffn_router_grad: float32 [2048, 4], replicated
- query_grad: float32 [4, 2048, 2048], P('expert', 'dp')
- attn_out_grad: float32 [4, 2048, 2048], P('expert', 'dp')
- kv_grad: float32 [2048, 4096], P('dp', 'expert')
- gate_up_grad: float32 [4, 2048, 11264], P('expert', 'dp')
- down_grad: float32 [4, 2048, 5632], P('expert', 'dp')
- query_clipped: bfloat16 [4, 2048, 2048], P('expert', 'dp')
- kv_clipped: bfloat16 [2048, 4096], P('dp', 'expert')
Inputs may be any that keep to these rules, and one draw needn't show every extreme that they name: `seq_lengths`: the two lengths of a group sum to 256; the shorter one is under 64, and which one comes first varies. `dealing`: for each micro-batch, the entries of one device's 64 rows are a permutation of 0 to 63. `attn_routes`: each row names 2 different experts; in each aligned block of 64 rows (the rows of one device) no expert is named by more than 48 rows. `ffn_routes`: each row names 2 different experts; in each aligned block of 64 rows (the rows of one device) no expert is named by more than 48 rows. `expert_table`: A permutation of the experts.
All inputs are finite; a program needn't handle non-finite values.
Results may differ from a plain program's by a relative error of at most 0.02.
Values may be sent and summed in bfloat16 or wider, within the bound.
No kernel may reach another device: no remote copies, remote signals or barrier semaphores. Data moves between devices by JAX's collectives and lax.ppermute only.
A program may use at most 448 MiB of HBM per device.

v0:
```python
import jax
import jax.numpy as jnp
from jax import lax
from jax.sharding import PartitionSpec as P

HEADS = 16
HDIM = 128
FF = 5632
TOP = 2


eps_norm = 1e-06
rope_base = 10000.0
very_low = -1e30


def contract_last(left, right):
    return lax.dot_general(
        left, right, (((1,), (1,)), ((), ())), preferred_element_type=jnp.float32
    )


def contract_first(left, right):
    return lax.dot_general(
        left, right, (((0,), (0,)), ((), ())), preferred_element_type=jnp.float32
    )


def rotation_tables(places):
    half_dim = HDIM // 2
    frequency = rope_base ** (-jnp.arange(half_dim, dtype=jnp.float32) * 2.0 / HDIM)
    angles = places.astype(jnp.float32)[:, None] * frequency[None, :]
    return (jnp.cos(angles)[:, None, :], jnp.sin(angles)[:, None, :])


def rotate(values, tables, inverse):
    cosine, sine = tables
    if inverse:
        sine = -sine
    row_count = values.shape[0]
    half_dim = HDIM // 2
    shaped = values.reshape(row_count, -1, HDIM)
    first_half = shaped[..., :half_dim]
    second_half = shaped[..., half_dim:]
    rotated = jnp.concatenate(
        [first_half * cosine - second_half * sine, second_half * cosine + first_half * sine],
        axis=-1,
    )
    return rotated.reshape(row_count, -1)


def normalize(values):
    row_scale = lax.rsqrt(jnp.mean(values * values, axis=-1, keepdims=True) + eps_norm)
    return (values * row_scale, row_scale)


def norm_back(grad_hat, normed, row_scale):
    return row_scale * (grad_hat - normed * jnp.mean(grad_hat * normed, axis=-1, keepdims=True))


def route_gates(logits, routes, expert_table):
    expert_ids = jnp.arange(expert_table.shape[0], dtype=jnp.int32)
    matches = routes[:, :, None] == expert_ids[None, None, :]
    picked = jnp.sum(jnp.where(matches, logits[:, None, :], 0.0), axis=-1)
    gate_vals = jax.nn.softmax(picked, axis=-1)
    slot_ids = jnp.sum(jnp.where(matches, expert_table[None, None, :], 0), axis=-1)
    return (gate_vals, matches, slot_ids)


def gate_back(slot_grad, gate_vals, matches, slot_ids):
    slot_range = jnp.arange(slot_grad.shape[1], dtype=jnp.int32)
    chosen = jnp.sum(
        jnp.where(slot_ids[:, :, None] == slot_range[None, None, :], slot_grad[:, None, :], 0.0),
        axis=-1,
    )
    inner_sum = jnp.sum(gate_vals * chosen, axis=-1, keepdims=True)
    picked_grad = gate_vals * (chosen - inner_sum)
    return jnp.sum(jnp.where(matches, picked_grad[:, :, None], 0.0), axis=1)


def select_rows(hits, block_count, block_rows, slot_cap):
    hit_blocks = hits.reshape(block_count, block_rows).astype(jnp.int32)
    rank_in_block = jnp.cumsum(hit_blocks, axis=1) - 1
    placed = (hit_blocks[:, None, :] > 0) & (
        rank_in_block[:, None, :] == jnp.arange(slot_cap, dtype=jnp.int32)[None, :, None]
    )
    row_in_block = jnp.sum(
        jnp.where(placed, jnp.arange(block_rows, dtype=jnp.int32)[None, None, :], 0), axis=-1
    )
    filled = jnp.any(placed, axis=-1)
    row_index = row_in_block + jnp.arange(block_count, dtype=jnp.int32)[:, None] * block_rows
    return (row_index.reshape(-1), filled.reshape(-1))


def unpack_weights(gathered):
    return (gathered[0][0], gathered[1][0], gathered[2][0], gathered[3][0], gathered[4][0])


def local(
    tokens,
    cotangent,
    seq_lengths,
    dealing,
    attn_routes,
    ffn_routes,
    expert_table,
    clip_limit,
    attn_gain,
    ffn_gain,
    attn_router,
    ffn_router,
    query_weight,
    attn_out_weight,
    kv_weight,
    gate_up_weight,
    down_weight,
):
    micro_count, tok_rows, model_width = tokens.shape
    group_count = lax.axis_size("dp")
    expert_count = lax.axis_size("expert")
    column_index = lax.axis_index("expert")
    group_index = lax.axis_index("dp")
    piece_rows = tok_rows // group_count
    slot_cap = tok_rows * TOP * 3 // (2 * expert_count)
    group_rows = tok_rows * expert_count
    query_width = HEADS * HDIM
    piece_width = kv_weight.shape[1]
    score_scale = HDIM ** (-0.5)
    own_start = column_index * tok_rows
    arrived, arrived_grad = (
        lax.all_to_all(
            tokens.reshape(micro_count, group_count, piece_rows, model_width),
            "dp",
            split_axis=1,
            concat_axis=1,
            tiled=True,
        ),
        lax.all_to_all(
            cotangent.reshape(micro_count, group_count, piece_rows, model_width),
            "dp",
            split_axis=1,
            concat_axis=1,
            tiled=True,
        ),
    )
    deal_index = dealing[:, :, None]
    work_tokens = jnp.take_along_axis(
        arrived.reshape(micro_count, tok_rows, model_width), deal_index, axis=1
    )
    work_grads = jnp.take_along_axis(
        arrived_grad.reshape(micro_count, tok_rows, model_width), deal_index, axis=1
    )
    gain_one = attn_gain.astype(jnp.float32)
    gain_two = ffn_gain.astype(jnp.float32)
    positions = jnp.arange(group_rows, dtype=jnp.int32)
    slot_range = jnp.arange(expert_count, dtype=jnp.int32)
    gain_one_grad = jnp.zeros((model_width,), jnp.float32)
    gain_two_grad = jnp.zeros((model_width,), jnp.float32)
    router_one_grad = jnp.zeros(attn_router.shape, jnp.float32)
    router_two_grad = jnp.zeros(ffn_router.shape, jnp.float32)
    head_peak = jnp.full((HEADS,), very_low, jnp.float32)
    outputs_list = []
    grads_list = []
    kept_pairs = [[], [], [], [], []]
    sharded = (query_weight, attn_out_weight, gate_up_weight, down_weight, kv_weight[None])
    for micro_index in range(micro_count):
        query_full, out_full, gate_up_full, down_full, kv_full = unpack_weights(
            (
                lax.all_gather(sharded[0], "dp", axis=1, tiled=True),
                lax.all_gather(sharded[1], "dp", axis=1, tiled=True),
                lax.all_gather(sharded[2], "dp", axis=1, tiled=True),
                lax.all_gather(sharded[3], "dp", axis=1, tiled=True),
                lax.all_gather(sharded[4], "dp", axis=1, tiled=True),
            )
        )
        group_x, group_dy = (
            lax.all_gather(work_tokens[micro_index], "expert", axis=0, tiled=True),
            lax.all_gather(work_grads[micro_index], "expert", axis=0, tiled=True),
        )
        first_len = seq_lengths[micro_index, group_index, 0]
        in_second = positions >= first_len
        places = positions - jnp.where(in_second, first_len, 0)
        tables = rotation_tables(places)
        x_float = group_x.astype(jnp.float32)
        normed_one, scale_one = normalize(x_float)
        hidden_one = (normed_one * gain_one).astype(jnp.bfloat16)
        logits_one = jnp.dot(hidden_one, attn_router, preferred_element_type=jnp.float32)
        gates_one, matches_one, slots_one = route_gates(
            logits_one, attn_routes[micro_index], expert_table
        )
        own_gate_one = jnp.sum(jnp.where(slots_one == column_index, gates_one, 0.0), axis=-1)
        hits_one = jnp.any(slots_one == column_index, axis=-1)
        kv_part = jnp.dot(hidden_one, kv_full, preferred_element_type=jnp.float32).astype(
            jnp.bfloat16
        )
        kv_group = lax.all_gather(kv_part, "expert", axis=1, tiled=True)
        key_rot = rotate(kv_group[:, :query_width].astype(jnp.float32), tables, False).astype(
            jnp.bfloat16
        )
        key_heads = key_rot.reshape(group_rows, HEADS, HDIM)
        value_heads = kv_group[:, query_width:].reshape(group_rows, HEADS, HDIM)
        rows_one, filled_one = select_rows(hits_one, expert_count, tok_rows, slot_cap)
        routed_count = rows_one.shape[0]
        row_gate_one = jnp.where(filled_one, own_gate_one[rows_one], 0.0)
        hidden_rows_one = hidden_one[rows_one]
        row_tables = rotation_tables(places[rows_one])
        query_pre = jnp.dot(hidden_rows_one, query_full, preferred_element_type=jnp.float32)
        query_rot = rotate(query_pre, row_tables, False).astype(jnp.bfloat16)
        query_heads = query_rot.reshape(routed_count, HEADS, HDIM)
        allowed = (positions[None, :] <= rows_one[:, None]) & (
            in_second[None, :] == in_second[rows_one][:, None]
        )
        raw_scores = jnp.einsum(
            "rhd,khd->hrk", query_heads, key_heads, preferred_element_type=jnp.float32
        )
        scores = jnp.where(allowed[None], raw_scores * score_scale, very_low)
        head_peak = jnp.maximum(
            head_peak, jnp.max(jnp.where(filled_one[None, :, None], scores, very_low), axis=(1, 2))
        )
        row_peak = jnp.max(scores, axis=-1, keepdims=True)
        expo = jnp.exp(scores - row_peak)
        denom = jnp.sum(expo, axis=-1, keepdims=True)
        probs_soft = expo / denom
        log_total = row_peak + jnp.log(denom)
        attn_vals = jnp.einsum(
            "hrk,khd->rhd",
            probs_soft.astype(jnp.bfloat16),
            value_heads,
            preferred_element_type=jnp.float32,
        )
        attn_vals = attn_vals.reshape(routed_count, query_width).astype(jnp.bfloat16)
        out_rows = contract_last(attn_vals, out_full)
        attn_part = (
            jnp.zeros((group_rows, model_width), jnp.float32)
            .at[rows_one]
            .add(row_gate_one[:, None] * out_rows)
        )
        attn_total = lax.psum(attn_part, "expert")
        resid = x_float + attn_total
        normed_two, scale_two = normalize(resid)
        hidden_two = (normed_two * gain_two).astype(jnp.bfloat16)
        logits_two = jnp.dot(hidden_two, ffn_router, preferred_element_type=jnp.float32)
        gates_two, matches_two, slots_two = route_gates(
            logits_two, ffn_routes[micro_index], expert_table
        )
        own_gate_two = jnp.sum(jnp.where(slots_two == column_index, gates_two, 0.0), axis=-1)
        hits_two = jnp.any(slots_two == column_index, axis=-1)
        rows_two, filled_two = select_rows(hits_two, expert_count, tok_rows, slot_cap)
        row_gate_two = jnp.where(filled_two, own_gate_two[rows_two], 0.0)
        hidden_rows_two = hidden_two[rows_two]
        joint = jnp.dot(hidden_rows_two, gate_up_full, preferred_element_type=jnp.float32)
        gate_pre = joint[:, :FF]
        up_pre = joint[:, FF:]
        sigma = jax.nn.sigmoid(gate_pre)
        silu_vals = gate_pre * sigma
        active = (silu_vals * up_pre).astype(jnp.bfloat16)
        ffn_rows = contract_last(active, down_full)
        ffn_part = (
            jnp.zeros((group_rows, model_width), jnp.float32)
            .at[rows_two]
            .add(row_gate_two[:, None] * ffn_rows)
        )
        ffn_own = lax.psum_scatter(
            ffn_part.astype(jnp.bfloat16), "expert", scatter_dimension=0, tiled=True
        ).astype(jnp.float32)
        resid_own = lax.dynamic_slice_in_dim(resid, own_start, tok_rows, 0)
        outputs_list.append((resid_own + ffn_own).astype(jnp.bfloat16))
        grad_out = group_dy.astype(jnp.float32)
        ffn_rows_grad = (row_gate_two[:, None] * grad_out[rows_two]).astype(jnp.bfloat16)
        gate_grad_two = jnp.where(filled_two, jnp.sum(ffn_rows * grad_out[rows_two], axis=-1), 0.0)
        slot_part_two = (
            jnp.zeros((group_rows, expert_count), jnp.float32)
            .at[rows_two, column_index]
            .add(gate_grad_two)
        )
        active_grad = jnp.dot(ffn_rows_grad, down_full, preferred_element_type=jnp.float32)
        gate_grad = active_grad * up_pre * sigma * (1.0 + gate_pre * (1.0 - sigma))
        up_grad = active_grad * silu_vals
        joint_grad = jnp.concatenate([gate_grad, up_grad], axis=1).astype(jnp.bfloat16)
        hidden_two_part = (
            jnp.zeros((group_rows, model_width), jnp.float32)
            .at[rows_two]
            .add(contract_last(joint_grad, gate_up_full))
        )
        hidden_two_grad, slot_two_grad = lax.psum((hidden_two_part, slot_part_two), "expert")
        logit_two_grad = gate_back(slot_two_grad, gates_two, matches_two, slots_two).astype(
            jnp.bfloat16
        )
        hidden_two_grad = hidden_two_grad + contract_last(logit_two_grad, ffn_router)
        router_two_grad = router_two_grad + contract_first(
            lax.dynamic_slice_in_dim(hidden_two, own_start, tok_rows, 0),
            lax.dynamic_slice_in_dim(logit_two_grad, own_start, tok_rows, 0),
        )
        gain_two_grad = gain_two_grad + jnp.sum(
            lax.dynamic_slice_in_dim(hidden_two_grad, own_start, tok_rows, 0)
            * lax.dynamic_slice_in_dim(normed_two, own_start, tok_rows, 0),
            axis=0,
        )
        resid_grad = grad_out + norm_back(hidden_two_grad * gain_two, normed_two, scale_two)
        attn_rows_grad = (row_gate_one[:, None] * resid_grad[rows_one]).astype(jnp.bfloat16)
        gate_grad_one = jnp.where(
            filled_one, jnp.sum(out_rows * resid_grad[rows_one], axis=-1), 0.0
        )
        slot_part_one = (
            jnp.zeros((group_rows, expert_count), jnp.float32)
            .at[rows_one, column_index]
            .add(gate_grad_one)
        )
        vals_grad = jnp.dot(attn_rows_grad, out_full, preferred_element_type=jnp.float32).astype(
            jnp.bfloat16
        )
        vals_heads = vals_grad.reshape(routed_count, HEADS, HDIM)
        raw_again = jnp.einsum(
            "rhd,khd->hrk", query_heads, key_heads, preferred_element_type=jnp.float32
        )
        scores_again = jnp.where(allowed[None], raw_again * score_scale, very_low)
        probs_again = jnp.exp(scores_again - log_total)
        prob_grad = jnp.einsum(
            "rhd,khd->hrk", vals_heads, value_heads, preferred_element_type=jnp.float32
        )
        inner_sum = jnp.sum(probs_again * prob_grad, axis=-1, keepdims=True)
        score_grad = (probs_again * (prob_grad - inner_sum) * score_scale).astype(jnp.bfloat16)
        query_rot_grad = jnp.einsum(
            "hrk,khd->rhd", score_grad, key_heads, preferred_element_type=jnp.float32
        ).reshape(routed_count, query_width)
        query_grad = rotate(query_rot_grad, row_tables, True).astype(jnp.bfloat16)
        key_rot_grad = jnp.einsum(
            "hrk,rhd->khd", score_grad, query_heads, preferred_element_type=jnp.float32
        ).reshape(group_rows, query_width)
        value_grad = jnp.einsum(
            "hrk,rhd->khd",
            probs_again.astype(jnp.bfloat16),
            vals_heads,
            preferred_element_type=jnp.float32,
        ).reshape(group_rows, query_width)
        key_grad = rotate(key_rot_grad, tables, True)
        kv_piece_grad = lax.psum_scatter(
            jnp.concatenate([key_grad, value_grad], axis=1).astype(jnp.bfloat16),
            "expert",
            scatter_dimension=1,
            tiled=True,
        )
        hidden_one_part = (
            jnp.zeros((group_rows, model_width), jnp.float32)
            .at[rows_one]
            .add(contract_last(query_grad, query_full))
        )
        hidden_one_part = hidden_one_part + contract_last(kv_piece_grad, kv_full)
        hidden_one_grad, slot_one_grad = (
            lax.psum_scatter(
                hidden_one_part.astype(jnp.bfloat16), "expert", scatter_dimension=0, tiled=True
            ).astype(jnp.float32),
            lax.psum_scatter(
                slot_part_one.astype(jnp.bfloat16), "expert", scatter_dimension=0, tiled=True
            ).astype(jnp.float32),
        )
        gates_own = lax.dynamic_slice_in_dim(gates_one, own_start, tok_rows, 0)
        matches_own = lax.dynamic_slice_in_dim(matches_one, own_start, tok_rows, 0)
        slots_own = lax.dynamic_slice_in_dim(slots_one, own_start, tok_rows, 0)
        logit_one_grad = gate_back(slot_one_grad, gates_own, matches_own, slots_own).astype(
            jnp.bfloat16
        )
        hidden_one_grad = hidden_one_grad + contract_last(logit_one_grad, attn_router)
        router_one_grad = router_one_grad + contract_first(
            lax.dynamic_slice_in_dim(hidden_one, own_start, tok_rows, 0), logit_one_grad
        )
        normed_own = lax.dynamic_slice_in_dim(normed_one, own_start, tok_rows, 0)
        scale_own = lax.dynamic_slice_in_dim(scale_one, own_start, tok_rows, 0)
        gain_one_grad = gain_one_grad + jnp.sum(hidden_one_grad * normed_own, axis=0)
        input_grad = lax.dynamic_slice_in_dim(resid_grad, own_start, tok_rows, 0) + norm_back(
            hidden_one_grad * gain_one, normed_own, scale_own
        )
        grads_list.append(input_grad.astype(jnp.bfloat16))
        kept_pairs[0].append((hidden_rows_one, query_grad))
        kept_pairs[1].append((attn_rows_grad, attn_vals))
        kept_pairs[2].append((hidden_rows_two, joint_grad))
        kept_pairs[3].append((ffn_rows_grad, active))
        kept_pairs[4].append((hidden_one, kv_piece_grad))
    gain_one_total, gain_two_total, router_one_total, router_two_total = lax.psum(
        (gain_one_grad, gain_two_grad, router_one_grad, router_two_grad), ("dp", "expert")
    )
    joined_pairs = []
    for pair_list in kept_pairs:
        joined_pairs.append(
            (
                jnp.concatenate([entry[0] for entry in pair_list], axis=0),
                jnp.concatenate([entry[1] for entry in pair_list], axis=0),
            )
        )
    pieces = []
    for left_rows, right_rows in joined_pairs:
        pieces.append(contract_first(left_rows, right_rows))
    stacked_grad = lax.psum_scatter(
        jnp.concatenate(pieces, axis=1).astype(jnp.bfloat16), "dp", scatter_dimension=0, tiled=True
    ).astype(jnp.float32)
    split_two = 2 * query_width
    split_three = split_two + 2 * FF
    split_four = split_three + FF
    query_grad_out = stacked_grad[:, :query_width][None]
    out_grad_out = stacked_grad[:, query_width:split_two][None]
    gate_up_grad_out = stacked_grad[:, split_two:split_three][None]
    down_grad_out = stacked_grad[:, split_three:split_four][None]
    kv_grad_out = stacked_grad[:, split_four:]
    peak_table = jnp.where(slot_range[:, None] == column_index, head_peak[None, :], very_low)
    peaks_all = lax.pmax(peak_table, ("dp", "expert"))
    limit = clip_limit[0].astype(jnp.float32)
    factor = limit / jnp.maximum(peaks_all, limit)
    own_factor = jnp.sum(jnp.where(slot_range[:, None] == column_index, factor, 0.0), axis=0)
    query_scale = jnp.repeat(jnp.sqrt(own_factor), HDIM)
    query_clipped = (query_weight.astype(jnp.float32) * query_scale[None, None, :]).astype(
        jnp.bfloat16
    )
    full_scale = jnp.concatenate(
        [jnp.repeat(jnp.sqrt(jnp.min(factor, axis=0)), HDIM), jnp.ones((query_width,), jnp.float32)]
    )
    piece_scale = lax.dynamic_slice_in_dim(full_scale, column_index * piece_width, piece_width)
    kv_clipped = (kv_weight.astype(jnp.float32) * piece_scale[None, :]).astype(jnp.bfloat16)
    batch_ids = jnp.arange(micro_count, dtype=jnp.int32)[:, None]
    stacked_out = jnp.stack(outputs_list)
    stacked_in = jnp.stack(grads_list)
    back_out = jnp.zeros_like(stacked_out).at[batch_ids, dealing].set(stacked_out)
    back_in = jnp.zeros_like(stacked_in).at[batch_ids, dealing].set(stacked_in)
    returned_out, returned_in = (
        lax.all_to_all(
            back_out.reshape(micro_count, group_count, piece_rows, model_width),
            "dp",
            split_axis=1,
            concat_axis=1,
            tiled=True,
        ),
        lax.all_to_all(
            back_in.reshape(micro_count, group_count, piece_rows, model_width),
            "dp",
            split_axis=1,
            concat_axis=1,
            tiled=True,
        ),
    )
    block_output = returned_out.reshape(micro_count, tok_rows, model_width)
    tokens_grad = returned_in.reshape(micro_count, tok_rows, model_width)
    return (
        block_output,
        tokens_grad,
        gain_one_total,
        gain_two_total,
        router_one_total,
        router_two_total,
        query_grad_out,
        out_grad_out,
        kv_grad_out,
        gate_up_grad_out,
        down_grad_out,
        query_clipped,
        kv_clipped,
    )


def solution(mesh):
    placed = (
        P(None, ("dp", "expert"), None),
        P(None, ("dp", "expert"), None),
        P(),
        P(None, ("dp", "expert")),
        P(None, "dp", None),
        P(None, "dp", None),
        P(),
        P(),
        P(),
        P(),
        P(),
        P(),
        P("expert", "dp", None),
        P("expert", "dp", None),
        P("dp", "expert"),
        P("expert", "dp", None),
        P("expert", "dp", None),
    )
    return jax.shard_map(
        local,
        mesh=mesh,
        in_specs=placed,
        out_specs=(
            P(None, ("dp", "expert"), None),
            P(None, ("dp", "expert"), None),
            P(),
            P(),
            P(),
            P(),
            P("expert", "dp", None),
            P("expert", "dp", None),
            P("dp", "expert"),
            P("expert", "dp", None),
            P("expert", "dp", None),
            P("expert", "dp", None),
            P("dp", "expert"),
        ),
        check_vma=False,
    )
```

profile of v0, /device:TPU:8, one launch (start us, length us, event | category | flops | bytes accessed | tf_op | source)
XLA Modules:
  0.0 2175.3 jit_solution(13260139579625172018)
XLA Ops:
  40.9 25.8 %all-gather.33.cloned.1.call-done = bf16[1,256,2048]{2,1,0:T(8,128)(2,1)} async-done(((bf16[1,64,2048]{2,1,0:T(8,128)(2,1)}), bf16[1,256,2048]{2,1,0:T(8,128)(2,1)}) %all-gather.33.cloned.1.call-update) | async-done | bytes 1048592 | tf_op jit(solution)/shard_map/all_gather | solution.py:177
  71.0 33.8 %all-gather.31.cloned.1.call-done = bf16[2048,1024]{1,0:T(8,128)(2,1)} async-done(((bf16[256,1024]{1,0:T(8,128)(2,1)}), bf16[2048,1024]{1,0:T(8,128)(2,1)}) %all-gather.31.cloned.1.call-update) | async-done | bytes 4194320 | tf_op jit(solution)/shard_map/all_gather | solution.py:173
  109.1 25.8 %all-gather.29.cloned.1.call-done = bf16[1,256,2048]{2,1,0:T(8,128)(2,1)} async-done(((bf16[1,64,2048]{2,1,0:T(8,128)(2,1)}), bf16[1,256,2048]{2,1,0:T(8,128)(2,1)}) %all-gather.29.cloned.1.call-update) | async-done | bytes 1048592 | tf_op jit(solution)/shard_map/all_gather | solution.py:177
  185.0 42.4 %all-gather.17.cloned.1.call-done = bf16[256,4096]{1,0:T(8,128)(2,1)} async-done(((bf16[256,1024]{1,0:T(8,128)(2,1)}), bf16[256,4096]{1,0:T(8,128)(2,1)}) %all-gather.17.cloned.1.call-update) | async-done | bytes 2097168 | tf_op jit(solution)/shard_map/all_gather | solution.py:196
  237.7 46.3 %all-gather.19.cloned.1.call-done = bf16[1,2048,2048]{2,1,0:T(8,128)(2,1)} async-done(((bf16[1,256,2048]{2,1,0:T(8,128)(2,1)}), bf16[1,2048,2048]{2,1,0:T(8,128)(2,1)}) %all-gather.19.cloned.1.call-update) | async-done | bytes 8388624 | tf_op jit(solution)/shard_map/all_gather | solution.py:169
  283.9 12.3 copy.180
  314.3 25.9 %all-gather.21.cloned.1.call-done = bf16[1,2048,2048]{2,1,0:T(8,128)(2,1)} async-done(((bf16[1,256,2048]{2,1,0:T(8,128)(2,1)}), bf16[1,2048,2048]{2,1,0:T(8,128)(2,1)}) %all-gather.21.cloned.1.call-update) | async-done | bytes 8388624 | tf_op jit(solution)/shard_map/all_gather | solution.py:170
  374.0 25.3 %all-gather.35.cloned.1.call-done = bf16[1,256,2048]{2,1,0:T(8,128)(2,1)} async-done(((bf16[1,64,2048]{2,1,0:T(8,128)(2,1)}), bf16[1,256,2048]{2,1,0:T(8,128)(2,1)}) %all-gather.35.cloned.1.call-update) | async-done | bytes 1048592 | tf_op jit(solution)/shard_map/all_gather | solution.py:178
  403.1 152.3 %all-reduce.18.cloned.1.call-done = (f32[256,2048]{1,0:T(8,128)}, f32[256,2048]{1,0:T(8,128)}) async-done(((f32[256,2048]{1,0:T(8,128)}, f32[256,2048]{1,0:T(8,128)}), (f32[256,2048]{1,0:T(8,128)}, f32[256,2048]{1,0:T(8,128)})) %all-reduce.18.cloned.1.call-update) | async-done | bytes 4194320 | tf_op jit(solution)/shard_map/psum | solution.py:238
  565.6 207.9 %all-gather.23.cloned.1.call-done = bf16[1,2048,11264]{2,1,0:T(8,128)(2,1)} async-done(((bf16[1,256,11264]{2,1,0:T(8,128)(2,1)}), bf16[1,2048,11264]{2,1,0:T(8,128)(2,1)}) %all-gather.23.cloned.1.call-update) | async-done | bytes 46137360 | tf_op jit(solution)/shard_map/all_gather | solution.py:171
  773.5 25.0 %fusion.6 = f32[192,11264]{1,0:T(8,128)} fusion(bf16[192,2048]{1,0:T(8,128)(2,1)S(1)} %gather_fusion.11, bf16[1,2048,11264]{2,1,0:T(8,128)(2,1)} %all-gather.23.cloned.1.call-done), kind=kOutput, calls=%fused_computation.38 | convolution fusion | flops 8858370048 | bytes 55574528 | tf_op jit(solution)/shard_map/dot_general | solution.py:251
  804.6 23.2 %fusion.8 = f32[192,11264]{1,0:T(8,128)} fusion(bf16[192,2048]{1,0:T(8,128)(2,1)S(1)} %copy-done.78, bf16[1,2048,11264]{2,1,0:T(8,128)(2,1)} %all-gather.23.cloned.1.call-done), kind=kOutput, calls=%fused_computation.40 | convolution fusion | flops 8858370048 | bytes 55574528 | tf_op jit(solution)/shard_map/dot_general | solution.py:251
  835.9 55.9 %all-gather.25.cloned.1.call-done = bf16[1,2048,5632]{2,1,0:T(8,128)(2,1)} async-done(((bf16[1,256,5632]{2,1,0:T(8,128)(2,1)}), bf16[1,2048,5632]{2,1,0:T(8,128)(2,1)}) %all-gather.25.cloned.1.call-update) | async-done | bytes 23068688 | tf_op jit(solution)/shard_map/all_gather | solution.py:172
  891.8 13.6 multiply_reduce_fusion.7
  905.5 13.8 multiply_reduce_fusion.9
  952.4 15.2 multiply_convert_fusion.1
  967.6 21.8 %fusion.2 = f32[192,2048]{1,0:T(8,128)S(1)} fusion(bf16[1,2048,11264]{2,1,0:T(8,128)(2,1)} %all-gather.23.cloned.1.call-done, bf16[192,5632]{1,0:T(8,128)(2,1)} %get-tuple-element.63, bf16[192,5632]{1,0:T(8,128)(2,1)} %get-tuple-element.62), kind=kOutput, calls=%fused_computation.34 | convolution fusion | flops 8867020800 | bytes 52035584 | tf_op jit(solution)/shard_map/dot_general | solution.py:18
  993.8 15.0 multiply_convert_fusion.3
  1008.8 21.7 fusion.4
  1035.8 152.6 %all-reduce.16.cloned.1.call-done = (f32[256,2048]{1,0:T(8,128)}, f32[256,2048]{1,0:T(8,128)}) async-done(((f32[256,2048]{1,0:T(8,128)}, f32[256,2048]{1,0:T(8,128)}), (f32[256,2048]{1,0:T(8,128)}, f32[256,2048]{1,0:T(8,128)})) %all-reduce.16.cloned.1.call-update) | async-done | bytes 4194320 | tf_op jit(solution)/shard_map/psum | solution.py:285
  1214.8 24.9 %fusion.84 = f32[256,16,128]{2,0,1:T(8,128)} fusion(f32[16,192,256]{2,1,0:T(8,128)} %fusion.158, f32[16,192,256]{2,1,0:T(8,128)} %copy-done.11, f32[16,192]{1,0:T(8,128)S(1)} %log_add_fusion.1, bf16[192,16,64]{2,0,1:T(8,128)(2,1)} %get-tuple-element.85, bf16[192,16,64]{2,0,1:T(8,128)(2,1)S(1)} %copy-done.49), kind=kOutput, calls=%fused_computation.164 | convolution fusion | flops 208407808 | bytes 9187328 | tf_op jit(solution)/shard_map/hrk,rhd->khd/dot_general | solution.py:327
  1262.8 23.3 %fusion.81 = f32[256,16,128]{2,0,1:T(8,128)} fusion(f32[16,192,256]{2,1,0:T(8,128)} %fusion.155, f32[16,192,256]{2,1,0:T(8,128)S(1)} %copy-done.10, f32[16,192]{1,0:T(8,128)S(1)} %log_add_fusion, bf16[192,16,64]{2,0,1:T(8,128)(2,1)} %copy-done.47, bf16[192,16,64]{2,0,1:T(8,128)(2,1)} %copy-done.46), kind=kOutput, calls=%fused_computation.163 | convolution fusion | flops 208407808 | bytes 9187328 | tf_op jit(solution)/shard_map/hrk,rhd->khd/dot_general | solution.py:327
  1327.8 22.6 %fusion.139 = f32[192,16,128]{2,0,1:T(8,128)} fusion(f32[16,192,256]{2,1,0:T(8,128)} %fusion.155, f32[16,192,256]{2,1,0:T(8,128)S(1)} %copy-done.10, f32[16,192]{1,0:T(8,128)S(1)} %log_add_fusion, bf16[256,16,64]{2,0,1:T(8,128)(2,1)} %get-tuple-element.67, bf16[256,16,64]{2,0,1:T(8,128)(2,1)} %get-tuple-element.66), kind=kOutput, calls=%fused_computation.225 | convolution fusion | flops 208932096 | bytes 8925184 | tf_op jit(solution)/shard_map/hrk,khd->rhd/dot_general | solution.py:323
  1350.4 24.6 %fusion.142 = f32[192,16,128]{2,0,1:T(8,128)} fusion(f32[16,192,256]{2,1,0:T(8,128)} %fusion.158, f32[16,192,256]{2,1,0:T(8,128)} %copy-done.11, f32[16,192]{1,0:T(8,128)S(1)} %log_add_fusion.1, bf16[256,16,64]{2,0,1:T(8,128)(2,1)} %get-tuple-element.65, bf16[256,16,64]{2,0,1:T(8,128)(2,1)} %get-tuple-element.64), kind=kOutput, calls=%fused_computation.226 | convolution fusion | flops 208932096 | bytes 8925184 | tf_op jit(solution)/shard_map/hrk,khd->rhd/dot_general | solution.py:323
  1406.8 12.3 copy.208
  1419.1 12.3 copy.209
  1483.4 32.9 %convert_dynamic-update-slice_fusion = bf16[2048,22016]{1,0:T(8,128)(2,1)} fusion(bf16[2048,22016]{1,0:T(8,128)(2,1)} %constant_dynamic-update-slice_fusion, bf16[192,5632]{1,0:T(8,128)(2,1)} %get-tuple-element.63, bf16[192,5632]{1,0:T(8,128)(2,1)} %get-tuple-element.62, bf16[192,5632]{1,0:T(8,128)(2,1)} %get-tuple-element.61, ...), kind=kOutput, calls=%fused_computation.42 | convolution fusion | flops 17777557504 | bytes 56360960 | tf_op jit(solution)/shard_map/dot_general | solution.py:24
  1516.3 18.9 convert_dynamic-update-slice_fusion.1
  1542.6 40.9 %pmax.7 = f32[4,16]{1,0:T(4,128)S(1)} all-reduce(f32[4,16]{1,0:T(4,128)S(1)} %broadcast_select_fusion.2), channel_id=1, replica_groups=mesh['dp'=8,'expert'=4] {'dp','expert'}, use_global_device_ids=true, to_apply=%region_105.107 | all-reduce | flops 64 | bytes 512 | tf_op jit(solution)/shard_map/pmax | solution.py:405
  1652.7 380.0 %reduce-scatter.32.cloned.1.call-done = bf16[256,22016]{1,0:T(8,128)(2,1)} async-done(((bf16[2048,22016]{1,0:T(8,128)(2,1)}), bf16[256,22016]{1,0:T(8,128)(2,1)}) %reduce-scatter.32.cloned.1.call-update) | async-done | bytes 11272208
  2032.7 12.7 convert_element_type.374
  2067.9 95.4 %all-reduce.14.cloned.1.call-done = (f32[2048]{0:T(1024)}, f32[2048]{0:T(1024)}, f32[2048,4]{0,1:T(4,128)}, f32[2048,4]{0,1:T(4,128)}) async-done(((f32[2048]{0:T(1024)}, f32[2048]{0:T(1024)}, f32[2048,4]{0,1:T(4,128)}, f32[2048,4]{0,1:T(4,128)}), (f32[2048]{0:T(1024)}, f32[2048]{0:T(1024)}, f32[2048,4]{0,1:T(4,128)}, f32[2048,4]{0,1:T(4,128)})) %all-reduce.14.cloned.1.call-update) | async-done | bytes 81936 | tf_op jit(solution)/shard_map/psum | solution.py:379
  (699 shorter events, 501.5 us)
Async XLA Ops:
  7.2 557.5 %copy-start = (bf16[2048,4]{0,1:T(4,128)(2,1)S(1)}, bf16[2048,4]{0,1:T(4,128)(2,1)}, u32[]{:S(2)}) copy-start(bf16[2048,4]{0,1:T(4,128)(2,1)} %param.30) | copy-start | bytes 49156
  9.2 13.5 all-to-all-start.2
  22.6 13.2 all-to-all-start
  26.1 40.5 %all-gather.33.cloned.1.call-start = ((), (), s32[]{:S(2)}) async-start(), calls=%async_computation.27 | async-start | bytes 1310720 | tf_op jit(solution)/shard_map/all_gather | solution.py:177
  39.3 65.5 %all-gather.31.cloned.1.call-start = ((), (), s32[]{:S(2)}) async-start(), calls=%async_computation.26 | async-start | bytes 4718592 | tf_op jit(solution)/shard_map/all_gather | solution.py:173
  40.1 94.8 %all-gather.29.cloned.1.call-start = ((), (), s32[]{:S(2)}) async-start(), calls=%async_computation.25 | async-start | bytes 1310720 | tf_op jit(solution)/shard_map/all_gather | solution.py:177
  40.8 140.0 %all-gather.27.cloned.1.call-start = ((), (), s32[]{:S(2)}) async-start(), calls=%async_computation.19 | async-start | bytes 2621440 | tf_op jit(solution)/shard_map/all_gather | solution.py:196
  109.1 118.3 %all-gather.17.cloned.1.call-start = ((), (), s32[]{:S(2)}) async-start(), calls=%async_computation.13 | async-start | bytes 2621440 | tf_op jit(solution)/shard_map/all_gather | solution.py:196
  141.5 142.4 %all-gather.19.cloned.1.call-start = ((), (), s32[]{:S(2)}) async-start(), calls=%async_computation.14 | async-start | bytes 9437184 | tf_op jit(solution)/shard_map/all_gather | solution.py:169
  142.1 198.1 %all-gather.21.cloned.1.call-start = ((), (), s32[]{:S(2)}) async-start(), calls=%async_computation.15 | async-start | bytes 9437184 | tf_op jit(solution)/shard_map/all_gather | solution.py:170
  142.9 227.4 %all-gather.37.cloned.1.call-start = ((), (), s32[]{:S(2)}) async-start(), calls=%async_computation.29 | async-start | bytes 1310720 | tf_op jit(solution)/shard_map/all_gather | solution.py:178
  143.0 422.0 %copy-start.114 = (s32[256,2]{0,1:T(2,128)}, s32[256,2]{0,1:T(2,128)S(1)}, u32[]{:S(2)}) copy-start(s32[256,2]{0,1:T(2,128)S(1)} %get-tuple-element.105) | copy-start | bytes 6148
  143.0 422.5 %copy-start.112 = (s32[256,2]{0,1:T(2,128)}, s32[256,2]{0,1:T(2,128)S(1)}, u32[]{:S(2)}) copy-start(s32[256,2]{0,1:T(2,128)S(1)} %get-tuple-element.106) | copy-start | bytes 6148
  149.0 214.7 %copy-start.136 = (s32[192,1]{0,1:T(1,128)}, s32[192,1]{0,1:T(1,128)S(1)}, u32[]{:S(2)}) copy-start(s32[192,1]{0,1:T(1,128)S(1)} %get-tuple-element.157) | copy-start | bytes 2308
  153.7 245.6 %all-gather.35.cloned.1.call-start = ((), (), s32[]{:S(2)}) async-start(), calls=%async_computation.28 | async-start | bytes 1310720 | tf_op jit(solution)/shard_map/all_gather | solution.py:178
  165.3 390.2 %all-reduce.18.cloned.1.call-start = ((), (), s32[]{:S(2)}) async-start(), calls=%async_computation.35 | async-start | bytes 8388608 | tf_op jit(solution)/shard_map/psum | solution.py:238
  368.3 405.2 %all-gather.23.cloned.1.call-start = ((), (), s32[]{:S(2)}) async-start(), calls=%async_computation.16 | async-start | bytes 51904512 | tf_op jit(solution)/shard_map/all_gather | solution.py:171
  369.1 522.8 %all-gather.25.cloned.1.call-start = ((), (), s32[]{:S(2)}) async-start(), calls=%async_computation.17 | async-start | bytes 25952256 | tf_op jit(solution)/shard_map/all_gather | solution.py:172
  369.7 818.8 %all-reduce.16.cloned.1.call-start = ((), (), s32[]{:S(2)}) async-start(), calls=%async_computation.34 | async-start | bytes 8388608 | tf_op jit(solution)/shard_map/psum | solution.py:285
  562.6 210.9 %copy-start.77 = (bf16[192,2048]{1,0:T(8,128)(2,1)}, bf16[192,2048]{1,0:T(8,128)(2,1)S(1)}, u32[]{:S(2)}) copy-start(bf16[192,2048]{1,0:T(8,128)(2,1)S(1)} %gather_fusion.11) | copy-start | bytes 2359300
  1035.0 403.9 %reduce-scatter.20.cloned.1.call-start = ((), (), s32[]{:S(2)}) async-start(), calls=%async_computation.21 | async-start | bytes 2621440 | tf_op jit(solution)/shard_map/reduce_scatter | solution.py:337
  1247.8 225.6 %reduce-scatter.24.cloned.1.call-start = ((), (), s32[]{:S(2)}) async-start(), calls=%async_computation.23 | async-start | bytes 2621440 | tf_op jit(solution)/shard_map/reduce_scatter | solution.py:337
  1296.7 288.3 %reduce-scatter.18.cloned.1.call-start = ((), (), s32[]{:S(2)}) async-start(), calls=%async_computation.20 | async-start | bytes 1310720 | tf_op jit(solution)/shard_map/reduce_scatter | solution.py:263
  1305.2 281.1 %reduce-scatter.16.cloned.1.call-start = ((), (), s32[]{:S(2)}) async-start(), calls=%async_computation.18 | async-start | bytes 1310720 | tf_op jit(solution)/shard_map/reduce_scatter | solution.py:263
  1313.4 303.2 %reduce-scatter.30.cloned.1.call-start = ((), (), s32[]{:S(2)}) async-start(), calls=%async_computation.31 | async-start | bytes 81920
  1377.7 239.7 %reduce-scatter.28.cloned.1.call-start = ((), (), s32[]{:S(2)}) async-start(), calls=%async_computation.30 | async-start | bytes 81920
  1431.4 187.4 %reduce-scatter.22.cloned.1.call-start = ((), (), s32[]{:S(2)}) async-start(), calls=%async_computation.22 | async-start | bytes 1310720 | tf_op jit(solution)/shard_map/reduce_scatter | solution.py:350
  1448.6 171.9 %reduce-scatter.26.cloned.1.call-start = ((), (), s32[]{:S(2)}) async-start(), calls=%async_computation.24 | async-start | bytes 1310720 | tf_op jit(solution)/shard_map/reduce_scatter | solution.py:350
  1482.9 549.8 %reduce-scatter.32.cloned.1.call-start = ((), (), s32[]{:S(2)}) async-start(), calls=%async_computation.32 | async-start | bytes 101449728
  1600.8 13.4 all-to-all-start.1
  1638.6 13.2 all-to-all-start.3
  1642.2 521.1 %all-reduce.14.cloned.1.call-start = ((), (), s32[]{:S(2)}) async-start(), calls=%async_computation.33 | async-start | bytes 163840 | tf_op jit(solution)/shard_map/psum | solution.py:379
  (165 other events, 3251.1 us)
Sparse Core Ops, SparseCore 0:
  39.4 27.1 all-gather.32
  68.5 36.2 all-gather.30
  107.0 27.8 all-gather.28
  136.9 43.8 all-gather.26
  182.8 44.5 all-gather.16
  229.1 54.7 all-gather.18
  285.8 54.3 all-gather.20
  341.8 27.8 all-gather.36
  371.9 27.4 all-gather.34
  402.8 152.7 all-reduce.17
  557.6 215.8 all-gather.22
  775.3 116.4 all-gather.24
  1035.2 153.2 all-reduce.15
  1248.0 42.7 reduce-scatter.19
  1296.8 42.6 reduce-scatter.23
  1341.7 26.7 reduce-scatter.17
  1370.8 25.7 reduce-scatter.15
  1398.7 16.9 reduce-scatter.29
  1431.5 17.6 reduce-scatter.27
  1451.4 26.0 reduce-scatter.21
  1483.0 26.5 reduce-scatter.25
  1541.0 491.6 reduce-scatter.31
  2039.4 123.8 all-reduce.13
where the time goes:
time: 2190 us; the launch traced here: 2180 us
  waiting for transfers between devices  1310 us (60%)
  matrix products  404 us (18%)
  other arithmetic  202 us (9%)
  local copies, waits for them, and re-layouts  178 us (8%)
  blocking collectives  49.9 us (2%)
    unnamed x26, waiting for transfers between devices  384 us
    all_gather x1, waiting for transfers between devices, local(): lax.all_gather(sharded[2], 'dp', axis=1, tiled=True)  208 us
    psum x1, waiting for transfers between devices, local(): lax.psum((hidden_two_part, slot_part_two), 'expert')  153 us
    psum x1, waiting for transfers between devices, local(): attn_total = lax.psum(attn_part, 'expert')  152 us
    dot_general x14, matrix products, contract_last(): lax.dot_general(left, right, (((1,), (1,)), ((), ())), preferred_element_...  112 us
    psum x1, waiting for transfers between devices, local(): lax.psum((gain_one_grad, gain_two_grad, router_one_grad, router_two_grad)...  95.4 us
    dot_general x9, matrix products, contract_first(): lax.dot_general(left, right, (((0,), (0,)), ((), ())), preferred_element_...  75.1 us
    all_gather x1, waiting for transfers between devices, local(): lax.all_gather(sharded[3], 'dp', axis=1, tiled=True)  55.9 us
  transfers between devices with their start and end apart: 27, of which 18 were waited for; matrix products, arithmetic and copies ran while one was open for 26% of the time, Pallas kernels for 0%

commit v1 on v0

v1 whole, which is shorter than its diff:
```python
import jax
import jax.numpy as jnp
from jax import lax
from jax.sharding import PartitionSpec as P

HEADS = 16
HDIM = 128
FF = 5632
TOP = 2

eps_norm = 1e-06
rope_base = 10000.0
very_low = -1e30

f32 = jnp.float32
bf16 = jnp.bfloat16


def dot(left, right):
    return jnp.dot(left, right, preferred_element_type=f32)


def dot_t(left, right):
    return lax.dot_general(left, right, (((1,), (1,)), ((), ())), preferred_element_type=f32)


def t_dot(left, right):
    return lax.dot_general(left, right, (((0,), (0,)), ((), ())), preferred_element_type=f32)


def swap(value, axis, step):
    count = lax.axis_size(axis)
    return lax.ppermute(value, axis, [(i, i ^ step) for i in range(count)])


def take(stacked, index):
    return lax.dynamic_index_in_dim(stacked, index, 0, keepdims=False)


def place(parts, positions):
    out = jnp.zeros((len(parts),) + parts[0].shape, parts[0].dtype)
    for part, position in zip(parts, positions):
        out = lax.dynamic_update_index_in_dim(out, part, position, 0)
    return out


def rotation_tables(places):
    half_dim = HDIM // 2
    frequency = rope_base ** (-jnp.arange(half_dim, dtype=f32) * 2.0 / HDIM)
    angles = places.astype(f32)[..., None] * frequency
    return jnp.cos(angles), jnp.sin(angles)


def rotate(values, tables, inverse):
    cosine, sine = tables
    if inverse:
        sine = -sine
    rows = values.shape[0]
    half_dim = HDIM // 2
    shaped = values.reshape(rows, -1, HDIM)
    first_half = shaped[..., :half_dim]
    second_half = shaped[..., half_dim:]
    cosine, sine = cosine[:, None, :], sine[:, None, :]
    rotated = jnp.concatenate(
        [first_half * cosine - second_half * sine, second_half * cosine + first_half * sine],
        axis=-1,
    )
    return rotated.reshape(rows, -1)


def normalize(values):
    row_scale = lax.rsqrt(jnp.mean(values * values, axis=-1, keepdims=True) + eps_norm)
    return values * row_scale, row_scale


def norm_back(grad_hat, normed, row_scale):
    return row_scale * (grad_hat - normed * jnp.mean(grad_hat * normed, axis=-1, keepdims=True))


def route_gates(logits, routes, expert_table):
    expert_ids = jnp.arange(expert_table.shape[0], dtype=jnp.int32)
    matches = routes[:, :, None] == expert_ids[None, None, :]
    picked = jnp.sum(jnp.where(matches, logits[:, None, :], 0.0), axis=-1)
    gate_vals = jax.nn.softmax(picked, axis=-1)
    slot_ids = route_slots(routes, expert_table)
    chosen = slot_ids[:, :, None] == expert_ids[None, None, :]
    gates = jnp.sum(jnp.where(chosen, gate_vals[:, :, None], 0.0), axis=1)
    return gates, matches, chosen, gate_vals


def route_slots(routes, expert_table):
    expert_ids = jnp.arange(expert_table.shape[0], dtype=jnp.int32)
    matches = routes[..., None] == expert_ids
    return jnp.sum(jnp.where(matches, expert_table, 0), axis=-1)


def gate_back(slot_grad, gate_vals, matches, chosen):
    picked = jnp.sum(jnp.where(chosen, slot_grad[:, None, :], 0.0), axis=-1)
    inner_sum = jnp.sum(gate_vals * picked, axis=-1, keepdims=True)
    picked_grad = gate_vals * (picked - inner_sum)
    return jnp.sum(jnp.where(matches, picked_grad[:, :, None], 0.0), axis=1)


def local(
    tokens,
    cotangent,
    seq_lengths,
    dealing,
    attn_routes,
    ffn_routes,
    expert_table,
    clip_limit,
    attn_gain,
    ffn_gain,
    attn_router,
    ffn_router,
    query_weight,
    attn_out_weight,
    kv_weight,
    gate_up_weight,
    down_weight,
):
    micro, tok_rows, width = tokens.shape
    dp_count = lax.axis_size("dp")
    slots = lax.axis_size("expert")
    col = lax.axis_index("expert")
    group = lax.axis_index("dp")
    piece_rows = tok_rows // dp_count
    cap = tok_rows * TOP * 3 // (2 * slots)
    group_rows = tok_rows * slots
    all_rows = micro * group_rows
    home_rows = micro * tok_rows
    query_width = HEADS * HDIM
    own_heads = HEADS // slots
    own_width = own_heads * HDIM
    shard_rows = query_weight.shape[1]
    score_scale = HDIM ** (-0.5)
    core = group % 2
    chip = group // 2
    side = chip % 2
    chips = dp_count // 2
    lines = chips // 2
    quarter = FF // 4
    chip_rows = 2 * shard_rows

    both = jnp.stack([tokens, cotangent]).reshape(2 * micro, dp_count, piece_rows, width)
    both = lax.all_to_all(both.transpose(1, 0, 2, 3), "dp", split_axis=0, concat_axis=0, tiled=True)
    both = both.transpose(1, 0, 2, 3).reshape(2, micro, tok_rows, width)
    deal = (dealing[:, :, None] == jnp.arange(tok_rows, dtype=jnp.int32)).astype(bf16)
    work = jnp.einsum("mtr,bmrd->bmtd", deal, both, preferred_element_type=f32)
    x_home = work[0].reshape(home_rows, width)
    dy_home = work[1].reshape(home_rows, width)

    def columns_of(shard):
        pieces = shard.reshape(shard_rows, slots, own_width)
        parts = [
            swap(lax.dynamic_index_in_dim(pieces, col ^ k, 1, keepdims=False), "expert", k)
            if k
            else lax.dynamic_index_in_dim(pieces, col, 1, keepdims=False)
            for k in range(slots)
        ]
        out = jnp.zeros((shard_rows, query_width), shard.dtype)
        for k, part in enumerate(parts):
            out = lax.dynamic_update_slice_in_dim(out, part, (col ^ k) * own_width, 1)
        return out

    def slots_of(columns):
        pieces = columns.reshape(shard_rows, slots, own_width)
        out = jnp.zeros((shard_rows, query_width), columns.dtype)
        for k in range(slots):
            part = lax.dynamic_index_in_dim(pieces, col ^ k, 1, keepdims=False)
            part = swap(part, "expert", k) if k else part
            out = lax.dynamic_update_slice_in_dim(out, part, (col ^ k) * own_width, 1)
        return out

    half_slots = slots // 2
    first_pairs = [(c, 2 * c) for c in range(half_slots)]
    first_pairs += [(c, 2 * (c - half_slots) + 1) for c in range(half_slots, slots)]
    second_pairs = [(c, 2 * c + 1) for c in range(half_slots)]
    second_pairs += [(c, 2 * (c - half_slots)) for c in range(half_slots, slots)]
    holds_keys = col < half_slots
    even_col = col % 2 == 0
    low_kv, high_kv = kv_weight[:, :own_width], kv_weight[:, own_width:]
    first_got = lax.ppermute(jnp.where(holds_keys, low_kv, high_kv), "expert", first_pairs)
    second_got = lax.ppermute(jnp.where(holds_keys, high_kv, low_kv), "expert", second_pairs)
    own_kv = jnp.concatenate(
        [
            jnp.where(even_col, first_got, second_got),
            jnp.where(even_col, second_got, first_got),
        ],
        axis=1,
    )
    kv_full = lax.all_gather(own_kv, "dp", axis=0, tiled=True)
    query_full = lax.all_gather(columns_of(query_weight[0]), "dp", axis=0, tiled=True)
    out_full = lax.all_gather(columns_of(attn_out_weight[0]), "dp", axis=0, tiled=True)

    def quarter_of(half, part):
        start = (2 * half + part) * quarter
        return jnp.concatenate(
            [
                lax.dynamic_slice_in_dim(gate_up_weight[0], start, quarter, 1),
                lax.dynamic_slice_in_dim(gate_up_weight[0], FF + start, quarter, 1),
                lax.dynamic_slice_in_dim(down_weight[0], start, quarter, 1),
            ],
            axis=1,
        )

    def pair_rows(own, other):
        return jnp.concatenate(
            [jnp.where(core == 0, own, other), jnp.where(core == 0, other, own)], axis=0
        )

    keep_side = pair_rows(quarter_of(side, core), swap(quarter_of(side, 1 - core), "dp", 1))
    send_side = pair_rows(quarter_of(1 - side, core), swap(quarter_of(1 - side, 1 - core), "dp", 1))
    from_side = swap(send_side, "dp", 2)
    chunk_parts = [keep_side, from_side]
    for line in range(1, lines):
        chunk_parts.append(swap(keep_side, "dp", 4 * line))
        chunk_parts.append(swap(from_side, "dp", 4 * line))
    chunk_at = [chip ^ k for k in range(chips)]
    ffn_full = place(chunk_parts, chunk_at).reshape(width, 3 * quarter)
    gate_up_full = ffn_full[:, : 2 * quarter]
    down_full = ffn_full[:, 2 * quarter :]

    positions = jnp.arange(group_rows, dtype=jnp.int32)
    first_len = lax.dynamic_index_in_dim(seq_lengths[:, :, 0], group, 1, keepdims=True)
    in_second = positions[None, :] >= first_len
    places = positions[None, :] - jnp.where(in_second, first_len, 0)
    allowed = (positions[None, None, :] <= positions[None, :, None]) & (
        in_second[:, None, :] == in_second[:, :, None]
    )
    tables = rotation_tables(places.reshape(all_rows))

    def gather_rows(value):
        shaped = value.reshape(micro, tok_rows, -1)
        out = jnp.zeros((micro, group_rows, shaped.shape[-1]), value.dtype)
        for k in range(slots):
            part = swap(shaped, "expert", k) if k else shaped
            out = lax.dynamic_update_slice_in_dim(out, part, (col ^ k) * tok_rows, 1)
        return out.reshape(all_rows, -1)

    def scatter_rows(value):
        shaped = value.reshape(micro, group_rows, -1)
        total = None
        for k in range(slots):
            part = lax.dynamic_slice_in_dim(shaped, (col ^ k) * tok_rows, tok_rows, 1)
            if k:
                part = swap(part.astype(bf16), "expert", k)
            part = part.astype(f32)
            total = part if total is None else total + part
        return total.reshape(home_rows, -1)

    home_routes = lax.dynamic_slice_in_dim(ffn_routes, col * tok_rows, tok_rows, 1)
    home_slots = route_slots(home_routes, expert_table)
    packs = []
    before = jnp.tril(jnp.ones((tok_rows, tok_rows), bf16), -1)
    for k in range(slots):
        hits = jnp.any(home_slots == (col ^ k), axis=-1)
        rank = jnp.einsum("ts,ms->mt", before, hits.astype(bf16), preferred_element_type=f32)
        packs.append(
            hits[:, None, :]
            & (rank[:, None, :] == jnp.arange(cap, dtype=jnp.int32).astype(f32)[None, :, None])
        )
    packs = jnp.stack(packs)
    packs_low = packs.astype(bf16)
    pack_rows = micro * cap
    sent_rows = slots * pack_rows

    def send_packed(value):
        packed = jnp.einsum(
            "kmct,mtd->kmcd", packs_low, value.reshape(micro, tok_rows, -1), preferred_element_type=f32
        ).astype(bf16)
        parts = [swap(packed[k], "expert", k) if k else packed[k] for k in range(slots)]
        return jnp.stack(parts).reshape(sent_rows, -1)

    def quad_rows(value):
        near = swap(value, "dp", 1)
        far = swap(value, "dp", 2)
        across = swap(far, "dp", 1)
        return jnp.concatenate([value, near, far, across], axis=0)

    def quad_sum(value):
        own, near, far, across = jnp.split(value, 4, axis=0)
        far_sum = far.astype(f32) + swap(across.astype(bf16), "dp", 1).astype(f32)
        own_sum = own.astype(f32) + swap(near.astype(bf16), "dp", 1).astype(f32)
        return own_sum + swap(far_sum.astype(bf16), "dp", 2).astype(f32)

    def return_packed(value):
        shaped = value.astype(bf16).reshape(slots, micro, cap, -1)
        parts = [swap(shaped[k], "expert", k) if k else shaped[k] for k in range(slots)]
        return jnp.stack(parts)

    def unpack(packed, scale):
        total = None
        for k in range(slots):
            rows = jnp.einsum("mct,mcd->mtd", packs_low[k], packed[k], preferred_element_type=f32)
            rows = rows.reshape(home_rows, -1) * take(scale.T, col ^ k)[:, None]
            total = rows if total is None else total + rows
        return total

    grad_rows = quad_rows(send_packed(dy_home.astype(bf16)))

    gain_one = attn_gain.astype(f32)
    gain_two = ffn_gain.astype(f32)
    normed_one, scale_one = normalize(x_home)
    hidden_one_home = (normed_one * gain_one).astype(bf16)
    hidden_one = gather_rows(hidden_one_home)
    logits_one = dot(hidden_one, attn_router)
    gates_one, matches_one, chosen_one, gate_vals_one = route_gates(
        logits_one, attn_routes.reshape(all_rows, TOP), expert_table
    )
    hits_one = jnp.any(chosen_one, axis=1)
    kv_part = dot(hidden_one, kv_full).astype(bf16)
    key_rot = rotate(kv_part[:, :own_width].astype(f32), tables, False).astype(bf16)
    query_rot = rotate(dot(hidden_one, query_full), tables, False).astype(bf16)
    keys = key_rot.reshape(micro, group_rows, own_heads, HDIM)
    values = kv_part[:, own_width:].reshape(micro, group_rows, own_heads, HDIM)
    queries = query_rot.reshape(micro, group_rows, slots, own_heads, HDIM)
    raw = jnp.einsum("mrshd,mkhd->mshrk", queries, keys, preferred_element_type=f32)
    scores = jnp.where(allowed[:, None, None], raw * score_scale, very_low)
    hits_grid = hits_one.reshape(micro, group_rows, slots).transpose(0, 2, 1)
    row_peak = jnp.max(scores, axis=-1, keepdims=True)
    own_peak = jnp.max(
        jnp.where(hits_grid[:, :, None, :], row_peak[..., 0], very_low), axis=(0, 3)
    )
    expo = jnp.exp(scores - row_peak)
    probs = expo / jnp.sum(expo, axis=-1, keepdims=True)
    probs_low = probs.astype(bf16)
    attn_vals = jnp.einsum("mshrk,mkhd->mrshd", probs_low, values, preferred_element_type=f32)
    attn_vals = attn_vals.astype(bf16).reshape(all_rows, slots, own_width)
    gated_vals = (gates_one[:, :, None] * attn_vals.astype(f32)).astype(bf16)
    gated_vals = gated_vals.reshape(all_rows, query_width)
    attn_home = scatter_rows(dot_t(gated_vals, out_full))

    resid = x_home + attn_home
    normed_two, scale_two = normalize(resid)
    hidden_two = (normed_two * gain_two).astype(bf16)
    logits_two = dot(hidden_two, ffn_router)
    gates_two, matches_two, chosen_two, gate_vals_two = route_gates(
        logits_two, home_routes.reshape(home_rows, TOP), expert_table
    )
    hidden_rows = quad_rows(send_packed(hidden_two))
    gates_by_slot = gates_two.reshape(micro, tok_rows, slots)
    gate_parts = []
    for k in range(slots):
        gate_col = lax.dynamic_index_in_dim(gates_by_slot, col ^ k, 2, keepdims=False)
        part = jnp.sum(jnp.where(packs[k], gate_col[:, None, :], 0.0), axis=-1).reshape(pack_rows)
        gate_parts.append(swap(part, "expert", k) if k else part)
    gate_rows = quad_rows(jnp.concatenate(gate_parts))

    joint = dot(hidden_rows, gate_up_full)
    gate_pre, up_pre = joint[:, :quarter], joint[:, quarter:]
    sigma = jax.nn.sigmoid(gate_pre)
    silu_vals = gate_pre * sigma
    active = (silu_vals * up_pre).astype(bf16)
    active_grad = dot(grad_rows, down_full)
    gate_grad = active_grad * up_pre * sigma * (1.0 + gate_pre * (1.0 - sigma))
    joint_grad = jnp.concatenate([gate_grad, active_grad * silu_vals], axis=1).astype(bf16)
    slot_part_two = jnp.sum(active.astype(f32) * active_grad, axis=-1, keepdims=True)
    slot_part_two = jnp.pad(slot_part_two, ((0, 0), (0, HDIM - 1))).astype(bf16)
    hidden_part = jnp.concatenate(
        [dot_t(joint_grad, gate_up_full).astype(bf16), slot_part_two], axis=1
    )
    back_packed = return_packed(quad_sum(hidden_part))
    slot_two_grad = jnp.zeros((slots, home_rows), f32)
    for k in range(slots):
        rows = jnp.sum(
            jnp.where(packs[k], back_packed[k][:, :, width].astype(f32)[:, :, None], 0.0), axis=1
        )
        slot_two_grad = lax.dynamic_update_index_in_dim(
            slot_two_grad, rows.reshape(home_rows), col ^ k, 0
        )
    hidden_two_grad = unpack(back_packed[..., :width], gates_two)
    logit_two_grad = gate_back(slot_two_grad.T, gate_vals_two, matches_two, chosen_two).astype(bf16)
    hidden_two_grad = hidden_two_grad + dot_t(logit_two_grad, ffn_router)
    router_two_grad = t_dot(logit_two_grad, hidden_two)
    gain_two_grad = jnp.sum(hidden_two_grad * normed_two, axis=0)
    resid_grad = dy_home + norm_back(hidden_two_grad * gain_two, normed_two, scale_two)

    ffn_packed = return_packed(quad_sum(dot_t(active, down_full)))
    out_home = (resid + unpack(ffn_packed, gates_two)).astype(bf16)

    resid_grad_all = gather_rows(resid_grad.astype(bf16))
    vals_grad = dot(resid_grad_all, out_full).reshape(all_rows, slots, own_width)
    slot_part_one = jnp.sum(attn_vals.astype(f32) * vals_grad, axis=-1)
    vals_grad = (gates_one[:, :, None] * vals_grad).astype(bf16)
    vals_grad = vals_grad.reshape(micro, group_rows, slots, own_heads, HDIM)
    prob_grad = jnp.einsum("mrshd,mkhd->mshrk", vals_grad, values, preferred_element_type=f32)
    inner_sum = jnp.sum(probs * prob_grad, axis=-1, keepdims=True)
    score_grad = (probs * (prob_grad - inner_sum) * score_scale).astype(bf16)
    query_rot_grad = jnp.einsum("mshrk,mkhd->mrshd", score_grad, keys, preferred_element_type=f32)
    query_grad = rotate(query_rot_grad.reshape(all_rows, query_width), tables, True).astype(bf16)
    key_rot_grad = jnp.einsum("mshrk,mrshd->mkhd", score_grad, queries, preferred_element_type=f32)
    value_grad = jnp.einsum("mshrk,mrshd->mkhd", probs_low, vals_grad, preferred_element_type=f32)
    key_grad = rotate(key_rot_grad.reshape(all_rows, own_width), tables, True)
    kv_grad = jnp.concatenate([key_grad, value_grad.reshape(all_rows, own_width)], axis=1)
    kv_grad = kv_grad.astype(bf16)
    hidden_one_part = dot_t(query_grad, query_full) + dot_t(kv_grad, kv_full)
    slot_part_one = jnp.pad(slot_part_one, ((0, 0), (0, HDIM - slots)))
    back_one = scatter_rows(
        jnp.concatenate([hidden_one_part.astype(bf16), slot_part_one.astype(bf16)], axis=1)
    )
    hidden_one_grad, slot_one_grad = back_one[:, :width], back_one[:, width : width + slots]

    def own(value):
        shaped = value.reshape((micro, group_rows) + value.shape[1:])
        part = lax.dynamic_slice_in_dim(shaped, col * tok_rows, tok_rows, 1)
        return part.reshape((home_rows,) + value.shape[1:])

    logit_one_grad = gate_back(
        slot_one_grad, own(gate_vals_one), own(matches_one), own(chosen_one)
    ).astype(bf16)
    hidden_one_grad = hidden_one_grad + dot_t(logit_one_grad, attn_router)
    router_one_grad = t_dot(logit_one_grad, hidden_one_home)
    gain_one_grad = jnp.sum(hidden_one_grad * normed_one, axis=0)
    in_home = resid_grad + norm_back(hidden_one_grad * gain_one, normed_one, scale_one)

    results = jnp.stack([out_home, in_home.astype(bf16)]).reshape(2, micro, tok_rows, width)
    results = jnp.einsum("mtr,bmtd->bmrd", deal, results, preferred_element_type=f32).astype(bf16)
    results = results.reshape(2 * micro, dp_count, piece_rows, width).transpose(1, 0, 2, 3)
    results = lax.all_to_all(results, "dp", split_axis=0, concat_axis=0, tiled=True)
    results = results.transpose(1, 0, 2, 3).reshape(2, micro, tok_rows, width)

    scaled_hidden = (hidden_rows.astype(f32) * gate_rows[:, None]).astype(bf16)
    scaled_grad = (grad_rows.astype(f32) * gate_rows[:, None]).astype(bf16)

    def chunk_grad(k):
        start = (chip ^ k) * chip_rows
        left = lax.dynamic_slice_in_dim(scaled_hidden, start, chip_rows, 1)
        right = lax.dynamic_slice_in_dim(scaled_grad, start, chip_rows, 1)
        return jnp.concatenate([t_dot(left, joint_grad), t_dot(right, active)], axis=1)

    side_grad, keep_grad = chunk_grad(1), chunk_grad(0)
    for line in range(1, lines):
        side_grad = side_grad + swap(chunk_grad(2 * line + 1).astype(bf16), "dp", 4 * line).astype(f32)
        keep_grad = keep_grad + swap(chunk_grad(2 * line).astype(bf16), "dp", 4 * line).astype(f32)
    other_grad = swap(side_grad.astype(bf16), "dp", 2)
    pair = jnp.stack([keep_grad.astype(bf16), other_grad]).reshape(2, 2, shard_rows, 3 * quarter)
    own_pair = lax.dynamic_index_in_dim(pair, core, 1, keepdims=False)
    near_pair = swap(lax.dynamic_index_in_dim(pair, 1 - core, 1, keepdims=False), "dp", 1)
    by_core = [jnp.where(core == 0, own_pair, near_pair), jnp.where(core == 0, near_pair, own_pair)]
    by_side = [[jnp.where(side == s, part[0], part[1]) for part in by_core] for s in range(2)]
    blocks = [part for row in by_side for part in row]
    gate_up_grad = jnp.concatenate(
        [b[:, :quarter] for b in blocks] + [b[:, quarter : 2 * quarter] for b in blocks], axis=1
    ).astype(f32)
    down_grad = jnp.concatenate([b[:, 2 * quarter :] for b in blocks], axis=1).astype(f32)

    def reduced(value):
        return lax.psum_scatter(value.astype(bf16), "dp", scatter_dimension=0, tiled=True)

    out_grad = slots_of(reduced(t_dot(resid_grad_all, gated_vals))).astype(f32)
    query_out = slots_of(reduced(t_dot(hidden_one, query_grad))).astype(f32)
    kv_own = reduced(t_dot(hidden_one, kv_grad))
    key_part, value_part = kv_own[:, :own_width], kv_own[:, own_width:]
    first_back = lax.ppermute(
        jnp.where(even_col, key_part, value_part), "expert", [(b, a) for a, b in first_pairs]
    )
    second_back = lax.ppermute(
        jnp.where(even_col, value_part, key_part), "expert", [(b, a) for a, b in second_pairs]
    )
    kv_out = jnp.concatenate(
        [
            jnp.where(holds_keys, first_back, second_back),
            jnp.where(holds_keys, second_back, first_back),
        ],
        axis=1,
    ).astype(f32)

    sums = lax.psum(
        jnp.concatenate(
            [gain_one_grad[None], gain_two_grad[None], router_one_grad, router_two_grad], axis=0
        ),
        ("dp", "expert"),
    )
    peaks = lax.all_gather(own_peak, "dp", axis=0)
    peaks = jnp.max(peaks, axis=0)
    peaks_all = lax.all_gather(peaks, "expert", axis=1, tiled=True)
    limit = clip_limit[0].astype(f32)
    factor = limit / jnp.maximum(peaks_all, limit)
    query_scale = jnp.repeat(jnp.sqrt(take(factor, col)), HDIM)
    query_clipped = (query_weight.astype(f32) * query_scale[None, None, :]).astype(bf16)
    full_scale = jnp.concatenate(
        [jnp.repeat(jnp.sqrt(jnp.min(factor, axis=0)), HDIM), jnp.ones((query_width,), f32)]
    )
    piece_width = kv_weight.shape[1]
    piece_scale = lax.dynamic_slice_in_dim(full_scale, col * piece_width, piece_width)
    kv_clipped = (kv_weight.astype(f32) * piece_scale[None, :]).astype(bf16)
    return (
        results[0],
        results[1],
        sums[0],
        sums[1],
        sums[2 : 2 + slots].T,
        sums[2 + slots :].T,
        query_out[None],
        out_grad[None],
        kv_out,
        gate_up_grad[None],
        down_grad[None],
        query_clipped,
        kv_clipped,
    )


def solution(mesh):
    placed = (
        P(None, ("dp", "expert"), None),
        P(None, ("dp", "expert"), None),
        P(),
        P(None, ("dp", "expert")),
        P(None, "dp", None),
        P(None, "dp", None),
        P(),
        P(),
        P(),
        P(),
        P(),
        P(),
        P("expert", "dp", None),
        P("expert", "dp", None),
        P("dp", "expert"),
        P("expert", "dp", None),
        P("expert", "dp", None),
    )
    return jax.shard_map(
        local,
        mesh=mesh,
        in_specs=placed,
        out_specs=(
            P(None, ("dp", "expert"), None),
            P(None, ("dp", "expert"), None),
            P(),
            P(),
            P(),
            P(),
            P("expert", "dp", None),
            P("expert", "dp", None),
            P("dp", "expert"),
            P("expert", "dp", None),
            P("expert", "dp", None),
            P("expert", "dp", None),
            P("dp", "expert"),
        ),
        check_vma=False,
    )
```

time: 2190 us -> 1320 us (0.60)
  waiting for transfers between devices: 1310 us -> 587 us
  matrix products: 404 us -> 279 us
  other arithmetic: 202 us -> 123 us
  starting transfers between devices: 17.1 us -> 87.4 us
    ppermute x0 -> x67, waiting for transfers between devices: none -> 555 us  [the longest x63 539 us: swap(): return lax.ppermute(value, axis, [(i, i ^ step) for i in range(count)])]
    all_gather x11 -> x3, waiting for transfers between devices: 496 us -> 0.02 us  [the longest x1 0.02 us: local(): lax.all_gather(columns_of(query_weight[0]), 'dp', axis=0, tiled=True)]
    psum x3 -> x1, waiting for transfers between devices: 400 us -> 0.01 us  [local(): lax.psum(jnp.concatenate([gain_one_grad[None], gain_two_grad[None], route...]
    unnamed x26 -> x7, waiting for transfers between devices: 384 us -> 0.12 us
    dot_general x49, matrix products: 404 us -> 279 us  [the longest x13 73.6 us: t_dot(): lax.dot_general(left, right, (((0,), (0,)), ((), ())), preferred_element_...]
    scatter-add x12 -> x0, other arithmetic: 80.5 us -> none  [the longest x2 20.3 us: local(): slot_part_one = jnp.zeros((group_rows, expert_count), jnp.float32).at[row...]
    ppermute x0 -> x67, starting transfers between devices: none -> 79 us  [the longest x63 68.7 us: swap(): return lax.ppermute(value, axis, [(i, i ^ step) for i in range(count)])]
    pmax x1 -> x0, blocking collectives: 40.9 us -> none  [local(): peaks_all = lax.pmax(peak_table, ('dp', 'expert'))]
  transfers between devices with their start and end apart: 27 -> 76, of which waited for: 18 -> 41; matrix products, arithmetic and copies ran while one was open for 26% -> 31% of each run, Pallas kernels for 0% -> 0%
where the time goes in v1:
time: 1320 us; the launch traced here: 1310 us
  waiting for transfers between devices  587 us (44%)
  matrix products  279 us (21%)
  local copies, waits for them, and re-layouts  184 us (14%)
  other arithmetic  123 us (9%)
  starting transfers between devices  87.4 us (7%)
  blocking collectives  28.3 us (2%)
  between operations  17.6 us (1%)
    ppermute x63, waiting for transfers between devices, swap(): return lax.ppermute(value, axis, [(i, i ^ step) for i in range(count)])  539 us
    dot_general x13, matrix products, t_dot(): lax.dot_general(left, right, (((0,), (0,)), ((), ())), preferred_element_...  73.6 us
    dot_general x7, matrix products, dot(): return jnp.dot(left, right, preferred_element_type=f32)  71 us
    ppermute x63, starting transfers between devices, swap(): return lax.ppermute(value, axis, [(i, i ^ step) for i in range(count)])  68.7 us
    dot_general x7, matrix products, dot_t(): lax.dot_general(left, right, (((1,), (1,)), ((), ())), preferred_element_...  63 us
  transfers between devices with their start and end apart: 76, of which 41 were waited for; matrix products, arithmetic and copies ran while one was open for 31% of the time, Pallas kernels for 0%

profile of v1, /device:TPU:8, one launch (start us, length us, event | category | flops | bytes accessed | tf_op | source)
XLA Modules:
  0.0 1307.3 jit_solution(16026178699655328132)
XLA Ops:
  38.3 11.1 collective-permute-done.6
  117.4 16.0 %collective-permute-done = bf16[2,64,2048]{2,1,0:T(8,128)(2,1)S(1)} collective-permute-done((bf16[2,64,2048]{2,1,0:T(8,128)(2,1)S(1)}, bf16[2,64,2048]{2,1,0:T(8,128)(2,1)S(1)}, u32[]{:S(2)}, u32[]{:S(2)}) %collective-permute-start) | collective-permute-done | bytes 524320 | tf_op jit(solution)/shard_map/ppermute | solution.py:33
  134.4 23.9 %collective-permute-done.1 = bf16[2,64,2048]{2,1,0:T(8,128)(2,1)S(1)} collective-permute-done((bf16[2,64,2048]{2,1,0:T(8,128)(2,1)S(1)}, bf16[2,64,2048]{2,1,0:T(8,128)(2,1)S(1)}, u32[]{:S(2)}, u32[]{:S(2)}) %collective-permute-start.1) | collective-permute-done | bytes 524320 | tf_op jit(solution)/shard_map/ppermute | solution.py:33
  158.4 12.2 collective-permute-done.2
  206.6 12.4 copy.531
  261.0 16.9 %collective-permute-done.13 = bf16[2,64,2048]{2,1,0:T(8,128)(2,1)S(1)} collective-permute-done((bf16[2,64,2048]{2,1,0:T(8,128)(2,1)S(1)}, bf16[2,64,2048]{2,1,0:T(8,128)(2,1)S(1)}, u32[]{:S(2)}, u32[]{:S(2)}) %collective-permute-start.13) | collective-permute-done | bytes 524320 | tf_op jit(solution)/shard_map/ppermute | solution.py:33
  277.9 18.3 %collective-permute-done.12 = bf16[2,64,2048]{2,1,0:T(8,128)(2,1)S(1)} collective-permute-done((bf16[2,64,2048]{2,1,0:T(8,128)(2,1)S(1)}, bf16[2,64,2048]{2,1,0:T(8,128)(2,1)S(1)}, u32[]{:S(2)}, u32[]{:S(2)}) %collective-permute-start.12) | collective-permute-done | bytes 524320 | tf_op jit(solution)/shard_map/ppermute | solution.py:33
  304.6 16.7 %collective-permute-done.31 = bf16[2,48,2048]{2,1,0:T(8,128)(2,1)S(1)} collective-permute-done((bf16[2,48,2048]{2,1,0:T(8,128)(2,1)S(1)}, bf16[2,48,2048]{2,1,0:T(8,128)(2,1)S(1)}, u32[]{:S(2)}, u32[]{:S(2)}) %collective-permute-start.31) | collective-permute-done | bytes 393248 | tf_op jit(solution)/shard_map/ppermute | solution.py:33
  328.8 15.0 %collective-permute-done.15 = bf16[2,48,2048]{2,1,0:T(8,128)(2,1)S(1)} collective-permute-done((bf16[2,48,2048]{2,1,0:T(8,128)(2,1)}, bf16[2,48,2048]{2,1,0:T(8,128)(2,1)S(1)}, u32[]{:S(2)}, u32[]{:S(2)}) %collective-permute-start.15) | collective-permute-done | bytes 393248 | tf_op jit(solution)/shard_map/ppermute | solution.py:33
  364.6 31.1 %collective-permute-done.23 = bf16[512,4224]{1,0:T(8,128)(2,1)} collective-permute-done((bf16[512,4224]{1,0:T(8,128)(2,1)}, bf16[512,4224]{1,0:T(8,128)(2,1)}, u32[]{:S(2)}, u32[]{:S(2)}) %collective-permute-start.23) | collective-permute-done | bytes 4325408 | tf_op jit(solution)/shard_map/ppermute | solution.py:33
  400.8 85.3 %collective-permute-done.24 = bf16[512,4224]{1,0:T(8,128)(2,1)} collective-permute-done((bf16[512,4224]{1,0:T(8,128)(2,1)}, bf16[512,4224]{1,0:T(8,128)(2,1)}, u32[]{:S(2)}, u32[]{:S(2)}) %collective-permute-start.24) | collective-permute-done | bytes 4325408 | tf_op jit(solution)/shard_map/ppermute | solution.py:33
  493.0 29.0 %fusion.4 = f32[1536,2816]{1,0:T(8,128)} fusion(bf16[2048,4224]{1,0:T(8,128)(2,1)} %bitcast.56, bf16[384,2048]{1,0:T(8,128)(2,1)} %copy-done.53, bf16[384,2048]{1,0:T(8,128)(2,1)} %copy-done.51, bf16[384,2048]{1,0:T(8,128)(2,1)} %copy-done.52, bf16[384,2048]{1,0:T(8,128)(2,1)S(1)} %bitcast.569), kind=kOutput, calls=%fused_computation.7 | convolution fusion | flops 17741905920 | bytes 35127296 | tf_op jit(solution)/shard_map/dot_general | solution.py:20
  522.0 22.0 %multiply_convert_fusion.3 = (bf16[1536,1408]{1,0:T(8,128)(2,1)}, bf16[1536,1408]{1,0:T(8,128)(2,1)}, bf16[1536]{0:T(1024)(128)(2,1)S(1)}, bf16[1536,1408]{1,0:T(8,128)(2,1)}) fusion(f32[1536,2816]{1,0:T(8,128)} %fusion.4, bf16[2048,4224]{1,0:T(8,128)(2,1)} %bitcast.56, bf16[384,2048]{1,0:T(8,128)(2,1)} %collective-permute-done.36, ...), kind=kOutput, calls=%fused_computation.20 | convolution fusion | flops 8922462208 | bytes 42339328 | tf_op jit(solution)/shard_map/dot_general | solution.py:20
  544.3 24.1 %fusion.14 = bf16[1536,2048]{1,0:T(8,128)(2,1)S(1)} fusion(bf16[2048,4224]{1,0:T(8,128)(2,1)} %bitcast.56, bf16[1536,1408]{1,0:T(8,128)(2,1)} %get-tuple-element.50, bf16[1536,1408]{1,0:T(8,128)(2,1)} %get-tuple-element.49), kind=kOutput, calls=%fused_computation.33 | convolution fusion | flops 17737187328 | bytes 26476544 | tf_op jit(solution)/shard_map/dot_general | solution.py:24
  593.1 12.4 copy.618
  605.7 17.3 %all-gather.1 = f32[8,4,4]{2,1,0:T(4,128)S(1)} all-gather(f32[1,4,4]{2,1,0:T(4,128)S(1)} %bitcast.623), channel_id=2, replica_groups=mesh['dp'=8,'expert'=4] {'dp'}, dimensions={0}, use_global_device_ids=true | all-gather | bytes 576 | tf_op jit(solution)/shard_map/all_gather | solution.py:476
  623.1 11.0 all-gather.2
  645.9 23.9 %collective-permute-done.42 = bf16[2,48,2176]{2,1,0:T(8,128)(2,1)} collective-permute-done((bf16[2,48,2176]{2,1,0:T(8,128)(2,1)}, bf16[2,48,2176]{2,1,0:T(8,128)(2,1)}, u32[]{:S(2)}, u32[]{:S(2)}) %collective-permute-start.42) | collective-permute-done | bytes 417824 | tf_op jit(solution)/shard_map/ppermute | solution.py:33
  692.0 17.3 %fusion.259 = (bf16[1536,2048]{1,0:T(8,128)(2,1)}, f32[1536,2048]{1,0:T(8,128)}) fusion(bf16[1536,1408]{1,0:T(8,128)(2,1)} %get-tuple-element.52, bf16[2048,4224]{1,0:T(8,128)(2,1)} %bitcast.56), kind=kOutput, calls=%fused_computation.537 | convolution fusion | flops 8861515776 | bytes 28966912 | tf_op jit(solution)/shard_map/dot_general | solution.py:24
  712.8 12.4 collective-permute-done.44
  725.3 12.0 collective-permute-done.45
  759.6 15.9 %fusion.77 = f32[2,256,4,128]{1,3,2,0:T(8,128)} fusion(f32[2,4,256,256,4]{3,2,4,1,0:T(8,128)} %fusion.54, bf16[2,256,4,4,128]{1,0,4,3,2:T(2,128)(2,1)} %convert_element_type.370, f32[2,4,256,256,4]{3,2,4,1,0:T(8,128)} %copy-done.4, f32[2,4,4,256]{3,1,2,0:T(4,128)S(1)} %copy-done.94, f32[2,4,4,256]{3,1,2,0:T(4,128)S(1)} %copy-done.71, ...), kind=kOutput, calls=%fused_computation.150 | convolution fusion | flops 564142336 | bytes 20119552 | tf_op jit(solution)/shard_map/mshrk,mrshd->mkhd/dot_general | solution.py:393
  775.6 17.9 %fusion.47 = f32[2,256,4,4,128]{1,4,2,3,0:T(8,128)} fusion(f32[2,4,256,256,4]{3,2,4,1,0:T(8,128)} %fusion.54, bf16[2,256,4,128,1]{3,1,0,2,4:T(8,128)(2,1)S(1)} %bitcast.578, f32[2,4,256,256,4]{3,2,4,1,0:T(8,128)} %copy-done.4, f32[2,4,4,256]{3,1,2,0:T(4,128)S(1)} %copy-done.94, f32[2,4,4,256]{3,1,2,0:T(4,128)S(1)} %copy-done.71, ...), kind=kOutput, calls=%fused_computation.117 | convolution fusion | flops 564142336 | bytes 21692416 | tf_op jit(solution)/shard_map/mshrk,mkhd->mrshd/dot_general | solution.py:391
  838.1 19.8 %collective-permute-done.48 = bf16[2,64,2176]{2,1,0:T(8,128)(2,1)S(1)} collective-permute-done((bf16[2,64,2176]{2,1,0:T(8,128)(2,1)S(1)}, bf16[2,64,2176]{2,1,0:T(8,128)(2,1)S(1)}, u32[]{:S(2)}, u32[]{:S(2)}) %collective-permute-start.48) | collective-permute-done | bytes 557088 | tf_op jit(solution)/shard_map/ppermute | solution.py:33
  857.9 9.5 collective-permute-done.47
  908.3 8.3 convolution_convert_fusion.2
  964.6 51.7 %collective-permute-done.64 = bf16[512,4224]{1,0:T(8,128)(2,1)} collective-permute-done((bf16[512,4224]{1,0:T(8,128)(2,1)}, bf16[512,4224]{1,0:T(8,128)(2,1)}, u32[]{:S(2)}, u32[]{:S(2)}) %collective-permute-start.64) | collective-permute-done | bytes 4325408 | tf_op jit(solution)/shard_map/ppermute | solution.py:33
  1039.8 11.3 collective-permute-done.29
  1064.4 83.2 %collective-permute-done.63 = bf16[512,4224]{1,0:T(8,128)(2,1)} collective-permute-done((bf16[512,4224]{1,0:T(8,128)(2,1)}, bf16[512,4224]{1,0:T(8,128)(2,1)}, u32[]{:S(2)}, u32[]{:S(2)}) %collective-permute-start.63) | collective-permute-done | bytes 4325408 | tf_op jit(solution)/shard_map/ppermute | solution.py:33
  1177.8 11.3 all-to-all-done.1
  1222.8 20.2 %reduce-scatter.4.cloned.1.call-done = bf16[256,2048]{1,0:T(8,128)(2,1)} async-done(((bf16[2048,2048]{1,0:T(8,128)(2,1)}), bf16[256,2048]{1,0:T(8,128)(2,1)}) %reduce-scatter.4.cloned.1.call-update) | async-done | bytes 1048592 | tf_op jit(solution)/shard_map/reduce_scatter | solution.py:450
  1271.0 17.8 %collective-permute-done.51 = bf16[256,512]{1,0:T(8,128)(2,1)S(1)} collective-permute-done((bf16[256,512]{1,0:T(8,128)(2,1)S(1)}, bf16[256,512]{1,0:T(8,128)(2,1)S(1)}, u32[]{:S(2)}, u32[]{:S(2)}) %collective-permute-start.51) | collective-permute-done | bytes 262176 | tf_op jit(solution)/shard_map/ppermute | solution.py:33
  (772 shorter events, 582.4 us)
Async XLA Ops:
  7.2 189.1 %all-gather.7.cloned.1.call-start = ((), (), s32[]{:S(2)}) async-start(), calls=%async_computation.5 | async-start | bytes 4718592 | tf_op jit(solution)/shard_map/all_gather | solution.py:193
  24.0 182.6 %all-gather.9.cloned.1.call-start = ((), (), s32[]{:S(2)}) async-start(), calls=%async_computation.6 | async-start | bytes 9437184 | tf_op jit(solution)/shard_map/all_gather | solution.py:194
  58.4 50.1 %all-to-all-start = ((bf16[8,4,8,2048]{3,2,1,0:T(8,128)(2,1)}), bf16[8,4,8,2048]{3,2,1,0:T(8,128)(2,1)S(1)}, u32[]{:S(2)}, u32[]{:S(2)}) async-start(bf16[8,4,8,2048]{3,2,1,0:T(8,128)(2,1)} %copy.519), calls=%async_computation | async-start | bytes 2097152 | tf_op jit(solution)/shard_map/all_to_all | solution.py:147
  62.2 184.8 %all-gather.11.cloned.1.call-start = ((), (), s32[]{:S(2)}) async-start(), calls=%async_computation.7 | async-start | bytes 9437184 | tf_op jit(solution)/shard_map/all_gather | solution.py:195
  80.2 112.4 %collective-permute-start.20 = (bf16[256,4224]{1,0:T(8,128)(2,1)}, bf16[256,4224]{1,0:T(8,128)(2,1)}, u32[]{:S(2)}, u32[]{:S(2)}) collective-permute-start(bf16[256,4224]{1,0:T(8,128)(2,1)} %pad_maximum_fusion.8), channel_id=1, source_target_pairs={{0,4},{4,0},{8,12},{12,8},{16,20},{20,16},{24,28},{28,24},{1,5},{5... | collective-permute-start | bytes 6488072 | tf_op jit(solution)/shard_map/ppermute | solution.py:33
  81.8 104.4 %collective-permute-start.21 = (bf16[256,4224]{1,0:T(8,128)(2,1)}, bf16[256,4224]{1,0:T(8,128)(2,1)}, u32[]{:S(2)}, u32[]{:S(2)}) collective-permute-start(bf16[256,4224]{1,0:T(8,128)(2,1)} %pad_maximum_fusion.10), channel_id=1, source_target_pairs={{0,4},{4,0},{8,12},{12,8},{16,20},{20,16},{24,28},{28,24},{1,5},{5... | collective-permute-start | bytes 6488072 | tf_op jit(solution)/shard_map/ppermute | solution.py:33
  96.5 1078.3 %all-reduce.5.cloned.1.call-start = ((), (), s32[]{:S(2)}) async-start(), calls=%async_computation.8 | async-start | bytes 262144 | tf_op jit(solution)/shard_map/psum | solution.py:470
  112.1 46.2 %collective-permute-start.1 = (bf16[2,64,2048]{2,1,0:T(8,128)(2,1)S(1)}, bf16[2,64,2048]{2,1,0:T(8,128)(2,1)S(1)}, u32[]{:S(2)}, u32[]{:S(2)}) collective-permute-start(bf16[2,64,2048]{2,1,0:T(8,128)(2,1)S(1)} %get-tuple-element.48), channel_id=1, source_target_pairs={{0,2},{1,3},{2,0},{3,1},{4,6},{5,7},{6,4},{7,5},{8,10},{9,11},{10,... | collective-permute-start | bytes 1572872 | tf_op jit(solution)/shard_map/ppermute | solution.py:33
  115.1 55.5 %collective-permute-start.2 = (bf16[2,64,2048]{2,1,0:T(8,128)(2,1)S(1)}, bf16[2,64,2048]{2,1,0:T(8,128)(2,1)S(1)}, u32[]{:S(2)}, u32[]{:S(2)}) collective-permute-start(bf16[2,64,2048]{2,1,0:T(8,128)(2,1)S(1)} %get-tuple-element.48), channel_id=1, source_target_pairs={{0,3},{1,2},{2,1},{3,0},{4,7},{5,6},{6,5},{7,4},{8,11},{9,10},{10,... | collective-permute-start | bytes 1572872 | tf_op jit(solution)/shard_map/ppermute | solution.py:33
  133.3 170.0 %collective-permute-start.33 = (bf16[2,48,2048]{2,1,0:T(8,128)(2,1)}, bf16[2,48,2048]{2,1,0:T(8,128)(2,1)}, u32[]{:S(2)}, u32[]{:S(2)}) collective-permute-start(bf16[2,48,2048]{2,1,0:T(8,128)(2,1)} %get-tuple-element.114), channel_id=1, source_target_pairs={{0,3},{1,2},{2,1},{3,0},{4,7},{5,6},{6,5},{7,4},{8,11},{9,10},{10,... | collective-permute-start | bytes 1179656 | tf_op jit(solution)/shard_map/ppermute | solution.py:33
  190.9 132.0 %collective-permute-start.22 = (bf16[512,4224]{1,0:T(8,128)(2,1)}, bf16[512,4224]{1,0:T(8,128)(2,1)}, u32[]{:S(2)}, u32[]{:S(2)}) collective-permute-start(bf16[512,4224]{1,0:T(8,128)(2,1)} %pad_maximum_fusion.4), channel_id=1, source_target_pairs={{0,8},{4,12},{8,0},{12,4},{16,24},{20,28},{24,16},{28,20},{1,9},{5... | collective-permute-start | bytes 12976136 | tf_op jit(solution)/shard_map/ppermute | solution.py:33
  256.6 39.6 %collective-permute-start.12 = (bf16[2,64,2048]{2,1,0:T(8,128)(2,1)S(1)}, bf16[2,64,2048]{2,1,0:T(8,128)(2,1)S(1)}, u32[]{:S(2)}, u32[]{:S(2)}) collective-permute-start(bf16[2,64,2048]{2,1,0:T(8,128)(2,1)S(1)} %get-tuple-element.84), channel_id=1, source_target_pairs={{0,2},{1,3},{2,0},{3,1},{4,6},{5,7},{6,4},{7,5},{8,10},{9,11},{10,... | collective-permute-start | bytes 1572872 | tf_op jit(solution)/shard_map/ppermute | solution.py:33
  256.6 42.4 %collective-permute-start.11 = (bf16[2,64,2048]{2,1,0:T(8,128)(2,1)S(1)}, bf16[2,64,2048]{2,1,0:T(8,128)(2,1)S(1)}, u32[]{:S(2)}, u32[]{:S(2)}) collective-permute-start(bf16[2,64,2048]{2,1,0:T(8,128)(2,1)S(1)} %get-tuple-element.82), channel_id=1, source_target_pairs={{0,1},{1,0},{2,3},{3,2},{4,5},{5,4},{6,7},{7,6},{8,9},{9,8},{10,11... | collective-permute-start | bytes 1572872 | tf_op jit(solution)/shard_map/ppermute | solution.py:33
  299.0 96.6 %collective-permute-start.23 = (bf16[512,4224]{1,0:T(8,128)(2,1)}, bf16[512,4224]{1,0:T(8,128)(2,1)}, u32[]{:S(2)}, u32[]{:S(2)}) collective-permute-start(bf16[512,4224]{1,0:T(8,128)(2,1)} %pad_maximum_fusion.3), channel_id=1, source_target_pairs={{0,16},{4,20},{8,24},{12,28},{16,0},{20,4},{24,8},{28,12},{1,17},{... | collective-permute-start | bytes 12976136 | tf_op jit(solution)/shard_map/ppermute | solution.py:33
  322.9 163.2 %collective-permute-start.24 = (bf16[512,4224]{1,0:T(8,128)(2,1)}, bf16[512,4224]{1,0:T(8,128)(2,1)}, u32[]{:S(2)}, u32[]{:S(2)}) collective-permute-start(bf16[512,4224]{1,0:T(8,128)(2,1)} %collective-permute-done.22), channel_id=1, source_target_pairs={{0,16},{4,20},{8,24},{12,28},{16,0},{20,4},{24,8},{28,12},{1,17},{... | collective-permute-start | bytes 12976136 | tf_op jit(solution)/shard_map/ppermute | solution.py:33
  343.8 178.2 %collective-permute-start.34 = (bf16[384,2048]{1,0:T(8,128)(2,1)S(1)}, bf16[384,2048]{1,0:T(8,128)(2,1)}, u32[]{:S(2)}, u32[]{:S(2)}) collective-permute-start(bf16[384,2048]{1,0:T(8,128)(2,1)S(1)} %bitcast.564), channel_id=1, source_target_pairs={{0,4},{4,0},{8,12},{12,8},{16,20},{20,16},{24,28},{28,24},{1,5},{5... | collective-permute-start | bytes 4718600 | tf_op jit(solution)/shard_map/ppermute | solution.py:33
  347.4 48.2 %collective-permute-start.18 = (bf16[384,2048]{1,0:T(8,128)(2,1)S(1)}, bf16[384,2048]{1,0:T(8,128)(2,1)S(1)}, u32[]{:S(2)}, u32[]{:S(2)}) collective-permute-start(bf16[384,2048]{1,0:T(8,128)(2,1)S(1)} %bitcast.567), channel_id=1, source_target_pairs={{0,8},{4,12},{8,0},{12,4},{16,24},{20,28},{24,16},{28,20},{1,9},{5... | collective-permute-start | bytes 4718600 | tf_op jit(solution)/shard_map/ppermute | solution.py:33
  359.9 162.0 %collective-permute-start.36 = (bf16[384,2048]{1,0:T(8,128)(2,1)}, bf16[384,2048]{1,0:T(8,128)(2,1)}, u32[]{:S(2)}, u32[]{:S(2)}) collective-permute-start(bf16[384,2048]{1,0:T(8,128)(2,1)} %collective-permute-done.35), channel_id=1, source_target_pairs={{0,4},{4,0},{8,12},{12,8},{16,20},{20,16},{24,28},{28,24},{1,5},{5... | collective-permute-start | bytes 4718600 | tf_op jit(solution)/shard_map/ppermute | solution.py:33
  395.6 95.0 %collective-permute-start.17 = (bf16[384,2048]{1,0:T(8,128)(2,1)S(1)}, bf16[384,2048]{1,0:T(8,128)(2,1)S(1)}, u32[]{:S(2)}, u32[]{:S(2)}) collective-permute-start(bf16[384,2048]{1,0:T(8,128)(2,1)S(1)} %bitcast.568), channel_id=1, source_target_pairs={{0,4},{4,0},{8,12},{12,8},{16,20},{20,16},{24,28},{28,24},{1,5},{5... | collective-permute-start | bytes 4718600 | tf_op jit(solution)/shard_map/ppermute | solution.py:33
  395.7 95.0 %collective-permute-start.19 = (bf16[384,2048]{1,0:T(8,128)(2,1)S(1)}, bf16[384,2048]{1,0:T(8,128)(2,1)S(1)}, u32[]{:S(2)}, u32[]{:S(2)}) collective-permute-start(bf16[384,2048]{1,0:T(8,128)(2,1)S(1)} %collective-permute-done.18), channel_id=1, source_target_pairs={{0,4},{4,0},{8,12},{12,8},{16,20},{20,16},{24,28},{28,24},{1,5},{5... | collective-permute-start | bytes 4718600 | tf_op jit(solution)/shard_map/ppermute | solution.py:33
  576.4 59.1 %collective-permute-start.37 = (bf16[384,2176]{1,0:T(8,128)(2,1)}, bf16[384,2176]{1,0:T(8,128)(2,1)}, u32[]{:S(2)}, u32[]{:S(2)}) collective-permute-start(bf16[384,2176]{1,0:T(8,128)(2,1)} %get-tuple-element.55), channel_id=1, source_target_pairs={{0,4},{4,0},{8,12},{12,8},{16,20},{20,16},{24,28},{28,24},{1,5},{5... | collective-permute-start | bytes 5013512 | tf_op jit(solution)/shard_map/ppermute | solution.py:33
  580.2 55.2 %collective-permute-start.39 = (bf16[384,2176]{1,0:T(8,128)(2,1)}, bf16[384,2176]{1,0:T(8,128)(2,1)}, u32[]{:S(2)}, u32[]{:S(2)}) collective-permute-start(bf16[384,2176]{1,0:T(8,128)(2,1)} %add_convert_fusion.2), channel_id=1, source_target_pairs={{0,8},{4,12},{8,0},{12,4},{16,24},{20,28},{24,16},{28,20},{1,9},{5... | collective-permute-start | bytes 5013512 | tf_op jit(solution)/shard_map/ppermute | solution.py:33
  837.9 51.7 %collective-permute-start.26 = (bf16[384,2048]{1,0:T(8,128)(2,1)}, bf16[384,2048]{1,0:T(8,128)(2,1)}, u32[]{:S(2)}, u32[]{:S(2)}) collective-permute-start(bf16[384,2048]{1,0:T(8,128)(2,1)} %get-tuple-element.58), channel_id=1, source_target_pairs={{0,4},{4,0},{8,12},{12,8},{16,20},{20,16},{24,28},{28,24},{1,5},{5... | collective-permute-start | bytes 4718600 | tf_op jit(solution)/shard_map/ppermute | solution.py:33
  871.0 318.3 %reduce-scatter.8.cloned.1.call-start = ((), (), s32[]{:S(2)}) async-start(), calls=%async_computation.11 | async-start | bytes 4718592 | tf_op jit(solution)/shard_map/reduce_scatter | solution.py:450
  877.3 343.6 %reduce-scatter.6.cloned.1.call-start = ((), (), s32[]{:S(2)}) async-start(), calls=%async_computation.10 | async-start | bytes 9437184 | tf_op jit(solution)/shard_map/reduce_scatter | solution.py:450
  887.2 40.6 %collective-permute-start.25 = (bf16[384,2048]{1,0:T(8,128)(2,1)}, bf16[384,2048]{1,0:T(8,128)(2,1)}, u32[]{:S(2)}, u32[]{:S(2)}) collective-permute-start(bf16[384,2048]{1,0:T(8,128)(2,1)} %get-tuple-element.57), channel_id=1, source_target_pairs={{0,4},{4,0},{8,12},{12,8},{16,20},{20,16},{24,28},{28,24},{1,5},{5... | collective-permute-start | bytes 4718600 | tf_op jit(solution)/shard_map/ppermute | solution.py:33
  919.1 97.1 %collective-permute-start.64 = (bf16[512,4224]{1,0:T(8,128)(2,1)}, bf16[512,4224]{1,0:T(8,128)(2,1)}, u32[]{:S(2)}, u32[]{:S(2)}) collective-permute-start(bf16[512,4224]{1,0:T(8,128)(2,1)} %pad_maximum_fusion.6), channel_id=1, source_target_pairs={{0,16},{4,20},{8,24},{12,28},{16,0},{20,4},{24,8},{28,12},{1,17},{... | collective-permute-start | bytes 12976136 | tf_op jit(solution)/shard_map/ppermute | solution.py:33
  927.6 315.5 %reduce-scatter.4.cloned.1.call-start = ((), (), s32[]{:S(2)}) async-start(), calls=%async_computation.9 | async-start | bytes 9437184 | tf_op jit(solution)/shard_map/reduce_scatter | solution.py:450
  935.9 99.3 %collective-permute-start.30 = (bf16[2,48,2048]{2,1,0:T(8,128)(2,1)}, bf16[2,48,2048]{2,1,0:T(8,128)(2,1)}, u32[]{:S(2)}, u32[]{:S(2)}) collective-permute-start(bf16[2,48,2048]{2,1,0:T(8,128)(2,1)} %bitcast.62), channel_id=1, source_target_pairs={{0,3},{1,2},{2,1},{3,0},{4,7},{5,6},{6,5},{7,4},{8,11},{9,10},{10,... | collective-permute-start | bytes 1179656 | tf_op jit(solution)/shard_map/ppermute | solution.py:33
  952.2 195.3 %collective-permute-start.63 = (bf16[512,4224]{1,0:T(8,128)(2,1)}, bf16[512,4224]{1,0:T(8,128)(2,1)}, u32[]{:S(2)}, u32[]{:S(2)}) collective-permute-start(bf16[512,4224]{1,0:T(8,128)(2,1)} %pad_maximum_fusion.5), channel_id=1, source_target_pairs={{0,16},{4,20},{8,24},{12,28},{16,0},{20,4},{24,8},{28,12},{1,17},{... | collective-permute-start | bytes 12976136 | tf_op jit(solution)/shard_map/ppermute | solution.py:33
  1020.4 133.7 %collective-permute-start.65 = (bf16[512,4224]{1,0:T(8,128)(2,1)}, bf16[512,4224]{1,0:T(8,128)(2,1)}, u32[]{:S(2)}, u32[]{:S(2)}) collective-permute-start(bf16[512,4224]{1,0:T(8,128)(2,1)} %fusion.7), channel_id=1, source_target_pairs={{0,8},{4,12},{8,0},{12,4},{16,24},{20,28},{24,16},{28,20},{1,9},{5... | collective-permute-start | bytes 12976136 | tf_op jit(solution)/shard_map/ppermute | solution.py:33
  1158.4 46.1 %collective-permute-start.66 = (bf16[2,256,4224]{2,1,0:T(8,128)(2,1)}, bf16[2,256,4224]{2,1,0:T(8,128)(2,1)}, u32[]{:S(2)}, u32[]{:S(2)}) collective-permute-start(bf16[2,256,4224]{2,1,0:T(8,128)(2,1)} %fusion.27), channel_id=1, source_target_pairs={{0,4},{4,0},{8,12},{12,8},{16,20},{20,16},{24,28},{28,24},{1,5},{5... | collective-permute-start | bytes 12976136 | tf_op jit(solution)/shard_map/ppermute | solution.py:33
  (209 other events, 3994.2 us)
Sparse Core Ops, SparseCore 0:
  24.1 38.6 all-gather.6
  64.7 54.4 all-gather.8
  121.1 54.3 all-gather.10
  871.1 128.4 all-reduce.4
  1002.8 67.3 reduce-scatter.7
  1074.0 93.8 reduce-scatter.5
  1171.3 71.7 reduce-scatter.3

commit v2 on v1

--- a/solution.py
+++ b/solution.py
@@ -1,6 +1,8 @@
 import jax
 import jax.numpy as jnp
 from jax import lax
+from jax.experimental import pallas as pl
+from jax.experimental.pallas import tpu as pltpu
 from jax.sharding import PartitionSpec as P
 
 HEADS = 16
@@ -44,28 +46,194 @@
     return out
 
 
+def after(value, *others):
+    return lax.optimization_barrier((value, *others))[0]
+
+
+def spread(value, combine):
+    for axis in ("expert", "dp"):
+        step = 1
+        while step < lax.axis_size(axis):
+            value = combine(value, swap(value, axis, step))
+            step *= 2
+    return value
+
+
 def rotation_tables(places):
     half_dim = HDIM // 2
     frequency = rope_base ** (-jnp.arange(half_dim, dtype=f32) * 2.0 / HDIM)
-    angles = places.astype(f32)[..., None] * frequency
-    return jnp.cos(angles), jnp.sin(angles)
-
-
-def rotate(values, tables, inverse):
-    cosine, sine = tables
-    if inverse:
-        sine = -sine
-    rows = values.shape[0]
-    half_dim = HDIM // 2
-    shaped = values.reshape(rows, -1, HDIM)
-    first_half = shaped[..., :half_dim]
-    second_half = shaped[..., half_dim:]
-    cosine, sine = cosine[:, None, :], sine[:, None, :]
-    rotated = jnp.concatenate(
-        [first_half * cosine - second_half * sine, second_half * cosine + first_half * sine],
-        axis=-1,
-    )
-    return rotated.reshape(rows, -1)
+    angles = places.astype(f32)[:, None] * frequency[None, :]
+    cosine, sine = jnp.cos(angles), jnp.sin(angles)
+    return (
+        jnp.concatenate([cosine, cosine], axis=1),
+        jnp.concatenate([-sine, sine], axis=1),
+    )
+
+
+def turn(values, cosine, sine):
+    return values * cosine + pltpu.roll(values, HDIM // 2, 1) * sine
+
+
+def lane_value(table, lane):
+    lanes = lax.broadcasted_iota(jnp.int32, table.shape, 1)
+    return jnp.sum(jnp.where(lanes == lane, table, 0.0), axis=1, keepdims=True)
+
+
+def allowed_pairs(rows, first_len):
+    query_at = lax.broadcasted_iota(jnp.int32, (rows, rows), 0)
+    key_at = lax.broadcasted_iota(jnp.int32, (rows, rows), 1)
+    return (key_at <= query_at) & ((key_at >= first_len) | (query_at < first_len))
+
+
+def forward_kernel(
+    lens, query, key, value, cosine, sine, gates, hits,
+    vals_out, gated_out, query_out, key_out, total_out, peak_out,
+):
+    m, h, s = pl.program_id(0), pl.program_id(1), pl.program_id(2)
+    slot_count = pl.num_programs(2)
+    rows = query.shape[0]
+    lane = h * slot_count + s
+
+    @pl.when(lane == 0)
+    def _():
+        total_out[...] = jnp.zeros_like(total_out)
+        peak_out[...] = jnp.full_like(peak_out, very_low)
+
+    @pl.when(s == 0)
+    def _():
+        key_out[...] = turn(key[...].astype(f32), cosine[...], sine[...]).astype(bf16)
+
+    turned = turn(query[...], cosine[...], sine[...]).astype(bf16)
+    query_out[...] = turned
+    raw = dot_t(turned, key_out[...])
+    scores = jnp.where(allowed_pairs(rows, lens[m]), raw * HDIM ** (-0.5), very_low)
+    row_peak = jnp.max(scores, axis=1, keepdims=True)
+    expo = jnp.exp(scores - row_peak)
+    denom = jnp.sum(expo, axis=1, keepdims=True)
+    probs = expo / denom
+    vals = dot(probs.astype(bf16), value[...]).astype(bf16)
+    vals_out[...] = vals
+    gated_out[...] = (lane_value(gates[...], s) * vals.astype(f32)).astype(bf16)
+    lanes = lax.broadcasted_iota(jnp.int32, total_out.shape, 1)
+    total_out[...] = jnp.where(lanes == lane, row_peak + jnp.log(denom), total_out[...])
+    seen = jnp.where(lane_value(hits[...], s) > 0.0, row_peak, very_low)
+    peak_lanes = lax.broadcasted_iota(jnp.int32, peak_out.shape, 1)
+    peak_out[...] = jnp.where(
+        peak_lanes == lane, jnp.max(seen, axis=0, keepdims=True), peak_out[...]
+    )
+
+
+def backward_kernel(
+    lens, query, key, value, vals, vals_grad, cosine, sine, gates, total,
+    query_grad, key_grad, value_grad, gate_grad, key_sum, value_sum,
+):
+    m, h, s = pl.program_id(0), pl.program_id(1), pl.program_id(2)
+    slot_count = pl.num_programs(2)
+    rows = query.shape[0]
+    lane = h * slot_count + s
+
+    @pl.when(lane == 0)
+    def _():
+        gate_grad[...] = jnp.zeros_like(gate_grad)
+
+    @pl.when(s == 0)
+    def _():
+        key_sum[...] = jnp.zeros_like(key_sum)
+        value_sum[...] = jnp.zeros_like(value_sum)
+
+    full_grad = vals_grad[...]
+    lanes = lax.broadcasted_iota(jnp.int32, gate_grad.shape, 1)
+    slot_sum = jnp.sum(vals[...].astype(f32) * full_grad, axis=1, keepdims=True)
+    gate_grad[...] += jnp.where(lanes == s, slot_sum, 0.0)
+    gated_grad = (lane_value(gates[...], s) * full_grad).astype(bf16)
+    raw = dot_t(query[...], key[...])
+    scores = jnp.where(allowed_pairs(rows, lens[m]), raw * HDIM ** (-0.5), very_low)
+    probs = jnp.exp(scores - lane_value(total[...], lane))
+    prob_grad = dot_t(gated_grad, value[...])
+    inner = jnp.sum(probs * prob_grad, axis=1, keepdims=True)
+    score_grad = (probs * (prob_grad - inner) * HDIM ** (-0.5)).astype(bf16)
+    back_sine = -sine[...]
+    turned = dot(score_grad, key[...])
+    query_grad[...] = turn(turned, cosine[...], back_sine).astype(bf16)
+    key_sum[...] += t_dot(score_grad, query[...])
+    value_sum[...] += t_dot(probs.astype(bf16), gated_grad)
+
+    @pl.when(s == slot_count - 1)
+    def _():
+        key_grad[...] = turn(key_sum[...], cosine[...], back_sine).astype(bf16)
+        value_grad[...] = value_sum[...].astype(bf16)
+
+
+def attention_specs(own_heads, rows):
+    def block(index):
+        return pl.BlockSpec((rows, HDIM), index)
+
+    return {
+        "query": block(lambda m, h, s, lens: (m, s * own_heads + h)),
+        "key": block(lambda m, h, s, lens: (m, h)),
+        "value": block(lambda m, h, s, lens: (m, own_heads + h)),
+        "rows": block(lambda m, h, s, lens: (m, 0)),
+        "peak": pl.BlockSpec((8, HDIM), lambda m, h, s, lens: (m, 0)),
+    }
+
+
+def attention_forward(lens, query, joint_kv, tables, gates, hits, own_heads, rows):
+    micro = lens.shape[0]
+    slots = query.shape[1] // (own_heads * HDIM)
+    at = attention_specs(own_heads, rows)
+    shape = jax.ShapeDtypeStruct
+    total_rows = micro * rows
+    return pl.pallas_call(
+        forward_kernel,
+        grid_spec=pltpu.PrefetchScalarGridSpec(
+            num_scalar_prefetch=1,
+            grid=(micro, own_heads, slots),
+            in_specs=[at["query"], at["key"], at["value"]] + [at["rows"]] * 4,
+            out_specs=[at["query"]] * 3 + [at["key"], at["rows"], at["peak"]],
+        ),
+        out_shape=[shape(query.shape, bf16)] * 3
+        + [
+            shape((total_rows, own_heads * HDIM), bf16),
+            shape((total_rows, HDIM), f32),
+            shape((micro * 8, HDIM), f32),
+        ],
+        cost_estimate=pl.CostEstimate(
+            flops=4 * rows * rows * HDIM * micro * HEADS,
+            bytes_accessed=14 * query.size,
+            transcendentals=rows * rows * micro * HEADS,
+        ),
+        name="attention_forward",
+    )(lens, query, joint_kv, joint_kv, tables[0], tables[1], gates, hits)
+
+
+def attention_backward(
+    lens, query, key, joint_kv, vals, vals_grad, tables, gates, total, own_heads, rows
+):
+    micro = lens.shape[0]
+    slots = query.shape[1] // (own_heads * HDIM)
+    at = attention_specs(own_heads, rows)
+    shape = jax.ShapeDtypeStruct
+    total_rows = micro * rows
+    return pl.pallas_call(
+        backward_kernel,
+        grid_spec=pltpu.PrefetchScalarGridSpec(
+            num_scalar_prefetch=1,
+            grid=(micro, own_heads, slots),
+            in_specs=[at["query"], at["key"], at["value"], at["query"], at["query"]]
+            + [at["rows"]] * 4,
+            out_specs=[at["query"], at["key"], at["key"], at["rows"]],
+            scratch_shapes=[pltpu.VMEM((rows, HDIM), f32)] * 2,
+        ),
+        out_shape=[shape(query.shape, bf16)]
+        + [shape((total_rows, own_heads * HDIM), bf16)] * 2
+        + [shape((total_rows, HDIM), f32)],
+        cost_estimate=pl.CostEstimate(
+            flops=10 * rows * rows * HDIM * micro * HEADS,
+            bytes_accessed=14 * query.size,
+            transcendentals=rows * rows * micro * HEADS,
+        ),
+        name="attention_backward",
+    )(lens, query, key, joint_kv, vals, vals_grad, tables[0], tables[1], gates, total)
 
 
 def normalize(values):
@@ -196,27 +364,39 @@
 
     def quarter_of(half, part):
         start = (2 * half + part) * quarter
+        return [
+            lax.dynamic_slice_in_dim(gate_up_weight[0], start, quarter, 1),
+            lax.dynamic_slice_in_dim(gate_up_weight[0], FF + start, quarter, 1),
+            lax.dynamic_slice_in_dim(down_weight[0], start, quarter, 1),
+        ]
+
+    def half_of(half):
+        return jnp.concatenate(quarter_of(half, 0) + quarter_of(half, 1), axis=1)
+
+    def part_of(piece, part):
+        return lax.dynamic_slice_in_dim(piece, part * 3 * quarter, 3 * quarter, 1)
+
+    keep_side = half_of(side)
+    from_side = swap(half_of(1 - side), "dp", 2)
+    keep_lines = [swap(keep_side, "dp", 4 * line) for line in range(1, lines)]
+    from_lines = []
+    for line in range(1, lines):
+        other_part = swap(part_of(from_side, 1 - core), "dp", 4 * line)
+        from_lines.append((swap(part_of(from_side, core), "dp", 4 * line), other_part))
+
+    def pair_rows(own, other):
+        near = swap(other, "dp", 1)
         return jnp.concatenate(
-            [
-                lax.dynamic_slice_in_dim(gate_up_weight[0], start, quarter, 1),
-                lax.dynamic_slice_in_dim(gate_up_weight[0], FF + start, quarter, 1),
-                lax.dynamic_slice_in_dim(down_weight[0], start, quarter, 1),
-            ],
-            axis=1,
+            [jnp.where(core == 0, own, near), jnp.where(core == 0, near, own)], axis=0
         )
 
-    def pair_rows(own, other):
-        return jnp.concatenate(
-            [jnp.where(core == 0, own, other), jnp.where(core == 0, other, own)], axis=0
-        )
-
-    keep_side = pair_rows(quarter_of(side, core), swap(quarter_of(side, 1 - core), "dp", 1))
-    send_side = pair_rows(quarter_of(1 - side, core), swap(quarter_of(1 - side, 1 - core), "dp", 1))
-    from_side = swap(send_side, "dp", 2)
-    chunk_parts = [keep_side, from_side]
+    chunk_parts = [
+        pair_rows(part_of(piece, core), part_of(piece, 1 - core)) for piece in (keep_side, from_side)
+    ]
     for line in range(1, lines):
-        chunk_parts.append(swap(keep_side, "dp", 4 * line))
-        chunk_parts.append(swap(from_side, "dp", 4 * line))
+        piece = keep_lines[line - 1]
+        chunk_parts.append(pair_rows(part_of(piece, core), part_of(piece, 1 - core)))
+        chunk_parts.append(pair_rows(*from_lines[line - 1]))
     chunk_at = [chip ^ k for k in range(chips)]
     ffn_full = place(chunk_parts, chunk_at).reshape(width, 3 * quarter)
     gate_up_full = ffn_full[:, : 2 * quarter]
@@ -226,9 +406,6 @@
     first_len = lax.dynamic_index_in_dim(seq_lengths[:, :, 0], group, 1, keepdims=True)
     in_second = positions[None, :] >= first_len
     places = positions[None, :] - jnp.where(in_second, first_len, 0)
-    allowed = (positions[None, None, :] <= positions[None, :, None]) & (
-        in_second[:, None, :] == in_second[:, :, None]
-    )
     tables = rotation_tables(places.reshape(all_rows))
 
     def gather_rows(value):
@@ -298,7 +475,8 @@
             total = rows if total is None else total + rows
         return total
 
-    grad_rows = quad_rows(send_packed(dy_home.astype(bf16)))
+    grad_sent = send_packed(dy_home.astype(bf16))
+    grad_rows = quad_rows(grad_sent)
 
     gain_one = attn_gain.astype(f32)
     gain_two = ffn_gain.astype(f32)
@@ -309,27 +487,24 @@
     gates_one, matches_one, chosen_one, gate_vals_one = route_gates(
         logits_one, attn_routes.reshape(all_rows, TOP), expert_table
     )
-    hits_one = jnp.any(chosen_one, axis=1)
+    hits_one = jnp.any(chosen_one, axis=1).astype(f32)
+
+    def wide(value):
+        return jnp.pad(value, ((0, 0), (0, HDIM - value.shape[1])))
+
     kv_part = dot(hidden_one, kv_full).astype(bf16)
-    key_rot = rotate(kv_part[:, :own_width].astype(f32), tables, False).astype(bf16)
-    query_rot = rotate(dot(hidden_one, query_full), tables, False).astype(bf16)
-    keys = key_rot.reshape(micro, group_rows, own_heads, HDIM)
-    values = kv_part[:, own_width:].reshape(micro, group_rows, own_heads, HDIM)
-    queries = query_rot.reshape(micro, group_rows, slots, own_heads, HDIM)
-    raw = jnp.einsum("mrshd,mkhd->mshrk", queries, keys, preferred_element_type=f32)
-    scores = jnp.where(allowed[:, None, None], raw * score_scale, very_low)
-    hits_grid = hits_one.reshape(micro, group_rows, slots).transpose(0, 2, 1)
-    row_peak = jnp.max(scores, axis=-1, keepdims=True)
-    own_peak = jnp.max(
-        jnp.where(hits_grid[:, :, None, :], row_peak[..., 0], very_low), axis=(0, 3)
-    )
-    expo = jnp.exp(scores - row_peak)
-    probs = expo / jnp.sum(expo, axis=-1, keepdims=True)
-    probs_low = probs.astype(bf16)
-    attn_vals = jnp.einsum("mshrk,mkhd->mrshd", probs_low, values, preferred_element_type=f32)
-    attn_vals = attn_vals.astype(bf16).reshape(all_rows, slots, own_width)
-    gated_vals = (gates_one[:, :, None] * attn_vals.astype(f32)).astype(bf16)
-    gated_vals = gated_vals.reshape(all_rows, query_width)
+    query_part = dot(after(hidden_one, from_side, *keep_lines), query_full)
+    lens = first_len[:, 0].astype(jnp.int32)
+    gates_wide = wide(gates_one)
+    attn_vals, gated_vals, query_rot, key_rot, log_total, peaks = attention_forward(
+        lens, query_part, kv_part, tables, gates_wide, wide(hits_one), own_heads, group_rows
+    )
+    peaks = jnp.max(peaks, axis=0)[: own_heads * slots].reshape(own_heads, slots).T
+    peak_table = lax.dynamic_update_slice_in_dim(
+        jnp.full((slots, HEADS), very_low, f32), peaks, col * own_heads, 1
+    )
+    peaks_all = spread(peak_table, jnp.maximum)
+    gated_vals = after(gated_vals, grad_sent, *[pair[1] for pair in from_lines])
     attn_home = scatter_rows(dot_t(gated_vals, out_full))
 
     resid = x_home + attn_home
@@ -339,7 +514,7 @@
     gates_two, matches_two, chosen_two, gate_vals_two = route_gates(
         logits_two, home_routes.reshape(home_rows, TOP), expert_table
     )
-    hidden_rows = quad_rows(send_packed(hidden_two))
+    hidden_rows = quad_rows(send_packed(after(hidden_two, grad_rows)))
     gates_by_slot = gates_two.reshape(micro, tok_rows, slots)
     gate_parts = []
     for k in range(slots):
@@ -380,23 +555,32 @@
     ffn_packed = return_packed(quad_sum(dot_t(active, down_full)))
     out_home = (resid + unpack(ffn_packed, gates_two)).astype(bf16)
 
-    resid_grad_all = gather_rows(resid_grad.astype(bf16))
-    vals_grad = dot(resid_grad_all, out_full).reshape(all_rows, slots, own_width)
-    slot_part_one = jnp.sum(attn_vals.astype(f32) * vals_grad, axis=-1)
-    vals_grad = (gates_one[:, :, None] * vals_grad).astype(bf16)
-    vals_grad = vals_grad.reshape(micro, group_rows, slots, own_heads, HDIM)
-    prob_grad = jnp.einsum("mrshd,mkhd->mshrk", vals_grad, values, preferred_element_type=f32)
-    inner_sum = jnp.sum(probs * prob_grad, axis=-1, keepdims=True)
-    score_grad = (probs * (prob_grad - inner_sum) * score_scale).astype(bf16)
-    query_rot_grad = jnp.einsum("mshrk,mkhd->mrshd", score_grad, keys, preferred_element_type=f32)
-    query_grad = rotate(query_rot_grad.reshape(all_rows, query_width), tables, True).astype(bf16)
-    key_rot_grad = jnp.einsum("mshrk,mrshd->mkhd", score_grad, queries, preferred_element_type=f32)
-    value_grad = jnp.einsum("mshrk,mrshd->mkhd", probs_low, vals_grad, preferred_element_type=f32)
-    key_grad = rotate(key_rot_grad.reshape(all_rows, own_width), tables, True)
-    kv_grad = jnp.concatenate([key_grad, value_grad.reshape(all_rows, own_width)], axis=1)
-    kv_grad = kv_grad.astype(bf16)
+    scaled_hidden = (hidden_rows.astype(f32) * gate_rows[:, None]).astype(bf16)
+    scaled_grad = (grad_rows.astype(f32) * gate_rows[:, None]).astype(bf16)
+
+    def chunk_grad(k):
+        start = (chip ^ k) * chip_rows
+        left = lax.dynamic_slice_in_dim(scaled_hidden, start, chip_rows, 1)
+        right = lax.dynamic_slice_in_dim(scaled_grad, start, chip_rows, 1)
+        return jnp.concatenate(
+            [t_dot(left, joint_grad).astype(bf16), t_dot(right, active).astype(bf16)], axis=1
+        )
+
+    chunk_grads = [chunk_grad(k) for k in range(chips)]
+    side_lines = [swap(chunk_grads[2 * line + 1], "dp", 4 * line) for line in range(1, lines)]
+    keep_lines_grad = [swap(chunk_grads[2 * line], "dp", 4 * line) for line in range(1, lines)]
+
+    resid_grad_low = after(resid_grad.astype(bf16), *chunk_grads[2:])
+    resid_grad_all = gather_rows(resid_grad_low)
+    out_part = t_dot(resid_grad_all, gated_vals).astype(bf16)
+    vals_grad = dot(resid_grad_all, out_full)
+    vals_grad = after(vals_grad, out_part, *chunk_grads[:2], *side_lines)
+    query_grad, key_grad, value_grad, slot_part_one = attention_backward(
+        lens, query_rot, key_rot, kv_part, attn_vals, vals_grad, tables, gates_wide, log_total,
+        own_heads, group_rows,
+    )
+    kv_grad = jnp.concatenate([key_grad, value_grad], axis=1)
     hidden_one_part = dot_t(query_grad, query_full) + dot_t(kv_grad, kv_full)
-    slot_part_one = jnp.pad(slot_part_one, ((0, 0), (0, HDIM - slots)))
     back_one = scatter_rows(
         jnp.concatenate([hidden_one_part.astype(bf16), slot_part_one.astype(bf16)], axis=1)
     )
@@ -421,19 +605,10 @@
     results = lax.all_to_all(results, "dp", split_axis=0, concat_axis=0, tiled=True)
     results = results.transpose(1, 0, 2, 3).reshape(2, micro, tok_rows, width)
 
-    scaled_hidden = (hidden_rows.astype(f32) * gate_rows[:, None]).astype(bf16)
-    scaled_grad = (grad_rows.astype(f32) * gate_rows[:, None]).astype(bf16)
-
-    def chunk_grad(k):
-        start = (chip ^ k) * chip_rows
-        left = lax.dynamic_slice_in_dim(scaled_hidden, start, chip_rows, 1)
-        right = lax.dynamic_slice_in_dim(scaled_grad, start, chip_rows, 1)
-        return jnp.concatenate([t_dot(left, joint_grad), t_dot(right, active)], axis=1)
-
-    side_grad, keep_grad = chunk_grad(1), chunk_grad(0)
-    for line in range(1, lines):
-        side_grad = side_grad + swap(chunk_grad(2 * line + 1).astype(bf16), "dp", 4 * line).astype(f32)
-        keep_grad = keep_grad + swap(chunk_grad(2 * line).astype(bf16), "dp", 4 * line).astype(f32)
+    side_grad, keep_grad = chunk_grads[1].astype(f32), chunk_grads[0].astype(f32)
+    for line in range(lines - 1):
+        side_grad = side_grad + side_lines[line].astype(f32)
+        keep_grad = keep_grad + keep_lines_grad[line].astype(f32)
     other_grad = swap(side_grad.astype(bf16), "dp", 2)
     pair = jnp.stack([keep_grad.astype(bf16), other_grad]).reshape(2, 2, shard_rows, 3 * quarter)
     own_pair = lax.dynamic_index_in_dim(pair, core, 1, keepdims=False)
@@ -449,7 +624,7 @@
     def reduced(value):
         return lax.psum_scatter(value.astype(bf16), "dp", scatter_dimension=0, tiled=True)
 
-    out_grad = slots_of(reduced(t_dot(resid_grad_all, gated_vals))).astype(f32)
+    out_grad = slots_of(reduced(out_part)).astype(f32)
     query_out = slots_of(reduced(t_dot(hidden_one, query_grad))).astype(f32)
     kv_own = reduced(t_dot(hidden_one, kv_grad))
     key_part, value_part = kv_own[:, :own_width], kv_own[:, own_width:]
@@ -467,15 +642,12 @@
         axis=1,
     ).astype(f32)
 
-    sums = lax.psum(
+    sums = spread(
         jnp.concatenate(
             [gain_one_grad[None], gain_two_grad[None], router_one_grad, router_two_grad], axis=0
         ),
-        ("dp", "expert"),
-    )
-    peaks = lax.all_gather(own_peak, "dp", axis=0)
-    peaks = jnp.max(peaks, axis=0)
-    peaks_all = lax.all_gather(peaks, "expert", axis=1, tiled=True)
+        jnp.add,
+    )
     limit = clip_limit[0].astype(f32)
     factor = limit / jnp.maximum(peaks_all, limit)
     query_scale = jnp.repeat(jnp.sqrt(take(factor, col)), HDIM)

time: 1320 us -> 1260 us (0.955)
  local copies, waits for them, and re-layouts: 184 us -> 88.9 us
  Pallas kernels: 0 us -> 58.7 us
  waiting for transfers between devices: 587 us -> 628 us
  matrix products: 279 us -> 239 us
  blocking collectives: 28.3 us -> 0 us
  starting transfers between devices: 87.4 us -> 105 us
    ppermute x63 -> x76, waiting for transfers between devices: 539 us -> 601 us  [swap(): return lax.ppermute(value, axis, [(i, i ^ step) for i in range(count)])]
    pallas_call x0 -> x2, Pallas kernels: none -> 58.7 us  [the longest x1 29.9 us: attention_backward(): pl.pallas_call(backward_kernel, grid_spec=pltpu.PrefetchScalarGridSpec(nu...]
    dot_general x6 -> x0, matrix products: 51.5 us -> none  [the longest x1 17.9 us: local(): jnp.einsum('mshrk,mkhd->mrshd', score_grad, keys, preferred_element_type=...]
    all_gather x2 -> x0, blocking collectives: 28.3 us -> none  [the longest x1 17.3 us: local(): peaks = lax.all_gather(own_peak, 'dp', axis=0)]
    dot_general x2 -> x0, local copies, waits for them, and re-layouts: 24.8 us -> none  [dot(): return jnp.dot(left, right, preferred_element_type=f32)]
    ppermute x63 -> x76, starting transfers between devices: 68.7 us -> 89.9 us  [swap(): return lax.ppermute(value, axis, [(i, i ^ step) for i in range(count)])]
    convert_element_type x4 -> x0, local copies, waits for them, and re-layouts: 16.2 us -> none  [the longest x3 12.1 us: local(): gated_vals = (gates_one[:, :, None] * attn_vals.astype(f32)).astype(bf16)]
    reduce_scatter x3, waiting for transfers between devices: 20.3 us -> 4.71 us  [reduced(): lax.psum_scatter(value.astype(bf16), 'dp', scatter_dimension=0, tiled=True)]
  transfers between devices with their start and end apart: 76 -> 88, of which waited for: 41 -> 48; matrix products, arithmetic and copies ran while one was open for 31% -> 26% of each run, Pallas kernels for 0% -> 5%
where the time goes in v2:
time: 1260 us; the launch traced here: 1250 us
  waiting for transfers between devices  628 us (50%)
  matrix products  239 us (19%)
  other arithmetic  118 us (9%)
  starting transfers between devices  105 us (8%)
  local copies, waits for them, and re-layouts  88.9 us (7%)
  Pallas kernels  58.7 us (5%)
  between operations  17.2 us (1%)
    ppermute x76, waiting for transfers between devices, swap(): return lax.ppermute(value, axis, [(i, i ^ step) for i in range(count)])  601 us
    ppermute x76, starting transfers between devices, swap(): return lax.ppermute(value, axis, [(i, i ^ step) for i in range(count)])  89.9 us
    dot_general x13, matrix products, t_dot(): lax.dot_general(left, right, (((0,), (0,)), ((), ())), preferred_element_...  78.6 us
    dot_general x7, matrix products, dot(): return jnp.dot(left, right, preferred_element_type=f32)  76.4 us
    dot_general x7, matrix products, dot_t(): lax.dot_general(left, right, (((1,), (1,)), ((), ())), preferred_element_...  67.7 us
    pallas_call x1, Pallas kernels, attention_backward(): pl.pallas_call(backward_kernel, grid_spec=pltpu.PrefetchScalarGridSpec(nu...  29.9 us
    pallas_call x1, Pallas kernels, attention_forward(): pl.pallas_call(forward_kernel, grid_spec=pltpu.PrefetchScalarGridSpec(num...  28.8 us
  transfers between devices with their start and end apart: 88, of which 48 were waited for; matrix products, arithmetic and copies ran while one was open for 26% of the time, Pallas kernels for 5%

profile of v2, /device:TPU:8, one launch (start us, length us, event | category | flops | bytes accessed | tf_op | source)
XLA Modules:
  0.0 1254.3 jit_solution(7578906301147067777)
XLA Ops:
  37.0 10.9 collective-permute-done.6
  64.7 11.4 collective-permute-done.15
  132.9 11.7 collective-permute-done.11
  158.5 23.2 %collective-permute-done.1 = bf16[2,64,2048]{2,1,0:T(8,128)(2,1)} collective-permute-done((bf16[2,64,2048]{2,1,0:T(8,128)(2,1)}, bf16[2,64,2048]{2,1,0:T(8,128)(2,1)}, u32[]{:S(2)}, u32[]{:S(2)}) %collective-permute-start.1) | collective-permute-done | bytes 524320 | tf_op jit(solution)/shard_map/ppermute | solution.py:35
  184.0 10.1 collective-permute-done.2
  210.2 40.5 %collective-permute-done.3 = bf16[256,8448]{1,0:T(8,128)(2,1)} collective-permute-done((bf16[256,8448]{1,0:T(8,128)(2,1)}, bf16[256,8448]{1,0:T(8,128)(2,1)}, u32[]{:S(2)}, u32[]{:S(2)}) %collective-permute-start.3) | collective-permute-done | bytes 4325408 | tf_op jit(solution)/shard_map/ppermute | solution.py:35
  255.2 26.3 %collective-permute-done.4 = bf16[256,8448]{1,0:T(8,128)(2,1)} collective-permute-done((bf16[256,8448]{1,0:T(8,128)(2,1)}, bf16[256,8448]{1,0:T(8,128)(2,1)}, u32[]{:S(2)}, u32[]{:S(2)}) %collective-permute-start.4) | collective-permute-done | bytes 4325408 | tf_op jit(solution)/shard_map/ppermute | solution.py:35
  290.8 10.5 fusion.186.query
  301.3 28.8 %attention_forward.1 = (bf16[512,2048]{1,0:T(8,128)(2,1)}, bf16[512,2048]{1,0:T(8,128)(2,1)}, bf16[512,2048]{1,0:T(8,128)(2,1)}, bf16[512,512]{1,0:T(8,128)(2,1)...) custom-call(s32[2]{0:T(128)} %copy-done.93, f32[512,2048]{1,0:T(8,128)} %fusion.186.query, ...), custom_call_target="tpu_custom_call" | custom-call | flops 1073741824 | bytes 14680064 | tf_op jit(solution)/shard_map/attention_forward/pallas_call | solution.py:186
  346.0 29.3 %collective-permute-done.19 = bf16[2,64,2048]{2,1,0:T(8,128)(2,1)S(1)} collective-permute-done((bf16[2,64,2048]{2,1,0:T(8,128)(2,1)S(1)}, bf16[2,64,2048]{2,1,0:T(8,128)(2,1)S(1)}, u32[]{:S(2)}, u32[]{:S(2)}) %collective-permute-start.19) | collective-permute-done | bytes 524320 | tf_op jit(solution)/shard_map/ppermute | solution.py:35
  375.3 9.5 collective-permute-done.18
  397.2 21.5 %collective-permute-done.25 = bf16[2,48,2048]{2,1,0:T(8,128)(2,1)S(1)} collective-permute-done((bf16[2,48,2048]{2,1,0:T(8,128)(2,1)S(1)}, bf16[2,48,2048]{2,1,0:T(8,128)(2,1)S(1)}, u32[]{:S(2)}, u32[]{:S(2)}) %collective-permute-start.25) | collective-permute-done | bytes 393248 | tf_op jit(solution)/shard_map/ppermute | solution.py:35
  435.0 37.9 %collective-permute-done.32 = bf16[256,4224]{1,0:T(8,128)(2,1)S(1)} collective-permute-done((bf16[256,4224]{1,0:T(8,128)(2,1)S(1)}, bf16[256,4224]{1,0:T(8,128)(2,1)S(1)}, u32[]{:S(2)}, u32[]{:S(2)}) %collective-permute-start.32) | collective-permute-done | bytes 2162720 | tf_op jit(solution)/shard_map/ppermute | solution.py:35
  479.7 29.4 %fusion.3 = f32[1536,2816]{1,0:T(8,128)} fusion(bf16[2048,4224]{1,0:T(8,128)(2,1)} %bitcast.63, bf16[384,2048]{1,0:T(8,128)(2,1)} %copy-done.25, bf16[384,2048]{1,0:T(8,128)(2,1)} %copy-done.23, bf16[384,2048]{1,0:T(8,128)(2,1)} %copy-done.24, bf16[384,2048]{1,0:T(8,128)(2,1)S(1)} %bitcast.423), kind=kOutput, calls=%fused_computation.6 | convolution fusion | flops 17741905920 | bytes 35127296 | tf_op jit(solution)/shard_map/dot_general | solution.py:22
  509.1 21.8 %multiply_convert_fusion.3 = (bf16[1536,1408]{1,0:T(8,128)(2,1)}, bf16[1536,1408]{1,0:T(8,128)(2,1)}, bf16[1536]{0:T(1024)(128)(2,1)S(1)}, bf16[1536,1408]{1,0:T(8,128)(2,1)}) fusion(f32[1536,2816]{1,0:T(8,128)} %fusion.3, bf16[2048,4224]{1,0:T(8,128)(2,1)} %bitcast.63, bf16[384,2048]{1,0:T(8,128)(2,1)} %collective-permute-done.22, ...), kind=kOutput, calls=%fused_computation.17 | convolution fusion | flops 8922462208 | bytes 42339328 | tf_op jit(solution)/shard_map/dot_general | solution.py:22
  531.2 25.0 %fusion.6 = bf16[1536,2048]{1,0:T(8,128)(2,1)} fusion(bf16[2048,4224]{1,0:T(8,128)(2,1)} %bitcast.63, bf16[1536,1408]{1,0:T(8,128)(2,1)} %get-tuple-element.84, bf16[1536,1408]{1,0:T(8,128)(2,1)} %get-tuple-element.83), kind=kOutput, calls=%fused_computation.21 | convolution fusion | flops 17737187328 | bytes 26476544 | tf_op jit(solution)/shard_map/dot_general | solution.py:26
  571.4 17.1 %fusion.184 = (bf16[1536,2048]{1,0:T(8,128)(2,1)}, f32[1536,2048]{1,0:T(8,128)}) fusion(bf16[1536,1408]{1,0:T(8,128)(2,1)} %get-tuple-element.86, bf16[2048,4224]{1,0:T(8,128)(2,1)} %bitcast.63), kind=kOutput, calls=%fused_computation.463 | convolution fusion | flops 8861515776 | bytes 28966912 | tf_op jit(solution)/shard_map/dot_general | solution.py:26
  588.5 21.0 %collective-permute-done.42 = bf16[384,2176]{1,0:T(8,128)(2,1)S(1)} collective-permute-done((bf16[384,2176]{1,0:T(8,128)(2,1)S(1)}, bf16[384,2176]{1,0:T(8,128)(2,1)S(1)}, u32[]{:S(2)}, u32[]{:S(2)}) %collective-permute-start.42) | collective-permute-done | bytes 1671200 | tf_op jit(solution)/shard_map/ppermute | solution.py:35
  618.7 23.8 %collective-permute-done.45 = bf16[2,48,2176]{2,1,0:T(8,128)(2,1)} collective-permute-done((bf16[2,48,2176]{2,1,0:T(8,128)(2,1)S(1)}, bf16[2,48,2176]{2,1,0:T(8,128)(2,1)}, u32[]{:S(2)}, u32[]{:S(2)}) %collective-permute-start.45) | collective-permute-done | bytes 417824 | tf_op jit(solution)/shard_map/ppermute | solution.py:35
  721.9 18.7 %collective-permute-done.52 = bf16[2,64,2048]{2,1,0:T(8,128)(2,1)S(1)} collective-permute-done((bf16[2,64,2048]{2,1,0:T(8,128)(2,1)S(1)}, bf16[2,64,2048]{2,1,0:T(8,128)(2,1)S(1)}, u32[]{:S(2)}, u32[]{:S(2)}) %collective-permute-start.52) | collective-permute-done | bytes 524320 | tf_op jit(solution)/shard_map/ppermute | solution.py:35
  740.7 13.1 %collective-permute-done.53 = bf16[2,64,2048]{2,1,0:T(8,128)(2,1)S(1)} collective-permute-done((bf16[2,64,2048]{2,1,0:T(8,128)(2,1)S(1)}, bf16[2,64,2048]{2,1,0:T(8,128)(2,1)S(1)}, u32[]{:S(2)}, u32[]{:S(2)}) %collective-permute-start.53) | collective-permute-done | bytes 524320 | tf_op jit(solution)/shard_map/ppermute | solution.py:35
  753.8 12.1 collective-permute-done.54
  778.8 28.9 %collective-permute-done.55 = bf16[512,4224]{1,0:T(8,128)(2,1)} collective-permute-done((bf16[512,4224]{1,0:T(8,128)(2,1)}, bf16[512,4224]{1,0:T(8,128)(2,1)}, u32[]{:S(2)}, u32[]{:S(2)}) %collective-permute-start.55) | collective-permute-done | bytes 4325408 | tf_op jit(solution)/shard_map/ppermute | solution.py:35
  807.7 29.9 %attention_backward.1 = (bf16[512,2048]{1,0:T(8,128)(2,1)}, bf16[512,512]{1,0:T(8,128)(2,1)}, bf16[512,512]{1,0:T(8,128)(2,1)}, f32[512,128]{1,0:T(8,128)}) custom-call(s32[2]{0:T(128)} %copy-done.93, bf16[512,2048]{1,0:T(8,128)(2,1)} %get-tuple-element.32.query, bf16[512,512]{1,0:T(8,128)(2,1)} %get-tuple-element.33.key, ...), custom_call_target="tpu_custom_call" | custom-call | flops 2684354560 | bytes 14680064 | tf_op jit(solution)/shard_map/attention_backward/pallas_call | solution.py:217
  863.7 34.3 %collective-permute-done.78 = f32[4,16]{1,0:T(4,128)S(1)} collective-permute-done((f32[4,16]{1,0:T(4,128)S(1)}, f32[4,16]{1,0:T(4,128)S(1)}, u32[]{:S(2)}, u32[]{:S(2)}) %collective-permute-start.78) | collective-permute-done | bytes 288 | tf_op jit(solution)/shard_map/ppermute | solution.py:35
  919.0 9.9 collective-permute-done.39
  980.6 10.0 add_convert_fusion.2
  996.7 72.4 %collective-permute-done.72 = bf16[512,4224]{1,0:T(8,128)(2,1)} collective-permute-done((bf16[512,4224]{1,0:T(8,128)(2,1)}, bf16[512,4224]{1,0:T(8,128)(2,1)}, u32[]{:S(2)}, u32[]{:S(2)}) %collective-permute-start.72) | collective-permute-done | bytes 4325408 | tf_op jit(solution)/shard_map/ppermute | solution.py:35
  1079.7 17.7 %collective-permute-done.73 = bf16[512,4224]{1,0:T(8,128)(2,1)} collective-permute-done((bf16[512,4224]{1,0:T(8,128)(2,1)}, bf16[512,4224]{1,0:T(8,128)(2,1)}, u32[]{:S(2)}, u32[]{:S(2)}) %collective-permute-start.73) | collective-permute-done | bytes 4325408 | tf_op jit(solution)/shard_map/ppermute | solution.py:35
  1130.7 18.2 %collective-permute-done.63 = f32[10,2048]{1,0:T(8,128)S(1)} collective-permute-done((f32[10,2048]{1,0:T(8,128)S(1)}, f32[10,2048]{1,0:T(8,128)S(1)}, u32[]{:S(2)}, u32[]{:S(2)}) %collective-permute-start.63) | collective-permute-done | bytes 81952 | tf_op jit(solution)/shard_map/ppermute | solution.py:35
  1155.5 10.4 collective-permute-done.70
  1218.0 17.8 %collective-permute-done.66 = bf16[256,512]{1,0:T(8,128)(2,1)S(1)} collective-permute-done((bf16[256,512]{1,0:T(8,128)(2,1)S(1)}, bf16[256,512]{1,0:T(8,128)(2,1)S(1)}, u32[]{:S(2)}, u32[]{:S(2)}) %collective-permute-start.66) | collective-permute-done | bytes 262176 | tf_op jit(solution)/shard_map/ppermute | solution.py:35
  (684 shorter events, 533.9 us)
Async XLA Ops:
  7.2 277.4 %all-gather.6.cloned.1.call-start = ((), (), s32[]{:S(2)}) async-start(), calls=%async_computation.6 | async-start | bytes 4718592 | tf_op jit(solution)/shard_map/all_gather | solution.py:361
  24.0 266.8 %all-gather.4.cloned.1.call-start = ((), (), s32[]{:S(2)}) async-start(), calls=%async_computation.5 | async-start | bytes 9437184 | tf_op jit(solution)/shard_map/all_gather | solution.py:362
  53.6 276.5 %all-gather.8.cloned.1.call-start = ((), (), s32[]{:S(2)}) async-start(), calls=%async_computation.7 | async-start | bytes 9437184 | tf_op jit(solution)/shard_map/all_gather | solution.py:363
  86.7 1063.6 %reduce-scatter.8.cloned.1.call-start = ((), (), s32[]{:S(2)}) async-start(), calls=%async_computation.10 | async-start | bytes 4718592 | tf_op jit(solution)/shard_map/reduce_scatter | solution.py:625
  98.5 152.1 %collective-permute-start.3 = (bf16[256,8448]{1,0:T(8,128)(2,1)}, bf16[256,8448]{1,0:T(8,128)(2,1)}, u32[]{:S(2)}, u32[]{:S(2)}) collective-permute-start(bf16[256,8448]{1,0:T(8,128)(2,1)} %get-tuple-element.115), channel_id=1, source_target_pairs={{0,8},{4,12},{8,0},{12,4},{16,24},{20,28},{24,16},{28,20},{1,9},{5... | collective-permute-start | bytes 12976136 | tf_op jit(solution)/shard_map/ppermute | solution.py:35
  129.5 69.2 %collective-permute-start.29 = (bf16[256,4224]{1,0:T(8,128)(2,1)}, bf16[256,4224]{1,0:T(8,128)(2,1)}, u32[]{:S(2)}, u32[]{:S(2)}) collective-permute-start(bf16[256,4224]{1,0:T(8,128)(2,1)} %constant_dynamic-slice_fusion.27), channel_id=1, source_target_pairs={{0,4},{4,0},{8,12},{12,8},{16,20},{20,16},{24,28},{28,24},{1,5},{5... | collective-permute-start | bytes 6488072 | tf_op jit(solution)/shard_map/ppermute | solution.py:35
  151.2 130.3 %collective-permute-start.4 = (bf16[256,8448]{1,0:T(8,128)(2,1)}, bf16[256,8448]{1,0:T(8,128)(2,1)}, u32[]{:S(2)}, u32[]{:S(2)}) collective-permute-start(bf16[256,8448]{1,0:T(8,128)(2,1)} %get-tuple-element.114), channel_id=1, source_target_pairs={{0,16},{4,20},{8,24},{12,28},{16,0},{20,4},{24,8},{28,12},{1,17},{... | collective-permute-start | bytes 12976136 | tf_op jit(solution)/shard_map/ppermute | solution.py:35
  152.7 41.3 %collective-permute-start.2 = (bf16[2,64,2048]{2,1,0:T(8,128)(2,1)}, bf16[2,64,2048]{2,1,0:T(8,128)(2,1)S(1)}, u32[]{:S(2)}, u32[]{:S(2)}) collective-permute-start(bf16[2,64,2048]{2,1,0:T(8,128)(2,1)} %get-tuple-element.82), channel_id=1, source_target_pairs={{0,3},{1,2},{2,1},{3,0},{4,7},{5,6},{6,5},{7,4},{8,11},{9,10},{10,... | collective-permute-start | bytes 1572872 | tf_op jit(solution)/shard_map/ppermute | solution.py:35
  181.7 215.4 %collective-permute-start.21 = (bf16[384,2048]{1,0:T(8,128)(2,1)}, bf16[384,2048]{1,0:T(8,128)(2,1)}, u32[]{:S(2)}, u32[]{:S(2)}) collective-permute-start(bf16[384,2048]{1,0:T(8,128)(2,1)} %bitcast.38), channel_id=1, source_target_pairs={{0,8},{4,12},{8,0},{12,4},{16,24},{20,28},{24,16},{28,20},{1,9},{5... | collective-permute-start | bytes 4718600 | tf_op jit(solution)/shard_map/ppermute | solution.py:35
  253.8 76.4 %collective-permute-start.13 = (bf16[256,4224]{1,0:T(8,128)(2,1)}, bf16[256,4224]{1,0:T(8,128)(2,1)}, u32[]{:S(2)}, u32[]{:S(2)}) collective-permute-start(bf16[256,4224]{1,0:T(8,128)(2,1)} %constant_dynamic-slice_fusion.32), channel_id=1, source_target_pairs={{0,16},{4,20},{8,24},{12,28},{16,0},{20,4},{24,8},{28,12},{1,17},{... | collective-permute-start | bytes 6488072 | tf_op jit(solution)/shard_map/ppermute | solution.py:35
  255.2 85.2 %collective-permute-start.30 = (bf16[256,4224]{1,0:T(8,128)(2,1)}, bf16[256,4224]{1,0:T(8,128)(2,1)}, u32[]{:S(2)}, u32[]{:S(2)}) collective-permute-start(bf16[256,4224]{1,0:T(8,128)(2,1)} %constant_dynamic-slice_fusion.32), channel_id=1, source_target_pairs={{0,4},{4,0},{8,12},{12,8},{16,20},{20,16},{24,28},{28,24},{1,5},{5... | collective-permute-start | bytes 6488072 | tf_op jit(solution)/shard_map/ppermute | solution.py:35
  284.6 141.9 %collective-permute-start.31 = (bf16[256,4224]{1,0:T(8,128)(2,1)}, bf16[256,4224]{1,0:T(8,128)(2,1)}, u32[]{:S(2)}, u32[]{:S(2)}) collective-permute-start(bf16[256,4224]{1,0:T(8,128)(2,1)} %constant_dynamic-slice_fusion.25), channel_id=1, source_target_pairs={{0,4},{4,0},{8,12},{12,8},{16,20},{20,16},{24,28},{28,24},{1,5},{5... | collective-permute-start | bytes 6488072 | tf_op jit(solution)/shard_map/ppermute | solution.py:35
  339.6 45.2 %collective-permute-start.18 = (bf16[2,64,2048]{2,1,0:T(8,128)(2,1)S(1)}, bf16[2,64,2048]{2,1,0:T(8,128)(2,1)S(1)}, u32[]{:S(2)}, u32[]{:S(2)}) collective-permute-start(bf16[2,64,2048]{2,1,0:T(8,128)(2,1)S(1)} %get-tuple-element.113), channel_id=1, source_target_pairs={{0,2},{1,3},{2,0},{3,1},{4,6},{5,7},{6,4},{7,5},{8,10},{9,11},{10,... | collective-permute-start | bytes 1572872 | tf_op jit(solution)/shard_map/ppermute | solution.py:35
  340.4 44.4 %collective-permute-start.17 = (bf16[2,64,2048]{2,1,0:T(8,128)(2,1)S(1)}, bf16[2,64,2048]{2,1,0:T(8,128)(2,1)S(1)}, u32[]{:S(2)}, u32[]{:S(2)}) collective-permute-start(bf16[2,64,2048]{2,1,0:T(8,128)(2,1)S(1)} %get-tuple-element.111), channel_id=1, source_target_pairs={{0,1},{1,0},{2,3},{3,2},{4,5},{5,4},{6,7},{7,6},{8,9},{9,8},{10,11... | collective-permute-start | bytes 1572872 | tf_op jit(solution)/shard_map/ppermute | solution.py:35
  397.1 112.0 %collective-permute-start.20 = (bf16[384,2048]{1,0:T(8,128)(2,1)}, bf16[384,2048]{1,0:T(8,128)(2,1)}, u32[]{:S(2)}, u32[]{:S(2)}) collective-permute-start(bf16[384,2048]{1,0:T(8,128)(2,1)} %bitcast.38), channel_id=1, source_target_pairs={{0,4},{4,0},{8,12},{12,8},{16,20},{20,16},{24,28},{28,24},{1,5},{5... | collective-permute-start | bytes 4718600 | tf_op jit(solution)/shard_map/ppermute | solution.py:35
  418.7 90.4 %collective-permute-start.22 = (bf16[384,2048]{1,0:T(8,128)(2,1)}, bf16[384,2048]{1,0:T(8,128)(2,1)}, u32[]{:S(2)}, u32[]{:S(2)}) collective-permute-start(bf16[384,2048]{1,0:T(8,128)(2,1)} %collective-permute-done.21), channel_id=1, source_target_pairs={{0,4},{4,0},{8,12},{12,8},{16,20},{20,16},{24,28},{28,24},{1,5},{5... | collective-permute-start | bytes 4718600 | tf_op jit(solution)/shard_map/ppermute | solution.py:35
  424.8 48.1 %collective-permute-start.32 = (bf16[256,4224]{1,0:T(8,128)(2,1)S(1)}, bf16[256,4224]{1,0:T(8,128)(2,1)S(1)}, u32[]{:S(2)}, u32[]{:S(2)}) collective-permute-start(bf16[256,4224]{1,0:T(8,128)(2,1)S(1)} %copy-done.8), channel_id=1, source_target_pairs={{0,16},{4,20},{8,24},{12,28},{16,0},{20,4},{24,8},{28,12},{1,17},{... | collective-permute-start | bytes 6488072 | tf_op jit(solution)/shard_map/ppermute | solution.py:35
  426.4 47.0 %collective-permute-start.33 = (bf16[256,4224]{1,0:T(8,128)(2,1)}, bf16[256,4224]{1,0:T(8,128)(2,1)S(1)}, u32[]{:S(2)}, u32[]{:S(2)}) collective-permute-start(bf16[256,4224]{1,0:T(8,128)(2,1)} %collective-permute-done.13), channel_id=1, source_target_pairs={{0,4},{4,0},{8,12},{12,8},{16,20},{20,16},{24,28},{28,24},{1,5},{5... | collective-permute-start | bytes 6488072 | tf_op jit(solution)/shard_map/ppermute | solution.py:35
  426.6 46.3 %collective-permute-start.27 = (bf16[384,2048]{1,0:T(8,128)(2,1)S(1)}, bf16[384,2048]{1,0:T(8,128)(2,1)S(1)}, u32[]{:S(2)}, u32[]{:S(2)}) collective-permute-start(bf16[384,2048]{1,0:T(8,128)(2,1)S(1)} %bitcast.421), channel_id=1, source_target_pairs={{0,8},{4,12},{8,0},{12,4},{16,24},{20,28},{24,16},{28,20},{1,9},{5... | collective-permute-start | bytes 4718600 | tf_op jit(solution)/shard_map/ppermute | solution.py:35
  711.6 96.1 %collective-permute-start.55 = (bf16[512,4224]{1,0:T(8,128)(2,1)}, bf16[512,4224]{1,0:T(8,128)(2,1)}, u32[]{:S(2)}, u32[]{:S(2)}) collective-permute-start(bf16[512,4224]{1,0:T(8,128)(2,1)} %pad_maximum_fusion.4), channel_id=1, source_target_pairs={{0,16},{4,20},{8,24},{12,28},{16,0},{20,4},{24,8},{28,12},{1,17},{... | collective-permute-start | bytes 12976136 | tf_op jit(solution)/shard_map/ppermute | solution.py:35
  720.4 126.5 %collective-permute-start.35 = (bf16[384,2048]{1,0:T(8,128)(2,1)}, bf16[384,2048]{1,0:T(8,128)(2,1)}, u32[]{:S(2)}, u32[]{:S(2)}) collective-permute-start(bf16[384,2048]{1,0:T(8,128)(2,1)} %get-tuple-element.96), channel_id=1, source_target_pairs={{0,4},{4,0},{8,12},{12,8},{16,20},{20,16},{24,28},{28,24},{1,5},{5... | collective-permute-start | bytes 4718600 | tf_op jit(solution)/shard_map/ppermute | solution.py:35
  720.4 45.4 %collective-permute-start.54 = (bf16[2,64,2048]{2,1,0:T(8,128)(2,1)S(1)}, bf16[2,64,2048]{2,1,0:T(8,128)(2,1)S(1)}, u32[]{:S(2)}, u32[]{:S(2)}) collective-permute-start(bf16[2,64,2048]{2,1,0:T(8,128)(2,1)S(1)} %bitcast.441), channel_id=1, source_target_pairs={{0,3},{1,2},{2,1},{3,0},{4,7},{5,6},{6,5},{7,4},{8,11},{9,10},{10,... | collective-permute-start | bytes 1572872 | tf_op jit(solution)/shard_map/ppermute | solution.py:35
  846.8 336.6 %reduce-scatter.6.cloned.1.call-start = ((), (), s32[]{:S(2)}) async-start(), calls=%async_computation.9 | async-start | bytes 9437184 | tf_op jit(solution)/shard_map/reduce_scatter | solution.py:625
  846.8 54.9 %collective-permute-start.34 = (bf16[384,2048]{1,0:T(8,128)(2,1)S(1)}, bf16[384,2048]{1,0:T(8,128)(2,1)}, u32[]{:S(2)}, u32[]{:S(2)}) collective-permute-start(bf16[384,2048]{1,0:T(8,128)(2,1)S(1)} %get-tuple-element.95), channel_id=1, source_target_pairs={{0,4},{4,0},{8,12},{12,8},{16,20},{20,16},{24,28},{28,24},{1,5},{5... | collective-permute-start | bytes 4718600 | tf_op jit(solution)/shard_map/ppermute | solution.py:35
  849.8 51.9 %collective-permute-start.36 = (bf16[384,2048]{1,0:T(8,128)(2,1)S(1)}, bf16[384,2048]{1,0:T(8,128)(2,1)}, u32[]{:S(2)}, u32[]{:S(2)}) collective-permute-start(bf16[384,2048]{1,0:T(8,128)(2,1)S(1)} %fusion.22), channel_id=1, source_target_pairs={{0,8},{4,12},{8,0},{12,4},{16,24},{20,28},{24,16},{28,20},{1,9},{5... | collective-permute-start | bytes 4718600 | tf_op jit(solution)/shard_map/ppermute | solution.py:35
  942.1 127.0 %collective-permute-start.72 = (bf16[512,4224]{1,0:T(8,128)(2,1)}, bf16[512,4224]{1,0:T(8,128)(2,1)}, u32[]{:S(2)}, u32[]{:S(2)}) collective-permute-start(bf16[512,4224]{1,0:T(8,128)(2,1)} %pad_maximum_fusion.3), channel_id=1, source_target_pairs={{0,16},{4,20},{8,24},{12,28},{16,0},{20,4},{24,8},{28,12},{1,17},{... | collective-permute-start | bytes 12976136 | tf_op jit(solution)/shard_map/ppermute | solution.py:35
  943.6 246.4 %reduce-scatter.4.cloned.1.call-start = ((), (), s32[]{:S(2)}) async-start(), calls=%async_computation.8 | async-start | bytes 9437184 | tf_op jit(solution)/shard_map/reduce_scatter | solution.py:625
  975.5 121.9 %collective-permute-start.73 = (bf16[512,4224]{1,0:T(8,128)(2,1)}, bf16[512,4224]{1,0:T(8,128)(2,1)}, u32[]{:S(2)}, u32[]{:S(2)}) collective-permute-start(bf16[512,4224]{1,0:T(8,128)(2,1)} %add_convert_fusion), channel_id=1, source_target_pairs={{0,8},{4,12},{8,0},{12,4},{16,24},{20,28},{24,16},{28,20},{1,9},{5... | collective-permute-start | bytes 12976136 | tf_op jit(solution)/shard_map/ppermute | solution.py:35
  991.0 82.3 %collective-permute-start.58 = (bf16[2,64,2176]{2,1,0:T(8,128)(2,1)S(1)}, bf16[2,64,2176]{2,1,0:T(8,128)(2,1)S(1)}, u32[]{:S(2)}, u32[]{:S(2)}) collective-permute-start(bf16[2,64,2176]{2,1,0:T(8,128)(2,1)S(1)} %get-tuple-element.119), channel_id=1, source_target_pairs={{0,3},{1,2},{2,1},{3,0},{4,7},{5,6},{6,5},{7,4},{8,11},{9,10},{10,... | collective-permute-start | bytes 1671176 | tf_op jit(solution)/shard_map/ppermute | solution.py:35
  992.1 81.2 %collective-permute-start.57 = (bf16[2,64,2176]{2,1,0:T(8,128)(2,1)S(1)}, bf16[2,64,2176]{2,1,0:T(8,128)(2,1)S(1)}, u32[]{:S(2)}, u32[]{:S(2)}) collective-permute-start(bf16[2,64,2176]{2,1,0:T(8,128)(2,1)S(1)} %get-tuple-element.120), channel_id=1, source_target_pairs={{0,2},{1,3},{2,0},{3,1},{4,6},{5,7},{6,4},{7,5},{8,10},{9,11},{10,... | collective-permute-start | bytes 1671176 | tf_op jit(solution)/shard_map/ppermute | solution.py:35
  996.6 76.7 %collective-permute-start.56 = (bf16[2,64,2176]{2,1,0:T(8,128)(2,1)S(1)}, bf16[2,64,2176]{2,1,0:T(8,128)(2,1)S(1)}, u32[]{:S(2)}, u32[]{:S(2)}) collective-permute-start(bf16[2,64,2176]{2,1,0:T(8,128)(2,1)S(1)} %get-tuple-element.118), channel_id=1, source_target_pairs={{0,1},{1,0},{2,3},{3,2},{4,5},{5,4},{6,7},{7,6},{8,9},{9,8},{10,11... | collective-permute-start | bytes 1671176 | tf_op jit(solution)/shard_map/ppermute | solution.py:35
  1102.3 64.8 %collective-permute-start.74 = (bf16[2,256,4224]{2,1,0:T(8,128)(2,1)}, bf16[2,256,4224]{2,1,0:T(8,128)(2,1)}, u32[]{:S(2)}, u32[]{:S(2)}) collective-permute-start(bf16[2,256,4224]{2,1,0:T(8,128)(2,1)} %fusion.15), channel_id=1, source_target_pairs={{0,4},{4,0},{8,12},{12,8},{16,20},{20,16},{24,28},{28,24},{1,5},{5... | collective-permute-start | bytes 12976136 | tf_op jit(solution)/shard_map/ppermute | solution.py:35
  (175 other events, 4233.8 us)
Sparse Core Ops, SparseCore 0:
  24.1 38.6 all-gather.5
  65.3 80.9 all-gather.3
  148.2 88.2 all-gather.7
  846.9 63.5 reduce-scatter.7
  943.7 105.1 reduce-scatter.5
  1111.1 78.8 reduce-scatter.3

commit v3 on v2

--- a/solution.py
+++ b/solution.py
@@ -267,6 +267,150 @@
     inner_sum = jnp.sum(gate_vals * picked, axis=-1, keepdims=True)
     picked_grad = gate_vals * (picked - inner_sum)
     return jnp.sum(jnp.where(matches, picked_grad[:, :, None], 0.0), axis=1)
+
+
+def unit_blocks(count):
+    return [(start, min(512, count - start)) for start in range(0, count, 512)]
+
+
+def expert_kernel(place_ref, hidden, grad, *refs):
+    piece_count = (len(refs) - 6) // 2
+    own_pieces, near_pieces = refs[:piece_count], refs[piece_count : 2 * piece_count]
+    out, hidden_out, act_out, joint_out, weights, sems = refs[2 * piece_count :]
+    core, chip = place_ref[0], place_ref[1]
+    rows, columns = near_pieces[0].shape
+    units = columns // 3
+    width = hidden.shape[1]
+
+    @pl.when(pl.program_id(0) == 0)
+    def _():
+        copies = []
+        for k in range(piece_count):
+            base = (chip ^ k) * (2 * rows)
+            own, near = own_pieces[k], near_pieces[k]
+            if own.shape[1] != columns:
+                own = own.at[:, pl.ds(pl.multiple_of(core * columns, HDIM), columns)]
+            for number, (piece, part) in enumerate(((own, core), (near, 1 - core))):
+                start = pl.multiple_of(base + part * rows, 16)
+                copies.append(
+                    pltpu.make_async_copy(
+                        piece, weights.at[pl.ds(start, rows)], sems.at[2 * k + number]
+                    )
+                )
+        for copy in copies:
+            copy.start()
+        for copy in copies:
+            copy.wait()
+
+    slot_sum = jnp.zeros((hidden.shape[0], 1), f32)
+    for start, size in unit_blocks(units):
+        gate_pre = dot(hidden[...], weights[:, start : start + size])
+        up_pre = dot(hidden[...], weights[:, units + start : units + start + size])
+        act_grad = dot(grad[...], weights[:, 2 * units + start : 2 * units + start + size])
+        sigma = 1.0 / (1.0 + jnp.exp(-gate_pre))
+        silu_vals = gate_pre * sigma
+        active = (silu_vals * up_pre).astype(bf16)
+        act_out[:, start : start + size] = active
+        slot_sum += jnp.sum(active.astype(f32) * act_grad, axis=1, keepdims=True)
+        gate_grad = act_grad * up_pre * sigma * (1.0 + gate_pre * (1.0 - sigma))
+        joint_out[:, start : start + size] = gate_grad.astype(bf16)
+        joint_out[:, units + start : units + start + size] = (act_grad * silu_vals).astype(bf16)
+    for start in range(0, width, 512):
+        block = weights[start : start + 512, : 2 * units]
+        hidden_out[:, start : start + 512] = dot_t(joint_out[...], block).astype(bf16)
+        block = weights[start : start + 512, 2 * units :]
+        out[:, start : start + 512] = dot_t(act_out[...], block).astype(bf16)
+    lanes = lax.broadcasted_iota(jnp.int32, (hidden.shape[0], HDIM), 1)
+    hidden_out[:, width:] = jnp.where(lanes == 0, slot_sum, 0.0).astype(bf16)
+
+
+def expert_rows(position, hidden, grad, own_pieces, near_pieces):
+    rows, width = hidden.shape
+    columns = near_pieces[0].shape[1]
+    units = columns // 3
+    tile = 256
+    shape = jax.ShapeDtypeStruct
+    count = len(own_pieces)
+
+    def tiled(size):
+        return pl.BlockSpec((tile, size), lambda i, at: (i, 0))
+
+    return pl.pallas_call(
+        expert_kernel,
+        grid_spec=pltpu.PrefetchScalarGridSpec(
+            num_scalar_prefetch=1,
+            grid=(rows // tile,),
+            in_specs=[tiled(width)] * 2 + [pl.BlockSpec(memory_space=pl.ANY)] * (2 * count),
+            out_specs=[tiled(width), tiled(width + HDIM), tiled(units), tiled(2 * units)],
+            scratch_shapes=[
+                pltpu.VMEM((width, columns), bf16),
+                pltpu.SemaphoreType.DMA((2 * count,)),
+            ],
+        ),
+        out_shape=[
+            shape((rows, width), bf16),
+            shape((rows, width + HDIM), bf16),
+            shape((rows, units), bf16),
+            shape((rows, 2 * units), bf16),
+        ],
+        compiler_params=pltpu.CompilerParams(vmem_limit_bytes=56 * 2**20),
+        cost_estimate=pl.CostEstimate(
+            flops=4 * rows * width * columns,
+            bytes_accessed=2 * (width * columns + 6 * rows * width),
+            transcendentals=rows * units,
+        ),
+        name="expert_rows",
+    )(position, hidden, grad, *own_pieces, *near_pieces)
+
+
+def expert_grad_kernel(order, hidden, grad, gates, joint, active, *outs):
+    gate = gates[...]
+    left = (hidden[...].astype(f32) * gate).astype(bf16)
+    right = (grad[...].astype(f32) * gate).astype(bf16)
+    units = active.shape[1]
+    step = pl.program_id(0)
+    for number, out in enumerate(outs):
+
+        @pl.when(step // 2 == number)
+        def _():
+            for start, size in unit_blocks(2 * units):
+                out[:, start : start + size] = t_dot(left, joint[:, start : start + size]).astype(bf16)
+            for start, size in unit_blocks(units):
+                out[:, 2 * units + start : 2 * units + start + size] = t_dot(
+                    right, active[:, start : start + size]
+                ).astype(bf16)
+
+
+def expert_grads(chunks, chunk_rows, hidden, grad, gates, joint, active):
+    rows, units = active.shape
+    half = chunk_rows // 2
+    count = len(chunks)
+    order = jnp.stack([2 * chunk + part for chunk in chunks for part in range(2)]).astype(jnp.int32)
+
+    def whole(size):
+        return pl.BlockSpec((rows, size), lambda i, at: (0, 0), pipeline_mode=pl.Buffered(1))
+
+    column = pl.BlockSpec((rows, half), lambda i, at: (0, at[i]))
+    return pl.pallas_call(
+        expert_grad_kernel,
+        grid_spec=pltpu.PrefetchScalarGridSpec(
+            num_scalar_prefetch=1,
+            grid=(2 * count,),
+            in_specs=[column, column, whole(1), whole(2 * units), whole(units)],
+            out_specs=[
+                pl.BlockSpec((half, 3 * units), lambda i, at, n=n: (jnp.clip(i - 2 * n, 0, 1), 0))
+                for n in range(count)
+            ],
+        ),
+        out_shape=[jax.ShapeDtypeStruct((chunk_rows, 3 * units), bf16)] * count,
+        compiler_params=pltpu.CompilerParams(vmem_limit_bytes=48 * 2**20),
+        cost_estimate=pl.CostEstimate(
+            flops=2 * count * chunk_rows * rows * 3 * units,
+            bytes_accessed=2 * (rows * 3 * units + count * chunk_rows * (2 * rows + 3 * units)),
+            transcendentals=0,
+        ),
+        name="expert_grads",
+    )(order, hidden, grad, gates, joint, active)
 
 
 def local(
@@ -360,7 +504,6 @@
     )
     kv_full = lax.all_gather(own_kv, "dp", axis=0, tiled=True)
     query_full = lax.all_gather(columns_of(query_weight[0]), "dp", axis=0, tiled=True)
-    out_full = lax.all_gather(columns_of(attn_out_weight[0]), "dp", axis=0, tiled=True)
 
     def quarter_of(half, part):
         start = (2 * half + part) * quarter
@@ -384,23 +527,14 @@
         other_part = swap(part_of(from_side, 1 - core), "dp", 4 * line)
         from_lines.append((swap(part_of(from_side, core), "dp", 4 * line), other_part))
 
-    def pair_rows(own, other):
-        near = swap(other, "dp", 1)
-        return jnp.concatenate(
-            [jnp.where(core == 0, own, near), jnp.where(core == 0, near, own)], axis=0
-        )
-
-    chunk_parts = [
-        pair_rows(part_of(piece, core), part_of(piece, 1 - core)) for piece in (keep_side, from_side)
-    ]
-    for line in range(1, lines):
-        piece = keep_lines[line - 1]
-        chunk_parts.append(pair_rows(part_of(piece, core), part_of(piece, 1 - core)))
-        chunk_parts.append(pair_rows(*from_lines[line - 1]))
-    chunk_at = [chip ^ k for k in range(chips)]
-    ffn_full = place(chunk_parts, chunk_at).reshape(width, 3 * quarter)
-    gate_up_full = ffn_full[:, : 2 * quarter]
-    down_full = ffn_full[:, 2 * quarter :]
+    own_pieces = [keep_side, from_side]
+    near_pieces = [swap(part_of(piece, 1 - core), "dp", 1) for piece in own_pieces]
+    for line in range(lines - 1):
+        own_pieces += [keep_lines[line], from_lines[line][0]]
+        near_pieces += [
+            swap(part_of(keep_lines[line], 1 - core), "dp", 1),
+            swap(from_lines[line][1], "dp", 1),
+        ]
 
     positions = jnp.arange(group_rows, dtype=jnp.int32)
     first_len = lax.dynamic_index_in_dim(seq_lengths[:, :, 0], group, 1, keepdims=True)
@@ -456,16 +590,16 @@
         across = swap(far, "dp", 1)
         return jnp.concatenate([value, near, far, across], axis=0)
 
-    def quad_sum(value):
+    def quad_sum(value, *others):
         own, near, far, across = jnp.split(value, 4, axis=0)
-        far_sum = far.astype(f32) + swap(across.astype(bf16), "dp", 1).astype(f32)
-        own_sum = own.astype(f32) + swap(near.astype(bf16), "dp", 1).astype(f32)
-        return own_sum + swap(far_sum.astype(bf16), "dp", 2).astype(f32)
-
-    def return_packed(value):
+        far_sum = far.astype(f32) + swap(across, "dp", 1).astype(f32)
+        own_sum = own.astype(f32) + swap(near, "dp", 1).astype(f32)
+        return own_sum + after(swap(far_sum.astype(bf16), "dp", 2), *others).astype(f32)
+
+    def return_packed(value, *others):
         shaped = value.astype(bf16).reshape(slots, micro, cap, -1)
         parts = [swap(shaped[k], "expert", k) if k else shaped[k] for k in range(slots)]
-        return jnp.stack(parts)
+        return after(parts, *others)
 
     def unpack(packed, scale):
         total = None
@@ -475,14 +609,18 @@
             total = rows if total is None else total + rows
         return total
 
-    grad_sent = send_packed(dy_home.astype(bf16))
-    grad_rows = quad_rows(grad_sent)
-
     gain_one = attn_gain.astype(f32)
     gain_two = ffn_gain.astype(f32)
     normed_one, scale_one = normalize(x_home)
     hidden_one_home = (normed_one * gain_one).astype(bf16)
-    hidden_one = gather_rows(hidden_one_home)
+    hidden_one_raw = gather_rows(hidden_one_home)
+    out_weight, dy_low = lax.optimization_barrier(
+        (attn_out_weight[0], dy_home.astype(bf16), hidden_one_raw)
+    )[:2]
+    out_full = lax.all_gather(columns_of(out_weight), "dp", axis=0, tiled=True)
+    grad_sent = send_packed(dy_low)
+    grad_rows = quad_rows(grad_sent)
+    hidden_one = after(hidden_one_raw, from_side, *keep_lines)
     logits_one = dot(hidden_one, attn_router)
     gates_one, matches_one, chosen_one, gate_vals_one = route_gates(
         logits_one, attn_routes.reshape(all_rows, TOP), expert_table
@@ -493,7 +631,7 @@
         return jnp.pad(value, ((0, 0), (0, HDIM - value.shape[1])))
 
     kv_part = dot(hidden_one, kv_full).astype(bf16)
-    query_part = dot(after(hidden_one, from_side, *keep_lines), query_full)
+    query_part = dot(hidden_one, query_full)
     lens = first_len[:, 0].astype(jnp.int32)
     gates_wide = wide(gates_one)
     attn_vals, gated_vals, query_rot, key_rot, log_total, peaks = attention_forward(
@@ -523,20 +661,24 @@
         gate_parts.append(swap(part, "expert", k) if k else part)
     gate_rows = quad_rows(jnp.concatenate(gate_parts))
 
-    joint = dot(hidden_rows, gate_up_full)
-    gate_pre, up_pre = joint[:, :quarter], joint[:, quarter:]
-    sigma = jax.nn.sigmoid(gate_pre)
-    silu_vals = gate_pre * sigma
-    active = (silu_vals * up_pre).astype(bf16)
-    active_grad = dot(grad_rows, down_full)
-    gate_grad = active_grad * up_pre * sigma * (1.0 + gate_pre * (1.0 - sigma))
-    joint_grad = jnp.concatenate([gate_grad, active_grad * silu_vals], axis=1).astype(bf16)
-    slot_part_two = jnp.sum(active.astype(f32) * active_grad, axis=-1, keepdims=True)
-    slot_part_two = jnp.pad(slot_part_two, ((0, 0), (0, HDIM - 1))).astype(bf16)
-    hidden_part = jnp.concatenate(
-        [dot_t(joint_grad, gate_up_full).astype(bf16), slot_part_two], axis=1
-    )
-    back_packed = return_packed(quad_sum(hidden_part))
+    hidden_rows = after(hidden_rows, gate_rows)
+    position = jnp.stack([core, chip]).astype(jnp.int32)
+    ffn_part, hidden_part, active, joint_grad = expert_rows(
+        position, hidden_rows, grad_rows, own_pieces, near_pieces
+    )
+
+    def block_grads(steps):
+        return expert_grads(
+            [chip ^ k for k in steps], chip_rows, hidden_rows, grad_rows, gate_rows[:, None],
+            joint_grad, active,
+        )
+
+    line_grads = block_grads([k ^ 1 for k in range(2, chips)])
+    side_lines = [swap(line_grads[2 * line], "dp", 4 * line + 4) for line in range(lines - 1)]
+    keep_lines_grad = [swap(line_grads[2 * line + 1], "dp", 4 * line + 4) for line in range(lines - 1)]
+    hidden_sum = quad_sum(hidden_part, *line_grads)
+    side_own, keep_own = block_grads([1, 0])
+    back_packed = return_packed(hidden_sum, side_own, keep_own)
     slot_two_grad = jnp.zeros((slots, home_rows), f32)
     for k in range(slots):
         rows = jnp.sum(
@@ -545,45 +687,33 @@
         slot_two_grad = lax.dynamic_update_index_in_dim(
             slot_two_grad, rows.reshape(home_rows), col ^ k, 0
         )
-    hidden_two_grad = unpack(back_packed[..., :width], gates_two)
+    hidden_two_grad = unpack([part[..., :width] for part in back_packed], gates_two)
     logit_two_grad = gate_back(slot_two_grad.T, gate_vals_two, matches_two, chosen_two).astype(bf16)
     hidden_two_grad = hidden_two_grad + dot_t(logit_two_grad, ffn_router)
     router_two_grad = t_dot(logit_two_grad, hidden_two)
     gain_two_grad = jnp.sum(hidden_two_grad * normed_two, axis=0)
     resid_grad = dy_home + norm_back(hidden_two_grad * gain_two, normed_two, scale_two)
 
-    ffn_packed = return_packed(quad_sum(dot_t(active, down_full)))
+    ffn_sum = quad_sum(after(ffn_part, *back_packed))
+
+    resid_grad_all = gather_rows(resid_grad.astype(bf16))
+    ffn_packed = return_packed(after(ffn_sum, resid_grad_all))
     out_home = (resid + unpack(ffn_packed, gates_two)).astype(bf16)
-
-    scaled_hidden = (hidden_rows.astype(f32) * gate_rows[:, None]).astype(bf16)
-    scaled_grad = (grad_rows.astype(f32) * gate_rows[:, None]).astype(bf16)
-
-    def chunk_grad(k):
-        start = (chip ^ k) * chip_rows
-        left = lax.dynamic_slice_in_dim(scaled_hidden, start, chip_rows, 1)
-        right = lax.dynamic_slice_in_dim(scaled_grad, start, chip_rows, 1)
-        return jnp.concatenate(
-            [t_dot(left, joint_grad).astype(bf16), t_dot(right, active).astype(bf16)], axis=1
-        )
-
-    chunk_grads = [chunk_grad(k) for k in range(chips)]
-    side_lines = [swap(chunk_grads[2 * line + 1], "dp", 4 * line) for line in range(1, lines)]
-    keep_lines_grad = [swap(chunk_grads[2 * line], "dp", 4 * line) for line in range(1, lines)]
-
-    resid_grad_low = after(resid_grad.astype(bf16), *chunk_grads[2:])
-    resid_grad_all = gather_rows(resid_grad_low)
     out_part = t_dot(resid_grad_all, gated_vals).astype(bf16)
-    vals_grad = dot(resid_grad_all, out_full)
-    vals_grad = after(vals_grad, out_part, *chunk_grads[:2], *side_lines)
+    vals_grad = after(dot(resid_grad_all, out_full), out_part, *side_lines)
     query_grad, key_grad, value_grad, slot_part_one = attention_backward(
         lens, query_rot, key_rot, kv_part, attn_vals, vals_grad, tables, gates_wide, log_total,
         own_heads, group_rows,
     )
     kv_grad = jnp.concatenate([key_grad, value_grad], axis=1)
     hidden_one_part = dot_t(query_grad, query_full) + dot_t(kv_grad, kv_full)
+    hidden_one_part = after(hidden_one_part.astype(bf16), *ffn_packed)
+    query_part_grad = t_dot(after(hidden_one, hidden_one_part), query_grad).astype(bf16)
+    kv_part_grad = t_dot(hidden_one, kv_grad).astype(bf16)
     back_one = scatter_rows(
-        jnp.concatenate([hidden_one_part.astype(bf16), slot_part_one.astype(bf16)], axis=1)
-    )
+        jnp.concatenate([hidden_one_part, slot_part_one.astype(bf16)], axis=1)
+    )
+    back_one = after(back_one, query_part_grad, kv_part_grad)
     hidden_one_grad, slot_one_grad = back_one[:, :width], back_one[:, width : width + slots]
 
     def own(value):
@@ -605,7 +735,7 @@
     results = lax.all_to_all(results, "dp", split_axis=0, concat_axis=0, tiled=True)
     results = results.transpose(1, 0, 2, 3).reshape(2, micro, tok_rows, width)
 
-    side_grad, keep_grad = chunk_grads[1].astype(f32), chunk_grads[0].astype(f32)
+    side_grad, keep_grad = side_own.astype(f32), keep_own.astype(f32)
     for line in range(lines - 1):
         side_grad = side_grad + side_lines[line].astype(f32)
         keep_grad = keep_grad + keep_lines_grad[line].astype(f32)
@@ -622,11 +752,11 @@
     down_grad = jnp.concatenate([b[:, 2 * quarter :] for b in blocks], axis=1).astype(f32)
 
     def reduced(value):
-        return lax.psum_scatter(value.astype(bf16), "dp", scatter_dimension=0, tiled=True)
+        return lax.psum_scatter(value, "dp", scatter_dimension=0, tiled=True)
 
     out_grad = slots_of(reduced(out_part)).astype(f32)
-    query_out = slots_of(reduced(t_dot(hidden_one, query_grad))).astype(f32)
-    kv_own = reduced(t_dot(hidden_one, kv_grad))
+    query_out = slots_of(reduced(query_part_grad)).astype(f32)
+    kv_own = reduced(kv_part_grad)
     key_part, value_part = kv_own[:, :own_width], kv_own[:, own_width:]
     first_back = lax.ppermute(
         jnp.where(even_col, key_part, value_part), "expert", [(b, a) for a, b in first_pairs]

time: 1260 us -> 1310 us (1.040)
  matrix products: 239 us -> 84.1 us
  waiting for transfers between devices: 628 us -> 750 us
  Pallas kernels: 58.7 us -> 178 us
  other arithmetic: 118 us -> 89.6 us
    pallas_call x0 -> x3, Pallas kernels: none -> 118 us  [the longest x1 70.4 us: expert_rows(): pl.pallas_call(expert_kernel, grid_spec=pltpu.PrefetchScalarGridSpec(num_...]
    ppermute x76, waiting for transfers between devices: 601 us -> 712 us  [swap(): return lax.ppermute(value, axis, [(i, i ^ step) for i in range(count)])]
    dot_general x13 -> x5, matrix products: 78.6 us -> 21.7 us  [t_dot(): lax.dot_general(left, right, (((0,), (0,)), ((), ())), preferred_element_...]
    dot_general x7 -> x5, matrix products: 76.4 us -> 25.6 us  [dot(): return jnp.dot(left, right, preferred_element_type=f32)]
    dot_general x7 -> x5, matrix products: 67.7 us -> 24.3 us  [dot_t(): lax.dot_general(left, right, (((1,), (1,)), ((), ())), preferred_element_...]
    all_to_all x1, waiting for transfers between devices: 0.01 us -> 15.3 us  [local(): lax.all_to_all(both.transpose(1, 0, 2, 3), 'dp', split_axis=0, concat_axi...]
  transfers between devices with their start and end apart: 88 -> 88, of which waited for: 48 -> 49; matrix products, arithmetic and copies ran while one was open for 26% -> 18% of each run, Pallas kernels for 5% -> 6%
where the time goes in v3:
time: 1310 us; the launch traced here: 1300 us
  waiting for transfers between devices  750 us (57%)
  Pallas kernels  178 us (14%)
  starting transfers between devices  94.5 us (7%)
  other arithmetic  89.6 us (7%)
  local copies, waits for them, and re-layouts  89.1 us (7%)
  matrix products  84.1 us (6%)
  between operations  16.8 us (1%)
    ppermute x76, waiting for transfers between devices, swap(): return lax.ppermute(value, axis, [(i, i ^ step) for i in range(count)])  712 us
    ppermute x76, starting transfers between devices, swap(): return lax.ppermute(value, axis, [(i, i ^ step) for i in range(count)])  79.4 us
    pallas_call x1, Pallas kernels, expert_rows(): pl.pallas_call(expert_kernel, grid_spec=pltpu.PrefetchScalarGridSpec(num_...  70.4 us
    pallas_call x2, Pallas kernels, expert_grads(): pl.pallas_call(expert_grad_kernel, grid_spec=pltpu.PrefetchScalarGridSpec...  48 us
    pallas_call x1, Pallas kernels, attention_backward(): pl.pallas_call(backward_kernel, grid_spec=pltpu.PrefetchScalarGridSpec(nu...  29.9 us
    pallas_call x1, Pallas kernels, attention_forward(): pl.pallas_call(forward_kernel, grid_spec=pltpu.PrefetchScalarGridSpec(num...  29.4 us
  transfers between devices with their start and end apart: 88, of which 49 were waited for; matrix products, arithmetic and copies ran while one was open for 18% of the time, Pallas kernels for 6%

profile of v3, /device:TPU:8, one launch (start us, length us, event | category | flops | bytes accessed | tf_op | source)
XLA Modules:
  0.0 1301.4 jit_solution(1749776083223813687)
XLA Ops:
  37.1 10.9 collective-permute-done.6
  58.7 15.3 %all-to-all-done = bf16[8,4,8,2048]{3,2,1,0:T(8,128)(2,1)S(1)} async-done(((bf16[8,4,8,2048]{3,2,1,0:T(8,128)(2,1)}), bf16[8,4,8,2048]{3,2,1,0:T(8,128)(2,1)S(1)}, u32[]{:S(2)}, u32[]{:S(2)}) %all-to-all-start) | async-done | bytes 1048608 | tf_op jit(solution)/shard_map/all_to_all | solution.py:459
  86.6 9.0 collective-permute-done
  97.5 21.4 %collective-permute-done.1 = bf16[2,64,2048]{2,1,0:T(8,128)(2,1)S(1)} collective-permute-done((bf16[2,64,2048]{2,1,0:T(8,128)(2,1)}, bf16[2,64,2048]{2,1,0:T(8,128)(2,1)S(1)}, u32[]{:S(2)}, u32[]{:S(2)}) %collective-permute-start.1) | collective-permute-done | bytes 524320 | tf_op jit(solution)/shard_map/ppermute | solution.py:35
  143.0 9.6 collective-permute-done.15
  182.8 20.8 %collective-permute-done.12 = bf16[2,48,2048]{2,1,0:T(8,128)(2,1)S(1)} collective-permute-done((bf16[2,48,2048]{2,1,0:T(8,128)(2,1)S(1)}, bf16[2,48,2048]{2,1,0:T(8,128)(2,1)S(1)}, u32[]{:S(2)}, u32[]{:S(2)}) %collective-permute-start.12) | collective-permute-done | bytes 393248 | tf_op jit(solution)/shard_map/ppermute | solution.py:35
  216.0 116.2 %collective-permute-done.21 = bf16[384,2048]{1,0:T(8,128)(2,1)} collective-permute-done((bf16[384,2048]{1,0:T(8,128)(2,1)}, bf16[384,2048]{1,0:T(8,128)(2,1)}, u32[]{:S(2)}, u32[]{:S(2)}) %collective-permute-start.21) | collective-permute-done | bytes 1572896 | tf_op jit(solution)/shard_map/ppermute | solution.py:35
  348.4 10.5 fusion.148.query
  358.9 29.4 %attention_forward.1 = (bf16[512,2048]{1,0:T(8,128)(2,1)}, bf16[512,2048]{1,0:T(8,128)(2,1)}, bf16[512,2048]{1,0:T(8,128)(2,1)}, bf16[512,512]{1,0:T(8,128)(2,1)...) custom-call(s32[2]{0:T(128)} %copy-done.44, f32[512,2048]{1,0:T(8,128)} %fusion.148.query, ...), custom_call_target="tpu_custom_call" | custom-call | flops 1073741824 | bytes 14680064 | tf_op jit(solution)/shard_map/attention_forward/pallas_call | solution.py:186
  405.9 27.6 %collective-permute-done.19 = bf16[2,64,2048]{2,1,0:T(8,128)(2,1)S(1)} collective-permute-done((bf16[2,64,2048]{2,1,0:T(8,128)(2,1)S(1)}, bf16[2,64,2048]{2,1,0:T(8,128)(2,1)S(1)}, u32[]{:S(2)}, u32[]{:S(2)}) %collective-permute-start.19) | collective-permute-done | bytes 524320 | tf_op jit(solution)/shard_map/ppermute | solution.py:35
  433.5 9.5 collective-permute-done.18
  451.7 24.1 %collective-permute-done.25 = bf16[2,48,2048]{2,1,0:T(8,128)(2,1)S(1)} collective-permute-done((bf16[2,48,2048]{2,1,0:T(8,128)(2,1)S(1)}, bf16[2,48,2048]{2,1,0:T(8,128)(2,1)S(1)}, u32[]{:S(2)}, u32[]{:S(2)}) %collective-permute-start.25) | collective-permute-done | bytes 393248 | tf_op jit(solution)/shard_map/ppermute | solution.py:35
  483.1 33.9 %collective-permute-done.27 = bf16[384,2048]{1,0:T(8,128)(2,1)} collective-permute-done((bf16[384,2048]{1,0:T(8,128)(2,1)}, bf16[384,2048]{1,0:T(8,128)(2,1)}, u32[]{:S(2)}, u32[]{:S(2)}) %collective-permute-start.27) | collective-permute-done | bytes 1572896 | tf_op jit(solution)/shard_map/ppermute | solution.py:35
  540.9 41.8 %collective-permute-done.35.refs_3_ = bf16[256,4224]{1,0:T(8,128)(2,1)} collective-permute-done((bf16[256,4224]{1,0:T(8,128)(2,1)}, bf16[256,4224]{1,0:T(8,128)(2,1)}, u32[]{:S(2)}, u32[]{:S(2)}) %collective-permute-start.35) | collective-permute-done | bytes 2162720 | tf_op jit(solution)/shard_map/ppermute | solution.py:35
  582.7 70.4 %expert_rows.1 = (bf16[1536,2048]{1,0:T(8,128)(2,1)}, bf16[1536,2176]{1,0:T(8,128)(2,1)}, bf16[1536,1408]{1,0:T(8,128)(2,1)}, bf16[1536,2816]{1,0:T(8,128)(2,1)}) custom-call(s32[2]{0:T(128)} %pad_add_fusion.1.place_ref, bf16[1536,2048]{1,0:T(8,128)(2,1)} %pad_maximum_fusion.1.hidden, bf16[1536,2048]{1,0:T(8,128)(2,1)} %pad_maximum_fusion.grad, ...), custom_call_target="tpu_custom_call" | custom-call | flops 53150220288 | bytes 55050240 | tf_op jit(solution)/shard_map/expert_rows/pallas_call | solution.py:338
  664.9 24.4 %expert_grads.2 = (bf16[512,4224]{1,0:T(8,128)(2,1)}, bf16[512,4224]{1,0:T(8,128)(2,1)}) custom-call(s32[4]{0:T(128)S(1)} %get-tuple-element.218.order, bf16[1536,2048]{1,0:T(8,128)(2,1)} %pad_maximum_fusion.1.hidden, bf16[1536,2048]{1,0:T(8,128)(2,1)} %pad_maximum_fusion.grad, f32[1536,1]{1,0:T(8,128)S(1)} %broadcast_in_dim.398.gates, ...), custom_call_target="tpu_custom_call" | custom-call | flops 13287555072 | bytes 27918336 | tf_op jit(solution)/shard_map/expert_grads/pallas_call | solution.py:394
  689.8 12.1 collective-permute-done.42
  709.7 23.6 %expert_grads.3 = (bf16[512,4224]{1,0:T(8,128)(2,1)S(1)}, bf16[512,4224]{1,0:T(8,128)(2,1)}) custom-call(s32[4]{0:T(128)S(1)} %get-tuple-element.219.order, bf16[1536,2048]{1,0:T(8,128)(2,1)} %pad_maximum_fusion.1.hidden, bf16[1536,2048]{1,0:T(8,128)(2,1)} %pad_maximum_fusion.grad, f32[1536,1]{1,0:T(8,128)S(1)} %broadcast_in_dim.398.gates, ...), custom_call_target="tpu_custom_call" | custom-call | flops 13287555072 | bytes 27918336 | tf_op jit(solution)/shard_map/expert_grads/pallas_call | solution.py:394
  759.2 16.1 %collective-permute-done.49 = bf16[2,64,2048]{2,1,0:T(8,128)(2,1)S(1)} collective-permute-done((bf16[2,64,2048]{2,1,0:T(8,128)(2,1)S(1)}, bf16[2,64,2048]{2,1,0:T(8,128)(2,1)S(1)}, u32[]{:S(2)}, u32[]{:S(2)}) %collective-permute-start.49) | collective-permute-done | bytes 524320 | tf_op jit(solution)/shard_map/ppermute | solution.py:35
  775.4 17.8 %collective-permute-done.50 = bf16[2,64,2048]{2,1,0:T(8,128)(2,1)S(1)} collective-permute-done((bf16[2,64,2048]{2,1,0:T(8,128)(2,1)S(1)}, bf16[2,64,2048]{2,1,0:T(8,128)(2,1)S(1)}, u32[]{:S(2)}, u32[]{:S(2)}) %collective-permute-start.50) | collective-permute-done | bytes 524320 | tf_op jit(solution)/shard_map/ppermute | solution.py:35
  793.3 9.5 collective-permute-done.51
  816.1 29.9 %attention_backward.1 = (bf16[512,2048]{1,0:T(8,128)(2,1)}, bf16[512,512]{1,0:T(8,128)(2,1)}, bf16[512,512]{1,0:T(8,128)(2,1)}, f32[512,128]{1,0:T(8,128)}) custom-call(s32[2]{0:T(128)} %copy-done.44, bf16[512,2048]{1,0:T(8,128)(2,1)} %get-tuple-element.78.query, bf16[512,512]{1,0:T(8,128)(2,1)} %get-tuple-element.79.key, ...), custom_call_target="tpu_custom_call" | custom-call | flops 2684354560 | bytes 14680064 | tf_op jit(solution)/shard_map/attention_backward/pallas_call | solution.py:217
  896.1 9.8 add_convert_fusion.2
  905.9 149.9 %collective-permute-done.48 = bf16[384,2048]{1,0:T(8,128)(2,1)S(1)} collective-permute-done((bf16[384,2048]{1,0:T(8,128)(2,1)}, bf16[384,2048]{1,0:T(8,128)(2,1)S(1)}, u32[]{:S(2)}, u32[]{:S(2)}) %collective-permute-start.48) | collective-permute-done | bytes 1572896 | tf_op jit(solution)/shard_map/ppermute | solution.py:35
  1075.3 12.9 collective-permute-done.53
  1088.2 19.9 %collective-permute-done.54 = bf16[2,48,2048]{2,1,0:T(8,128)(2,1)S(1)} collective-permute-done((bf16[2,48,2048]{2,1,0:T(8,128)(2,1)S(1)}, bf16[2,48,2048]{2,1,0:T(8,128)(2,1)S(1)}, u32[]{:S(2)}, u32[]{:S(2)}) %collective-permute-start.54) | collective-permute-done | bytes 393248 | tf_op jit(solution)/shard_map/ppermute | solution.py:35
  1126.2 11.1 collective-permute-done.58
  1137.3 8.7 collective-permute-done.57
  1181.2 14.2 %collective-permute-done.63 = f32[10,2048]{1,0:T(8,128)S(1)} collective-permute-done((f32[10,2048]{1,0:T(8,128)S(1)}, f32[10,2048]{1,0:T(8,128)S(1)}, u32[]{:S(2)}, u32[]{:S(2)}) %collective-permute-start.63) | collective-permute-done | bytes 81952 | tf_op jit(solution)/shard_map/ppermute | solution.py:35
  1202.2 11.1 collective-permute-done.70
  1245.4 13.5 %collective-permute-done.68 = bf16[256,512]{1,0:T(8,128)(2,1)S(1)} collective-permute-done((bf16[256,512]{1,0:T(8,128)(2,1)S(1)}, bf16[256,512]{1,0:T(8,128)(2,1)S(1)}, u32[]{:S(2)}, u32[]{:S(2)}) %collective-permute-start.68) | collective-permute-done | bytes 262176 | tf_op jit(solution)/shard_map/ppermute | solution.py:35
  1274.9 11.2 collective-permute-done.65
  (544 shorter events, 438.5 us)
Async XLA Ops:
  7.2 335.0 %all-gather.6.cloned.1.call-start = ((), (), s32[]{:S(2)}) async-start(), calls=%async_computation.6 | async-start | bytes 4718592 | tf_op jit(solution)/shard_map/all_gather | solution.py:505
  24.0 324.4 %all-gather.4.cloned.1.call-start = ((), (), s32[]{:S(2)}) async-start(), calls=%async_computation.5 | async-start | bytes 9437184 | tf_op jit(solution)/shard_map/all_gather | solution.py:506
  58.6 329.7 %all-gather.8.cloned.1.call-start = ((), (), s32[]{:S(2)}) async-start(), calls=%async_computation.7 | async-start | bytes 9437184 | tf_op jit(solution)/shard_map/all_gather | solution.py:620
  81.0 37.9 %collective-permute-start.1 = (bf16[2,64,2048]{2,1,0:T(8,128)(2,1)}, bf16[2,64,2048]{2,1,0:T(8,128)(2,1)S(1)}, u32[]{:S(2)}, u32[]{:S(2)}) collective-permute-start(bf16[2,64,2048]{2,1,0:T(8,128)(2,1)} %get-tuple-element.120), channel_id=1, source_target_pairs={{0,2},{1,3},{2,0},{3,1},{4,6},{5,7},{6,4},{7,5},{8,10},{9,11},{10,... | collective-permute-start | bytes 1572872 | tf_op jit(solution)/shard_map/ppermute | solution.py:35
  83.9 43.1 %collective-permute-start.2 = (bf16[2,64,2048]{2,1,0:T(8,128)(2,1)}, bf16[2,64,2048]{2,1,0:T(8,128)(2,1)S(1)}, u32[]{:S(2)}, u32[]{:S(2)}) collective-permute-start(bf16[2,64,2048]{2,1,0:T(8,128)(2,1)} %get-tuple-element.120), channel_id=1, source_target_pairs={{0,3},{1,2},{2,1},{3,0},{4,7},{5,6},{6,5},{7,4},{8,11},{9,10},{10,... | collective-permute-start | bytes 1572872 | tf_op jit(solution)/shard_map/ppermute | solution.py:35
  157.3 1039.5 %reduce-scatter.8.cloned.1.call-start = ((), (), s32[]{:S(2)}) async-start(), calls=%async_computation.10 | async-start | bytes 4718592 | tf_op jit(solution)/shard_map/reduce_scatter | solution.py:755
  170.5 161.7 %collective-permute-start.3 = (bf16[256,8448]{1,0:T(8,128)(2,1)}, bf16[256,8448]{1,0:T(8,128)(2,1)}, u32[]{:S(2)}, u32[]{:S(2)}) collective-permute-start(bf16[256,8448]{1,0:T(8,128)(2,1)} %get-tuple-element.145), channel_id=1, source_target_pairs={{0,8},{4,12},{8,0},{12,4},{16,24},{20,28},{24,16},{28,20},{1,9},{5... | collective-permute-start | bytes 12976136 | tf_op jit(solution)/shard_map/ppermute | solution.py:35
  177.1 155.1 %collective-permute-start.4 = (bf16[256,8448]{1,0:T(8,128)(2,1)}, bf16[256,8448]{1,0:T(8,128)(2,1)}, u32[]{:S(2)}, u32[]{:S(2)}) collective-permute-start(bf16[256,8448]{1,0:T(8,128)(2,1)} %get-tuple-element.144.refs_0_), channel_id=1, source_target_pairs={{0,16},{4,20},{8,24},{12,28},{16,0},{20,4},{24,8},{28,12},{1,17},{... | collective-permute-start | bytes 12976136 | tf_op jit(solution)/shard_map/ppermute | solution.py:35
  212.3 119.9 %collective-permute-start.21 = (bf16[384,2048]{1,0:T(8,128)(2,1)}, bf16[384,2048]{1,0:T(8,128)(2,1)}, u32[]{:S(2)}, u32[]{:S(2)}) collective-permute-start(bf16[384,2048]{1,0:T(8,128)(2,1)} %bitcast.40), channel_id=1, source_target_pairs={{0,8},{4,12},{8,0},{12,4},{16,24},{20,28},{24,16},{28,20},{1,9},{5... | collective-permute-start | bytes 4718600 | tf_op jit(solution)/shard_map/ppermute | solution.py:35
  216.0 183.9 %collective-permute-start.20 = (bf16[384,2048]{1,0:T(8,128)(2,1)}, bf16[384,2048]{1,0:T(8,128)(2,1)}, u32[]{:S(2)}, u32[]{:S(2)}) collective-permute-start(bf16[384,2048]{1,0:T(8,128)(2,1)} %bitcast.40), channel_id=1, source_target_pairs={{0,4},{4,0},{8,12},{12,8},{16,20},{20,16},{24,28},{28,24},{1,5},{5... | collective-permute-start | bytes 4718600 | tf_op jit(solution)/shard_map/ppermute | solution.py:35
  332.2 67.8 %collective-permute-start.22 = (bf16[384,2048]{1,0:T(8,128)(2,1)}, bf16[384,2048]{1,0:T(8,128)(2,1)}, u32[]{:S(2)}, u32[]{:S(2)}) collective-permute-start(bf16[384,2048]{1,0:T(8,128)(2,1)} %collective-permute-done.21), channel_id=1, source_target_pairs={{0,4},{4,0},{8,12},{12,8},{16,20},{20,16},{24,28},{28,24},{1,5},{5... | collective-permute-start | bytes 4718600 | tf_op jit(solution)/shard_map/ppermute | solution.py:35
  336.8 51.5 %collective-permute-start.13 = (bf16[256,4224]{1,0:T(8,128)(2,1)}, bf16[256,4224]{1,0:T(8,128)(2,1)}, u32[]{:S(2)}, u32[]{:S(2)}) collective-permute-start(bf16[256,4224]{1,0:T(8,128)(2,1)} %get-tuple-element.140), channel_id=1, source_target_pairs={{0,16},{4,20},{8,24},{12,28},{16,0},{20,4},{24,8},{28,12},{1,17},{... | collective-permute-start | bytes 6488072 | tf_op jit(solution)/shard_map/ppermute | solution.py:35
  397.8 45.3 %collective-permute-start.18 = (bf16[2,64,2048]{2,1,0:T(8,128)(2,1)S(1)}, bf16[2,64,2048]{2,1,0:T(8,128)(2,1)S(1)}, u32[]{:S(2)}, u32[]{:S(2)}) collective-permute-start(bf16[2,64,2048]{2,1,0:T(8,128)(2,1)S(1)} %get-tuple-element.143), channel_id=1, source_target_pairs={{0,2},{1,3},{2,0},{3,1},{4,6},{5,7},{6,4},{7,5},{8,10},{9,11},{10,... | collective-permute-start | bytes 1572872 | tf_op jit(solution)/shard_map/ppermute | solution.py:35
  399.2 43.9 %collective-permute-start.17 = (bf16[2,64,2048]{2,1,0:T(8,128)(2,1)S(1)}, bf16[2,64,2048]{2,1,0:T(8,128)(2,1)S(1)}, u32[]{:S(2)}, u32[]{:S(2)}) collective-permute-start(bf16[2,64,2048]{2,1,0:T(8,128)(2,1)S(1)} %get-tuple-element.141), channel_id=1, source_target_pairs={{0,1},{1,0},{2,3},{3,2},{4,5},{5,4},{6,7},{7,6},{8,9},{9,8},{10,11... | collective-permute-start | bytes 1572872 | tf_op jit(solution)/shard_map/ppermute | solution.py:35
  483.1 50.7 %collective-permute-start.26 = (bf16[384,2048]{1,0:T(8,128)(2,1)}, bf16[384,2048]{1,0:T(8,128)(2,1)}, u32[]{:S(2)}, u32[]{:S(2)}) collective-permute-start(bf16[384,2048]{1,0:T(8,128)(2,1)} %bitcast.62), channel_id=1, source_target_pairs={{0,4},{4,0},{8,12},{12,8},{16,20},{20,16},{24,28},{28,24},{1,5},{5... | collective-permute-start | bytes 4718600 | tf_op jit(solution)/shard_map/ppermute | solution.py:35
  532.9 49.8 %collective-permute-start.37 = (bf16[256,4224]{1,0:T(8,128)(2,1)}, bf16[256,4224]{1,0:T(8,128)(2,1)}, u32[]{:S(2)}, u32[]{:S(2)}) collective-permute-start(bf16[256,4224]{1,0:T(8,128)(2,1)} %get-tuple-element.140), channel_id=1, source_target_pairs={{0,4},{4,0},{8,12},{12,8},{16,20},{20,16},{24,28},{28,24},{1,5},{5... | collective-permute-start | bytes 6488072 | tf_op jit(solution)/shard_map/ppermute | solution.py:35
  533.3 49.4 %collective-permute-start.35 = (bf16[256,4224]{1,0:T(8,128)(2,1)}, bf16[256,4224]{1,0:T(8,128)(2,1)}, u32[]{:S(2)}, u32[]{:S(2)}) collective-permute-start(bf16[256,4224]{1,0:T(8,128)(2,1)} %get-tuple-element.139), channel_id=1, source_target_pairs={{0,16},{4,20},{8,24},{12,28},{16,0},{20,4},{24,8},{28,12},{1,17},{... | collective-permute-start | bytes 6488072 | tf_op jit(solution)/shard_map/ppermute | solution.py:35
  533.8 48.9 %collective-permute-start.38 = (bf16[256,4224]{1,0:T(8,128)(2,1)}, bf16[256,4224]{1,0:T(8,128)(2,1)}, u32[]{:S(2)}, u32[]{:S(2)}) collective-permute-start(bf16[256,4224]{1,0:T(8,128)(2,1)} %constant_dynamic-slice_fusion.21), channel_id=1, source_target_pairs={{0,4},{4,0},{8,12},{12,8},{16,20},{20,16},{24,28},{28,24},{1,5},{5... | collective-permute-start | bytes 6488072 | tf_op jit(solution)/shard_map/ppermute | solution.py:35
  533.8 48.8 %collective-permute-start.39 = (bf16[256,4224]{1,0:T(8,128)(2,1)}, bf16[256,4224]{1,0:T(8,128)(2,1)}, u32[]{:S(2)}, u32[]{:S(2)}) collective-permute-start(bf16[256,4224]{1,0:T(8,128)(2,1)} %collective-permute-done.13), channel_id=1, source_target_pairs={{0,4},{4,0},{8,12},{12,8},{16,20},{20,16},{24,28},{28,24},{1,5},{5... | collective-permute-start | bytes 6488072 | tf_op jit(solution)/shard_map/ppermute | solution.py:35
  663.1 38.9 %collective-permute-start.42 = (bf16[384,2176]{1,0:T(8,128)(2,1)}, bf16[384,2176]{1,0:T(8,128)(2,1)}, u32[]{:S(2)}, u32[]{:S(2)}) collective-permute-start(bf16[384,2176]{1,0:T(8,128)(2,1)} %add_convert_fusion.4), channel_id=1, source_target_pairs={{0,8},{4,12},{8,0},{12,4},{16,24},{20,28},{24,16},{28,20},{1,9},{5... | collective-permute-start | bytes 5013512 | tf_op jit(solution)/shard_map/ppermute | solution.py:35
  664.5 37.4 %collective-permute-start.40 = (bf16[384,2176]{1,0:T(8,128)(2,1)}, bf16[384,2176]{1,0:T(8,128)(2,1)}, u32[]{:S(2)}, u32[]{:S(2)}) collective-permute-start(bf16[384,2176]{1,0:T(8,128)(2,1)} %get-tuple-element.123), channel_id=1, source_target_pairs={{0,4},{4,0},{8,12},{12,8},{16,20},{20,16},{24,28},{28,24},{1,5},{5... | collective-permute-start | bytes 5013512 | tf_op jit(solution)/shard_map/ppermute | solution.py:35
  689.3 126.8 %collective-permute-start.55 = (bf16[512,4224]{1,0:T(8,128)(2,1)}, bf16[512,4224]{1,0:T(8,128)(2,1)}, u32[]{:S(2)}, u32[]{:S(2)}) collective-permute-start(bf16[512,4224]{1,0:T(8,128)(2,1)} %get-tuple-element.63), channel_id=1, source_target_pairs={{0,16},{4,20},{8,24},{12,28},{16,0},{20,4},{24,8},{28,12},{1,17},{... | collective-permute-start | bytes 12976136 | tf_op jit(solution)/shard_map/ppermute | solution.py:35
  755.5 37.8 %collective-permute-start.50 = (bf16[2,64,2048]{2,1,0:T(8,128)(2,1)S(1)}, bf16[2,64,2048]{2,1,0:T(8,128)(2,1)S(1)}, u32[]{:S(2)}, u32[]{:S(2)}) collective-permute-start(bf16[2,64,2048]{2,1,0:T(8,128)(2,1)S(1)} %bitcast.407), channel_id=1, source_target_pairs={{0,2},{1,3},{2,0},{3,1},{4,6},{5,7},{6,4},{7,5},{8,10},{9,11},{10,... | collective-permute-start | bytes 1572872 | tf_op jit(solution)/shard_map/ppermute | solution.py:35
  758.4 44.4 %collective-permute-start.51 = (bf16[2,64,2048]{2,1,0:T(8,128)(2,1)S(1)}, bf16[2,64,2048]{2,1,0:T(8,128)(2,1)S(1)}, u32[]{:S(2)}, u32[]{:S(2)}) collective-permute-start(bf16[2,64,2048]{2,1,0:T(8,128)(2,1)S(1)} %bitcast.408), channel_id=1, source_target_pairs={{0,3},{1,2},{2,1},{3,0},{4,7},{5,6},{6,5},{7,4},{8,11},{9,10},{10,... | collective-permute-start | bytes 1572872 | tf_op jit(solution)/shard_map/ppermute | solution.py:35
  855.3 372.5 %reduce-scatter.6.cloned.1.call-start = ((), (), s32[]{:S(2)}) async-start(), calls=%async_computation.9 | async-start | bytes 9437184 | tf_op jit(solution)/shard_map/reduce_scatter | solution.py:755
  874.8 187.6 %collective-permute-start.72 = (bf16[512,4224]{1,0:T(8,128)(2,1)}, bf16[512,4224]{1,0:T(8,128)(2,1)}, u32[]{:S(2)}, u32[]{:S(2)}) collective-permute-start(bf16[512,4224]{1,0:T(8,128)(2,1)} %get-tuple-element.64), channel_id=1, source_target_pairs={{0,16},{4,20},{8,24},{12,28},{16,0},{20,4},{24,8},{28,12},{1,17},{... | collective-permute-start | bytes 12976136 | tf_op jit(solution)/shard_map/ppermute | solution.py:35
  878.7 177.1 %collective-permute-start.46 = (bf16[384,2048]{1,0:T(8,128)(2,1)S(1)}, bf16[384,2048]{1,0:T(8,128)(2,1)}, u32[]{:S(2)}, u32[]{:S(2)}) collective-permute-start(bf16[384,2048]{1,0:T(8,128)(2,1)S(1)} %get-tuple-element.125), channel_id=1, source_target_pairs={{0,4},{4,0},{8,12},{12,8},{16,20},{20,16},{24,28},{28,24},{1,5},{5... | collective-permute-start | bytes 4718600 | tf_op jit(solution)/shard_map/ppermute | solution.py:35
  886.3 264.5 %collective-permute-start.73 = (bf16[512,4224]{1,0:T(8,128)(2,1)}, bf16[512,4224]{1,0:T(8,128)(2,1)}, u32[]{:S(2)}, u32[]{:S(2)}) collective-permute-start(bf16[512,4224]{1,0:T(8,128)(2,1)} %add_convert_fusion), channel_id=1, source_target_pairs={{0,8},{4,12},{8,0},{12,4},{16,24},{20,28},{24,16},{28,20},{1,9},{5... | collective-permute-start | bytes 12976136 | tf_op jit(solution)/shard_map/ppermute | solution.py:35
  895.5 160.3 %collective-permute-start.48 = (bf16[384,2048]{1,0:T(8,128)(2,1)}, bf16[384,2048]{1,0:T(8,128)(2,1)S(1)}, u32[]{:S(2)}, u32[]{:S(2)}) collective-permute-start(bf16[384,2048]{1,0:T(8,128)(2,1)} %add_convert_fusion.5), channel_id=1, source_target_pairs={{0,8},{4,12},{8,0},{12,4},{16,24},{20,28},{24,16},{28,20},{1,9},{5... | collective-permute-start | bytes 4718600 | tf_op jit(solution)/shard_map/ppermute | solution.py:35
  1061.8 46.3 %collective-permute-start.54 = (bf16[2,48,2048]{2,1,0:T(8,128)(2,1)S(1)}, bf16[2,48,2048]{2,1,0:T(8,128)(2,1)S(1)}, u32[]{:S(2)}, u32[]{:S(2)}) collective-permute-start(bf16[2,48,2048]{2,1,0:T(8,128)(2,1)S(1)} %bitcast.420), channel_id=1, source_target_pairs={{0,3},{1,2},{2,1},{3,0},{4,7},{5,6},{6,5},{7,4},{8,11},{9,10},{10,... | collective-permute-start | bytes 1179656 | tf_op jit(solution)/shard_map/ppermute | solution.py:35
  1155.8 58.7 %collective-permute-start.74 = (bf16[2,256,4224]{2,1,0:T(8,128)(2,1)}, bf16[2,256,4224]{2,1,0:T(8,128)(2,1)}, u32[]{:S(2)}, u32[]{:S(2)}) collective-permute-start(bf16[2,256,4224]{2,1,0:T(8,128)(2,1)} %fusion.1), channel_id=1, source_target_pairs={{0,4},{4,0},{8,12},{12,8},{16,20},{20,16},{24,28},{28,24},{1,5},{5... | collective-permute-start | bytes 12976136 | tf_op jit(solution)/shard_map/ppermute | solution.py:35
  1178.2 80.7 %reduce-scatter.4.cloned.1.call-start = ((), (), s32[]{:S(2)}) async-start(), calls=%async_computation.8 | async-start | bytes 9437184 | tf_op jit(solution)/shard_map/reduce_scatter | solution.py:755
  (115 other events, 3695.3 us)
Sparse Core Ops, SparseCore 0:
  24.1 38.6 all-gather.5
  65.3 63.2 all-gather.3
  157.5 90.9 all-gather.7
  855.4 67.3 reduce-scatter.7
  927.1 105.0 reduce-scatter.5
  1182.2 73.7 reduce-scatter.3

commit v4 on v3

--- a/solution.py
+++ b/solution.py
@@ -1,3 +1,5 @@
+import functools
+
 import jax
 import jax.numpy as jnp
 from jax import lax
@@ -287,10 +289,9 @@
         copies = []
         for k in range(piece_count):
             base = (chip ^ k) * (2 * rows)
-            own, near = own_pieces[k], near_pieces[k]
-            if own.shape[1] != columns:
-                own = own.at[:, pl.ds(pl.multiple_of(core * columns, HDIM), columns)]
-            for number, (piece, part) in enumerate(((own, core), (near, 1 - core))):
+            for number, (piece, part) in enumerate(
+                ((own_pieces[k], core), (near_pieces[k], 1 - core))
+            ):
                 start = pl.multiple_of(base + part * rows, 16)
                 copies.append(
                     pltpu.make_async_copy(
@@ -371,7 +372,7 @@
     step = pl.program_id(0)
     for number, out in enumerate(outs):
 
-        @pl.when(step // 2 == number)
+        @pl.when(step == number)
         def _():
             for start, size in unit_blocks(2 * units):
                 out[:, start : start + size] = t_dot(left, joint[:, start : start + size]).astype(bf16)
@@ -398,11 +399,10 @@
             grid=(2 * count,),
             in_specs=[column, column, whole(1), whole(2 * units), whole(units)],
             out_specs=[
-                pl.BlockSpec((half, 3 * units), lambda i, at, n=n: (jnp.clip(i - 2 * n, 0, 1), 0))
-                for n in range(count)
+                pl.BlockSpec((half, 3 * units), lambda i, at: (0, 0)) for _ in range(2 * count)
             ],
         ),
-        out_shape=[jax.ShapeDtypeStruct((chunk_rows, 3 * units), bf16)] * count,
+        out_shape=[jax.ShapeDtypeStruct((half, 3 * units), bf16)] * (2 * count),
         compiler_params=pltpu.CompilerParams(vmem_limit_bytes=48 * 2**20),
         cost_estimate=pl.CostEstimate(
             flops=2 * count * chunk_rows * rows * 3 * units,
@@ -457,23 +457,55 @@
 
     both = jnp.stack([tokens, cotangent]).reshape(2 * micro, dp_count, piece_rows, width)
     both = lax.all_to_all(both.transpose(1, 0, 2, 3), "dp", split_axis=0, concat_axis=0, tiled=True)
+    def quarter_of(half, part):
+        start = (2 * half + part) * quarter
+        return jnp.concatenate(
+            [
+                lax.dynamic_slice_in_dim(gate_up_weight[0], start, quarter, 1),
+                lax.dynamic_slice_in_dim(gate_up_weight[0], FF + start, quarter, 1),
+                lax.dynamic_slice_in_dim(down_weight[0], start, quarter, 1),
+            ],
+            axis=1,
+        )
+
+    parts = (1 - core, core)
+    keep_pair = [quarter_of(side, part) for part in parts]
+    send_pair = [quarter_of(1 - side, part) for part in parts]
+    both, keep_pair, send_pair, kv_in, query_in, out_in = lax.optimization_barrier(
+        (both, keep_pair, send_pair, kv_weight, query_weight[0], attn_out_weight[0])
+    )
+    side_pair = [swap(piece, "dp", 2) for piece in send_pair]
+    line_steps = [4 * line for line in range(1, lines)]
+    keep_lines = [[swap(piece, "dp", step) for step in line_steps] for piece in keep_pair]
+    side_lines = [[swap(piece, "dp", step) for step in line_steps] for piece in side_pair]
+    pairs = [keep_pair, side_pair]
+    for line in range(lines - 1):
+        pairs += [[part[line] for part in keep_lines], [part[line] for part in side_lines]]
+    near_pieces = [swap(pair[0], "dp", 1) for pair in pairs]
+    own_pieces = [pair[1] for pair in pairs]
+
     both = both.transpose(1, 0, 2, 3).reshape(2, micro, tok_rows, width)
     deal = (dealing[:, :, None] == jnp.arange(tok_rows, dtype=jnp.int32)).astype(bf16)
     work = jnp.einsum("mtr,bmrd->bmtd", deal, both, preferred_element_type=f32)
     x_home = work[0].reshape(home_rows, width)
     dy_home = work[1].reshape(home_rows, width)
 
-    def columns_of(shard):
-        pieces = shard.reshape(shard_rows, slots, own_width)
-        parts = [
-            swap(lax.dynamic_index_in_dim(pieces, col ^ k, 1, keepdims=False), "expert", k)
-            if k
-            else lax.dynamic_index_in_dim(pieces, col, 1, keepdims=False)
-            for k in range(slots)
-        ]
-        out = jnp.zeros((shard_rows, query_width), shard.dtype)
-        for k, part in enumerate(parts):
-            out = lax.dynamic_update_slice_in_dim(out, part, (col ^ k) * own_width, 1)
+    def columns_of(*shards):
+        pieces = [shard.reshape(shard_rows, slots, own_width) for shard in shards]
+        out = jnp.zeros((shard_rows, len(shards) * query_width), shards[0].dtype)
+        for k in range(slots):
+            part = jnp.concatenate(
+                [lax.dynamic_index_in_dim(piece, col ^ k, 1, keepdims=False) for piece in pieces],
+                axis=1,
+            )
+            part = swap(part, "expert", k) if k else part
+            for number in range(len(shards)):
+                out = lax.dynamic_update_slice_in_dim(
+                    out,
+                    part[:, number * own_width : (number + 1) * own_width],
+                    number * query_width + (col ^ k) * own_width,
+                    1,
+                )
         return out
 
     def slots_of(columns):
@@ -492,7 +524,7 @@
     second_pairs += [(c, 2 * (c - half_slots)) for c in range(half_slots, slots)]
     holds_keys = col < half_slots
     even_col = col % 2 == 0
-    low_kv, high_kv = kv_weight[:, :own_width], kv_weight[:, own_width:]
+    low_kv, high_kv = kv_in[:, :own_width], kv_in[:, own_width:]
     first_got = lax.ppermute(jnp.where(holds_keys, low_kv, high_kv), "expert", first_pairs)
     second_got = lax.ppermute(jnp.where(holds_keys, high_kv, low_kv), "expert", second_pairs)
     own_kv = jnp.concatenate(
@@ -503,38 +535,10 @@
         axis=1,
     )
     kv_full = lax.all_gather(own_kv, "dp", axis=0, tiled=True)
-    query_full = lax.all_gather(columns_of(query_weight[0]), "dp", axis=0, tiled=True)
-
-    def quarter_of(half, part):
-        start = (2 * half + part) * quarter
-        return [
-            lax.dynamic_slice_in_dim(gate_up_weight[0], start, quarter, 1),
-            lax.dynamic_slice_in_dim(gate_up_weight[0], FF + start, quarter, 1),
-            lax.dynamic_slice_in_dim(down_weight[0], start, quarter, 1),
-        ]
-
-    def half_of(half):
-        return jnp.concatenate(quarter_of(half, 0) + quarter_of(half, 1), axis=1)
-
-    def part_of(piece, part):
-        return lax.dynamic_slice_in_dim(piece, part * 3 * quarter, 3 * quarter, 1)
-
-    keep_side = half_of(side)
-    from_side = swap(half_of(1 - side), "dp", 2)
-    keep_lines = [swap(keep_side, "dp", 4 * line) for line in range(1, lines)]
-    from_lines = []
-    for line in range(1, lines):
-        other_part = swap(part_of(from_side, 1 - core), "dp", 4 * line)
-        from_lines.append((swap(part_of(from_side, core), "dp", 4 * line), other_part))
-
-    own_pieces = [keep_side, from_side]
-    near_pieces = [swap(part_of(piece, 1 - core), "dp", 1) for piece in own_pieces]
-    for line in range(lines - 1):
-        own_pieces += [keep_lines[line], from_lines[line][0]]
-        near_pieces += [
-            swap(part_of(keep_lines[line], 1 - core), "dp", 1),
-            swap(from_lines[line][1], "dp", 1),
-        ]
+    joint_full = lax.all_gather(
+        after(columns_of(query_in, out_in), side_pair[0], *keep_lines[0]), "dp", axis=0, tiled=True
+    )
+    query_full, out_full = joint_full[:, :query_width], joint_full[:, query_width:]
 
     positions = jnp.arange(group_rows, dtype=jnp.int32)
     first_len = lax.dynamic_index_in_dim(seq_lengths[:, :, 0], group, 1, keepdims=True)
@@ -614,13 +618,9 @@
     normed_one, scale_one = normalize(x_home)
     hidden_one_home = (normed_one * gain_one).astype(bf16)
     hidden_one_raw = gather_rows(hidden_one_home)
-    out_weight, dy_low = lax.optimization_barrier(
-        (attn_out_weight[0], dy_home.astype(bf16), hidden_one_raw)
-    )[:2]
-    out_full = lax.all_gather(columns_of(out_weight), "dp", axis=0, tiled=True)
-    grad_sent = send_packed(dy_low)
+    hidden_one = after(hidden_one_raw, side_pair[1], *keep_lines[1])
+    grad_sent = send_packed(after(dy_home.astype(bf16), hidden_one))
     grad_rows = quad_rows(grad_sent)
-    hidden_one = after(hidden_one_raw, from_side, *keep_lines)
     logits_one = dot(hidden_one, attn_router)
     gates_one, matches_one, chosen_one, gate_vals_one = route_gates(
         logits_one, attn_routes.reshape(all_rows, TOP), expert_table
@@ -641,8 +641,7 @@
     peak_table = lax.dynamic_update_slice_in_dim(
         jnp.full((slots, HEADS), very_low, f32), peaks, col * own_heads, 1
     )
-    peaks_all = spread(peak_table, jnp.maximum)
-    gated_vals = after(gated_vals, grad_sent, *[pair[1] for pair in from_lines])
+    gated_vals = after(gated_vals, grad_sent, *side_lines[0])
     attn_home = scatter_rows(dot_t(gated_vals, out_full))
 
     resid = x_home + attn_home
@@ -652,7 +651,8 @@
     gates_two, matches_two, chosen_two, gate_vals_two = route_gates(
         logits_two, home_routes.reshape(home_rows, TOP), expert_table
     )
-    hidden_rows = quad_rows(send_packed(after(hidden_two, grad_rows)))
+    hidden_sent = send_packed(after(hidden_two, grad_rows))
+    hidden_rows = quad_rows(after(hidden_sent, *side_lines[1], *near_pieces))
     gates_by_slot = gates_two.reshape(micro, tok_rows, slots)
     gate_parts = []
     for k in range(slots):
@@ -674,11 +674,21 @@
         )
 
     line_grads = block_grads([k ^ 1 for k in range(2, chips)])
-    side_lines = [swap(line_grads[2 * line], "dp", 4 * line + 4) for line in range(lines - 1)]
-    keep_lines_grad = [swap(line_grads[2 * line + 1], "dp", 4 * line + 4) for line in range(lines - 1)]
+    side_got, keep_got = [
+        [
+            [swap(line_grads[4 * line + 2 * which + part], "dp", 4 * line + 4) for line in range(lines - 1)]
+            for part in range(2)
+        ]
+        for which in range(2)
+    ]
     hidden_sum = quad_sum(hidden_part, *line_grads)
-    side_own, keep_own = block_grads([1, 0])
-    back_packed = return_packed(hidden_sum, side_own, keep_own)
+    own_grads = block_grads([1, 0])
+    back_packed = return_packed(hidden_sum, *own_grads)
+
+    def total(own, got):
+        return functools.reduce(jnp.add, [part.astype(f32) for part in [own] + got]).astype(bf16)
+
+    other_sums = [swap(total(own_grads[part], side_got[part]), "dp", 2) for part in range(2)]
     slot_two_grad = jnp.zeros((slots, home_rows), f32)
     for k in range(slots):
         rows = jnp.sum(
@@ -694,26 +704,31 @@
     gain_two_grad = jnp.sum(hidden_two_grad * normed_two, axis=0)
     resid_grad = dy_home + norm_back(hidden_two_grad * gain_two, normed_two, scale_two)
 
-    ffn_sum = quad_sum(after(ffn_part, *back_packed))
-
-    resid_grad_all = gather_rows(resid_grad.astype(bf16))
+    ffn_sum = quad_sum(after(ffn_part, hidden_sum))
+
+    resid_grad_low = after(resid_grad.astype(bf16), ffn_sum, *side_got[0])
+    resid_grad_all = after(gather_rows(resid_grad_low), *side_got[1])
     ffn_packed = return_packed(after(ffn_sum, resid_grad_all))
     out_home = (resid + unpack(ffn_packed, gates_two)).astype(bf16)
     out_part = t_dot(resid_grad_all, gated_vals).astype(bf16)
-    vals_grad = after(dot(resid_grad_all, out_full), out_part, *side_lines)
+    vals_grad = after(dot(resid_grad_all, out_full), out_part, *keep_got[0])
     query_grad, key_grad, value_grad, slot_part_one = attention_backward(
         lens, query_rot, key_rot, kv_part, attn_vals, vals_grad, tables, gates_wide, log_total,
         own_heads, group_rows,
     )
+    query_grad, key_grad, value_grad, slot_part_one = lax.optimization_barrier(
+        (query_grad, key_grad, value_grad, slot_part_one, ffn_packed, keep_got[1])
+    )[:4]
     kv_grad = jnp.concatenate([key_grad, value_grad], axis=1)
     hidden_one_part = dot_t(query_grad, query_full) + dot_t(kv_grad, kv_full)
-    hidden_one_part = after(hidden_one_part.astype(bf16), *ffn_packed)
-    query_part_grad = t_dot(after(hidden_one, hidden_one_part), query_grad).astype(bf16)
-    kv_part_grad = t_dot(hidden_one, kv_grad).astype(bf16)
+    hidden_one_part = after(hidden_one_part.astype(bf16), other_sums[0])
+    hidden_one_late = after(hidden_one, hidden_one_part)
+    query_part_grad = t_dot(hidden_one_late, query_grad).astype(bf16)
+    kv_part_grad = t_dot(after(hidden_one_late, query_part_grad), kv_grad).astype(bf16)
     back_one = scatter_rows(
         jnp.concatenate([hidden_one_part, slot_part_one.astype(bf16)], axis=1)
     )
-    back_one = after(back_one, query_part_grad, kv_part_grad)
+    back_one = after(back_one, query_part_grad, kv_part_grad, other_sums[1])
     hidden_one_grad, slot_one_grad = back_one[:, :width], back_one[:, width : width + slots]
 
     def own(value):
@@ -729,20 +744,10 @@
     gain_one_grad = jnp.sum(hidden_one_grad * normed_one, axis=0)
     in_home = resid_grad + norm_back(hidden_one_grad * gain_one, normed_one, scale_one)
 
-    results = jnp.stack([out_home, in_home.astype(bf16)]).reshape(2, micro, tok_rows, width)
-    results = jnp.einsum("mtr,bmtd->bmrd", deal, results, preferred_element_type=f32).astype(bf16)
-    results = results.reshape(2 * micro, dp_count, piece_rows, width).transpose(1, 0, 2, 3)
-    results = lax.all_to_all(results, "dp", split_axis=0, concat_axis=0, tiled=True)
-    results = results.transpose(1, 0, 2, 3).reshape(2, micro, tok_rows, width)
-
-    side_grad, keep_grad = side_own.astype(f32), keep_own.astype(f32)
-    for line in range(lines - 1):
-        side_grad = side_grad + side_lines[line].astype(f32)
-        keep_grad = keep_grad + keep_lines_grad[line].astype(f32)
-    other_grad = swap(side_grad.astype(bf16), "dp", 2)
-    pair = jnp.stack([keep_grad.astype(bf16), other_grad]).reshape(2, 2, shard_rows, 3 * quarter)
-    own_pair = lax.dynamic_index_in_dim(pair, core, 1, keepdims=False)
-    near_pair = swap(lax.dynamic_index_in_dim(pair, 1 - core, 1, keepdims=False), "dp", 1)
+    keep_sums = [total(own_grads[2 + part], keep_got[part]) for part in range(2)]
+    by_rows = [jnp.stack([keep_sums[part], other_sums[part]]) for part in range(2)]
+    own_pair = jnp.where(core == 0, by_rows[0], by_rows[1])
+    near_pair = swap(jnp.where(core == 0, by_rows[1], by_rows[0]), "dp", 1)
     by_core = [jnp.where(core == 0, own_pair, near_pair), jnp.where(core == 0, near_pair, own_pair)]
     by_side = [[jnp.where(side == s, part[0], part[1]) for part in by_core] for s in range(2)]
     blocks = [part for row in by_side for part in row]
@@ -751,12 +756,23 @@
     ).astype(f32)
     down_grad = jnp.concatenate([b[:, 2 * quarter :] for b in blocks], axis=1).astype(f32)
 
+    results = jnp.stack([out_home, in_home.astype(bf16)]).reshape(2, micro, tok_rows, width)
+    results = jnp.einsum("mtr,bmtd->bmrd", deal, results, preferred_element_type=f32).astype(bf16)
+    results = results.reshape(2 * micro, dp_count, piece_rows, width).transpose(1, 0, 2, 3)
+    results = lax.all_to_all(results, "dp", split_axis=0, concat_axis=0, tiled=True)
+    results = results.transpose(1, 0, 2, 3).reshape(2, micro, tok_rows, width)
+
     def reduced(value):
         return lax.psum_scatter(value, "dp", scatter_dimension=0, tiled=True)
 
-    out_grad = slots_of(reduced(out_part)).astype(f32)
-    query_out = slots_of(reduced(query_part_grad)).astype(f32)
+    out_grad = slots_of(reduced(out_part))
+    query_own = reduced(query_part_grad)
     kv_own = reduced(kv_part_grad)
+    results, out_grad, query_own, kv_own = lax.optimization_barrier(
+        (results, out_grad, query_own, kv_own)
+    )
+    out_grad = out_grad.astype(f32)
+    query_out = slots_of(query_own).astype(f32)
     key_part, value_part = kv_own[:, :own_width], kv_own[:, own_width:]
     first_back = lax.ppermute(
         jnp.where(even_col, key_part, value_part), "expert", [(b, a) for a, b in first_pairs]
@@ -772,12 +788,18 @@
         axis=1,
     ).astype(f32)
 
+    sum_rows = 2 + 2 * slots
+    peak_rows = jnp.pad(peak_table, ((0, 0), (0, width - HEADS)))
     sums = spread(
         jnp.concatenate(
-            [gain_one_grad[None], gain_two_grad[None], router_one_grad, router_two_grad], axis=0
-        ),
-        jnp.add,
-    )
+            [gain_one_grad[None], gain_two_grad[None], router_one_grad, router_two_grad, peak_rows],
+            axis=0,
+        ),
+        lambda left, right: jnp.where(
+            jnp.arange(sum_rows + slots)[:, None] < sum_rows, left + right, jnp.maximum(left, right)
+        ),
+    )
+    peaks_all = sums[sum_rows:, :HEADS]
     limit = clip_limit[0].astype(f32)
     factor = limit / jnp.maximum(peaks_all, limit)
     query_scale = jnp.repeat(jnp.sqrt(take(factor, col)), HDIM)
@@ -794,7 +816,7 @@
         sums[0],
         sums[1],
         sums[2 : 2 + slots].T,
-        sums[2 + slots :].T,
+        sums[2 + slots : sum_rows].T,
         query_out[None],
         out_grad[None],
         kv_out,

time: 1310 us -> 1150 us (0.88)
  waiting for transfers between devices: 750 us -> 588 us
  local copies, waits for them, and re-layouts: 89.1 us -> 71.9 us
    ppermute x76 -> x73, waiting for transfers between devices: 712 us -> 575 us  [swap(): return lax.ppermute(value, axis, [(i, i ^ step) for i in range(count)])]
    all_to_all x1, waiting for transfers between devices: 15.3 us -> 1.32 us  [local(): lax.all_to_all(both.transpose(1, 0, 2, 3), 'dp', split_axis=0, concat_axi...]
    ppermute x76 -> x73, starting transfers between devices: 79.4 us -> 81.5 us  [swap(): return lax.ppermute(value, axis, [(i, i ^ step) for i in range(count)])]
  transfers between devices with their start and end apart: 88 -> 84, of which waited for: 49 -> 47; matrix products, arithmetic and copies ran while one was open for 18% -> 19% of each run, Pallas kernels for 6% -> 10%
where the time goes in v4:
time: 1150 us; the launch traced here: 1140 us
  waiting for transfers between devices  588 us (51%)
  Pallas kernels  180 us (16%)
  starting transfers between devices  97.9 us (9%)
  other arithmetic  97.6 us (8%)
  matrix products  88.7 us (8%)
  local copies, waits for them, and re-layouts  71.9 us (6%)
  between operations  16.7 us (1%)
    ppermute x73, waiting for transfers between devices, swap(): return lax.ppermute(value, axis, [(i, i ^ step) for i in range(count)])  575 us
    ppermute x73, starting transfers between devices, swap(): return lax.ppermute(value, axis, [(i, i ^ step) for i in range(count)])  81.5 us
    pallas_call x1, Pallas kernels, expert_rows(): pl.pallas_call(expert_kernel, grid_spec=pltpu.PrefetchScalarGridSpec(num_...  70.6 us
    pallas_call x2, Pallas kernels, expert_grads(): pl.pallas_call(expert_grad_kernel, grid_spec=pltpu.PrefetchScalarGridSpec...  50.5 us
    dot_general x5, matrix products, dot(): return jnp.dot(left, right, preferred_element_type=f32)  30.1 us
    pallas_call x1, Pallas kernels, attention_backward(): pl.pallas_call(backward_kernel, grid_spec=pltpu.PrefetchScalarGridSpec(nu...  30 us
    pallas_call x1, Pallas kernels, attention_forward(): pl.pallas_call(forward_kernel, grid_spec=pltpu.PrefetchScalarGridSpec(num...  29 us
    dot_general x5, matrix products, dot_t(): lax.dot_general(left, right, (((1,), (1,)), ((), ())), preferred_element_...  23.7 us
  transfers between devices with their start and end apart: 84, of which 47 were waited for; matrix products, arithmetic and copies ran while one was open for 19% of the time, Pallas kernels for 10%

profile of v4, /device:TPU:8, one launch (start us, length us, event | category | flops | bytes accessed | tf_op | source)
XLA Modules:
  0.0 1141.4 jit_solution(802470637998236843)
XLA Ops:
  65.8 15.4 %collective-permute-done.5 = bf16[256,1024]{1,0:T(8,128)(2,1)} collective-permute-done((bf16[256,1024]{1,0:T(8,128)(2,1)}, bf16[256,1024]{1,0:T(8,128)(2,1)}, u32[]{:S(2)}, u32[]{:S(2)}) %collective-permute-start.5) | collective-permute-done | bytes 524320 | tf_op jit(solution)/shard_map/ppermute | solution.py:37
  83.3 15.5 %collective-permute-done.6 = bf16[256,1024]{1,0:T(8,128)(2,1)} collective-permute-done((bf16[256,1024]{1,0:T(8,128)(2,1)}, bf16[256,1024]{1,0:T(8,128)(2,1)}, u32[]{:S(2)}, u32[]{:S(2)}) %collective-permute-start.6) | collective-permute-done | bytes 524320 | tf_op jit(solution)/shard_map/ppermute | solution.py:37
  132.3 15.8 %collective-permute-done = bf16[2,64,2048]{2,1,0:T(8,128)(2,1)} collective-permute-done((bf16[2,64,2048]{2,1,0:T(8,128)(2,1)}, bf16[2,64,2048]{2,1,0:T(8,128)(2,1)}, u32[]{:S(2)}, u32[]{:S(2)}) %collective-permute-start) | collective-permute-done | bytes 524320 | tf_op jit(solution)/shard_map/ppermute | solution.py:37
  150.1 15.4 %collective-permute-done.1 = bf16[2,64,2048]{2,1,0:T(8,128)(2,1)S(1)} collective-permute-done((bf16[2,64,2048]{2,1,0:T(8,128)(2,1)}, bf16[2,64,2048]{2,1,0:T(8,128)(2,1)S(1)}, u32[]{:S(2)}, u32[]{:S(2)}) %collective-permute-start.1) | collective-permute-done | bytes 524320 | tf_op jit(solution)/shard_map/ppermute | solution.py:37
  175.2 22.4 %collective-permute-done.3.refs_1_ = bf16[256,4224]{1,0:T(8,128)(2,1)} collective-permute-done((bf16[256,4224]{1,0:T(8,128)(2,1)}, bf16[256,4224]{1,0:T(8,128)(2,1)}, u32[]{:S(2)}, u32[]{:S(2)}) %collective-permute-start.3) | collective-permute-done | bytes 2162720 | tf_op jit(solution)/shard_map/ppermute | solution.py:37
  206.4 16.7 %collective-permute-done.14 = bf16[2,48,2048]{2,1,0:T(8,128)(2,1)S(1)} collective-permute-done((bf16[2,48,2048]{2,1,0:T(8,128)(2,1)S(1)}, bf16[2,48,2048]{2,1,0:T(8,128)(2,1)S(1)}, u32[]{:S(2)}, u32[]{:S(2)}) %collective-permute-start.14) | collective-permute-done | bytes 393248 | tf_op jit(solution)/shard_map/ppermute | solution.py:37
  237.8 30.5 %collective-permute-done.20 = bf16[384,2048]{1,0:T(8,128)(2,1)} collective-permute-done((bf16[384,2048]{1,0:T(8,128)(2,1)}, bf16[384,2048]{1,0:T(8,128)(2,1)}, u32[]{:S(2)}, u32[]{:S(2)}) %collective-permute-start.20) | collective-permute-done | bytes 1572896 | tf_op jit(solution)/shard_map/ppermute | solution.py:37
  274.5 10.5 fusion.6.query
  285.0 29.0 %attention_forward.1 = (bf16[512,2048]{1,0:T(8,128)(2,1)}, bf16[512,2048]{1,0:T(8,128)(2,1)}, bf16[512,2048]{1,0:T(8,128)(2,1)}, bf16[512,512]{1,0:T(8,128)(2,1)...) custom-call(s32[2]{0:T(128)} %copy-done.67, f32[512,2048]{1,0:T(8,128)} %fusion.6.query, ...), custom_call_target="tpu_custom_call" | custom-call | flops 1073741824 | bytes 14680064 | tf_op jit(solution)/shard_map/attention_forward/pallas_call | solution.py:188
  332.7 26.5 %collective-permute-done.18 = bf16[2,64,2048]{2,1,0:T(8,128)(2,1)S(1)} collective-permute-done((bf16[2,64,2048]{2,1,0:T(8,128)(2,1)S(1)}, bf16[2,64,2048]{2,1,0:T(8,128)(2,1)S(1)}, u32[]{:S(2)}, u32[]{:S(2)}) %collective-permute-start.18) | collective-permute-done | bytes 524320 | tf_op jit(solution)/shard_map/ppermute | solution.py:37
  359.2 8.8 collective-permute-done.17
  379.2 21.5 %collective-permute-done.24 = bf16[2,48,2048]{2,1,0:T(8,128)(2,1)S(1)} collective-permute-done((bf16[2,48,2048]{2,1,0:T(8,128)(2,1)S(1)}, bf16[2,48,2048]{2,1,0:T(8,128)(2,1)S(1)}, u32[]{:S(2)}, u32[]{:S(2)}) %collective-permute-start.24) | collective-permute-done | bytes 393248 | tf_op jit(solution)/shard_map/ppermute | solution.py:37
  408.8 18.5 %collective-permute-done.25.refs_3_ = bf16[256,4224]{1,0:T(8,128)(2,1)S(1)} collective-permute-done((bf16[256,4224]{1,0:T(8,128)(2,1)}, bf16[256,4224]{1,0:T(8,128)(2,1)S(1)}, u32[]{:S(2)}, u32[]{:S(2)}) %collective-permute-start.25) | collective-permute-done | bytes 2162720 | tf_op jit(solution)/shard_map/ppermute | solution.py:37
  428.0 35.7 %collective-permute-done.31 = bf16[384,2048]{1,0:T(8,128)(2,1)} collective-permute-done((bf16[384,2048]{1,0:T(8,128)(2,1)}, bf16[384,2048]{1,0:T(8,128)(2,1)}, u32[]{:S(2)}, u32[]{:S(2)}) %collective-permute-start.31) | collective-permute-done | bytes 1572896 | tf_op jit(solution)/shard_map/ppermute | solution.py:37
  482.1 70.6 %expert_rows.1 = (bf16[1536,2048]{1,0:T(8,128)(2,1)}, bf16[1536,2176]{1,0:T(8,128)(2,1)}, bf16[1536,1408]{1,0:T(8,128)(2,1)}, bf16[1536,2816]{1,0:T(8,128)(2,1)}) custom-call(s32[2]{0:T(128)} %pad_add_fusion.1.place_ref, bf16[1536,2048]{1,0:T(8,128)(2,1)} %pad_maximum_fusion.1.hidden, bf16[1536,2048]{1,0:T(8,128)(2,1)} %pad_maximum_fusion.grad, ...), custom_call_target="tpu_custom_call" | custom-call | flops 53150220288 | bytes 55050240 | tf_op jit(solution)/shard_map/expert_rows/pallas_call | solution.py:339
  563.9 25.5 %expert_grads.2 = (bf16[256,4224]{1,0:T(8,128)(2,1)}, bf16[256,4224]{1,0:T(8,128)(2,1)}, bf16[256,4224]{1,0:T(8,128)(2,1)}, bf16[256,4224]{1,0:T(8,128)(2,1)}) custom-call(s32[4]{0:T(128)S(1)} %get-tuple-element.264.order, bf16[1536,2048]{1,0:T(8,128)(2,1)} %pad_maximum_fusion.1.hidden, bf16[1536,2048]{1,0:T(8,128)(2,1)} %pad_maximum_fusion.grad, ...), custom_call_target="tpu_custom_call" | custom-call | flops 13287555072 | bytes 27918336 | tf_op jit(solution)/shard_map/expert_grads/pallas_call | solution.py:395
  591.4 25.0 %expert_grads.3 = (bf16[256,4224]{1,0:T(8,128)(2,1)S(1)}, bf16[256,4224]{1,0:T(8,128)(2,1)S(1)}, bf16[256,4224]{1,0:T(8,128)(2,1)}, bf16[256,4224]{1,0:T(8,128)(2,1)}) custom-call(s32[4]{0:T(128)S(1)} %get-tuple-element.265.order, bf16[1536,2048]{1,0:T(8,128)(2,1)} %pad_maximum_fusion.1.hidden, bf16[1536,2048]{1,0:T(8,128)(2,1)} %pad_maximum_fusion.grad, ...), custom_call_target="tpu_custom_call" | custom-call | flops 13287555072 | bytes 27918336 | tf_op jit(solution)/shard_map/expert_grads/pallas_call | solution.py:395
  626.5 12.8 %collective-permute-done.45 = bf16[2,48,2176]{2,1,0:T(8,128)(2,1)S(1)} collective-permute-done((bf16[2,48,2176]{2,1,0:T(8,128)(2,1)S(1)}, bf16[2,48,2176]{2,1,0:T(8,128)(2,1)S(1)}, u32[]{:S(2)}, u32[]{:S(2)}) %collective-permute-start.45) | collective-permute-done | bytes 417824 | tf_op jit(solution)/shard_map/ppermute | solution.py:37
  639.3 12.7 %collective-permute-done.46 = bf16[2,48,2176]{2,1,0:T(8,128)(2,1)S(1)} collective-permute-done((bf16[2,48,2176]{2,1,0:T(8,128)(2,1)S(1)}, bf16[2,48,2176]{2,1,0:T(8,128)(2,1)S(1)}, u32[]{:S(2)}, u32[]{:S(2)}) %collective-permute-start.46) | collective-permute-done | bytes 417824 | tf_op jit(solution)/shard_map/ppermute | solution.py:37
  672.2 30.5 %collective-permute-done.44 = bf16[384,2048]{1,0:T(8,128)(2,1)S(1)} collective-permute-done((bf16[384,2048]{1,0:T(8,128)(2,1)S(1)}, bf16[384,2048]{1,0:T(8,128)(2,1)S(1)}, u32[]{:S(2)}, u32[]{:S(2)}) %collective-permute-start.44) | collective-permute-done | bytes 1572896 | tf_op jit(solution)/shard_map/ppermute | solution.py:37
  710.4 14.8 %collective-permute-done.49 = bf16[2,64,2048]{2,1,0:T(8,128)(2,1)S(1)} collective-permute-done((bf16[2,64,2048]{2,1,0:T(8,128)(2,1)S(1)}, bf16[2,64,2048]{2,1,0:T(8,128)(2,1)S(1)}, u32[]{:S(2)}, u32[]{:S(2)}) %collective-permute-start.49) | collective-permute-done | bytes 524320 | tf_op jit(solution)/shard_map/ppermute | solution.py:37
  725.3 19.2 %collective-permute-done.50 = bf16[2,64,2048]{2,1,0:T(8,128)(2,1)S(1)} collective-permute-done((bf16[2,64,2048]{2,1,0:T(8,128)(2,1)S(1)}, bf16[2,64,2048]{2,1,0:T(8,128)(2,1)S(1)}, u32[]{:S(2)}, u32[]{:S(2)}) %collective-permute-start.50) | collective-permute-done | bytes 524320 | tf_op jit(solution)/shard_map/ppermute | solution.py:37
  744.5 8.5 collective-permute-done.51
  772.0 11.0 fusion.vals_grad
  783.0 51.1 %collective-permute-done.56 = bf16[256,4224]{1,0:T(8,128)(2,1)} collective-permute-done((bf16[256,4224]{1,0:T(8,128)(2,1)}, bf16[256,4224]{1,0:T(8,128)(2,1)}, u32[]{:S(2)}, u32[]{:S(2)}) %collective-permute-start.56) | collective-permute-done | bytes 2162720 | tf_op jit(solution)/shard_map/ppermute | solution.py:37
  835.6 30.0 %attention_backward.1 = (bf16[512,2048]{1,0:T(8,128)(2,1)}, bf16[512,512]{1,0:T(8,128)(2,1)}, bf16[512,512]{1,0:T(8,128)(2,1)}, f32[512,128]{1,0:T(8,128)}) custom-call(s32[2]{0:T(128)} %copy-done.67, bf16[512,2048]{1,0:T(8,128)(2,1)} %get-tuple-element.117.query, bf16[512,512]{1,0:T(8,128)(2,1)} %get-tuple-element.118.key, ...), custom_call_target="tpu_custom_call" | custom-call | flops 2684354560 | bytes 14680064 | tf_op jit(solution)/shard_map/attention_backward/pallas_call | solution.py:219
  865.7 21.5 %collective-permute-done.57 = bf16[256,4224]{1,0:T(8,128)(2,1)} collective-permute-done((bf16[256,4224]{1,0:T(8,128)(2,1)}, bf16[256,4224]{1,0:T(8,128)(2,1)}, u32[]{:S(2)}, u32[]{:S(2)}) %collective-permute-start.57) | collective-permute-done | bytes 2162720 | tf_op jit(solution)/shard_map/ppermute | solution.py:37
  895.1 9.4 add_convert_fusion.4
  937.0 47.9 %collective-permute-done.62 = bf16[256,4224]{1,0:T(8,128)(2,1)S(1)} collective-permute-done((bf16[256,4224]{1,0:T(8,128)(2,1)S(1)}, bf16[256,4224]{1,0:T(8,128)(2,1)S(1)}, u32[]{:S(2)}, u32[]{:S(2)}) %collective-permute-start.62) | collective-permute-done | bytes 2162720 | tf_op jit(solution)/shard_map/ppermute | solution.py:37
  1058.2 8.4 convert_element_type.350
  1070.9 15.7 %collective-permute-done.64 = bf16[256,512]{1,0:T(8,128)(2,1)S(1)} collective-permute-done((bf16[256,512]{1,0:T(8,128)(2,1)S(1)}, bf16[256,512]{1,0:T(8,128)(2,1)S(1)}, u32[]{:S(2)}, u32[]{:S(2)}) %collective-permute-start.64) | collective-permute-done | bytes 262176 | tf_op jit(solution)/shard_map/ppermute | solution.py:37
  1107.6 15.9 %collective-permute-done.72 = bf16[256,512]{1,0:T(8,128)(2,1)S(1)} collective-permute-done((bf16[256,512]{1,0:T(8,128)(2,1)S(1)}, bf16[256,512]{1,0:T(8,128)(2,1)S(1)}, u32[]{:S(2)}, u32[]{:S(2)}) %collective-permute-start.72) | collective-permute-done | bytes 262176 | tf_op jit(solution)/shard_map/ppermute | solution.py:37
  (577 shorter events, 412.0 us)
Async XLA Ops:
  13.3 255.1 %all-gather.5.cloned.1.call-start = ((), (), s32[]{:S(2)}) async-start(), calls=%async_computation.6 | async-start | bytes 4718592 | tf_op jit(solution)/shard_map/all_gather | solution.py:537
  46.6 227.9 %all-gather.3.cloned.1.call-start = ((), (), s32[]{:S(2)}) async-start(), calls=%async_computation.5 | async-start | bytes 18874368 | tf_op jit(solution)/shard_map/all_gather | solution.py:538
  51.4 65.4 %collective-permute-start.8 = (bf16[256,4224]{1,0:T(8,128)(2,1)}, bf16[256,4224]{1,0:T(8,128)(2,1)}, u32[]{:S(2)}, u32[]{:S(2)}) collective-permute-start(bf16[256,4224]{1,0:T(8,128)(2,1)} %get-tuple-element.82), channel_id=1, source_target_pairs={{0,8},{4,12},{8,0},{12,4},{16,24},{20,28},{24,16},{28,20},{1,9},{5... | collective-permute-start | bytes 6488072 | tf_op jit(solution)/shard_map/ppermute | solution.py:37
  53.1 65.1 %collective-permute-start.9 = (bf16[256,4224]{1,0:T(8,128)(2,1)}, bf16[256,4224]{1,0:T(8,128)(2,1)}, u32[]{:S(2)}, u32[]{:S(2)}) collective-permute-start(bf16[256,4224]{1,0:T(8,128)(2,1)} %get-tuple-element.83), channel_id=1, source_target_pairs={{0,16},{4,20},{8,24},{12,28},{16,0},{20,4},{24,8},{28,12},{1,17},{... | collective-permute-start | bytes 6488072 | tf_op jit(solution)/shard_map/ppermute | solution.py:37
  64.0 44.7 %collective-permute-start.7 = (bf16[256,1024]{1,0:T(8,128)(2,1)S(1)}, bf16[256,1024]{1,0:T(8,128)(2,1)S(1)}, u32[]{:S(2)}, u32[]{:S(2)}) collective-permute-start(bf16[256,1024]{1,0:T(8,128)(2,1)S(1)} %pad_maximum_fusion.14), channel_id=1, source_target_pairs={{0,3},{1,2},{2,1},{3,0},{4,7},{5,6},{6,5},{7,4},{8,11},{9,10},{10,... | collective-permute-start | bytes 1572872 | tf_op jit(solution)/shard_map/ppermute | solution.py:37
  118.3 929.8 %reduce-scatter.4.cloned.1.call-start = ((), (), s32[]{:S(2)}) async-start(), calls=%async_computation.7 | async-start | bytes 9437184 | tf_op jit(solution)/shard_map/reduce_scatter | solution.py:766
  119.8 77.9 %collective-permute-start.3 = (bf16[256,4224]{1,0:T(8,128)(2,1)}, bf16[256,4224]{1,0:T(8,128)(2,1)}, u32[]{:S(2)}, u32[]{:S(2)}) collective-permute-start(bf16[256,4224]{1,0:T(8,128)(2,1)} %get-tuple-element.77), channel_id=1, source_target_pairs={{0,8},{4,12},{8,0},{12,4},{16,24},{20,28},{24,16},{28,20},{1,9},{5... | collective-permute-start | bytes 6488072 | tf_op jit(solution)/shard_map/ppermute | solution.py:37
  120.2 78.2 %collective-permute-start.4 = (bf16[256,4224]{1,0:T(8,128)(2,1)}, bf16[256,4224]{1,0:T(8,128)(2,1)}, u32[]{:S(2)}, u32[]{:S(2)}) collective-permute-start(bf16[256,4224]{1,0:T(8,128)(2,1)} %get-tuple-element.78.refs_0_), channel_id=1, source_target_pairs={{0,16},{4,20},{8,24},{12,28},{16,0},{20,4},{24,8},{28,12},{1,17},{... | collective-permute-start | bytes 6488072 | tf_op jit(solution)/shard_map/ppermute | solution.py:37
  130.3 44.1 %collective-permute-start.2 = (bf16[2,64,2048]{2,1,0:T(8,128)(2,1)}, bf16[2,64,2048]{2,1,0:T(8,128)(2,1)S(1)}, u32[]{:S(2)}, u32[]{:S(2)}) collective-permute-start(bf16[2,64,2048]{2,1,0:T(8,128)(2,1)} %get-tuple-element.168), channel_id=1, source_target_pairs={{0,3},{1,2},{2,1},{3,0},{4,7},{5,6},{6,5},{7,4},{8,11},{9,10},{10,... | collective-permute-start | bytes 1572872 | tf_op jit(solution)/shard_map/ppermute | solution.py:37
  233.7 80.4 %collective-permute-start.15 = (bf16[256,4224]{1,0:T(8,128)(2,1)}, bf16[256,4224]{1,0:T(8,128)(2,1)}, u32[]{:S(2)}, u32[]{:S(2)}) collective-permute-start(bf16[256,4224]{1,0:T(8,128)(2,1)} %collective-permute-done.8), channel_id=1, source_target_pairs={{0,16},{4,20},{8,24},{12,28},{16,0},{20,4},{24,8},{28,12},{1,17},{... | collective-permute-start | bytes 6488072 | tf_op jit(solution)/shard_map/ppermute | solution.py:37
  237.8 89.0 %collective-permute-start.19 = (bf16[384,2048]{1,0:T(8,128)(2,1)}, bf16[384,2048]{1,0:T(8,128)(2,1)}, u32[]{:S(2)}, u32[]{:S(2)}) collective-permute-start(bf16[384,2048]{1,0:T(8,128)(2,1)} %bitcast.46), channel_id=1, source_target_pairs={{0,4},{4,0},{8,12},{12,8},{16,20},{20,16},{24,28},{28,24},{1,5},{5... | collective-permute-start | bytes 4718600 | tf_op jit(solution)/shard_map/ppermute | solution.py:37
  268.3 58.5 %collective-permute-start.21 = (bf16[384,2048]{1,0:T(8,128)(2,1)}, bf16[384,2048]{1,0:T(8,128)(2,1)}, u32[]{:S(2)}, u32[]{:S(2)}) collective-permute-start(bf16[384,2048]{1,0:T(8,128)(2,1)} %collective-permute-done.20), channel_id=1, source_target_pairs={{0,4},{4,0},{8,12},{12,8},{16,20},{20,16},{24,28},{28,24},{1,5},{5... | collective-permute-start | bytes 4718600 | tf_op jit(solution)/shard_map/ppermute | solution.py:37
  322.4 45.6 %collective-permute-start.17 = (bf16[2,64,2048]{2,1,0:T(8,128)(2,1)S(1)}, bf16[2,64,2048]{2,1,0:T(8,128)(2,1)S(1)}, u32[]{:S(2)}, u32[]{:S(2)}) collective-permute-start(bf16[2,64,2048]{2,1,0:T(8,128)(2,1)S(1)} %get-tuple-element.189), channel_id=1, source_target_pairs={{0,2},{1,3},{2,0},{3,1},{4,6},{5,7},{6,4},{7,5},{8,10},{9,11},{10,... | collective-permute-start | bytes 1572872 | tf_op jit(solution)/shard_map/ppermute | solution.py:37
  377.7 49.7 %collective-permute-start.25 = (bf16[256,4224]{1,0:T(8,128)(2,1)}, bf16[256,4224]{1,0:T(8,128)(2,1)S(1)}, u32[]{:S(2)}, u32[]{:S(2)}) collective-permute-start(bf16[256,4224]{1,0:T(8,128)(2,1)} %collective-permute-done.3.refs_1_), channel_id=1, source_target_pairs={{0,16},{4,20},{8,24},{12,28},{16,0},{20,4},{24,8},{28,12},{1,17},{... | collective-permute-start | bytes 6488072 | tf_op jit(solution)/shard_map/ppermute | solution.py:37
  428.0 48.2 %collective-permute-start.30 = (bf16[384,2048]{1,0:T(8,128)(2,1)}, bf16[384,2048]{1,0:T(8,128)(2,1)}, u32[]{:S(2)}, u32[]{:S(2)}) collective-permute-start(bf16[384,2048]{1,0:T(8,128)(2,1)} %bitcast.63), channel_id=1, source_target_pairs={{0,4},{4,0},{8,12},{12,8},{16,20},{20,16},{24,28},{28,24},{1,5},{5... | collective-permute-start | bytes 4718600 | tf_op jit(solution)/shard_map/ppermute | solution.py:37
  556.6 59.8 %collective-permute-start.39 = (bf16[384,2176]{1,0:T(8,128)(2,1)}, bf16[384,2176]{1,0:T(8,128)(2,1)S(1)}, u32[]{:S(2)}, u32[]{:S(2)}) collective-permute-start(bf16[384,2176]{1,0:T(8,128)(2,1)} %get-tuple-element.171), channel_id=1, source_target_pairs={{0,4},{4,0},{8,12},{12,8},{16,20},{20,16},{24,28},{28,24},{1,5},{5... | collective-permute-start | bytes 5013512 | tf_op jit(solution)/shard_map/ppermute | solution.py:37
  563.3 53.1 %collective-permute-start.41 = (bf16[384,2176]{1,0:T(8,128)(2,1)}, bf16[384,2176]{1,0:T(8,128)(2,1)}, u32[]{:S(2)}, u32[]{:S(2)}) collective-permute-start(bf16[384,2176]{1,0:T(8,128)(2,1)} %add_convert_fusion.5), channel_id=1, source_target_pairs={{0,8},{4,12},{8,0},{12,4},{16,24},{20,28},{24,16},{28,20},{1,9},{5... | collective-permute-start | bytes 5013512 | tf_op jit(solution)/shard_map/ppermute | solution.py:37
  589.4 117.2 %collective-permute-start.48 = (bf16[256,4224]{1,0:T(8,128)(2,1)}, bf16[256,4224]{1,0:T(8,128)(2,1)}, u32[]{:S(2)}, u32[]{:S(2)}) collective-permute-start(bf16[256,4224]{1,0:T(8,128)(2,1)} %get-tuple-element.96), channel_id=1, source_target_pairs={{0,16},{4,20},{8,24},{12,28},{16,0},{20,4},{24,8},{28,12},{1,17},{... | collective-permute-start | bytes 6488072 | tf_op jit(solution)/shard_map/ppermute | solution.py:37
  590.9 162.2 %collective-permute-start.52 = (bf16[256,4224]{1,0:T(8,128)(2,1)}, bf16[256,4224]{1,0:T(8,128)(2,1)}, u32[]{:S(2)}, u32[]{:S(2)}) collective-permute-start(bf16[256,4224]{1,0:T(8,128)(2,1)} %get-tuple-element.97), channel_id=1, source_target_pairs={{0,16},{4,20},{8,24},{12,28},{16,0},{20,4},{24,8},{28,12},{1,17},{... | collective-permute-start | bytes 6488072 | tf_op jit(solution)/shard_map/ppermute | solution.py:37
  652.0 50.7 %collective-permute-start.42 = (bf16[384,2048]{1,0:T(8,128)(2,1)}, bf16[384,2048]{1,0:T(8,128)(2,1)}, u32[]{:S(2)}, u32[]{:S(2)}) collective-permute-start(bf16[384,2048]{1,0:T(8,128)(2,1)} %get-tuple-element.173), channel_id=1, source_target_pairs={{0,4},{4,0},{8,12},{12,8},{16,20},{20,16},{24,28},{28,24},{1,5},{5... | collective-permute-start | bytes 4718600 | tf_op jit(solution)/shard_map/ppermute | solution.py:37
  761.2 331.0 %reduce-scatter.8.cloned.1.call-start = ((), (), s32[]{:S(2)}) async-start(), calls=%async_computation.9 | async-start | bytes 4718592 | tf_op jit(solution)/shard_map/reduce_scatter | solution.py:766
  761.3 72.8 %collective-permute-start.56 = (bf16[256,4224]{1,0:T(8,128)(2,1)}, bf16[256,4224]{1,0:T(8,128)(2,1)}, u32[]{:S(2)}, u32[]{:S(2)}) collective-permute-start(bf16[256,4224]{1,0:T(8,128)(2,1)} %get-tuple-element.98), channel_id=1, source_target_pairs={{0,16},{4,20},{8,24},{12,28},{16,0},{20,4},{24,8},{28,12},{1,17},{... | collective-permute-start | bytes 6488072 | tf_op jit(solution)/shard_map/ppermute | solution.py:37
  762.8 124.3 %collective-permute-start.57 = (bf16[256,4224]{1,0:T(8,128)(2,1)}, bf16[256,4224]{1,0:T(8,128)(2,1)}, u32[]{:S(2)}, u32[]{:S(2)}) collective-permute-start(bf16[256,4224]{1,0:T(8,128)(2,1)} %get-tuple-element.99), channel_id=1, source_target_pairs={{0,16},{4,20},{8,24},{12,28},{16,0},{20,4},{24,8},{28,12},{1,17},{... | collective-permute-start | bytes 6488072 | tf_op jit(solution)/shard_map/ppermute | solution.py:37
  768.5 97.1 %collective-permute-start.53 = (bf16[2,48,2048]{2,1,0:T(8,128)(2,1)}, bf16[2,48,2048]{2,1,0:T(8,128)(2,1)}, u32[]{:S(2)}, u32[]{:S(2)}) collective-permute-start(bf16[2,48,2048]{2,1,0:T(8,128)(2,1)} %bitcast.92), channel_id=1, source_target_pairs={{0,1},{1,0},{2,3},{3,2},{4,5},{5,4},{6,7},{7,6},{8,9},{9,8},{10,11... | collective-permute-start | bytes 1179656 | tf_op jit(solution)/shard_map/ppermute | solution.py:37
  768.5 97.1 %collective-permute-start.54 = (bf16[2,48,2048]{2,1,0:T(8,128)(2,1)}, bf16[2,48,2048]{2,1,0:T(8,128)(2,1)}, u32[]{:S(2)}, u32[]{:S(2)}) collective-permute-start(bf16[2,48,2048]{2,1,0:T(8,128)(2,1)} %bitcast.93), channel_id=1, source_target_pairs={{0,2},{1,3},{2,0},{3,1},{4,6},{5,7},{6,4},{7,5},{8,10},{9,11},{10,... | collective-permute-start | bytes 1179656 | tf_op jit(solution)/shard_map/ppermute | solution.py:37
  771.5 94.1 %collective-permute-start.55 = (bf16[2,48,2048]{2,1,0:T(8,128)(2,1)S(1)}, bf16[2,48,2048]{2,1,0:T(8,128)(2,1)S(1)}, u32[]{:S(2)}, u32[]{:S(2)}) collective-permute-start(bf16[2,48,2048]{2,1,0:T(8,128)(2,1)S(1)} %bitcast.415), channel_id=1, source_target_pairs={{0,3},{1,2},{2,1},{3,0},{4,7},{5,6},{6,5},{7,4},{8,11},{9,10},{10,... | collective-permute-start | bytes 1179656 | tf_op jit(solution)/shard_map/ppermute | solution.py:37
  834.1 70.4 %collective-permute-start.58 = (bf16[256,4224]{1,0:T(8,128)(2,1)}, bf16[256,4224]{1,0:T(8,128)(2,1)}, u32[]{:S(2)}, u32[]{:S(2)}) collective-permute-start(bf16[256,4224]{1,0:T(8,128)(2,1)} %add_convert_fusion.3), channel_id=1, source_target_pairs={{0,8},{4,12},{8,0},{12,4},{16,24},{20,28},{24,16},{28,20},{1,9},{5... | collective-permute-start | bytes 6488072 | tf_op jit(solution)/shard_map/ppermute | solution.py:37
  919.2 173.1 %reduce-scatter.6.cloned.1.call-start = ((), (), s32[]{:S(2)}) async-start(), calls=%async_computation.8 | async-start | bytes 9437184 | tf_op jit(solution)/shard_map/reduce_scatter | solution.py:766
  923.5 61.4 %collective-permute-start.62 = (bf16[256,4224]{1,0:T(8,128)(2,1)S(1)}, bf16[256,4224]{1,0:T(8,128)(2,1)S(1)}, u32[]{:S(2)}, u32[]{:S(2)}) collective-permute-start(bf16[256,4224]{1,0:T(8,128)(2,1)S(1)} %add_convert_fusion.2), channel_id=1, source_target_pairs={{0,8},{4,12},{8,0},{12,4},{16,24},{20,28},{24,16},{28,20},{1,9},{5... | collective-permute-start | bytes 6488072 | tf_op jit(solution)/shard_map/ppermute | solution.py:37
  933.5 58.7 %collective-permute-start.61 = (bf16[2,64,2176]{2,1,0:T(8,128)(2,1)}, bf16[2,64,2176]{2,1,0:T(8,128)(2,1)S(1)}, u32[]{:S(2)}, u32[]{:S(2)}) collective-permute-start(bf16[2,64,2176]{2,1,0:T(8,128)(2,1)} %get-tuple-element.195), channel_id=1, source_target_pairs={{0,3},{1,2},{2,1},{3,0},{4,7},{5,6},{6,5},{7,4},{8,11},{9,10},{10,... | collective-permute-start | bytes 1671176 | tf_op jit(solution)/shard_map/ppermute | solution.py:37
  935.1 57.2 %collective-permute-start.60 = (bf16[2,64,2176]{2,1,0:T(8,128)(2,1)S(1)}, bf16[2,64,2176]{2,1,0:T(8,128)(2,1)}, u32[]{:S(2)}, u32[]{:S(2)}) collective-permute-start(bf16[2,64,2176]{2,1,0:T(8,128)(2,1)S(1)} %get-tuple-element.196), channel_id=1, source_target_pairs={{0,2},{1,3},{2,0},{3,1},{4,6},{5,7},{6,4},{7,5},{8,10},{9,11},{10,... | collective-permute-start | bytes 1671176 | tf_op jit(solution)/shard_map/ppermute | solution.py:37
  935.1 57.2 %collective-permute-start.59 = (bf16[2,64,2176]{2,1,0:T(8,128)(2,1)S(1)}, bf16[2,64,2176]{2,1,0:T(8,128)(2,1)}, u32[]{:S(2)}, u32[]{:S(2)}) collective-permute-start(bf16[2,64,2176]{2,1,0:T(8,128)(2,1)S(1)} %get-tuple-element.194), channel_id=1, source_target_pairs={{0,1},{1,0},{2,3},{3,2},{4,5},{5,4},{6,7},{7,6},{8,9},{9,8},{10,11... | collective-permute-start | bytes 1671176 | tf_op jit(solution)/shard_map/ppermute | solution.py:37
  (134 other events, 3638.7 us)
Sparse Core Ops, SparseCore 0:
  46.7 55.8 all-gather.4
  118.4 125.5 all-gather.2
  761.3 105.1 reduce-scatter.3
  919.3 64.5 reduce-scatter.7
  989.6 85.6 reduce-scatter.5

commit v5 on v4

--- a/solution.py
+++ b/solution.py
@@ -49,7 +49,7 @@
 
 
 def after(value, *others):
-    return lax.optimization_barrier((value, *others))[0]
+    return lax.optimization_barrier((value, others))[0]
 
 
 def spread(value, combine):
@@ -282,7 +282,7 @@
     core, chip = place_ref[0], place_ref[1]
     rows, columns = near_pieces[0].shape
     units = columns // 3
-    width = hidden.shape[1]
+    width = grad.shape[1]
 
     @pl.when(pl.program_id(0) == 0)
     def _():
@@ -305,8 +305,8 @@
 
     slot_sum = jnp.zeros((hidden.shape[0], 1), f32)
     for start, size in unit_blocks(units):
-        gate_pre = dot(hidden[...], weights[:, start : start + size])
-        up_pre = dot(hidden[...], weights[:, units + start : units + start + size])
+        gate_pre = dot(hidden[:, :width], weights[:, start : start + size])
+        up_pre = dot(hidden[:, :width], weights[:, units + start : units + start + size])
         act_grad = dot(grad[...], weights[:, 2 * units + start : 2 * units + start + size])
         sigma = 1.0 / (1.0 + jnp.exp(-gate_pre))
         silu_vals = gate_pre * sigma
@@ -326,7 +326,7 @@
 
 
 def expert_rows(position, hidden, grad, own_pieces, near_pieces):
-    rows, width = hidden.shape
+    rows, width = grad.shape
     columns = near_pieces[0].shape[1]
     units = columns // 3
     tile = 256
@@ -341,7 +341,8 @@
         grid_spec=pltpu.PrefetchScalarGridSpec(
             num_scalar_prefetch=1,
             grid=(rows // tile,),
-            in_specs=[tiled(width)] * 2 + [pl.BlockSpec(memory_space=pl.ANY)] * (2 * count),
+            in_specs=[tiled(width + HDIM), tiled(width)]
+            + [pl.BlockSpec(memory_space=pl.ANY)] * (2 * count),
             out_specs=[tiled(width), tiled(width + HDIM), tiled(units), tiled(2 * units)],
             scratch_shapes=[
                 pltpu.VMEM((width, columns), bf16),
@@ -364,32 +365,45 @@
     )(position, hidden, grad, *own_pieces, *near_pieces)
 
 
-def expert_grad_kernel(order, hidden, grad, gates, joint, active, *outs):
-    gate = gates[...]
-    left = (hidden[...].astype(f32) * gate).astype(bf16)
-    right = (grad[...].astype(f32) * gate).astype(bf16)
-    units = active.shape[1]
+def expert_grad_kernel(order, *refs):
+    hidden, grad, gates, joint, active = [refs[2 * n : 2 * n + 2] for n in range(5)]
+    outs = refs[10:]
+    units = active[0].shape[1]
+
+    def scaled(blocks):
+        return [
+            (block[...].astype(f32) * gate[:, :1].astype(f32)).astype(bf16)
+            for block, gate in zip(blocks, gates)
+        ]
+
+    left, right = scaled(hidden), scaled(grad)
     step = pl.program_id(0)
     for number, out in enumerate(outs):
 
         @pl.when(step == number)
         def _():
             for start, size in unit_blocks(2 * units):
-                out[:, start : start + size] = t_dot(left, joint[:, start : start + size]).astype(bf16)
+                out[:, start : start + size] = sum(
+                    t_dot(rows, part[:, start : start + size]) for rows, part in zip(left, joint)
+                ).astype(bf16)
             for start, size in unit_blocks(units):
-                out[:, 2 * units + start : 2 * units + start + size] = t_dot(
-                    right, active[:, start : start + size]
+                out[:, 2 * units + start : 2 * units + start + size] = sum(
+                    t_dot(rows, part[:, start : start + size]) for rows, part in zip(right, active)
                 ).astype(bf16)
 
 
-def expert_grads(chunks, chunk_rows, hidden, grad, gates, joint, active):
-    rows, units = active.shape
+def expert_grads(chunks, chunk_rows, rows_of, joints, actives):
+    hidden, grad = rows_of[:2], rows_of[2:]
+    rows, units = actives[0].shape
+    width = grad[0].shape[1]
     half = chunk_rows // 2
     count = len(chunks)
     order = jnp.stack([2 * chunk + part for chunk in chunks for part in range(2)]).astype(jnp.int32)
 
-    def whole(size):
-        return pl.BlockSpec((rows, size), lambda i, at: (0, 0), pipeline_mode=pl.Buffered(1))
+    def whole(size, column=0):
+        return pl.BlockSpec(
+            (rows, size), lambda i, at: (0, column), pipeline_mode=pl.Buffered(1)
+        )
 
     column = pl.BlockSpec((rows, half), lambda i, at: (0, at[i]))
     return pl.pallas_call(
@@ -397,20 +411,23 @@
         grid_spec=pltpu.PrefetchScalarGridSpec(
             num_scalar_prefetch=1,
             grid=(2 * count,),
-            in_specs=[column, column, whole(1), whole(2 * units), whole(units)],
+            in_specs=[column] * 4
+            + [whole(HDIM, width // HDIM)] * 2
+            + [whole(2 * units)] * 2
+            + [whole(units)] * 2,
             out_specs=[
                 pl.BlockSpec((half, 3 * units), lambda i, at: (0, 0)) for _ in range(2 * count)
             ],
         ),
         out_shape=[jax.ShapeDtypeStruct((half, 3 * units), bf16)] * (2 * count),
-        compiler_params=pltpu.CompilerParams(vmem_limit_bytes=48 * 2**20),
+        compiler_params=pltpu.CompilerParams(vmem_limit_bytes=56 * 2**20),
         cost_estimate=pl.CostEstimate(
-            flops=2 * count * chunk_rows * rows * 3 * units,
-            bytes_accessed=2 * (rows * 3 * units + count * chunk_rows * (2 * rows + 3 * units)),
+            flops=4 * count * chunk_rows * rows * 3 * units,
+            bytes_accessed=2 * (rows * 6 * units + count * chunk_rows * (4 * rows + 3 * units)),
             transcendentals=0,
         ),
         name="expert_grads",
-    )(order, hidden, grad, gates, joint, active)
+    )(order, *hidden, *grad, *hidden, *joints, *actives)
 
 
 def local(
@@ -471,8 +488,8 @@
     parts = (1 - core, core)
     keep_pair = [quarter_of(side, part) for part in parts]
     send_pair = [quarter_of(1 - side, part) for part in parts]
-    both, keep_pair, send_pair, kv_in, query_in, out_in = lax.optimization_barrier(
-        (both, keep_pair, send_pair, kv_weight, query_weight[0], attn_out_weight[0])
+    keep_pair, send_pair, kv_in, query_in, out_in = lax.optimization_barrier(
+        (keep_pair, send_pair, kv_weight, query_weight[0], attn_out_weight[0])
     )
     side_pair = [swap(piece, "dp", 2) for piece in send_pair]
     line_steps = [4 * line for line in range(1, lines)]
@@ -534,7 +551,7 @@
         ],
         axis=1,
     )
-    kv_full = lax.all_gather(own_kv, "dp", axis=0, tiled=True)
+    kv_full = lax.all_gather(after(own_kv, work), "dp", axis=0, tiled=True)
     joint_full = lax.all_gather(
         after(columns_of(query_in, out_in), side_pair[0], *keep_lines[0]), "dp", axis=0, tiled=True
     )
@@ -581,24 +598,25 @@
     pack_rows = micro * cap
     sent_rows = slots * pack_rows
 
-    def send_packed(value):
+    def send_packed(value, lane=None):
         packed = jnp.einsum(
             "kmct,mtd->kmcd", packs_low, value.reshape(micro, tok_rows, -1), preferred_element_type=f32
         ).astype(bf16)
+        if lane is not None:
+            lanes = jnp.pad(lane[..., None], ((0, 0), (0, 0), (0, 0), (0, HDIM - 1)))
+            packed = jnp.concatenate([packed, lanes.astype(bf16)], axis=-1)
         parts = [swap(packed[k], "expert", k) if k else packed[k] for k in range(slots)]
         return jnp.stack(parts).reshape(sent_rows, -1)
 
-    def quad_rows(value):
-        near = swap(value, "dp", 1)
-        far = swap(value, "dp", 2)
-        across = swap(far, "dp", 1)
-        return jnp.concatenate([value, near, far, across], axis=0)
-
-    def quad_sum(value, *others):
-        own, near, far, across = jnp.split(value, 4, axis=0)
+    def near_rows(value):
+        return jnp.concatenate([value, swap(value, "dp", 1)], axis=0)
+
+    def quad_sums(value):
+        near_half, far_half = value
+        own, near = jnp.split(near_half, 2, axis=0)
+        far, across = jnp.split(far_half, 2, axis=0)
         far_sum = far.astype(f32) + swap(across, "dp", 1).astype(f32)
-        own_sum = own.astype(f32) + swap(near, "dp", 1).astype(f32)
-        return own_sum + after(swap(far_sum.astype(bf16), "dp", 2), *others).astype(f32)
+        return own.astype(f32) + swap(near, "dp", 1).astype(f32), far_sum.astype(bf16)
 
     def return_packed(value, *others):
         shaped = value.astype(bf16).reshape(slots, micro, cap, -1)
@@ -620,7 +638,6 @@
     hidden_one_raw = gather_rows(hidden_one_home)
     hidden_one = after(hidden_one_raw, side_pair[1], *keep_lines[1])
     grad_sent = send_packed(after(dy_home.astype(bf16), hidden_one))
-    grad_rows = quad_rows(grad_sent)
     logits_one = dot(hidden_one, attn_router)
     gates_one, matches_one, chosen_one, gate_vals_one = route_gates(
         logits_one, attn_routes.reshape(all_rows, TOP), expert_table
@@ -632,6 +649,8 @@
 
     kv_part = dot(hidden_one, kv_full).astype(bf16)
     query_part = dot(hidden_one, query_full)
+    grad_sent = after(grad_sent, kv_part)
+    grad_near, grad_far = near_rows(grad_sent), near_rows(swap(grad_sent, "dp", 2))
     lens = first_len[:, 0].astype(jnp.int32)
     gates_wide = wide(gates_one)
     attn_vals, gated_vals, query_rot, key_rot, log_total, peaks = attention_forward(
@@ -642,7 +661,7 @@
         jnp.full((slots, HEADS), very_low, f32), peaks, col * own_heads, 1
     )
     gated_vals = after(gated_vals, grad_sent, *side_lines[0])
-    attn_home = scatter_rows(dot_t(gated_vals, out_full))
+    attn_home = after(scatter_rows(dot_t(gated_vals, out_full)), *side_lines[1], *near_pieces)
 
     resid = x_home + attn_home
     normed_two, scale_two = normalize(resid)
@@ -651,39 +670,41 @@
     gates_two, matches_two, chosen_two, gate_vals_two = route_gates(
         logits_two, home_routes.reshape(home_rows, TOP), expert_table
     )
-    hidden_sent = send_packed(after(hidden_two, grad_rows))
-    hidden_rows = quad_rows(after(hidden_sent, *side_lines[1], *near_pieces))
     gates_by_slot = gates_two.reshape(micro, tok_rows, slots)
     gate_parts = []
     for k in range(slots):
         gate_col = lax.dynamic_index_in_dim(gates_by_slot, col ^ k, 2, keepdims=False)
-        part = jnp.sum(jnp.where(packs[k], gate_col[:, None, :], 0.0), axis=-1).reshape(pack_rows)
-        gate_parts.append(swap(part, "expert", k) if k else part)
-    gate_rows = quad_rows(jnp.concatenate(gate_parts))
-
-    hidden_rows = after(hidden_rows, gate_rows)
+        gate_parts.append(jnp.sum(jnp.where(packs[k], gate_col[:, None, :], 0.0), axis=-1))
+    hidden_sent = send_packed(hidden_two, jnp.stack(gate_parts))
+    hidden_near, hidden_far = near_rows(hidden_sent), swap(hidden_sent, "dp", 2)
     position = jnp.stack([core, chip]).astype(jnp.int32)
-    ffn_part, hidden_part, active, joint_grad = expert_rows(
-        position, hidden_rows, grad_rows, own_pieces, near_pieces
-    )
-
-    def block_grads(steps):
-        return expert_grads(
-            [chip ^ k for k in steps], chip_rows, hidden_rows, grad_rows, gate_rows[:, None],
-            joint_grad, active,
-        )
-
-    line_grads = block_grads([k ^ 1 for k in range(2, chips)])
-    side_got, keep_got = [
-        [
-            [swap(line_grads[4 * line + 2 * which + part], "dp", 4 * line + 4) for line in range(lines - 1)]
-            for part in range(2)
-        ]
-        for which in range(2)
-    ]
-    hidden_sum = quad_sum(hidden_part, *line_grads)
-    own_grads = block_grads([1, 0])
+    near_results = expert_rows(
+        position, hidden_near, after(grad_near, grad_far), own_pieces, near_pieces
+    )
+    hidden_far = near_rows(after(hidden_far, near_results))
+    far_results = expert_rows(position, hidden_far, grad_far, own_pieces, near_pieces)
+    ffn_parts, hidden_parts, actives, joint_grads = zip(near_results, far_results)
+
+    def block_grads(steps, *others):
+        rows = after((hidden_near, hidden_far, grad_near, grad_far), *others)
+        return expert_grads([chip ^ k for k in steps], chip_rows, rows, joint_grads, actives)
+
+    hidden_sum, hidden_far_sum = quad_sums(hidden_parts)
+    ffn_sum, ffn_far_sum = quad_sums(ffn_parts)
+    line_grads = block_grads([k ^ 1 for k in range(2, chips)], hidden_far_sum)
+    side_got, keep_got = [[], []], [[], []]
+    last = ()
+    for which, got in enumerate((side_got, keep_got)):
+        for part in range(2):
+            for line in range(lines - 1):
+                block = after(line_grads[4 * line + 2 * which + part], *last)
+                got[part].append(swap(block, "dp", 4 * line + 4))
+            last = got[part][-1:]
+    hidden_got = after(swap(hidden_far_sum, "dp", 2), *line_grads, ffn_far_sum, ffn_sum)
+    hidden_sum = hidden_sum + hidden_got.astype(f32)
+    own_grads = block_grads([1, 0], hidden_sum)
     back_packed = return_packed(hidden_sum, *own_grads)
+    ffn_sum = ffn_sum + swap(after(ffn_far_sum, hidden_got), "dp", 2).astype(f32)
 
     def total(own, got):
         return functools.reduce(jnp.add, [part.astype(f32) for part in [own] + got]).astype(bf16)
@@ -704,10 +725,8 @@
     gain_two_grad = jnp.sum(hidden_two_grad * normed_two, axis=0)
     resid_grad = dy_home + norm_back(hidden_two_grad * gain_two, normed_two, scale_two)
 
-    ffn_sum = quad_sum(after(ffn_part, hidden_sum))
-
-    resid_grad_low = after(resid_grad.astype(bf16), ffn_sum, *side_got[0])
-    resid_grad_all = after(gather_rows(resid_grad_low), *side_got[1])
+    resid_grad_low = after(resid_grad.astype(bf16), *side_got[0])
+    resid_grad_all = after(gather_rows(resid_grad_low), ffn_sum, *side_got[1])
     ffn_packed = return_packed(after(ffn_sum, resid_grad_all))
     out_home = (resid + unpack(ffn_packed, gates_two)).astype(bf16)
     out_part = t_dot(resid_grad_all, gated_vals).astype(bf16)
@@ -721,14 +740,14 @@
     )[:4]
     kv_grad = jnp.concatenate([key_grad, value_grad], axis=1)
     hidden_one_part = dot_t(query_grad, query_full) + dot_t(kv_grad, kv_full)
-    hidden_one_part = after(hidden_one_part.astype(bf16), other_sums[0])
+    hidden_one_part = hidden_one_part.astype(bf16)
     hidden_one_late = after(hidden_one, hidden_one_part)
     query_part_grad = t_dot(hidden_one_late, query_grad).astype(bf16)
-    kv_part_grad = t_dot(after(hidden_one_late, query_part_grad), kv_grad).astype(bf16)
+    kv_part_grad = t_dot(hidden_one_late, kv_grad).astype(bf16)
     back_one = scatter_rows(
         jnp.concatenate([hidden_one_part, slot_part_one.astype(bf16)], axis=1)
     )
-    back_one = after(back_one, query_part_grad, kv_part_grad, other_sums[1])
+    back_one = after(back_one, query_part_grad, kv_part_grad, other_sums[0])
     hidden_one_grad, slot_one_grad = back_one[:, :width], back_one[:, width : width + slots]
 
     def own(value):
@@ -756,21 +775,22 @@
     ).astype(f32)
     down_grad = jnp.concatenate([b[:, 2 * quarter :] for b in blocks], axis=1).astype(f32)
 
-    results = jnp.stack([out_home, in_home.astype(bf16)]).reshape(2, micro, tok_rows, width)
+    def reduced(value):
+        return lax.psum_scatter(value, "dp", scatter_dimension=0, tiled=True)
+
+    out_grad = slots_of(reduced(out_part))
+    joint_own = reduced(jnp.concatenate([query_part_grad, kv_part_grad], axis=1))
+
+    in_low, out_grad, joint_own = lax.optimization_barrier(
+        (in_home.astype(bf16), out_grad, joint_own, other_sums[1])
+    )[:3]
+    query_own, kv_own = joint_own[:, :query_width], joint_own[:, query_width:]
+    results = jnp.stack([out_home, in_low]).reshape(2, micro, tok_rows, width)
     results = jnp.einsum("mtr,bmtd->bmrd", deal, results, preferred_element_type=f32).astype(bf16)
     results = results.reshape(2 * micro, dp_count, piece_rows, width).transpose(1, 0, 2, 3)
     results = lax.all_to_all(results, "dp", split_axis=0, concat_axis=0, tiled=True)
     results = results.transpose(1, 0, 2, 3).reshape(2, micro, tok_rows, width)
 
-    def reduced(value):
-        return lax.psum_scatter(value, "dp", scatter_dimension=0, tiled=True)
-
-    out_grad = slots_of(reduced(out_part))
-    query_own = reduced(query_part_grad)
-    kv_own = reduced(kv_part_grad)
-    results, out_grad, query_own, kv_own = lax.optimization_barrier(
-        (results, out_grad, query_own, kv_own)
-    )
     out_grad = out_grad.astype(f32)
     query_out = slots_of(query_own).astype(f32)
     key_part, value_part = kv_own[:, :own_width], kv_own[:, own_width:]

time: 1150 us -> 1030 us (0.90)
  waiting for transfers between devices: 588 us -> 459 us
  starting transfers between devices: 97.9 us -> 84.8 us
  local copies, waits for them, and re-layouts: 71.9 us -> 84.2 us
  Pallas kernels: 180 us -> 192 us
    ppermute x73 -> x67, waiting for transfers between devices: 575 us -> 402 us  [swap(): return lax.ppermute(value, axis, [(i, i ^ step) for i in range(count)])]
    all_gather x1, waiting for transfers between devices: 0.01 us -> 27.4 us  [local(): lax.all_gather(after(columns_of(query_in, out_in), side_pair[0], *keep_li...]
    reduce_scatter x3 -> x2, waiting for transfers between devices: 0.04 us -> 17.5 us  [reduced(): return lax.psum_scatter(value, 'dp', scatter_dimension=0, tiled=True)]
    ppermute x73 -> x67, starting transfers between devices: 81.5 us -> 69 us  [swap(): return lax.ppermute(value, axis, [(i, i ^ step) for i in range(count)])]
    pallas_call x1 -> x2, Pallas kernels: 70.6 us -> 80.7 us  [expert_rows(): pl.pallas_call(expert_kernel, grid_spec=pltpu.PrefetchScalarGridSpec(num_...]
    unnamed x184 -> x215, local copies, waits for them, and re-layouts: 18.1 us -> 27.5 us
  transfers between devices with their start and end apart: 84 -> 77, of which waited for: 47 -> 42; matrix products, arithmetic and copies ran while one was open for 19% -> 24% of each run, Pallas kernels for 10% -> 15%
where the time goes in v5:
time: 1030 us; the launch traced here: 1020 us
  waiting for transfers between devices  459 us (45%)
  Pallas kernels  192 us (19%)
  other arithmetic  104 us (10%)
  starting transfers between devices  84.8 us (8%)
  local copies, waits for them, and re-layouts  84.2 us (8%)
  matrix products  81.4 us (8%)
  between operations  16.7 us (2%)
    ppermute x67, waiting for transfers between devices, swap(): return lax.ppermute(value, axis, [(i, i ^ step) for i in range(count)])  402 us
    pallas_call x2, Pallas kernels, expert_rows(): pl.pallas_call(expert_kernel, grid_spec=pltpu.PrefetchScalarGridSpec(num_...  80.7 us
    ppermute x67, starting transfers between devices, swap(): return lax.ppermute(value, axis, [(i, i ^ step) for i in range(count)])  69 us
    pallas_call x2, Pallas kernels, expert_grads(): pl.pallas_call(expert_grad_kernel, grid_spec=pltpu.PrefetchScalarGridSpec...  52.6 us
    pallas_call x1, Pallas kernels, attention_backward(): pl.pallas_call(backward_kernel, grid_spec=pltpu.PrefetchScalarGridSpec(nu...  30 us
    pallas_call x1, Pallas kernels, attention_forward(): pl.pallas_call(forward_kernel, grid_spec=pltpu.PrefetchScalarGridSpec(num...  28.9 us
    unnamed x215, local copies, waits for them, and re-layouts  27.5 us
    all_gather x1, waiting for transfers between devices, local(): lax.all_gather(after(columns_of(query_in, out_in), side_pair[0], *keep_li...  27.4 us
  transfers between devices with their start and end apart: 77, of which 42 were waited for; matrix products, arithmetic and copies ran while one was open for 24% of the time, Pallas kernels for 15%

profile of v5, /device:TPU:8, one launch (start us, length us, event | category | flops | bytes accessed | tf_op | source)
XLA Modules:
  0.0 1022.2 jit_solution(9254895490269361056)
XLA Ops:
  65.6 15.9 %collective-permute-done.5 = bf16[256,1024]{1,0:T(8,128)(2,1)} collective-permute-done((bf16[256,1024]{1,0:T(8,128)(2,1)}, bf16[256,1024]{1,0:T(8,128)(2,1)}, u32[]{:S(2)}, u32[]{:S(2)}) %collective-permute-start.5) | collective-permute-done | bytes 524320 | tf_op jit(solution)/shard_map/ppermute | solution.py:37
  84.9 12.0 %collective-permute-done.6 = bf16[256,1024]{1,0:T(8,128)(2,1)} collective-permute-done((bf16[256,1024]{1,0:T(8,128)(2,1)}, bf16[256,1024]{1,0:T(8,128)(2,1)}, u32[]{:S(2)}, u32[]{:S(2)}) %collective-permute-start.6) | collective-permute-done | bytes 524320 | tf_op jit(solution)/shard_map/ppermute | solution.py:37
  125.2 16.0 %collective-permute-done = bf16[2,64,2048]{2,1,0:T(8,128)(2,1)S(1)} collective-permute-done((bf16[2,64,2048]{2,1,0:T(8,128)(2,1)S(1)}, bf16[2,64,2048]{2,1,0:T(8,128)(2,1)S(1)}, u32[]{:S(2)}, u32[]{:S(2)}) %collective-permute-start) | collective-permute-done | bytes 524320 | tf_op jit(solution)/shard_map/ppermute | solution.py:37
  141.2 17.2 %collective-permute-done.1 = bf16[2,64,2048]{2,1,0:T(8,128)(2,1)S(1)} collective-permute-done((bf16[2,64,2048]{2,1,0:T(8,128)(2,1)S(1)}, bf16[2,64,2048]{2,1,0:T(8,128)(2,1)S(1)}, u32[]{:S(2)}, u32[]{:S(2)}) %collective-permute-start.1) | collective-permute-done | bytes 524320 | tf_op jit(solution)/shard_map/ppermute | solution.py:37
  167.2 20.8 %collective-permute-done.3.refs_1_ = bf16[256,4224]{1,0:T(8,128)(2,1)} collective-permute-done((bf16[256,4224]{1,0:T(8,128)(2,1)}, bf16[256,4224]{1,0:T(8,128)(2,1)}, u32[]{:S(2)}, u32[]{:S(2)}) %collective-permute-start.3) | collective-permute-done | bytes 2162720 | tf_op jit(solution)/shard_map/ppermute | solution.py:37
  207.4 9.5 collective-permute-done.13
  231.1 27.4 %all-gather.3.cloned.1.call-done = bf16[2048,4096]{1,0:T(8,128)(2,1)} async-done(((bf16[256,4096]{1,0:T(8,128)(2,1)}), bf16[2048,4096]{1,0:T(8,128)(2,1)}) %all-gather.3.cloned.1.call-update) | async-done | bytes 16777232 | tf_op jit(solution)/shard_map/all_gather | solution.py:555
  258.5 9.5 fusion.6.query
  268.0 28.9 %attention_forward.1 = (bf16[512,2048]{1,0:T(8,128)(2,1)}, bf16[512,2048]{1,0:T(8,128)(2,1)}, bf16[512,2048]{1,0:T(8,128)(2,1)}, bf16[512,512]{1,0:T(8,128)(2,1)...) custom-call(s32[2]{0:T(128)} %copy-done.86, f32[512,2048]{1,0:T(8,128)} %fusion.6.query, ...), custom_call_target="tpu_custom_call" | custom-call | flops 1073741824 | bytes 14680064 | tf_op jit(solution)/shard_map/attention_forward/pallas_call | solution.py:188
  312.2 19.1 %collective-permute-done.16 = bf16[2,64,2048]{2,1,0:T(8,128)(2,1)S(1)} collective-permute-done((bf16[2,64,2048]{2,1,0:T(8,128)(2,1)S(1)}, bf16[2,64,2048]{2,1,0:T(8,128)(2,1)S(1)}, u32[]{:S(2)}, u32[]{:S(2)}) %collective-permute-start.16) | collective-permute-done | bytes 524320 | tf_op jit(solution)/shard_map/ppermute | solution.py:37
  331.3 14.4 %collective-permute-done.17 = bf16[2,64,2048]{2,1,0:T(8,128)(2,1)S(1)} collective-permute-done((bf16[2,64,2048]{2,1,0:T(8,128)(2,1)S(1)}, bf16[2,64,2048]{2,1,0:T(8,128)(2,1)S(1)}, u32[]{:S(2)}, u32[]{:S(2)}) %collective-permute-start.17) | collective-permute-done | bytes 524320 | tf_op jit(solution)/shard_map/ppermute | solution.py:37
  345.6 11.5 %collective-permute-done.18 = bf16[2,64,2048]{2,1,0:T(8,128)(2,1)S(1)} collective-permute-done((bf16[2,64,2048]{2,1,0:T(8,128)(2,1)S(1)}, bf16[2,64,2048]{2,1,0:T(8,128)(2,1)S(1)}, u32[]{:S(2)}, u32[]{:S(2)}) %collective-permute-start.18) | collective-permute-done | bytes 524320 | tf_op jit(solution)/shard_map/ppermute | solution.py:37
  368.6 28.7 %collective-permute-done.29 = bf16[384,2048]{1,0:T(8,128)(2,1)} collective-permute-done((bf16[384,2048]{1,0:T(8,128)(2,1)}, bf16[384,2048]{1,0:T(8,128)(2,1)}, u32[]{:S(2)}, u32[]{:S(2)}) %collective-permute-start.29) | collective-permute-done | bytes 1572896 | tf_op jit(solution)/shard_map/ppermute | solution.py:37
  414.2 40.3 %expert_rows.2 = (bf16[768,2048]{1,0:T(8,128)(2,1)}, bf16[768,2176]{1,0:T(8,128)(2,1)}, bf16[768,1408]{1,0:T(8,128)(2,1)}, bf16[768,2816]{1,0:T(8,128)(2,1)}) custom-call(s32[2]{0:T(128)} %pad_add_fusion.1.place_ref, bf16[768,2176]{1,0:T(8,128)(2,1)} %pad_maximum_fusion.3.hidden.refs_0_.refs_4_, bf16[768,2048]{1,0:T(8,128)(2,1)} %copy-done.34, ...), custom_call_target="tpu_custom_call" | custom-call | flops 26575110144 | bytes 36175872 | tf_op jit(solution)/shard_map/expert_rows/pallas_call | solution.py:339
  460.0 40.4 %expert_rows.3 = (bf16[768,2048]{1,0:T(8,128)(2,1)}, bf16[768,2176]{1,0:T(8,128)(2,1)}, bf16[768,1408]{1,0:T(8,128)(2,1)}, bf16[768,2816]{1,0:T(8,128)(2,1)}) custom-call(s32[2]{0:T(128)} %pad_add_fusion.1.place_ref, bf16[768,2176]{1,0:T(8,128)(2,1)} %copy-done.32, bf16[768,2048]{1,0:T(8,128)(2,1)} %copy-done.33, ...), custom_call_target="tpu_custom_call" | custom-call | flops 26575110144 | bytes 36175872 | tf_op jit(solution)/shard_map/expert_rows/pallas_call | solution.py:339
  517.7 26.2 %expert_grads.2 = (bf16[256,4224]{1,0:T(8,128)(2,1)}, bf16[256,4224]{1,0:T(8,128)(2,1)}, bf16[256,4224]{1,0:T(8,128)(2,1)}, bf16[256,4224]{1,0:T(8,128)(2,1)}) custom-call(s32[4]{0:T(128)} %get-tuple-element.370.order, bf16[768,2176]{1,0:T(8,128)(2,1)} %pad_maximum_fusion.3.hidden.refs_0_.refs_4_, bf16[768,2176]{1,0:T(8,128)(2,1)} %copy-done.32, ...), custom_call_target="tpu_custom_call" | custom-call | flops 13287555072 | bytes 27918336 | tf_op jit(solution)/shard_map/expert_grads/pallas_call | solution.py:409
  558.3 26.4 %expert_grads.3 = (bf16[256,4224]{1,0:T(8,128)(2,1)}, bf16[256,4224]{1,0:T(8,128)(2,1)}, bf16[256,4224]{1,0:T(8,128)(2,1)}, bf16[256,4224]{1,0:T(8,128)(2,1)}) custom-call(s32[4]{0:T(128)} %get-tuple-element.371.order, bf16[768,2176]{1,0:T(8,128)(2,1)} %pad_maximum_fusion.3.hidden.refs_0_.refs_4_, bf16[768,2176]{1,0:T(8,128)(2,1)} %copy-done.32, ...), custom_call_target="tpu_custom_call" | custom-call | flops 13287555072 | bytes 27918336 | tf_op jit(solution)/shard_map/expert_grads/pallas_call | solution.py:409
  611.3 13.6 %collective-permute-done.43 = bf16[2,64,2048]{2,1,0:T(8,128)(2,1)S(1)} collective-permute-done((bf16[2,64,2048]{2,1,0:T(8,128)(2,1)S(1)}, bf16[2,64,2048]{2,1,0:T(8,128)(2,1)S(1)}, u32[]{:S(2)}, u32[]{:S(2)}) %collective-permute-start.43) | collective-permute-done | bytes 524320 | tf_op jit(solution)/shard_map/ppermute | solution.py:37
  625.8 14.1 %collective-permute-done.44 = bf16[2,64,2048]{2,1,0:T(8,128)(2,1)S(1)} collective-permute-done((bf16[2,64,2048]{2,1,0:T(8,128)(2,1)S(1)}, bf16[2,64,2048]{2,1,0:T(8,128)(2,1)S(1)}, u32[]{:S(2)}, u32[]{:S(2)}) %collective-permute-start.44) | collective-permute-done | bytes 524320 | tf_op jit(solution)/shard_map/ppermute | solution.py:37
  640.8 10.1 collective-permute-done.45
  672.0 10.4 %fusion.vals_grad = f32[512,2048]{1,0:T(8,128)} fusion(bf16[512,2048]{1,0:T(8,128)(2,1)S(1)} %bitcast.414, bf16[2048,4096]{1,0:T(8,128)(2,1)} %all-gather.3.cloned.1.call-done), kind=kOutput, calls=%fused_computation.3 | convolution fusion | flops 4294967296 | bytes 14680064 | tf_op jit(solution)/shard_map/dot_general | solution.py:24
  683.7 9.8 collective-permute-done.48
  706.2 22.4 %collective-permute-done.50 = bf16[256,4224]{1,0:T(8,128)(2,1)} collective-permute-done((bf16[256,4224]{1,0:T(8,128)(2,1)}, bf16[256,4224]{1,0:T(8,128)(2,1)}, u32[]{:S(2)}, u32[]{:S(2)}) %collective-permute-start.50) | collective-permute-done | bytes 2162720 | tf_op jit(solution)/shard_map/ppermute | solution.py:37
  731.5 30.0 %attention_backward.1 = (bf16[512,2048]{1,0:T(8,128)(2,1)}, bf16[512,512]{1,0:T(8,128)(2,1)}, bf16[512,512]{1,0:T(8,128)(2,1)}, f32[512,128]{1,0:T(8,128)}) custom-call(s32[2]{0:T(128)} %copy-done.86, bf16[512,2048]{1,0:T(8,128)(2,1)} %get-tuple-element.144.query, bf16[512,512]{1,0:T(8,128)(2,1)} %get-tuple-element.145.key, ...), custom_call_target="tpu_custom_call" | custom-call | flops 2684354560 | bytes 14680064 | tf_op jit(solution)/shard_map/attention_backward/pallas_call | solution.py:219
  764.4 26.5 %collective-permute-done.51 = bf16[256,4224]{1,0:T(8,128)(2,1)} collective-permute-done((bf16[256,4224]{1,0:T(8,128)(2,1)}, bf16[256,4224]{1,0:T(8,128)(2,1)}, u32[]{:S(2)}, u32[]{:S(2)}) %collective-permute-start.51) | collective-permute-done | bytes 2162720 | tf_op jit(solution)/shard_map/ppermute | solution.py:37
  826.3 17.4 %collective-permute-done.53 = bf16[2,64,2176]{2,1,0:T(8,128)(2,1)S(1)} collective-permute-done((bf16[2,64,2176]{2,1,0:T(8,128)(2,1)S(1)}, bf16[2,64,2176]{2,1,0:T(8,128)(2,1)S(1)}, u32[]{:S(2)}, u32[]{:S(2)}) %collective-permute-start.53) | collective-permute-done | bytes 557088 | tf_op jit(solution)/shard_map/ppermute | solution.py:37
  843.7 11.7 %collective-permute-done.54 = bf16[2,64,2176]{2,1,0:T(8,128)(2,1)S(1)} collective-permute-done((bf16[2,64,2176]{2,1,0:T(8,128)(2,1)S(1)}, bf16[2,64,2176]{2,1,0:T(8,128)(2,1)S(1)}, u32[]{:S(2)}, u32[]{:S(2)}) %collective-permute-start.54) | collective-permute-done | bytes 557088 | tf_op jit(solution)/shard_map/ppermute | solution.py:37
  862.0 14.7 %pad_maximum_fusion = bf16[2048,3072]{0,1:T(8,128)(2,1)} fusion(bf16[2048,1024]{0,1:T(8,128)(2,1)} %convolution_convert_fusion.2, bf16[2048,2048]{0,1:T(8,128)(2,1)} %convolution_convert_fusion), kind=kLoop, calls=%fused_computation | loop fusion | flops 25165824 | bytes 25165824 | tf_op jit(solution)/shard_map/concatenate | solution.py:782
  923.6 8.8 convert_element_type.351
  934.2 14.2 %collective-permute-done.57 = bf16[256,512]{1,0:T(8,128)(2,1)S(1)} collective-permute-done((bf16[256,512]{1,0:T(8,128)(2,1)S(1)}, bf16[256,512]{1,0:T(8,128)(2,1)S(1)}, u32[]{:S(2)}, u32[]{:S(2)}) %collective-permute-start.57) | collective-permute-done | bytes 262176 | tf_op jit(solution)/shard_map/ppermute | solution.py:37
  954.8 17.5 %reduce-scatter.5.cloned.1.call-done = bf16[256,3072]{0,1:T(8,128)(2,1)} async-done(((bf16[2048,3072]{0,1:T(8,128)(2,1)}), bf16[256,3072]{0,1:T(8,128)(2,1)}) %reduce-scatter.5.cloned.1.call-update) | async-done | bytes 1572880 | tf_op jit(solution)/shard_map/reduce_scatter | solution.py:779
  994.5 12.7 %collective-permute-done.66 = bf16[256,512]{1,0:T(8,128)(2,1)} collective-permute-done((bf16[256,512]{1,0:T(8,128)(2,1)}, bf16[256,512]{1,0:T(8,128)(2,1)}, u32[]{:S(2)}, u32[]{:S(2)}) %collective-permute-start.66) | collective-permute-done | bytes 262176 | tf_op jit(solution)/shard_map/ppermute | solution.py:37
  (598 shorter events, 407.3 us)
Async XLA Ops:
  13.3 212.3 %all-gather.5.cloned.1.call-start = ((), (), s32[]{:S(2)}) async-start(), calls=%async_computation.5 | async-start | bytes 4718592 | tf_op jit(solution)/shard_map/all_gather | solution.py:554
  43.5 215.0 %all-gather.3.cloned.1.call-start = ((), (), s32[]{:S(2)}) async-start(), calls=%async_computation.4 | async-start | bytes 18874368 | tf_op jit(solution)/shard_map/all_gather | solution.py:555
  43.6 65.8 %collective-permute-start.8 = (bf16[256,4224]{1,0:T(8,128)(2,1)}, bf16[256,4224]{1,0:T(8,128)(2,1)}, u32[]{:S(2)}, u32[]{:S(2)}) collective-permute-start(bf16[256,4224]{1,0:T(8,128)(2,1)} %pad_maximum_fusion.7), channel_id=1, source_target_pairs={{0,8},{4,12},{8,0},{12,4},{16,24},{20,28},{24,16},{28,20},{1,9},{5... | collective-permute-start | bytes 6488072 | tf_op jit(solution)/shard_map/ppermute | solution.py:37
  45.3 65.2 %collective-permute-start.9 = (bf16[256,4224]{1,0:T(8,128)(2,1)}, bf16[256,4224]{1,0:T(8,128)(2,1)}, u32[]{:S(2)}, u32[]{:S(2)}) collective-permute-start(bf16[256,4224]{1,0:T(8,128)(2,1)} %pad_maximum_fusion.5), channel_id=1, source_target_pairs={{0,16},{4,20},{8,24},{12,28},{16,0},{20,4},{24,8},{28,12},{1,17},{... | collective-permute-start | bytes 6488072 | tf_op jit(solution)/shard_map/ppermute | solution.py:37
  52.3 48.0 %collective-permute-start.7 = (bf16[256,1024]{1,0:T(8,128)(2,1)}, bf16[256,1024]{1,0:T(8,128)(2,1)}, u32[]{:S(2)}, u32[]{:S(2)}) collective-permute-start(bf16[256,1024]{1,0:T(8,128)(2,1)} %pad_maximum_fusion.14), channel_id=1, source_target_pairs={{0,3},{1,2},{2,1},{3,0},{4,7},{5,6},{6,5},{7,4},{8,11},{9,10},{10,... | collective-permute-start | bytes 1572872 | tf_op jit(solution)/shard_map/ppermute | solution.py:37
  110.5 805.1 %reduce-scatter.3.cloned.1.call-start = ((), (), s32[]{:S(2)}) async-start(), calls=%async_computation.6 | async-start | bytes 9437184 | tf_op jit(solution)/shard_map/reduce_scatter | solution.py:779
  111.0 77.0 %collective-permute-start.3 = (bf16[256,4224]{1,0:T(8,128)(2,1)}, bf16[256,4224]{1,0:T(8,128)(2,1)}, u32[]{:S(2)}, u32[]{:S(2)}) collective-permute-start(bf16[256,4224]{1,0:T(8,128)(2,1)} %pad_maximum_fusion.8), channel_id=1, source_target_pairs={{0,8},{4,12},{8,0},{12,4},{16,24},{20,28},{24,16},{28,20},{1,9},{5... | collective-permute-start | bytes 6488072 | tf_op jit(solution)/shard_map/ppermute | solution.py:37
  111.8 77.7 %collective-permute-start.4 = (bf16[256,4224]{1,0:T(8,128)(2,1)}, bf16[256,4224]{1,0:T(8,128)(2,1)}, u32[]{:S(2)}, u32[]{:S(2)}) collective-permute-start(bf16[256,4224]{1,0:T(8,128)(2,1)} %pad_maximum_fusion.6.refs_0_), channel_id=1, source_target_pairs={{0,16},{4,20},{8,24},{12,28},{16,0},{20,4},{24,8},{28,12},{1,17},{... | collective-permute-start | bytes 6488072 | tf_op jit(solution)/shard_map/ppermute | solution.py:37
  123.5 43.6 %collective-permute-start.2 = (bf16[2,64,2048]{2,1,0:T(8,128)(2,1)S(1)}, bf16[2,64,2048]{2,1,0:T(8,128)(2,1)S(1)}, u32[]{:S(2)}, u32[]{:S(2)}) collective-permute-start(bf16[2,64,2048]{2,1,0:T(8,128)(2,1)S(1)} %get-tuple-element.279), channel_id=1, source_target_pairs={{0,3},{1,2},{2,1},{3,0},{4,7},{5,6},{6,5},{7,4},{8,11},{9,10},{10,... | collective-permute-start | bytes 1572872 | tf_op jit(solution)/shard_map/ppermute | solution.py:37
  200.0 96.9 %collective-permute-start.15 = (bf16[256,4224]{1,0:T(8,128)(2,1)}, bf16[256,4224]{1,0:T(8,128)(2,1)}, u32[]{:S(2)}, u32[]{:S(2)}) collective-permute-start(bf16[256,4224]{1,0:T(8,128)(2,1)} %collective-permute-done.8), channel_id=1, source_target_pairs={{0,16},{4,20},{8,24},{12,28},{16,0},{20,4},{24,8},{28,12},{1,17},{... | collective-permute-start | bytes 6488072 | tf_op jit(solution)/shard_map/ppermute | solution.py:37
  308.9 36.8 %collective-permute-start.17 = (bf16[2,64,2048]{2,1,0:T(8,128)(2,1)S(1)}, bf16[2,64,2048]{2,1,0:T(8,128)(2,1)S(1)}, u32[]{:S(2)}, u32[]{:S(2)}) collective-permute-start(bf16[2,64,2048]{2,1,0:T(8,128)(2,1)S(1)} %get-tuple-element.296), channel_id=1, source_target_pairs={{0,2},{1,3},{2,0},{3,1},{4,6},{5,7},{6,4},{7,5},{8,10},{9,11},{10,... | collective-permute-start | bytes 1572872 | tf_op jit(solution)/shard_map/ppermute | solution.py:37
  310.8 46.3 %collective-permute-start.18 = (bf16[2,64,2048]{2,1,0:T(8,128)(2,1)S(1)}, bf16[2,64,2048]{2,1,0:T(8,128)(2,1)S(1)}, u32[]{:S(2)}, u32[]{:S(2)}) collective-permute-start(bf16[2,64,2048]{2,1,0:T(8,128)(2,1)S(1)} %get-tuple-element.295), channel_id=1, source_target_pairs={{0,3},{1,2},{2,1},{3,0},{4,7},{5,6},{6,5},{7,4},{8,11},{9,10},{10,... | collective-permute-start | bytes 1572872 | tf_op jit(solution)/shard_map/ppermute | solution.py:37
  311.3 48.8 %collective-permute-start.20 = (bf16[256,4224]{1,0:T(8,128)(2,1)}, bf16[256,4224]{1,0:T(8,128)(2,1)}, u32[]{:S(2)}, u32[]{:S(2)}) collective-permute-start(bf16[256,4224]{1,0:T(8,128)(2,1)} %pad_maximum_fusion.5), channel_id=1, source_target_pairs={{0,4},{4,0},{8,12},{12,8},{16,20},{20,16},{24,28},{28,24},{1,5},{5... | collective-permute-start | bytes 6488072 | tf_op jit(solution)/shard_map/ppermute | solution.py:37
  311.3 50.0 %collective-permute-start.19 = (bf16[256,4224]{1,0:T(8,128)(2,1)}, bf16[256,4224]{1,0:T(8,128)(2,1)}, u32[]{:S(2)}, u32[]{:S(2)}) collective-permute-start(bf16[256,4224]{1,0:T(8,128)(2,1)} %collective-permute-done.3.refs_1_), channel_id=1, source_target_pairs={{0,16},{4,20},{8,24},{12,28},{16,0},{20,4},{24,8},{28,12},{1,17},{... | collective-permute-start | bytes 6488072 | tf_op jit(solution)/shard_map/ppermute | solution.py:37
  360.1 37.2 %collective-permute-start.29 = (bf16[384,2048]{1,0:T(8,128)(2,1)}, bf16[384,2048]{1,0:T(8,128)(2,1)}, u32[]{:S(2)}, u32[]{:S(2)}) collective-permute-start(bf16[384,2048]{1,0:T(8,128)(2,1)} %bitcast.47), channel_id=1, source_target_pairs={{0,8},{4,12},{8,0},{12,4},{16,24},{20,28},{24,16},{28,20},{1,9},{5... | collective-permute-start | bytes 4718600 | tf_op jit(solution)/shard_map/ppermute | solution.py:37
  368.1 36.8 %collective-permute-start.26 = (bf16[2,48,2176]{2,1,0:T(8,128)(2,1)S(1)}, bf16[2,48,2176]{2,1,0:T(8,128)(2,1)S(1)}, u32[]{:S(2)}, u32[]{:S(2)}) collective-permute-start(bf16[2,48,2176]{2,1,0:T(8,128)(2,1)S(1)} %get-tuple-element.313), channel_id=1, source_target_pairs={{0,3},{1,2},{2,1},{3,0},{4,7},{5,6},{6,5},{7,4},{8,11},{9,10},{10,... | collective-permute-start | bytes 1253384 | tf_op jit(solution)/shard_map/ppermute | solution.py:37
  368.6 40.2 %collective-permute-start.28 = (bf16[384,2048]{1,0:T(8,128)(2,1)}, bf16[384,2048]{1,0:T(8,128)(2,1)S(1)}, u32[]{:S(2)}, u32[]{:S(2)}) collective-permute-start(bf16[384,2048]{1,0:T(8,128)(2,1)} %bitcast.47), channel_id=1, source_target_pairs={{0,4},{4,0},{8,12},{12,8},{16,20},{20,16},{24,28},{28,24},{1,5},{5... | collective-permute-start | bytes 4718600 | tf_op jit(solution)/shard_map/ppermute | solution.py:37
  411.1 43.4 %collective-permute-start.32 = (bf16[384,2176]{1,0:T(8,128)(2,1)S(1)}, bf16[384,2176]{1,0:T(8,128)(2,1)S(1)}, u32[]{:S(2)}, u32[]{:S(2)}) collective-permute-start(bf16[384,2176]{1,0:T(8,128)(2,1)S(1)} %bitcast.403), channel_id=1, source_target_pairs={{0,8},{4,12},{8,0},{12,4},{16,24},{20,28},{24,16},{28,20},{1,9},{5... | collective-permute-start | bytes 5013512 | tf_op jit(solution)/shard_map/ppermute | solution.py:37
  511.5 41.0 %collective-permute-start.38 = (bf16[384,2176]{1,0:T(8,128)(2,1)}, bf16[384,2176]{1,0:T(8,128)(2,1)}, u32[]{:S(2)}, u32[]{:S(2)}) collective-permute-start(bf16[384,2176]{1,0:T(8,128)(2,1)} %split.31), channel_id=1, source_target_pairs={{0,4},{4,0},{8,12},{12,8},{16,20},{20,16},{24,28},{28,24},{1,5},{5... | collective-permute-start | bytes 5013512 | tf_op jit(solution)/shard_map/ppermute | solution.py:37
  511.8 139.3 %collective-permute-start.31 = (bf16[384,2048]{1,0:T(8,128)(2,1)}, bf16[384,2048]{1,0:T(8,128)(2,1)}, u32[]{:S(2)}, u32[]{:S(2)}) collective-permute-start(bf16[384,2048]{1,0:T(8,128)(2,1)} %split.25), channel_id=1, source_target_pairs={{0,4},{4,0},{8,12},{12,8},{16,20},{20,16},{24,28},{28,24},{1,5},{5... | collective-permute-start | bytes 4718600 | tf_op jit(solution)/shard_map/ppermute | solution.py:37
  513.7 38.8 %collective-permute-start.36 = (bf16[384,2176]{1,0:T(8,128)(2,1)}, bf16[384,2176]{1,0:T(8,128)(2,1)S(1)}, u32[]{:S(2)}, u32[]{:S(2)}) collective-permute-start(bf16[384,2176]{1,0:T(8,128)(2,1)} %add_convert_fusion.5), channel_id=1, source_target_pairs={{0,8},{4,12},{8,0},{12,4},{16,24},{20,28},{24,16},{28,20},{1,9},{5... | collective-permute-start | bytes 5013512 | tf_op jit(solution)/shard_map/ppermute | solution.py:37
  543.9 59.8 %collective-permute-start.42 = (bf16[256,4224]{1,0:T(8,128)(2,1)}, bf16[256,4224]{1,0:T(8,128)(2,1)}, u32[]{:S(2)}, u32[]{:S(2)}) collective-permute-start(bf16[256,4224]{1,0:T(8,128)(2,1)} %get-tuple-element.118), channel_id=1, source_target_pairs={{0,16},{4,20},{8,24},{12,28},{16,0},{20,4},{24,8},{28,12},{1,17},{... | collective-permute-start | bytes 6488072 | tf_op jit(solution)/shard_map/ppermute | solution.py:37
  584.7 66.3 %collective-permute-start.37 = (bf16[384,2048]{1,0:T(8,128)(2,1)}, bf16[384,2048]{1,0:T(8,128)(2,1)}, u32[]{:S(2)}, u32[]{:S(2)}) collective-permute-start(bf16[384,2048]{1,0:T(8,128)(2,1)} %add_convert_fusion.6), channel_id=1, source_target_pairs={{0,8},{4,12},{8,0},{12,4},{16,24},{20,28},{24,16},{28,20},{1,9},{5... | collective-permute-start | bytes 4718600 | tf_op jit(solution)/shard_map/ppermute | solution.py:37
  603.7 36.2 %collective-permute-start.44 = (bf16[2,64,2048]{2,1,0:T(8,128)(2,1)S(1)}, bf16[2,64,2048]{2,1,0:T(8,128)(2,1)S(1)}, u32[]{:S(2)}, u32[]{:S(2)}) collective-permute-start(bf16[2,64,2048]{2,1,0:T(8,128)(2,1)S(1)} %bitcast.420), channel_id=1, source_target_pairs={{0,2},{1,3},{2,0},{3,1},{4,6},{5,7},{6,4},{7,5},{8,10},{9,11},{10,... | collective-permute-start | bytes 1572872 | tf_op jit(solution)/shard_map/ppermute | solution.py:37
  606.7 47.8 %collective-permute-start.46 = (bf16[256,4224]{1,0:T(8,128)(2,1)S(1)}, bf16[256,4224]{1,0:T(8,128)(2,1)}, u32[]{:S(2)}, u32[]{:S(2)}) collective-permute-start(bf16[256,4224]{1,0:T(8,128)(2,1)S(1)} %copy-done.93), channel_id=1, source_target_pairs={{0,16},{4,20},{8,24},{12,28},{16,0},{20,4},{24,8},{28,12},{1,17},{... | collective-permute-start | bytes 6488072 | tf_op jit(solution)/shard_map/ppermute | solution.py:37
  639.9 216.7 %collective-permute-start.55 = (bf16[256,4224]{1,0:T(8,128)(2,1)}, bf16[256,4224]{1,0:T(8,128)(2,1)}, u32[]{:S(2)}, u32[]{:S(2)}) collective-permute-start(bf16[256,4224]{1,0:T(8,128)(2,1)} %add_convert_fusion.3), channel_id=1, source_target_pairs={{0,8},{4,12},{8,0},{12,4},{16,24},{20,28},{24,16},{28,20},{1,9},{5... | collective-permute-start | bytes 6488072 | tf_op jit(solution)/shard_map/ppermute | solution.py:37
  661.5 67.1 %collective-permute-start.50 = (bf16[256,4224]{1,0:T(8,128)(2,1)}, bf16[256,4224]{1,0:T(8,128)(2,1)}, u32[]{:S(2)}, u32[]{:S(2)}) collective-permute-start(bf16[256,4224]{1,0:T(8,128)(2,1)} %get-tuple-element.147), channel_id=1, source_target_pairs={{0,16},{4,20},{8,24},{12,28},{16,0},{20,4},{24,8},{28,12},{1,17},{... | collective-permute-start | bytes 6488072 | tf_op jit(solution)/shard_map/ppermute | solution.py:37
  667.3 305.0 %reduce-scatter.5.cloned.1.call-start = ((), (), s32[]{:S(2)}) async-start(), calls=%async_computation.7 | async-start | bytes 14155776 | tf_op jit(solution)/shard_map/reduce_scatter | solution.py:779
  682.4 200.6 %collective-permute-start.59 = (bf16[256,4224]{1,0:T(8,128)(2,1)}, bf16[256,4224]{1,0:T(8,128)(2,1)}, u32[]{:S(2)}, u32[]{:S(2)}) collective-permute-start(bf16[256,4224]{1,0:T(8,128)(2,1)} %add_convert_fusion.2), channel_id=1, source_target_pairs={{0,8},{4,12},{8,0},{12,4},{16,24},{20,28},{24,16},{28,20},{1,9},{5... | collective-permute-start | bytes 6488072 | tf_op jit(solution)/shard_map/ppermute | solution.py:37
  728.6 62.4 %collective-permute-start.51 = (bf16[256,4224]{1,0:T(8,128)(2,1)}, bf16[256,4224]{1,0:T(8,128)(2,1)}, u32[]{:S(2)}, u32[]{:S(2)}) collective-permute-start(bf16[256,4224]{1,0:T(8,128)(2,1)} %get-tuple-element.154), channel_id=1, source_target_pairs={{0,16},{4,20},{8,24},{12,28},{16,0},{20,4},{24,8},{28,12},{1,17},{... | collective-permute-start | bytes 6488072 | tf_op jit(solution)/shard_map/ppermute | solution.py:37
  804.8 38.9 %collective-permute-start.53 = (bf16[2,64,2176]{2,1,0:T(8,128)(2,1)S(1)}, bf16[2,64,2176]{2,1,0:T(8,128)(2,1)S(1)}, u32[]{:S(2)}, u32[]{:S(2)}) collective-permute-start(bf16[2,64,2176]{2,1,0:T(8,128)(2,1)S(1)} %get-tuple-element.303), channel_id=1, source_target_pairs={{0,2},{1,3},{2,0},{3,1},{4,6},{5,7},{6,4},{7,5},{8,10},{9,11},{10,... | collective-permute-start | bytes 1671176 | tf_op jit(solution)/shard_map/ppermute | solution.py:37
  806.7 48.6 %collective-permute-start.54 = (bf16[2,64,2176]{2,1,0:T(8,128)(2,1)S(1)}, bf16[2,64,2176]{2,1,0:T(8,128)(2,1)S(1)}, u32[]{:S(2)}, u32[]{:S(2)}) collective-permute-start(bf16[2,64,2176]{2,1,0:T(8,128)(2,1)S(1)} %get-tuple-element.302), channel_id=1, source_target_pairs={{0,3},{1,2},{2,1},{3,0},{4,7},{5,6},{6,5},{7,4},{8,11},{9,10},{10,... | collective-permute-start | bytes 1671176 | tf_op jit(solution)/shard_map/ppermute | solution.py:37
  (143 other events, 2589.2 us)
Sparse Core Ops, SparseCore 0:
  43.6 56.5 all-gather.4
  110.6 147.8 all-gather.2
  667.4 104.2 reduce-scatter.2
  876.8 95.4 reduce-scatter.4

commit v6 on v5

--- a/solution.py
+++ b/solution.py
@@ -50,15 +50,6 @@
 
 def after(value, *others):
     return lax.optimization_barrier((value, others))[0]
-
-
-def spread(value, combine):
-    for axis in ("expert", "dp"):
-        step = 1
-        while step < lax.axis_size(axis):
-            value = combine(value, swap(value, axis, step))
-            step *= 2
-    return value
 
 
 def rotation_tables(places):
@@ -329,7 +320,7 @@
     rows, width = grad.shape
     columns = near_pieces[0].shape[1]
     units = columns // 3
-    tile = 256
+    tile = 384 if rows % 384 == 0 else 256
     shape = jax.ShapeDtypeStruct
     count = len(own_pieces)
 
@@ -488,19 +479,6 @@
     parts = (1 - core, core)
     keep_pair = [quarter_of(side, part) for part in parts]
     send_pair = [quarter_of(1 - side, part) for part in parts]
-    keep_pair, send_pair, kv_in, query_in, out_in = lax.optimization_barrier(
-        (keep_pair, send_pair, kv_weight, query_weight[0], attn_out_weight[0])
-    )
-    side_pair = [swap(piece, "dp", 2) for piece in send_pair]
-    line_steps = [4 * line for line in range(1, lines)]
-    keep_lines = [[swap(piece, "dp", step) for step in line_steps] for piece in keep_pair]
-    side_lines = [[swap(piece, "dp", step) for step in line_steps] for piece in side_pair]
-    pairs = [keep_pair, side_pair]
-    for line in range(lines - 1):
-        pairs += [[part[line] for part in keep_lines], [part[line] for part in side_lines]]
-    near_pieces = [swap(pair[0], "dp", 1) for pair in pairs]
-    own_pieces = [pair[1] for pair in pairs]
-
     both = both.transpose(1, 0, 2, 3).reshape(2, micro, tok_rows, width)
     deal = (dealing[:, :, None] == jnp.arange(tok_rows, dtype=jnp.int32)).astype(bf16)
     work = jnp.einsum("mtr,bmrd->bmtd", deal, both, preferred_element_type=f32)
@@ -541,7 +519,7 @@
     second_pairs += [(c, 2 * (c - half_slots)) for c in range(half_slots, slots)]
     holds_keys = col < half_slots
     even_col = col % 2 == 0
-    low_kv, high_kv = kv_in[:, :own_width], kv_in[:, own_width:]
+    low_kv, high_kv = kv_weight[:, :own_width], kv_weight[:, own_width:]
     first_got = lax.ppermute(jnp.where(holds_keys, low_kv, high_kv), "expert", first_pairs)
     second_got = lax.ppermute(jnp.where(holds_keys, high_kv, low_kv), "expert", second_pairs)
     own_kv = jnp.concatenate(
@@ -552,9 +530,24 @@
         axis=1,
     )
     kv_full = lax.all_gather(after(own_kv, work), "dp", axis=0, tiled=True)
+    line_steps = [4 * line for line in range(1, lines)]
+    side_first = swap(send_pair[0], "dp", 2)
+    keep_first = [swap(keep_pair[0], "dp", step) for step in line_steps]
+    joint_own = columns_of(query_weight[0], attn_out_weight[0])
     joint_full = lax.all_gather(
-        after(columns_of(query_in, out_in), side_pair[0], *keep_lines[0]), "dp", axis=0, tiled=True
-    )
+        after(joint_own, side_first, keep_first), "dp", axis=0, tiled=True
+    )
+    late_pair = after((keep_pair[1], send_pair[1], side_first), joint_full)
+    keep_second = [swap(late_pair[0], "dp", step) for step in line_steps]
+    side_second = swap(late_pair[1], "dp", 2)
+    first_lines = [swap(late_pair[2], "dp", step) for step in line_steps]
+    second_lines = [swap(after(side_second, first_lines), "dp", step) for step in line_steps]
+    firsts, seconds = [keep_pair[0], side_first], [keep_pair[1], side_second]
+    for line in range(lines - 1):
+        firsts += [keep_first[line], first_lines[line]]
+        seconds += [keep_second[line], second_lines[line]]
+    near_pieces = [swap(piece, "dp", 1) for piece in firsts]
+    own_pieces = seconds
     query_full, out_full = joint_full[:, :query_width], joint_full[:, query_width:]
 
     positions = jnp.arange(group_rows, dtype=jnp.int32)
@@ -636,7 +629,7 @@
     normed_one, scale_one = normalize(x_home)
     hidden_one_home = (normed_one * gain_one).astype(bf16)
     hidden_one_raw = gather_rows(hidden_one_home)
-    hidden_one = after(hidden_one_raw, side_pair[1], *keep_lines[1])
+    hidden_one = hidden_one_raw
     grad_sent = send_packed(after(dy_home.astype(bf16), hidden_one))
     logits_one = dot(hidden_one, attn_router)
     gates_one, matches_one, chosen_one, gate_vals_one = route_gates(
@@ -649,19 +642,16 @@
 
     kv_part = dot(hidden_one, kv_full).astype(bf16)
     query_part = dot(hidden_one, query_full)
-    grad_sent = after(grad_sent, kv_part)
+    grad_sent = after(grad_sent, kv_part, joint_full)
     grad_near, grad_far = near_rows(grad_sent), near_rows(swap(grad_sent, "dp", 2))
     lens = first_len[:, 0].astype(jnp.int32)
     gates_wide = wide(gates_one)
     attn_vals, gated_vals, query_rot, key_rot, log_total, peaks = attention_forward(
         lens, query_part, kv_part, tables, gates_wide, wide(hits_one), own_heads, group_rows
     )
-    peaks = jnp.max(peaks, axis=0)[: own_heads * slots].reshape(own_heads, slots).T
-    peak_table = lax.dynamic_update_slice_in_dim(
-        jnp.full((slots, HEADS), very_low, f32), peaks, col * own_heads, 1
-    )
-    gated_vals = after(gated_vals, grad_sent, *side_lines[0])
-    attn_home = after(scatter_rows(dot_t(gated_vals, out_full)), *side_lines[1], *near_pieces)
+    peaks = jnp.max(peaks, axis=0)[: own_heads * slots]
+    gated_vals = after(gated_vals, keep_second, side_second)
+    attn_home = after(scatter_rows(dot_t(gated_vals, out_full)), first_lines, grad_near, grad_far)
 
     resid = x_home + attn_home
     normed_two, scale_two = normalize(resid)
@@ -677,6 +667,7 @@
         gate_parts.append(jnp.sum(jnp.where(packs[k], gate_col[:, None, :], 0.0), axis=-1))
     hidden_sent = send_packed(hidden_two, jnp.stack(gate_parts))
     hidden_near, hidden_far = near_rows(hidden_sent), swap(hidden_sent, "dp", 2)
+    hidden_near = after(hidden_near, second_lines, near_pieces)
     position = jnp.stack([core, chip]).astype(jnp.int32)
     near_results = expert_rows(
         position, hidden_near, after(grad_near, grad_far), own_pieces, near_pieces
@@ -726,17 +717,17 @@
     resid_grad = dy_home + norm_back(hidden_two_grad * gain_two, normed_two, scale_two)
 
     resid_grad_low = after(resid_grad.astype(bf16), *side_got[0])
-    resid_grad_all = after(gather_rows(resid_grad_low), ffn_sum, *side_got[1])
-    ffn_packed = return_packed(after(ffn_sum, resid_grad_all))
+    resid_grad_all = after(gather_rows(resid_grad_low), ffn_sum)
+    out_part = t_dot(resid_grad_all, gated_vals).astype(bf16)
+    vals_grad = after(dot(resid_grad_all, out_full), out_part, side_got[1])
+    ffn_packed = return_packed(after(ffn_sum, vals_grad))
     out_home = (resid + unpack(ffn_packed, gates_two)).astype(bf16)
-    out_part = t_dot(resid_grad_all, gated_vals).astype(bf16)
-    vals_grad = after(dot(resid_grad_all, out_full), out_part, *keep_got[0])
     query_grad, key_grad, value_grad, slot_part_one = attention_backward(
         lens, query_rot, key_rot, kv_part, attn_vals, vals_grad, tables, gates_wide, log_total,
         own_heads, group_rows,
     )
     query_grad, key_grad, value_grad, slot_part_one = lax.optimization_barrier(
-        (query_grad, key_grad, value_grad, slot_part_one, ffn_packed, keep_got[1])
+        (query_grad, key_grad, value_grad, slot_part_one, ffn_packed, keep_got[0])
     )[:4]
     kv_grad = jnp.concatenate([key_grad, value_grad], axis=1)
     hidden_one_part = dot_t(query_grad, query_full) + dot_t(kv_grad, kv_full)
@@ -747,7 +738,7 @@
     back_one = scatter_rows(
         jnp.concatenate([hidden_one_part, slot_part_one.astype(bf16)], axis=1)
     )
-    back_one = after(back_one, query_part_grad, kv_part_grad, other_sums[0])
+    back_one = after(back_one, query_part_grad, kv_part_grad, keep_got[1])
     hidden_one_grad, slot_one_grad = back_one[:, :width], back_one[:, width : width + slots]
 
     def own(value):
@@ -781,15 +772,44 @@
     out_grad = slots_of(reduced(out_part))
     joint_own = reduced(jnp.concatenate([query_part_grad, kv_part_grad], axis=1))
 
-    in_low, out_grad, joint_own = lax.optimization_barrier(
-        (in_home.astype(bf16), out_grad, joint_own, other_sums[1])
-    )[:3]
     query_own, kv_own = joint_own[:, :query_width], joint_own[:, query_width:]
+    in_low, out_grad = lax.optimization_barrier(
+        (in_home.astype(bf16), out_grad, other_sums[0])
+    )[:2]
     results = jnp.stack([out_home, in_low]).reshape(2, micro, tok_rows, width)
     results = jnp.einsum("mtr,bmtd->bmrd", deal, results, preferred_element_type=f32).astype(bf16)
     results = results.reshape(2 * micro, dp_count, piece_rows, width).transpose(1, 0, 2, 3)
+    results = results.reshape(dp_count, 2 * micro * piece_rows, width)
+    sent_back = results.shape[1]
+    small = jnp.concatenate(
+        [gain_one_grad[None], gain_two_grad[None], router_one_grad, router_two_grad], axis=0
+    ).astype(bf16)
+    sum_rows = small.shape[0]
+    peak_count = own_heads * slots
+    peak_parts, rest = [], peaks
+    for _ in range(3):
+        peak_parts.append(lax.reduce_precision(rest, 8, 7))
+        rest = rest - peak_parts[-1]
+    peak_row = jnp.concatenate(peak_parts).astype(bf16)
+    small = jnp.pad(small, ((0, -sum_rows % 16 or 16), (0, 0)))
+    small = lax.dynamic_update_slice(small, peak_row[None], (sum_rows, 0))
+    small = jnp.broadcast_to(small[None], (dp_count,) + small.shape)
+    results = jnp.concatenate([results, small], axis=1)
     results = lax.all_to_all(results, "dp", split_axis=0, concat_axis=0, tiled=True)
+    small = results[:, sent_back:].astype(f32)
+    results = results[:, :sent_back].reshape(dp_count, 2 * micro, piece_rows, width)
     results = results.transpose(1, 0, 2, 3).reshape(2, micro, tok_rows, width)
+    peak_row = small[:, sum_rows, : 3 * peak_count].reshape(dp_count, 3, peak_count)
+    peak_row = jnp.max((peak_row[:, 0] + peak_row[:, 1]) + peak_row[:, 2], axis=0)
+    small = jnp.sum(small, axis=0)
+    small = lax.dynamic_update_slice(small, peak_row[None], (sum_rows, 0))
+    small = place(
+        [swap(small, "expert", k) if k else small for k in range(slots)],
+        [col ^ k for k in range(slots)],
+    )
+    sums = jnp.sum(small[:, :sum_rows], axis=0)
+    peaks_all = small[:, sum_rows, :peak_count].reshape(slots, own_heads, slots)
+    peaks_all = peaks_all.transpose(2, 0, 1).reshape(slots, HEADS)
 
     out_grad = out_grad.astype(f32)
     query_out = slots_of(query_own).astype(f32)
@@ -808,18 +828,6 @@
         axis=1,
     ).astype(f32)
 
-    sum_rows = 2 + 2 * slots
-    peak_rows = jnp.pad(peak_table, ((0, 0), (0, width - HEADS)))
-    sums = spread(
-        jnp.concatenate(
-            [gain_one_grad[None], gain_two_grad[None], router_one_grad, router_two_grad, peak_rows],
-            axis=0,
-        ),
-        lambda left, right: jnp.where(
-            jnp.arange(sum_rows + slots)[:, None] < sum_rows, left + right, jnp.maximum(left, right)
-        ),
-    )
-    peaks_all = sums[sum_rows:, :HEADS]
     limit = clip_limit[0].astype(f32)
     factor = limit / jnp.maximum(peaks_all, limit)
     query_scale = jnp.repeat(jnp.sqrt(take(factor, col)), HDIM)

time: 1030 us -> 1050 us (1.019)
  other arithmetic: 104 us -> 119 us
  local copies, waits for them, and re-layouts: 84.2 us -> 95.5 us
    all_gather x1, waiting for transfers between devices: 27.4 us -> 0.01 us  [local(): lax.all_gather(after(joint_own, side_first, keep_first), 'dp', axis=0, ti...]
    ppermute x1, waiting for transfers between devices: 0.01 us -> 19.1 us  [local(): lax.ppermute(jnp.where(even_col, key_part, value_part), 'expert', [(b, a)...]
    ppermute x67 -> x65, waiting for transfers between devices: 402 us -> 420 us  [swap(): return lax.ppermute(value, axis, [(i, i ^ step) for i in range(count)])]
    reduce_scatter x2, waiting for transfers between devices: 17.5 us -> 0.01 us  [reduced(): return lax.psum_scatter(value, 'dp', scatter_dimension=0, tiled=True)]
    unnamed x215 -> x250, local copies, waits for them, and re-layouts: 27.5 us -> 35.3 us
    ppermute x67 -> x65, starting transfers between devices: 69 us -> 66.9 us  [swap(): return lax.ppermute(value, axis, [(i, i ^ step) for i in range(count)])]
  transfers between devices with their start and end apart: 77 -> 75, of which waited for: 42 -> 43; matrix products, arithmetic and copies ran while one was open for 24% -> 25% of each run, Pallas kernels for 15% -> 15%
where the time goes in v6:
time: 1050 us; the launch traced here: 1040 us
  waiting for transfers between devices  459 us (44%)
  Pallas kernels  193 us (18%)
  other arithmetic  119 us (11%)
  local copies, waits for them, and re-layouts  95.5 us (9%)
  starting transfers between devices  83 us (8%)
  matrix products  76.7 us (7%)
  between operations  17.2 us (2%)
    ppermute x65, waiting for transfers between devices, swap(): return lax.ppermute(value, axis, [(i, i ^ step) for i in range(count)])  420 us
    pallas_call x2, Pallas kernels, expert_rows(): pl.pallas_call(expert_kernel, grid_spec=pltpu.PrefetchScalarGridSpec(num_...  81.7 us
    ppermute x65, starting transfers between devices, swap(): return lax.ppermute(value, axis, [(i, i ^ step) for i in range(count)])  66.9 us
    pallas_call x2, Pallas kernels, expert_grads(): pl.pallas_call(expert_grad_kernel, grid_spec=pltpu.PrefetchScalarGridSpec...  52.6 us
    unnamed x250, local copies, waits for them, and re-layouts  35.3 us
    pallas_call x1, Pallas kernels, attention_backward(): pl.pallas_call(backward_kernel, grid_spec=pltpu.PrefetchScalarGridSpec(nu...  30.2 us
    pallas_call x1, Pallas kernels, attention_forward(): pl.pallas_call(forward_kernel, grid_spec=pltpu.PrefetchScalarGridSpec(num...  28.8 us
    dot_general x5, matrix products, dot(): return jnp.dot(left, right, preferred_element_type=f32)  26.7 us
  transfers between devices with their start and end apart: 75, of which 43 were waited for; matrix products, arithmetic and copies ran while one was open for 25% of the time, Pallas kernels for 15%

profile of v6, /device:TPU:8, one launch (start us, length us, event | category | flops | bytes accessed | tf_op | source)
XLA Modules:
  0.0 1043.3 jit_solution(3601839529979737420)
XLA Ops:
  34.2 12.3 %collective-permute-done.3 = bf16[256,1024]{1,0:T(8,128)(2,1)} collective-permute-done((bf16[256,1024]{1,0:T(8,128)(2,1)}, bf16[256,1024]{1,0:T(8,128)(2,1)}, u32[]{:S(2)}, u32[]{:S(2)}) %collective-permute-start.3) | collective-permute-done | bytes 524320 | tf_op jit(solution)/shard_map/ppermute | solution.py:37
  48.5 16.4 %collective-permute-done.4 = bf16[256,1024]{1,0:T(8,128)(2,1)} collective-permute-done((bf16[256,1024]{1,0:T(8,128)(2,1)}, bf16[256,1024]{1,0:T(8,128)(2,1)}, u32[]{:S(2)}, u32[]{:S(2)}) %collective-permute-start.4) | collective-permute-done | bytes 524320 | tf_op jit(solution)/shard_map/ppermute | solution.py:37
  132.1 11.6 %collective-permute-done = bf16[2,64,2048]{2,1,0:T(8,128)(2,1)S(1)} collective-permute-done((bf16[2,64,2048]{2,1,0:T(8,128)(2,1)S(1)}, bf16[2,64,2048]{2,1,0:T(8,128)(2,1)S(1)}, u32[]{:S(2)}, u32[]{:S(2)}) %collective-permute-start) | collective-permute-done | bytes 524320 | tf_op jit(solution)/shard_map/ppermute | solution.py:37
  143.7 21.5 %collective-permute-done.1 = bf16[2,64,2048]{2,1,0:T(8,128)(2,1)S(1)} collective-permute-done((bf16[2,64,2048]{2,1,0:T(8,128)(2,1)S(1)}, bf16[2,64,2048]{2,1,0:T(8,128)(2,1)S(1)}, u32[]{:S(2)}, u32[]{:S(2)}) %collective-permute-start.1) | collective-permute-done | bytes 524320 | tf_op jit(solution)/shard_map/ppermute | solution.py:37
  186.4 14.9 %collective-permute-done.17 = bf16[2,48,2048]{2,1,0:T(8,128)(2,1)} collective-permute-done((bf16[2,48,2048]{2,1,0:T(8,128)(2,1)}, bf16[2,48,2048]{2,1,0:T(8,128)(2,1)}, u32[]{:S(2)}, u32[]{:S(2)}) %collective-permute-start.17) | collective-permute-done | bytes 393248 | tf_op jit(solution)/shard_map/ppermute | solution.py:37
  227.9 9.5 fusion.6.query
  237.5 28.8 %attention_forward.1 = (bf16[512,2048]{1,0:T(8,128)(2,1)}, bf16[512,2048]{1,0:T(8,128)(2,1)}, bf16[512,2048]{1,0:T(8,128)(2,1)}, bf16[512,512]{1,0:T(8,128)(2,1)...) custom-call(s32[2]{0:T(128)} %copy-done.103, f32[512,2048]{1,0:T(8,128)} %fusion.6.query, ...), custom_call_target="tpu_custom_call" | custom-call | flops 1073741824 | bytes 14680064 | tf_op jit(solution)/shard_map/attention_forward/pallas_call | solution.py:179
  266.3 26.9 %collective-permute-done.20 = bf16[384,2048]{1,0:T(8,128)(2,1)} collective-permute-done((bf16[384,2048]{1,0:T(8,128)(2,1)}, bf16[384,2048]{1,0:T(8,128)(2,1)}, u32[]{:S(2)}, u32[]{:S(2)}) %collective-permute-start.20) | collective-permute-done | bytes 1572896 | tf_op jit(solution)/shard_map/ppermute | solution.py:37
  307.8 16.5 %collective-permute-done.12 = bf16[2,64,2048]{2,1,0:T(8,128)(2,1)S(1)} collective-permute-done((bf16[2,64,2048]{2,1,0:T(8,128)(2,1)S(1)}, bf16[2,64,2048]{2,1,0:T(8,128)(2,1)S(1)}, u32[]{:S(2)}, u32[]{:S(2)}) %collective-permute-start.12) | collective-permute-done | bytes 524320 | tf_op jit(solution)/shard_map/ppermute | solution.py:37
  324.3 14.6 %collective-permute-done.13 = bf16[2,64,2048]{2,1,0:T(8,128)(2,1)S(1)} collective-permute-done((bf16[2,64,2048]{2,1,0:T(8,128)(2,1)S(1)}, bf16[2,64,2048]{2,1,0:T(8,128)(2,1)S(1)}, u32[]{:S(2)}, u32[]{:S(2)}) %collective-permute-start.13) | collective-permute-done | bytes 524320 | tf_op jit(solution)/shard_map/ppermute | solution.py:37
  338.9 11.5 %collective-permute-done.14 = bf16[2,64,2048]{2,1,0:T(8,128)(2,1)S(1)} collective-permute-done((bf16[2,64,2048]{2,1,0:T(8,128)(2,1)S(1)}, bf16[2,64,2048]{2,1,0:T(8,128)(2,1)S(1)}, u32[]{:S(2)}, u32[]{:S(2)}) %collective-permute-start.14) | collective-permute-done | bytes 524320 | tf_op jit(solution)/shard_map/ppermute | solution.py:37
  357.9 13.2 %collective-permute-done.22 = bf16[2,48,2176]{2,1,0:T(8,128)(2,1)S(1)} collective-permute-done((bf16[2,48,2176]{2,1,0:T(8,128)(2,1)S(1)}, bf16[2,48,2176]{2,1,0:T(8,128)(2,1)S(1)}, u32[]{:S(2)}, u32[]{:S(2)}) %collective-permute-start.22) | collective-permute-done | bytes 417824 | tf_op jit(solution)/shard_map/ppermute | solution.py:37
  371.1 14.3 %collective-permute-done.23 = bf16[2,48,2176]{2,1,0:T(8,128)(2,1)S(1)} collective-permute-done((bf16[2,48,2176]{2,1,0:T(8,128)(2,1)S(1)}, bf16[2,48,2176]{2,1,0:T(8,128)(2,1)S(1)}, u32[]{:S(2)}, u32[]{:S(2)}) %collective-permute-start.23) | collective-permute-done | bytes 417824 | tf_op jit(solution)/shard_map/ppermute | solution.py:37
  411.2 32.8 %collective-permute-done.26.refs_3_ = bf16[256,4224]{1,0:T(8,128)(2,1)S(1)} collective-permute-done((bf16[256,4224]{1,0:T(8,128)(2,1)}, bf16[256,4224]{1,0:T(8,128)(2,1)S(1)}, u32[]{:S(2)}, u32[]{:S(2)}) %collective-permute-start.26) | collective-permute-done | bytes 2162720 | tf_op jit(solution)/shard_map/ppermute | solution.py:37
  445.3 40.7 %expert_rows.2 = (bf16[768,2048]{1,0:T(8,128)(2,1)}, bf16[768,2176]{1,0:T(8,128)(2,1)}, bf16[768,1408]{1,0:T(8,128)(2,1)}, bf16[768,2816]{1,0:T(8,128)(2,1)}) custom-call(s32[2]{0:T(128)} %pad_add_fusion.1.place_ref, bf16[768,2176]{1,0:T(8,128)(2,1)} %pad_maximum_fusion.3.hidden.refs_0_.refs_4_, bf16[768,2048]{1,0:T(8,128)(2,1)} %copy-done.52, ...), custom_call_target="tpu_custom_call" | custom-call | flops 26575110144 | bytes 36175872 | tf_op jit(solution)/shard_map/expert_rows/pallas_call | solution.py:330
  491.0 40.9 %expert_rows.3 = (bf16[768,2048]{1,0:T(8,128)(2,1)}, bf16[768,2176]{1,0:T(8,128)(2,1)}, bf16[768,1408]{1,0:T(8,128)(2,1)}, bf16[768,2816]{1,0:T(8,128)(2,1)}) custom-call(s32[2]{0:T(128)} %pad_add_fusion.1.place_ref, bf16[768,2176]{1,0:T(8,128)(2,1)} %constant_dynamic-update-slice_fusion.4.hidden.refs_1_.refs_5_, bf16[768,2048]{1,0:T(8,128)(2,1)} %copy-done.53, ...), custom_call_target="tpu_custom_call" | custom-call | flops 26575110144 | bytes 36175872 | tf_op jit(solution)/shard_map/expert_rows/pallas_call | solution.py:330
  549.8 26.2 %expert_grads.2 = (bf16[256,4224]{1,0:T(8,128)(2,1)}, bf16[256,4224]{1,0:T(8,128)(2,1)}, bf16[256,4224]{1,0:T(8,128)(2,1)}, bf16[256,4224]{1,0:T(8,128)(2,1)}) custom-call(s32[4]{0:T(128)} %get-tuple-element.365.order, bf16[768,2176]{1,0:T(8,128)(2,1)} %pad_maximum_fusion.3.hidden.refs_0_.refs_4_, ...), custom_call_target="tpu_custom_call" | custom-call | flops 13287555072 | bytes 27918336 | tf_op jit(solution)/shard_map/expert_grads/pallas_call | solution.py:400
  590.5 26.4 %expert_grads.3 = (bf16[256,4224]{1,0:T(8,128)(2,1)}, bf16[256,4224]{1,0:T(8,128)(2,1)}, bf16[256,4224]{1,0:T(8,128)(2,1)}, bf16[256,4224]{1,0:T(8,128)(2,1)}) custom-call(s32[4]{0:T(128)} %get-tuple-element.366.order, bf16[768,2176]{1,0:T(8,128)(2,1)} %pad_maximum_fusion.3.hidden.refs_0_.refs_4_, ...), custom_call_target="tpu_custom_call" | custom-call | flops 13287555072 | bytes 27918336 | tf_op jit(solution)/shard_map/expert_grads/pallas_call | solution.py:400
  643.1 12.4 %collective-permute-done.43 = bf16[2,64,2048]{2,1,0:T(8,128)(2,1)S(1)} collective-permute-done((bf16[2,64,2048]{2,1,0:T(8,128)(2,1)S(1)}, bf16[2,64,2048]{2,1,0:T(8,128)(2,1)S(1)}, u32[]{:S(2)}, u32[]{:S(2)}) %collective-permute-start.43) | collective-permute-done | bytes 524320 | tf_op jit(solution)/shard_map/ppermute | solution.py:37
  657.0 16.6 %collective-permute-done.44 = bf16[2,64,2048]{2,1,0:T(8,128)(2,1)S(1)} collective-permute-done((bf16[2,64,2048]{2,1,0:T(8,128)(2,1)S(1)}, bf16[2,64,2048]{2,1,0:T(8,128)(2,1)S(1)}, u32[]{:S(2)}, u32[]{:S(2)}) %collective-permute-start.44) | collective-permute-done | bytes 524320 | tf_op jit(solution)/shard_map/ppermute | solution.py:37
  674.2 8.7 collective-permute-done.45
  693.4 10.7 %fusion.vals_grad = f32[512,2048]{1,0:T(8,128)} fusion(bf16[512,2048]{1,0:T(8,128)(2,1)} %bitcast.430, bf16[2048,4096]{1,0:T(8,128)(2,1)} %all-gather.3.cloned.1.call-done), kind=kOutput, calls=%fused_computation.3 | convolution fusion | flops 4294967296 | bytes 14680064 | tf_op jit(solution)/shard_map/dot_general | solution.py:24
  713.7 30.2 %attention_backward.1 = (bf16[512,2048]{1,0:T(8,128)(2,1)}, bf16[512,512]{1,0:T(8,128)(2,1)}, bf16[512,512]{1,0:T(8,128)(2,1)}, f32[512,128]{1,0:T(8,128)}) custom-call(s32[2]{0:T(128)} %copy-done.103, bf16[512,2048]{1,0:T(8,128)(2,1)} %get-tuple-element.138.query, bf16[512,512]{1,0:T(8,128)(2,1)} %get-tuple-element.139.key, ...), custom_call_target="tpu_custom_call" | custom-call | flops 2684354560 | bytes 14680064 | tf_op jit(solution)/shard_map/attention_backward/pallas_call | solution.py:210
  747.8 26.0 %collective-permute-done.50 = bf16[256,4224]{1,0:T(8,128)(2,1)} collective-permute-done((bf16[256,4224]{1,0:T(8,128)(2,1)}, bf16[256,4224]{1,0:T(8,128)(2,1)}, u32[]{:S(2)}, u32[]{:S(2)}) %collective-permute-start.50) | collective-permute-done | bytes 2162720 | tf_op jit(solution)/shard_map/ppermute | solution.py:37
  780.9 8.8 add_convert_fusion.4
  801.0 29.5 %collective-permute-done.54 = bf16[256,4224]{1,0:T(8,128)(2,1)} collective-permute-done((bf16[256,4224]{1,0:T(8,128)(2,1)}, bf16[256,4224]{1,0:T(8,128)(2,1)}, u32[]{:S(2)}, u32[]{:S(2)}) %collective-permute-start.54) | collective-permute-done | bytes 2162720 | tf_op jit(solution)/shard_map/ppermute | solution.py:37
  845.0 14.6 %pad_maximum_fusion = bf16[2048,3072]{0,1:T(8,128)(2,1)} fusion(bf16[2048,1024]{0,1:T(8,128)(2,1)S(1)} %convolution_convert_fusion.2, bf16[2048,2048]{0,1:T(8,128)(2,1)S(1)} %convolution_convert_fusion), kind=kLoop, calls=%fused_computation | loop fusion | flops 25165824 | bytes 25165824 | tf_op jit(solution)/shard_map/concatenate | solution.py:773
  864.2 15.1 %collective-permute-done.52 = bf16[2,64,2176]{2,1,0:T(8,128)(2,1)} collective-permute-done((bf16[2,64,2176]{2,1,0:T(8,128)(2,1)}, bf16[2,64,2176]{2,1,0:T(8,128)(2,1)}, u32[]{:S(2)}, u32[]{:S(2)}) %collective-permute-start.52) | collective-permute-done | bytes 557088 | tf_op jit(solution)/shard_map/ppermute | solution.py:37
  879.3 12.2 %collective-permute-done.53 = bf16[2,64,2176]{2,1,0:T(8,128)(2,1)} collective-permute-done((bf16[2,64,2176]{2,1,0:T(8,128)(2,1)}, bf16[2,64,2176]{2,1,0:T(8,128)(2,1)}, u32[]{:S(2)}, u32[]{:S(2)}) %collective-permute-start.53) | collective-permute-done | bytes 557088 | tf_op jit(solution)/shard_map/ppermute | solution.py:37
  930.0 13.1 %collective-permute-done.56 = bf16[256,512]{1,0:T(8,128)(2,1)S(1)} collective-permute-done((bf16[256,512]{1,0:T(8,128)(2,1)S(1)}, bf16[256,512]{1,0:T(8,128)(2,1)S(1)}, u32[]{:S(2)}, u32[]{:S(2)}) %collective-permute-start.56) | collective-permute-done | bytes 262176 | tf_op jit(solution)/shard_map/ppermute | solution.py:37
  956.1 8.6 convert_element_type.366
  1006.6 19.1 %collective-permute-done.65 = bf16[256,512]{0,1:T(8,128)(2,1)S(1)} collective-permute-done((bf16[256,512]{0,1:T(8,128)(2,1)}, bf16[256,512]{0,1:T(8,128)(2,1)S(1)}, u32[]{:S(2)}, u32[]{:S(2)}) %collective-permute-start.65) | collective-permute-done | bytes 262176 | tf_op jit(solution)/shard_map/ppermute | solution.py:817
  (644 shorter events, 421.2 us)
Async XLA Ops:
  7.2 202.2 %all-gather.3.cloned.1.call-start = ((), (), s32[]{:S(2)}) async-start(), calls=%async_computation.4 | async-start | bytes 18874368 | tf_op jit(solution)/shard_map/all_gather | solution.py:537
  14.5 62.6 %collective-permute-start.7 = (bf16[256,4224]{1,0:T(8,128)(2,1)}, bf16[256,4224]{1,0:T(8,128)(2,1)}, u32[]{:S(2)}, u32[]{:S(2)}) collective-permute-start(bf16[256,4224]{1,0:T(8,128)(2,1)} %pad_maximum_fusion.6), channel_id=1, source_target_pairs={{0,16},{4,20},{8,24},{12,28},{16,0},{20,4},{24,8},{28,12},{1,17},{... | collective-permute-start | bytes 6488072 | tf_op jit(solution)/shard_map/ppermute | solution.py:37
  17.5 59.6 %collective-permute-start.6 = (bf16[256,4224]{1,0:T(8,128)(2,1)}, bf16[256,4224]{1,0:T(8,128)(2,1)}, u32[]{:S(2)}, u32[]{:S(2)}) collective-permute-start(bf16[256,4224]{1,0:T(8,128)(2,1)} %pad_maximum_fusion.5), channel_id=1, source_target_pairs={{0,8},{4,12},{8,0},{12,4},{16,24},{20,28},{24,16},{28,20},{1,9},{5... | collective-permute-start | bytes 6488072 | tf_op jit(solution)/shard_map/ppermute | solution.py:37
  31.0 44.1 %collective-permute-start.5 = (bf16[256,1024]{1,0:T(8,128)(2,1)}, bf16[256,1024]{1,0:T(8,128)(2,1)}, u32[]{:S(2)}, u32[]{:S(2)}) collective-permute-start(bf16[256,1024]{1,0:T(8,128)(2,1)} %pad_maximum_fusion.15), channel_id=1, source_target_pairs={{0,3},{1,2},{2,1},{3,0},{4,7},{5,6},{6,5},{7,4},{8,11},{9,10},{10,... | collective-permute-start | bytes 1572872 | tf_op jit(solution)/shard_map/ppermute | solution.py:37
  84.4 131.9 %all-gather.5.cloned.1.call-start = ((), (), s32[]{:S(2)}) async-start(), calls=%async_computation.5 | async-start | bytes 4718592 | tf_op jit(solution)/shard_map/all_gather | solution.py:532
  111.6 804.7 %reduce-scatter.3.cloned.1.call-start = ((), (), s32[]{:S(2)}) async-start(), calls=%async_computation.6 | async-start | bytes 9437184 | tf_op jit(solution)/shard_map/reduce_scatter | solution.py:770
  130.6 41.6 %collective-permute-start.2 = (bf16[2,64,2048]{2,1,0:T(8,128)(2,1)S(1)}, bf16[2,64,2048]{2,1,0:T(8,128)(2,1)S(1)}, u32[]{:S(2)}, u32[]{:S(2)}) collective-permute-start(bf16[2,64,2048]{2,1,0:T(8,128)(2,1)S(1)} %get-tuple-element.269), channel_id=1, source_target_pairs={{0,3},{1,2},{2,1},{3,0},{4,7},{5,6},{6,5},{7,4},{8,11},{9,10},{10,... | collective-permute-start | bytes 1572872 | tf_op jit(solution)/shard_map/ppermute | solution.py:37
  209.4 83.8 %collective-permute-start.11 = (bf16[256,4224]{1,0:T(8,128)(2,1)}, bf16[256,4224]{1,0:T(8,128)(2,1)}, u32[]{:S(2)}, u32[]{:S(2)}) collective-permute-start(bf16[256,4224]{1,0:T(8,128)(2,1)} %pad_maximum_fusion.8), channel_id=1, source_target_pairs={{0,8},{4,12},{8,0},{12,4},{16,24},{20,28},{24,16},{28,20},{1,9},{5... | collective-permute-start | bytes 6488072 | tf_op jit(solution)/shard_map/ppermute | solution.py:37
  213.2 79.9 %collective-permute-start.10 = (bf16[256,4224]{1,0:T(8,128)(2,1)}, bf16[256,4224]{1,0:T(8,128)(2,1)}, u32[]{:S(2)}, u32[]{:S(2)}) collective-permute-start(bf16[256,4224]{1,0:T(8,128)(2,1)} %pad_maximum_fusion.7.refs_0_), channel_id=1, source_target_pairs={{0,16},{4,20},{8,24},{12,28},{16,0},{20,4},{24,8},{28,12},{1,17},{... | collective-permute-start | bytes 6488072 | tf_op jit(solution)/shard_map/ppermute | solution.py:37
  221.7 71.4 %collective-permute-start.20 = (bf16[384,2048]{1,0:T(8,128)(2,1)}, bf16[384,2048]{1,0:T(8,128)(2,1)}, u32[]{:S(2)}, u32[]{:S(2)}) collective-permute-start(bf16[384,2048]{1,0:T(8,128)(2,1)} %bitcast.47), channel_id=1, source_target_pairs={{0,8},{4,12},{8,0},{12,4},{16,24},{20,28},{24,16},{28,20},{1,9},{5... | collective-permute-start | bytes 4718600 | tf_op jit(solution)/shard_map/ppermute | solution.py:37
  224.6 79.5 %collective-permute-start.19 = (bf16[384,2048]{1,0:T(8,128)(2,1)}, bf16[384,2048]{1,0:T(8,128)(2,1)}, u32[]{:S(2)}, u32[]{:S(2)}) collective-permute-start(bf16[384,2048]{1,0:T(8,128)(2,1)} %bitcast.47), channel_id=1, source_target_pairs={{0,4},{4,0},{8,12},{12,8},{16,20},{20,16},{24,28},{28,24},{1,5},{5... | collective-permute-start | bytes 4718600 | tf_op jit(solution)/shard_map/ppermute | solution.py:37
  224.6 126.3 %collective-permute-start.15 = (bf16[256,4224]{1,0:T(8,128)(2,1)}, bf16[256,4224]{1,0:T(8,128)(2,1)}, u32[]{:S(2)}, u32[]{:S(2)}) collective-permute-start(bf16[256,4224]{1,0:T(8,128)(2,1)} %collective-permute-done.6), channel_id=1, source_target_pairs={{0,16},{4,20},{8,24},{12,28},{16,0},{20,4},{24,8},{28,12},{1,17},{... | collective-permute-start | bytes 6488072 | tf_op jit(solution)/shard_map/ppermute | solution.py:37
  293.2 57.5 %collective-permute-start.21 = (bf16[384,2048]{1,0:T(8,128)(2,1)}, bf16[384,2048]{1,0:T(8,128)(2,1)S(1)}, u32[]{:S(2)}, u32[]{:S(2)}) collective-permute-start(bf16[384,2048]{1,0:T(8,128)(2,1)} %collective-permute-done.20), channel_id=1, source_target_pairs={{0,4},{4,0},{8,12},{12,8},{16,20},{20,16},{24,28},{28,24},{1,5},{5... | collective-permute-start | bytes 4718600 | tf_op jit(solution)/shard_map/ppermute | solution.py:37
  304.1 46.3 %collective-permute-start.14 = (bf16[2,64,2048]{2,1,0:T(8,128)(2,1)S(1)}, bf16[2,64,2048]{2,1,0:T(8,128)(2,1)S(1)}, u32[]{:S(2)}, u32[]{:S(2)}) collective-permute-start(bf16[2,64,2048]{2,1,0:T(8,128)(2,1)S(1)} %get-tuple-element.285), channel_id=1, source_target_pairs={{0,3},{1,2},{2,1},{3,0},{4,7},{5,6},{6,5},{7,4},{8,11},{9,10},{10,... | collective-permute-start | bytes 1572872 | tf_op jit(solution)/shard_map/ppermute | solution.py:37
  394.8 49.2 %collective-permute-start.26 = (bf16[256,4224]{1,0:T(8,128)(2,1)}, bf16[256,4224]{1,0:T(8,128)(2,1)S(1)}, u32[]{:S(2)}, u32[]{:S(2)}) collective-permute-start(bf16[256,4224]{1,0:T(8,128)(2,1)} %collective-permute-done.11.refs_1_), channel_id=1, source_target_pairs={{0,16},{4,20},{8,24},{12,28},{16,0},{20,4},{24,8},{28,12},{1,17},{... | collective-permute-start | bytes 6488072 | tf_op jit(solution)/shard_map/ppermute | solution.py:37
  398.9 46.4 %collective-permute-start.30 = (bf16[256,4224]{1,0:T(8,128)(2,1)}, bf16[256,4224]{1,0:T(8,128)(2,1)}, u32[]{:S(2)}, u32[]{:S(2)}) collective-permute-start(bf16[256,4224]{1,0:T(8,128)(2,1)} %collective-permute-done.15), channel_id=1, source_target_pairs={{0,4},{4,0},{8,12},{12,8},{16,20},{20,16},{24,28},{28,24},{1,5},{5... | collective-permute-start | bytes 6488072 | tf_op jit(solution)/shard_map/ppermute | solution.py:37
  401.5 84.5 %collective-permute-start.32 = (bf16[384,2176]{1,0:T(8,128)(2,1)S(1)}, bf16[384,2176]{1,0:T(8,128)(2,1)S(1)}, u32[]{:S(2)}, u32[]{:S(2)}) collective-permute-start(bf16[384,2176]{1,0:T(8,128)(2,1)S(1)} %bitcast.420), channel_id=1, source_target_pairs={{0,8},{4,12},{8,0},{12,4},{16,24},{20,28},{24,16},{28,20},{1,9},{5... | collective-permute-start | bytes 5013512 | tf_op jit(solution)/shard_map/ppermute | solution.py:37
  543.9 40.9 %collective-permute-start.38 = (bf16[384,2176]{1,0:T(8,128)(2,1)}, bf16[384,2176]{1,0:T(8,128)(2,1)}, u32[]{:S(2)}, u32[]{:S(2)}) collective-permute-start(bf16[384,2176]{1,0:T(8,128)(2,1)} %split.31), channel_id=1, source_target_pairs={{0,4},{4,0},{8,12},{12,8},{16,20},{20,16},{24,28},{28,24},{1,5},{5... | collective-permute-start | bytes 5013512 | tf_op jit(solution)/shard_map/ppermute | solution.py:37
  544.0 138.9 %collective-permute-start.31 = (bf16[384,2048]{1,0:T(8,128)(2,1)}, bf16[384,2048]{1,0:T(8,128)(2,1)}, u32[]{:S(2)}, u32[]{:S(2)}) collective-permute-start(bf16[384,2048]{1,0:T(8,128)(2,1)} %split.25), channel_id=1, source_target_pairs={{0,4},{4,0},{8,12},{12,8},{16,20},{20,16},{24,28},{28,24},{1,5},{5... | collective-permute-start | bytes 4718600 | tf_op jit(solution)/shard_map/ppermute | solution.py:37
  546.0 38.8 %collective-permute-start.36 = (bf16[384,2176]{1,0:T(8,128)(2,1)}, bf16[384,2176]{1,0:T(8,128)(2,1)S(1)}, u32[]{:S(2)}, u32[]{:S(2)}) collective-permute-start(bf16[384,2176]{1,0:T(8,128)(2,1)} %add_convert_fusion.5), channel_id=1, source_target_pairs={{0,8},{4,12},{8,0},{12,4},{16,24},{20,28},{24,16},{28,20},{1,9},{5... | collective-permute-start | bytes 5013512 | tf_op jit(solution)/shard_map/ppermute | solution.py:37
  576.0 59.8 %collective-permute-start.42 = (bf16[256,4224]{1,0:T(8,128)(2,1)}, bf16[256,4224]{1,0:T(8,128)(2,1)}, u32[]{:S(2)}, u32[]{:S(2)}) collective-permute-start(bf16[256,4224]{1,0:T(8,128)(2,1)} %get-tuple-element.111), channel_id=1, source_target_pairs={{0,16},{4,20},{8,24},{12,28},{16,0},{20,4},{24,8},{28,12},{1,17},{... | collective-permute-start | bytes 6488072 | tf_op jit(solution)/shard_map/ppermute | solution.py:37
  616.9 66.1 %collective-permute-start.37 = (bf16[384,2048]{1,0:T(8,128)(2,1)}, bf16[384,2048]{1,0:T(8,128)(2,1)}, u32[]{:S(2)}, u32[]{:S(2)}) collective-permute-start(bf16[384,2048]{1,0:T(8,128)(2,1)} %add_convert_fusion.6), channel_id=1, source_target_pairs={{0,8},{4,12},{8,0},{12,4},{16,24},{20,28},{24,16},{28,20},{1,9},{5... | collective-permute-start | bytes 4718600 | tf_op jit(solution)/shard_map/ppermute | solution.py:37
  638.8 44.1 %collective-permute-start.45 = (bf16[2,64,2048]{2,1,0:T(8,128)(2,1)S(1)}, bf16[2,64,2048]{2,1,0:T(8,128)(2,1)S(1)}, u32[]{:S(2)}, u32[]{:S(2)}) collective-permute-start(bf16[2,64,2048]{2,1,0:T(8,128)(2,1)S(1)} %bitcast.437), channel_id=1, source_target_pairs={{0,3},{1,2},{2,1},{3,0},{4,7},{5,6},{6,5},{7,4},{8,11},{9,10},{10,... | collective-permute-start | bytes 1572872 | tf_op jit(solution)/shard_map/ppermute | solution.py:37
  655.5 48.7 %collective-permute-start.46 = (bf16[256,4224]{1,0:T(8,128)(2,1)}, bf16[256,4224]{1,0:T(8,128)(2,1)}, u32[]{:S(2)}, u32[]{:S(2)}) collective-permute-start(bf16[256,4224]{1,0:T(8,128)(2,1)} %get-tuple-element.131), channel_id=1, source_target_pairs={{0,16},{4,20},{8,24},{12,28},{16,0},{20,4},{24,8},{28,12},{1,17},{... | collective-permute-start | bytes 6488072 | tf_op jit(solution)/shard_map/ppermute | solution.py:37
  673.6 159.1 %collective-permute-start.58 = (bf16[256,4224]{1,0:T(8,128)(2,1)}, bf16[256,4224]{1,0:T(8,128)(2,1)}, u32[]{:S(2)}, u32[]{:S(2)}) collective-permute-start(bf16[256,4224]{1,0:T(8,128)(2,1)} %add_convert_fusion.3), channel_id=1, source_target_pairs={{0,8},{4,12},{8,0},{12,4},{16,24},{20,28},{24,16},{28,20},{1,9},{5... | collective-permute-start | bytes 6488072 | tf_op jit(solution)/shard_map/ppermute | solution.py:37
  693.4 302.9 %reduce-scatter.5.cloned.1.call-start = ((), (), s32[]{:S(2)}) async-start(), calls=%async_computation.7 | async-start | bytes 14155776 | tf_op jit(solution)/shard_map/reduce_scatter | solution.py:770
  704.2 69.7 %collective-permute-start.50 = (bf16[256,4224]{1,0:T(8,128)(2,1)}, bf16[256,4224]{1,0:T(8,128)(2,1)}, u32[]{:S(2)}, u32[]{:S(2)}) collective-permute-start(bf16[256,4224]{1,0:T(8,128)(2,1)} %get-tuple-element.146), channel_id=1, source_target_pairs={{0,16},{4,20},{8,24},{12,28},{16,0},{20,4},{24,8},{28,12},{1,17},{... | collective-permute-start | bytes 6488072 | tf_op jit(solution)/shard_map/ppermute | solution.py:37
  743.9 88.8 %collective-permute-start.67 = (bf16[256,4224]{1,0:T(8,128)(2,1)}, bf16[256,4224]{1,0:T(8,128)(2,1)S(1)}, u32[]{:S(2)}, u32[]{:S(2)}) collective-permute-start(bf16[256,4224]{1,0:T(8,128)(2,1)} %add_convert_fusion), channel_id=1, source_target_pairs={{0,8},{4,12},{8,0},{12,4},{16,24},{20,28},{24,16},{28,20},{1,9},{5... | collective-permute-start | bytes 6488072 | tf_op jit(solution)/shard_map/ppermute | solution.py:37
  773.9 56.7 %collective-permute-start.54 = (bf16[256,4224]{1,0:T(8,128)(2,1)}, bf16[256,4224]{1,0:T(8,128)(2,1)}, u32[]{:S(2)}, u32[]{:S(2)}) collective-permute-start(bf16[256,4224]{1,0:T(8,128)(2,1)} %get-tuple-element.152), channel_id=1, source_target_pairs={{0,16},{4,20},{8,24},{12,28},{16,0},{20,4},{24,8},{28,12},{1,17},{... | collective-permute-start | bytes 6488072 | tf_op jit(solution)/shard_map/ppermute | solution.py:37
  837.8 64.6 %collective-permute-start.68 = (bf16[2,256,4224]{2,1,0:T(8,128)(2,1)}, bf16[2,256,4224]{2,1,0:T(8,128)(2,1)}, u32[]{:S(2)}, u32[]{:S(2)}) collective-permute-start(bf16[2,256,4224]{2,1,0:T(8,128)(2,1)} %broadcast_select_fusion.2), channel_id=1, source_target_pairs={{0,4},{4,0},{8,12},{12,8},{16,20},{20,16},{24,28},{28,24},{1,5},{5... | collective-permute-start | bytes 12976136 | tf_op jit(solution)/shard_map/ppermute | solution.py:37
  839.8 39.4 %collective-permute-start.52 = (bf16[2,64,2176]{2,1,0:T(8,128)(2,1)}, bf16[2,64,2176]{2,1,0:T(8,128)(2,1)}, u32[]{:S(2)}, u32[]{:S(2)}) collective-permute-start(bf16[2,64,2176]{2,1,0:T(8,128)(2,1)} %get-tuple-element.293), channel_id=1, source_target_pairs={{0,2},{1,3},{2,0},{3,1},{4,6},{5,7},{6,4},{7,5},{8,10},{9,11},{10,... | collective-permute-start | bytes 1671176 | tf_op jit(solution)/shard_map/ppermute | solution.py:37
  842.1 49.4 %collective-permute-start.53 = (bf16[2,64,2176]{2,1,0:T(8,128)(2,1)}, bf16[2,64,2176]{2,1,0:T(8,128)(2,1)}, u32[]{:S(2)}, u32[]{:S(2)}) collective-permute-start(bf16[2,64,2176]{2,1,0:T(8,128)(2,1)} %get-tuple-element.292), channel_id=1, source_target_pairs={{0,3},{1,2},{2,1},{3,0},{4,7},{5,6},{6,5},{7,4},{8,11},{9,10},{10,... | collective-permute-start | bytes 1671176 | tf_op jit(solution)/shard_map/ppermute | solution.py:37
  (156 other events, 2460.5 us)
Sparse Core Ops, SparseCore 0:
  78.5 97.0 all-gather.2
  178.1 38.1 all-gather.4
  693.5 104.1 reduce-scatter.2
  859.8 92.1 reduce-scatter.4

commit v7 on v6

--- a/solution.py
+++ b/solution.py
@@ -82,105 +82,107 @@
     lens, query, key, value, cosine, sine, gates, hits,
     vals_out, gated_out, query_out, key_out, total_out, peak_out,
 ):
-    m, h, s = pl.program_id(0), pl.program_id(1), pl.program_id(2)
-    slot_count = pl.num_programs(2)
+    m, h = pl.program_id(0), pl.program_id(1)
+    heads = pl.num_programs(1)
     rows = query.shape[0]
-    lane = h * slot_count + s
-
-    @pl.when(lane == 0)
+    slots = query.shape[1] // (heads * HDIM)
+
+    @pl.when(h == 0)
     def _():
         total_out[...] = jnp.zeros_like(total_out)
         peak_out[...] = jnp.full_like(peak_out, very_low)
 
-    @pl.when(s == 0)
-    def _():
-        key_out[...] = turn(key[...].astype(f32), cosine[...], sine[...]).astype(bf16)
-
-    turned = turn(query[...], cosine[...], sine[...]).astype(bf16)
-    query_out[...] = turned
-    raw = dot_t(turned, key_out[...])
-    scores = jnp.where(allowed_pairs(rows, lens[m]), raw * HDIM ** (-0.5), very_low)
-    row_peak = jnp.max(scores, axis=1, keepdims=True)
-    expo = jnp.exp(scores - row_peak)
-    denom = jnp.sum(expo, axis=1, keepdims=True)
-    probs = expo / denom
-    vals = dot(probs.astype(bf16), value[...]).astype(bf16)
-    vals_out[...] = vals
-    gated_out[...] = (lane_value(gates[...], s) * vals.astype(f32)).astype(bf16)
+    cos_part, sin_part = cosine[...], sine[...]
+    allowed = allowed_pairs(rows, lens[m])
+    keys = turn(key[...].astype(f32), cos_part, sin_part).astype(bf16)
+    key_out[...] = keys
+    values = value[...]
     lanes = lax.broadcasted_iota(jnp.int32, total_out.shape, 1)
-    total_out[...] = jnp.where(lanes == lane, row_peak + jnp.log(denom), total_out[...])
-    seen = jnp.where(lane_value(hits[...], s) > 0.0, row_peak, very_low)
     peak_lanes = lax.broadcasted_iota(jnp.int32, peak_out.shape, 1)
-    peak_out[...] = jnp.where(
-        peak_lanes == lane, jnp.max(seen, axis=0, keepdims=True), peak_out[...]
-    )
+    totals, peaks = total_out[...], peak_out[...]
+    for s in range(slots):
+        columns = pl.ds(pl.multiple_of((s * heads + h) * HDIM, HDIM), HDIM)
+        turned = turn(query[:, columns], cos_part, sin_part).astype(bf16)
+        query_out[:, columns] = turned
+        scores = jnp.where(allowed, dot_t(turned, keys) * HDIM ** (-0.5), very_low)
+        row_peak = jnp.max(scores, axis=1, keepdims=True)
+        expo = jnp.exp(scores - row_peak)
+        denom = jnp.sum(expo, axis=1, keepdims=True)
+        probs = expo * (1.0 / denom)
+        vals = dot(probs.astype(bf16), values).astype(bf16)
+        vals_out[:, columns] = vals
+        gated_out[:, columns] = (gates[:, s : s + 1] * vals.astype(f32)).astype(bf16)
+        lane = h * slots + s
+        totals = jnp.where(lanes == lane, row_peak + jnp.log(denom), totals)
+        seen = jnp.where(hits[:, s : s + 1] > 0.0, row_peak, very_low)
+        peaks = jnp.where(peak_lanes == lane, jnp.max(seen, axis=0, keepdims=True), peaks)
+    total_out[...] = totals
+    peak_out[...] = peaks
 
 
 def backward_kernel(
     lens, query, key, value, vals, vals_grad, cosine, sine, gates, total,
-    query_grad, key_grad, value_grad, gate_grad, key_sum, value_sum,
+    query_grad, key_grad, value_grad, gate_grad,
 ):
-    m, h, s = pl.program_id(0), pl.program_id(1), pl.program_id(2)
-    slot_count = pl.num_programs(2)
+    m, h = pl.program_id(0), pl.program_id(1)
+    heads = pl.num_programs(1)
     rows = query.shape[0]
-    lane = h * slot_count + s
-
-    @pl.when(lane == 0)
+    slots = query.shape[1] // (heads * HDIM)
+
+    @pl.when(h == 0)
     def _():
         gate_grad[...] = jnp.zeros_like(gate_grad)
 
-    @pl.when(s == 0)
-    def _():
-        key_sum[...] = jnp.zeros_like(key_sum)
-        value_sum[...] = jnp.zeros_like(value_sum)
-
-    full_grad = vals_grad[...]
+    allowed = allowed_pairs(rows, lens[m])
+    cos_part, back_sine = cosine[...], -sine[...]
+    keys, values, totals = key[...], value[...], total[...]
     lanes = lax.broadcasted_iota(jnp.int32, gate_grad.shape, 1)
-    slot_sum = jnp.sum(vals[...].astype(f32) * full_grad, axis=1, keepdims=True)
-    gate_grad[...] += jnp.where(lanes == s, slot_sum, 0.0)
-    gated_grad = (lane_value(gates[...], s) * full_grad).astype(bf16)
-    raw = dot_t(query[...], key[...])
-    scores = jnp.where(allowed_pairs(rows, lens[m]), raw * HDIM ** (-0.5), very_low)
-    probs = jnp.exp(scores - lane_value(total[...], lane))
-    prob_grad = dot_t(gated_grad, value[...])
-    inner = jnp.sum(probs * prob_grad, axis=1, keepdims=True)
-    score_grad = (probs * (prob_grad - inner) * HDIM ** (-0.5)).astype(bf16)
-    back_sine = -sine[...]
-    turned = dot(score_grad, key[...])
-    query_grad[...] = turn(turned, cosine[...], back_sine).astype(bf16)
-    key_sum[...] += t_dot(score_grad, query[...])
-    value_sum[...] += t_dot(probs.astype(bf16), gated_grad)
-
-    @pl.when(s == slot_count - 1)
-    def _():
-        key_grad[...] = turn(key_sum[...], cosine[...], back_sine).astype(bf16)
-        value_grad[...] = value_sum[...].astype(bf16)
-
-
-def attention_specs(own_heads, rows):
-    def block(index):
-        return pl.BlockSpec((rows, HDIM), index)
+    slot_sums = gate_grad[...]
+    key_sum = jnp.zeros(key.shape, f32)
+    value_sum = jnp.zeros(value.shape, f32)
+    for s in range(slots):
+        columns = pl.ds(pl.multiple_of((s * heads + h) * HDIM, HDIM), HDIM)
+        full_grad = vals_grad[:, columns]
+        slot_sum = jnp.sum(vals[:, columns].astype(f32) * full_grad, axis=1, keepdims=True)
+        slot_sums += jnp.where(lanes == s, slot_sum, 0.0)
+        gated_grad = (gates[:, s : s + 1] * full_grad).astype(bf16)
+        queries = query[:, columns]
+        scores = jnp.where(allowed, dot_t(queries, keys) * HDIM ** (-0.5), very_low)
+        probs = jnp.exp(scores - lane_value(totals, h * slots + s))
+        prob_grad = dot_t(gated_grad, values)
+        inner = jnp.sum(probs * prob_grad, axis=1, keepdims=True)
+        score_grad = (probs * (prob_grad - inner) * HDIM ** (-0.5)).astype(bf16)
+        query_grad[:, columns] = turn(dot(score_grad, keys), cos_part, back_sine).astype(bf16)
+        key_sum += t_dot(score_grad, queries)
+        value_sum += t_dot(probs.astype(bf16), gated_grad)
+    gate_grad[...] = slot_sums
+    key_grad[...] = turn(key_sum, cos_part, back_sine).astype(bf16)
+    value_grad[...] = value_sum.astype(bf16)
+
+
+def attention_specs(own_heads, rows, width):
+    def block(columns, index):
+        return pl.BlockSpec((rows, columns), index)
 
     return {
-        "query": block(lambda m, h, s, lens: (m, s * own_heads + h)),
-        "key": block(lambda m, h, s, lens: (m, h)),
-        "value": block(lambda m, h, s, lens: (m, own_heads + h)),
-        "rows": block(lambda m, h, s, lens: (m, 0)),
-        "peak": pl.BlockSpec((8, HDIM), lambda m, h, s, lens: (m, 0)),
+        "query": block(width, lambda m, h, lens: (m, 0)),
+        "key": block(HDIM, lambda m, h, lens: (m, h)),
+        "value": block(HDIM, lambda m, h, lens: (m, own_heads + h)),
+        "rows": block(HDIM, lambda m, h, lens: (m, 0)),
+        "peak": pl.BlockSpec((8, HDIM), lambda m, h, lens: (m, 0)),
     }
 
 
 def attention_forward(lens, query, joint_kv, tables, gates, hits, own_heads, rows):
     micro = lens.shape[0]
-    slots = query.shape[1] // (own_heads * HDIM)
-    at = attention_specs(own_heads, rows)
+    at = attention_specs(own_heads, rows, query.shape[1])
     shape = jax.ShapeDtypeStruct
     total_rows = micro * rows
     return pl.pallas_call(
         forward_kernel,
         grid_spec=pltpu.PrefetchScalarGridSpec(
             num_scalar_prefetch=1,
-            grid=(micro, own_heads, slots),
+            grid=(micro, own_heads),
             in_specs=[at["query"], at["key"], at["value"]] + [at["rows"]] * 4,
             out_specs=[at["query"]] * 3 + [at["key"], at["rows"], at["peak"]],
         ),
@@ -190,6 +192,7 @@
             shape((total_rows, HDIM), f32),
             shape((micro * 8, HDIM), f32),
         ],
+        compiler_params=pltpu.CompilerParams(vmem_limit_bytes=48 * 2**20),
         cost_estimate=pl.CostEstimate(
             flops=4 * rows * rows * HDIM * micro * HEADS,
             bytes_accessed=14 * query.size,
@@ -203,23 +206,22 @@
     lens, query, key, joint_kv, vals, vals_grad, tables, gates, total, own_heads, rows
 ):
     micro = lens.shape[0]
-    slots = query.shape[1] // (own_heads * HDIM)
-    at = attention_specs(own_heads, rows)
+    at = attention_specs(own_heads, rows, query.shape[1])
     shape = jax.ShapeDtypeStruct
     total_rows = micro * rows
     return pl.pallas_call(
         backward_kernel,
         grid_spec=pltpu.PrefetchScalarGridSpec(
             num_scalar_prefetch=1,
-            grid=(micro, own_heads, slots),
+            grid=(micro, own_heads),
             in_specs=[at["query"], at["key"], at["value"], at["query"], at["query"]]
             + [at["rows"]] * 4,
             out_specs=[at["query"], at["key"], at["key"], at["rows"]],
-            scratch_shapes=[pltpu.VMEM((rows, HDIM), f32)] * 2,
         ),
         out_shape=[shape(query.shape, bf16)]
         + [shape((total_rows, own_heads * HDIM), bf16)] * 2
         + [shape((total_rows, HDIM), f32)],
+        compiler_params=pltpu.CompilerParams(vmem_limit_bytes=48 * 2**20),
         cost_estimate=pl.CostEstimate(
             flops=10 * rows * rows * HDIM * micro * HEADS,
             bytes_accessed=14 * query.size,
@@ -529,11 +531,11 @@
         ],
         axis=1,
     )
-    kv_full = lax.all_gather(after(own_kv, work), "dp", axis=0, tiled=True)
     line_steps = [4 * line for line in range(1, lines)]
     side_first = swap(send_pair[0], "dp", 2)
     keep_first = [swap(keep_pair[0], "dp", step) for step in line_steps]
     joint_own = columns_of(query_weight[0], attn_out_weight[0])
+    joint_own = jnp.concatenate([joint_own, own_kv], axis=1)
     joint_full = lax.all_gather(
         after(joint_own, side_first, keep_first), "dp", axis=0, tiled=True
     )
@@ -541,14 +543,16 @@
     keep_second = [swap(late_pair[0], "dp", step) for step in line_steps]
     side_second = swap(late_pair[1], "dp", 2)
     first_lines = [swap(late_pair[2], "dp", step) for step in line_steps]
-    second_lines = [swap(after(side_second, first_lines), "dp", step) for step in line_steps]
+    second_lines = [swap(side_second, "dp", step) for step in line_steps]
     firsts, seconds = [keep_pair[0], side_first], [keep_pair[1], side_second]
     for line in range(lines - 1):
         firsts += [keep_first[line], first_lines[line]]
         seconds += [keep_second[line], second_lines[line]]
     near_pieces = [swap(piece, "dp", 1) for piece in firsts]
     own_pieces = seconds
-    query_full, out_full = joint_full[:, :query_width], joint_full[:, query_width:]
+    query_full = joint_full[:, :query_width]
+    out_full = joint_full[:, query_width : 2 * query_width]
+    kv_full = joint_full[:, 2 * query_width :]
 
     positions = jnp.arange(group_rows, dtype=jnp.int32)
     first_len = lax.dynamic_index_in_dim(seq_lengths[:, :, 0], group, 1, keepdims=True)
@@ -642,7 +646,7 @@
 
     kv_part = dot(hidden_one, kv_full).astype(bf16)
     query_part = dot(hidden_one, query_full)
-    grad_sent = after(grad_sent, kv_part, joint_full)
+    grad_sent = after(grad_sent, kv_part)
     grad_near, grad_far = near_rows(grad_sent), near_rows(swap(grad_sent, "dp", 2))
     lens = first_len[:, 0].astype(jnp.int32)
     gates_wide = wide(gates_one)
@@ -651,7 +655,7 @@
     )
     peaks = jnp.max(peaks, axis=0)[: own_heads * slots]
     gated_vals = after(gated_vals, keep_second, side_second)
-    attn_home = after(scatter_rows(dot_t(gated_vals, out_full)), first_lines, grad_near, grad_far)
+    attn_home = after(scatter_rows(dot_t(gated_vals, out_full)), first_lines, second_lines)
 
     resid = x_home + attn_home
     normed_two, scale_two = normalize(resid)
@@ -667,7 +671,7 @@
         gate_parts.append(jnp.sum(jnp.where(packs[k], gate_col[:, None, :], 0.0), axis=-1))
     hidden_sent = send_packed(hidden_two, jnp.stack(gate_parts))
     hidden_near, hidden_far = near_rows(hidden_sent), swap(hidden_sent, "dp", 2)
-    hidden_near = after(hidden_near, second_lines, near_pieces)
+    hidden_near = after(hidden_near, near_pieces, grad_near, grad_far)
     position = jnp.stack([core, chip]).astype(jnp.int32)
     near_results = expert_rows(
         position, hidden_near, after(grad_near, grad_far), own_pieces, near_pieces
@@ -691,7 +695,9 @@
                 block = after(line_grads[4 * line + 2 * which + part], *last)
                 got[part].append(swap(block, "dp", 4 * line + 4))
             last = got[part][-1:]
-    hidden_got = after(swap(hidden_far_sum, "dp", 2), *line_grads, ffn_far_sum, ffn_sum)
+    hidden_got, ffn_far_sum, ffn_sum = lax.optimization_barrier(
+        (swap(hidden_far_sum, "dp", 2), ffn_far_sum, ffn_sum, line_grads)
+    )[:3]
     hidden_sum = hidden_sum + hidden_got.astype(f32)
     own_grads = block_grads([1, 0], hidden_sum)
     back_packed = return_packed(hidden_sum, *own_grads)
@@ -727,18 +733,20 @@
         own_heads, group_rows,
     )
     query_grad, key_grad, value_grad, slot_part_one = lax.optimization_barrier(
-        (query_grad, key_grad, value_grad, slot_part_one, ffn_packed, keep_got[0])
+        (query_grad, key_grad, value_grad, slot_part_one, ffn_packed)
     )[:4]
     kv_grad = jnp.concatenate([key_grad, value_grad], axis=1)
     hidden_one_part = dot_t(query_grad, query_full) + dot_t(kv_grad, kv_full)
     hidden_one_part = hidden_one_part.astype(bf16)
-    hidden_one_late = after(hidden_one, hidden_one_part)
+    hidden_one_late = after(hidden_one, hidden_one_part, keep_got[0])
     query_part_grad = t_dot(hidden_one_late, query_grad).astype(bf16)
     kv_part_grad = t_dot(hidden_one_late, kv_grad).astype(bf16)
     back_one = scatter_rows(
         jnp.concatenate([hidden_one_part, slot_part_one.astype(bf16)], axis=1)
     )
-    back_one = after(back_one, query_part_grad, kv_part_grad, keep_got[1])
+    back_one, keep_got, other_sums = lax.optimization_barrier(
+        (back_one, keep_got, other_sums, query_part_grad, kv_part_grad)
+    )[:3]
     hidden_one_grad, slot_one_grad = back_one[:, :width], back_one[:, width : width + slots]
 
     def own(value):
@@ -769,13 +777,11 @@
     def reduced(value):
         return lax.psum_scatter(value, "dp", scatter_dimension=0, tiled=True)
 
-    out_grad = slots_of(reduced(out_part))
+    in_low = in_home.astype(bf16)
+    out_grad = slots_of(after(reduced(out_part), in_low))
     joint_own = reduced(jnp.concatenate([query_part_grad, kv_part_grad], axis=1))
 
     query_own, kv_own = joint_own[:, :query_width], joint_own[:, query_width:]
-    in_low, out_grad = lax.optimization_barrier(
-        (in_home.astype(bf16), out_grad, other_sums[0])
-    )[:2]
     results = jnp.stack([out_home, in_low]).reshape(2, micro, tok_rows, width)
     results = jnp.einsum("mtr,bmtd->bmrd", deal, results, preferred_element_type=f32).astype(bf16)
     results = results.reshape(2 * micro, dp_count, piece_rows, width).transpose(1, 0, 2, 3)

time: 1050 us -> 1000 us (0.952)
  Pallas kernels: 193 us -> 169 us
  other arithmetic: 119 us -> 108 us
    ppermute x65, waiting for transfers between devices: 420 us -> 380 us  [swap(): return lax.ppermute(value, axis, [(i, i ^ step) for i in range(count)])]
    all_gather x1, waiting for transfers between devices: 0.01 us -> 27.8 us  [local(): lax.all_gather(after(joint_own, side_first, keep_first), 'dp', axis=0, ti...]
    all_to_all x1, waiting for transfers between devices: 7.09 us -> 27.3 us  [local(): lax.all_to_all(results, 'dp', split_axis=0, concat_axis=0, tiled=True)]
    ppermute x1, waiting for transfers between devices: 19.1 us -> 2.25 us  [local(): lax.ppermute(jnp.where(even_col, key_part, value_part), 'expert', [(b, a)...]
    pallas_call x1, Pallas kernels: 28.8 us -> 14.6 us  [attention_forward(): pl.pallas_call(forward_kernel, grid_spec=pltpu.PrefetchScalarGridSpec(num...]
    unnamed x250 -> x182, local copies, waits for them, and re-layouts: 35.3 us -> 21.6 us
  transfers between devices with their start and end apart: 75 -> 74, of which waited for: 43 -> 39; matrix products, arithmetic and copies ran while one was open for 25% -> 26% of each run, Pallas kernels for 15% -> 17%
where the time goes in v7:
time: 1000 us; the launch traced here: 998 us
  waiting for transfers between devices  452 us (45%)
  Pallas kernels  169 us (17%)
  other arithmetic  108 us (11%)
  local copies, waits for them, and re-layouts  96 us (10%)
  starting transfers between devices  82.1 us (8%)
  matrix products  73.2 us (7%)
  between operations  16.8 us (2%)
    ppermute x65, waiting for transfers between devices, swap(): return lax.ppermute(value, axis, [(i, i ^ step) for i in range(count)])  380 us
    pallas_call x2, Pallas kernels, expert_rows(): pl.pallas_call(expert_kernel, grid_spec=pltpu.PrefetchScalarGridSpec(num_...  81.7 us
    ppermute x65, starting transfers between devices, swap(): return lax.ppermute(value, axis, [(i, i ^ step) for i in range(count)])  64 us
    pallas_call x2, Pallas kernels, expert_grads(): pl.pallas_call(expert_grad_kernel, grid_spec=pltpu.PrefetchScalarGridSpec...  52.7 us
    all_gather x1, waiting for transfers between devices, local(): lax.all_gather(after(joint_own, side_first, keep_first), 'dp', axis=0, ti...  27.8 us
    all_to_all x1, waiting for transfers between devices, local(): lax.all_to_all(results, 'dp', split_axis=0, concat_axis=0, tiled=True)  27.3 us
    dot_general x5, matrix products, dot(): return jnp.dot(left, right, preferred_element_type=f32)  25.8 us
    dot_general x5, matrix products, dot_t(): lax.dot_general(left, right, (((1,), (1,)), ((), ())), preferred_element_...  21.7 us
  transfers between devices with their start and end apart: 74, of which 39 were waited for; matrix products, arithmetic and copies ran while one was open for 26% of the time, Pallas kernels for 17%

profile of v7, /device:TPU:8, one launch (start us, length us, event | category | flops | bytes accessed | tf_op | source)
XLA Modules:
  0.0 997.7 jit_solution(15921404799367342406)
XLA Ops:
  45.9 13.5 %collective-permute-done.4 = bf16[256,1024]{1,0:T(8,128)(2,1)} collective-permute-done((bf16[256,1024]{1,0:T(8,128)(2,1)}, bf16[256,1024]{1,0:T(8,128)(2,1)}, u32[]{:S(2)}, u32[]{:S(2)}) %collective-permute-start.4) | collective-permute-done | bytes 524320 | tf_op jit(solution)/shard_map/ppermute | solution.py:37
  61.4 9.0 collective-permute-done.5
  74.1 12.1 %collective-permute-done.8 = bf16[256,4224]{1,0:T(8,128)(2,1)} collective-permute-done((bf16[256,4224]{1,0:T(8,128)(2,1)}, bf16[256,4224]{1,0:T(8,128)(2,1)}, u32[]{:S(2)}, u32[]{:S(2)}) %collective-permute-start.8) | collective-permute-done | bytes 2162720 | tf_op jit(solution)/shard_map/ppermute | solution.py:37
  100.6 15.5 %all-to-all-done = bf16[8,4,8,2048]{3,2,1,0:T(8,128)(2,1)S(1)} async-done(((bf16[8,4,8,2048]{3,2,1,0:T(8,128)(2,1)}), bf16[8,4,8,2048]{3,2,1,0:T(8,128)(2,1)S(1)}, u32[]{:S(2)}, u32[]{:S(2)}) %all-to-all-start) | async-done | bytes 1048608 | tf_op jit(solution)/shard_map/all_to_all | solution.py:469
  121.9 15.9 %collective-permute-done = bf16[2,64,2048]{2,1,0:T(8,128)(2,1)S(1)} collective-permute-done((bf16[2,64,2048]{2,1,0:T(8,128)(2,1)S(1)}, bf16[2,64,2048]{2,1,0:T(8,128)(2,1)S(1)}, u32[]{:S(2)}, u32[]{:S(2)}) %collective-permute-start) | collective-permute-done | bytes 524320 | tf_op jit(solution)/shard_map/ppermute | solution.py:37
  137.9 20.3 %collective-permute-done.1 = bf16[2,64,2048]{2,1,0:T(8,128)(2,1)S(1)} collective-permute-done((bf16[2,64,2048]{2,1,0:T(8,128)(2,1)S(1)}, bf16[2,64,2048]{2,1,0:T(8,128)(2,1)S(1)}, u32[]{:S(2)}, u32[]{:S(2)}) %collective-permute-start.1) | collective-permute-done | bytes 524320 | tf_op jit(solution)/shard_map/ppermute | solution.py:37
  172.6 27.8 %all-gather.2.cloned.1.call-done = bf16[2048,5120]{1,0:T(8,128)(2,1)} async-done(((bf16[256,5120]{1,0:T(8,128)(2,1)}), bf16[2048,5120]{1,0:T(8,128)(2,1)}) %all-gather.2.cloned.1.call-update) | async-done | bytes 20971536 | tf_op jit(solution)/shard_map/all_gather | solution.py:539
  211.0 9.6 fusion.6.query
  220.6 14.6 %attention_forward.1 = (bf16[512,2048]{1,0:T(8,128)(2,1)S(1)}, bf16[512,2048]{1,0:T(8,128)(2,1)}, bf16[512,2048]{1,0:T(8,128)(2,1)}, bf16[512,512]{1,0:T(8,128)(...) custom-call(s32[2]{0:T(128)S(1)} %fusion.132.lens, f32[512,2048]{1,0:T(8,128)} %fusion.6.query, ...), custom_call_target="tpu_custom_call" | custom-call | flops 1073741824 | bytes 14680064 | tf_op jit(solution)/shard_map/attention_forward/pallas_call | solution.py:181
  235.2 15.4 %collective-permute-done.10.refs_2_ = bf16[256,4224]{1,0:T(8,128)(2,1)} collective-permute-done((bf16[256,4224]{1,0:T(8,128)(2,1)}, bf16[256,4224]{1,0:T(8,128)(2,1)}, u32[]{:S(2)}, u32[]{:S(2)}) %collective-permute-start.10) | collective-permute-done | bytes 2162720 | tf_op jit(solution)/shard_map/ppermute | solution.py:37
  264.5 19.3 %collective-permute-done.30 = bf16[384,2048]{1,0:T(8,128)(2,1)S(1)} collective-permute-done((bf16[384,2048]{1,0:T(8,128)(2,1)S(1)}, bf16[384,2048]{1,0:T(8,128)(2,1)S(1)}, u32[]{:S(2)}, u32[]{:S(2)}) %collective-permute-start.30) | collective-permute-done | bytes 1572896 | tf_op jit(solution)/shard_map/ppermute | solution.py:37
  286.2 10.9 %collective-permute-done.14 = bf16[2,64,2048]{2,1,0:T(8,128)(2,1)} collective-permute-done((bf16[2,64,2048]{2,1,0:T(8,128)(2,1)}, bf16[2,64,2048]{2,1,0:T(8,128)(2,1)}, u32[]{:S(2)}, u32[]{:S(2)}) %collective-permute-start.14) | collective-permute-done | bytes 524320 | tf_op jit(solution)/shard_map/ppermute | solution.py:37
  297.1 9.1 collective-permute-done.13
  309.3 33.3 %collective-permute-done.16.refs_3_ = bf16[256,4224]{1,0:T(8,128)(2,1)} collective-permute-done((bf16[256,4224]{1,0:T(8,128)(2,1)}, bf16[256,4224]{1,0:T(8,128)(2,1)}, u32[]{:S(2)}, u32[]{:S(2)}) %collective-permute-start.16) | collective-permute-done | bytes 2162720 | tf_op jit(solution)/shard_map/ppermute | solution.py:37
  352.2 26.0 %collective-permute-done.19 = bf16[2,48,2176]{2,1,0:T(8,128)(2,1)S(1)} collective-permute-done((bf16[2,48,2176]{2,1,0:T(8,128)(2,1)S(1)}, bf16[2,48,2176]{2,1,0:T(8,128)(2,1)S(1)}, u32[]{:S(2)}, u32[]{:S(2)}) %collective-permute-start.19) | collective-permute-done | bytes 417824 | tf_op jit(solution)/shard_map/ppermute | solution.py:37
  402.4 41.0 %expert_rows.2 = (bf16[768,2048]{1,0:T(8,128)(2,1)}, bf16[768,2176]{1,0:T(8,128)(2,1)}, bf16[768,1408]{1,0:T(8,128)(2,1)}, bf16[768,2816]{1,0:T(8,128)(2,1)}) custom-call(s32[2]{0:T(128)} %pad_add_fusion.1.place_ref, bf16[768,2176]{1,0:T(8,128)(2,1)} %pad_maximum_fusion.3.hidden.refs_0_.refs_4_, bf16[768,2048]{1,0:T(8,128)(2,1)} %copy-done.46, ...), custom_call_target="tpu_custom_call" | custom-call | flops 26575110144 | bytes 36175872 | tf_op jit(solution)/shard_map/expert_rows/pallas_call | solution.py:332
  449.4 40.7 %expert_rows.3 = (bf16[768,2048]{1,0:T(8,128)(2,1)}, bf16[768,2176]{1,0:T(8,128)(2,1)}, bf16[768,1408]{1,0:T(8,128)(2,1)}, bf16[768,2816]{1,0:T(8,128)(2,1)}) custom-call(s32[2]{0:T(128)} %pad_add_fusion.1.place_ref, bf16[768,2176]{1,0:T(8,128)(2,1)} %constant_dynamic-update-slice_fusion.4.hidden.refs_1_.refs_5_, bf16[768,2048]{1,0:T(8,128)(2,1)} %copy-done.45, ...), custom_call_target="tpu_custom_call" | custom-call | flops 26575110144 | bytes 36175872 | tf_op jit(solution)/shard_map/expert_rows/pallas_call | solution.py:332
  509.0 26.6 %expert_grads.2 = (bf16[256,4224]{1,0:T(8,128)(2,1)}, bf16[256,4224]{1,0:T(8,128)(2,1)}, bf16[256,4224]{1,0:T(8,128)(2,1)}, bf16[256,4224]{1,0:T(8,128)(2,1)}) custom-call(s32[4]{0:T(128)} %get-tuple-element.371.order, bf16[768,2176]{1,0:T(8,128)(2,1)} %pad_maximum_fusion.3.hidden.refs_0_.refs_4_, ...), custom_call_target="tpu_custom_call" | custom-call | flops 13287555072 | bytes 27918336 | tf_op jit(solution)/shard_map/expert_grads/pallas_call | solution.py:402
  536.2 9.9 collective-permute-done.34
  553.3 26.1 %expert_grads.3 = (bf16[256,4224]{1,0:T(8,128)(2,1)}, bf16[256,4224]{1,0:T(8,128)(2,1)}, bf16[256,4224]{1,0:T(8,128)(2,1)}, bf16[256,4224]{1,0:T(8,128)(2,1)}) custom-call(s32[4]{0:T(128)} %get-tuple-element.372.order, bf16[768,2176]{1,0:T(8,128)(2,1)} %pad_maximum_fusion.3.hidden.refs_0_.refs_4_, ...), custom_call_target="tpu_custom_call" | custom-call | flops 13287555072 | bytes 27918336 | tf_op jit(solution)/shard_map/expert_grads/pallas_call | solution.py:402
  603.0 15.9 %collective-permute-done.43 = bf16[2,64,2048]{2,1,0:T(8,128)(2,1)S(1)} collective-permute-done((bf16[2,64,2048]{2,1,0:T(8,128)(2,1)S(1)}, bf16[2,64,2048]{2,1,0:T(8,128)(2,1)S(1)}, u32[]{:S(2)}, u32[]{:S(2)}) %collective-permute-start.43) | collective-permute-done | bytes 524320 | tf_op jit(solution)/shard_map/ppermute | solution.py:37
  619.0 17.1 %collective-permute-done.44 = bf16[2,64,2048]{2,1,0:T(8,128)(2,1)S(1)} collective-permute-done((bf16[2,64,2048]{2,1,0:T(8,128)(2,1)S(1)}, bf16[2,64,2048]{2,1,0:T(8,128)(2,1)S(1)}, u32[]{:S(2)}, u32[]{:S(2)}) %collective-permute-start.44) | collective-permute-done | bytes 524320 | tf_op jit(solution)/shard_map/ppermute | solution.py:37
  636.1 10.0 %collective-permute-done.45 = bf16[2,64,2048]{2,1,0:T(8,128)(2,1)S(1)} collective-permute-done((bf16[2,64,2048]{2,1,0:T(8,128)(2,1)S(1)}, bf16[2,64,2048]{2,1,0:T(8,128)(2,1)S(1)}, u32[]{:S(2)}, u32[]{:S(2)}) %collective-permute-start.45) | collective-permute-done | bytes 524320 | tf_op jit(solution)/shard_map/ppermute | solution.py:37
  661.8 10.8 %fusion.vals_grad = f32[512,2048]{1,0:T(8,128)} fusion(bf16[512,2048]{1,0:T(8,128)(2,1)S(1)} %bitcast.435, bf16[2048,5120]{1,0:T(8,128)(2,1)} %all-gather.2.cloned.1.call-done), kind=kOutput, calls=%fused_computation.3 | convolution fusion | flops 4294967296 | bytes 14680064 | tf_op jit(solution)/shard_map/dot_general | solution.py:24
  680.4 20.1 %attention_backward.1 = (bf16[512,2048]{1,0:T(8,128)(2,1)S(1)}, bf16[512,512]{1,0:T(8,128)(2,1)S(1)}, bf16[512,512]{1,0:T(8,128)(2,1)S(1)}, f32[512,128]{1,0:T(8,128)S(1)}) custom-call(s32[2]{0:T(128)S(1)} %fusion.132.lens, bf16[512,2048]{1,0:T(8,128)(2,1)} %get-tuple-element.141.query, bf16[512,512]{1,0:T(8,128)(2,1)S(1)} %get-tuple-element.142.key, ...), custom_call_target="tpu_custom_call" | custom-call | flops 2684354560 | bytes 14680064 | tf_op jit(solution)/shard_map/attention_backward/pallas_call | solution.py:212
  728.0 24.9 %collective-permute-done.52 = bf16[2,64,2176]{2,1,0:T(8,128)(2,1)S(1)} collective-permute-done((bf16[2,64,2176]{2,1,0:T(8,128)(2,1)S(1)}, bf16[2,64,2176]{2,1,0:T(8,128)(2,1)S(1)}, u32[]{:S(2)}, u32[]{:S(2)}) %collective-permute-start.52) | collective-permute-done | bytes 557088 | tf_op jit(solution)/shard_map/ppermute | solution.py:37
  771.1 14.7 %pad_maximum_fusion = bf16[2048,3072]{0,1:T(8,128)(2,1)} fusion(bf16[2048,1024]{0,1:T(8,128)(2,1)S(1)} %convolution_convert_fusion.2, bf16[2048,2048]{0,1:T(8,128)(2,1)S(1)} %convolution_convert_fusion), kind=kLoop, calls=%fused_computation | loop fusion | flops 25165824 | bytes 25165824 | tf_op jit(solution)/shard_map/concatenate | solution.py:782
  785.8 12.5 %collective-permute-done.56 = bf16[256,4224]{1,0:T(8,128)(2,1)} collective-permute-done((bf16[256,4224]{1,0:T(8,128)(2,1)}, bf16[256,4224]{1,0:T(8,128)(2,1)}, u32[]{:S(2)}, u32[]{:S(2)}) %collective-permute-start.56) | collective-permute-done | bytes 2162720 | tf_op jit(solution)/shard_map/ppermute | solution.py:37
  798.3 13.0 %collective-permute-done.54 = bf16[256,4224]{1,0:T(8,128)(2,1)} collective-permute-done((bf16[256,4224]{1,0:T(8,128)(2,1)}, bf16[256,4224]{1,0:T(8,128)(2,1)}, u32[]{:S(2)}, u32[]{:S(2)}) %collective-permute-start.54) | collective-permute-done | bytes 2162720 | tf_op jit(solution)/shard_map/ppermute | solution.py:37
  832.1 27.3 %all-to-all-done.1 = bf16[8,48,2048]{2,1,0:T(8,128)(2,1)} async-done(((bf16[8,48,2048]{2,1,0:T(8,128)(2,1)}), bf16[8,48,2048]{2,1,0:T(8,128)(2,1)}, u32[]{:S(2)}, u32[]{:S(2)}) %all-to-all-start.1) | async-done | bytes 1572896 | tf_op jit(solution)/shard_map/all_to_all | solution.py:804
  928.2 13.2 %collective-permute-done.64 = bf16[256,512]{1,0:T(8,128)(2,1)S(1)} collective-permute-done((bf16[256,512]{1,0:T(8,128)(2,1)S(1)}, bf16[256,512]{1,0:T(8,128)(2,1)S(1)}, u32[]{:S(2)}, u32[]{:S(2)}) %collective-permute-start.64) | collective-permute-done | bytes 262176 | tf_op jit(solution)/shard_map/ppermute | solution.py:37
  963.7 15.3 %collective-permute-done.61 = bf16[256,512]{1,0:T(8,128)(2,1)S(1)} collective-permute-done((bf16[256,512]{1,0:T(8,128)(2,1)S(1)}, bf16[256,512]{1,0:T(8,128)(2,1)S(1)}, u32[]{:S(2)}, u32[]{:S(2)}) %collective-permute-start.61) | collective-permute-done | bytes 262176 | tf_op jit(solution)/shard_map/ppermute | solution.py:37
  (577 shorter events, 389.2 us)
Async XLA Ops:
  7.2 193.2 %all-gather.2.cloned.1.call-start = ((), (), s32[]{:S(2)}) async-start(), calls=%async_computation.4 | async-start | bytes 23592960 | tf_op jit(solution)/shard_map/all_gather | solution.py:539
  24.4 46.0 %collective-permute-start.5 = (bf16[256,1024]{1,0:T(8,128)(2,1)}, bf16[256,1024]{1,0:T(8,128)(2,1)}, u32[]{:S(2)}, u32[]{:S(2)}) collective-permute-start(bf16[256,1024]{1,0:T(8,128)(2,1)} %pad_maximum_fusion.16), channel_id=1, source_target_pairs={{0,3},{1,2},{2,1},{3,0},{4,7},{5,6},{6,5},{7,4},{8,11},{9,10},{10,... | collective-permute-start | bytes 1572872 | tf_op jit(solution)/shard_map/ppermute | solution.py:37
  38.2 48.0 %collective-permute-start.8 = (bf16[256,4224]{1,0:T(8,128)(2,1)}, bf16[256,4224]{1,0:T(8,128)(2,1)}, u32[]{:S(2)}, u32[]{:S(2)}) collective-permute-start(bf16[256,4224]{1,0:T(8,128)(2,1)} %pad_maximum_fusion.6), channel_id=1, source_target_pairs={{0,8},{4,12},{8,0},{12,4},{16,24},{20,28},{24,16},{28,20},{1,9},{5... | collective-permute-start | bytes 6488072 | tf_op jit(solution)/shard_map/ppermute | solution.py:37
  39.8 47.7 %collective-permute-start.9 = (bf16[256,4224]{1,0:T(8,128)(2,1)}, bf16[256,4224]{1,0:T(8,128)(2,1)}, u32[]{:S(2)}, u32[]{:S(2)}) collective-permute-start(bf16[256,4224]{1,0:T(8,128)(2,1)} %pad_maximum_fusion.7), channel_id=1, source_target_pairs={{0,16},{4,20},{8,24},{12,28},{16,0},{20,4},{24,8},{28,12},{1,17},{... | collective-permute-start | bytes 6488072 | tf_op jit(solution)/shard_map/ppermute | solution.py:37
  92.4 817.3 %reduce-scatter.5.cloned.1.call-start = ((), (), s32[]{:S(2)}) async-start(), calls=%async_computation.6 | async-start | bytes 9437184 | tf_op jit(solution)/shard_map/reduce_scatter | solution.py:778
  119.1 39.1 %collective-permute-start.1 = (bf16[2,64,2048]{2,1,0:T(8,128)(2,1)S(1)}, bf16[2,64,2048]{2,1,0:T(8,128)(2,1)S(1)}, u32[]{:S(2)}, u32[]{:S(2)}) collective-permute-start(bf16[2,64,2048]{2,1,0:T(8,128)(2,1)S(1)} %get-tuple-element.275), channel_id=1, source_target_pairs={{0,2},{1,3},{2,0},{3,1},{4,6},{5,7},{6,4},{7,5},{8,10},{9,11},{10,... | collective-permute-start | bytes 1572872 | tf_op jit(solution)/shard_map/ppermute | solution.py:37
  119.1 47.6 %collective-permute-start.2 = (bf16[2,64,2048]{2,1,0:T(8,128)(2,1)S(1)}, bf16[2,64,2048]{2,1,0:T(8,128)(2,1)S(1)}, u32[]{:S(2)}, u32[]{:S(2)}) collective-permute-start(bf16[2,64,2048]{2,1,0:T(8,128)(2,1)S(1)} %get-tuple-element.275), channel_id=1, source_target_pairs={{0,3},{1,2},{2,1},{3,0},{4,7},{5,6},{6,5},{7,4},{8,11},{9,10},{10,... | collective-permute-start | bytes 1572872 | tf_op jit(solution)/shard_map/ppermute | solution.py:37
  200.4 50.2 %collective-permute-start.10 = (bf16[256,4224]{1,0:T(8,128)(2,1)}, bf16[256,4224]{1,0:T(8,128)(2,1)}, u32[]{:S(2)}, u32[]{:S(2)}) collective-permute-start(bf16[256,4224]{1,0:T(8,128)(2,1)} %pad_maximum_fusion.8.refs_0_), channel_id=1, source_target_pairs={{0,16},{4,20},{8,24},{12,28},{16,0},{20,4},{24,8},{28,12},{1,17},{... | collective-permute-start | bytes 6488072 | tf_op jit(solution)/shard_map/ppermute | solution.py:37
  201.0 50.2 %collective-permute-start.11 = (bf16[256,4224]{1,0:T(8,128)(2,1)}, bf16[256,4224]{1,0:T(8,128)(2,1)}, u32[]{:S(2)}, u32[]{:S(2)}) collective-permute-start(bf16[256,4224]{1,0:T(8,128)(2,1)} %pad_maximum_fusion.9), channel_id=1, source_target_pairs={{0,8},{4,12},{8,0},{12,4},{16,24},{20,28},{24,16},{28,20},{1,9},{5... | collective-permute-start | bytes 6488072 | tf_op jit(solution)/shard_map/ppermute | solution.py:37
  204.3 105.0 %collective-permute-start.15 = (bf16[256,4224]{1,0:T(8,128)(2,1)}, bf16[256,4224]{1,0:T(8,128)(2,1)}, u32[]{:S(2)}, u32[]{:S(2)}) collective-permute-start(bf16[256,4224]{1,0:T(8,128)(2,1)} %collective-permute-done.8), channel_id=1, source_target_pairs={{0,16},{4,20},{8,24},{12,28},{16,0},{20,4},{24,8},{28,12},{1,17},{... | collective-permute-start | bytes 6488072 | tf_op jit(solution)/shard_map/ppermute | solution.py:37
  210.4 73.4 %collective-permute-start.30 = (bf16[384,2048]{1,0:T(8,128)(2,1)S(1)}, bf16[384,2048]{1,0:T(8,128)(2,1)S(1)}, u32[]{:S(2)}, u32[]{:S(2)}) collective-permute-start(bf16[384,2048]{1,0:T(8,128)(2,1)S(1)} %bitcast.423), channel_id=1, source_target_pairs={{0,8},{4,12},{8,0},{12,4},{16,24},{20,28},{24,16},{28,20},{1,9},{5... | collective-permute-start | bytes 4718600 | tf_op jit(solution)/shard_map/ppermute | solution.py:37
  251.2 91.4 %collective-permute-start.16 = (bf16[256,4224]{1,0:T(8,128)(2,1)}, bf16[256,4224]{1,0:T(8,128)(2,1)}, u32[]{:S(2)}, u32[]{:S(2)}) collective-permute-start(bf16[256,4224]{1,0:T(8,128)(2,1)} %collective-permute-done.11.refs_1_), channel_id=1, source_target_pairs={{0,16},{4,20},{8,24},{12,28},{16,0},{20,4},{24,8},{28,12},{1,17},{... | collective-permute-start | bytes 6488072 | tf_op jit(solution)/shard_map/ppermute | solution.py:37
  263.1 43.2 %collective-permute-start.13 = (bf16[2,64,2048]{2,1,0:T(8,128)(2,1)S(1)}, bf16[2,64,2048]{2,1,0:T(8,128)(2,1)}, u32[]{:S(2)}, u32[]{:S(2)}) collective-permute-start(bf16[2,64,2048]{2,1,0:T(8,128)(2,1)S(1)} %get-tuple-element.292), channel_id=1, source_target_pairs={{0,2},{1,3},{2,0},{3,1},{4,6},{5,7},{6,4},{7,5},{8,10},{9,11},{10,... | collective-permute-start | bytes 1572872 | tf_op jit(solution)/shard_map/ppermute | solution.py:37
  297.1 55.1 %collective-permute-start.29 = (bf16[384,2048]{1,0:T(8,128)(2,1)}, bf16[384,2048]{1,0:T(8,128)(2,1)}, u32[]{:S(2)}, u32[]{:S(2)}) collective-permute-start(bf16[384,2048]{1,0:T(8,128)(2,1)} %bitcast.424), channel_id=1, source_target_pairs={{0,4},{4,0},{8,12},{12,8},{16,20},{20,16},{24,28},{28,24},{1,5},{5... | collective-permute-start | bytes 4718600 | tf_op jit(solution)/shard_map/ppermute | solution.py:37
  306.2 79.7 %collective-permute-start.31 = (bf16[384,2048]{1,0:T(8,128)(2,1)}, bf16[384,2048]{1,0:T(8,128)(2,1)}, u32[]{:S(2)}, u32[]{:S(2)}) collective-permute-start(bf16[384,2048]{1,0:T(8,128)(2,1)} %copy-done.41), channel_id=1, source_target_pairs={{0,4},{4,0},{8,12},{12,8},{16,20},{20,16},{24,28},{28,24},{1,5},{5... | collective-permute-start | bytes 4718600 | tf_op jit(solution)/shard_map/ppermute | solution.py:37
  352.2 46.1 %collective-permute-start.22 = (bf16[256,4224]{1,0:T(8,128)(2,1)S(1)}, bf16[256,4224]{1,0:T(8,128)(2,1)S(1)}, u32[]{:S(2)}, u32[]{:S(2)}) collective-permute-start(bf16[256,4224]{1,0:T(8,128)(2,1)S(1)} %copy-done.36), channel_id=1, source_target_pairs={{0,4},{4,0},{8,12},{12,8},{16,20},{20,16},{24,28},{28,24},{1,5},{5... | collective-permute-start | bytes 6488072 | tf_op jit(solution)/shard_map/ppermute | solution.py:37
  394.9 48.5 %collective-permute-start.20 = (bf16[384,2176]{1,0:T(8,128)(2,1)S(1)}, bf16[384,2176]{1,0:T(8,128)(2,1)S(1)}, u32[]{:S(2)}, u32[]{:S(2)}) collective-permute-start(bf16[384,2176]{1,0:T(8,128)(2,1)S(1)} %bitcast.421), channel_id=1, source_target_pairs={{0,8},{4,12},{8,0},{12,4},{16,24},{20,28},{24,16},{28,20},{1,9},{5... | collective-permute-start | bytes 5013512 | tf_op jit(solution)/shard_map/ppermute | solution.py:37
  446.3 53.3 %collective-permute-start.36 = (bf16[384,2048]{1,0:T(8,128)(2,1)}, bf16[384,2048]{1,0:T(8,128)(2,1)}, u32[]{:S(2)}, u32[]{:S(2)}) collective-permute-start(bf16[384,2048]{1,0:T(8,128)(2,1)} %split.29), channel_id=1, source_target_pairs={{0,4},{4,0},{8,12},{12,8},{16,20},{20,16},{24,28},{28,24},{1,5},{5... | collective-permute-start | bytes 4718600 | tf_op jit(solution)/shard_map/ppermute | solution.py:37
  499.7 46.4 %collective-permute-start.38 = (bf16[384,2176]{1,0:T(8,128)(2,1)}, bf16[384,2176]{1,0:T(8,128)(2,1)}, u32[]{:S(2)}, u32[]{:S(2)}) collective-permute-start(bf16[384,2176]{1,0:T(8,128)(2,1)} %split.31), channel_id=1, source_target_pairs={{0,4},{4,0},{8,12},{12,8},{16,20},{20,16},{24,28},{28,24},{1,5},{5... | collective-permute-start | bytes 5013512 | tf_op jit(solution)/shard_map/ppermute | solution.py:37
  506.6 39.4 %collective-permute-start.34 = (bf16[384,2176]{1,0:T(8,128)(2,1)}, bf16[384,2176]{1,0:T(8,128)(2,1)}, u32[]{:S(2)}, u32[]{:S(2)}) collective-permute-start(bf16[384,2176]{1,0:T(8,128)(2,1)} %add_convert_fusion.5), channel_id=1, source_target_pairs={{0,8},{4,12},{8,0},{12,4},{16,24},{20,28},{24,16},{28,20},{1,9},{5... | collective-permute-start | bytes 5013512 | tf_op jit(solution)/shard_map/ppermute | solution.py:37
  535.6 62.6 %collective-permute-start.42 = (bf16[256,4224]{1,0:T(8,128)(2,1)}, bf16[256,4224]{1,0:T(8,128)(2,1)}, u32[]{:S(2)}, u32[]{:S(2)}) collective-permute-start(bf16[256,4224]{1,0:T(8,128)(2,1)} %get-tuple-element.112), channel_id=1, source_target_pairs={{0,16},{4,20},{8,24},{12,28},{16,0},{20,4},{24,8},{28,12},{1,17},{... | collective-permute-start | bytes 6488072 | tf_op jit(solution)/shard_map/ppermute | solution.py:37
  552.8 93.4 %collective-permute-start.37 = (bf16[384,2048]{1,0:T(8,128)(2,1)}, bf16[384,2048]{1,0:T(8,128)(2,1)}, u32[]{:S(2)}, u32[]{:S(2)}) collective-permute-start(bf16[384,2048]{1,0:T(8,128)(2,1)} %add_convert_fusion.6), channel_id=1, source_target_pairs={{0,8},{4,12},{8,0},{12,4},{16,24},{20,28},{24,16},{28,20},{1,9},{5... | collective-permute-start | bytes 4718600 | tf_op jit(solution)/shard_map/ppermute | solution.py:37
  601.4 44.7 %collective-permute-start.45 = (bf16[2,64,2048]{2,1,0:T(8,128)(2,1)S(1)}, bf16[2,64,2048]{2,1,0:T(8,128)(2,1)S(1)}, u32[]{:S(2)}, u32[]{:S(2)}) collective-permute-start(bf16[2,64,2048]{2,1,0:T(8,128)(2,1)S(1)} %bitcast.442), channel_id=1, source_target_pairs={{0,3},{1,2},{2,1},{3,0},{4,7},{5,6},{6,5},{7,4},{8,11},{9,10},{10,... | collective-permute-start | bytes 1572872 | tf_op jit(solution)/shard_map/ppermute | solution.py:37
  602.4 70.3 %collective-permute-start.46 = (bf16[256,4224]{1,0:T(8,128)(2,1)}, bf16[256,4224]{1,0:T(8,128)(2,1)}, u32[]{:S(2)}, u32[]{:S(2)}) collective-permute-start(bf16[256,4224]{1,0:T(8,128)(2,1)} %get-tuple-element.134), channel_id=1, source_target_pairs={{0,16},{4,20},{8,24},{12,28},{16,0},{20,4},{24,8},{28,12},{1,17},{... | collective-permute-start | bytes 6488072 | tf_op jit(solution)/shard_map/ppermute | solution.py:37
  657.0 291.3 %reduce-scatter.3.cloned.1.call-start = ((), (), s32[]{:S(2)}) async-start(), calls=%async_computation.5 | async-start | bytes 14155776 | tf_op jit(solution)/shard_map/reduce_scatter | solution.py:778
  661.3 124.5 %collective-permute-start.55 = (bf16[256,4224]{1,0:T(8,128)(2,1)}, bf16[256,4224]{1,0:T(8,128)(2,1)}, u32[]{:S(2)}, u32[]{:S(2)}) collective-permute-start(bf16[256,4224]{1,0:T(8,128)(2,1)} %add_convert_fusion.3), channel_id=1, source_target_pairs={{0,8},{4,12},{8,0},{12,4},{16,24},{20,28},{24,16},{28,20},{1,9},{5... | collective-permute-start | bytes 6488072 | tf_op jit(solution)/shard_map/ppermute | solution.py:37
  676.3 85.9 %collective-permute-start.53 = (bf16[256,4224]{1,0:T(8,128)(2,1)}, bf16[256,4224]{1,0:T(8,128)(2,1)}, u32[]{:S(2)}, u32[]{:S(2)}) collective-permute-start(bf16[256,4224]{1,0:T(8,128)(2,1)} %get-tuple-element.153), channel_id=1, source_target_pairs={{0,16},{4,20},{8,24},{12,28},{16,0},{20,4},{24,8},{28,12},{1,17},{... | collective-permute-start | bytes 6488072 | tf_op jit(solution)/shard_map/ppermute | solution.py:37
  723.5 38.4 %collective-permute-start.51 = (bf16[2,64,2176]{2,1,0:T(8,128)(2,1)S(1)}, bf16[2,64,2176]{2,1,0:T(8,128)(2,1)S(1)}, u32[]{:S(2)}, u32[]{:S(2)}) collective-permute-start(bf16[2,64,2176]{2,1,0:T(8,128)(2,1)S(1)} %get-tuple-element.299), channel_id=1, source_target_pairs={{0,2},{1,3},{2,0},{3,1},{4,6},{5,7},{6,4},{7,5},{8,10},{9,11},{10,... | collective-permute-start | bytes 1671176 | tf_op jit(solution)/shard_map/ppermute | solution.py:37
  753.0 45.3 %collective-permute-start.56 = (bf16[256,4224]{1,0:T(8,128)(2,1)}, bf16[256,4224]{1,0:T(8,128)(2,1)}, u32[]{:S(2)}, u32[]{:S(2)}) collective-permute-start(bf16[256,4224]{1,0:T(8,128)(2,1)} %add_convert_fusion.2), channel_id=1, source_target_pairs={{0,8},{4,12},{8,0},{12,4},{16,24},{20,28},{24,16},{28,20},{1,9},{5... | collective-permute-start | bytes 6488072 | tf_op jit(solution)/shard_map/ppermute | solution.py:37
  762.2 49.1 %collective-permute-start.54 = (bf16[256,4224]{1,0:T(8,128)(2,1)}, bf16[256,4224]{1,0:T(8,128)(2,1)}, u32[]{:S(2)}, u32[]{:S(2)}) collective-permute-start(bf16[256,4224]{1,0:T(8,128)(2,1)} %get-tuple-element.154), channel_id=1, source_target_pairs={{0,16},{4,20},{8,24},{12,28},{16,0},{20,4},{24,8},{28,12},{1,17},{... | collective-permute-start | bytes 6488072 | tf_op jit(solution)/shard_map/ppermute | solution.py:37
  816.7 42.7 %all-to-all-start.1 = ((bf16[8,48,2048]{2,1,0:T(8,128)(2,1)}), bf16[8,48,2048]{2,1,0:T(8,128)(2,1)}, u32[]{:S(2)}, u32[]{:S(2)}) async-start(bf16[8,48,2048]{2,1,0:T(8,128)(2,1)} %pad_maximum_fusion.12), calls=%async_computation.1 | async-start | bytes 3145728 | tf_op jit(solution)/shard_map/all_to_all | solution.py:804
  831.4 63.4 %collective-permute-start.68 = (bf16[2,256,4224]{2,1,0:T(8,128)(2,1)}, bf16[2,256,4224]{2,1,0:T(8,128)(2,1)}, u32[]{:S(2)}, u32[]{:S(2)}) collective-permute-start(bf16[2,256,4224]{2,1,0:T(8,128)(2,1)} %broadcast_select_fusion.2), channel_id=1, source_target_pairs={{0,4},{4,0},{8,12},{12,8},{16,20},{20,16},{24,28},{28,24},{1,5},{5... | collective-permute-start | bytes 12976136 | tf_op jit(solution)/shard_map/ppermute | solution.py:37
  (122 other events, 2348.6 us)
Sparse Core Ops, SparseCore 0:
  87.6 112.7 all-gather.1
  657.1 99.2 reduce-scatter.4
  785.9 110.0 reduce-scatter.2

commit v8 on v7

--- a/solution.py
+++ b/solution.py
@@ -269,9 +269,10 @@
 
 
 def expert_kernel(place_ref, hidden, grad, *refs):
-    piece_count = (len(refs) - 6) // 2
+    piece_count = (len(refs) - 8) // 2
     own_pieces, near_pieces = refs[:piece_count], refs[piece_count : 2 * piece_count]
-    out, hidden_out, act_out, joint_out, weights, sems = refs[2 * piece_count :]
+    out_pair, hidden_pair = refs[2 * piece_count :][:2], refs[2 * piece_count :][2:4]
+    act_out, joint_out, weights, sems = refs[2 * piece_count + 4 :]
     core, chip = place_ref[0], place_ref[1]
     rows, columns = near_pieces[0].shape
     units = columns // 3
@@ -309,25 +310,34 @@
         gate_grad = act_grad * up_pre * sigma * (1.0 + gate_pre * (1.0 - sigma))
         joint_out[:, start : start + size] = gate_grad.astype(bf16)
         joint_out[:, units + start : units + start + size] = (act_grad * silu_vals).astype(bf16)
-    for start in range(0, width, 512):
-        block = weights[start : start + 512, : 2 * units]
-        hidden_out[:, start : start + 512] = dot_t(joint_out[...], block).astype(bf16)
-        block = weights[start : start + 512, 2 * units :]
-        out[:, start : start + 512] = dot_t(act_out[...], block).astype(bf16)
     lanes = lax.broadcasted_iota(jnp.int32, (hidden.shape[0], HDIM), 1)
-    hidden_out[:, width:] = jnp.where(lanes == 0, slot_sum, 0.0).astype(bf16)
+    last = jnp.where(lanes == 0, slot_sum, 0.0).astype(bf16)
+    for number in range(2):
+
+        @pl.when(pl.program_id(0) == number)
+        def _():
+            out, hidden_out = out_pair[number], hidden_pair[number]
+            for start in range(0, width, 512):
+                block = weights[start : start + 512, : 2 * units]
+                hidden_out[:, start : start + 512] = dot_t(joint_out[...], block).astype(bf16)
+                block = weights[start : start + 512, 2 * units :]
+                out[:, start : start + 512] = dot_t(act_out[...], block).astype(bf16)
+            hidden_out[:, width:] = last
 
 
 def expert_rows(position, hidden, grad, own_pieces, near_pieces):
     rows, width = grad.shape
     columns = near_pieces[0].shape[1]
     units = columns // 3
-    tile = 384 if rows % 384 == 0 else 256
+    tile = rows // 2
     shape = jax.ShapeDtypeStruct
     count = len(own_pieces)
 
     def tiled(size):
         return pl.BlockSpec((tile, size), lambda i, at: (i, 0))
+
+    def fixed(size):
+        return pl.BlockSpec((tile, size), lambda i, at: (0, 0))
 
     return pl.pallas_call(
         expert_kernel,
@@ -336,15 +346,19 @@
             grid=(rows // tile,),
             in_specs=[tiled(width + HDIM), tiled(width)]
             + [pl.BlockSpec(memory_space=pl.ANY)] * (2 * count),
-            out_specs=[tiled(width), tiled(width + HDIM), tiled(units), tiled(2 * units)],
+            out_specs=[fixed(width)] * 2
+            + [fixed(width + HDIM)] * 2
+            + [tiled(units), tiled(2 * units)],
             scratch_shapes=[
                 pltpu.VMEM((width, columns), bf16),
                 pltpu.SemaphoreType.DMA((2 * count,)),
             ],
         ),
         out_shape=[
-            shape((rows, width), bf16),
-            shape((rows, width + HDIM), bf16),
+            shape((tile, width), bf16),
+            shape((tile, width), bf16),
+            shape((tile, width + HDIM), bf16),
+            shape((tile, width + HDIM), bf16),
             shape((rows, units), bf16),
             shape((rows, 2 * units), bf16),
         ],
@@ -609,9 +623,7 @@
         return jnp.concatenate([value, swap(value, "dp", 1)], axis=0)
 
     def quad_sums(value):
-        near_half, far_half = value
-        own, near = jnp.split(near_half, 2, axis=0)
-        far, across = jnp.split(far_half, 2, axis=0)
+        (own, near), (far, across) = value
         far_sum = far.astype(f32) + swap(across, "dp", 1).astype(f32)
         return own.astype(f32) + swap(near, "dp", 1).astype(f32), far_sum.astype(bf16)
 
@@ -633,7 +645,7 @@
     normed_one, scale_one = normalize(x_home)
     hidden_one_home = (normed_one * gain_one).astype(bf16)
     hidden_one_raw = gather_rows(hidden_one_home)
-    hidden_one = hidden_one_raw
+    hidden_one = after(hidden_one_raw, near_pieces[:3])
     grad_sent = send_packed(after(dy_home.astype(bf16), hidden_one))
     logits_one = dot(hidden_one, attn_router)
     gates_one, matches_one, chosen_one, gate_vals_one = route_gates(
@@ -646,16 +658,16 @@
 
     kv_part = dot(hidden_one, kv_full).astype(bf16)
     query_part = dot(hidden_one, query_full)
-    grad_sent = after(grad_sent, kv_part)
-    grad_near, grad_far = near_rows(grad_sent), near_rows(swap(grad_sent, "dp", 2))
     lens = first_len[:, 0].astype(jnp.int32)
     gates_wide = wide(gates_one)
     attn_vals, gated_vals, query_rot, key_rot, log_total, peaks = attention_forward(
         lens, query_part, kv_part, tables, gates_wide, wide(hits_one), own_heads, group_rows
     )
     peaks = jnp.max(peaks, axis=0)[: own_heads * slots]
-    gated_vals = after(gated_vals, keep_second, side_second)
-    attn_home = after(scatter_rows(dot_t(gated_vals, out_full)), first_lines, second_lines)
+    attn_part = after(dot_t(gated_vals, out_full), keep_second, side_second)
+    attn_home = after(scatter_rows(attn_part), first_lines)
+    grad_sent = after(grad_sent, attn_home)
+    grad_near, grad_far = near_rows(grad_sent), near_rows(swap(grad_sent, "dp", 2))
 
     resid = x_home + attn_home
     normed_two, scale_two = normalize(resid)
@@ -669,7 +681,9 @@
     for k in range(slots):
         gate_col = lax.dynamic_index_in_dim(gates_by_slot, col ^ k, 2, keepdims=False)
         gate_parts.append(jnp.sum(jnp.where(packs[k], gate_col[:, None, :], 0.0), axis=-1))
-    hidden_sent = send_packed(hidden_two, jnp.stack(gate_parts))
+    hidden_sent = after(
+        send_packed(hidden_two, jnp.stack(gate_parts)), second_lines
+    )
     hidden_near, hidden_far = near_rows(hidden_sent), swap(hidden_sent, "dp", 2)
     hidden_near = after(hidden_near, near_pieces, grad_near, grad_far)
     position = jnp.stack([core, chip]).astype(jnp.int32)
@@ -678,7 +692,9 @@
     )
     hidden_far = near_rows(after(hidden_far, near_results))
     far_results = expert_rows(position, hidden_far, grad_far, own_pieces, near_pieces)
-    ffn_parts, hidden_parts, actives, joint_grads = zip(near_results, far_results)
+    ffn_parts = near_results[:2], far_results[:2]
+    hidden_parts = near_results[2:4], far_results[2:4]
+    actives, joint_grads = zip(near_results[4:], far_results[4:])
 
     def block_grads(steps, *others):
         rows = after((hidden_near, hidden_far, grad_near, grad_far), *others)
@@ -706,7 +722,6 @@
     def total(own, got):
         return functools.reduce(jnp.add, [part.astype(f32) for part in [own] + got]).astype(bf16)
 
-    other_sums = [swap(total(own_grads[part], side_got[part]), "dp", 2) for part in range(2)]
     slot_two_grad = jnp.zeros((slots, home_rows), f32)
     for k in range(slots):
         rows = jnp.sum(
@@ -736,17 +751,17 @@
         (query_grad, key_grad, value_grad, slot_part_one, ffn_packed)
     )[:4]
     kv_grad = jnp.concatenate([key_grad, value_grad], axis=1)
+    side_own = after((own_grads[:2], side_got), query_grad)
+    other_sums = [swap(total(*pair), "dp", 2) for pair in zip(*side_own)]
     hidden_one_part = dot_t(query_grad, query_full) + dot_t(kv_grad, kv_full)
     hidden_one_part = hidden_one_part.astype(bf16)
-    hidden_one_late = after(hidden_one, hidden_one_part, keep_got[0])
-    query_part_grad = t_dot(hidden_one_late, query_grad).astype(bf16)
-    kv_part_grad = t_dot(hidden_one_late, kv_grad).astype(bf16)
+    joint_part_grad = t_dot(
+        after(hidden_one, hidden_one_part), jnp.concatenate([query_grad, kv_grad], axis=1)
+    ).astype(bf16)
     back_one = scatter_rows(
         jnp.concatenate([hidden_one_part, slot_part_one.astype(bf16)], axis=1)
     )
-    back_one, keep_got, other_sums = lax.optimization_barrier(
-        (back_one, keep_got, other_sums, query_part_grad, kv_part_grad)
-    )[:3]
+    back_one, keep_first_got = lax.optimization_barrier((back_one, keep_got[0], joint_part_grad))[:2]
     hidden_one_grad, slot_one_grad = back_one[:, :width], back_one[:, width : width + slots]
 
     def own(value):
@@ -762,24 +777,12 @@
     gain_one_grad = jnp.sum(hidden_one_grad * normed_one, axis=0)
     in_home = resid_grad + norm_back(hidden_one_grad * gain_one, normed_one, scale_one)
 
-    keep_sums = [total(own_grads[2 + part], keep_got[part]) for part in range(2)]
-    by_rows = [jnp.stack([keep_sums[part], other_sums[part]]) for part in range(2)]
-    own_pair = jnp.where(core == 0, by_rows[0], by_rows[1])
-    near_pair = swap(jnp.where(core == 0, by_rows[1], by_rows[0]), "dp", 1)
-    by_core = [jnp.where(core == 0, own_pair, near_pair), jnp.where(core == 0, near_pair, own_pair)]
-    by_side = [[jnp.where(side == s, part[0], part[1]) for part in by_core] for s in range(2)]
-    blocks = [part for row in by_side for part in row]
-    gate_up_grad = jnp.concatenate(
-        [b[:, :quarter] for b in blocks] + [b[:, quarter : 2 * quarter] for b in blocks], axis=1
-    ).astype(f32)
-    down_grad = jnp.concatenate([b[:, 2 * quarter :] for b in blocks], axis=1).astype(f32)
-
     def reduced(value):
         return lax.psum_scatter(value, "dp", scatter_dimension=0, tiled=True)
 
     in_low = in_home.astype(bf16)
     out_grad = slots_of(after(reduced(out_part), in_low))
-    joint_own = reduced(jnp.concatenate([query_part_grad, kv_part_grad], axis=1))
+    joint_own = reduced(joint_part_grad)
 
     query_own, kv_own = joint_own[:, :query_width], joint_own[:, query_width:]
     results = jnp.stack([out_home, in_low]).reshape(2, micro, tok_rows, width)
@@ -802,6 +805,9 @@
     small = jnp.broadcast_to(small[None], (dp_count,) + small.shape)
     results = jnp.concatenate([results, small], axis=1)
     results = lax.all_to_all(results, "dp", split_axis=0, concat_axis=0, tiled=True)
+    results, keep_last_got, other_sums, out_grad = lax.optimization_barrier(
+        (results, keep_got[1], other_sums, out_grad)
+    )
     small = results[:, sent_back:].astype(f32)
     results = results[:, :sent_back].reshape(dp_count, 2 * micro, piece_rows, width)
     results = results.transpose(1, 0, 2, 3).reshape(2, micro, tok_rows, width)
@@ -816,6 +822,19 @@
     sums = jnp.sum(small[:, :sum_rows], axis=0)
     peaks_all = small[:, sum_rows, :peak_count].reshape(slots, own_heads, slots)
     peaks_all = peaks_all.transpose(2, 0, 1).reshape(slots, HEADS)
+
+    keep_parts = keep_first_got, keep_last_got
+    keep_sums = [total(own_grads[2 + part], keep_parts[part]) for part in range(2)]
+    by_rows = [jnp.stack([keep_sums[part], other_sums[part]]) for part in range(2)]
+    own_pair = jnp.where(core == 0, by_rows[0], by_rows[1])
+    near_pair = swap(jnp.where(core == 0, by_rows[1], by_rows[0]), "dp", 1)
+    by_core = [jnp.where(core == 0, own_pair, near_pair), jnp.where(core == 0, near_pair, own_pair)]
+    by_side = [[jnp.where(side == s, part[0], part[1]) for part in by_core] for s in range(2)]
+    blocks = [part for row in by_side for part in row]
+    gate_up_grad = jnp.concatenate(
+        [b[:, :quarter] for b in blocks] + [b[:, quarter : 2 * quarter] for b in blocks], axis=1
+    ).astype(f32)
+    down_grad = jnp.concatenate([b[:, 2 * quarter :] for b in blocks], axis=1).astype(f32)
 
     out_grad = out_grad.astype(f32)
     query_out = slots_of(query_own).astype(f32)

time: 1000 us -> 1030 us (1.030)
  waiting for transfers between devices: 452 us -> 501 us
  local copies, waits for them, and re-layouts: 96 us -> 71.6 us
  other arithmetic: 108 us -> 92.8 us
  Pallas kernels: 169 us -> 183 us
    ppermute x65, waiting for transfers between devices: 380 us -> 416 us  [swap(): return lax.ppermute(value, axis, [(i, i ^ step) for i in range(count)])]
    ppermute x1, waiting for transfers between devices: 0.01 us -> 21.9 us  [local(): lax.ppermute(jnp.where(holds_keys, high_kv, low_kv), 'expert', second_pairs)]
    pallas_call x2, Pallas kernels: 81.7 us -> 96.5 us  [expert_rows(): pl.pallas_call(expert_kernel, grid_spec=pltpu.PrefetchScalarGridSpec(num_...]
    concatenate x1 -> x0, other arithmetic: 14.7 us -> none  [local(): jnp.concatenate([query_part_grad, kv_part_grad], axis=1)]
    unnamed x182 -> x169, local copies, waits for them, and re-layouts: 21.6 us -> 19.3 us
  transfers between devices with their start and end apart: 74 -> 74, of which waited for: 39 -> 34; matrix products, arithmetic and copies ran while one was open for 26% -> 20% of each run, Pallas kernels for 17% -> 18%
where the time goes in v8:
time: 1030 us; the launch traced here: 1020 us
  waiting for transfers between devices  501 us (49%)
  Pallas kernels  183 us (18%)
  other arithmetic  92.8 us (9%)
  matrix products  78.9 us (8%)
  starting transfers between devices  77.6 us (8%)
  local copies, waits for them, and re-layouts  71.6 us (7%)
  between operations  17 us (2%)
    ppermute x65, waiting for transfers between devices, swap(): return lax.ppermute(value, axis, [(i, i ^ step) for i in range(count)])  416 us
    pallas_call x2, Pallas kernels, expert_rows(): pl.pallas_call(expert_kernel, grid_spec=pltpu.PrefetchScalarGridSpec(num_...  96.5 us
    ppermute x65, starting transfers between devices, swap(): return lax.ppermute(value, axis, [(i, i ^ step) for i in range(count)])  60.8 us
    pallas_call x2, Pallas kernels, expert_grads(): pl.pallas_call(expert_grad_kernel, grid_spec=pltpu.PrefetchScalarGridSpec...  52 us
    dot_general x5, matrix products, dot(): return jnp.dot(left, right, preferred_element_type=f32)  27.2 us
    all_gather x1, waiting for transfers between devices, local(): lax.all_gather(after(joint_own, side_first, keep_first), 'dp', axis=0, ti...  25.3 us
    dot_general x5, matrix products, dot_t(): lax.dot_general(left, right, (((1,), (1,)), ((), ())), preferred_element_...  22.2 us
    ppermute x1, waiting for transfers between devices, local(): lax.ppermute(jnp.where(holds_keys, high_kv, low_kv), 'expert', second_pairs)  21.9 us
  transfers between devices with their start and end apart: 74, of which 34 were waited for; matrix products, arithmetic and copies ran while one was open for 20% of the time, Pallas kernels for 18%

profile of v8, /device:TPU:8, one launch (start us, length us, event | category | flops | bytes accessed | tf_op | source)
XLA Modules:
  0.0 1022.4 jit_solution(12066078363624255621)
XLA Ops:
  38.1 21.9 %collective-permute-done.12 = bf16[256,512]{1,0:T(8,128)(2,1)} collective-permute-done((bf16[256,512]{1,0:T(8,128)(2,1)}, bf16[256,512]{1,0:T(8,128)(2,1)}, u32[]{:S(2)}, u32[]{:S(2)}) %collective-permute-start.12) | collective-permute-done | bytes 262176 | tf_op jit(solution)/shard_map/ppermute | solution.py:540
  63.0 13.9 %collective-permute-done.9 = bf16[256,1024]{1,0:T(8,128)(2,1)S(1)} collective-permute-done((bf16[256,1024]{1,0:T(8,128)(2,1)}, bf16[256,1024]{1,0:T(8,128)(2,1)S(1)}, u32[]{:S(2)}, u32[]{:S(2)}) %collective-permute-start.9) | collective-permute-done | bytes 524320 | tf_op jit(solution)/shard_map/ppermute | solution.py:37
  77.0 9.8 collective-permute-done.10
  102.4 17.6 %all-to-all-done = bf16[8,4,8,2048]{3,2,1,0:T(8,128)(2,1)S(1)} async-done(((bf16[8,4,8,2048]{3,2,1,0:T(8,128)(2,1)}), bf16[8,4,8,2048]{3,2,1,0:T(8,128)(2,1)S(1)}, u32[]{:S(2)}, u32[]{:S(2)}) %all-to-all-start) | async-done | bytes 1048608 | tf_op jit(solution)/shard_map/all_to_all | solution.py:483
  126.8 18.0 %collective-permute-done = bf16[2,64,2048]{2,1,0:T(8,128)(2,1)S(1)} collective-permute-done((bf16[2,64,2048]{2,1,0:T(8,128)(2,1)S(1)}, bf16[2,64,2048]{2,1,0:T(8,128)(2,1)S(1)}, u32[]{:S(2)}, u32[]{:S(2)}) %collective-permute-start) | collective-permute-done | bytes 524320 | tf_op jit(solution)/shard_map/ppermute | solution.py:37
  145.3 14.9 %collective-permute-done.1 = bf16[2,64,2048]{2,1,0:T(8,128)(2,1)S(1)} collective-permute-done((bf16[2,64,2048]{2,1,0:T(8,128)(2,1)S(1)}, bf16[2,64,2048]{2,1,0:T(8,128)(2,1)S(1)}, u32[]{:S(2)}, u32[]{:S(2)}) %collective-permute-start.1) | collective-permute-done | bytes 524320 | tf_op jit(solution)/shard_map/ppermute | solution.py:37
  160.2 10.7 %collective-permute-done.2 = bf16[2,64,2048]{2,1,0:T(8,128)(2,1)S(1)} collective-permute-done((bf16[2,64,2048]{2,1,0:T(8,128)(2,1)S(1)}, bf16[2,64,2048]{2,1,0:T(8,128)(2,1)S(1)}, u32[]{:S(2)}, u32[]{:S(2)}) %collective-permute-start.2) | collective-permute-done | bytes 524320 | tf_op jit(solution)/shard_map/ppermute | solution.py:37
  178.0 25.3 %all-gather.2.cloned.1.call-done = bf16[2048,5120]{1,0:T(8,128)(2,1)} async-done(((bf16[256,5120]{1,0:T(8,128)(2,1)}), bf16[2048,5120]{1,0:T(8,128)(2,1)}) %all-gather.2.cloned.1.call-update) | async-done | bytes 20971536 | tf_op jit(solution)/shard_map/all_gather | solution.py:553
  211.9 9.4 fusion.6.query
  221.4 14.6 %attention_forward.1 = (bf16[512,2048]{1,0:T(8,128)(2,1)S(1)}, bf16[512,2048]{1,0:T(8,128)(2,1)}, bf16[512,2048]{1,0:T(8,128)(2,1)}, bf16[512,512]{1,0:T(8,128)(...) custom-call(s32[2]{0:T(128)S(1)} %fusion.141.lens, f32[512,2048]{1,0:T(8,128)} %fusion.6.query, ...), custom_call_target="tpu_custom_call" | custom-call | flops 1073741824 | bytes 14680064 | tf_op jit(solution)/shard_map/attention_forward/pallas_call | solution.py:181
  260.1 12.9 %collective-permute-done.28 = bf16[2,48,2048]{2,1,0:T(8,128)(2,1)} collective-permute-done((bf16[2,48,2048]{2,1,0:T(8,128)(2,1)}, bf16[2,48,2048]{2,1,0:T(8,128)(2,1)}, u32[]{:S(2)}, u32[]{:S(2)}) %collective-permute-start.28) | collective-permute-done | bytes 393248 | tf_op jit(solution)/shard_map/ppermute | solution.py:37
  278.8 27.9 %collective-permute-done.16 = bf16[2,64,2048]{2,1,0:T(8,128)(2,1)} collective-permute-done((bf16[2,64,2048]{2,1,0:T(8,128)(2,1)}, bf16[2,64,2048]{2,1,0:T(8,128)(2,1)}, u32[]{:S(2)}, u32[]{:S(2)}) %collective-permute-start.16) | collective-permute-done | bytes 524320 | tf_op jit(solution)/shard_map/ppermute | solution.py:37
  306.7 10.2 %collective-permute-done.17 = bf16[2,64,2048]{2,1,0:T(8,128)(2,1)} collective-permute-done((bf16[2,64,2048]{2,1,0:T(8,128)(2,1)}, bf16[2,64,2048]{2,1,0:T(8,128)(2,1)}, u32[]{:S(2)}, u32[]{:S(2)}) %collective-permute-start.17) | collective-permute-done | bytes 524320 | tf_op jit(solution)/shard_map/ppermute | solution.py:37
  329.6 11.9 %collective-permute-done.19 = bf16[2,48,2176]{2,1,0:T(8,128)(2,1)S(1)} collective-permute-done((bf16[2,48,2176]{2,1,0:T(8,128)(2,1)S(1)}, bf16[2,48,2176]{2,1,0:T(8,128)(2,1)S(1)}, u32[]{:S(2)}, u32[]{:S(2)}) %collective-permute-start.19) | collective-permute-done | bytes 417824 | tf_op jit(solution)/shard_map/ppermute | solution.py:37
  341.5 15.6 %collective-permute-done.20 = bf16[2,48,2176]{2,1,0:T(8,128)(2,1)S(1)} collective-permute-done((bf16[2,48,2176]{2,1,0:T(8,128)(2,1)S(1)}, bf16[2,48,2176]{2,1,0:T(8,128)(2,1)S(1)}, u32[]{:S(2)}, u32[]{:S(2)}) %collective-permute-start.20) | collective-permute-done | bytes 417824 | tf_op jit(solution)/shard_map/ppermute | solution.py:37
  373.9 53.2 %expert_rows.2 = (bf16[384,2048]{1,0:T(8,128)(2,1)}, bf16[384,2048]{1,0:T(8,128)(2,1)}, bf16[384,2176]{1,0:T(8,128)(2,1)}, bf16[384,2176]{1,0:T(8,128)(2,1)}, bf...) custom-call(s32[2]{0:T(128)} %pad_add_fusion.1.place_ref, bf16[768,2176]{1,0:T(8,128)(2,1)} %pad_maximum_fusion.2.hidden.refs_0_.refs_4_, ...), custom_call_target="tpu_custom_call" | custom-call | flops 26575110144 | bytes 36175872 | tf_op jit(solution)/shard_map/expert_rows/pallas_call | solution.py:342
  434.6 43.2 %expert_rows.3 = (bf16[384,2048]{1,0:T(8,128)(2,1)}, bf16[384,2048]{1,0:T(8,128)(2,1)}, bf16[384,2176]{1,0:T(8,128)(2,1)}, bf16[384,2176]{1,0:T(8,128)(2,1)}, bf...) custom-call(s32[2]{0:T(128)} %pad_add_fusion.1.place_ref, bf16[768,2176]{1,0:T(8,128)(2,1)} %copy-done.41, ...), custom_call_target="tpu_custom_call" | custom-call | flops 26575110144 | bytes 36175872 | tf_op jit(solution)/shard_map/expert_rows/pallas_call | solution.py:342
  489.1 26.0 %expert_grads.2 = (bf16[256,4224]{1,0:T(8,128)(2,1)}, bf16[256,4224]{1,0:T(8,128)(2,1)}, bf16[256,4224]{1,0:T(8,128)(2,1)}, bf16[256,4224]{1,0:T(8,128)(2,1)}) custom-call(s32[4]{0:T(128)} %get-tuple-element.302.order, bf16[768,2176]{1,0:T(8,128)(2,1)} %pad_maximum_fusion.2.hidden.refs_0_.refs_4_, bf16[768,2176]{1,0:T(8,128)(2,1)} %copy-done.41, ...), custom_call_target="tpu_custom_call" | custom-call | flops 13287555072 | bytes 27918336 | tf_op jit(solution)/shard_map/expert_grads/pallas_call | solution.py:416
  515.6 10.2 collective-permute-done.34
  532.0 26.0 %expert_grads.3 = (bf16[256,4224]{1,0:T(8,128)(2,1)}, bf16[256,4224]{1,0:T(8,128)(2,1)}, bf16[256,4224]{1,0:T(8,128)(2,1)}, bf16[256,4224]{1,0:T(8,128)(2,1)}) custom-call(s32[4]{0:T(128)} %get-tuple-element.303.order, bf16[768,2176]{1,0:T(8,128)(2,1)} %pad_maximum_fusion.2.hidden.refs_0_.refs_4_, bf16[768,2176]{1,0:T(8,128)(2,1)} %copy-done.41, ...), custom_call_target="tpu_custom_call" | custom-call | flops 13287555072 | bytes 27918336 | tf_op jit(solution)/shard_map/expert_grads/pallas_call | solution.py:416
  582.0 14.7 %collective-permute-done.43 = bf16[2,64,2048]{2,1,0:T(8,128)(2,1)S(1)} collective-permute-done((bf16[2,64,2048]{2,1,0:T(8,128)(2,1)S(1)}, bf16[2,64,2048]{2,1,0:T(8,128)(2,1)S(1)}, u32[]{:S(2)}, u32[]{:S(2)}) %collective-permute-start.43) | collective-permute-done | bytes 524320 | tf_op jit(solution)/shard_map/ppermute | solution.py:37
  596.9 18.2 %collective-permute-done.44 = bf16[2,64,2048]{2,1,0:T(8,128)(2,1)S(1)} collective-permute-done((bf16[2,64,2048]{2,1,0:T(8,128)(2,1)S(1)}, bf16[2,64,2048]{2,1,0:T(8,128)(2,1)S(1)}, u32[]{:S(2)}, u32[]{:S(2)}) %collective-permute-start.44) | collective-permute-done | bytes 524320 | tf_op jit(solution)/shard_map/ppermute | solution.py:37
  615.1 9.8 collective-permute-done.45
  637.6 11.7 %fusion.vals_grad = f32[512,2048]{1,0:T(8,128)} fusion(bf16[512,2048]{1,0:T(8,128)(2,1)} %bitcast.430, bf16[2048,5120]{1,0:T(8,128)(2,1)} %all-gather.2.cloned.1.call-done), kind=kOutput, calls=%fused_computation.2 | convolution fusion | flops 4294967296 | bytes 14680064 | tf_op jit(solution)/shard_map/dot_general | solution.py:24
  649.3 57.4 %collective-permute-done.46 = bf16[256,4224]{1,0:T(8,128)(2,1)} collective-permute-done((bf16[256,4224]{1,0:T(8,128)(2,1)}, bf16[256,4224]{1,0:T(8,128)(2,1)}, u32[]{:S(2)}, u32[]{:S(2)}) %collective-permute-start.46) | collective-permute-done | bytes 2162720 | tf_op jit(solution)/shard_map/ppermute | solution.py:37
  711.1 20.3 %attention_backward.1 = (bf16[512,2048]{1,0:T(8,128)(2,1)S(1)}, bf16[512,512]{1,0:T(8,128)(2,1)S(1)}, bf16[512,512]{1,0:T(8,128)(2,1)S(1)}, f32[512,128]{1,0:T(8,128)S(1)}) custom-call(s32[2]{0:T(128)S(1)} %fusion.141.lens, bf16[512,2048]{1,0:T(8,128)(2,1)} %get-tuple-element.159.query, bf16[512,512]{1,0:T(8,128)(2,1)S(1)} %get-tuple-element.160.key, ...), custom_call_target="tpu_custom_call" | custom-call | flops 2684354560 | bytes 14680064 | tf_op jit(solution)/shard_map/attention_backward/pallas_call | solution.py:212
  757.2 10.1 convolution_convert_fusion
  773.0 10.3 %collective-permute-done.51 = bf16[2,64,2176]{2,1,0:T(8,128)(2,1)} collective-permute-done((bf16[2,64,2176]{2,1,0:T(8,128)(2,1)}, bf16[2,64,2176]{2,1,0:T(8,128)(2,1)}, u32[]{:S(2)}, u32[]{:S(2)}) %collective-permute-start.51) | collective-permute-done | bytes 557088 | tf_op jit(solution)/shard_map/ppermute | solution.py:37
  819.0 11.2 %collective-permute-done.58 = bf16[256,512]{1,0:T(8,128)(2,1)S(1)} collective-permute-done((bf16[256,512]{1,0:T(8,128)(2,1)S(1)}, bf16[256,512]{1,0:T(8,128)(2,1)S(1)}, u32[]{:S(2)}, u32[]{:S(2)}) %collective-permute-start.58) | collective-permute-done | bytes 262176 | tf_op jit(solution)/shard_map/ppermute | solution.py:37
  837.6 54.8 %collective-permute-done.55 = bf16[256,4224]{1,0:T(8,128)(2,1)} collective-permute-done((bf16[256,4224]{1,0:T(8,128)(2,1)}, bf16[256,4224]{1,0:T(8,128)(2,1)}, u32[]{:S(2)}, u32[]{:S(2)}) %collective-permute-start.55) | collective-permute-done | bytes 2162720 | tf_op jit(solution)/shard_map/ppermute | solution.py:37
  892.4 17.4 %all-to-all-done.1 = bf16[8,48,2048]{2,1,0:T(8,128)(2,1)} async-done(((bf16[8,48,2048]{2,1,0:T(8,128)(2,1)}), bf16[8,48,2048]{2,1,0:T(8,128)(2,1)}, u32[]{:S(2)}, u32[]{:S(2)}) %all-to-all-start.1) | async-done | bytes 1572896 | tf_op jit(solution)/shard_map/all_to_all | solution.py:807
  982.5 24.3 %collective-permute-done.64 = bf16[256,512]{1,0:T(8,128)(2,1)S(1)} collective-permute-done((bf16[256,512]{1,0:T(8,128)(2,1)S(1)}, bf16[256,512]{1,0:T(8,128)(2,1)S(1)}, u32[]{:S(2)}, u32[]{:S(2)}) %collective-permute-start.64) | collective-permute-done | bytes 262176 | tf_op jit(solution)/shard_map/ppermute | solution.py:37
  (551 shorter events, 351.7 us)
Async XLA Ops:
  7.2 196.1 %all-gather.2.cloned.1.call-start = ((), (), s32[]{:S(2)}) async-start(), calls=%async_computation.4 | async-start | bytes 23592960 | tf_op jit(solution)/shard_map/all_gather | solution.py:553
  14.8 73.8 %collective-permute-start.4 = (bf16[256,4224]{1,0:T(8,128)(2,1)}, bf16[256,4224]{1,0:T(8,128)(2,1)}, u32[]{:S(2)}, u32[]{:S(2)}) collective-permute-start(bf16[256,4224]{1,0:T(8,128)(2,1)} %pad_maximum_fusion.6), channel_id=1, source_target_pairs={{0,8},{4,12},{8,0},{12,4},{16,24},{20,28},{24,16},{28,20},{1,9},{5... | collective-permute-start | bytes 6488072 | tf_op jit(solution)/shard_map/ppermute | solution.py:37
  17.8 70.8 %collective-permute-start.6 = (bf16[256,4224]{1,0:T(8,128)(2,1)}, bf16[256,4224]{1,0:T(8,128)(2,1)}, u32[]{:S(2)}, u32[]{:S(2)}) collective-permute-start(bf16[256,4224]{1,0:T(8,128)(2,1)} %pad_maximum_fusion.5), channel_id=1, source_target_pairs={{0,16},{4,20},{8,24},{12,28},{16,0},{20,4},{24,8},{28,12},{1,17},{... | collective-permute-start | bytes 6488072 | tf_op jit(solution)/shard_map/ppermute | solution.py:37
  38.1 38.9 %collective-permute-start.9 = (bf16[256,1024]{1,0:T(8,128)(2,1)}, bf16[256,1024]{1,0:T(8,128)(2,1)S(1)}, u32[]{:S(2)}, u32[]{:S(2)}) collective-permute-start(bf16[256,1024]{1,0:T(8,128)(2,1)} %pad_maximum_fusion.14), channel_id=1, source_target_pairs={{0,2},{1,3},{2,0},{3,1},{4,6},{5,7},{6,4},{7,5},{8,10},{9,11},{10,... | collective-permute-start | bytes 1572872 | tf_op jit(solution)/shard_map/ppermute | solution.py:37
  88.6 82.4 %collective-permute-start.3 = (bf16[256,4224]{1,0:T(8,128)(2,1)}, bf16[256,4224]{1,0:T(8,128)(2,1)}, u32[]{:S(2)}, u32[]{:S(2)}) collective-permute-start(bf16[256,4224]{1,0:T(8,128)(2,1)} %pad_maximum_fusion.5), channel_id=1, source_target_pairs={{0,4},{4,0},{8,12},{12,8},{16,20},{20,16},{24,28},{28,24},{1,5},{5... | collective-permute-start | bytes 6488072 | tf_op jit(solution)/shard_map/ppermute | solution.py:37
  94.7 709.9 %reduce-scatter.3.cloned.1.call-start = ((), (), s32[]{:S(2)}) async-start(), calls=%async_computation.5 | async-start | bytes 9437184 | tf_op jit(solution)/shard_map/reduce_scatter | solution.py:781
  120.8 50.3 %collective-permute-start.5 = (bf16[256,4224]{1,0:T(8,128)(2,1)}, bf16[256,4224]{1,0:T(8,128)(2,1)S(1)}, u32[]{:S(2)}, u32[]{:S(2)}) collective-permute-start(bf16[256,4224]{1,0:T(8,128)(2,1)} %collective-permute-done.4), channel_id=1, source_target_pairs={{0,4},{4,0},{8,12},{12,8},{16,20},{20,16},{24,28},{28,24},{1,5},{5... | collective-permute-start | bytes 6488072 | tf_op jit(solution)/shard_map/ppermute | solution.py:37
  120.9 50.2 %collective-permute-start.7 = (bf16[256,4224]{1,0:T(8,128)(2,1)}, bf16[256,4224]{1,0:T(8,128)(2,1)S(1)}, u32[]{:S(2)}, u32[]{:S(2)}) collective-permute-start(bf16[256,4224]{1,0:T(8,128)(2,1)} %collective-permute-done.6), channel_id=1, source_target_pairs={{0,4},{4,0},{8,12},{12,8},{16,20},{20,16},{24,28},{28,24},{1,5},{5... | collective-permute-start | bytes 6488072 | tf_op jit(solution)/shard_map/ppermute | solution.py:37
  173.2 85.2 %collective-permute-start.26 = (bf16[2,48,2048]{2,1,0:T(8,128)(2,1)}, bf16[2,48,2048]{2,1,0:T(8,128)(2,1)}, u32[]{:S(2)}, u32[]{:S(2)}) collective-permute-start(bf16[2,48,2048]{2,1,0:T(8,128)(2,1)} %get-tuple-element.251), channel_id=1, source_target_pairs={{0,1},{1,0},{2,3},{3,2},{4,5},{5,4},{6,7},{7,6},{8,9},{9,8},{10,11... | collective-permute-start | bytes 1179656 | tf_op jit(solution)/shard_map/ppermute | solution.py:37
  173.2 85.2 %collective-permute-start.27 = (bf16[2,48,2048]{2,1,0:T(8,128)(2,1)}, bf16[2,48,2048]{2,1,0:T(8,128)(2,1)}, u32[]{:S(2)}, u32[]{:S(2)}) collective-permute-start(bf16[2,48,2048]{2,1,0:T(8,128)(2,1)} %get-tuple-element.253), channel_id=1, source_target_pairs={{0,2},{1,3},{2,0},{3,1},{4,6},{5,7},{6,4},{7,5},{8,10},{9,11},{10,... | collective-permute-start | bytes 1179656 | tf_op jit(solution)/shard_map/ppermute | solution.py:37
  203.3 50.1 %collective-permute-start.13 = (bf16[256,4224]{1,0:T(8,128)(2,1)}, bf16[256,4224]{1,0:T(8,128)(2,1)S(1)}, u32[]{:S(2)}, u32[]{:S(2)}) collective-permute-start(bf16[256,4224]{1,0:T(8,128)(2,1)} %get-tuple-element.103.refs_0_), channel_id=1, source_target_pairs={{0,16},{4,20},{8,24},{12,28},{16,0},{20,4},{24,8},{28,12},{1,17},{... | collective-permute-start | bytes 6488072 | tf_op jit(solution)/shard_map/ppermute | solution.py:37
  203.8 51.0 %collective-permute-start.14 = (bf16[256,4224]{1,0:T(8,128)(2,1)}, bf16[256,4224]{1,0:T(8,128)(2,1)}, u32[]{:S(2)}, u32[]{:S(2)}) collective-permute-start(bf16[256,4224]{1,0:T(8,128)(2,1)} %get-tuple-element.104), channel_id=1, source_target_pairs={{0,8},{4,12},{8,0},{12,4},{16,24},{20,28},{24,16},{28,20},{1,9},{5... | collective-permute-start | bytes 6488072 | tf_op jit(solution)/shard_map/ppermute | solution.py:37
  205.3 113.6 %collective-permute-start.18 = (bf16[256,4224]{1,0:T(8,128)(2,1)}, bf16[256,4224]{1,0:T(8,128)(2,1)}, u32[]{:S(2)}, u32[]{:S(2)}) collective-permute-start(bf16[256,4224]{1,0:T(8,128)(2,1)} %collective-permute-done.4), channel_id=1, source_target_pairs={{0,16},{4,20},{8,24},{12,28},{16,0},{20,4},{24,8},{28,12},{1,17},{... | collective-permute-start | bytes 6488072 | tf_op jit(solution)/shard_map/ppermute | solution.py:37
  258.4 48.3 %collective-permute-start.16 = (bf16[2,64,2048]{2,1,0:T(8,128)(2,1)}, bf16[2,64,2048]{2,1,0:T(8,128)(2,1)}, u32[]{:S(2)}, u32[]{:S(2)}) collective-permute-start(bf16[2,64,2048]{2,1,0:T(8,128)(2,1)} %get-tuple-element.225), channel_id=1, source_target_pairs={{0,2},{1,3},{2,0},{3,1},{4,6},{5,7},{6,4},{7,5},{8,10},{9,11},{10,... | collective-permute-start | bytes 1572872 | tf_op jit(solution)/shard_map/ppermute | solution.py:37
  258.4 58.5 %collective-permute-start.17 = (bf16[2,64,2048]{2,1,0:T(8,128)(2,1)}, bf16[2,64,2048]{2,1,0:T(8,128)(2,1)}, u32[]{:S(2)}, u32[]{:S(2)}) collective-permute-start(bf16[2,64,2048]{2,1,0:T(8,128)(2,1)} %get-tuple-element.224), channel_id=1, source_target_pairs={{0,3},{1,2},{2,1},{3,0},{4,7},{5,6},{6,5},{7,4},{8,11},{9,10},{10,... | collective-permute-start | bytes 1572872 | tf_op jit(solution)/shard_map/ppermute | solution.py:37
  275.6 89.2 %collective-permute-start.22 = (bf16[256,4224]{1,0:T(8,128)(2,1)}, bf16[256,4224]{1,0:T(8,128)(2,1)}, u32[]{:S(2)}, u32[]{:S(2)}) collective-permute-start(bf16[256,4224]{1,0:T(8,128)(2,1)} %collective-permute-done.14.refs_1_), channel_id=1, source_target_pairs={{0,16},{4,20},{8,24},{12,28},{16,0},{20,4},{24,8},{28,12},{1,17},{... | collective-permute-start | bytes 6488072 | tf_op jit(solution)/shard_map/ppermute | solution.py:37
  368.6 58.5 %collective-permute-start.23 = (bf16[384,2176]{1,0:T(8,128)(2,1)S(1)}, bf16[384,2176]{1,0:T(8,128)(2,1)}, u32[]{:S(2)}, u32[]{:S(2)}) collective-permute-start(bf16[384,2176]{1,0:T(8,128)(2,1)S(1)} %bitcast.420), channel_id=1, source_target_pairs={{0,8},{4,12},{8,0},{12,4},{16,24},{20,28},{24,16},{28,20},{1,9},{5... | collective-permute-start | bytes 5013512 | tf_op jit(solution)/shard_map/ppermute | solution.py:37
  427.7 51.8 %collective-permute-start.36 = (bf16[384,2048]{1,0:T(8,128)(2,1)}, bf16[384,2048]{1,0:T(8,128)(2,1)}, u32[]{:S(2)}, u32[]{:S(2)}) collective-permute-start(bf16[384,2048]{1,0:T(8,128)(2,1)} %get-tuple-element.114), channel_id=1, source_target_pairs={{0,4},{4,0},{8,12},{12,8},{16,20},{20,16},{24,28},{28,24},{1,5},{5... | collective-permute-start | bytes 4718600 | tf_op jit(solution)/shard_map/ppermute | solution.py:37
  479.1 46.7 %collective-permute-start.38 = (bf16[384,2176]{1,0:T(8,128)(2,1)}, bf16[384,2176]{1,0:T(8,128)(2,1)S(1)}, u32[]{:S(2)}, u32[]{:S(2)}) collective-permute-start(bf16[384,2176]{1,0:T(8,128)(2,1)} %get-tuple-element.116), channel_id=1, source_target_pairs={{0,4},{4,0},{8,12},{12,8},{16,20},{20,16},{24,28},{28,24},{1,5},{5... | collective-permute-start | bytes 5013512 | tf_op jit(solution)/shard_map/ppermute | solution.py:37
  486.9 38.9 %collective-permute-start.34 = (bf16[384,2176]{1,0:T(8,128)(2,1)}, bf16[384,2176]{1,0:T(8,128)(2,1)}, u32[]{:S(2)}, u32[]{:S(2)}) collective-permute-start(bf16[384,2176]{1,0:T(8,128)(2,1)} %add_convert_fusion.5), channel_id=1, source_target_pairs={{0,8},{4,12},{8,0},{12,4},{16,24},{20,28},{24,16},{28,20},{1,9},{5... | collective-permute-start | bytes 5013512 | tf_op jit(solution)/shard_map/ppermute | solution.py:37
  515.1 63.1 %collective-permute-start.42 = (bf16[256,4224]{1,0:T(8,128)(2,1)}, bf16[256,4224]{1,0:T(8,128)(2,1)}, u32[]{:S(2)}, u32[]{:S(2)}) collective-permute-start(bf16[256,4224]{1,0:T(8,128)(2,1)} %get-tuple-element.130), channel_id=1, source_target_pairs={{0,16},{4,20},{8,24},{12,28},{16,0},{20,4},{24,8},{28,12},{1,17},{... | collective-permute-start | bytes 6488072 | tf_op jit(solution)/shard_map/ppermute | solution.py:37
  528.0 97.0 %collective-permute-start.37 = (bf16[384,2048]{1,0:T(8,128)(2,1)}, bf16[384,2048]{1,0:T(8,128)(2,1)}, u32[]{:S(2)}, u32[]{:S(2)}) collective-permute-start(bf16[384,2048]{1,0:T(8,128)(2,1)} %add_convert_fusion.6), channel_id=1, source_target_pairs={{0,8},{4,12},{8,0},{12,4},{16,24},{20,28},{24,16},{28,20},{1,9},{5... | collective-permute-start | bytes 4718600 | tf_op jit(solution)/shard_map/ppermute | solution.py:37
  580.2 44.7 %collective-permute-start.45 = (bf16[2,64,2048]{2,1,0:T(8,128)(2,1)S(1)}, bf16[2,64,2048]{2,1,0:T(8,128)(2,1)S(1)}, u32[]{:S(2)}, u32[]{:S(2)}) collective-permute-start(bf16[2,64,2048]{2,1,0:T(8,128)(2,1)S(1)} %bitcast.437), channel_id=1, source_target_pairs={{0,3},{1,2},{2,1},{3,0},{4,7},{5,6},{6,5},{7,4},{8,11},{9,10},{10,... | collective-permute-start | bytes 1572872 | tf_op jit(solution)/shard_map/ppermute | solution.py:37
  635.8 332.6 %reduce-scatter.5.cloned.1.call-start = ((), (), s32[]{:S(2)}) async-start(), calls=%async_computation.6 | async-start | bytes 14155776 | tf_op jit(solution)/shard_map/reduce_scatter | solution.py:781
  635.9 70.8 %collective-permute-start.46 = (bf16[256,4224]{1,0:T(8,128)(2,1)}, bf16[256,4224]{1,0:T(8,128)(2,1)}, u32[]{:S(2)}, u32[]{:S(2)}) collective-permute-start(bf16[256,4224]{1,0:T(8,128)(2,1)} %get-tuple-element.152), channel_id=1, source_target_pairs={{0,16},{4,20},{8,24},{12,28},{16,0},{20,4},{24,8},{28,12},{1,17},{... | collective-permute-start | bytes 6488072 | tf_op jit(solution)/shard_map/ppermute | solution.py:37
  710.5 83.4 %collective-permute-start.53 = (bf16[256,4224]{1,0:T(8,128)(2,1)}, bf16[256,4224]{1,0:T(8,128)(2,1)}, u32[]{:S(2)}, u32[]{:S(2)}) collective-permute-start(bf16[256,4224]{1,0:T(8,128)(2,1)} %get-tuple-element.171), channel_id=1, source_target_pairs={{0,16},{4,20},{8,24},{12,28},{16,0},{20,4},{24,8},{28,12},{1,17},{... | collective-permute-start | bytes 6488072 | tf_op jit(solution)/shard_map/ppermute | solution.py:37
  747.6 44.5 %collective-permute-start.52 = (bf16[2,64,2176]{2,1,0:T(8,128)(2,1)}, bf16[2,64,2176]{2,1,0:T(8,128)(2,1)}, u32[]{:S(2)}, u32[]{:S(2)}) collective-permute-start(bf16[2,64,2176]{2,1,0:T(8,128)(2,1)} %get-tuple-element.231), channel_id=1, source_target_pairs={{0,3},{1,2},{2,1},{3,0},{4,7},{5,6},{6,5},{7,4},{8,11},{9,10},{10,... | collective-permute-start | bytes 1671176 | tf_op jit(solution)/shard_map/ppermute | solution.py:37
  752.6 85.0 %collective-permute-start.56 = (bf16[256,4224]{1,0:T(8,128)(2,1)}, bf16[256,4224]{1,0:T(8,128)(2,1)}, u32[]{:S(2)}, u32[]{:S(2)}) collective-permute-start(bf16[256,4224]{1,0:T(8,128)(2,1)} %add_convert_fusion.2), channel_id=1, source_target_pairs={{0,8},{4,12},{8,0},{12,4},{16,24},{20,28},{24,16},{28,20},{1,9},{5... | collective-permute-start | bytes 6488072 | tf_op jit(solution)/shard_map/ppermute | solution.py:37
  772.8 119.6 %collective-permute-start.55 = (bf16[256,4224]{1,0:T(8,128)(2,1)}, bf16[256,4224]{1,0:T(8,128)(2,1)}, u32[]{:S(2)}, u32[]{:S(2)}) collective-permute-start(bf16[256,4224]{1,0:T(8,128)(2,1)} %add_convert_fusion.3), channel_id=1, source_target_pairs={{0,8},{4,12},{8,0},{12,4},{16,24},{20,28},{24,16},{28,20},{1,9},{5... | collective-permute-start | bytes 6488072 | tf_op jit(solution)/shard_map/ppermute | solution.py:37
  794.9 114.9 %collective-permute-start.54 = (bf16[256,4224]{1,0:T(8,128)(2,1)}, bf16[256,4224]{1,0:T(8,128)(2,1)}, u32[]{:S(2)}, u32[]{:S(2)}) collective-permute-start(bf16[256,4224]{1,0:T(8,128)(2,1)} %get-tuple-element.175), channel_id=1, source_target_pairs={{0,16},{4,20},{8,24},{12,28},{16,0},{20,4},{24,8},{28,12},{1,17},{... | collective-permute-start | bytes 6488072 | tf_op jit(solution)/shard_map/ppermute | solution.py:37
  800.3 109.5 %all-to-all-start.1 = ((bf16[8,48,2048]{2,1,0:T(8,128)(2,1)}), bf16[8,48,2048]{2,1,0:T(8,128)(2,1)}, u32[]{:S(2)}, u32[]{:S(2)}) async-start(bf16[8,48,2048]{2,1,0:T(8,128)(2,1)} %pad_maximum_fusion.11), calls=%async_computation.1 | async-start | bytes 3145728 | tf_op jit(solution)/shard_map/all_to_all | solution.py:807
  975.1 39.2 %collective-permute-start.66 = (bf16[256,512]{1,0:T(8,128)(2,1)S(1)}, bf16[256,512]{1,0:T(8,128)(2,1)S(1)}, u32[]{:S(2)}, u32[]{:S(2)}) collective-permute-start(bf16[256,512]{1,0:T(8,128)(2,1)S(1)} %get-tuple-element.244), channel_id=1, source_target_pairs={{0,0},{2,1},{1,2},{3,3},{4,4},{6,5},{5,6},{7,7},{8,8},{10,9},{9,10... | collective-permute-start | bytes 786440 | tf_op jit(solution)/shard_map/ppermute | solution.py:842
  (116 other events, 1987.8 us)
Sparse Core Ops, SparseCore 0:
  88.8 114.4 all-gather.1
  635.9 99.4 reduce-scatter.2
  767.4 139.4 reduce-scatter.4

commit v9 on v8

--- a/solution.py
+++ b/solution.py
@@ -269,10 +269,9 @@
 
 
 def expert_kernel(place_ref, hidden, grad, *refs):
-    piece_count = (len(refs) - 8) // 2
+    piece_count = (len(refs) - 6) // 2
     own_pieces, near_pieces = refs[:piece_count], refs[piece_count : 2 * piece_count]
-    out_pair, hidden_pair = refs[2 * piece_count :][:2], refs[2 * piece_count :][2:4]
-    act_out, joint_out, weights, sems = refs[2 * piece_count + 4 :]
+    out, hidden_out, act_out, joint_out, weights, sems = refs[2 * piece_count :]
     core, chip = place_ref[0], place_ref[1]
     rows, columns = near_pieces[0].shape
     units = columns // 3
@@ -310,19 +309,13 @@
         gate_grad = act_grad * up_pre * sigma * (1.0 + gate_pre * (1.0 - sigma))
         joint_out[:, start : start + size] = gate_grad.astype(bf16)
         joint_out[:, units + start : units + start + size] = (act_grad * silu_vals).astype(bf16)
+    for start in range(0, width, 512):
+        block = weights[start : start + 512, : 2 * units]
+        hidden_out[:, start : start + 512] = dot_t(joint_out[...], block).astype(bf16)
+        block = weights[start : start + 512, 2 * units :]
+        out[:, start : start + 512] = dot_t(act_out[...], block).astype(bf16)
     lanes = lax.broadcasted_iota(jnp.int32, (hidden.shape[0], HDIM), 1)
-    last = jnp.where(lanes == 0, slot_sum, 0.0).astype(bf16)
-    for number in range(2):
-
-        @pl.when(pl.program_id(0) == number)
-        def _():
-            out, hidden_out = out_pair[number], hidden_pair[number]
-            for start in range(0, width, 512):
-                block = weights[start : start + 512, : 2 * units]
-                hidden_out[:, start : start + 512] = dot_t(joint_out[...], block).astype(bf16)
-                block = weights[start : start + 512, 2 * units :]
-                out[:, start : start + 512] = dot_t(act_out[...], block).astype(bf16)
-            hidden_out[:, width:] = last
+    hidden_out[:, width:] = jnp.where(lanes == 0, slot_sum, 0.0).astype(bf16)
 
 
 def expert_rows(position, hidden, grad, own_pieces, near_pieces):
@@ -336,9 +329,6 @@
     def tiled(size):
         return pl.BlockSpec((tile, size), lambda i, at: (i, 0))
 
-    def fixed(size):
-        return pl.BlockSpec((tile, size), lambda i, at: (0, 0))
-
     return pl.pallas_call(
         expert_kernel,
         grid_spec=pltpu.PrefetchScalarGridSpec(
@@ -346,19 +336,15 @@
             grid=(rows // tile,),
             in_specs=[tiled(width + HDIM), tiled(width)]
             + [pl.BlockSpec(memory_space=pl.ANY)] * (2 * count),
-            out_specs=[fixed(width)] * 2
-            + [fixed(width + HDIM)] * 2
-            + [tiled(units), tiled(2 * units)],
+            out_specs=[tiled(width), tiled(width + HDIM), tiled(units), tiled(2 * units)],
             scratch_shapes=[
                 pltpu.VMEM((width, columns), bf16),
                 pltpu.SemaphoreType.DMA((2 * count,)),
             ],
         ),
         out_shape=[
-            shape((tile, width), bf16),
-            shape((tile, width), bf16),
-            shape((tile, width + HDIM), bf16),
-            shape((tile, width + HDIM), bf16),
+            shape((rows, width), bf16),
+            shape((rows, width + HDIM), bf16),
             shape((rows, units), bf16),
             shape((rows, 2 * units), bf16),
         ],
@@ -372,7 +358,7 @@
     )(position, hidden, grad, *own_pieces, *near_pieces)
 
 
-def expert_grad_kernel(order, *refs):
+def expert_grad_kernel(cuts, order, *refs):
     hidden, grad, gates, joint, active = [refs[2 * n : 2 * n + 2] for n in range(5)]
     outs = refs[10:]
     units = active[0].shape[1]
@@ -385,9 +371,12 @@
 
     left, right = scaled(hidden), scaled(grad)
     step = pl.program_id(0)
-    for number, out in enumerate(outs):
-
-        @pl.when(step == number)
+    first = [0]
+    for cut in cuts:
+        first.append(first[-1] + cut)
+    for out, start, cut in zip(outs, first, cuts):
+
+        @pl.when((step >= start) & (step < start + cut))
         def _():
             for start, size in unit_blocks(2 * units):
                 out[:, start : start + size] = sum(
@@ -399,7 +388,7 @@
                 ).astype(bf16)
 
 
-def expert_grads(chunks, chunk_rows, rows_of, joints, actives):
+def expert_grads(chunks, cuts, chunk_rows, rows_of, joints, actives):
     hidden, grad = rows_of[:2], rows_of[2:]
     rows, units = actives[0].shape
     width = grad[0].shape[1]
@@ -414,7 +403,7 @@
 
     column = pl.BlockSpec((rows, half), lambda i, at: (0, at[i]))
     return pl.pallas_call(
-        expert_grad_kernel,
+        functools.partial(expert_grad_kernel, cuts),
         grid_spec=pltpu.PrefetchScalarGridSpec(
             num_scalar_prefetch=1,
             grid=(2 * count,),
@@ -423,10 +412,14 @@
             + [whole(2 * units)] * 2
             + [whole(units)] * 2,
             out_specs=[
-                pl.BlockSpec((half, 3 * units), lambda i, at: (0, 0)) for _ in range(2 * count)
+                pl.BlockSpec(
+                    (half, 3 * units),
+                    lambda i, at, start=sum(cuts[:n]), cut=cut: (jnp.clip(i - start, 0, cut - 1), 0),
+                )
+                for n, cut in enumerate(cuts)
             ],
         ),
-        out_shape=[jax.ShapeDtypeStruct((half, 3 * units), bf16)] * (2 * count),
+        out_shape=[jax.ShapeDtypeStruct((cut * half, 3 * units), bf16) for cut in cuts],
         compiler_params=pltpu.CompilerParams(vmem_limit_bytes=56 * 2**20),
         cost_estimate=pl.CostEstimate(
             flops=4 * count * chunk_rows * rows * 3 * units,
@@ -549,14 +542,16 @@
     side_first = swap(send_pair[0], "dp", 2)
     keep_first = [swap(keep_pair[0], "dp", step) for step in line_steps]
     joint_own = columns_of(query_weight[0], attn_out_weight[0])
-    joint_own = jnp.concatenate([joint_own, own_kv], axis=1)
-    joint_full = lax.all_gather(
-        after(joint_own, side_first, keep_first), "dp", axis=0, tiled=True
-    )
+    first_own = jnp.concatenate([joint_own[:, :query_width], own_kv], axis=1)
+    first_own, second_own = lax.optimization_barrier(
+        (first_own, joint_own[:, query_width:], side_first, keep_first)
+    )[:2]
+    joint_full = lax.all_gather(first_own, "dp", axis=0, tiled=True)
+    out_full = lax.all_gather(second_own, "dp", axis=0, tiled=True)
     late_pair = after((keep_pair[1], send_pair[1], side_first), joint_full)
     keep_second = [swap(late_pair[0], "dp", step) for step in line_steps]
     side_second = swap(late_pair[1], "dp", 2)
-    first_lines = [swap(late_pair[2], "dp", step) for step in line_steps]
+    first_lines = [swap(after(late_pair[2], out_full), "dp", step) for step in line_steps]
     second_lines = [swap(side_second, "dp", step) for step in line_steps]
     firsts, seconds = [keep_pair[0], side_first], [keep_pair[1], side_second]
     for line in range(lines - 1):
@@ -565,8 +560,7 @@
     near_pieces = [swap(piece, "dp", 1) for piece in firsts]
     own_pieces = seconds
     query_full = joint_full[:, :query_width]
-    out_full = joint_full[:, query_width : 2 * query_width]
-    kv_full = joint_full[:, 2 * query_width :]
+    kv_full = joint_full[:, query_width:]
 
     positions = jnp.arange(group_rows, dtype=jnp.int32)
     first_len = lax.dynamic_index_in_dim(seq_lengths[:, :, 0], group, 1, keepdims=True)
@@ -623,7 +617,7 @@
         return jnp.concatenate([value, swap(value, "dp", 1)], axis=0)
 
     def quad_sums(value):
-        (own, near), (far, across) = value
+        (own, near), (far, across) = [jnp.split(half, 2, axis=0) for half in value]
         far_sum = far.astype(f32) + swap(across, "dp", 1).astype(f32)
         return own.astype(f32) + swap(near, "dp", 1).astype(f32), far_sum.astype(bf16)
 
@@ -644,8 +638,8 @@
     gain_two = ffn_gain.astype(f32)
     normed_one, scale_one = normalize(x_home)
     hidden_one_home = (normed_one * gain_one).astype(bf16)
-    hidden_one_raw = gather_rows(hidden_one_home)
-    hidden_one = after(hidden_one_raw, near_pieces[:3])
+    hidden_one_raw = gather_rows(after(hidden_one_home, near_pieces[:3]))
+    hidden_one = hidden_one_raw
     grad_sent = send_packed(after(dy_home.astype(bf16), hidden_one))
     logits_one = dot(hidden_one, attn_router)
     gates_one, matches_one, chosen_one, gate_vals_one = route_gates(
@@ -692,32 +686,28 @@
     )
     hidden_far = near_rows(after(hidden_far, near_results))
     far_results = expert_rows(position, hidden_far, grad_far, own_pieces, near_pieces)
-    ffn_parts = near_results[:2], far_results[:2]
-    hidden_parts = near_results[2:4], far_results[2:4]
-    actives, joint_grads = zip(near_results[4:], far_results[4:])
+    ffn_parts, hidden_parts, actives, joint_grads = zip(near_results, far_results)
 
     def block_grads(steps, *others):
         rows = after((hidden_near, hidden_far, grad_near, grad_far), *others)
-        return expert_grads([chip ^ k for k in steps], chip_rows, rows, joint_grads, actives)
+        cuts = (2, 1, 1) * (len(steps) // 2)
+        return expert_grads([chip ^ k for k in steps], cuts, chip_rows, rows, joint_grads, actives)
 
     hidden_sum, hidden_far_sum = quad_sums(hidden_parts)
     ffn_sum, ffn_far_sum = quad_sums(ffn_parts)
     line_grads = block_grads([k ^ 1 for k in range(2, chips)], hidden_far_sum)
-    side_got, keep_got = [[], []], [[], []]
-    last = ()
-    for which, got in enumerate((side_got, keep_got)):
-        for part in range(2):
-            for line in range(lines - 1):
-                block = after(line_grads[4 * line + 2 * which + part], *last)
-                got[part].append(swap(block, "dp", 4 * line + 4))
-            last = got[part][-1:]
+    side_got = [swap(line_grads[3 * line], "dp", step) for line, step in enumerate(line_steps)]
+    keep_got = []
+    for part in range(2):
+        blocks = after(line_grads[part + 1 :: 3], side_got, keep_got)
+        keep_got.append([swap(block, "dp", step) for block, step in zip(blocks, line_steps)])
     hidden_got, ffn_far_sum, ffn_sum = lax.optimization_barrier(
         (swap(hidden_far_sum, "dp", 2), ffn_far_sum, ffn_sum, line_grads)
     )[:3]
     hidden_sum = hidden_sum + hidden_got.astype(f32)
     own_grads = block_grads([1, 0], hidden_sum)
     back_packed = return_packed(hidden_sum, *own_grads)
-    ffn_sum = ffn_sum + swap(after(ffn_far_sum, hidden_got), "dp", 2).astype(f32)
+    ffn_sum = ffn_sum + swap(after(ffn_far_sum, back_packed), "dp", 2).astype(f32)
 
     def total(own, got):
         return functools.reduce(jnp.add, [part.astype(f32) for part in [own] + got]).astype(bf16)
@@ -737,10 +727,12 @@
     gain_two_grad = jnp.sum(hidden_two_grad * normed_two, axis=0)
     resid_grad = dy_home + norm_back(hidden_two_grad * gain_two, normed_two, scale_two)
 
-    resid_grad_low = after(resid_grad.astype(bf16), *side_got[0])
-    resid_grad_all = after(gather_rows(resid_grad_low), ffn_sum)
+    resid_grad_all = after(gather_rows(resid_grad.astype(bf16)), side_got)
     out_part = t_dot(resid_grad_all, gated_vals).astype(bf16)
-    vals_grad = after(dot(resid_grad_all, out_full), out_part, side_got[1])
+    vals_grad = after(dot(resid_grad_all, out_full), out_part)
+    side_own = after((own_grads[0], side_got), vals_grad)
+    vals_grad, side_sum = lax.optimization_barrier((vals_grad, total(*side_own)))
+    other_sum = swap(side_sum, "dp", 2)
     ffn_packed = return_packed(after(ffn_sum, vals_grad))
     out_home = (resid + unpack(ffn_packed, gates_two)).astype(bf16)
     query_grad, key_grad, value_grad, slot_part_one = attention_backward(
@@ -748,11 +740,9 @@
         own_heads, group_rows,
     )
     query_grad, key_grad, value_grad, slot_part_one = lax.optimization_barrier(
-        (query_grad, key_grad, value_grad, slot_part_one, ffn_packed)
+        (query_grad, key_grad, value_grad, slot_part_one, ffn_packed, keep_got[0])
     )[:4]
     kv_grad = jnp.concatenate([key_grad, value_grad], axis=1)
-    side_own = after((own_grads[:2], side_got), query_grad)
-    other_sums = [swap(total(*pair), "dp", 2) for pair in zip(*side_own)]
     hidden_one_part = dot_t(query_grad, query_full) + dot_t(kv_grad, kv_full)
     hidden_one_part = hidden_one_part.astype(bf16)
     joint_part_grad = t_dot(
@@ -761,7 +751,7 @@
     back_one = scatter_rows(
         jnp.concatenate([hidden_one_part, slot_part_one.astype(bf16)], axis=1)
     )
-    back_one, keep_first_got = lax.optimization_barrier((back_one, keep_got[0], joint_part_grad))[:2]
+    back_one, keep_got = lax.optimization_barrier((back_one, keep_got, joint_part_grad))[:2]
     hidden_one_grad, slot_one_grad = back_one[:, :width], back_one[:, width : width + slots]
 
     def own(value):
@@ -784,7 +774,6 @@
     out_grad = slots_of(after(reduced(out_part), in_low))
     joint_own = reduced(joint_part_grad)
 
-    query_own, kv_own = joint_own[:, :query_width], joint_own[:, query_width:]
     results = jnp.stack([out_home, in_low]).reshape(2, micro, tok_rows, width)
     results = jnp.einsum("mtr,bmtd->bmrd", deal, results, preferred_element_type=f32).astype(bf16)
     results = results.reshape(2 * micro, dp_count, piece_rows, width).transpose(1, 0, 2, 3)
@@ -805,9 +794,10 @@
     small = jnp.broadcast_to(small[None], (dp_count,) + small.shape)
     results = jnp.concatenate([results, small], axis=1)
     results = lax.all_to_all(results, "dp", split_axis=0, concat_axis=0, tiled=True)
-    results, keep_last_got, other_sums, out_grad = lax.optimization_barrier(
-        (results, keep_got[1], other_sums, out_grad)
-    )
+    results, keep_got, other_sum, out_grad, joint_own = lax.optimization_barrier(
+        (results, keep_got, other_sum, out_grad, joint_own)
+    )
+    query_own, kv_own = joint_own[:, :query_width], joint_own[:, query_width:]
     small = results[:, sent_back:].astype(f32)
     results = results[:, :sent_back].reshape(dp_count, 2 * micro, piece_rows, width)
     results = results.transpose(1, 0, 2, 3).reshape(2, micro, tok_rows, width)
@@ -815,16 +805,17 @@
     peak_row = jnp.max((peak_row[:, 0] + peak_row[:, 1]) + peak_row[:, 2], axis=0)
     small = jnp.sum(small, axis=0)
     small = lax.dynamic_update_slice(small, peak_row[None], (sum_rows, 0))
-    small = place(
-        [swap(small, "expert", k) if k else small for k in range(slots)],
-        [col ^ k for k in range(slots)],
-    )
-    sums = jnp.sum(small[:, :sum_rows], axis=0)
-    peaks_all = small[:, sum_rows, :peak_count].reshape(slots, own_heads, slots)
-    peaks_all = peaks_all.transpose(2, 0, 1).reshape(slots, HEADS)
-
-    keep_parts = keep_first_got, keep_last_got
-    keep_sums = [total(own_grads[2 + part], keep_parts[part]) for part in range(2)]
+    smalls = [swap(small, "expert", k) if k else small for k in range(slots)]
+    peaks_all = jnp.zeros((slots, HEADS), f32)
+    for k, part in enumerate(smalls):
+        part = part[sum_rows, :peak_count].reshape(own_heads, slots).T
+        peaks_all = lax.dynamic_update_slice(peaks_all, part, (0, (col ^ k) * own_heads))
+    while len(smalls) > 1:
+        smalls = [left + right for left, right in zip(smalls[::2], smalls[1::2])]
+    sums = smalls[0][:sum_rows]
+
+    keep_sums = [total(own_grads[1 + part], keep_got[part]) for part in range(2)]
+    other_sums = other_sum.reshape(2, shard_rows, 3 * quarter)
     by_rows = [jnp.stack([keep_sums[part], other_sums[part]]) for part in range(2)]
     own_pair = jnp.where(core == 0, by_rows[0], by_rows[1])
     near_pair = swap(jnp.where(core == 0, by_rows[1], by_rows[0]), "dp", 1)

time: 1030 us -> 1040 us (level)
  local copies, waits for them, and re-layouts: 71.6 us -> 93 us
  starting transfers between devices: 77.6 us -> 93.2 us
  Pallas kernels: 183 us -> 168 us
    all_gather x1 -> x2, waiting for transfers between devices: 25.3 us -> 66.4 us  [the longest x1 66.4 us: local(): out_full = lax.all_gather(second_own, 'dp', axis=0, tiled=True)]
    ppermute x1, waiting for transfers between devices: 21.9 us -> 1.05 us  [local(): lax.ppermute(jnp.where(holds_keys, high_kv, low_kv), 'expert', second_pairs)]
    ppermute x65 -> x63, waiting for transfers between devices: 416 us -> 398 us  [swap(): return lax.ppermute(value, axis, [(i, i ^ step) for i in range(count)])]
    pallas_call x2, Pallas kernels: 96.5 us -> 81.9 us  [expert_rows(): pl.pallas_call(expert_kernel, grid_spec=pltpu.PrefetchScalarGridSpec(num_...]
    dynamic_update_slice x4, local copies, waits for them, and re-layouts: 13.8 us -> 0.73 us  [local(): lax.dynamic_update_slice(peaks_all, part, (0, (col ^ k) * own_heads))]
    ppermute x65 -> x63, starting transfers between devices: 60.8 us -> 73.5 us  [swap(): return lax.ppermute(value, axis, [(i, i ^ step) for i in range(count)])]
    unnamed x169 -> x230, local copies, waits for them, and re-layouts: 19.3 us -> 26.8 us
  transfers between devices with their start and end apart: 74 -> 73, of which waited for: 34 -> 33; matrix products, arithmetic and copies ran while one was open for 20% -> 20% of each run, Pallas kernels for 18% -> 16%
where the time goes in v9:
time: 1040 us; the launch traced here: 1030 us
  waiting for transfers between devices  497 us (48%)
  Pallas kernels  168 us (16%)
  starting transfers between devices  93.2 us (9%)
  local copies, waits for them, and re-layouts  93 us (9%)
  other arithmetic  86.4 us (8%)
  matrix products  73.5 us (7%)
  between operations  17.1 us (2%)
    ppermute x63, waiting for transfers between devices, swap(): return lax.ppermute(value, axis, [(i, i ^ step) for i in range(count)])  398 us
    pallas_call x2, Pallas kernels, expert_rows(): pl.pallas_call(expert_kernel, grid_spec=pltpu.PrefetchScalarGridSpec(num_...  81.9 us
    ppermute x63, starting transfers between devices, swap(): return lax.ppermute(value, axis, [(i, i ^ step) for i in range(count)])  73.5 us
    all_gather x1, waiting for transfers between devices, local(): out_full = lax.all_gather(second_own, 'dp', axis=0, tiled=True)  66.4 us
    pallas_call x2, Pallas kernels, expert_grads(): pl.pallas_call(functools.partial(expert_grad_kernel, cuts), grid_spec=plt...  50.8 us
    unnamed x230, local copies, waits for them, and re-layouts  26.8 us
    dot_general x5, matrix products, dot(): return jnp.dot(left, right, preferred_element_type=f32)  24 us
    dot_general x5, matrix products, dot_t(): lax.dot_general(left, right, (((1,), (1,)), ((), ())), preferred_element_...  22.6 us
  transfers between devices with their start and end apart: 73, of which 33 were waited for; matrix products, arithmetic and copies ran while one was open for 20% of the time, Pallas kernels for 16%

profile of v9, /device:TPU:8, one launch (start us, length us, event | category | flops | bytes accessed | tf_op | source)
XLA Modules:
  0.0 1028.3 jit_solution(11767139591895705552)
XLA Ops:
  38.3 14.2 %collective-permute-done.8 = bf16[256,1024]{1,0:T(8,128)(2,1)} collective-permute-done((bf16[256,1024]{1,0:T(8,128)(2,1)}, bf16[256,1024]{1,0:T(8,128)(2,1)}, u32[]{:S(2)}, u32[]{:S(2)}) %collective-permute-start.8) | collective-permute-done | bytes 524320 | tf_op jit(solution)/shard_map/ppermute | solution.py:37
  54.5 15.2 %collective-permute-done.9 = bf16[256,1024]{1,0:T(8,128)(2,1)S(1)} collective-permute-done((bf16[256,1024]{1,0:T(8,128)(2,1)}, bf16[256,1024]{1,0:T(8,128)(2,1)S(1)}, u32[]{:S(2)}, u32[]{:S(2)}) %collective-permute-start.9) | collective-permute-done | bytes 524320 | tf_op jit(solution)/shard_map/ppermute | solution.py:37
  69.8 12.0 %collective-permute-done.10 = bf16[256,1024]{1,0:T(8,128)(2,1)S(1)} collective-permute-done((bf16[256,1024]{1,0:T(8,128)(2,1)}, bf16[256,1024]{1,0:T(8,128)(2,1)S(1)}, u32[]{:S(2)}, u32[]{:S(2)}) %collective-permute-start.10) | collective-permute-done | bytes 524320 | tf_op jit(solution)/shard_map/ppermute | solution.py:37
  97.9 18.6 %all-to-all-done = bf16[8,4,8,2048]{3,2,1,0:T(8,128)(2,1)S(1)} async-done(((bf16[8,4,8,2048]{3,2,1,0:T(8,128)(2,1)}), bf16[8,4,8,2048]{3,2,1,0:T(8,128)(2,1)S(1)}, u32[]{:S(2)}, u32[]{:S(2)}) %all-to-all-start) | async-done | bytes 1048608 | tf_op jit(solution)/shard_map/all_to_all | solution.py:476
  125.4 14.4 %collective-permute-done.5 = bf16[2,64,2048]{2,1,0:T(8,128)(2,1)S(1)} collective-permute-done((bf16[2,64,2048]{2,1,0:T(8,128)(2,1)S(1)}, bf16[2,64,2048]{2,1,0:T(8,128)(2,1)S(1)}, u32[]{:S(2)}, u32[]{:S(2)}) %collective-permute-start.5) | collective-permute-done | bytes 524320 | tf_op jit(solution)/shard_map/ppermute | solution.py:37
  139.8 17.9 %collective-permute-done.6 = bf16[2,64,2048]{2,1,0:T(8,128)(2,1)S(1)} collective-permute-done((bf16[2,64,2048]{2,1,0:T(8,128)(2,1)S(1)}, bf16[2,64,2048]{2,1,0:T(8,128)(2,1)S(1)}, u32[]{:S(2)}, u32[]{:S(2)}) %collective-permute-start.6) | collective-permute-done | bytes 524320 | tf_op jit(solution)/shard_map/ppermute | solution.py:37
  157.8 13.6 %collective-permute-done.7 = bf16[2,64,2048]{2,1,0:T(8,128)(2,1)S(1)} collective-permute-done((bf16[2,64,2048]{2,1,0:T(8,128)(2,1)S(1)}, bf16[2,64,2048]{2,1,0:T(8,128)(2,1)S(1)}, u32[]{:S(2)}, u32[]{:S(2)}) %collective-permute-start.7) | collective-permute-done | bytes 524320 | tf_op jit(solution)/shard_map/ppermute | solution.py:37
  183.9 66.4 %all-gather.5.cloned.1.call-done = bf16[2048,2048]{1,0:T(8,128)(2,1)} async-done(((bf16[256,2048]{1,0:T(8,128)(2,1)}), bf16[2048,2048]{1,0:T(8,128)(2,1)}) %all-gather.5.cloned.1.call-update) | async-done | bytes 8388624 | tf_op jit(solution)/shard_map/all_gather | solution.py:550
  264.9 14.7 %attention_forward.1 = (bf16[512,2048]{1,0:T(8,128)(2,1)S(1)}, bf16[512,2048]{1,0:T(8,128)(2,1)}, bf16[512,2048]{1,0:T(8,128)(2,1)}, bf16[512,512]{1,0:T(8,128)(...) custom-call(s32[2]{0:T(128)S(1)} %fusion.133.lens, f32[512,2048]{1,0:T(8,128)} %fusion.2.query, ...), custom_call_target="tpu_custom_call" | custom-call | flops 1073741824 | bytes 14680064 | tf_op jit(solution)/shard_map/attention_forward/pallas_call | solution.py:181
  302.4 25.0 %collective-permute-done.17 = bf16[2,64,2048]{2,1,0:T(8,128)(2,1)} collective-permute-done((bf16[2,64,2048]{2,1,0:T(8,128)(2,1)}, bf16[2,64,2048]{2,1,0:T(8,128)(2,1)}, u32[]{:S(2)}, u32[]{:S(2)}) %collective-permute-start.17) | collective-permute-done | bytes 524320 | tf_op jit(solution)/shard_map/ppermute | solution.py:37
  327.4 9.2 collective-permute-done.16
  351.1 25.6 %collective-permute-done.21 = bf16[2,48,2176]{2,1,0:T(8,128)(2,1)S(1)} collective-permute-done((bf16[2,48,2176]{2,1,0:T(8,128)(2,1)S(1)}, bf16[2,48,2176]{2,1,0:T(8,128)(2,1)S(1)}, u32[]{:S(2)}, u32[]{:S(2)}) %collective-permute-start.21) | collective-permute-done | bytes 417824 | tf_op jit(solution)/shard_map/ppermute | solution.py:37
  394.2 40.8 %expert_rows.2 = (bf16[768,2048]{1,0:T(8,128)(2,1)}, bf16[768,2176]{1,0:T(8,128)(2,1)}, bf16[768,1408]{1,0:T(8,128)(2,1)}, bf16[768,2816]{1,0:T(8,128)(2,1)}) custom-call(s32[2]{0:T(128)} %pad_add_fusion.1.place_ref, bf16[768,2176]{1,0:T(8,128)(2,1)} %pad_maximum_fusion.2.hidden.refs_0_.refs_4_, bf16[768,2048]{1,0:T(8,128)(2,1)} %copy-done.48, ...), custom_call_target="tpu_custom_call" | custom-call | flops 26575110144 | bytes 36175872 | tf_op jit(solution)/shard_map/expert_rows/pallas_call | solution.py:332
  440.9 41.1 %expert_rows.3 = (bf16[768,2048]{1,0:T(8,128)(2,1)}, bf16[768,2176]{1,0:T(8,128)(2,1)}, bf16[768,1408]{1,0:T(8,128)(2,1)}, bf16[768,2816]{1,0:T(8,128)(2,1)}) custom-call(s32[2]{0:T(128)} %pad_add_fusion.1.place_ref, bf16[768,2176]{1,0:T(8,128)(2,1)} %constant_dynamic-update-slice_fusion.4.hidden.refs_1_.refs_5_, bf16[768,2048]{1,0:T(8,128)(2,1)} %copy-done.47, ...), custom_call_target="tpu_custom_call" | custom-call | flops 26575110144 | bytes 36175872 | tf_op jit(solution)/shard_map/expert_rows/pallas_call | solution.py:332
  500.2 25.4 %expert_grads.2 = (bf16[512,4224]{1,0:T(8,128)(2,1)}, bf16[256,4224]{1,0:T(8,128)(2,1)}, bf16[256,4224]{1,0:T(8,128)(2,1)}) custom-call(s32[4]{0:T(128)} %get-tuple-element.298.order, bf16[768,2176]{1,0:T(8,128)(2,1)} %pad_maximum_fusion.2.hidden.refs_0_.refs_4_, bf16[768,2176]{1,0:T(8,128)(2,1)} %constant_dynamic-update-slice_fusion.4.hidden.refs_1_.refs_5_, ...), custom_call_target="tpu_custom_call" | custom-call | flops 13287555072 | bytes 27918336 | tf_op jit(solution)/shard_map/expert_grads/pallas_call | solution.py:405
  527.0 9.9 collective-permute-done.34
  544.6 25.4 %expert_grads.3 = (bf16[512,4224]{1,0:T(8,128)(2,1)}, bf16[256,4224]{1,0:T(8,128)(2,1)}, bf16[256,4224]{1,0:T(8,128)(2,1)}) custom-call(s32[4]{0:T(128)} %get-tuple-element.299.order, bf16[768,2176]{1,0:T(8,128)(2,1)} %pad_maximum_fusion.2.hidden.refs_0_.refs_4_, bf16[768,2176]{1,0:T(8,128)(2,1)} %constant_dynamic-update-slice_fusion.4.hidden.refs_1_.refs_5_, ...), custom_call_target="tpu_custom_call" | custom-call | flops 13287555072 | bytes 27918336 | tf_op jit(solution)/shard_map/expert_grads/pallas_call | solution.py:405
  571.2 9.2 collective-permute-done.40
  606.1 15.6 %collective-permute-done.42 = bf16[2,64,2048]{2,1,0:T(8,128)(2,1)S(1)} collective-permute-done((bf16[2,64,2048]{2,1,0:T(8,128)(2,1)S(1)}, bf16[2,64,2048]{2,1,0:T(8,128)(2,1)S(1)}, u32[]{:S(2)}, u32[]{:S(2)}) %collective-permute-start.42) | collective-permute-done | bytes 524320 | tf_op jit(solution)/shard_map/ppermute | solution.py:37
  621.7 17.4 %collective-permute-done.43 = bf16[2,64,2048]{2,1,0:T(8,128)(2,1)S(1)} collective-permute-done((bf16[2,64,2048]{2,1,0:T(8,128)(2,1)S(1)}, bf16[2,64,2048]{2,1,0:T(8,128)(2,1)S(1)}, u32[]{:S(2)}, u32[]{:S(2)}) %collective-permute-start.43) | collective-permute-done | bytes 524320 | tf_op jit(solution)/shard_map/ppermute | solution.py:37
  639.2 10.3 %collective-permute-done.44 = bf16[2,64,2048]{2,1,0:T(8,128)(2,1)S(1)} collective-permute-done((bf16[2,64,2048]{2,1,0:T(8,128)(2,1)S(1)}, bf16[2,64,2048]{2,1,0:T(8,128)(2,1)S(1)}, u32[]{:S(2)}, u32[]{:S(2)}) %collective-permute-start.44) | collective-permute-done | bytes 524320 | tf_op jit(solution)/shard_map/ppermute | solution.py:37
  658.5 46.1 %collective-permute-done.41 = bf16[384,2048]{1,0:T(8,128)(2,1)S(1)} collective-permute-done((bf16[384,2048]{1,0:T(8,128)(2,1)}, bf16[384,2048]{1,0:T(8,128)(2,1)S(1)}, u32[]{:S(2)}, u32[]{:S(2)}) %collective-permute-start.41) | collective-permute-done | bytes 1572896 | tf_op jit(solution)/shard_map/ppermute | solution.py:37
  707.2 9.7 fusion.179.vals_grad
  726.1 20.2 %attention_backward.1 = (bf16[512,2048]{1,0:T(8,128)(2,1)S(1)}, bf16[512,512]{1,0:T(8,128)(2,1)S(1)}, bf16[512,512]{1,0:T(8,128)(2,1)S(1)}, f32[512,128]{1,0:T(8,128)S(1)}) custom-call(s32[2]{0:T(128)S(1)} %fusion.133.lens, bf16[512,2048]{1,0:T(8,128)(2,1)} %get-tuple-element.152.query, bf16[512,512]{1,0:T(8,128)(2,1)S(1)} %get-tuple-element.153.key, ...), custom_call_target="tpu_custom_call" | custom-call | flops 2684354560 | bytes 14680064 | tf_op jit(solution)/shard_map/attention_backward/pallas_call | solution.py:212
  749.2 16.8 %collective-permute-done.49 = bf16[256,4224]{1,0:T(8,128)(2,1)S(1)} collective-permute-done((bf16[256,4224]{1,0:T(8,128)(2,1)S(1)}, bf16[256,4224]{1,0:T(8,128)(2,1)S(1)}, u32[]{:S(2)}, u32[]{:S(2)}) %collective-permute-start.49) | collective-permute-done | bytes 2162720 | tf_op jit(solution)/shard_map/ppermute | solution.py:37
  771.5 9.3 add_convert_fusion.3
  780.7 10.1 convolution_convert_fusion
  801.2 29.1 %collective-permute-done.52 = bf16[2,64,2176]{2,1,0:T(8,128)(2,1)S(1)} collective-permute-done((bf16[2,64,2176]{2,1,0:T(8,128)(2,1)S(1)}, bf16[2,64,2176]{2,1,0:T(8,128)(2,1)S(1)}, u32[]{:S(2)}, u32[]{:S(2)}) %collective-permute-start.52) | collective-permute-done | bytes 557088 | tf_op jit(solution)/shard_map/ppermute | solution.py:37
  835.9 20.3 %collective-permute-done.53 = bf16[256,4224]{1,0:T(8,128)(2,1)} collective-permute-done((bf16[256,4224]{1,0:T(8,128)(2,1)S(1)}, bf16[256,4224]{1,0:T(8,128)(2,1)}, u32[]{:S(2)}, u32[]{:S(2)}) %collective-permute-start.53) | collective-permute-done | bytes 2162720 | tf_op jit(solution)/shard_map/ppermute | solution.py:37
  887.3 11.2 %collective-permute-done.56 = bf16[256,512]{1,0:T(8,128)(2,1)S(1)} collective-permute-done((bf16[256,512]{1,0:T(8,128)(2,1)S(1)}, bf16[256,512]{1,0:T(8,128)(2,1)S(1)}, u32[]{:S(2)}, u32[]{:S(2)}) %collective-permute-start.56) | collective-permute-done | bytes 262176 | tf_op jit(solution)/shard_map/ppermute | solution.py:37
  904.6 30.2 %collective-permute-done.54 = bf16[512,4224]{1,0:T(8,128)(2,1)} collective-permute-done((bf16[512,4224]{1,0:T(8,128)(2,1)}, bf16[512,4224]{1,0:T(8,128)(2,1)}, u32[]{:S(2)}, u32[]{:S(2)}) %collective-permute-start.54) | collective-permute-done | bytes 4325408 | tf_op jit(solution)/shard_map/ppermute | solution.py:37
  934.9 9.1 all-to-all-done.1
  (622 shorter events, 357.0 us)
Async XLA Ops:
  7.2 169.3 %all-gather.3.cloned.1.call-start = ((), (), s32[]{:S(2)}) async-start(), calls=%async_computation.4 | async-start | bytes 14155776 | tf_op jit(solution)/shard_map/all_gather | solution.py:549
  14.9 69.4 %collective-permute-start.1 = (bf16[256,4224]{1,0:T(8,128)(2,1)}, bf16[256,4224]{1,0:T(8,128)(2,1)}, u32[]{:S(2)}, u32[]{:S(2)}) collective-permute-start(bf16[256,4224]{1,0:T(8,128)(2,1)} %pad_maximum_fusion.5), channel_id=1, source_target_pairs={{0,8},{4,12},{8,0},{12,4},{16,24},{20,28},{24,16},{28,20},{1,9},{5... | collective-permute-start | bytes 6488072 | tf_op jit(solution)/shard_map/ppermute | solution.py:37
  17.9 66.4 %collective-permute-start.3 = (bf16[256,4224]{1,0:T(8,128)(2,1)}, bf16[256,4224]{1,0:T(8,128)(2,1)}, u32[]{:S(2)}, u32[]{:S(2)}) collective-permute-start(bf16[256,4224]{1,0:T(8,128)(2,1)} %pad_maximum_fusion.4), channel_id=1, source_target_pairs={{0,16},{4,20},{8,24},{12,28},{16,0},{20,4},{24,8},{28,12},{1,17},{... | collective-permute-start | bytes 6488072 | tf_op jit(solution)/shard_map/ppermute | solution.py:37
  35.6 46.1 %collective-permute-start.10 = (bf16[256,1024]{1,0:T(8,128)(2,1)}, bf16[256,1024]{1,0:T(8,128)(2,1)S(1)}, u32[]{:S(2)}, u32[]{:S(2)}) collective-permute-start(bf16[256,1024]{1,0:T(8,128)(2,1)} %pad_maximum_fusion.15), channel_id=1, source_target_pairs={{0,3},{1,2},{2,1},{3,0},{4,7},{5,6},{6,5},{7,4},{8,11},{9,10},{10,... | collective-permute-start | bytes 1572872 | tf_op jit(solution)/shard_map/ppermute | solution.py:37
  84.3 166.0 %all-gather.5.cloned.1.call-start = ((), (), s32[]{:S(2)}) async-start(), calls=%async_computation.5 | async-start | bytes 9437184 | tf_op jit(solution)/shard_map/all_gather | solution.py:550
  90.1 775.5 %reduce-scatter.3.cloned.1.call-start = ((), (), s32[]{:S(2)}) async-start(), calls=%async_computation.6 | async-start | bytes 9437184 | tf_op jit(solution)/shard_map/reduce_scatter | solution.py:771
  122.9 48.4 %collective-permute-start.7 = (bf16[2,64,2048]{2,1,0:T(8,128)(2,1)S(1)}, bf16[2,64,2048]{2,1,0:T(8,128)(2,1)S(1)}, u32[]{:S(2)}, u32[]{:S(2)}) collective-permute-start(bf16[2,64,2048]{2,1,0:T(8,128)(2,1)S(1)} %bitcast.435), channel_id=1, source_target_pairs={{0,3},{1,2},{2,1},{3,0},{4,7},{5,6},{6,5},{7,4},{8,11},{9,10},{10,... | collective-permute-start | bytes 1572872 | tf_op jit(solution)/shard_map/ppermute | solution.py:37
  176.4 114.9 %collective-permute-start.28 = (bf16[2,48,2048]{2,1,0:T(8,128)(2,1)}, bf16[2,48,2048]{2,1,0:T(8,128)(2,1)}, u32[]{:S(2)}, u32[]{:S(2)}) collective-permute-start(bf16[2,48,2048]{2,1,0:T(8,128)(2,1)} %get-tuple-element.248), channel_id=1, source_target_pairs={{0,3},{1,2},{2,1},{3,0},{4,7},{5,6},{6,5},{7,4},{8,11},{9,10},{10,... | collective-permute-start | bytes 1179656 | tf_op jit(solution)/shard_map/ppermute | solution.py:37
  176.4 116.3 %collective-permute-start.27 = (bf16[2,48,2048]{2,1,0:T(8,128)(2,1)}, bf16[2,48,2048]{2,1,0:T(8,128)(2,1)}, u32[]{:S(2)}, u32[]{:S(2)}) collective-permute-start(bf16[2,48,2048]{2,1,0:T(8,128)(2,1)} %get-tuple-element.249), channel_id=1, source_target_pairs={{0,2},{1,3},{2,0},{3,1},{4,6},{5,7},{6,4},{7,5},{8,10},{9,11},{10,... | collective-permute-start | bytes 1179656 | tf_op jit(solution)/shard_map/ppermute | solution.py:37
  176.5 110.1 %collective-permute-start.13 = (bf16[256,4224]{1,0:T(8,128)(2,1)}, bf16[256,4224]{1,0:T(8,128)(2,1)}, u32[]{:S(2)}, u32[]{:S(2)}) collective-permute-start(bf16[256,4224]{1,0:T(8,128)(2,1)} %get-tuple-element.100.refs_0_), channel_id=1, source_target_pairs={{0,16},{4,20},{8,24},{12,28},{16,0},{20,4},{24,8},{28,12},{1,17},{... | collective-permute-start | bytes 6488072 | tf_op jit(solution)/shard_map/ppermute | solution.py:37
  182.4 104.8 %collective-permute-start.14 = (bf16[256,4224]{1,0:T(8,128)(2,1)}, bf16[256,4224]{1,0:T(8,128)(2,1)}, u32[]{:S(2)}, u32[]{:S(2)}) collective-permute-start(bf16[256,4224]{1,0:T(8,128)(2,1)} %get-tuple-element.101), channel_id=1, source_target_pairs={{0,8},{4,12},{8,0},{12,4},{16,24},{20,28},{24,16},{28,20},{1,9},{5... | collective-permute-start | bytes 6488072 | tf_op jit(solution)/shard_map/ppermute | solution.py:37
  250.3 88.3 %collective-permute-start.18 = (bf16[256,4224]{1,0:T(8,128)(2,1)}, bf16[256,4224]{1,0:T(8,128)(2,1)}, u32[]{:S(2)}, u32[]{:S(2)}) collective-permute-start(bf16[256,4224]{1,0:T(8,128)(2,1)} %collective-permute-done.1), channel_id=1, source_target_pairs={{0,16},{4,20},{8,24},{12,28},{16,0},{20,4},{24,8},{28,12},{1,17},{... | collective-permute-start | bytes 6488072 | tf_op jit(solution)/shard_map/ppermute | solution.py:37
  289.8 37.6 %collective-permute-start.17 = (bf16[2,64,2048]{2,1,0:T(8,128)(2,1)}, bf16[2,64,2048]{2,1,0:T(8,128)(2,1)}, u32[]{:S(2)}, u32[]{:S(2)}) collective-permute-start(bf16[2,64,2048]{2,1,0:T(8,128)(2,1)} %get-tuple-element.218), channel_id=1, source_target_pairs={{0,3},{1,2},{2,1},{3,0},{4,7},{5,6},{6,5},{7,4},{8,11},{9,10},{10,... | collective-permute-start | bytes 1572872 | tf_op jit(solution)/shard_map/ppermute | solution.py:37
  291.3 45.3 %collective-permute-start.16 = (bf16[2,64,2048]{2,1,0:T(8,128)(2,1)}, bf16[2,64,2048]{2,1,0:T(8,128)(2,1)}, u32[]{:S(2)}, u32[]{:S(2)}) collective-permute-start(bf16[2,64,2048]{2,1,0:T(8,128)(2,1)} %get-tuple-element.219), channel_id=1, source_target_pairs={{0,2},{1,3},{2,0},{3,1},{4,6},{5,7},{6,4},{7,5},{8,10},{9,11},{10,... | collective-permute-start | bytes 1572872 | tf_op jit(solution)/shard_map/ppermute | solution.py:37
  292.7 43.9 %collective-permute-start.15 = (bf16[2,64,2048]{2,1,0:T(8,128)(2,1)}, bf16[2,64,2048]{2,1,0:T(8,128)(2,1)}, u32[]{:S(2)}, u32[]{:S(2)}) collective-permute-start(bf16[2,64,2048]{2,1,0:T(8,128)(2,1)} %get-tuple-element.217), channel_id=1, source_target_pairs={{0,1},{1,0},{2,3},{3,2},{4,5},{5,4},{6,7},{7,6},{8,9},{9,8},{10,11... | collective-permute-start | bytes 1572872 | tf_op jit(solution)/shard_map/ppermute | solution.py:37
  301.5 81.1 %collective-permute-start.22 = (bf16[256,4224]{1,0:T(8,128)(2,1)}, bf16[256,4224]{1,0:T(8,128)(2,1)}, u32[]{:S(2)}, u32[]{:S(2)}) collective-permute-start(bf16[256,4224]{1,0:T(8,128)(2,1)} %collective-permute-done.14.refs_1_), channel_id=1, source_target_pairs={{0,16},{4,20},{8,24},{12,28},{16,0},{20,4},{24,8},{28,12},{1,17},{... | collective-permute-start | bytes 6488072 | tf_op jit(solution)/shard_map/ppermute | solution.py:37
  342.6 39.3 %collective-permute-start.30 = (bf16[384,2048]{1,0:T(8,128)(2,1)}, bf16[384,2048]{1,0:T(8,128)(2,1)}, u32[]{:S(2)}, u32[]{:S(2)}) collective-permute-start(bf16[384,2048]{1,0:T(8,128)(2,1)} %bitcast.419), channel_id=1, source_target_pairs={{0,8},{4,12},{8,0},{12,4},{16,24},{20,28},{24,16},{28,20},{1,9},{5... | collective-permute-start | bytes 4718600 | tf_op jit(solution)/shard_map/ppermute | solution.py:37
  385.1 49.8 %collective-permute-start.23 = (bf16[384,2176]{1,0:T(8,128)(2,1)S(1)}, bf16[384,2176]{1,0:T(8,128)(2,1)S(1)}, u32[]{:S(2)}, u32[]{:S(2)}) collective-permute-start(bf16[384,2176]{1,0:T(8,128)(2,1)S(1)} %bitcast.417), channel_id=1, source_target_pairs={{0,8},{4,12},{8,0},{12,4},{16,24},{20,28},{24,16},{28,20},{1,9},{5... | collective-permute-start | bytes 5013512 | tf_op jit(solution)/shard_map/ppermute | solution.py:37
  438.2 53.0 %collective-permute-start.36 = (bf16[384,2048]{1,0:T(8,128)(2,1)}, bf16[384,2048]{1,0:T(8,128)(2,1)}, u32[]{:S(2)}, u32[]{:S(2)}) collective-permute-start(bf16[384,2048]{1,0:T(8,128)(2,1)} %split.29), channel_id=1, source_target_pairs={{0,4},{4,0},{8,12},{12,8},{16,20},{20,16},{24,28},{28,24},{1,5},{5... | collective-permute-start | bytes 4718600 | tf_op jit(solution)/shard_map/ppermute | solution.py:37
  490.8 46.2 %collective-permute-start.37 = (bf16[384,2176]{1,0:T(8,128)(2,1)}, bf16[384,2176]{1,0:T(8,128)(2,1)}, u32[]{:S(2)}, u32[]{:S(2)}) collective-permute-start(bf16[384,2176]{1,0:T(8,128)(2,1)} %split.31), channel_id=1, source_target_pairs={{0,4},{4,0},{8,12},{12,8},{16,20},{20,16},{24,28},{28,24},{1,5},{5... | collective-permute-start | bytes 5013512 | tf_op jit(solution)/shard_map/ppermute | solution.py:37
  498.1 38.8 %collective-permute-start.34 = (bf16[384,2176]{1,0:T(8,128)(2,1)}, bf16[384,2176]{1,0:T(8,128)(2,1)}, u32[]{:S(2)}, u32[]{:S(2)}) collective-permute-start(bf16[384,2176]{1,0:T(8,128)(2,1)} %add_convert_fusion.4), channel_id=1, source_target_pairs={{0,8},{4,12},{8,0},{12,4},{16,24},{20,28},{24,16},{28,20},{1,9},{5... | collective-permute-start | bytes 5013512 | tf_op jit(solution)/shard_map/ppermute | solution.py:37
  525.7 123.9 %collective-permute-start.45 = (bf16[512,4224]{1,0:T(8,128)(2,1)}, bf16[512,4224]{1,0:T(8,128)(2,1)}, u32[]{:S(2)}, u32[]{:S(2)}) collective-permute-start(bf16[512,4224]{1,0:T(8,128)(2,1)} %get-tuple-element.124), channel_id=1, source_target_pairs={{0,16},{4,20},{8,24},{12,28},{16,0},{20,4},{24,8},{28,12},{1,17},{... | collective-permute-start | bytes 12976136 | tf_op jit(solution)/shard_map/ppermute | solution.py:37
  604.3 45.2 %collective-permute-start.44 = (bf16[2,64,2048]{2,1,0:T(8,128)(2,1)S(1)}, bf16[2,64,2048]{2,1,0:T(8,128)(2,1)S(1)}, u32[]{:S(2)}, u32[]{:S(2)}) collective-permute-start(bf16[2,64,2048]{2,1,0:T(8,128)(2,1)S(1)} %bitcast.443), channel_id=1, source_target_pairs={{0,3},{1,2},{2,1},{3,0},{4,7},{5,6},{6,5},{7,4},{8,11},{9,10},{10,... | collective-permute-start | bytes 1572872 | tf_op jit(solution)/shard_map/ppermute | solution.py:37
  658.1 285.8 %reduce-scatter.5.cloned.1.call-start = ((), (), s32[]{:S(2)}) async-start(), calls=%async_computation.7 | async-start | bytes 14155776 | tf_op jit(solution)/shard_map/reduce_scatter | solution.py:771
  658.2 46.4 %collective-permute-start.41 = (bf16[384,2048]{1,0:T(8,128)(2,1)}, bf16[384,2048]{1,0:T(8,128)(2,1)S(1)}, u32[]{:S(2)}, u32[]{:S(2)}) collective-permute-start(bf16[384,2048]{1,0:T(8,128)(2,1)} %add_convert_fusion.5), channel_id=1, source_target_pairs={{0,8},{4,12},{8,0},{12,4},{16,24},{20,28},{24,16},{28,20},{1,9},{5... | collective-permute-start | bytes 4718600 | tf_op jit(solution)/shard_map/ppermute | solution.py:37
  716.9 49.2 %collective-permute-start.49 = (bf16[256,4224]{1,0:T(8,128)(2,1)S(1)}, bf16[256,4224]{1,0:T(8,128)(2,1)S(1)}, u32[]{:S(2)}, u32[]{:S(2)}) collective-permute-start(bf16[256,4224]{1,0:T(8,128)(2,1)S(1)} %copy-done.97), channel_id=1, source_target_pairs={{0,16},{4,20},{8,24},{12,28},{16,0},{20,4},{24,8},{28,12},{1,17},{... | collective-permute-start | bytes 6488072 | tf_op jit(solution)/shard_map/ppermute | solution.py:37
  792.2 142.7 %collective-permute-start.54 = (bf16[512,4224]{1,0:T(8,128)(2,1)}, bf16[512,4224]{1,0:T(8,128)(2,1)}, u32[]{:S(2)}, u32[]{:S(2)}) collective-permute-start(bf16[512,4224]{1,0:T(8,128)(2,1)} %add_convert_fusion), channel_id=1, source_target_pairs={{0,8},{4,12},{8,0},{12,4},{16,24},{20,28},{24,16},{28,20},{1,9},{5... | collective-permute-start | bytes 12976136 | tf_op jit(solution)/shard_map/ppermute | solution.py:37
  794.8 61.5 %collective-permute-start.53 = (bf16[256,4224]{1,0:T(8,128)(2,1)S(1)}, bf16[256,4224]{1,0:T(8,128)(2,1)}, u32[]{:S(2)}, u32[]{:S(2)}) collective-permute-start(bf16[256,4224]{1,0:T(8,128)(2,1)S(1)} %copy-done.96), channel_id=1, source_target_pairs={{0,16},{4,20},{8,24},{12,28},{16,0},{20,4},{24,8},{28,12},{1,17},{... | collective-permute-start | bytes 6488072 | tf_op jit(solution)/shard_map/ppermute | solution.py:37
  796.8 38.8 %collective-permute-start.51 = (bf16[2,64,2176]{2,1,0:T(8,128)(2,1)S(1)}, bf16[2,64,2176]{2,1,0:T(8,128)(2,1)S(1)}, u32[]{:S(2)}, u32[]{:S(2)}) collective-permute-start(bf16[2,64,2176]{2,1,0:T(8,128)(2,1)S(1)} %get-tuple-element.226), channel_id=1, source_target_pairs={{0,2},{1,3},{2,0},{3,1},{4,6},{5,7},{6,4},{7,5},{8,10},{9,11},{10,... | collective-permute-start | bytes 1671176 | tf_op jit(solution)/shard_map/ppermute | solution.py:37
  796.8 38.8 %collective-permute-start.50 = (bf16[2,64,2176]{2,1,0:T(8,128)(2,1)S(1)}, bf16[2,64,2176]{2,1,0:T(8,128)(2,1)S(1)}, u32[]{:S(2)}, u32[]{:S(2)}) collective-permute-start(bf16[2,64,2176]{2,1,0:T(8,128)(2,1)S(1)} %get-tuple-element.224), channel_id=1, source_target_pairs={{0,1},{1,0},{2,3},{3,2},{4,5},{5,4},{6,7},{7,6},{8,9},{9,8},{10,11... | collective-permute-start | bytes 1671176 | tf_op jit(solution)/shard_map/ppermute | solution.py:37
  861.5 82.5 %all-to-all-start.1 = ((bf16[8,48,2048]{2,1,0:T(8,128)(2,1)}), bf16[8,48,2048]{2,1,0:T(8,128)(2,1)S(1)}, u32[]{:S(2)}, u32[]{:S(2)}) async-start(bf16[8,48,2048]{2,1,0:T(8,128)(2,1)} %pad_maximum_fusion.11), calls=%async_computation.1 | async-start | bytes 3145728 | tf_op jit(solution)/shard_map/all_to_all | solution.py:796
  945.5 39.3 %collective-permute-start.59 = (f32[16,2048]{1,0:T(8,128)S(1)}, f32[16,2048]{1,0:T(8,128)S(1)}, u32[]{:S(2)}, u32[]{:S(2)}) collective-permute-start(f32[16,2048]{1,0:T(8,128)S(1)} %dynamic_update_slice.134), channel_id=1, source_target_pairs={{0,2},{1,3},{2,0},{3,1},{4,6},{5,7},{6,4},{7,5},{8,10},{9,11},{10,... | collective-permute-start | bytes 393224 | tf_op jit(solution)/shard_map/ppermute | solution.py:37
  (145 other events, 2168.8 us)
Sparse Core Ops, SparseCore 0:
  84.4 78.6 all-gather.2
  165.6 84.6 all-gather.4
  658.2 96.3 reduce-scatter.2
  791.1 140.7 reduce-scatter.4

commit v10 on v9

--- a/solution.py
+++ b/solution.py
@@ -551,7 +551,7 @@
     late_pair = after((keep_pair[1], send_pair[1], side_first), joint_full)
     keep_second = [swap(late_pair[0], "dp", step) for step in line_steps]
     side_second = swap(late_pair[1], "dp", 2)
-    first_lines = [swap(after(late_pair[2], out_full), "dp", step) for step in line_steps]
+    first_lines = [swap(late_pair[2], "dp", step) for step in line_steps]
     second_lines = [swap(side_second, "dp", step) for step in line_steps]
     firsts, seconds = [keep_pair[0], side_first], [keep_pair[1], side_second]
     for line in range(lines - 1):
@@ -690,24 +690,22 @@
 
     def block_grads(steps, *others):
         rows = after((hidden_near, hidden_far, grad_near, grad_far), *others)
-        cuts = (2, 1, 1) * (len(steps) // 2)
+        cuts = (2,) * len(steps)
         return expert_grads([chip ^ k for k in steps], cuts, chip_rows, rows, joint_grads, actives)
 
     hidden_sum, hidden_far_sum = quad_sums(hidden_parts)
     ffn_sum, ffn_far_sum = quad_sums(ffn_parts)
     line_grads = block_grads([k ^ 1 for k in range(2, chips)], hidden_far_sum)
-    side_got = [swap(line_grads[3 * line], "dp", step) for line, step in enumerate(line_steps)]
-    keep_got = []
-    for part in range(2):
-        blocks = after(line_grads[part + 1 :: 3], side_got, keep_got)
-        keep_got.append([swap(block, "dp", step) for block, step in zip(blocks, line_steps)])
+    side_got = [swap(line_grads[2 * line], "dp", step) for line, step in enumerate(line_steps)]
+    blocks = after(line_grads[1::2], side_got)
+    keep_got = [swap(block, "dp", step) for block, step in zip(blocks, line_steps)]
     hidden_got, ffn_far_sum, ffn_sum = lax.optimization_barrier(
         (swap(hidden_far_sum, "dp", 2), ffn_far_sum, ffn_sum, line_grads)
     )[:3]
     hidden_sum = hidden_sum + hidden_got.astype(f32)
     own_grads = block_grads([1, 0], hidden_sum)
     back_packed = return_packed(hidden_sum, *own_grads)
-    ffn_sum = ffn_sum + swap(after(ffn_far_sum, back_packed), "dp", 2).astype(f32)
+    ffn_sum = ffn_sum + swap(after(ffn_far_sum, hidden_got), "dp", 2).astype(f32)
 
     def total(own, got):
         return functools.reduce(jnp.add, [part.astype(f32) for part in [own] + got]).astype(bf16)
@@ -727,7 +725,9 @@
     gain_two_grad = jnp.sum(hidden_two_grad * normed_two, axis=0)
     resid_grad = dy_home + norm_back(hidden_two_grad * gain_two, normed_two, scale_two)
 
-    resid_grad_all = after(gather_rows(resid_grad.astype(bf16)), side_got)
+    resid_grad_all, ffn_sum = lax.optimization_barrier(
+        (gather_rows(resid_grad.astype(bf16)), ffn_sum, side_got)
+    )[:2]
     out_part = t_dot(resid_grad_all, gated_vals).astype(bf16)
     vals_grad = after(dot(resid_grad_all, out_full), out_part)
     side_own = after((own_grads[0], side_got), vals_grad)
@@ -740,18 +740,18 @@
         own_heads, group_rows,
     )
     query_grad, key_grad, value_grad, slot_part_one = lax.optimization_barrier(
-        (query_grad, key_grad, value_grad, slot_part_one, ffn_packed, keep_got[0])
+        (query_grad, key_grad, value_grad, slot_part_one, ffn_packed)
     )[:4]
     kv_grad = jnp.concatenate([key_grad, value_grad], axis=1)
     hidden_one_part = dot_t(query_grad, query_full) + dot_t(kv_grad, kv_full)
-    hidden_one_part = hidden_one_part.astype(bf16)
+    hidden_one_part, keep_got = lax.optimization_barrier((hidden_one_part.astype(bf16), keep_got))
     joint_part_grad = t_dot(
         after(hidden_one, hidden_one_part), jnp.concatenate([query_grad, kv_grad], axis=1)
     ).astype(bf16)
     back_one = scatter_rows(
         jnp.concatenate([hidden_one_part, slot_part_one.astype(bf16)], axis=1)
     )
-    back_one, keep_got = lax.optimization_barrier((back_one, keep_got, joint_part_grad))[:2]
+    back_one, other_sum = lax.optimization_barrier((back_one, other_sum, joint_part_grad))[:2]
     hidden_one_grad, slot_one_grad = back_one[:, :width], back_one[:, width : width + slots]
 
     def own(value):
@@ -770,7 +770,9 @@
     def reduced(value):
         return lax.psum_scatter(value, "dp", scatter_dimension=0, tiled=True)
 
-    in_low = in_home.astype(bf16)
+    in_low, keep_got, other_sum = lax.optimization_barrier(
+        (in_home.astype(bf16), keep_got, other_sum)
+    )
     out_grad = slots_of(after(reduced(out_part), in_low))
     joint_own = reduced(joint_part_grad)
 
@@ -794,9 +796,7 @@
     small = jnp.broadcast_to(small[None], (dp_count,) + small.shape)
     results = jnp.concatenate([results, small], axis=1)
     results = lax.all_to_all(results, "dp", split_axis=0, concat_axis=0, tiled=True)
-    results, keep_got, other_sum, out_grad, joint_own = lax.optimization_barrier(
-        (results, keep_got, other_sum, out_grad, joint_own)
-    )
+    results, out_grad, joint_own = lax.optimization_barrier((results, out_grad, joint_own))
     query_own, kv_own = joint_own[:, :query_width], joint_own[:, query_width:]
     small = results[:, sent_back:].astype(f32)
     results = results[:, :sent_back].reshape(dp_count, 2 * micro, piece_rows, width)
@@ -814,7 +814,7 @@
         smalls = [left + right for left, right in zip(smalls[::2], smalls[1::2])]
     sums = smalls[0][:sum_rows]
 
-    keep_sums = [total(own_grads[1 + part], keep_got[part]) for part in range(2)]
+    keep_sums = total(own_grads[1], keep_got).reshape(2, shard_rows, 3 * quarter)
     other_sums = other_sum.reshape(2, shard_rows, 3 * quarter)
     by_rows = [jnp.stack([keep_sums[part], other_sums[part]]) for part in range(2)]
     own_pair = jnp.where(core == 0, by_rows[0], by_rows[1])

time: 1040 us -> 964 us (0.927)
  waiting for transfers between devices: 497 us -> 425 us
  starting transfers between devices: 93.2 us -> 81.8 us
  other arithmetic: 86.4 us -> 97 us
    ppermute x63 -> x62, waiting for transfers between devices: 398 us -> 364 us  [swap(): return lax.ppermute(value, axis, [(i, i ^ step) for i in range(count)])]
    all_gather x1, waiting for transfers between devices: 66.4 us -> 38.5 us  [local(): out_full = lax.all_gather(second_own, 'dp', axis=0, tiled=True)]
    ppermute x63 -> x62, starting transfers between devices: 73.5 us -> 62.6 us  [swap(): return lax.ppermute(value, axis, [(i, i ^ step) for i in range(count)])]
    unnamed x230 -> x200, local copies, waits for them, and re-layouts: 26.8 us -> 27.9 us
  transfers between devices with their start and end apart: 73 -> 72, of which waited for: 33 -> 32; matrix products, arithmetic and copies ran while one was open for 20% -> 24% of each run, Pallas kernels for 16% -> 17%
where the time goes in v10:
time: 964 us; the launch traced here: 957 us
  waiting for transfers between devices  425 us (44%)
  Pallas kernels  167 us (17%)
  other arithmetic  97 us (10%)
  local copies, waits for them, and re-layouts  93.8 us (10%)
  starting transfers between devices  81.8 us (8%)
  matrix products  74.5 us (8%)
  between operations  17.1 us (2%)
    ppermute x62, waiting for transfers between devices, swap(): return lax.ppermute(value, axis, [(i, i ^ step) for i in range(count)])  364 us
    pallas_call x2, Pallas kernels, expert_rows(): pl.pallas_call(expert_kernel, grid_spec=pltpu.PrefetchScalarGridSpec(num_...  81.9 us
    ppermute x62, starting transfers between devices, swap(): return lax.ppermute(value, axis, [(i, i ^ step) for i in range(count)])  62.6 us
    pallas_call x2, Pallas kernels, expert_grads(): pl.pallas_call(functools.partial(expert_grad_kernel, cuts), grid_spec=plt...  49.9 us
    all_gather x1, waiting for transfers between devices, local(): out_full = lax.all_gather(second_own, 'dp', axis=0, tiled=True)  38.5 us
    unnamed x200, local copies, waits for them, and re-layouts  27.9 us
    dot_general x5, matrix products, dot(): return jnp.dot(left, right, preferred_element_type=f32)  23.5 us
    dot_general x5, matrix products, dot_t(): lax.dot_general(left, right, (((1,), (1,)), ((), ())), preferred_element_...  21.5 us
  transfers between devices with their start and end apart: 72, of which 32 were waited for; matrix products, arithmetic and copies ran while one was open for 24% of the time, Pallas kernels for 17%

profile of v10, /device:TPU:8, one launch (start us, length us, event | category | flops | bytes accessed | tf_op | source)
XLA Modules:
  0.0 956.6 jit_solution(1735102144442063456)
XLA Ops:
  38.3 14.2 %collective-permute-done.8 = bf16[256,1024]{1,0:T(8,128)(2,1)} collective-permute-done((bf16[256,1024]{1,0:T(8,128)(2,1)}, bf16[256,1024]{1,0:T(8,128)(2,1)}, u32[]{:S(2)}, u32[]{:S(2)}) %collective-permute-start.8) | collective-permute-done | bytes 524320 | tf_op jit(solution)/shard_map/ppermute | solution.py:37
  54.5 15.2 %collective-permute-done.9 = bf16[256,1024]{1,0:T(8,128)(2,1)S(1)} collective-permute-done((bf16[256,1024]{1,0:T(8,128)(2,1)}, bf16[256,1024]{1,0:T(8,128)(2,1)S(1)}, u32[]{:S(2)}, u32[]{:S(2)}) %collective-permute-start.9) | collective-permute-done | bytes 524320 | tf_op jit(solution)/shard_map/ppermute | solution.py:37
  69.8 12.0 %collective-permute-done.10 = bf16[256,1024]{1,0:T(8,128)(2,1)S(1)} collective-permute-done((bf16[256,1024]{1,0:T(8,128)(2,1)}, bf16[256,1024]{1,0:T(8,128)(2,1)S(1)}, u32[]{:S(2)}, u32[]{:S(2)}) %collective-permute-start.10) | collective-permute-done | bytes 524320 | tf_op jit(solution)/shard_map/ppermute | solution.py:37
  97.6 19.0 %all-to-all-done = bf16[8,4,8,2048]{3,2,1,0:T(8,128)(2,1)S(1)} async-done(((bf16[8,4,8,2048]{3,2,1,0:T(8,128)(2,1)}), bf16[8,4,8,2048]{3,2,1,0:T(8,128)(2,1)S(1)}, u32[]{:S(2)}, u32[]{:S(2)}) %all-to-all-start) | async-done | bytes 1048608 | tf_op jit(solution)/shard_map/all_to_all | solution.py:476
  125.4 14.3 %collective-permute-done.5 = bf16[2,64,2048]{2,1,0:T(8,128)(2,1)S(1)} collective-permute-done((bf16[2,64,2048]{2,1,0:T(8,128)(2,1)S(1)}, bf16[2,64,2048]{2,1,0:T(8,128)(2,1)S(1)}, u32[]{:S(2)}, u32[]{:S(2)}) %collective-permute-start.5) | collective-permute-done | bytes 524320 | tf_op jit(solution)/shard_map/ppermute | solution.py:37
  139.7 18.0 %collective-permute-done.6 = bf16[2,64,2048]{2,1,0:T(8,128)(2,1)S(1)} collective-permute-done((bf16[2,64,2048]{2,1,0:T(8,128)(2,1)S(1)}, bf16[2,64,2048]{2,1,0:T(8,128)(2,1)S(1)}, u32[]{:S(2)}, u32[]{:S(2)}) %collective-permute-start.6) | collective-permute-done | bytes 524320 | tf_op jit(solution)/shard_map/ppermute | solution.py:37
  157.8 13.5 %collective-permute-done.7 = bf16[2,64,2048]{2,1,0:T(8,128)(2,1)S(1)} collective-permute-done((bf16[2,64,2048]{2,1,0:T(8,128)(2,1)S(1)}, bf16[2,64,2048]{2,1,0:T(8,128)(2,1)S(1)}, u32[]{:S(2)}, u32[]{:S(2)}) %collective-permute-start.7) | collective-permute-done | bytes 524320 | tf_op jit(solution)/shard_map/ppermute | solution.py:37
  195.3 15.2 %attention_forward.1 = (bf16[512,2048]{1,0:T(8,128)(2,1)S(1)}, bf16[512,2048]{1,0:T(8,128)(2,1)}, bf16[512,2048]{1,0:T(8,128)(2,1)}, bf16[512,512]{1,0:T(8,128)(...) custom-call(s32[2]{0:T(128)S(1)} %fusion.131.lens, f32[512,2048]{1,0:T(8,128)} %fusion.2.query, ...), custom_call_target="tpu_custom_call" | custom-call | flops 1073741824 | bytes 14680064 | tf_op jit(solution)/shard_map/attention_forward/pallas_call | solution.py:181
  211.8 38.5 %all-gather.5.cloned.1.call-done = bf16[2048,2048]{1,0:T(8,128)(2,1)} async-done(((bf16[256,2048]{1,0:T(8,128)(2,1)}), bf16[2048,2048]{1,0:T(8,128)(2,1)}) %all-gather.5.cloned.1.call-update) | async-done | bytes 8388624 | tf_op jit(solution)/shard_map/all_gather | solution.py:550
  250.4 7.6 fusion.175
  275.1 23.9 %collective-permute-done.17 = bf16[2,64,2048]{2,1,0:T(8,128)(2,1)} collective-permute-done((bf16[2,64,2048]{2,1,0:T(8,128)(2,1)}, bf16[2,64,2048]{2,1,0:T(8,128)(2,1)}, u32[]{:S(2)}, u32[]{:S(2)}) %collective-permute-start.17) | collective-permute-done | bytes 524320 | tf_op jit(solution)/shard_map/ppermute | solution.py:37
  299.0 9.3 collective-permute-done.16
  322.9 25.6 %collective-permute-done.21 = bf16[2,48,2176]{2,1,0:T(8,128)(2,1)S(1)} collective-permute-done((bf16[2,48,2176]{2,1,0:T(8,128)(2,1)S(1)}, bf16[2,48,2176]{2,1,0:T(8,128)(2,1)S(1)}, u32[]{:S(2)}, u32[]{:S(2)}) %collective-permute-start.21) | collective-permute-done | bytes 417824 | tf_op jit(solution)/shard_map/ppermute | solution.py:37
  366.0 41.0 %expert_rows.2 = (bf16[768,2048]{1,0:T(8,128)(2,1)}, bf16[768,2176]{1,0:T(8,128)(2,1)}, bf16[768,1408]{1,0:T(8,128)(2,1)}, bf16[768,2816]{1,0:T(8,128)(2,1)}) custom-call(s32[2]{0:T(128)} %pad_add_fusion.1.place_ref, bf16[768,2176]{1,0:T(8,128)(2,1)} %pad_maximum_fusion.2.hidden.refs_0_.refs_4_, bf16[768,2048]{1,0:T(8,128)(2,1)} %copy-done.46, ...), custom_call_target="tpu_custom_call" | custom-call | flops 26575110144 | bytes 36175872 | tf_op jit(solution)/shard_map/expert_rows/pallas_call | solution.py:332
  413.1 40.9 %expert_rows.3 = (bf16[768,2048]{1,0:T(8,128)(2,1)}, bf16[768,2176]{1,0:T(8,128)(2,1)}, bf16[768,1408]{1,0:T(8,128)(2,1)}, bf16[768,2816]{1,0:T(8,128)(2,1)}) custom-call(s32[2]{0:T(128)} %pad_add_fusion.1.place_ref, bf16[768,2176]{1,0:T(8,128)(2,1)} %constant_dynamic-update-slice_fusion.4.hidden.refs_1_.refs_5_, bf16[768,2048]{1,0:T(8,128)(2,1)} %copy-done.45, ...), custom_call_target="tpu_custom_call" | custom-call | flops 26575110144 | bytes 36175872 | tf_op jit(solution)/shard_map/expert_rows/pallas_call | solution.py:332
  472.3 25.0 %expert_grads.2 = (bf16[512,4224]{1,0:T(8,128)(2,1)}, bf16[512,4224]{1,0:T(8,128)(2,1)}) custom-call(s32[4]{0:T(128)} %get-tuple-element.296.order, bf16[768,2176]{1,0:T(8,128)(2,1)} %pad_maximum_fusion.2.hidden.refs_0_.refs_4_, bf16[768,2176]{1,0:T(8,128)(2,1)} %constant_dynamic-update-slice_fusion.4.hidden.refs_1_.refs_5_, bf16[768,2048]{1,0:T(8,128)(2,1)} %copy-done.46, ...), custom_call_target="tpu_custom_call" | custom-call | flops 13287555072 | bytes 27918336 | tf_op jit(solution)/shard_map/expert_grads/pallas_call | solution.py:405
  498.5 10.4 %collective-permute-done.35 = bf16[384,2176]{1,0:T(8,128)(2,1)} collective-permute-done((bf16[384,2176]{1,0:T(8,128)(2,1)}, bf16[384,2176]{1,0:T(8,128)(2,1)}, u32[]{:S(2)}, u32[]{:S(2)}) %collective-permute-start.35) | collective-permute-done | bytes 1671200 | tf_op jit(solution)/shard_map/ppermute | solution.py:37
  517.0 25.0 %expert_grads.3 = (bf16[512,4224]{1,0:T(8,128)(2,1)}, bf16[512,4224]{1,0:T(8,128)(2,1)}) custom-call(s32[4]{0:T(128)} %get-tuple-element.297.order, bf16[768,2176]{1,0:T(8,128)(2,1)} %pad_maximum_fusion.2.hidden.refs_0_.refs_4_, bf16[768,2176]{1,0:T(8,128)(2,1)} %constant_dynamic-update-slice_fusion.4.hidden.refs_1_.refs_5_, bf16[768,2048]{1,0:T(8,128)(2,1)} %copy-done.46, ...), custom_call_target="tpu_custom_call" | custom-call | flops 13287555072 | bytes 27918336 | tf_op jit(solution)/shard_map/expert_grads/pallas_call | solution.py:405
  543.2 9.2 collective-permute-done.40
  577.7 15.6 %collective-permute-done.41 = bf16[2,64,2048]{2,1,0:T(8,128)(2,1)S(1)} collective-permute-done((bf16[2,64,2048]{2,1,0:T(8,128)(2,1)S(1)}, bf16[2,64,2048]{2,1,0:T(8,128)(2,1)S(1)}, u32[]{:S(2)}, u32[]{:S(2)}) %collective-permute-start.41) | collective-permute-done | bytes 524320 | tf_op jit(solution)/shard_map/ppermute | solution.py:37
  593.3 17.4 %collective-permute-done.42 = bf16[2,64,2048]{2,1,0:T(8,128)(2,1)S(1)} collective-permute-done((bf16[2,64,2048]{2,1,0:T(8,128)(2,1)S(1)}, bf16[2,64,2048]{2,1,0:T(8,128)(2,1)S(1)}, u32[]{:S(2)}, u32[]{:S(2)}) %collective-permute-start.42) | collective-permute-done | bytes 524320 | tf_op jit(solution)/shard_map/ppermute | solution.py:37
  610.8 10.4 %collective-permute-done.43 = bf16[2,64,2048]{2,1,0:T(8,128)(2,1)S(1)} collective-permute-done((bf16[2,64,2048]{2,1,0:T(8,128)(2,1)S(1)}, bf16[2,64,2048]{2,1,0:T(8,128)(2,1)S(1)}, u32[]{:S(2)}, u32[]{:S(2)}) %collective-permute-start.43) | collective-permute-done | bytes 524320 | tf_op jit(solution)/shard_map/ppermute | solution.py:37
  632.2 11.4 %fusion.177.vals_grad = f32[512,2048]{1,0:T(8,128)} fusion(bf16[512,2048]{1,0:T(8,128)(2,1)} %bitcast.430, bf16[2048,2048]{1,0:T(8,128)(2,1)} %all-gather.5.cloned.1.call-done), kind=kOutput, calls=%fused_computation.453 | convolution fusion | flops 4294967296 | bytes 14680064 | tf_op jit(solution)/shard_map/dot_general | solution.py:24
  643.7 7.5 add_convert_fusion.1
  656.4 20.1 %attention_backward.1 = (bf16[512,2048]{1,0:T(8,128)(2,1)S(1)}, bf16[512,512]{1,0:T(8,128)(2,1)S(1)}, bf16[512,512]{1,0:T(8,128)(2,1)S(1)}, f32[512,128]{1,0:T(8,128)S(1)}) custom-call(s32[2]{0:T(128)S(1)} %fusion.131.lens, bf16[512,2048]{1,0:T(8,128)(2,1)} %get-tuple-element.148.query, bf16[512,512]{1,0:T(8,128)(2,1)S(1)} %get-tuple-element.149.key, ...), custom_call_target="tpu_custom_call" | custom-call | flops 2684354560 | bytes 14680064 | tf_op jit(solution)/shard_map/attention_backward/pallas_call | solution.py:212
  692.3 8.1 add_convert_fusion.2
  700.4 69.4 %collective-permute-done.49 = bf16[512,4224]{1,0:T(8,128)(2,1)} collective-permute-done((bf16[512,4224]{1,0:T(8,128)(2,1)}, bf16[512,4224]{1,0:T(8,128)(2,1)}, u32[]{:S(2)}, u32[]{:S(2)}) %collective-permute-start.49) | collective-permute-done | bytes 4325408 | tf_op jit(solution)/shard_map/ppermute | solution.py:37
  775.8 9.9 %convolution_convert_fusion = bf16[2048,3072]{1,0:T(8,128)(2,1)} fusion(bf16[512,2048]{1,0:T(8,128)(2,1)S(1)} %bitcast.414, bf16[512,512]{1,0:T(8,128)(2,1)S(1)} %get-tuple-element.158, bf16[512,512]{1,0:T(8,128)(2,1)S(1)} %get-tuple-element.157, bf16[512,2048]{1,0:T(8,128)(2,1)S(1)} %get-tuple-element.156), kind=kOutput, calls=%fused_computation | convolution fusion | flops 6458179584 | bytes 17825792 | tf_op jit(solution)/shard_map/dot_general | solution.py:32
  785.8 10.5 %collective-permute-done.52 = bf16[2,64,2176]{2,1,0:T(8,128)(2,1)S(1)} collective-permute-done((bf16[2,64,2176]{2,1,0:T(8,128)(2,1)}, bf16[2,64,2176]{2,1,0:T(8,128)(2,1)S(1)}, u32[]{:S(2)}, u32[]{:S(2)}) %collective-permute-start.52) | collective-permute-done | bytes 557088 | tf_op jit(solution)/shard_map/ppermute | solution.py:37
  796.3 9.8 %collective-permute-done.51 = bf16[2,64,2176]{2,1,0:T(8,128)(2,1)S(1)} collective-permute-done((bf16[2,64,2176]{2,1,0:T(8,128)(2,1)S(1)}, bf16[2,64,2176]{2,1,0:T(8,128)(2,1)S(1)}, u32[]{:S(2)}, u32[]{:S(2)}) %collective-permute-start.51) | collective-permute-done | bytes 557088 | tf_op jit(solution)/shard_map/ppermute | solution.py:37
  859.3 8.6 convert_element_type.337
  870.6 17.0 %collective-permute-done.55 = bf16[256,512]{1,0:T(8,128)(2,1)S(1)} collective-permute-done((bf16[256,512]{1,0:T(8,128)(2,1)S(1)}, bf16[256,512]{1,0:T(8,128)(2,1)S(1)}, u32[]{:S(2)}, u32[]{:S(2)}) %collective-permute-start.55) | collective-permute-done | bytes 262176 | tf_op jit(solution)/shard_map/ppermute | solution.py:37
  (589 shorter events, 346.0 us)
Async XLA Ops:
  7.2 168.8 %all-gather.3.cloned.1.call-start = ((), (), s32[]{:S(2)}) async-start(), calls=%async_computation.4 | async-start | bytes 14155776 | tf_op jit(solution)/shard_map/all_gather | solution.py:549
  14.9 69.4 %collective-permute-start.1 = (bf16[256,4224]{1,0:T(8,128)(2,1)}, bf16[256,4224]{1,0:T(8,128)(2,1)}, u32[]{:S(2)}, u32[]{:S(2)}) collective-permute-start(bf16[256,4224]{1,0:T(8,128)(2,1)} %pad_maximum_fusion.5), channel_id=1, source_target_pairs={{0,8},{4,12},{8,0},{12,4},{16,24},{20,28},{24,16},{28,20},{1,9},{5... | collective-permute-start | bytes 6488072 | tf_op jit(solution)/shard_map/ppermute | solution.py:37
  17.9 66.4 %collective-permute-start.3 = (bf16[256,4224]{1,0:T(8,128)(2,1)}, bf16[256,4224]{1,0:T(8,128)(2,1)}, u32[]{:S(2)}, u32[]{:S(2)}) collective-permute-start(bf16[256,4224]{1,0:T(8,128)(2,1)} %pad_maximum_fusion.4), channel_id=1, source_target_pairs={{0,16},{4,20},{8,24},{12,28},{16,0},{20,4},{24,8},{28,12},{1,17},{... | collective-permute-start | bytes 6488072 | tf_op jit(solution)/shard_map/ppermute | solution.py:37
  35.6 46.1 %collective-permute-start.10 = (bf16[256,1024]{1,0:T(8,128)(2,1)}, bf16[256,1024]{1,0:T(8,128)(2,1)S(1)}, u32[]{:S(2)}, u32[]{:S(2)}) collective-permute-start(bf16[256,1024]{1,0:T(8,128)(2,1)} %pad_maximum_fusion.15), channel_id=1, source_target_pairs={{0,3},{1,2},{2,1},{3,0},{4,7},{5,6},{6,5},{7,4},{8,11},{9,10},{10,... | collective-permute-start | bytes 1572872 | tf_op jit(solution)/shard_map/ppermute | solution.py:37
  84.3 166.1 %all-gather.5.cloned.1.call-start = ((), (), s32[]{:S(2)}) async-start(), calls=%async_computation.5 | async-start | bytes 9437184 | tf_op jit(solution)/shard_map/all_gather | solution.py:550
  85.0 36.3 %collective-permute-start = (bf16[256,4224]{1,0:T(8,128)(2,1)}, bf16[256,4224]{1,0:T(8,128)(2,1)}, u32[]{:S(2)}, u32[]{:S(2)}) collective-permute-start(bf16[256,4224]{1,0:T(8,128)(2,1)} %pad_maximum_fusion.4), channel_id=1, source_target_pairs={{0,4},{4,0},{8,12},{12,8},{16,20},{20,16},{24,28},{28,24},{1,5},{5... | collective-permute-start | bytes 6488072 | tf_op jit(solution)/shard_map/ppermute | solution.py:37
  90.1 762.4 %reduce-scatter.3.cloned.1.call-start = ((), (), s32[]{:S(2)}) async-start(), calls=%async_computation.6 | async-start | bytes 9437184 | tf_op jit(solution)/shard_map/reduce_scatter | solution.py:771
  121.4 36.3 %collective-permute-start.6 = (bf16[2,64,2048]{2,1,0:T(8,128)(2,1)S(1)}, bf16[2,64,2048]{2,1,0:T(8,128)(2,1)S(1)}, u32[]{:S(2)}, u32[]{:S(2)}) collective-permute-start(bf16[2,64,2048]{2,1,0:T(8,128)(2,1)S(1)} %bitcast.432), channel_id=1, source_target_pairs={{0,2},{1,3},{2,0},{3,1},{4,6},{5,7},{6,4},{7,5},{8,10},{9,11},{10,... | collective-permute-start | bytes 1572872 | tf_op jit(solution)/shard_map/ppermute | solution.py:37
  123.0 48.4 %collective-permute-start.7 = (bf16[2,64,2048]{2,1,0:T(8,128)(2,1)S(1)}, bf16[2,64,2048]{2,1,0:T(8,128)(2,1)S(1)}, u32[]{:S(2)}, u32[]{:S(2)}) collective-permute-start(bf16[2,64,2048]{2,1,0:T(8,128)(2,1)S(1)} %bitcast.433), channel_id=1, source_target_pairs={{0,3},{1,2},{2,1},{3,0},{4,7},{5,6},{6,5},{7,4},{8,11},{9,10},{10,... | collective-permute-start | bytes 1572872 | tf_op jit(solution)/shard_map/ppermute | solution.py:37
  175.9 87.6 %collective-permute-start.27 = (bf16[2,48,2048]{2,1,0:T(8,128)(2,1)}, bf16[2,48,2048]{2,1,0:T(8,128)(2,1)}, u32[]{:S(2)}, u32[]{:S(2)}) collective-permute-start(bf16[2,48,2048]{2,1,0:T(8,128)(2,1)} %get-tuple-element.246), channel_id=1, source_target_pairs={{0,3},{1,2},{2,1},{3,0},{4,7},{5,6},{6,5},{7,4},{8,11},{9,10},{10,... | collective-permute-start | bytes 1179656 | tf_op jit(solution)/shard_map/ppermute | solution.py:37
  175.9 88.8 %collective-permute-start.26 = (bf16[2,48,2048]{2,1,0:T(8,128)(2,1)}, bf16[2,48,2048]{2,1,0:T(8,128)(2,1)}, u32[]{:S(2)}, u32[]{:S(2)}) collective-permute-start(bf16[2,48,2048]{2,1,0:T(8,128)(2,1)} %get-tuple-element.247), channel_id=1, source_target_pairs={{0,2},{1,3},{2,0},{3,1},{4,6},{5,7},{6,4},{7,5},{8,10},{9,11},{10,... | collective-permute-start | bytes 1179656 | tf_op jit(solution)/shard_map/ppermute | solution.py:37
  176.1 83.1 %collective-permute-start.13 = (bf16[256,4224]{1,0:T(8,128)(2,1)}, bf16[256,4224]{1,0:T(8,128)(2,1)}, u32[]{:S(2)}, u32[]{:S(2)}) collective-permute-start(bf16[256,4224]{1,0:T(8,128)(2,1)} %get-tuple-element.98.refs_0_), channel_id=1, source_target_pairs={{0,16},{4,20},{8,24},{12,28},{16,0},{20,4},{24,8},{28,12},{1,17},{... | collective-permute-start | bytes 6488072 | tf_op jit(solution)/shard_map/ppermute | solution.py:37
  182.0 78.2 %collective-permute-start.14 = (bf16[256,4224]{1,0:T(8,128)(2,1)}, bf16[256,4224]{1,0:T(8,128)(2,1)}, u32[]{:S(2)}, u32[]{:S(2)}) collective-permute-start(bf16[256,4224]{1,0:T(8,128)(2,1)} %get-tuple-element.99), channel_id=1, source_target_pairs={{0,8},{4,12},{8,0},{12,4},{16,24},{20,28},{24,16},{28,20},{1,9},{5... | collective-permute-start | bytes 6488072 | tf_op jit(solution)/shard_map/ppermute | solution.py:37
  183.5 126.9 %collective-permute-start.18 = (bf16[256,4224]{1,0:T(8,128)(2,1)}, bf16[256,4224]{1,0:T(8,128)(2,1)}, u32[]{:S(2)}, u32[]{:S(2)}) collective-permute-start(bf16[256,4224]{1,0:T(8,128)(2,1)} %collective-permute-done.1), channel_id=1, source_target_pairs={{0,16},{4,20},{8,24},{12,28},{16,0},{20,4},{24,8},{28,12},{1,17},{... | collective-permute-start | bytes 6488072 | tf_op jit(solution)/shard_map/ppermute | solution.py:37
  261.4 37.6 %collective-permute-start.17 = (bf16[2,64,2048]{2,1,0:T(8,128)(2,1)}, bf16[2,64,2048]{2,1,0:T(8,128)(2,1)}, u32[]{:S(2)}, u32[]{:S(2)}) collective-permute-start(bf16[2,64,2048]{2,1,0:T(8,128)(2,1)} %get-tuple-element.216), channel_id=1, source_target_pairs={{0,3},{1,2},{2,1},{3,0},{4,7},{5,6},{6,5},{7,4},{8,11},{9,10},{10,... | collective-permute-start | bytes 1572872 | tf_op jit(solution)/shard_map/ppermute | solution.py:37
  263.5 44.9 %collective-permute-start.16 = (bf16[2,64,2048]{2,1,0:T(8,128)(2,1)}, bf16[2,64,2048]{2,1,0:T(8,128)(2,1)}, u32[]{:S(2)}, u32[]{:S(2)}) collective-permute-start(bf16[2,64,2048]{2,1,0:T(8,128)(2,1)} %get-tuple-element.217), channel_id=1, source_target_pairs={{0,2},{1,3},{2,0},{3,1},{4,6},{5,7},{6,4},{7,5},{8,10},{9,11},{10,... | collective-permute-start | bytes 1572872 | tf_op jit(solution)/shard_map/ppermute | solution.py:37
  264.7 43.6 %collective-permute-start.15 = (bf16[2,64,2048]{2,1,0:T(8,128)(2,1)}, bf16[2,64,2048]{2,1,0:T(8,128)(2,1)}, u32[]{:S(2)}, u32[]{:S(2)}) collective-permute-start(bf16[2,64,2048]{2,1,0:T(8,128)(2,1)} %get-tuple-element.215), channel_id=1, source_target_pairs={{0,1},{1,0},{2,3},{3,2},{4,5},{5,4},{6,7},{7,6},{8,9},{9,8},{10,11... | collective-permute-start | bytes 1572872 | tf_op jit(solution)/shard_map/ppermute | solution.py:37
  274.2 80.3 %collective-permute-start.22 = (bf16[256,4224]{1,0:T(8,128)(2,1)}, bf16[256,4224]{1,0:T(8,128)(2,1)}, u32[]{:S(2)}, u32[]{:S(2)}) collective-permute-start(bf16[256,4224]{1,0:T(8,128)(2,1)} %collective-permute-done.14.refs_1_), channel_id=1, source_target_pairs={{0,16},{4,20},{8,24},{12,28},{16,0},{20,4},{24,8},{28,12},{1,17},{... | collective-permute-start | bytes 6488072 | tf_op jit(solution)/shard_map/ppermute | solution.py:37
  314.4 39.3 %collective-permute-start.29 = (bf16[384,2048]{1,0:T(8,128)(2,1)}, bf16[384,2048]{1,0:T(8,128)(2,1)}, u32[]{:S(2)}, u32[]{:S(2)}) collective-permute-start(bf16[384,2048]{1,0:T(8,128)(2,1)} %bitcast.419), channel_id=1, source_target_pairs={{0,8},{4,12},{8,0},{12,4},{16,24},{20,28},{24,16},{28,20},{1,9},{5... | collective-permute-start | bytes 4718600 | tf_op jit(solution)/shard_map/ppermute | solution.py:37
  356.9 50.2 %collective-permute-start.32 = (bf16[384,2176]{1,0:T(8,128)(2,1)S(1)}, bf16[384,2176]{1,0:T(8,128)(2,1)S(1)}, u32[]{:S(2)}, u32[]{:S(2)}) collective-permute-start(bf16[384,2176]{1,0:T(8,128)(2,1)S(1)} %bitcast.417), channel_id=1, source_target_pairs={{0,8},{4,12},{8,0},{12,4},{16,24},{20,28},{24,16},{28,20},{1,9},{5... | collective-permute-start | bytes 5013512 | tf_op jit(solution)/shard_map/ppermute | solution.py:37
  410.3 52.9 %collective-permute-start.37 = (bf16[384,2048]{1,0:T(8,128)(2,1)}, bf16[384,2048]{1,0:T(8,128)(2,1)}, u32[]{:S(2)}, u32[]{:S(2)}) collective-permute-start(bf16[384,2048]{1,0:T(8,128)(2,1)} %split.31), channel_id=1, source_target_pairs={{0,4},{4,0},{8,12},{12,8},{16,20},{20,16},{24,28},{28,24},{1,5},{5... | collective-permute-start | bytes 4718600 | tf_op jit(solution)/shard_map/ppermute | solution.py:37
  462.8 46.2 %collective-permute-start.31 = (bf16[384,2176]{1,0:T(8,128)(2,1)}, bf16[384,2176]{1,0:T(8,128)(2,1)}, u32[]{:S(2)}, u32[]{:S(2)}) collective-permute-start(bf16[384,2176]{1,0:T(8,128)(2,1)} %split.25), channel_id=1, source_target_pairs={{0,4},{4,0},{8,12},{12,8},{16,20},{20,16},{24,28},{28,24},{1,5},{5... | collective-permute-start | bytes 5013512 | tf_op jit(solution)/shard_map/ppermute | solution.py:37
  470.2 38.8 %collective-permute-start.35 = (bf16[384,2176]{1,0:T(8,128)(2,1)}, bf16[384,2176]{1,0:T(8,128)(2,1)}, u32[]{:S(2)}, u32[]{:S(2)}) collective-permute-start(bf16[384,2176]{1,0:T(8,128)(2,1)} %add_convert_fusion.3), channel_id=1, source_target_pairs={{0,8},{4,12},{8,0},{12,4},{16,24},{20,28},{24,16},{28,20},{1,9},{5... | collective-permute-start | bytes 5013512 | tf_op jit(solution)/shard_map/ppermute | solution.py:37
  497.2 127.9 %collective-permute-start.45 = (bf16[512,4224]{1,0:T(8,128)(2,1)}, bf16[512,4224]{1,0:T(8,128)(2,1)}, u32[]{:S(2)}, u32[]{:S(2)}) collective-permute-start(bf16[512,4224]{1,0:T(8,128)(2,1)} %get-tuple-element.121), channel_id=1, source_target_pairs={{0,16},{4,20},{8,24},{12,28},{16,0},{20,4},{24,8},{28,12},{1,17},{... | collective-permute-start | bytes 12976136 | tf_op jit(solution)/shard_map/ppermute | solution.py:37
  515.2 37.2 %collective-permute-start.40 = (bf16[2,48,2176]{2,1,0:T(8,128)(2,1)S(1)}, bf16[2,48,2176]{2,1,0:T(8,128)(2,1)S(1)}, u32[]{:S(2)}, u32[]{:S(2)}) collective-permute-start(bf16[2,48,2176]{2,1,0:T(8,128)(2,1)S(1)} %bitcast.458), channel_id=1, source_target_pairs={{0,3},{1,2},{2,1},{3,0},{4,7},{5,6},{6,5},{7,4},{8,11},{9,10},{10,... | collective-permute-start | bytes 1253384 | tf_op jit(solution)/shard_map/ppermute | solution.py:37
  516.7 104.6 %collective-permute-start.44 = (bf16[384,2048]{1,0:T(8,128)(2,1)}, bf16[384,2048]{1,0:T(8,128)(2,1)}, u32[]{:S(2)}, u32[]{:S(2)}) collective-permute-start(bf16[384,2048]{1,0:T(8,128)(2,1)} %add_convert_fusion.4), channel_id=1, source_target_pairs={{0,8},{4,12},{8,0},{12,4},{16,24},{20,28},{24,16},{28,20},{1,9},{5... | collective-permute-start | bytes 4718600 | tf_op jit(solution)/shard_map/ppermute | solution.py:37
  573.9 36.8 %collective-permute-start.42 = (bf16[2,64,2048]{2,1,0:T(8,128)(2,1)S(1)}, bf16[2,64,2048]{2,1,0:T(8,128)(2,1)S(1)}, u32[]{:S(2)}, u32[]{:S(2)}) collective-permute-start(bf16[2,64,2048]{2,1,0:T(8,128)(2,1)S(1)} %bitcast.440), channel_id=1, source_target_pairs={{0,2},{1,3},{2,0},{3,1},{4,6},{5,7},{6,4},{7,5},{8,10},{9,11},{10,... | collective-permute-start | bytes 1572872 | tf_op jit(solution)/shard_map/ppermute | solution.py:37
  575.9 45.3 %collective-permute-start.43 = (bf16[2,64,2048]{2,1,0:T(8,128)(2,1)S(1)}, bf16[2,64,2048]{2,1,0:T(8,128)(2,1)S(1)}, u32[]{:S(2)}, u32[]{:S(2)}) collective-permute-start(bf16[2,64,2048]{2,1,0:T(8,128)(2,1)S(1)} %bitcast.441), channel_id=1, source_target_pairs={{0,3},{1,2},{2,1},{3,0},{4,7},{5,6},{6,5},{7,4},{8,11},{9,10},{10,... | collective-permute-start | bytes 1572872 | tf_op jit(solution)/shard_map/ppermute | solution.py:37
  632.0 261.8 %reduce-scatter.5.cloned.1.call-start = ((), (), s32[]{:S(2)}) async-start(), calls=%async_computation.7 | async-start | bytes 14155776 | tf_op jit(solution)/shard_map/reduce_scatter | solution.py:771
  643.7 126.2 %collective-permute-start.49 = (bf16[512,4224]{1,0:T(8,128)(2,1)}, bf16[512,4224]{1,0:T(8,128)(2,1)}, u32[]{:S(2)}, u32[]{:S(2)}) collective-permute-start(bf16[512,4224]{1,0:T(8,128)(2,1)} %get-tuple-element.159), channel_id=1, source_target_pairs={{0,16},{4,20},{8,24},{12,28},{16,0},{20,4},{24,8},{28,12},{1,17},{... | collective-permute-start | bytes 12976136 | tf_op jit(solution)/shard_map/ppermute | solution.py:37
  655.8 151.8 %collective-permute-start.53 = (bf16[512,4224]{1,0:T(8,128)(2,1)}, bf16[512,4224]{1,0:T(8,128)(2,1)}, u32[]{:S(2)}, u32[]{:S(2)}) collective-permute-start(bf16[512,4224]{1,0:T(8,128)(2,1)} %add_convert_fusion.1), channel_id=1, source_target_pairs={{0,8},{4,12},{8,0},{12,4},{16,24},{20,28},{24,16},{28,20},{1,9},{5... | collective-permute-start | bytes 12976136 | tf_op jit(solution)/shard_map/ppermute | solution.py:37
  832.5 61.3 %all-to-all-start.1 = ((bf16[8,48,2048]{2,1,0:T(8,128)(2,1)}), bf16[8,48,2048]{2,1,0:T(8,128)(2,1)}, u32[]{:S(2)}, u32[]{:S(2)}) async-start(bf16[8,48,2048]{2,1,0:T(8,128)(2,1)} %pad_maximum_fusion.11), calls=%async_computation.1 | async-start | bytes 3145728 | tf_op jit(solution)/shard_map/all_to_all | solution.py:798
  (130 other events, 1762.2 us)
Sparse Core Ops, SparseCore 0:
  84.4 78.6 all-gather.2
  165.6 84.7 all-gather.4
  632.1 102.8 reduce-scatter.2
  785.9 105.5 reduce-scatter.4

commit v11 on v10

--- a/solution.py
+++ b/solution.py
@@ -488,6 +488,9 @@
     parts = (1 - core, core)
     keep_pair = [quarter_of(side, part) for part in parts]
     send_pair = [quarter_of(1 - side, part) for part in parts]
+    kv_in, query_in, out_in = after(
+        (kv_weight, query_weight[0], attn_out_weight[0]), keep_pair[0], send_pair[0]
+    )
     both = both.transpose(1, 0, 2, 3).reshape(2, micro, tok_rows, width)
     deal = (dealing[:, :, None] == jnp.arange(tok_rows, dtype=jnp.int32)).astype(bf16)
     work = jnp.einsum("mtr,bmrd->bmtd", deal, both, preferred_element_type=f32)
@@ -528,7 +531,7 @@
     second_pairs += [(c, 2 * (c - half_slots)) for c in range(half_slots, slots)]
     holds_keys = col < half_slots
     even_col = col % 2 == 0
-    low_kv, high_kv = kv_weight[:, :own_width], kv_weight[:, own_width:]
+    low_kv, high_kv = kv_in[:, :own_width], kv_in[:, own_width:]
     first_got = lax.ppermute(jnp.where(holds_keys, low_kv, high_kv), "expert", first_pairs)
     second_got = lax.ppermute(jnp.where(holds_keys, high_kv, low_kv), "expert", second_pairs)
     own_kv = jnp.concatenate(
@@ -541,7 +544,7 @@
     line_steps = [4 * line for line in range(1, lines)]
     side_first = swap(send_pair[0], "dp", 2)
     keep_first = [swap(keep_pair[0], "dp", step) for step in line_steps]
-    joint_own = columns_of(query_weight[0], attn_out_weight[0])
+    joint_own = columns_of(query_in, out_in)
     first_own = jnp.concatenate([joint_own[:, :query_width], own_kv], axis=1)
     first_own, second_own = lax.optimization_barrier(
         (first_own, joint_own[:, query_width:], side_first, keep_first)
@@ -639,8 +642,8 @@
     normed_one, scale_one = normalize(x_home)
     hidden_one_home = (normed_one * gain_one).astype(bf16)
     hidden_one_raw = gather_rows(after(hidden_one_home, near_pieces[:3]))
-    hidden_one = hidden_one_raw
-    grad_sent = send_packed(after(dy_home.astype(bf16), hidden_one))
+    grad_sent = send_packed(dy_home.astype(bf16))
+    hidden_one = after(hidden_one_raw, grad_sent)
     logits_one = dot(hidden_one, attn_router)
     gates_one, matches_one, chosen_one, gate_vals_one = route_gates(
         logits_one, attn_routes.reshape(all_rows, TOP), expert_table
@@ -694,7 +697,7 @@
         return expert_grads([chip ^ k for k in steps], cuts, chip_rows, rows, joint_grads, actives)
 
     hidden_sum, hidden_far_sum = quad_sums(hidden_parts)
-    ffn_sum, ffn_far_sum = quad_sums(ffn_parts)
+    ffn_sum, ffn_far_sum = quad_sums(after(ffn_parts, hidden_far_sum))
     line_grads = block_grads([k ^ 1 for k in range(2, chips)], hidden_far_sum)
     side_got = [swap(line_grads[2 * line], "dp", step) for line, step in enumerate(line_steps)]
     blocks = after(line_grads[1::2], side_got)
@@ -744,14 +747,16 @@
     )[:4]
     kv_grad = jnp.concatenate([key_grad, value_grad], axis=1)
     hidden_one_part = dot_t(query_grad, query_full) + dot_t(kv_grad, kv_full)
-    hidden_one_part, keep_got = lax.optimization_barrier((hidden_one_part.astype(bf16), keep_got))
+    hidden_one_part = hidden_one_part.astype(bf16)
     joint_part_grad = t_dot(
         after(hidden_one, hidden_one_part), jnp.concatenate([query_grad, kv_grad], axis=1)
     ).astype(bf16)
     back_one = scatter_rows(
         jnp.concatenate([hidden_one_part, slot_part_one.astype(bf16)], axis=1)
     )
-    back_one, other_sum = lax.optimization_barrier((back_one, other_sum, joint_part_grad))[:2]
+    back_one, other_sum, keep_got = lax.optimization_barrier(
+        (back_one, other_sum, keep_got, joint_part_grad)
+    )[:3]
     hidden_one_grad, slot_one_grad = back_one[:, :width], back_one[:, width : width + slots]
 
     def own(value):
@@ -773,7 +778,7 @@
     in_low, keep_got, other_sum = lax.optimization_barrier(
         (in_home.astype(bf16), keep_got, other_sum)
     )
-    out_grad = slots_of(after(reduced(out_part), in_low))
+    out_grad = slots_of(after(reduced(out_part), back_one))
     joint_own = reduced(joint_part_grad)
 
     results = jnp.stack([out_home, in_low]).reshape(2, micro, tok_rows, width)

time: 964 us -> 963 us (level)
  waiting for transfers between devices: 425 us -> 410 us
    all_gather x1, waiting for transfers between devices: 38.5 us -> 0.01 us  [local(): out_full = lax.all_gather(second_own, 'dp', axis=0, tiled=True)]
    ppermute x62, waiting for transfers between devices: 364 us -> 393 us  [swap(): return lax.ppermute(value, axis, [(i, i ^ step) for i in range(count)])]
    unnamed x200 -> x246, local copies, waits for them, and re-layouts: 27.9 us -> 28.9 us
  transfers between devices with their start and end apart: 72 -> 72, of which waited for: 32 -> 34; matrix products, arithmetic and copies ran while one was open for 24% -> 26% of each run, Pallas kernels for 17% -> 13%
where the time goes in v11:
time: 963 us; the launch traced here: 955 us
  waiting for transfers between devices  410 us (43%)
  Pallas kernels  166 us (17%)
  local copies, waits for them, and re-layouts  103 us (11%)
  other arithmetic  101 us (10%)
  starting transfers between devices  81.1 us (8%)
  matrix products  75.8 us (8%)
  between operations  17.3 us (2%)
    ppermute x62, waiting for transfers between devices, swap(): return lax.ppermute(value, axis, [(i, i ^ step) for i in range(count)])  393 us
    pallas_call x2, Pallas kernels, expert_rows(): pl.pallas_call(expert_kernel, grid_spec=pltpu.PrefetchScalarGridSpec(num_...  81.7 us
    ppermute x62, starting transfers between devices, swap(): return lax.ppermute(value, axis, [(i, i ^ step) for i in range(count)])  61.9 us
    pallas_call x2, Pallas kernels, expert_grads(): pl.pallas_call(functools.partial(expert_grad_kernel, cuts), grid_spec=plt...  49.8 us
    unnamed x246, local copies, waits for them, and re-layouts  28.9 us
    dot_general x5, matrix products, dot(): return jnp.dot(left, right, preferred_element_type=f32)  23.7 us
    dot_general x5, matrix products, dot_t(): lax.dot_general(left, right, (((1,), (1,)), ((), ())), preferred_element_...  21.7 us
    pallas_call x1, Pallas kernels, attention_backward(): pl.pallas_call(backward_kernel, grid_spec=pltpu.PrefetchScalarGridSpec(nu...  20.1 us
  transfers between devices with their start and end apart: 72, of which 34 were waited for; matrix products, arithmetic and copies ran while one was open for 26% of the time, Pallas kernels for 13%

profile of v11, /device:TPU:8, one launch (start us, length us, event | category | flops | bytes accessed | tf_op | source)
XLA Modules:
  0.0 954.5 jit_solution(14088690339622287049)
XLA Ops:
  49.1 38.6 %collective-permute-done.12 = bf16[256,1024]{1,0:T(8,128)(2,1)S(1)} collective-permute-done((bf16[256,1024]{1,0:T(8,128)(2,1)}, bf16[256,1024]{1,0:T(8,128)(2,1)S(1)}, u32[]{:S(2)}, u32[]{:S(2)}) %collective-permute-start.12) | collective-permute-done | bytes 524320 | tf_op jit(solution)/shard_map/ppermute | solution.py:37
  104.4 16.0 %all-to-all-done = bf16[8,4,8,2048]{3,2,1,0:T(8,128)(2,1)S(1)} async-done(((bf16[8,4,8,2048]{3,2,1,0:T(8,128)(2,1)}), bf16[8,4,8,2048]{3,2,1,0:T(8,128)(2,1)S(1)}, u32[]{:S(2)}, u32[]{:S(2)}) %all-to-all-start) | async-done | bytes 1048608 | tf_op jit(solution)/shard_map/all_to_all | solution.py:476
  137.5 8.0 collective-permute-done.8
  145.4 10.9 %collective-permute-done.9 = bf16[2,48,2048]{2,1,0:T(8,128)(2,1)} collective-permute-done((bf16[2,48,2048]{2,1,0:T(8,128)(2,1)}, bf16[2,48,2048]{2,1,0:T(8,128)(2,1)}, u32[]{:S(2)}, u32[]{:S(2)}) %collective-permute-start.9) | collective-permute-done | bytes 393248 | tf_op jit(solution)/shard_map/ppermute | solution.py:37
  156.3 33.0 %collective-permute-done.10 = bf16[2,48,2048]{2,1,0:T(8,128)(2,1)} collective-permute-done((bf16[2,48,2048]{2,1,0:T(8,128)(2,1)}, bf16[2,48,2048]{2,1,0:T(8,128)(2,1)}, u32[]{:S(2)}, u32[]{:S(2)}) %collective-permute-start.10) | collective-permute-done | bytes 393248 | tf_op jit(solution)/shard_map/ppermute | solution.py:37
  198.6 12.3 %collective-permute-done.7 = bf16[2,64,2048]{2,1,0:T(8,128)(2,1)S(1)} collective-permute-done((bf16[2,64,2048]{2,1,0:T(8,128)(2,1)S(1)}, bf16[2,64,2048]{2,1,0:T(8,128)(2,1)S(1)}, u32[]{:S(2)}, u32[]{:S(2)}) %collective-permute-start.7) | collective-permute-done | bytes 524320 | tf_op jit(solution)/shard_map/ppermute | solution.py:37
  226.8 14.7 %attention_forward.1 = (bf16[512,2048]{1,0:T(8,128)(2,1)S(1)}, bf16[512,2048]{1,0:T(8,128)(2,1)}, bf16[512,2048]{1,0:T(8,128)(2,1)}, bf16[512,512]{1,0:T(8,128)(...) custom-call(s32[2]{0:T(128)S(1)} %fusion.133.lens, f32[512,2048]{1,0:T(8,128)} %fusion.2.query, ...), custom_call_target="tpu_custom_call" | custom-call | flops 1073741824 | bytes 14680064 | tf_op jit(solution)/shard_map/attention_forward/pallas_call | solution.py:181
  242.9 7.6 fusion.178
  250.6 23.0 %collective-permute-done.16.refs_2_ = bf16[256,4224]{1,0:T(8,128)(2,1)} collective-permute-done((bf16[256,4224]{1,0:T(8,128)(2,1)}, bf16[256,4224]{1,0:T(8,128)(2,1)}, u32[]{:S(2)}, u32[]{:S(2)}) %collective-permute-start.16) | collective-permute-done | bytes 2162720 | tf_op jit(solution)/shard_map/ppermute | solution.py:37
  279.4 16.3 %collective-permute-done.18 = bf16[2,64,2048]{2,1,0:T(8,128)(2,1)} collective-permute-done((bf16[2,64,2048]{2,1,0:T(8,128)(2,1)}, bf16[2,64,2048]{2,1,0:T(8,128)(2,1)}, u32[]{:S(2)}, u32[]{:S(2)}) %collective-permute-start.18) | collective-permute-done | bytes 524320 | tf_op jit(solution)/shard_map/ppermute | solution.py:37
  295.8 17.1 %collective-permute-done.19 = bf16[2,64,2048]{2,1,0:T(8,128)(2,1)} collective-permute-done((bf16[2,64,2048]{2,1,0:T(8,128)(2,1)}, bf16[2,64,2048]{2,1,0:T(8,128)(2,1)}, u32[]{:S(2)}, u32[]{:S(2)}) %collective-permute-start.19) | collective-permute-done | bytes 524320 | tf_op jit(solution)/shard_map/ppermute | solution.py:37
  312.9 10.0 %collective-permute-done.20 = bf16[2,64,2048]{2,1,0:T(8,128)(2,1)} collective-permute-done((bf16[2,64,2048]{2,1,0:T(8,128)(2,1)S(1)}, bf16[2,64,2048]{2,1,0:T(8,128)(2,1)}, u32[]{:S(2)}, u32[]{:S(2)}) %collective-permute-start.20) | collective-permute-done | bytes 524320 | tf_op jit(solution)/shard_map/ppermute | solution.py:37
  335.4 10.7 %collective-permute-done.22 = bf16[2,48,2176]{2,1,0:T(8,128)(2,1)S(1)} collective-permute-done((bf16[2,48,2176]{2,1,0:T(8,128)(2,1)S(1)}, bf16[2,48,2176]{2,1,0:T(8,128)(2,1)S(1)}, u32[]{:S(2)}, u32[]{:S(2)}) %collective-permute-start.22) | collective-permute-done | bytes 417824 | tf_op jit(solution)/shard_map/ppermute | solution.py:37
  346.1 16.7 %collective-permute-done.23 = bf16[2,48,2176]{2,1,0:T(8,128)(2,1)S(1)} collective-permute-done((bf16[2,48,2176]{2,1,0:T(8,128)(2,1)S(1)}, bf16[2,48,2176]{2,1,0:T(8,128)(2,1)S(1)}, u32[]{:S(2)}, u32[]{:S(2)}) %collective-permute-start.23) | collective-permute-done | bytes 417824 | tf_op jit(solution)/shard_map/ppermute | solution.py:37
  378.7 41.0 %expert_rows.2 = (bf16[768,2048]{1,0:T(8,128)(2,1)}, bf16[768,2176]{1,0:T(8,128)(2,1)}, bf16[768,1408]{1,0:T(8,128)(2,1)}, bf16[768,2816]{1,0:T(8,128)(2,1)}) custom-call(s32[2]{0:T(128)} %pad_add_fusion.1.place_ref, bf16[768,2176]{1,0:T(8,128)(2,1)} %pad_maximum_fusion.2.hidden.refs_0_.refs_4_, bf16[768,2048]{1,0:T(8,128)(2,1)} %copy-done.44, ...), custom_call_target="tpu_custom_call" | custom-call | flops 26575110144 | bytes 36175872 | tf_op jit(solution)/shard_map/expert_rows/pallas_call | solution.py:332
  425.6 40.7 %expert_rows.3 = (bf16[768,2048]{1,0:T(8,128)(2,1)}, bf16[768,2176]{1,0:T(8,128)(2,1)}, bf16[768,1408]{1,0:T(8,128)(2,1)}, bf16[768,2816]{1,0:T(8,128)(2,1)}) custom-call(s32[2]{0:T(128)} %pad_add_fusion.1.place_ref, bf16[768,2176]{1,0:T(8,128)(2,1)} %copy-done.42, bf16[768,2048]{1,0:T(8,128)(2,1)} %copy-done.43, ...), custom_call_target="tpu_custom_call" | custom-call | flops 26575110144 | bytes 36175872 | tf_op jit(solution)/shard_map/expert_rows/pallas_call | solution.py:332
  480.5 24.8 %expert_grads.2 = (bf16[512,4224]{1,0:T(8,128)(2,1)}, bf16[512,4224]{1,0:T(8,128)(2,1)}) custom-call(s32[4]{0:T(128)} %get-tuple-element.304.order, bf16[768,2176]{1,0:T(8,128)(2,1)} %pad_maximum_fusion.2.hidden.refs_0_.refs_4_, bf16[768,2176]{1,0:T(8,128)(2,1)} %copy-done.42, bf16[768,2048]{1,0:T(8,128)(2,1)} %copy-done.44, bf16[768,2048]{1,0:T(8,128)(2,1)} %copy-done.43, ...), custom_call_target="tpu_custom_call" | custom-call | flops 13287555072 | bytes 27918336 | tf_op jit(solution)/shard_map/expert_grads/pallas_call | solution.py:405
  525.5 25.1 %expert_grads.3 = (bf16[512,4224]{1,0:T(8,128)(2,1)}, bf16[512,4224]{1,0:T(8,128)(2,1)}) custom-call(s32[4]{0:T(128)} %get-tuple-element.305.order, bf16[768,2176]{1,0:T(8,128)(2,1)} %pad_maximum_fusion.2.hidden.refs_0_.refs_4_, bf16[768,2176]{1,0:T(8,128)(2,1)} %copy-done.42, bf16[768,2048]{1,0:T(8,128)(2,1)} %copy-done.44, bf16[768,2048]{1,0:T(8,128)(2,1)} %copy-done.43, ...), custom_call_target="tpu_custom_call" | custom-call | flops 13287555072 | bytes 27918336 | tf_op jit(solution)/shard_map/expert_grads/pallas_call | solution.py:405
  552.9 8.0 collective-permute-done.40
  586.2 15.7 %collective-permute-done.41 = bf16[2,64,2048]{2,1,0:T(8,128)(2,1)S(1)} collective-permute-done((bf16[2,64,2048]{2,1,0:T(8,128)(2,1)S(1)}, bf16[2,64,2048]{2,1,0:T(8,128)(2,1)S(1)}, u32[]{:S(2)}, u32[]{:S(2)}) %collective-permute-start.41) | collective-permute-done | bytes 524320 | tf_op jit(solution)/shard_map/ppermute | solution.py:37
  601.9 18.3 %collective-permute-done.42 = bf16[2,64,2048]{2,1,0:T(8,128)(2,1)S(1)} collective-permute-done((bf16[2,64,2048]{2,1,0:T(8,128)(2,1)S(1)}, bf16[2,64,2048]{2,1,0:T(8,128)(2,1)S(1)}, u32[]{:S(2)}, u32[]{:S(2)}) %collective-permute-start.42) | collective-permute-done | bytes 524320 | tf_op jit(solution)/shard_map/ppermute | solution.py:37
  620.2 9.1 collective-permute-done.43
  640.4 10.8 %fusion.180.vals_grad = f32[512,2048]{1,0:T(8,128)} fusion(bf16[512,2048]{1,0:T(8,128)(2,1)} %bitcast.430, bf16[2048,2048]{1,0:T(8,128)(2,1)} %all-gather.5.cloned.1.call-done), kind=kOutput, calls=%fused_computation.455 | convolution fusion | flops 4294967296 | bytes 14680064 | tf_op jit(solution)/shard_map/dot_general | solution.py:24
  651.2 8.1 add_convert_fusion.1
  666.4 20.1 %attention_backward.1 = (bf16[512,2048]{1,0:T(8,128)(2,1)S(1)}, bf16[512,512]{1,0:T(8,128)(2,1)S(1)}, bf16[512,512]{1,0:T(8,128)(2,1)S(1)}, f32[512,128]{1,0:T(8,128)S(1)}) custom-call(s32[2]{0:T(128)S(1)} %fusion.133.lens, bf16[512,2048]{1,0:T(8,128)(2,1)} %get-tuple-element.157.query, bf16[512,512]{1,0:T(8,128)(2,1)S(1)} %get-tuple-element.158.key, ...), custom_call_target="tpu_custom_call" | custom-call | flops 2684354560 | bytes 14680064 | tf_op jit(solution)/shard_map/attention_backward/pallas_call | solution.py:212
  699.6 8.2 add_convert_fusion.2
  713.8 10.1 %convolution_convert_fusion = bf16[2048,3072]{1,0:T(8,128)(2,1)} fusion(bf16[512,2048]{1,0:T(8,128)(2,1)S(1)} %bitcast.415, bf16[512,512]{1,0:T(8,128)(2,1)S(1)} %get-tuple-element.167, bf16[512,512]{1,0:T(8,128)(2,1)S(1)} %get-tuple-element.166, bf16[512,2048]{1,0:T(8,128)(2,1)S(1)} %get-tuple-element.165), kind=kOutput, calls=%fused_computation | convolution fusion | flops 6458179584 | bytes 17825792 | tf_op jit(solution)/shard_map/dot_general | solution.py:32
  728.1 22.1 %collective-permute-done.50 = bf16[2,64,2176]{2,1,0:T(8,128)(2,1)} collective-permute-done((bf16[2,64,2176]{2,1,0:T(8,128)(2,1)S(1)}, bf16[2,64,2176]{2,1,0:T(8,128)(2,1)}, u32[]{:S(2)}, u32[]{:S(2)}) %collective-permute-start.50) | collective-permute-done | bytes 557088 | tf_op jit(solution)/shard_map/ppermute | solution.py:37
  759.9 43.6 %collective-permute-done.53 = bf16[512,4224]{1,0:T(8,128)(2,1)} collective-permute-done((bf16[512,4224]{1,0:T(8,128)(2,1)}, bf16[512,4224]{1,0:T(8,128)(2,1)}, u32[]{:S(2)}, u32[]{:S(2)}) %collective-permute-start.53) | collective-permute-done | bytes 4325408 | tf_op jit(solution)/shard_map/ppermute | solution.py:37
  856.0 8.4 convert_element_type.342
  867.0 16.8 %collective-permute-done.55 = bf16[256,512]{1,0:T(8,128)(2,1)S(1)} collective-permute-done((bf16[256,512]{1,0:T(8,128)(2,1)S(1)}, bf16[256,512]{1,0:T(8,128)(2,1)S(1)}, u32[]{:S(2)}, u32[]{:S(2)}) %collective-permute-start.55) | collective-permute-done | bytes 262176 | tf_op jit(solution)/shard_map/ppermute | solution.py:37
  930.9 8.6 collective-permute-done.61
  (634 shorter events, 362.7 us)
Async XLA Ops:
  7.2 205.3 %all-gather.3.cloned.1.call-start = ((), (), s32[]{:S(2)}) async-start(), calls=%async_computation.4 | async-start | bytes 14155776 | tf_op jit(solution)/shard_map/all_gather | solution.py:552
  14.3 76.1 %collective-permute-start.1 = (bf16[256,4224]{1,0:T(8,128)(2,1)}, bf16[256,4224]{1,0:T(8,128)(2,1)}, u32[]{:S(2)}, u32[]{:S(2)}) collective-permute-start(bf16[256,4224]{1,0:T(8,128)(2,1)} %pad_maximum_fusion.5), channel_id=1, source_target_pairs={{0,8},{4,12},{8,0},{12,4},{16,24},{20,28},{24,16},{28,20},{1,9},{5... | collective-permute-start | bytes 6488072 | tf_op jit(solution)/shard_map/ppermute | solution.py:37
  17.2 73.1 %collective-permute-start.3 = (bf16[256,4224]{1,0:T(8,128)(2,1)}, bf16[256,4224]{1,0:T(8,128)(2,1)}, u32[]{:S(2)}, u32[]{:S(2)}) collective-permute-start(bf16[256,4224]{1,0:T(8,128)(2,1)} %pad_maximum_fusion.4), channel_id=1, source_target_pairs={{0,16},{4,20},{8,24},{12,28},{16,0},{20,4},{24,8},{28,12},{1,17},{... | collective-permute-start | bytes 6488072 | tf_op jit(solution)/shard_map/ppermute | solution.py:37
  43.1 44.7 %collective-permute-start.13 = (bf16[256,1024]{1,0:T(8,128)(2,1)}, bf16[256,1024]{1,0:T(8,128)(2,1)S(1)}, u32[]{:S(2)}, u32[]{:S(2)}) collective-permute-start(bf16[256,1024]{1,0:T(8,128)(2,1)} %pad_maximum_fusion.15), channel_id=1, source_target_pairs={{0,3},{1,2},{2,1},{3,0},{4,7},{5,6},{6,5},{7,4},{8,11},{9,10},{10,... | collective-permute-start | bytes 1572872 | tf_op jit(solution)/shard_map/ppermute | solution.py:37
  44.4 43.3 %collective-permute-start.12 = (bf16[256,1024]{1,0:T(8,128)(2,1)}, bf16[256,1024]{1,0:T(8,128)(2,1)S(1)}, u32[]{:S(2)}, u32[]{:S(2)}) collective-permute-start(bf16[256,1024]{1,0:T(8,128)(2,1)} %pad_maximum_fusion.14), channel_id=1, source_target_pairs={{0,2},{1,3},{2,0},{3,1},{4,6},{5,7},{6,4},{7,5},{8,10},{9,11},{10,... | collective-permute-start | bytes 1572872 | tf_op jit(solution)/shard_map/ppermute | solution.py:37
  90.3 152.6 %all-gather.5.cloned.1.call-start = ((), (), s32[]{:S(2)}) async-start(), calls=%async_computation.5 | async-start | bytes 9437184 | tf_op jit(solution)/shard_map/all_gather | solution.py:553
  91.1 41.6 %collective-permute-start = (bf16[256,4224]{1,0:T(8,128)(2,1)}, bf16[256,4224]{1,0:T(8,128)(2,1)}, u32[]{:S(2)}, u32[]{:S(2)}) collective-permute-start(bf16[256,4224]{1,0:T(8,128)(2,1)} %pad_maximum_fusion.4), channel_id=1, source_target_pairs={{0,4},{4,0},{8,12},{12,8},{16,20},{20,16},{24,28},{28,24},{1,5},{5... | collective-permute-start | bytes 6488072 | tf_op jit(solution)/shard_map/ppermute | solution.py:37
  96.0 753.6 %reduce-scatter.3.cloned.1.call-start = ((), (), s32[]{:S(2)}) async-start(), calls=%async_computation.6 | async-start | bytes 9437184 | tf_op jit(solution)/shard_map/reduce_scatter | solution.py:776
  132.7 56.6 %collective-permute-start.10 = (bf16[2,48,2048]{2,1,0:T(8,128)(2,1)}, bf16[2,48,2048]{2,1,0:T(8,128)(2,1)}, u32[]{:S(2)}, u32[]{:S(2)}) collective-permute-start(bf16[2,48,2048]{2,1,0:T(8,128)(2,1)} %get-tuple-element.254), channel_id=1, source_target_pairs={{0,3},{1,2},{2,1},{3,0},{4,7},{5,6},{6,5},{7,4},{8,11},{9,10},{10,... | collective-permute-start | bytes 1179656 | tf_op jit(solution)/shard_map/ppermute | solution.py:37
  134.4 57.7 %collective-permute-start.5 = (bf16[2,64,2048]{2,1,0:T(8,128)(2,1)S(1)}, bf16[2,64,2048]{2,1,0:T(8,128)(2,1)}, u32[]{:S(2)}, u32[]{:S(2)}) collective-permute-start(bf16[2,64,2048]{2,1,0:T(8,128)(2,1)S(1)} %bitcast.431), channel_id=1, source_target_pairs={{0,1},{1,0},{2,3},{3,2},{4,5},{5,4},{6,7},{7,6},{8,9},{9,8},{10,11... | collective-permute-start | bytes 1572872 | tf_op jit(solution)/shard_map/ppermute | solution.py:37
  137.4 61.1 %collective-permute-start.6 = (bf16[2,64,2048]{2,1,0:T(8,128)(2,1)S(1)}, bf16[2,64,2048]{2,1,0:T(8,128)(2,1)S(1)}, u32[]{:S(2)}, u32[]{:S(2)}) collective-permute-start(bf16[2,64,2048]{2,1,0:T(8,128)(2,1)S(1)} %bitcast.432), channel_id=1, source_target_pairs={{0,2},{1,3},{2,0},{3,1},{4,6},{5,7},{6,4},{7,5},{8,10},{9,11},{10,... | collective-permute-start | bytes 1572872 | tf_op jit(solution)/shard_map/ppermute | solution.py:37
  212.5 61.1 %collective-permute-start.16 = (bf16[256,4224]{1,0:T(8,128)(2,1)}, bf16[256,4224]{1,0:T(8,128)(2,1)}, u32[]{:S(2)}, u32[]{:S(2)}) collective-permute-start(bf16[256,4224]{1,0:T(8,128)(2,1)} %get-tuple-element.106.refs_0_), channel_id=1, source_target_pairs={{0,16},{4,20},{8,24},{12,28},{16,0},{20,4},{24,8},{28,12},{1,17},{... | collective-permute-start | bytes 6488072 | tf_op jit(solution)/shard_map/ppermute | solution.py:37
  213.2 60.5 %collective-permute-start.17 = (bf16[256,4224]{1,0:T(8,128)(2,1)}, bf16[256,4224]{1,0:T(8,128)(2,1)}, u32[]{:S(2)}, u32[]{:S(2)}) collective-permute-start(bf16[256,4224]{1,0:T(8,128)(2,1)} %get-tuple-element.107), channel_id=1, source_target_pairs={{0,8},{4,12},{8,0},{12,4},{16,24},{20,28},{24,16},{28,20},{1,9},{5... | collective-permute-start | bytes 6488072 | tf_op jit(solution)/shard_map/ppermute | solution.py:37
  213.7 111.2 %collective-permute-start.21 = (bf16[256,4224]{1,0:T(8,128)(2,1)}, bf16[256,4224]{1,0:T(8,128)(2,1)}, u32[]{:S(2)}, u32[]{:S(2)}) collective-permute-start(bf16[256,4224]{1,0:T(8,128)(2,1)} %collective-permute-done.1), channel_id=1, source_target_pairs={{0,16},{4,20},{8,24},{12,28},{16,0},{20,4},{24,8},{28,12},{1,17},{... | collective-permute-start | bytes 6488072 | tf_op jit(solution)/shard_map/ppermute | solution.py:37
  277.7 45.2 %collective-permute-start.20 = (bf16[2,64,2048]{2,1,0:T(8,128)(2,1)S(1)}, bf16[2,64,2048]{2,1,0:T(8,128)(2,1)}, u32[]{:S(2)}, u32[]{:S(2)}) collective-permute-start(bf16[2,64,2048]{2,1,0:T(8,128)(2,1)S(1)} %get-tuple-element.224), channel_id=1, source_target_pairs={{0,3},{1,2},{2,1},{3,0},{4,7},{5,6},{6,5},{7,4},{8,11},{9,10},{10,... | collective-permute-start | bytes 1572872 | tf_op jit(solution)/shard_map/ppermute | solution.py:37
  278.5 91.1 %collective-permute-start.25 = (bf16[256,4224]{1,0:T(8,128)(2,1)}, bf16[256,4224]{1,0:T(8,128)(2,1)}, u32[]{:S(2)}, u32[]{:S(2)}) collective-permute-start(bf16[256,4224]{1,0:T(8,128)(2,1)} %collective-permute-done.17.refs_1_), channel_id=1, source_target_pairs={{0,16},{4,20},{8,24},{12,28},{16,0},{20,4},{24,8},{28,12},{1,17},{... | collective-permute-start | bytes 6488072 | tf_op jit(solution)/shard_map/ppermute | solution.py:37
  325.2 37.6 %collective-permute-start.29 = (bf16[384,2048]{1,0:T(8,128)(2,1)}, bf16[384,2048]{1,0:T(8,128)(2,1)}, u32[]{:S(2)}, u32[]{:S(2)}) collective-permute-start(bf16[384,2048]{1,0:T(8,128)(2,1)} %bitcast.27), channel_id=1, source_target_pairs={{0,8},{4,12},{8,0},{12,4},{16,24},{20,28},{24,16},{28,20},{1,9},{5... | collective-permute-start | bytes 4718600 | tf_op jit(solution)/shard_map/ppermute | solution.py:37
  373.4 46.3 %collective-permute-start.32 = (bf16[384,2176]{1,0:T(8,128)(2,1)S(1)}, bf16[384,2176]{1,0:T(8,128)(2,1)}, u32[]{:S(2)}, u32[]{:S(2)}) collective-permute-start(bf16[384,2176]{1,0:T(8,128)(2,1)S(1)} %bitcast.418), channel_id=1, source_target_pairs={{0,8},{4,12},{8,0},{12,4},{16,24},{20,28},{24,16},{28,20},{1,9},{5... | collective-permute-start | bytes 5013512 | tf_op jit(solution)/shard_map/ppermute | solution.py:37
  478.9 39.2 %collective-permute-start.31 = (bf16[384,2176]{1,0:T(8,128)(2,1)}, bf16[384,2176]{1,0:T(8,128)(2,1)}, u32[]{:S(2)}, u32[]{:S(2)}) collective-permute-start(bf16[384,2176]{1,0:T(8,128)(2,1)} %split.25), channel_id=1, source_target_pairs={{0,4},{4,0},{8,12},{12,8},{16,20},{20,16},{24,28},{28,24},{1,5},{5... | collective-permute-start | bytes 5013512 | tf_op jit(solution)/shard_map/ppermute | solution.py:37
  479.1 39.1 %collective-permute-start.35 = (bf16[384,2176]{1,0:T(8,128)(2,1)}, bf16[384,2176]{1,0:T(8,128)(2,1)}, u32[]{:S(2)}, u32[]{:S(2)}) collective-permute-start(bf16[384,2176]{1,0:T(8,128)(2,1)} %add_convert_fusion.3), channel_id=1, source_target_pairs={{0,8},{4,12},{8,0},{12,4},{16,24},{20,28},{24,16},{28,20},{1,9},{5... | collective-permute-start | bytes 5013512 | tf_op jit(solution)/shard_map/ppermute | solution.py:37
  505.2 128.2 %collective-permute-start.45 = (bf16[512,4224]{1,0:T(8,128)(2,1)}, bf16[512,4224]{1,0:T(8,128)(2,1)}, u32[]{:S(2)}, u32[]{:S(2)}) collective-permute-start(bf16[512,4224]{1,0:T(8,128)(2,1)} %get-tuple-element.130), channel_id=1, source_target_pairs={{0,16},{4,20},{8,24},{12,28},{16,0},{20,4},{24,8},{28,12},{1,17},{... | collective-permute-start | bytes 12976136 | tf_op jit(solution)/shard_map/ppermute | solution.py:37
  520.8 108.6 %collective-permute-start.44 = (bf16[384,2048]{1,0:T(8,128)(2,1)}, bf16[384,2048]{1,0:T(8,128)(2,1)}, u32[]{:S(2)}, u32[]{:S(2)}) collective-permute-start(bf16[384,2048]{1,0:T(8,128)(2,1)} %add_convert_fusion.4), channel_id=1, source_target_pairs={{0,8},{4,12},{8,0},{12,4},{16,24},{20,28},{24,16},{28,20},{1,9},{5... | collective-permute-start | bytes 4718600 | tf_op jit(solution)/shard_map/ppermute | solution.py:37
  582.4 37.8 %collective-permute-start.42 = (bf16[2,64,2048]{2,1,0:T(8,128)(2,1)S(1)}, bf16[2,64,2048]{2,1,0:T(8,128)(2,1)S(1)}, u32[]{:S(2)}, u32[]{:S(2)}) collective-permute-start(bf16[2,64,2048]{2,1,0:T(8,128)(2,1)S(1)} %bitcast.439), channel_id=1, source_target_pairs={{0,2},{1,3},{2,0},{3,1},{4,6},{5,7},{6,4},{7,5},{8,10},{9,11},{10,... | collective-permute-start | bytes 1572872 | tf_op jit(solution)/shard_map/ppermute | solution.py:37
  585.3 44.0 %collective-permute-start.43 = (bf16[2,64,2048]{2,1,0:T(8,128)(2,1)S(1)}, bf16[2,64,2048]{2,1,0:T(8,128)(2,1)S(1)}, u32[]{:S(2)}, u32[]{:S(2)}) collective-permute-start(bf16[2,64,2048]{2,1,0:T(8,128)(2,1)S(1)} %bitcast.440), channel_id=1, source_target_pairs={{0,3},{1,2},{2,1},{3,0},{4,7},{5,6},{6,5},{7,4},{8,11},{9,10},{10,... | collective-permute-start | bytes 1572872 | tf_op jit(solution)/shard_map/ppermute | solution.py:37
  640.2 249.9 %reduce-scatter.5.cloned.1.call-start = ((), (), s32[]{:S(2)}) async-start(), calls=%async_computation.7 | async-start | bytes 14155776 | tf_op jit(solution)/shard_map/reduce_scatter | solution.py:776
  664.0 139.6 %collective-permute-start.53 = (bf16[512,4224]{1,0:T(8,128)(2,1)}, bf16[512,4224]{1,0:T(8,128)(2,1)}, u32[]{:S(2)}, u32[]{:S(2)}) collective-permute-start(bf16[512,4224]{1,0:T(8,128)(2,1)} %get-tuple-element.170), channel_id=1, source_target_pairs={{0,16},{4,20},{8,24},{12,28},{16,0},{20,4},{24,8},{28,12},{1,17},{... | collective-permute-start | bytes 12976136 | tf_op jit(solution)/shard_map/ppermute | solution.py:37
  665.1 139.7 %collective-permute-start.52 = (bf16[512,4224]{1,0:T(8,128)(2,1)}, bf16[512,4224]{1,0:T(8,128)(2,1)}, u32[]{:S(2)}, u32[]{:S(2)}) collective-permute-start(bf16[512,4224]{1,0:T(8,128)(2,1)} %add_convert_fusion.1), channel_id=1, source_target_pairs={{0,8},{4,12},{8,0},{12,4},{16,24},{20,28},{24,16},{28,20},{1,9},{5... | collective-permute-start | bytes 12976136 | tf_op jit(solution)/shard_map/ppermute | solution.py:37
  710.3 39.9 %collective-permute-start.50 = (bf16[2,64,2176]{2,1,0:T(8,128)(2,1)S(1)}, bf16[2,64,2176]{2,1,0:T(8,128)(2,1)}, u32[]{:S(2)}, u32[]{:S(2)}) collective-permute-start(bf16[2,64,2176]{2,1,0:T(8,128)(2,1)S(1)} %get-tuple-element.232), channel_id=1, source_target_pairs={{0,2},{1,3},{2,0},{3,1},{4,6},{5,7},{6,4},{7,5},{8,10},{9,11},{10,... | collective-permute-start | bytes 1671176 | tf_op jit(solution)/shard_map/ppermute | solution.py:37
  713.3 44.5 %collective-permute-start.51 = (bf16[2,64,2176]{2,1,0:T(8,128)(2,1)S(1)}, bf16[2,64,2176]{2,1,0:T(8,128)(2,1)}, u32[]{:S(2)}, u32[]{:S(2)}) collective-permute-start(bf16[2,64,2176]{2,1,0:T(8,128)(2,1)S(1)} %get-tuple-element.231), channel_id=1, source_target_pairs={{0,3},{1,2},{2,1},{3,0},{4,7},{5,6},{6,5},{7,4},{8,11},{9,10},{10,... | collective-permute-start | bytes 1671176 | tf_op jit(solution)/shard_map/ppermute | solution.py:37
  829.5 60.6 %all-to-all-start.1 = ((bf16[8,48,2048]{2,1,0:T(8,128)(2,1)}), bf16[8,48,2048]{2,1,0:T(8,128)(2,1)}, u32[]{:S(2)}, u32[]{:S(2)}) async-start(bf16[8,48,2048]{2,1,0:T(8,128)(2,1)} %pad_maximum_fusion.11), calls=%async_computation.1 | async-start | bytes 3145728 | tf_op jit(solution)/shard_map/all_to_all | solution.py:803
  902.5 42.8 %collective-permute-start.63 = (bf16[256,512]{1,0:T(8,128)(2,1)}, bf16[256,512]{1,0:T(8,128)(2,1)}, u32[]{:S(2)}, u32[]{:S(2)}) collective-permute-start(bf16[256,512]{1,0:T(8,128)(2,1)} %get-tuple-element.246), channel_id=1, source_target_pairs={{0,0},{2,1},{1,2},{3,3},{4,4},{6,5},{5,6},{7,7},{8,8},{10,9},{9,10... | collective-permute-start | bytes 786440 | tf_op jit(solution)/shard_map/ppermute | solution.py:838
  905.8 39.5 %collective-permute-start.64 = (bf16[256,512]{1,0:T(8,128)(2,1)}, bf16[256,512]{1,0:T(8,128)(2,1)}, u32[]{:S(2)}, u32[]{:S(2)}) collective-permute-start(bf16[256,512]{1,0:T(8,128)(2,1)} %get-tuple-element.247), channel_id=1, source_target_pairs={{1,0},{3,1},{0,2},{2,3},{5,4},{7,5},{4,6},{6,7},{9,8},{11,9},{8,10... | collective-permute-start | bytes 786440 | tf_op jit(solution)/shard_map/ppermute | solution.py:841
  (152 other events, 2263.2 us)
Sparse Core Ops, SparseCore 0:
  90.5 81.2 all-gather.2
  174.2 65.9 all-gather.4
  640.3 104.2 reduce-scatter.2
  748.4 115.3 reduce-scatter.4

commit v12 on v11

--- a/solution.py
+++ b/solution.py
@@ -757,6 +757,9 @@
     back_one, other_sum, keep_got = lax.optimization_barrier(
         (back_one, other_sum, keep_got, joint_part_grad)
     )[:3]
+    out_own = lax.psum_scatter(out_part, "dp", scatter_dimension=0, tiled=True)
+    out_grad = slots_of(after(out_own, back_one))
+    back_one, out_grad = lax.optimization_barrier((back_one, out_grad))
     hidden_one_grad, slot_one_grad = back_one[:, :width], back_one[:, width : width + slots]
 
     def own(value):
@@ -778,7 +781,6 @@
     in_low, keep_got, other_sum = lax.optimization_barrier(
         (in_home.astype(bf16), keep_got, other_sum)
     )
-    out_grad = slots_of(after(reduced(out_part), back_one))
     joint_own = reduced(joint_part_grad)
 
     results = jnp.stack([out_home, in_low]).reshape(2, micro, tok_rows, width)
@@ -801,7 +803,7 @@
     small = jnp.broadcast_to(small[None], (dp_count,) + small.shape)
     results = jnp.concatenate([results, small], axis=1)
     results = lax.all_to_all(results, "dp", split_axis=0, concat_axis=0, tiled=True)
-    results, out_grad, joint_own = lax.optimization_barrier((results, out_grad, joint_own))
+    results, joint_own = lax.optimization_barrier((results, joint_own))
     query_own, kv_own = joint_own[:, :query_width], joint_own[:, query_width:]
     small = results[:, sent_back:].astype(f32)
     results = results[:, :sent_back].reshape(dp_count, 2 * micro, piece_rows, width)

time: 963 us -> 975 us (1.012)
  waiting for transfers between devices: 410 us -> 424 us
    reduce_scatter x2 -> x1, waiting for transfers between devices: 0.02 us -> 25.7 us  [reduced(): return lax.psum_scatter(value, 'dp', scatter_dimension=0, tiled=True)]
    ppermute x62, waiting for transfers between devices: 393 us -> 372 us  [swap(): return lax.ppermute(value, axis, [(i, i ^ step) for i in range(count)])]
    unnamed x246 -> x256, local copies, waits for them, and re-layouts: 28.9 us -> 24.5 us
  transfers between devices with their start and end apart: 72 -> 72, of which waited for: 34 -> 37; matrix products, arithmetic and copies ran while one was open for 26% -> 24% of each run, Pallas kernels for 13% -> 13%
where the time goes in v12:
time: 975 us; the launch traced here: 968 us
  waiting for transfers between devices  424 us (43%)
  Pallas kernels  166 us (17%)
  local copies, waits for them, and re-layouts  102 us (10%)
  other arithmetic  99 us (10%)
  starting transfers between devices  82.6 us (8%)
  matrix products  76.2 us (8%)
  between operations  17.3 us (2%)
    ppermute x62, waiting for transfers between devices, swap(): return lax.ppermute(value, axis, [(i, i ^ step) for i in range(count)])  372 us
    pallas_call x2, Pallas kernels, expert_rows(): pl.pallas_call(expert_kernel, grid_spec=pltpu.PrefetchScalarGridSpec(num_...  81.9 us
    ppermute x62, starting transfers between devices, swap(): return lax.ppermute(value, axis, [(i, i ^ step) for i in range(count)])  62.9 us
    pallas_call x2, Pallas kernels, expert_grads(): pl.pallas_call(functools.partial(expert_grad_kernel, cuts), grid_spec=plt...  49.7 us
    reduce_scatter x1, waiting for transfers between devices, reduced(): return lax.psum_scatter(value, 'dp', scatter_dimension=0, tiled=True)  25.7 us
    unnamed x256, local copies, waits for them, and re-layouts  24.5 us
    dot_general x5, matrix products, dot(): return jnp.dot(left, right, preferred_element_type=f32)  23.8 us
    dot_general x5, matrix products, dot_t(): lax.dot_general(left, right, (((1,), (1,)), ((), ())), preferred_element_...  22.2 us
  transfers between devices with their start and end apart: 72, of which 37 were waited for; matrix products, arithmetic and copies ran while one was open for 24% of the time, Pallas kernels for 13%

profile of v12, /device:TPU:8, one launch (start us, length us, event | category | flops | bytes accessed | tf_op | source)
XLA Modules:
  0.0 967.6 jit_solution(3273448049611289962)
XLA Ops:
  49.0 38.6 %collective-permute-done.12 = bf16[256,1024]{1,0:T(8,128)(2,1)S(1)} collective-permute-done((bf16[256,1024]{1,0:T(8,128)(2,1)}, bf16[256,1024]{1,0:T(8,128)(2,1)S(1)}, u32[]{:S(2)}, u32[]{:S(2)}) %collective-permute-start.12) | collective-permute-done | bytes 524320 | tf_op jit(solution)/shard_map/ppermute | solution.py:37
  103.6 16.7 %all-to-all-done = bf16[8,4,8,2048]{3,2,1,0:T(8,128)(2,1)S(1)} async-done(((bf16[8,4,8,2048]{3,2,1,0:T(8,128)(2,1)}), bf16[8,4,8,2048]{3,2,1,0:T(8,128)(2,1)S(1)}, u32[]{:S(2)}, u32[]{:S(2)}) %all-to-all-start) | async-done | bytes 1048608 | tf_op jit(solution)/shard_map/all_to_all | solution.py:476
  137.4 8.0 collective-permute-done.8
  145.4 10.9 %collective-permute-done.9 = bf16[2,48,2048]{2,1,0:T(8,128)(2,1)} collective-permute-done((bf16[2,48,2048]{2,1,0:T(8,128)(2,1)}, bf16[2,48,2048]{2,1,0:T(8,128)(2,1)}, u32[]{:S(2)}, u32[]{:S(2)}) %collective-permute-start.9) | collective-permute-done | bytes 393248 | tf_op jit(solution)/shard_map/ppermute | solution.py:37
  156.3 33.0 %collective-permute-done.10 = bf16[2,48,2048]{2,1,0:T(8,128)(2,1)} collective-permute-done((bf16[2,48,2048]{2,1,0:T(8,128)(2,1)}, bf16[2,48,2048]{2,1,0:T(8,128)(2,1)}, u32[]{:S(2)}, u32[]{:S(2)}) %collective-permute-start.10) | collective-permute-done | bytes 393248 | tf_op jit(solution)/shard_map/ppermute | solution.py:37
  198.5 12.3 %collective-permute-done.7 = bf16[2,64,2048]{2,1,0:T(8,128)(2,1)S(1)} collective-permute-done((bf16[2,64,2048]{2,1,0:T(8,128)(2,1)S(1)}, bf16[2,64,2048]{2,1,0:T(8,128)(2,1)S(1)}, u32[]{:S(2)}, u32[]{:S(2)}) %collective-permute-start.7) | collective-permute-done | bytes 524320 | tf_op jit(solution)/shard_map/ppermute | solution.py:37
  226.7 14.7 %attention_forward.1 = (bf16[512,2048]{1,0:T(8,128)(2,1)S(1)}, bf16[512,2048]{1,0:T(8,128)(2,1)}, bf16[512,2048]{1,0:T(8,128)(2,1)}, bf16[512,512]{1,0:T(8,128)(...) custom-call(s32[2]{0:T(128)S(1)} %fusion.133.lens, f32[512,2048]{1,0:T(8,128)} %fusion.2.query, ...), custom_call_target="tpu_custom_call" | custom-call | flops 1073741824 | bytes 14680064 | tf_op jit(solution)/shard_map/attention_forward/pallas_call | solution.py:181
  242.8 7.6 fusion.178
  250.5 23.1 %collective-permute-done.16.refs_2_ = bf16[256,4224]{1,0:T(8,128)(2,1)} collective-permute-done((bf16[256,4224]{1,0:T(8,128)(2,1)}, bf16[256,4224]{1,0:T(8,128)(2,1)}, u32[]{:S(2)}, u32[]{:S(2)}) %collective-permute-start.16) | collective-permute-done | bytes 2162720 | tf_op jit(solution)/shard_map/ppermute | solution.py:37
  279.4 16.3 %collective-permute-done.18 = bf16[2,64,2048]{2,1,0:T(8,128)(2,1)} collective-permute-done((bf16[2,64,2048]{2,1,0:T(8,128)(2,1)}, bf16[2,64,2048]{2,1,0:T(8,128)(2,1)}, u32[]{:S(2)}, u32[]{:S(2)}) %collective-permute-start.18) | collective-permute-done | bytes 524320 | tf_op jit(solution)/shard_map/ppermute | solution.py:37
  295.7 17.1 %collective-permute-done.19 = bf16[2,64,2048]{2,1,0:T(8,128)(2,1)} collective-permute-done((bf16[2,64,2048]{2,1,0:T(8,128)(2,1)}, bf16[2,64,2048]{2,1,0:T(8,128)(2,1)}, u32[]{:S(2)}, u32[]{:S(2)}) %collective-permute-start.19) | collective-permute-done | bytes 524320 | tf_op jit(solution)/shard_map/ppermute | solution.py:37
  312.8 10.0 %collective-permute-done.20 = bf16[2,64,2048]{2,1,0:T(8,128)(2,1)} collective-permute-done((bf16[2,64,2048]{2,1,0:T(8,128)(2,1)S(1)}, bf16[2,64,2048]{2,1,0:T(8,128)(2,1)}, u32[]{:S(2)}, u32[]{:S(2)}) %collective-permute-start.20) | collective-permute-done | bytes 524320 | tf_op jit(solution)/shard_map/ppermute | solution.py:37
  335.3 10.7 %collective-permute-done.22 = bf16[2,48,2176]{2,1,0:T(8,128)(2,1)S(1)} collective-permute-done((bf16[2,48,2176]{2,1,0:T(8,128)(2,1)S(1)}, bf16[2,48,2176]{2,1,0:T(8,128)(2,1)S(1)}, u32[]{:S(2)}, u32[]{:S(2)}) %collective-permute-start.22) | collective-permute-done | bytes 417824 | tf_op jit(solution)/shard_map/ppermute | solution.py:37
  346.1 16.7 %collective-permute-done.23 = bf16[2,48,2176]{2,1,0:T(8,128)(2,1)S(1)} collective-permute-done((bf16[2,48,2176]{2,1,0:T(8,128)(2,1)S(1)}, bf16[2,48,2176]{2,1,0:T(8,128)(2,1)S(1)}, u32[]{:S(2)}, u32[]{:S(2)}) %collective-permute-start.23) | collective-permute-done | bytes 417824 | tf_op jit(solution)/shard_map/ppermute | solution.py:37
  378.6 41.0 %expert_rows.2 = (bf16[768,2048]{1,0:T(8,128)(2,1)}, bf16[768,2176]{1,0:T(8,128)(2,1)}, bf16[768,1408]{1,0:T(8,128)(2,1)}, bf16[768,2816]{1,0:T(8,128)(2,1)}) custom-call(s32[2]{0:T(128)} %pad_add_fusion.1.place_ref, bf16[768,2176]{1,0:T(8,128)(2,1)} %pad_maximum_fusion.2.hidden.refs_0_.refs_4_, bf16[768,2048]{1,0:T(8,128)(2,1)} %copy-done.48, ...), custom_call_target="tpu_custom_call" | custom-call | flops 26575110144 | bytes 36175872 | tf_op jit(solution)/shard_map/expert_rows/pallas_call | solution.py:332
  425.6 40.9 %expert_rows.3 = (bf16[768,2048]{1,0:T(8,128)(2,1)}, bf16[768,2176]{1,0:T(8,128)(2,1)}, bf16[768,1408]{1,0:T(8,128)(2,1)}, bf16[768,2816]{1,0:T(8,128)(2,1)}) custom-call(s32[2]{0:T(128)} %pad_add_fusion.1.place_ref, bf16[768,2176]{1,0:T(8,128)(2,1)} %copy-done.46, bf16[768,2048]{1,0:T(8,128)(2,1)} %copy-done.47, ...), custom_call_target="tpu_custom_call" | custom-call | flops 26575110144 | bytes 36175872 | tf_op jit(solution)/shard_map/expert_rows/pallas_call | solution.py:332
  480.5 24.8 %expert_grads.2 = (bf16[512,4224]{1,0:T(8,128)(2,1)}, bf16[512,4224]{1,0:T(8,128)(2,1)}) custom-call(s32[4]{0:T(128)} %get-tuple-element.306.order, bf16[768,2176]{1,0:T(8,128)(2,1)} %pad_maximum_fusion.2.hidden.refs_0_.refs_4_, bf16[768,2176]{1,0:T(8,128)(2,1)} %copy-done.46, bf16[768,2048]{1,0:T(8,128)(2,1)} %copy-done.48, bf16[768,2048]{1,0:T(8,128)(2,1)} %copy-done.47, ...), custom_call_target="tpu_custom_call" | custom-call | flops 13287555072 | bytes 27918336 | tf_op jit(solution)/shard_map/expert_grads/pallas_call | solution.py:405
  525.5 25.0 %expert_grads.3 = (bf16[512,4224]{1,0:T(8,128)(2,1)}, bf16[512,4224]{1,0:T(8,128)(2,1)}) custom-call(s32[4]{0:T(128)} %get-tuple-element.307.order, bf16[768,2176]{1,0:T(8,128)(2,1)} %pad_maximum_fusion.2.hidden.refs_0_.refs_4_, bf16[768,2176]{1,0:T(8,128)(2,1)} %copy-done.46, bf16[768,2048]{1,0:T(8,128)(2,1)} %copy-done.48, bf16[768,2048]{1,0:T(8,128)(2,1)} %copy-done.47, ...), custom_call_target="tpu_custom_call" | custom-call | flops 13287555072 | bytes 27918336 | tf_op jit(solution)/shard_map/expert_grads/pallas_call | solution.py:405
  553.0 8.0 collective-permute-done.40
  586.3 15.7 %collective-permute-done.41 = bf16[2,64,2048]{2,1,0:T(8,128)(2,1)S(1)} collective-permute-done((bf16[2,64,2048]{2,1,0:T(8,128)(2,1)S(1)}, bf16[2,64,2048]{2,1,0:T(8,128)(2,1)S(1)}, u32[]{:S(2)}, u32[]{:S(2)}) %collective-permute-start.41) | collective-permute-done | bytes 524320 | tf_op jit(solution)/shard_map/ppermute | solution.py:37
  602.0 18.3 %collective-permute-done.42 = bf16[2,64,2048]{2,1,0:T(8,128)(2,1)S(1)} collective-permute-done((bf16[2,64,2048]{2,1,0:T(8,128)(2,1)S(1)}, bf16[2,64,2048]{2,1,0:T(8,128)(2,1)S(1)}, u32[]{:S(2)}, u32[]{:S(2)}) %collective-permute-start.42) | collective-permute-done | bytes 524320 | tf_op jit(solution)/shard_map/ppermute | solution.py:37
  620.3 9.2 collective-permute-done.43
  640.6 10.8 %fusion.180.vals_grad = f32[512,2048]{1,0:T(8,128)} fusion(bf16[512,2048]{1,0:T(8,128)(2,1)} %bitcast.428, bf16[2048,2048]{1,0:T(8,128)(2,1)} %all-gather.5.cloned.1.call-done), kind=kOutput, calls=%fused_computation.455 | convolution fusion | flops 4294967296 | bytes 14680064 | tf_op jit(solution)/shard_map/dot_general | solution.py:24
  651.3 8.1 add_convert_fusion.1
  667.1 20.1 %attention_backward.1 = (bf16[512,2048]{1,0:T(8,128)(2,1)S(1)}, bf16[512,512]{1,0:T(8,128)(2,1)S(1)}, bf16[512,512]{1,0:T(8,128)(2,1)S(1)}, f32[512,128]{1,0:T(8,128)S(1)}) custom-call(s32[2]{0:T(128)S(1)} %fusion.133.lens, bf16[512,2048]{1,0:T(8,128)(2,1)} %get-tuple-element.158.query, bf16[512,512]{1,0:T(8,128)(2,1)S(1)} %get-tuple-element.159.key, ...), custom_call_target="tpu_custom_call" | custom-call | flops 2684354560 | bytes 14680064 | tf_op jit(solution)/shard_map/attention_backward/pallas_call | solution.py:212
  699.8 8.2 add_convert_fusion.2
  712.9 9.9 %convolution_convert_fusion = bf16[2048,3072]{1,0:T(8,128)(2,1)} fusion(bf16[512,2048]{1,0:T(8,128)(2,1)S(1)} %bitcast.415, bf16[512,512]{1,0:T(8,128)(2,1)S(1)} %get-tuple-element.168, bf16[512,512]{1,0:T(8,128)(2,1)S(1)} %get-tuple-element.167, bf16[512,2048]{1,0:T(8,128)(2,1)S(1)} %get-tuple-element.166), kind=kOutput, calls=%fused_computation | convolution fusion | flops 6458179584 | bytes 17825792 | tf_op jit(solution)/shard_map/dot_general | solution.py:32
  727.1 22.5 %collective-permute-done.50 = bf16[2,64,2176]{2,1,0:T(8,128)(2,1)} collective-permute-done((bf16[2,64,2176]{2,1,0:T(8,128)(2,1)}, bf16[2,64,2176]{2,1,0:T(8,128)(2,1)}, u32[]{:S(2)}, u32[]{:S(2)}) %collective-permute-start.50) | collective-permute-done | bytes 557088 | tf_op jit(solution)/shard_map/ppermute | solution.py:37
  758.7 31.5 %collective-permute-done.53 = bf16[512,4224]{1,0:T(8,128)(2,1)} collective-permute-done((bf16[512,4224]{1,0:T(8,128)(2,1)}, bf16[512,4224]{1,0:T(8,128)(2,1)}, u32[]{:S(2)}, u32[]{:S(2)}) %collective-permute-start.53) | collective-permute-done | bytes 4325408 | tf_op jit(solution)/shard_map/ppermute | solution.py:37
  807.2 9.7 %collective-permute-done.55 = bf16[256,512]{1,0:T(8,128)(2,1)S(1)} collective-permute-done((bf16[256,512]{1,0:T(8,128)(2,1)S(1)}, bf16[256,512]{1,0:T(8,128)(2,1)S(1)}, u32[]{:S(2)}, u32[]{:S(2)}) %collective-permute-start.55) | collective-permute-done | bytes 262176 | tf_op jit(solution)/shard_map/ppermute | solution.py:37
  871.4 8.3 all-to-all-done.1
  879.7 25.7 %reduce-scatter.5.cloned.1.call-done = bf16[256,3072]{1,0:T(8,128)(2,1)} async-done(((bf16[2048,3072]{1,0:T(8,128)(2,1)}), bf16[256,3072]{1,0:T(8,128)(2,1)}) %reduce-scatter.5.cloned.1.call-update) | async-done | bytes 1572880 | tf_op jit(solution)/shard_map/reduce_scatter | solution.py:779
  (644 shorter events, 377.1 us)
Async XLA Ops:
  7.2 205.2 %all-gather.3.cloned.1.call-start = ((), (), s32[]{:S(2)}) async-start(), calls=%async_computation.4 | async-start | bytes 14155776 | tf_op jit(solution)/shard_map/all_gather | solution.py:552
  14.3 76.0 %collective-permute-start.1 = (bf16[256,4224]{1,0:T(8,128)(2,1)}, bf16[256,4224]{1,0:T(8,128)(2,1)}, u32[]{:S(2)}, u32[]{:S(2)}) collective-permute-start(bf16[256,4224]{1,0:T(8,128)(2,1)} %pad_maximum_fusion.5), channel_id=1, source_target_pairs={{0,8},{4,12},{8,0},{12,4},{16,24},{20,28},{24,16},{28,20},{1,9},{5... | collective-permute-start | bytes 6488072 | tf_op jit(solution)/shard_map/ppermute | solution.py:37
  17.2 73.0 %collective-permute-start.3 = (bf16[256,4224]{1,0:T(8,128)(2,1)}, bf16[256,4224]{1,0:T(8,128)(2,1)}, u32[]{:S(2)}, u32[]{:S(2)}) collective-permute-start(bf16[256,4224]{1,0:T(8,128)(2,1)} %pad_maximum_fusion.4), channel_id=1, source_target_pairs={{0,16},{4,20},{8,24},{12,28},{16,0},{20,4},{24,8},{28,12},{1,17},{... | collective-permute-start | bytes 6488072 | tf_op jit(solution)/shard_map/ppermute | solution.py:37
  43.0 44.7 %collective-permute-start.13 = (bf16[256,1024]{1,0:T(8,128)(2,1)}, bf16[256,1024]{1,0:T(8,128)(2,1)S(1)}, u32[]{:S(2)}, u32[]{:S(2)}) collective-permute-start(bf16[256,1024]{1,0:T(8,128)(2,1)} %pad_maximum_fusion.15), channel_id=1, source_target_pairs={{0,3},{1,2},{2,1},{3,0},{4,7},{5,6},{6,5},{7,4},{8,11},{9,10},{10,... | collective-permute-start | bytes 1572872 | tf_op jit(solution)/shard_map/ppermute | solution.py:37
  44.4 43.3 %collective-permute-start.12 = (bf16[256,1024]{1,0:T(8,128)(2,1)}, bf16[256,1024]{1,0:T(8,128)(2,1)S(1)}, u32[]{:S(2)}, u32[]{:S(2)}) collective-permute-start(bf16[256,1024]{1,0:T(8,128)(2,1)} %pad_maximum_fusion.14), channel_id=1, source_target_pairs={{0,2},{1,3},{2,0},{3,1},{4,6},{5,7},{6,4},{7,5},{8,10},{9,11},{10,... | collective-permute-start | bytes 1572872 | tf_op jit(solution)/shard_map/ppermute | solution.py:37
  90.3 152.5 %all-gather.5.cloned.1.call-start = ((), (), s32[]{:S(2)}) async-start(), calls=%async_computation.5 | async-start | bytes 9437184 | tf_op jit(solution)/shard_map/all_gather | solution.py:553
  91.0 41.6 %collective-permute-start = (bf16[256,4224]{1,0:T(8,128)(2,1)}, bf16[256,4224]{1,0:T(8,128)(2,1)}, u32[]{:S(2)}, u32[]{:S(2)}) collective-permute-start(bf16[256,4224]{1,0:T(8,128)(2,1)} %pad_maximum_fusion.4), channel_id=1, source_target_pairs={{0,4},{4,0},{8,12},{12,8},{16,20},{20,16},{24,28},{28,24},{1,5},{5... | collective-permute-start | bytes 6488072 | tf_op jit(solution)/shard_map/ppermute | solution.py:37
  95.9 695.2 %reduce-scatter.3.cloned.1.call-start = ((), (), s32[]{:S(2)}) async-start(), calls=%async_computation.6 | async-start | bytes 9437184 | tf_op jit(solution)/shard_map/reduce_scatter | solution.py:760
  132.6 56.7 %collective-permute-start.10 = (bf16[2,48,2048]{2,1,0:T(8,128)(2,1)}, bf16[2,48,2048]{2,1,0:T(8,128)(2,1)}, u32[]{:S(2)}, u32[]{:S(2)}) collective-permute-start(bf16[2,48,2048]{2,1,0:T(8,128)(2,1)} %get-tuple-element.256), channel_id=1, source_target_pairs={{0,3},{1,2},{2,1},{3,0},{4,7},{5,6},{6,5},{7,4},{8,11},{9,10},{10,... | collective-permute-start | bytes 1179656 | tf_op jit(solution)/shard_map/ppermute | solution.py:37
  134.4 57.7 %collective-permute-start.5 = (bf16[2,64,2048]{2,1,0:T(8,128)(2,1)S(1)}, bf16[2,64,2048]{2,1,0:T(8,128)(2,1)}, u32[]{:S(2)}, u32[]{:S(2)}) collective-permute-start(bf16[2,64,2048]{2,1,0:T(8,128)(2,1)S(1)} %bitcast.429), channel_id=1, source_target_pairs={{0,1},{1,0},{2,3},{3,2},{4,5},{5,4},{6,7},{7,6},{8,9},{9,8},{10,11... | collective-permute-start | bytes 1572872 | tf_op jit(solution)/shard_map/ppermute | solution.py:37
  137.4 61.1 %collective-permute-start.6 = (bf16[2,64,2048]{2,1,0:T(8,128)(2,1)S(1)}, bf16[2,64,2048]{2,1,0:T(8,128)(2,1)S(1)}, u32[]{:S(2)}, u32[]{:S(2)}) collective-permute-start(bf16[2,64,2048]{2,1,0:T(8,128)(2,1)S(1)} %bitcast.430), channel_id=1, source_target_pairs={{0,2},{1,3},{2,0},{3,1},{4,6},{5,7},{6,4},{7,5},{8,10},{9,11},{10,... | collective-permute-start | bytes 1572872 | tf_op jit(solution)/shard_map/ppermute | solution.py:37
  212.5 61.1 %collective-permute-start.16 = (bf16[256,4224]{1,0:T(8,128)(2,1)}, bf16[256,4224]{1,0:T(8,128)(2,1)}, u32[]{:S(2)}, u32[]{:S(2)}) collective-permute-start(bf16[256,4224]{1,0:T(8,128)(2,1)} %get-tuple-element.107.refs_0_), channel_id=1, source_target_pairs={{0,16},{4,20},{8,24},{12,28},{16,0},{20,4},{24,8},{28,12},{1,17},{... | collective-permute-start | bytes 6488072 | tf_op jit(solution)/shard_map/ppermute | solution.py:37
  213.1 60.5 %collective-permute-start.17 = (bf16[256,4224]{1,0:T(8,128)(2,1)}, bf16[256,4224]{1,0:T(8,128)(2,1)}, u32[]{:S(2)}, u32[]{:S(2)}) collective-permute-start(bf16[256,4224]{1,0:T(8,128)(2,1)} %get-tuple-element.108), channel_id=1, source_target_pairs={{0,8},{4,12},{8,0},{12,4},{16,24},{20,28},{24,16},{28,20},{1,9},{5... | collective-permute-start | bytes 6488072 | tf_op jit(solution)/shard_map/ppermute | solution.py:37
  213.6 111.2 %collective-permute-start.21 = (bf16[256,4224]{1,0:T(8,128)(2,1)}, bf16[256,4224]{1,0:T(8,128)(2,1)}, u32[]{:S(2)}, u32[]{:S(2)}) collective-permute-start(bf16[256,4224]{1,0:T(8,128)(2,1)} %collective-permute-done.1), channel_id=1, source_target_pairs={{0,16},{4,20},{8,24},{12,28},{16,0},{20,4},{24,8},{28,12},{1,17},{... | collective-permute-start | bytes 6488072 | tf_op jit(solution)/shard_map/ppermute | solution.py:37
  275.7 37.2 %collective-permute-start.19 = (bf16[2,64,2048]{2,1,0:T(8,128)(2,1)}, bf16[2,64,2048]{2,1,0:T(8,128)(2,1)}, u32[]{:S(2)}, u32[]{:S(2)}) collective-permute-start(bf16[2,64,2048]{2,1,0:T(8,128)(2,1)} %get-tuple-element.227), channel_id=1, source_target_pairs={{0,2},{1,3},{2,0},{3,1},{4,6},{5,7},{6,4},{7,5},{8,10},{9,11},{10,... | collective-permute-start | bytes 1572872 | tf_op jit(solution)/shard_map/ppermute | solution.py:37
  277.7 45.2 %collective-permute-start.20 = (bf16[2,64,2048]{2,1,0:T(8,128)(2,1)S(1)}, bf16[2,64,2048]{2,1,0:T(8,128)(2,1)}, u32[]{:S(2)}, u32[]{:S(2)}) collective-permute-start(bf16[2,64,2048]{2,1,0:T(8,128)(2,1)S(1)} %get-tuple-element.226), channel_id=1, source_target_pairs={{0,3},{1,2},{2,1},{3,0},{4,7},{5,6},{6,5},{7,4},{8,11},{9,10},{10,... | collective-permute-start | bytes 1572872 | tf_op jit(solution)/shard_map/ppermute | solution.py:37
  278.4 91.1 %collective-permute-start.25 = (bf16[256,4224]{1,0:T(8,128)(2,1)}, bf16[256,4224]{1,0:T(8,128)(2,1)}, u32[]{:S(2)}, u32[]{:S(2)}) collective-permute-start(bf16[256,4224]{1,0:T(8,128)(2,1)} %collective-permute-done.17.refs_1_), channel_id=1, source_target_pairs={{0,16},{4,20},{8,24},{12,28},{16,0},{20,4},{24,8},{28,12},{1,17},{... | collective-permute-start | bytes 6488072 | tf_op jit(solution)/shard_map/ppermute | solution.py:37
  325.1 37.7 %collective-permute-start.29 = (bf16[384,2048]{1,0:T(8,128)(2,1)}, bf16[384,2048]{1,0:T(8,128)(2,1)}, u32[]{:S(2)}, u32[]{:S(2)}) collective-permute-start(bf16[384,2048]{1,0:T(8,128)(2,1)} %bitcast.27), channel_id=1, source_target_pairs={{0,8},{4,12},{8,0},{12,4},{16,24},{20,28},{24,16},{28,20},{1,9},{5... | collective-permute-start | bytes 4718600 | tf_op jit(solution)/shard_map/ppermute | solution.py:37
  373.4 46.2 %collective-permute-start.32 = (bf16[384,2176]{1,0:T(8,128)(2,1)S(1)}, bf16[384,2176]{1,0:T(8,128)(2,1)}, u32[]{:S(2)}, u32[]{:S(2)}) collective-permute-start(bf16[384,2176]{1,0:T(8,128)(2,1)S(1)} %bitcast.418), channel_id=1, source_target_pairs={{0,8},{4,12},{8,0},{12,4},{16,24},{20,28},{24,16},{28,20},{1,9},{5... | collective-permute-start | bytes 5013512 | tf_op jit(solution)/shard_map/ppermute | solution.py:37
  479.0 39.2 %collective-permute-start.31 = (bf16[384,2176]{1,0:T(8,128)(2,1)}, bf16[384,2176]{1,0:T(8,128)(2,1)}, u32[]{:S(2)}, u32[]{:S(2)}) collective-permute-start(bf16[384,2176]{1,0:T(8,128)(2,1)} %split.25), channel_id=1, source_target_pairs={{0,4},{4,0},{8,12},{12,8},{16,20},{20,16},{24,28},{28,24},{1,5},{5... | collective-permute-start | bytes 5013512 | tf_op jit(solution)/shard_map/ppermute | solution.py:37
  479.2 39.1 %collective-permute-start.35 = (bf16[384,2176]{1,0:T(8,128)(2,1)}, bf16[384,2176]{1,0:T(8,128)(2,1)}, u32[]{:S(2)}, u32[]{:S(2)}) collective-permute-start(bf16[384,2176]{1,0:T(8,128)(2,1)} %add_convert_fusion.3), channel_id=1, source_target_pairs={{0,8},{4,12},{8,0},{12,4},{16,24},{20,28},{24,16},{28,20},{1,9},{5... | collective-permute-start | bytes 5013512 | tf_op jit(solution)/shard_map/ppermute | solution.py:37
  505.3 128.2 %collective-permute-start.45 = (bf16[512,4224]{1,0:T(8,128)(2,1)}, bf16[512,4224]{1,0:T(8,128)(2,1)}, u32[]{:S(2)}, u32[]{:S(2)}) collective-permute-start(bf16[512,4224]{1,0:T(8,128)(2,1)} %get-tuple-element.131), channel_id=1, source_target_pairs={{0,16},{4,20},{8,24},{12,28},{16,0},{20,4},{24,8},{28,12},{1,17},{... | collective-permute-start | bytes 12976136 | tf_op jit(solution)/shard_map/ppermute | solution.py:37
  520.9 108.6 %collective-permute-start.44 = (bf16[384,2048]{1,0:T(8,128)(2,1)}, bf16[384,2048]{1,0:T(8,128)(2,1)}, u32[]{:S(2)}, u32[]{:S(2)}) collective-permute-start(bf16[384,2048]{1,0:T(8,128)(2,1)} %add_convert_fusion.4), channel_id=1, source_target_pairs={{0,8},{4,12},{8,0},{12,4},{16,24},{20,28},{24,16},{28,20},{1,9},{5... | collective-permute-start | bytes 4718600 | tf_op jit(solution)/shard_map/ppermute | solution.py:37
  582.5 37.8 %collective-permute-start.42 = (bf16[2,64,2048]{2,1,0:T(8,128)(2,1)S(1)}, bf16[2,64,2048]{2,1,0:T(8,128)(2,1)S(1)}, u32[]{:S(2)}, u32[]{:S(2)}) collective-permute-start(bf16[2,64,2048]{2,1,0:T(8,128)(2,1)S(1)} %bitcast.437), channel_id=1, source_target_pairs={{0,2},{1,3},{2,0},{3,1},{4,6},{5,7},{6,4},{7,5},{8,10},{9,11},{10,... | collective-permute-start | bytes 1572872 | tf_op jit(solution)/shard_map/ppermute | solution.py:37
  585.4 44.1 %collective-permute-start.43 = (bf16[2,64,2048]{2,1,0:T(8,128)(2,1)S(1)}, bf16[2,64,2048]{2,1,0:T(8,128)(2,1)S(1)}, u32[]{:S(2)}, u32[]{:S(2)}) collective-permute-start(bf16[2,64,2048]{2,1,0:T(8,128)(2,1)S(1)} %bitcast.438), channel_id=1, source_target_pairs={{0,3},{1,2},{2,1},{3,0},{4,7},{5,6},{6,5},{7,4},{8,11},{9,10},{10,... | collective-permute-start | bytes 1572872 | tf_op jit(solution)/shard_map/ppermute | solution.py:37
  640.3 265.1 %reduce-scatter.5.cloned.1.call-start = ((), (), s32[]{:S(2)}) async-start(), calls=%async_computation.7 | async-start | bytes 14155776 | tf_op jit(solution)/shard_map/reduce_scatter | solution.py:779
  664.6 125.6 %collective-permute-start.53 = (bf16[512,4224]{1,0:T(8,128)(2,1)}, bf16[512,4224]{1,0:T(8,128)(2,1)}, u32[]{:S(2)}, u32[]{:S(2)}) collective-permute-start(bf16[512,4224]{1,0:T(8,128)(2,1)} %get-tuple-element.171), channel_id=1, source_target_pairs={{0,16},{4,20},{8,24},{12,28},{16,0},{20,4},{24,8},{28,12},{1,17},{... | collective-permute-start | bytes 12976136 | tf_op jit(solution)/shard_map/ppermute | solution.py:37
  665.8 125.3 %collective-permute-start.52 = (bf16[512,4224]{1,0:T(8,128)(2,1)}, bf16[512,4224]{1,0:T(8,128)(2,1)}, u32[]{:S(2)}, u32[]{:S(2)}) collective-permute-start(bf16[512,4224]{1,0:T(8,128)(2,1)} %add_convert_fusion.1), channel_id=1, source_target_pairs={{0,8},{4,12},{8,0},{12,4},{16,24},{20,28},{24,16},{28,20},{1,9},{5... | collective-permute-start | bytes 12976136 | tf_op jit(solution)/shard_map/ppermute | solution.py:37
  709.4 40.2 %collective-permute-start.50 = (bf16[2,64,2176]{2,1,0:T(8,128)(2,1)}, bf16[2,64,2176]{2,1,0:T(8,128)(2,1)}, u32[]{:S(2)}, u32[]{:S(2)}) collective-permute-start(bf16[2,64,2176]{2,1,0:T(8,128)(2,1)} %get-tuple-element.234), channel_id=1, source_target_pairs={{0,2},{1,3},{2,0},{3,1},{4,6},{5,7},{6,4},{7,5},{8,10},{9,11},{10,... | collective-permute-start | bytes 1671176 | tf_op jit(solution)/shard_map/ppermute | solution.py:37
  712.3 44.7 %collective-permute-start.51 = (bf16[2,64,2176]{2,1,0:T(8,128)(2,1)S(1)}, bf16[2,64,2176]{2,1,0:T(8,128)(2,1)}, u32[]{:S(2)}, u32[]{:S(2)}) collective-permute-start(bf16[2,64,2176]{2,1,0:T(8,128)(2,1)S(1)} %get-tuple-element.233), channel_id=1, source_target_pairs={{0,3},{1,2},{2,1},{3,0},{4,7},{5,6},{6,5},{7,4},{8,11},{9,10},{10,... | collective-permute-start | bytes 1671176 | tf_op jit(solution)/shard_map/ppermute | solution.py:37
  914.7 43.8 %collective-permute-start.63 = (bf16[256,512]{1,0:T(8,128)(2,1)}, bf16[256,512]{1,0:T(8,128)(2,1)}, u32[]{:S(2)}, u32[]{:S(2)}) collective-permute-start(bf16[256,512]{1,0:T(8,128)(2,1)} %get-tuple-element.248), channel_id=1, source_target_pairs={{0,0},{2,1},{1,2},{3,3},{4,4},{6,5},{5,6},{7,7},{8,8},{10,9},{9,10... | collective-permute-start | bytes 786440 | tf_op jit(solution)/shard_map/ppermute | solution.py:840
  918.1 40.4 %collective-permute-start.64 = (bf16[256,512]{1,0:T(8,128)(2,1)}, bf16[256,512]{1,0:T(8,128)(2,1)}, u32[]{:S(2)}, u32[]{:S(2)}) collective-permute-start(bf16[256,512]{1,0:T(8,128)(2,1)} %get-tuple-element.249), channel_id=1, source_target_pairs={{1,0},{3,1},{0,2},{2,3},{5,4},{7,5},{4,6},{6,7},{9,8},{11,9},{8,10... | collective-permute-start | bytes 786440 | tf_op jit(solution)/shard_map/ppermute | solution.py:843
  (158 other events, 2051.4 us)
Sparse Core Ops, SparseCore 0:
  90.4 81.2 all-gather.2
  174.1 65.9 all-gather.4
  640.5 104.2 reduce-scatter.2
  798.2 107.1 reduce-scatter.4

commit v13 on v12

--- a/solution.py
+++ b/solution.py
@@ -754,12 +754,11 @@
     back_one = scatter_rows(
         jnp.concatenate([hidden_one_part, slot_part_one.astype(bf16)], axis=1)
     )
-    back_one, other_sum, keep_got = lax.optimization_barrier(
-        (back_one, other_sum, keep_got, joint_part_grad)
-    )[:3]
+    joint_part_grad, other_sum, keep_got = lax.optimization_barrier(
+        (joint_part_grad, other_sum, keep_got)
+    )
     out_own = lax.psum_scatter(out_part, "dp", scatter_dimension=0, tiled=True)
     out_grad = slots_of(after(out_own, back_one))
-    back_one, out_grad = lax.optimization_barrier((back_one, out_grad))
     hidden_one_grad, slot_one_grad = back_one[:, :width], back_one[:, width : width + slots]
 
     def own(value):
@@ -778,9 +777,7 @@
     def reduced(value):
         return lax.psum_scatter(value, "dp", scatter_dimension=0, tiled=True)
 
-    in_low, keep_got, other_sum = lax.optimization_barrier(
-        (in_home.astype(bf16), keep_got, other_sum)
-    )
+    in_low = in_home.astype(bf16)
     joint_own = reduced(joint_part_grad)
 
     results = jnp.stack([out_home, in_low]).reshape(2, micro, tok_rows, width)
@@ -803,7 +800,6 @@
     small = jnp.broadcast_to(small[None], (dp_count,) + small.shape)
     results = jnp.concatenate([results, small], axis=1)
     results = lax.all_to_all(results, "dp", split_axis=0, concat_axis=0, tiled=True)
-    results, joint_own = lax.optimization_barrier((results, joint_own))
     query_own, kv_own = joint_own[:, :query_width], joint_own[:, query_width:]
     small = results[:, sent_back:].astype(f32)
     results = results[:, :sent_back].reshape(dp_count, 2 * micro, piece_rows, width)

time: 975 us -> 967 us (level)
  local copies, waits for them, and re-layouts: 102 us -> 84.8 us
  waiting for transfers between devices: 424 us -> 436 us
    all_to_all x1, waiting for transfers between devices: 8.31 us -> 28 us  [local(): lax.all_to_all(results, 'dp', split_axis=0, concat_axis=0, tiled=True)]
    reduce_scatter x1, waiting for transfers between devices: 25.7 us -> 15.7 us  [reduced(): return lax.psum_scatter(value, 'dp', scatter_dimension=0, tiled=True)]
    unnamed x256 -> x210, local copies, waits for them, and re-layouts: 24.5 us -> 24.8 us
  transfers between devices with their start and end apart: 72 -> 72, of which waited for: 37 -> 35; matrix products, arithmetic and copies ran while one was open for 24% -> 23% of each run, Pallas kernels for 13% -> 13%
where the time goes in v13:
time: 967 us; the launch traced here: 960 us
  waiting for transfers between devices  436 us (45%)
  Pallas kernels  166 us (17%)
  other arithmetic  97.9 us (10%)
  local copies, waits for them, and re-layouts  84.8 us (9%)
  starting transfers between devices  81.6 us (8%)
  matrix products  75.9 us (8%)
  between operations  16.9 us (2%)
    ppermute x62, waiting for transfers between devices, swap(): return lax.ppermute(value, axis, [(i, i ^ step) for i in range(count)])  375 us
    pallas_call x2, Pallas kernels, expert_rows(): pl.pallas_call(expert_kernel, grid_spec=pltpu.PrefetchScalarGridSpec(num_...  81.7 us
    ppermute x62, starting transfers between devices, swap(): return lax.ppermute(value, axis, [(i, i ^ step) for i in range(count)])  62.8 us
    pallas_call x2, Pallas kernels, expert_grads(): pl.pallas_call(functools.partial(expert_grad_kernel, cuts), grid_spec=plt...  49.8 us
    all_to_all x1, waiting for transfers between devices, local(): lax.all_to_all(results, 'dp', split_axis=0, concat_axis=0, tiled=True)  28 us
    unnamed x210, local copies, waits for them, and re-layouts  24.8 us
    dot_general x5, matrix products, dot(): return jnp.dot(left, right, preferred_element_type=f32)  23.8 us
    dot_general x5, matrix products, dot_t(): lax.dot_general(left, right, (((1,), (1,)), ((), ())), preferred_element_...  21.8 us
  transfers between devices with their start and end apart: 72, of which 35 were waited for; matrix products, arithmetic and copies ran while one was open for 23% of the time, Pallas kernels for 13%

profile of v13, /device:TPU:8, one launch (start us, length us, event | category | flops | bytes accessed | tf_op | source)
XLA Modules:
  0.0 959.7 jit_solution(7876439428636370387)
XLA Ops:
  49.1 38.6 %collective-permute-done.12 = bf16[256,1024]{1,0:T(8,128)(2,1)S(1)} collective-permute-done((bf16[256,1024]{1,0:T(8,128)(2,1)}, bf16[256,1024]{1,0:T(8,128)(2,1)S(1)}, u32[]{:S(2)}, u32[]{:S(2)}) %collective-permute-start.12) | collective-permute-done | bytes 524320 | tf_op jit(solution)/shard_map/ppermute | solution.py:37
  104.4 16.1 %all-to-all-done = bf16[8,4,8,2048]{3,2,1,0:T(8,128)(2,1)S(1)} async-done(((bf16[8,4,8,2048]{3,2,1,0:T(8,128)(2,1)}), bf16[8,4,8,2048]{3,2,1,0:T(8,128)(2,1)S(1)}, u32[]{:S(2)}, u32[]{:S(2)}) %all-to-all-start) | async-done | bytes 1048608 | tf_op jit(solution)/shard_map/all_to_all | solution.py:476
  145.5 10.9 %collective-permute-done.9 = bf16[2,48,2048]{2,1,0:T(8,128)(2,1)} collective-permute-done((bf16[2,48,2048]{2,1,0:T(8,128)(2,1)}, bf16[2,48,2048]{2,1,0:T(8,128)(2,1)}, u32[]{:S(2)}, u32[]{:S(2)}) %collective-permute-start.9) | collective-permute-done | bytes 393248 | tf_op jit(solution)/shard_map/ppermute | solution.py:37
  156.4 33.0 %collective-permute-done.10 = bf16[2,48,2048]{2,1,0:T(8,128)(2,1)} collective-permute-done((bf16[2,48,2048]{2,1,0:T(8,128)(2,1)}, bf16[2,48,2048]{2,1,0:T(8,128)(2,1)}, u32[]{:S(2)}, u32[]{:S(2)}) %collective-permute-start.10) | collective-permute-done | bytes 393248 | tf_op jit(solution)/shard_map/ppermute | solution.py:37
  198.7 12.3 %collective-permute-done.7 = bf16[2,64,2048]{2,1,0:T(8,128)(2,1)S(1)} collective-permute-done((bf16[2,64,2048]{2,1,0:T(8,128)(2,1)S(1)}, bf16[2,64,2048]{2,1,0:T(8,128)(2,1)S(1)}, u32[]{:S(2)}, u32[]{:S(2)}) %collective-permute-start.7) | collective-permute-done | bytes 524320 | tf_op jit(solution)/shard_map/ppermute | solution.py:37
  226.8 14.8 %attention_forward.1 = (bf16[512,2048]{1,0:T(8,128)(2,1)S(1)}, bf16[512,2048]{1,0:T(8,128)(2,1)}, bf16[512,2048]{1,0:T(8,128)(2,1)}, bf16[512,512]{1,0:T(8,128)(...) custom-call(s32[2]{0:T(128)S(1)} %fusion.133.lens, f32[512,2048]{1,0:T(8,128)} %fusion.2.query, ...), custom_call_target="tpu_custom_call" | custom-call | flops 1073741824 | bytes 14680064 | tf_op jit(solution)/shard_map/attention_forward/pallas_call | solution.py:181
  250.6 23.0 %collective-permute-done.16.refs_2_ = bf16[256,4224]{1,0:T(8,128)(2,1)} collective-permute-done((bf16[256,4224]{1,0:T(8,128)(2,1)}, bf16[256,4224]{1,0:T(8,128)(2,1)}, u32[]{:S(2)}, u32[]{:S(2)}) %collective-permute-start.16) | collective-permute-done | bytes 2162720 | tf_op jit(solution)/shard_map/ppermute | solution.py:37
  279.4 16.4 %collective-permute-done.18 = bf16[2,64,2048]{2,1,0:T(8,128)(2,1)} collective-permute-done((bf16[2,64,2048]{2,1,0:T(8,128)(2,1)}, bf16[2,64,2048]{2,1,0:T(8,128)(2,1)}, u32[]{:S(2)}, u32[]{:S(2)}) %collective-permute-start.18) | collective-permute-done | bytes 524320 | tf_op jit(solution)/shard_map/ppermute | solution.py:37
  295.8 17.1 %collective-permute-done.19 = bf16[2,64,2048]{2,1,0:T(8,128)(2,1)} collective-permute-done((bf16[2,64,2048]{2,1,0:T(8,128)(2,1)}, bf16[2,64,2048]{2,1,0:T(8,128)(2,1)}, u32[]{:S(2)}, u32[]{:S(2)}) %collective-permute-start.19) | collective-permute-done | bytes 524320 | tf_op jit(solution)/shard_map/ppermute | solution.py:37
  312.9 10.0 %collective-permute-done.20 = bf16[2,64,2048]{2,1,0:T(8,128)(2,1)} collective-permute-done((bf16[2,64,2048]{2,1,0:T(8,128)(2,1)S(1)}, bf16[2,64,2048]{2,1,0:T(8,128)(2,1)}, u32[]{:S(2)}, u32[]{:S(2)}) %collective-permute-start.20) | collective-permute-done | bytes 524320 | tf_op jit(solution)/shard_map/ppermute | solution.py:37
  334.9 10.7 %collective-permute-done.22 = bf16[2,48,2176]{2,1,0:T(8,128)(2,1)S(1)} collective-permute-done((bf16[2,48,2176]{2,1,0:T(8,128)(2,1)S(1)}, bf16[2,48,2176]{2,1,0:T(8,128)(2,1)S(1)}, u32[]{:S(2)}, u32[]{:S(2)}) %collective-permute-start.22) | collective-permute-done | bytes 417824 | tf_op jit(solution)/shard_map/ppermute | solution.py:37
  345.6 16.7 %collective-permute-done.23 = bf16[2,48,2176]{2,1,0:T(8,128)(2,1)S(1)} collective-permute-done((bf16[2,48,2176]{2,1,0:T(8,128)(2,1)S(1)}, bf16[2,48,2176]{2,1,0:T(8,128)(2,1)S(1)}, u32[]{:S(2)}, u32[]{:S(2)}) %collective-permute-start.23) | collective-permute-done | bytes 417824 | tf_op jit(solution)/shard_map/ppermute | solution.py:37
  378.2 40.9 %expert_rows.2 = (bf16[768,2048]{1,0:T(8,128)(2,1)}, bf16[768,2176]{1,0:T(8,128)(2,1)}, bf16[768,1408]{1,0:T(8,128)(2,1)}, bf16[768,2816]{1,0:T(8,128)(2,1)}) custom-call(s32[2]{0:T(128)} %pad_add_fusion.1.place_ref, bf16[768,2176]{1,0:T(8,128)(2,1)} %pad_maximum_fusion.2.hidden.refs_0_.refs_4_, bf16[768,2048]{1,0:T(8,128)(2,1)} %copy-done.48, ...), custom_call_target="tpu_custom_call" | custom-call | flops 26575110144 | bytes 36175872 | tf_op jit(solution)/shard_map/expert_rows/pallas_call | solution.py:332
  425.0 40.7 %expert_rows.3 = (bf16[768,2048]{1,0:T(8,128)(2,1)}, bf16[768,2176]{1,0:T(8,128)(2,1)}, bf16[768,1408]{1,0:T(8,128)(2,1)}, bf16[768,2816]{1,0:T(8,128)(2,1)}) custom-call(s32[2]{0:T(128)} %pad_add_fusion.1.place_ref, bf16[768,2176]{1,0:T(8,128)(2,1)} %copy-done.46, bf16[768,2048]{1,0:T(8,128)(2,1)} %copy-done.47, ...), custom_call_target="tpu_custom_call" | custom-call | flops 26575110144 | bytes 36175872 | tf_op jit(solution)/shard_map/expert_rows/pallas_call | solution.py:332
  482.7 24.9 %expert_grads.2 = (bf16[512,4224]{1,0:T(8,128)(2,1)}, bf16[512,4224]{1,0:T(8,128)(2,1)}) custom-call(s32[4]{0:T(128)} %get-tuple-element.292.order, bf16[768,2176]{1,0:T(8,128)(2,1)} %pad_maximum_fusion.2.hidden.refs_0_.refs_4_, bf16[768,2176]{1,0:T(8,128)(2,1)} %copy-done.46, bf16[768,2048]{1,0:T(8,128)(2,1)} %copy-done.48, bf16[768,2048]{1,0:T(8,128)(2,1)} %copy-done.47, ...), custom_call_target="tpu_custom_call" | custom-call | flops 13287555072 | bytes 27918336 | tf_op jit(solution)/shard_map/expert_grads/pallas_call | solution.py:405
  527.7 25.0 %expert_grads.3 = (bf16[512,4224]{1,0:T(8,128)(2,1)}, bf16[512,4224]{1,0:T(8,128)(2,1)}) custom-call(s32[4]{0:T(128)} %get-tuple-element.293.order, bf16[768,2176]{1,0:T(8,128)(2,1)} %pad_maximum_fusion.2.hidden.refs_0_.refs_4_, bf16[768,2176]{1,0:T(8,128)(2,1)} %copy-done.46, bf16[768,2048]{1,0:T(8,128)(2,1)} %copy-done.48, bf16[768,2048]{1,0:T(8,128)(2,1)} %copy-done.47, ...), custom_call_target="tpu_custom_call" | custom-call | flops 13287555072 | bytes 27918336 | tf_op jit(solution)/shard_map/expert_grads/pallas_call | solution.py:405
  555.2 8.0 collective-permute-done.40
  576.7 15.6 %collective-permute-done.41 = bf16[2,64,2048]{2,1,0:T(8,128)(2,1)S(1)} collective-permute-done((bf16[2,64,2048]{2,1,0:T(8,128)(2,1)S(1)}, bf16[2,64,2048]{2,1,0:T(8,128)(2,1)S(1)}, u32[]{:S(2)}, u32[]{:S(2)}) %collective-permute-start.41) | collective-permute-done | bytes 524320 | tf_op jit(solution)/shard_map/ppermute | solution.py:37
  592.3 18.3 %collective-permute-done.42 = bf16[2,64,2048]{2,1,0:T(8,128)(2,1)S(1)} collective-permute-done((bf16[2,64,2048]{2,1,0:T(8,128)(2,1)S(1)}, bf16[2,64,2048]{2,1,0:T(8,128)(2,1)S(1)}, u32[]{:S(2)}, u32[]{:S(2)}) %collective-permute-start.42) | collective-permute-done | bytes 524320 | tf_op jit(solution)/shard_map/ppermute | solution.py:37
  610.6 9.1 collective-permute-done.43
  630.8 10.8 %fusion.180.vals_grad = f32[512,2048]{1,0:T(8,128)} fusion(bf16[512,2048]{1,0:T(8,128)(2,1)} %bitcast.431, bf16[2048,2048]{1,0:T(8,128)(2,1)} %all-gather.5.cloned.1.call-done), kind=kOutput, calls=%fused_computation.454 | convolution fusion | flops 4294967296 | bytes 14680064 | tf_op jit(solution)/shard_map/dot_general | solution.py:24
  641.6 8.1 add_convert_fusion.1
  655.9 20.1 %attention_backward.1 = (bf16[512,2048]{1,0:T(8,128)(2,1)S(1)}, bf16[512,512]{1,0:T(8,128)(2,1)S(1)}, bf16[512,512]{1,0:T(8,128)(2,1)S(1)}, f32[512,128]{1,0:T(8,128)S(1)}) custom-call(s32[2]{0:T(128)S(1)} %fusion.133.lens, bf16[512,2048]{1,0:T(8,128)(2,1)} %get-tuple-element.151.query, bf16[512,512]{1,0:T(8,128)(2,1)S(1)} %get-tuple-element.152.key, ...), custom_call_target="tpu_custom_call" | custom-call | flops 2684354560 | bytes 14680064 | tf_op jit(solution)/shard_map/attention_backward/pallas_call | solution.py:212
  689.2 8.4 add_convert_fusion.2
  704.5 11.6 %collective-permute-done.49 = bf16[2,64,2176]{2,1,0:T(8,128)(2,1)S(1)} collective-permute-done((bf16[2,64,2176]{2,1,0:T(8,128)(2,1)S(1)}, bf16[2,64,2176]{2,1,0:T(8,128)(2,1)S(1)}, u32[]{:S(2)}, u32[]{:S(2)}) %collective-permute-start.49) | collective-permute-done | bytes 557088 | tf_op jit(solution)/shard_map/ppermute | solution.py:37
  716.1 21.8 %collective-permute-done.50 = bf16[2,64,2176]{2,1,0:T(8,128)(2,1)S(1)} collective-permute-done((bf16[2,64,2176]{2,1,0:T(8,128)(2,1)S(1)}, bf16[2,64,2176]{2,1,0:T(8,128)(2,1)S(1)}, u32[]{:S(2)}, u32[]{:S(2)}) %collective-permute-start.50) | collective-permute-done | bytes 557088 | tf_op jit(solution)/shard_map/ppermute | solution.py:37
  757.3 11.9 %convolution_convert_fusion = bf16[2048,3072]{1,0:T(8,128)(2,1)} fusion(bf16[512,2048]{1,0:T(8,128)(2,1)} %bitcast.417, bf16[512,512]{1,0:T(8,128)(2,1)S(1)} %copy-done.5, bf16[512,512]{1,0:T(8,128)(2,1)S(1)} %get-tuple-element.160, bf16[512,2048]{1,0:T(8,128)(2,1)S(1)} %copy-done.3), kind=kOutput, calls=%fused_computation | convolution fusion | flops 6458179584 | bytes 17825792 | tf_op jit(solution)/shard_map/dot_general | solution.py:32
  769.2 28.0 %all-to-all-done.1 = bf16[8,48,2048]{2,1,0:T(8,128)(2,1)} async-done(((bf16[8,48,2048]{2,1,0:T(8,128)(2,1)}), bf16[8,48,2048]{2,1,0:T(8,128)(2,1)}, u32[]{:S(2)}, u32[]{:S(2)}) %all-to-all-start.1) | async-done | bytes 1572896 | tf_op jit(solution)/shard_map/all_to_all | solution.py:802
  855.8 8.5 convert_element_type.342
  866.3 16.3 %collective-permute-done.61 = bf16[256,512]{1,0:T(8,128)(2,1)S(1)} collective-permute-done((bf16[256,512]{1,0:T(8,128)(2,1)S(1)}, bf16[256,512]{1,0:T(8,128)(2,1)S(1)}, u32[]{:S(2)}, u32[]{:S(2)}) %collective-permute-start.61) | collective-permute-done | bytes 262176 | tf_op jit(solution)/shard_map/ppermute | solution.py:37
  891.2 15.7 %reduce-scatter.3.cloned.1.call-done = bf16[256,3072]{1,0:T(8,128)(2,1)} async-done(((bf16[2048,3072]{1,0:T(8,128)(2,1)}), bf16[256,3072]{1,0:T(8,128)(2,1)}) %reduce-scatter.3.cloned.1.call-update) | async-done | bytes 1572880 | tf_op jit(solution)/shard_map/reduce_scatter | solution.py:778
  920.4 24.8 %collective-permute-done.58 = bf16[256,512]{1,0:T(8,128)(2,1)S(1)} collective-permute-done((bf16[256,512]{1,0:T(8,128)(2,1)S(1)}, bf16[256,512]{1,0:T(8,128)(2,1)S(1)}, u32[]{:S(2)}, u32[]{:S(2)}) %collective-permute-start.58) | collective-permute-done | bytes 262176 | tf_op jit(solution)/shard_map/ppermute | solution.py:37
  (598 shorter events, 354.5 us)
Async XLA Ops:
  7.2 205.3 %all-gather.3.cloned.1.call-start = ((), (), s32[]{:S(2)}) async-start(), calls=%async_computation.4 | async-start | bytes 14155776 | tf_op jit(solution)/shard_map/all_gather | solution.py:552
  14.3 76.1 %collective-permute-start.1 = (bf16[256,4224]{1,0:T(8,128)(2,1)}, bf16[256,4224]{1,0:T(8,128)(2,1)}, u32[]{:S(2)}, u32[]{:S(2)}) collective-permute-start(bf16[256,4224]{1,0:T(8,128)(2,1)} %pad_maximum_fusion.5), channel_id=1, source_target_pairs={{0,8},{4,12},{8,0},{12,4},{16,24},{20,28},{24,16},{28,20},{1,9},{5... | collective-permute-start | bytes 6488072 | tf_op jit(solution)/shard_map/ppermute | solution.py:37
  17.3 73.1 %collective-permute-start.3 = (bf16[256,4224]{1,0:T(8,128)(2,1)}, bf16[256,4224]{1,0:T(8,128)(2,1)}, u32[]{:S(2)}, u32[]{:S(2)}) collective-permute-start(bf16[256,4224]{1,0:T(8,128)(2,1)} %pad_maximum_fusion.4), channel_id=1, source_target_pairs={{0,16},{4,20},{8,24},{12,28},{16,0},{20,4},{24,8},{28,12},{1,17},{... | collective-permute-start | bytes 6488072 | tf_op jit(solution)/shard_map/ppermute | solution.py:37
  43.1 44.7 %collective-permute-start.13 = (bf16[256,1024]{1,0:T(8,128)(2,1)}, bf16[256,1024]{1,0:T(8,128)(2,1)S(1)}, u32[]{:S(2)}, u32[]{:S(2)}) collective-permute-start(bf16[256,1024]{1,0:T(8,128)(2,1)} %pad_maximum_fusion.15), channel_id=1, source_target_pairs={{0,3},{1,2},{2,1},{3,0},{4,7},{5,6},{6,5},{7,4},{8,11},{9,10},{10,... | collective-permute-start | bytes 1572872 | tf_op jit(solution)/shard_map/ppermute | solution.py:37
  44.4 43.3 %collective-permute-start.12 = (bf16[256,1024]{1,0:T(8,128)(2,1)}, bf16[256,1024]{1,0:T(8,128)(2,1)S(1)}, u32[]{:S(2)}, u32[]{:S(2)}) collective-permute-start(bf16[256,1024]{1,0:T(8,128)(2,1)} %pad_maximum_fusion.14), channel_id=1, source_target_pairs={{0,2},{1,3},{2,0},{3,1},{4,6},{5,7},{6,4},{7,5},{8,10},{9,11},{10,... | collective-permute-start | bytes 1572872 | tf_op jit(solution)/shard_map/ppermute | solution.py:37
  90.4 152.6 %all-gather.5.cloned.1.call-start = ((), (), s32[]{:S(2)}) async-start(), calls=%async_computation.5 | async-start | bytes 9437184 | tf_op jit(solution)/shard_map/all_gather | solution.py:553
  91.1 41.7 %collective-permute-start = (bf16[256,4224]{1,0:T(8,128)(2,1)}, bf16[256,4224]{1,0:T(8,128)(2,1)}, u32[]{:S(2)}, u32[]{:S(2)}) collective-permute-start(bf16[256,4224]{1,0:T(8,128)(2,1)} %pad_maximum_fusion.4), channel_id=1, source_target_pairs={{0,4},{4,0},{8,12},{12,8},{16,20},{20,16},{24,28},{28,24},{1,5},{5... | collective-permute-start | bytes 6488072 | tf_op jit(solution)/shard_map/ppermute | solution.py:37
  96.0 751.8 %reduce-scatter.5.cloned.1.call-start = ((), (), s32[]{:S(2)}) async-start(), calls=%async_computation.7 | async-start | bytes 9437184 | tf_op jit(solution)/shard_map/reduce_scatter | solution.py:760
  132.8 56.6 %collective-permute-start.10 = (bf16[2,48,2048]{2,1,0:T(8,128)(2,1)}, bf16[2,48,2048]{2,1,0:T(8,128)(2,1)}, u32[]{:S(2)}, u32[]{:S(2)}) collective-permute-start(bf16[2,48,2048]{2,1,0:T(8,128)(2,1)} %get-tuple-element.242), channel_id=1, source_target_pairs={{0,3},{1,2},{2,1},{3,0},{4,7},{5,6},{6,5},{7,4},{8,11},{9,10},{10,... | collective-permute-start | bytes 1179656 | tf_op jit(solution)/shard_map/ppermute | solution.py:37
  134.5 57.7 %collective-permute-start.5 = (bf16[2,64,2048]{2,1,0:T(8,128)(2,1)S(1)}, bf16[2,64,2048]{2,1,0:T(8,128)(2,1)}, u32[]{:S(2)}, u32[]{:S(2)}) collective-permute-start(bf16[2,64,2048]{2,1,0:T(8,128)(2,1)S(1)} %bitcast.432), channel_id=1, source_target_pairs={{0,1},{1,0},{2,3},{3,2},{4,5},{5,4},{6,7},{7,6},{8,9},{9,8},{10,11... | collective-permute-start | bytes 1572872 | tf_op jit(solution)/shard_map/ppermute | solution.py:37
  137.5 61.1 %collective-permute-start.6 = (bf16[2,64,2048]{2,1,0:T(8,128)(2,1)S(1)}, bf16[2,64,2048]{2,1,0:T(8,128)(2,1)S(1)}, u32[]{:S(2)}, u32[]{:S(2)}) collective-permute-start(bf16[2,64,2048]{2,1,0:T(8,128)(2,1)S(1)} %bitcast.433), channel_id=1, source_target_pairs={{0,2},{1,3},{2,0},{3,1},{4,6},{5,7},{6,4},{7,5},{8,10},{9,11},{10,... | collective-permute-start | bytes 1572872 | tf_op jit(solution)/shard_map/ppermute | solution.py:37
  212.5 61.1 %collective-permute-start.16 = (bf16[256,4224]{1,0:T(8,128)(2,1)}, bf16[256,4224]{1,0:T(8,128)(2,1)}, u32[]{:S(2)}, u32[]{:S(2)}) collective-permute-start(bf16[256,4224]{1,0:T(8,128)(2,1)} %get-tuple-element.100.refs_0_), channel_id=1, source_target_pairs={{0,16},{4,20},{8,24},{12,28},{16,0},{20,4},{24,8},{28,12},{1,17},{... | collective-permute-start | bytes 6488072 | tf_op jit(solution)/shard_map/ppermute | solution.py:37
  213.1 60.5 %collective-permute-start.17 = (bf16[256,4224]{1,0:T(8,128)(2,1)}, bf16[256,4224]{1,0:T(8,128)(2,1)}, u32[]{:S(2)}, u32[]{:S(2)}) collective-permute-start(bf16[256,4224]{1,0:T(8,128)(2,1)} %get-tuple-element.101), channel_id=1, source_target_pairs={{0,8},{4,12},{8,0},{12,4},{16,24},{20,28},{24,16},{28,20},{1,9},{5... | collective-permute-start | bytes 6488072 | tf_op jit(solution)/shard_map/ppermute | solution.py:37
  213.7 111.2 %collective-permute-start.21 = (bf16[256,4224]{1,0:T(8,128)(2,1)}, bf16[256,4224]{1,0:T(8,128)(2,1)}, u32[]{:S(2)}, u32[]{:S(2)}) collective-permute-start(bf16[256,4224]{1,0:T(8,128)(2,1)} %collective-permute-done.1), channel_id=1, source_target_pairs={{0,16},{4,20},{8,24},{12,28},{16,0},{20,4},{24,8},{28,12},{1,17},{... | collective-permute-start | bytes 6488072 | tf_op jit(solution)/shard_map/ppermute | solution.py:37
  275.8 37.2 %collective-permute-start.19 = (bf16[2,64,2048]{2,1,0:T(8,128)(2,1)}, bf16[2,64,2048]{2,1,0:T(8,128)(2,1)}, u32[]{:S(2)}, u32[]{:S(2)}) collective-permute-start(bf16[2,64,2048]{2,1,0:T(8,128)(2,1)} %get-tuple-element.213), channel_id=1, source_target_pairs={{0,2},{1,3},{2,0},{3,1},{4,6},{5,7},{6,4},{7,5},{8,10},{9,11},{10,... | collective-permute-start | bytes 1572872 | tf_op jit(solution)/shard_map/ppermute | solution.py:37
  277.8 45.2 %collective-permute-start.20 = (bf16[2,64,2048]{2,1,0:T(8,128)(2,1)S(1)}, bf16[2,64,2048]{2,1,0:T(8,128)(2,1)}, u32[]{:S(2)}, u32[]{:S(2)}) collective-permute-start(bf16[2,64,2048]{2,1,0:T(8,128)(2,1)S(1)} %get-tuple-element.212), channel_id=1, source_target_pairs={{0,3},{1,2},{2,1},{3,0},{4,7},{5,6},{6,5},{7,4},{8,11},{9,10},{10,... | collective-permute-start | bytes 1572872 | tf_op jit(solution)/shard_map/ppermute | solution.py:37
  278.5 90.6 %collective-permute-start.25 = (bf16[256,4224]{1,0:T(8,128)(2,1)}, bf16[256,4224]{1,0:T(8,128)(2,1)}, u32[]{:S(2)}, u32[]{:S(2)}) collective-permute-start(bf16[256,4224]{1,0:T(8,128)(2,1)} %collective-permute-done.17.refs_1_), channel_id=1, source_target_pairs={{0,16},{4,20},{8,24},{12,28},{16,0},{20,4},{24,8},{28,12},{1,17},{... | collective-permute-start | bytes 6488072 | tf_op jit(solution)/shard_map/ppermute | solution.py:37
  325.2 37.1 %collective-permute-start.29 = (bf16[384,2048]{1,0:T(8,128)(2,1)}, bf16[384,2048]{1,0:T(8,128)(2,1)}, u32[]{:S(2)}, u32[]{:S(2)}) collective-permute-start(bf16[384,2048]{1,0:T(8,128)(2,1)} %bitcast.27), channel_id=1, source_target_pairs={{0,8},{4,12},{8,0},{12,4},{16,24},{20,28},{24,16},{28,20},{1,9},{5... | collective-permute-start | bytes 4718600 | tf_op jit(solution)/shard_map/ppermute | solution.py:37
  373.0 46.2 %collective-permute-start.32 = (bf16[384,2176]{1,0:T(8,128)(2,1)S(1)}, bf16[384,2176]{1,0:T(8,128)(2,1)}, u32[]{:S(2)}, u32[]{:S(2)}) collective-permute-start(bf16[384,2176]{1,0:T(8,128)(2,1)S(1)} %bitcast.421), channel_id=1, source_target_pairs={{0,8},{4,12},{8,0},{12,4},{16,24},{20,28},{24,16},{28,20},{1,9},{5... | collective-permute-start | bytes 5013512 | tf_op jit(solution)/shard_map/ppermute | solution.py:37
  481.2 39.2 %collective-permute-start.31 = (bf16[384,2176]{1,0:T(8,128)(2,1)}, bf16[384,2176]{1,0:T(8,128)(2,1)}, u32[]{:S(2)}, u32[]{:S(2)}) collective-permute-start(bf16[384,2176]{1,0:T(8,128)(2,1)} %split.25), channel_id=1, source_target_pairs={{0,4},{4,0},{8,12},{12,8},{16,20},{20,16},{24,28},{28,24},{1,5},{5... | collective-permute-start | bytes 5013512 | tf_op jit(solution)/shard_map/ppermute | solution.py:37
  481.3 39.1 %collective-permute-start.35 = (bf16[384,2176]{1,0:T(8,128)(2,1)}, bf16[384,2176]{1,0:T(8,128)(2,1)}, u32[]{:S(2)}, u32[]{:S(2)}) collective-permute-start(bf16[384,2176]{1,0:T(8,128)(2,1)} %add_convert_fusion.3), channel_id=1, source_target_pairs={{0,8},{4,12},{8,0},{12,4},{16,24},{20,28},{24,16},{28,20},{1,9},{5... | collective-permute-start | bytes 5013512 | tf_op jit(solution)/shard_map/ppermute | solution.py:37
  507.6 116.2 %collective-permute-start.45 = (bf16[512,4224]{1,0:T(8,128)(2,1)}, bf16[512,4224]{1,0:T(8,128)(2,1)}, u32[]{:S(2)}, u32[]{:S(2)}) collective-permute-start(bf16[512,4224]{1,0:T(8,128)(2,1)} %get-tuple-element.124), channel_id=1, source_target_pairs={{0,16},{4,20},{8,24},{12,28},{16,0},{20,4},{24,8},{28,12},{1,17},{... | collective-permute-start | bytes 12976136 | tf_op jit(solution)/shard_map/ppermute | solution.py:37
  523.1 96.7 %collective-permute-start.44 = (bf16[384,2048]{1,0:T(8,128)(2,1)}, bf16[384,2048]{1,0:T(8,128)(2,1)}, u32[]{:S(2)}, u32[]{:S(2)}) collective-permute-start(bf16[384,2048]{1,0:T(8,128)(2,1)} %add_convert_fusion.4), channel_id=1, source_target_pairs={{0,8},{4,12},{8,0},{12,4},{16,24},{20,28},{24,16},{28,20},{1,9},{5... | collective-permute-start | bytes 4718600 | tf_op jit(solution)/shard_map/ppermute | solution.py:37
  572.8 37.8 %collective-permute-start.42 = (bf16[2,64,2048]{2,1,0:T(8,128)(2,1)S(1)}, bf16[2,64,2048]{2,1,0:T(8,128)(2,1)S(1)}, u32[]{:S(2)}, u32[]{:S(2)}) collective-permute-start(bf16[2,64,2048]{2,1,0:T(8,128)(2,1)S(1)} %bitcast.440), channel_id=1, source_target_pairs={{0,2},{1,3},{2,0},{3,1},{4,6},{5,7},{6,4},{7,5},{8,10},{9,11},{10,... | collective-permute-start | bytes 1572872 | tf_op jit(solution)/shard_map/ppermute | solution.py:37
  575.8 44.0 %collective-permute-start.43 = (bf16[2,64,2048]{2,1,0:T(8,128)(2,1)S(1)}, bf16[2,64,2048]{2,1,0:T(8,128)(2,1)S(1)}, u32[]{:S(2)}, u32[]{:S(2)}) collective-permute-start(bf16[2,64,2048]{2,1,0:T(8,128)(2,1)S(1)} %bitcast.441), channel_id=1, source_target_pairs={{0,3},{1,2},{2,1},{3,0},{4,7},{5,6},{6,5},{7,4},{8,11},{9,10},{10,... | collective-permute-start | bytes 1572872 | tf_op jit(solution)/shard_map/ppermute | solution.py:37
  653.5 149.9 %collective-permute-start.56 = (bf16[512,4224]{1,0:T(8,128)(2,1)}, bf16[512,4224]{1,0:T(8,128)(2,1)}, u32[]{:S(2)}, u32[]{:S(2)}) collective-permute-start(bf16[512,4224]{1,0:T(8,128)(2,1)} %get-tuple-element.166), channel_id=1, source_target_pairs={{0,16},{4,20},{8,24},{12,28},{16,0},{20,4},{24,8},{28,12},{1,17},{... | collective-permute-start | bytes 12976136 | tf_op jit(solution)/shard_map/ppermute | solution.py:37
  654.7 148.7 %collective-permute-start.55 = (bf16[512,4224]{1,0:T(8,128)(2,1)}, bf16[512,4224]{1,0:T(8,128)(2,1)}, u32[]{:S(2)}, u32[]{:S(2)}) collective-permute-start(bf16[512,4224]{1,0:T(8,128)(2,1)} %add_convert_fusion.1), channel_id=1, source_target_pairs={{0,8},{4,12},{8,0},{12,4},{16,24},{20,28},{24,16},{28,20},{1,9},{5... | collective-permute-start | bytes 12976136 | tf_op jit(solution)/shard_map/ppermute | solution.py:37
  698.1 39.9 %collective-permute-start.50 = (bf16[2,64,2176]{2,1,0:T(8,128)(2,1)S(1)}, bf16[2,64,2176]{2,1,0:T(8,128)(2,1)S(1)}, u32[]{:S(2)}, u32[]{:S(2)}) collective-permute-start(bf16[2,64,2176]{2,1,0:T(8,128)(2,1)S(1)} %get-tuple-element.220), channel_id=1, source_target_pairs={{0,2},{1,3},{2,0},{3,1},{4,6},{5,7},{6,4},{7,5},{8,10},{9,11},{10,... | collective-permute-start | bytes 1671176 | tf_op jit(solution)/shard_map/ppermute | solution.py:37
  701.0 44.9 %collective-permute-start.51 = (bf16[2,64,2176]{2,1,0:T(8,128)(2,1)S(1)}, bf16[2,64,2176]{2,1,0:T(8,128)(2,1)S(1)}, u32[]{:S(2)}, u32[]{:S(2)}) collective-permute-start(bf16[2,64,2176]{2,1,0:T(8,128)(2,1)S(1)} %get-tuple-element.219), channel_id=1, source_target_pairs={{0,3},{1,2},{2,1},{3,0},{4,7},{5,6},{6,5},{7,4},{8,11},{9,10},{10,... | collective-permute-start | bytes 1671176 | tf_op jit(solution)/shard_map/ppermute | solution.py:37
  752.0 45.3 %all-to-all-start.1 = ((bf16[8,48,2048]{2,1,0:T(8,128)(2,1)}), bf16[8,48,2048]{2,1,0:T(8,128)(2,1)}, u32[]{:S(2)}, u32[]{:S(2)}) async-start(bf16[8,48,2048]{2,1,0:T(8,128)(2,1)} %pad_maximum_fusion.11), calls=%async_computation.1 | async-start | bytes 3145728 | tf_op jit(solution)/shard_map/all_to_all | solution.py:802
  756.6 150.3 %reduce-scatter.3.cloned.1.call-start = ((), (), s32[]{:S(2)}) async-start(), calls=%async_computation.6 | async-start | bytes 14155776 | tf_op jit(solution)/shard_map/reduce_scatter | solution.py:778
  911.8 40.0 %collective-permute-start.63 = (bf16[256,512]{1,0:T(8,128)(2,1)S(1)}, bf16[256,512]{1,0:T(8,128)(2,1)S(1)}, u32[]{:S(2)}, u32[]{:S(2)}) collective-permute-start(bf16[256,512]{1,0:T(8,128)(2,1)S(1)} %get-tuple-element.234), channel_id=1, source_target_pairs={{0,0},{2,1},{1,2},{3,3},{4,4},{6,5},{5,6},{7,7},{8,8},{10,9},{9,10... | collective-permute-start | bytes 786440 | tf_op jit(solution)/shard_map/ppermute | solution.py:836
  (135 other events, 2035.4 us)
Sparse Core Ops, SparseCore 0:
  90.5 81.2 all-gather.2
  174.2 65.9 all-gather.4
  630.9 104.3 reduce-scatter.4
  810.2 96.6 reduce-scatter.2

commit v14 on v13

--- a/solution.py
+++ b/solution.py
@@ -754,9 +754,7 @@
     back_one = scatter_rows(
         jnp.concatenate([hidden_one_part, slot_part_one.astype(bf16)], axis=1)
     )
-    joint_part_grad, other_sum, keep_got = lax.optimization_barrier(
-        (joint_part_grad, other_sum, keep_got)
-    )
+    back_one = after(back_one, joint_part_grad)
     out_own = lax.psum_scatter(out_part, "dp", scatter_dimension=0, tiled=True)
     out_grad = slots_of(after(out_own, back_one))
     hidden_one_grad, slot_one_grad = back_one[:, :width], back_one[:, width : width + slots]
@@ -801,6 +799,7 @@
     results = jnp.concatenate([results, small], axis=1)
     results = lax.all_to_all(results, "dp", split_axis=0, concat_axis=0, tiled=True)
     query_own, kv_own = joint_own[:, :query_width], joint_own[:, query_width:]
+    results, other_sum, keep_got = lax.optimization_barrier((results, other_sum, keep_got))
     small = results[:, sent_back:].astype(f32)
     results = results[:, :sent_back].reshape(dp_count, 2 * micro, piece_rows, width)
     results = results.transpose(1, 0, 2, 3).reshape(2, micro, tok_rows, width)

time: 967 us -> 949 us (0.981)
  waiting for transfers between devices: 436 us -> 422 us
    ppermute x62, waiting for transfers between devices: 375 us -> 325 us  [swap(): return lax.ppermute(value, axis, [(i, i ^ step) for i in range(count)])]
    all_to_all x1, waiting for transfers between devices: 28 us -> 55 us  [local(): lax.all_to_all(results, 'dp', split_axis=0, concat_axis=0, tiled=True)]
    all_gather x1, waiting for transfers between devices: 0.01 us -> 20 us  [local(): out_full = lax.all_gather(second_own, 'dp', axis=0, tiled=True)]
    reduce_scatter x1, waiting for transfers between devices: 15.7 us -> 0.01 us  [reduced(): return lax.psum_scatter(value, 'dp', scatter_dimension=0, tiled=True)]
  transfers between devices with their start and end apart: 72 -> 72, of which waited for: 35 -> 36; matrix products, arithmetic and copies ran while one was open for 23% -> 23% of each run, Pallas kernels for 13% -> 13%
where the time goes in v14:
time: 949 us; the launch traced here: 937 us
  waiting for transfers between devices  422 us (44%)
  Pallas kernels  166 us (17%)
  other arithmetic  96.4 us (10%)
  matrix products  80.5 us (8%)
  local copies, waits for them, and re-layouts  80.4 us (8%)
  starting transfers between devices  74.2 us (8%)
  between operations  16.8 us (2%)
    ppermute x62, waiting for transfers between devices, swap(): return lax.ppermute(value, axis, [(i, i ^ step) for i in range(count)])  325 us
    pallas_call x2, Pallas kernels, expert_rows(): pl.pallas_call(expert_kernel, grid_spec=pltpu.PrefetchScalarGridSpec(num_...  81.7 us
    ppermute x62, starting transfers between devices, swap(): return lax.ppermute(value, axis, [(i, i ^ step) for i in range(count)])  57.6 us
    all_to_all x1, waiting for transfers between devices, local(): lax.all_to_all(results, 'dp', split_axis=0, concat_axis=0, tiled=True)  55 us
    pallas_call x2, Pallas kernels, expert_grads(): pl.pallas_call(functools.partial(expert_grad_kernel, cuts), grid_spec=plt...  49.7 us
    dot_general x5, matrix products, dot(): return jnp.dot(left, right, preferred_element_type=f32)  25 us
    dot_general x5, matrix products, dot_t(): lax.dot_general(left, right, (((1,), (1,)), ((), ())), preferred_element_...  23.2 us
    unnamed x210, local copies, waits for them, and re-layouts  22.5 us
  transfers between devices with their start and end apart: 72, of which 36 were waited for; matrix products, arithmetic and copies ran while one was open for 23% of the time, Pallas kernels for 13%

profile of v14, /device:TPU:8, one launch (start us, length us, event | category | flops | bytes accessed | tf_op | source)
XLA Modules:
  0.0 936.9 jit_solution(3524963427717393211)
XLA Ops:
  51.3 26.3 %collective-permute-done.12 = bf16[256,1024]{1,0:T(8,128)(2,1)S(1)} collective-permute-done((bf16[256,1024]{1,0:T(8,128)(2,1)}, bf16[256,1024]{1,0:T(8,128)(2,1)S(1)}, u32[]{:S(2)}, u32[]{:S(2)}) %collective-permute-start.12) | collective-permute-done | bytes 524320 | tf_op jit(solution)/shard_map/ppermute | solution.py:37
  77.7 12.2 %collective-permute-done.13 = bf16[256,1024]{1,0:T(8,128)(2,1)S(1)} collective-permute-done((bf16[256,1024]{1,0:T(8,128)(2,1)}, bf16[256,1024]{1,0:T(8,128)(2,1)S(1)}, u32[]{:S(2)}, u32[]{:S(2)}) %collective-permute-start.13) | collective-permute-done | bytes 524320 | tf_op jit(solution)/shard_map/ppermute | solution.py:37
  106.2 18.4 %all-to-all-done = bf16[8,4,8,2048]{3,2,1,0:T(8,128)(2,1)S(1)} async-done(((bf16[8,4,8,2048]{3,2,1,0:T(8,128)(2,1)}), bf16[8,4,8,2048]{3,2,1,0:T(8,128)(2,1)S(1)}, u32[]{:S(2)}, u32[]{:S(2)}) %all-to-all-start) | async-done | bytes 1048608 | tf_op jit(solution)/shard_map/all_to_all | solution.py:476
  136.8 12.2 %collective-permute-done.10 = bf16[2,48,2048]{2,1,0:T(8,128)(2,1)S(1)} collective-permute-done((bf16[2,48,2048]{2,1,0:T(8,128)(2,1)}, bf16[2,48,2048]{2,1,0:T(8,128)(2,1)S(1)}, u32[]{:S(2)}, u32[]{:S(2)}) %collective-permute-start.10) | collective-permute-done | bytes 393248 | tf_op jit(solution)/shard_map/ppermute | solution.py:37
  167.8 20.9 %collective-permute-done.6 = bf16[2,64,2048]{2,1,0:T(8,128)(2,1)S(1)} collective-permute-done((bf16[2,64,2048]{2,1,0:T(8,128)(2,1)S(1)}, bf16[2,64,2048]{2,1,0:T(8,128)(2,1)S(1)}, u32[]{:S(2)}, u32[]{:S(2)}) %collective-permute-start.6) | collective-permute-done | bytes 524320 | tf_op jit(solution)/shard_map/ppermute | solution.py:37
  188.7 12.8 %collective-permute-done.7 = bf16[2,64,2048]{2,1,0:T(8,128)(2,1)S(1)} collective-permute-done((bf16[2,64,2048]{2,1,0:T(8,128)(2,1)S(1)}, bf16[2,64,2048]{2,1,0:T(8,128)(2,1)S(1)}, u32[]{:S(2)}, u32[]{:S(2)}) %collective-permute-start.7) | collective-permute-done | bytes 524320 | tf_op jit(solution)/shard_map/ppermute | solution.py:37
  218.7 14.8 %attention_forward.1 = (bf16[512,2048]{1,0:T(8,128)(2,1)S(1)}, bf16[512,2048]{1,0:T(8,128)(2,1)}, bf16[512,2048]{1,0:T(8,128)(2,1)}, bf16[512,512]{1,0:T(8,128)(...) custom-call(s32[2]{0:T(128)S(1)} %fusion.133.lens, f32[512,2048]{1,0:T(8,128)} %fusion.2.query, ...), custom_call_target="tpu_custom_call" | custom-call | flops 1073741824 | bytes 14680064 | tf_op jit(solution)/shard_map/attention_forward/pallas_call | solution.py:181
  234.8 20.0 %all-gather.5.cloned.1.call-done = bf16[2048,2048]{1,0:T(8,128)(2,1)} async-done(((bf16[256,2048]{1,0:T(8,128)(2,1)}), bf16[2048,2048]{1,0:T(8,128)(2,1)}) %all-gather.5.cloned.1.call-update) | async-done | bytes 8388624 | tf_op jit(solution)/shard_map/all_gather | solution.py:553
  254.8 7.6 fusion.178
  262.5 13.5 %collective-permute-done.16.refs_2_ = bf16[256,4224]{1,0:T(8,128)(2,1)} collective-permute-done((bf16[256,4224]{1,0:T(8,128)(2,1)}, bf16[256,4224]{1,0:T(8,128)(2,1)}, u32[]{:S(2)}, u32[]{:S(2)}) %collective-permute-start.16) | collective-permute-done | bytes 2162720 | tf_op jit(solution)/shard_map/ppermute | solution.py:37
  281.4 22.3 %collective-permute-done.20 = bf16[2,64,2048]{2,1,0:T(8,128)(2,1)} collective-permute-done((bf16[2,64,2048]{2,1,0:T(8,128)(2,1)}, bf16[2,64,2048]{2,1,0:T(8,128)(2,1)}, u32[]{:S(2)}, u32[]{:S(2)}) %collective-permute-start.20) | collective-permute-done | bytes 524320 | tf_op jit(solution)/shard_map/ppermute | solution.py:37
  303.6 11.1 %collective-permute-done.19 = bf16[2,64,2048]{2,1,0:T(8,128)(2,1)} collective-permute-done((bf16[2,64,2048]{2,1,0:T(8,128)(2,1)}, bf16[2,64,2048]{2,1,0:T(8,128)(2,1)}, u32[]{:S(2)}, u32[]{:S(2)}) %collective-permute-start.19) | collective-permute-done | bytes 524320 | tf_op jit(solution)/shard_map/ppermute | solution.py:37
  331.6 23.6 %collective-permute-done.24 = bf16[2,48,2176]{2,1,0:T(8,128)(2,1)S(1)} collective-permute-done((bf16[2,48,2176]{2,1,0:T(8,128)(2,1)S(1)}, bf16[2,48,2176]{2,1,0:T(8,128)(2,1)S(1)}, u32[]{:S(2)}, u32[]{:S(2)}) %collective-permute-start.24) | collective-permute-done | bytes 417824 | tf_op jit(solution)/shard_map/ppermute | solution.py:37
  374.6 41.0 %expert_rows.2 = (bf16[768,2048]{1,0:T(8,128)(2,1)}, bf16[768,2176]{1,0:T(8,128)(2,1)}, bf16[768,1408]{1,0:T(8,128)(2,1)}, bf16[768,2816]{1,0:T(8,128)(2,1)}) custom-call(s32[2]{0:T(128)} %pad_add_fusion.1.place_ref, bf16[768,2176]{1,0:T(8,128)(2,1)} %pad_maximum_fusion.2.hidden.refs_0_.refs_4_, bf16[768,2048]{1,0:T(8,128)(2,1)} %copy-done.48, ...), custom_call_target="tpu_custom_call" | custom-call | flops 26575110144 | bytes 36175872 | tf_op jit(solution)/shard_map/expert_rows/pallas_call | solution.py:332
  420.7 40.7 %expert_rows.3 = (bf16[768,2048]{1,0:T(8,128)(2,1)}, bf16[768,2176]{1,0:T(8,128)(2,1)}, bf16[768,1408]{1,0:T(8,128)(2,1)}, bf16[768,2816]{1,0:T(8,128)(2,1)}) custom-call(s32[2]{0:T(128)} %pad_add_fusion.1.place_ref, bf16[768,2176]{1,0:T(8,128)(2,1)} %constant_dynamic-update-slice_fusion.4.hidden.refs_1_.refs_5_, bf16[768,2048]{1,0:T(8,128)(2,1)} %copy-done.47, ...), custom_call_target="tpu_custom_call" | custom-call | flops 26575110144 | bytes 36175872 | tf_op jit(solution)/shard_map/expert_rows/pallas_call | solution.py:332
  477.7 24.8 %expert_grads.2 = (bf16[512,4224]{1,0:T(8,128)(2,1)}, bf16[512,4224]{1,0:T(8,128)(2,1)}) custom-call(s32[4]{0:T(128)} %get-tuple-element.294.order, bf16[768,2176]{1,0:T(8,128)(2,1)} %pad_maximum_fusion.2.hidden.refs_0_.refs_4_, bf16[768,2176]{1,0:T(8,128)(2,1)} %constant_dynamic-update-slice_fusion.4.hidden.refs_1_.refs_5_, bf16[768,2048]{1,0:T(8,128)(2,1)} %copy-done.48, ...), custom_call_target="tpu_custom_call" | custom-call | flops 13287555072 | bytes 27918336 | tf_op jit(solution)/shard_map/expert_grads/pallas_call | solution.py:405
  524.0 24.9 %expert_grads.3 = (bf16[512,4224]{1,0:T(8,128)(2,1)}, bf16[512,4224]{1,0:T(8,128)(2,1)}) custom-call(s32[4]{0:T(128)} %get-tuple-element.295.order, bf16[768,2176]{1,0:T(8,128)(2,1)} %pad_maximum_fusion.2.hidden.refs_0_.refs_4_, bf16[768,2176]{1,0:T(8,128)(2,1)} %constant_dynamic-update-slice_fusion.4.hidden.refs_1_.refs_5_, bf16[768,2048]{1,0:T(8,128)(2,1)} %copy-done.48, ...), custom_call_target="tpu_custom_call" | custom-call | flops 13287555072 | bytes 27918336 | tf_op jit(solution)/shard_map/expert_grads/pallas_call | solution.py:405
  549.5 9.1 collective-permute-done.40
  572.1 16.1 %collective-permute-done.41 = bf16[2,64,2048]{2,1,0:T(8,128)(2,1)S(1)} collective-permute-done((bf16[2,64,2048]{2,1,0:T(8,128)(2,1)S(1)}, bf16[2,64,2048]{2,1,0:T(8,128)(2,1)S(1)}, u32[]{:S(2)}, u32[]{:S(2)}) %collective-permute-start.41) | collective-permute-done | bytes 524320 | tf_op jit(solution)/shard_map/ppermute | solution.py:37
  588.2 17.2 %collective-permute-done.42 = bf16[2,64,2048]{2,1,0:T(8,128)(2,1)S(1)} collective-permute-done((bf16[2,64,2048]{2,1,0:T(8,128)(2,1)S(1)}, bf16[2,64,2048]{2,1,0:T(8,128)(2,1)S(1)}, u32[]{:S(2)}, u32[]{:S(2)}) %collective-permute-start.42) | collective-permute-done | bytes 524320 | tf_op jit(solution)/shard_map/ppermute | solution.py:37
  605.5 10.3 %collective-permute-done.43 = bf16[2,64,2048]{2,1,0:T(8,128)(2,1)S(1)} collective-permute-done((bf16[2,64,2048]{2,1,0:T(8,128)(2,1)S(1)}, bf16[2,64,2048]{2,1,0:T(8,128)(2,1)S(1)}, u32[]{:S(2)}, u32[]{:S(2)}) %collective-permute-start.43) | collective-permute-done | bytes 524320 | tf_op jit(solution)/shard_map/ppermute | solution.py:37
  626.8 10.8 %fusion.180.vals_grad = f32[512,2048]{1,0:T(8,128)} fusion(bf16[512,2048]{1,0:T(8,128)(2,1)} %bitcast.433, bf16[2048,2048]{1,0:T(8,128)(2,1)} %all-gather.5.cloned.1.call-done), kind=kOutput, calls=%fused_computation.454 | convolution fusion | flops 4294967296 | bytes 14680064 | tf_op jit(solution)/shard_map/dot_general | solution.py:24
  637.5 8.0 add_convert_fusion.1
  651.9 20.1 %attention_backward.1 = (bf16[512,2048]{1,0:T(8,128)(2,1)S(1)}, bf16[512,512]{1,0:T(8,128)(2,1)S(1)}, bf16[512,512]{1,0:T(8,128)(2,1)S(1)}, f32[512,128]{1,0:T(8,128)S(1)}) custom-call(s32[2]{0:T(128)S(1)} %fusion.133.lens, bf16[512,2048]{1,0:T(8,128)(2,1)} %get-tuple-element.152.query, bf16[512,512]{1,0:T(8,128)(2,1)S(1)} %get-tuple-element.153.key, ...), custom_call_target="tpu_custom_call" | custom-call | flops 2684354560 | bytes 14680064 | tf_op jit(solution)/shard_map/attention_backward/pallas_call | solution.py:212
  685.9 8.5 add_convert_fusion.2
  705.0 9.9 %convolution_convert_fusion = bf16[2048,3072]{1,0:T(8,128)(2,1)} fusion(bf16[512,2048]{1,0:T(8,128)(2,1)S(1)} %bitcast.415, bf16[512,512]{1,0:T(8,128)(2,1)S(1)} %get-tuple-element.162, bf16[512,512]{1,0:T(8,128)(2,1)S(1)} %get-tuple-element.161, bf16[512,2048]{1,0:T(8,128)(2,1)S(1)} %get-tuple-element.160), kind=kOutput, calls=%fused_computation | convolution fusion | flops 6458179584 | bytes 17825792 | tf_op jit(solution)/shard_map/dot_general | solution.py:32
  718.3 7.9 collective-permute-done.51
  726.2 8.8 collective-permute-done.50
  748.4 55.0 %all-to-all-done.1 = bf16[8,48,2048]{2,1,0:T(8,128)(2,1)S(1)} async-done(((bf16[8,48,2048]{2,1,0:T(8,128)(2,1)}), bf16[8,48,2048]{2,1,0:T(8,128)(2,1)S(1)}, u32[]{:S(2)}, u32[]{:S(2)}) %all-to-all-start.1) | async-done | bytes 1572896 | tf_op jit(solution)/shard_map/all_to_all | solution.py:800
  850.6 8.4 convert_element_type.342
  862.8 16.2 %collective-permute-done.61 = bf16[256,512]{1,0:T(8,128)(2,1)S(1)} collective-permute-done((bf16[256,512]{1,0:T(8,128)(2,1)S(1)}, bf16[256,512]{1,0:T(8,128)(2,1)S(1)}, u32[]{:S(2)}, u32[]{:S(2)}) %collective-permute-start.61) | collective-permute-done | bytes 262176 | tf_op jit(solution)/shard_map/ppermute | solution.py:37
  902.4 15.3 %collective-permute-done.58 = bf16[256,512]{1,0:T(8,128)(2,1)S(1)} collective-permute-done((bf16[256,512]{1,0:T(8,128)(2,1)S(1)}, bf16[256,512]{1,0:T(8,128)(2,1)S(1)}, u32[]{:S(2)}, u32[]{:S(2)}) %collective-permute-start.58) | collective-permute-done | bytes 262176 | tf_op jit(solution)/shard_map/ppermute | solution.py:37
  (598 shorter events, 351.5 us)
Async XLA Ops:
  7.2 196.0 %all-gather.3.cloned.1.call-start = ((), (), s32[]{:S(2)}) async-start(), calls=%async_computation.4 | async-start | bytes 14155776 | tf_op jit(solution)/shard_map/all_gather | solution.py:552
  14.3 78.1 %collective-permute-start.1 = (bf16[256,4224]{1,0:T(8,128)(2,1)}, bf16[256,4224]{1,0:T(8,128)(2,1)}, u32[]{:S(2)}, u32[]{:S(2)}) collective-permute-start(bf16[256,4224]{1,0:T(8,128)(2,1)} %pad_maximum_fusion.5), channel_id=1, source_target_pairs={{0,8},{4,12},{8,0},{12,4},{16,24},{20,28},{24,16},{28,20},{1,9},{5... | collective-permute-start | bytes 6488072 | tf_op jit(solution)/shard_map/ppermute | solution.py:37
  17.3 75.2 %collective-permute-start.3 = (bf16[256,4224]{1,0:T(8,128)(2,1)}, bf16[256,4224]{1,0:T(8,128)(2,1)}, u32[]{:S(2)}, u32[]{:S(2)}) collective-permute-start(bf16[256,4224]{1,0:T(8,128)(2,1)} %pad_maximum_fusion.4), channel_id=1, source_target_pairs={{0,16},{4,20},{8,24},{12,28},{16,0},{20,4},{24,8},{28,12},{1,17},{... | collective-permute-start | bytes 6488072 | tf_op jit(solution)/shard_map/ppermute | solution.py:37
  42.0 35.6 %collective-permute-start.12 = (bf16[256,1024]{1,0:T(8,128)(2,1)}, bf16[256,1024]{1,0:T(8,128)(2,1)S(1)}, u32[]{:S(2)}, u32[]{:S(2)}) collective-permute-start(bf16[256,1024]{1,0:T(8,128)(2,1)} %pad_maximum_fusion.14), channel_id=1, source_target_pairs={{0,2},{1,3},{2,0},{3,1},{4,6},{5,7},{6,4},{7,5},{8,10},{9,11},{10,... | collective-permute-start | bytes 1572872 | tf_op jit(solution)/shard_map/ppermute | solution.py:37
  42.8 47.1 %collective-permute-start.13 = (bf16[256,1024]{1,0:T(8,128)(2,1)}, bf16[256,1024]{1,0:T(8,128)(2,1)S(1)}, u32[]{:S(2)}, u32[]{:S(2)}) collective-permute-start(bf16[256,1024]{1,0:T(8,128)(2,1)} %pad_maximum_fusion.15), channel_id=1, source_target_pairs={{0,3},{1,2},{2,1},{3,0},{4,7},{5,6},{6,5},{7,4},{8,11},{9,10},{10,... | collective-permute-start | bytes 1572872 | tf_op jit(solution)/shard_map/ppermute | solution.py:37
  92.4 162.4 %all-gather.5.cloned.1.call-start = ((), (), s32[]{:S(2)}) async-start(), calls=%async_computation.5 | async-start | bytes 9437184 | tf_op jit(solution)/shard_map/all_gather | solution.py:553
  93.2 38.3 %collective-permute-start = (bf16[256,4224]{1,0:T(8,128)(2,1)}, bf16[256,4224]{1,0:T(8,128)(2,1)}, u32[]{:S(2)}, u32[]{:S(2)}) collective-permute-start(bf16[256,4224]{1,0:T(8,128)(2,1)} %pad_maximum_fusion.4), channel_id=1, source_target_pairs={{0,4},{4,0},{8,12},{12,8},{16,20},{20,16},{24,28},{28,24},{1,5},{5... | collective-permute-start | bytes 6488072 | tf_op jit(solution)/shard_map/ppermute | solution.py:37
  98.1 747.1 %reduce-scatter.5.cloned.1.call-start = ((), (), s32[]{:S(2)}) async-start(), calls=%async_computation.7 | async-start | bytes 9437184 | tf_op jit(solution)/shard_map/reduce_scatter | solution.py:758
  135.2 53.4 %collective-permute-start.6 = (bf16[2,64,2048]{2,1,0:T(8,128)(2,1)S(1)}, bf16[2,64,2048]{2,1,0:T(8,128)(2,1)S(1)}, u32[]{:S(2)}, u32[]{:S(2)}) collective-permute-start(bf16[2,64,2048]{2,1,0:T(8,128)(2,1)S(1)} %bitcast.435), channel_id=1, source_target_pairs={{0,2},{1,3},{2,0},{3,1},{4,6},{5,7},{6,4},{7,5},{8,10},{9,11},{10,... | collective-permute-start | bytes 1572872 | tf_op jit(solution)/shard_map/ppermute | solution.py:37
  157.6 44.0 %collective-permute-start.7 = (bf16[2,64,2048]{2,1,0:T(8,128)(2,1)S(1)}, bf16[2,64,2048]{2,1,0:T(8,128)(2,1)S(1)}, u32[]{:S(2)}, u32[]{:S(2)}) collective-permute-start(bf16[2,64,2048]{2,1,0:T(8,128)(2,1)S(1)} %bitcast.436), channel_id=1, source_target_pairs={{0,3},{1,2},{2,1},{3,0},{4,7},{5,6},{6,5},{7,4},{8,11},{9,10},{10,... | collective-permute-start | bytes 1572872 | tf_op jit(solution)/shard_map/ppermute | solution.py:37
  203.2 72.8 %collective-permute-start.16 = (bf16[256,4224]{1,0:T(8,128)(2,1)}, bf16[256,4224]{1,0:T(8,128)(2,1)}, u32[]{:S(2)}, u32[]{:S(2)}) collective-permute-start(bf16[256,4224]{1,0:T(8,128)(2,1)} %get-tuple-element.101.refs_0_), channel_id=1, source_target_pairs={{0,16},{4,20},{8,24},{12,28},{16,0},{20,4},{24,8},{28,12},{1,17},{... | collective-permute-start | bytes 6488072 | tf_op jit(solution)/shard_map/ppermute | solution.py:37
  203.8 72.2 %collective-permute-start.17 = (bf16[256,4224]{1,0:T(8,128)(2,1)}, bf16[256,4224]{1,0:T(8,128)(2,1)}, u32[]{:S(2)}, u32[]{:S(2)}) collective-permute-start(bf16[256,4224]{1,0:T(8,128)(2,1)} %get-tuple-element.102), channel_id=1, source_target_pairs={{0,8},{4,12},{8,0},{12,4},{16,24},{20,28},{24,16},{28,20},{1,9},{5... | collective-permute-start | bytes 6488072 | tf_op jit(solution)/shard_map/ppermute | solution.py:37
  204.4 118.0 %collective-permute-start.21 = (bf16[256,4224]{1,0:T(8,128)(2,1)}, bf16[256,4224]{1,0:T(8,128)(2,1)}, u32[]{:S(2)}, u32[]{:S(2)}) collective-permute-start(bf16[256,4224]{1,0:T(8,128)(2,1)} %collective-permute-done.1), channel_id=1, source_target_pairs={{0,16},{4,20},{8,24},{12,28},{16,0},{20,4},{24,8},{28,12},{1,17},{... | collective-permute-start | bytes 6488072 | tf_op jit(solution)/shard_map/ppermute | solution.py:37
  277.4 37.3 %collective-permute-start.19 = (bf16[2,64,2048]{2,1,0:T(8,128)(2,1)}, bf16[2,64,2048]{2,1,0:T(8,128)(2,1)}, u32[]{:S(2)}, u32[]{:S(2)}) collective-permute-start(bf16[2,64,2048]{2,1,0:T(8,128)(2,1)} %get-tuple-element.215), channel_id=1, source_target_pairs={{0,2},{1,3},{2,0},{3,1},{4,6},{5,7},{6,4},{7,5},{8,10},{9,11},{10,... | collective-permute-start | bytes 1572872 | tf_op jit(solution)/shard_map/ppermute | solution.py:37
  277.4 37.3 %collective-permute-start.18 = (bf16[2,64,2048]{2,1,0:T(8,128)(2,1)S(1)}, bf16[2,64,2048]{2,1,0:T(8,128)(2,1)}, u32[]{:S(2)}, u32[]{:S(2)}) collective-permute-start(bf16[2,64,2048]{2,1,0:T(8,128)(2,1)S(1)} %get-tuple-element.213), channel_id=1, source_target_pairs={{0,1},{1,0},{2,3},{3,2},{4,5},{5,4},{6,7},{7,6},{8,9},{9,8},{10,11... | collective-permute-start | bytes 1572872 | tf_op jit(solution)/shard_map/ppermute | solution.py:37
  280.8 86.1 %collective-permute-start.25 = (bf16[256,4224]{1,0:T(8,128)(2,1)}, bf16[256,4224]{1,0:T(8,128)(2,1)}, u32[]{:S(2)}, u32[]{:S(2)}) collective-permute-start(bf16[256,4224]{1,0:T(8,128)(2,1)} %collective-permute-done.17.refs_1_), channel_id=1, source_target_pairs={{0,16},{4,20},{8,24},{12,28},{16,0},{20,4},{24,8},{28,12},{1,17},{... | collective-permute-start | bytes 6488072 | tf_op jit(solution)/shard_map/ppermute | solution.py:37
  325.8 35.6 %collective-permute-start.29 = (bf16[384,2048]{1,0:T(8,128)(2,1)}, bf16[384,2048]{1,0:T(8,128)(2,1)}, u32[]{:S(2)}, u32[]{:S(2)}) collective-permute-start(bf16[384,2048]{1,0:T(8,128)(2,1)} %bitcast.420), channel_id=1, source_target_pairs={{0,8},{4,12},{8,0},{12,4},{16,24},{20,28},{24,16},{28,20},{1,9},{5... | collective-permute-start | bytes 4718600 | tf_op jit(solution)/shard_map/ppermute | solution.py:37
  369.3 46.3 %collective-permute-start.32 = (bf16[384,2176]{1,0:T(8,128)(2,1)S(1)}, bf16[384,2176]{1,0:T(8,128)(2,1)S(1)}, u32[]{:S(2)}, u32[]{:S(2)}) collective-permute-start(bf16[384,2176]{1,0:T(8,128)(2,1)S(1)} %bitcast.418), channel_id=1, source_target_pairs={{0,8},{4,12},{8,0},{12,4},{16,24},{20,28},{24,16},{28,20},{1,9},{5... | collective-permute-start | bytes 5013512 | tf_op jit(solution)/shard_map/ppermute | solution.py:37
  476.8 39.2 %collective-permute-start.31 = (bf16[384,2176]{1,0:T(8,128)(2,1)}, bf16[384,2176]{1,0:T(8,128)(2,1)}, u32[]{:S(2)}, u32[]{:S(2)}) collective-permute-start(bf16[384,2176]{1,0:T(8,128)(2,1)} %split.25), channel_id=1, source_target_pairs={{0,4},{4,0},{8,12},{12,8},{16,20},{20,16},{24,28},{28,24},{1,5},{5... | collective-permute-start | bytes 5013512 | tf_op jit(solution)/shard_map/ppermute | solution.py:37
  477.0 39.1 %collective-permute-start.35 = (bf16[384,2176]{1,0:T(8,128)(2,1)}, bf16[384,2176]{1,0:T(8,128)(2,1)}, u32[]{:S(2)}, u32[]{:S(2)}) collective-permute-start(bf16[384,2176]{1,0:T(8,128)(2,1)} %add_convert_fusion.3), channel_id=1, source_target_pairs={{0,8},{4,12},{8,0},{12,4},{16,24},{20,28},{24,16},{28,20},{1,9},{5... | collective-permute-start | bytes 5013512 | tf_op jit(solution)/shard_map/ppermute | solution.py:37
  502.5 117.2 %collective-permute-start.45 = (bf16[512,4224]{1,0:T(8,128)(2,1)}, bf16[512,4224]{1,0:T(8,128)(2,1)}, u32[]{:S(2)}, u32[]{:S(2)}) collective-permute-start(bf16[512,4224]{1,0:T(8,128)(2,1)} %get-tuple-element.125), channel_id=1, source_target_pairs={{0,16},{4,20},{8,24},{12,28},{16,0},{20,4},{24,8},{28,12},{1,17},{... | collective-permute-start | bytes 12976136 | tf_op jit(solution)/shard_map/ppermute | solution.py:37
  521.5 37.1 %collective-permute-start.40 = (bf16[2,48,2176]{2,1,0:T(8,128)(2,1)S(1)}, bf16[2,48,2176]{2,1,0:T(8,128)(2,1)S(1)}, u32[]{:S(2)}, u32[]{:S(2)}) collective-permute-start(bf16[2,48,2176]{2,1,0:T(8,128)(2,1)S(1)} %bitcast.460), channel_id=1, source_target_pairs={{0,3},{1,2},{2,1},{3,0},{4,7},{5,6},{6,5},{7,4},{8,11},{9,10},{10,... | collective-permute-start | bytes 1253384 | tf_op jit(solution)/shard_map/ppermute | solution.py:37
  522.6 93.3 %collective-permute-start.44 = (bf16[384,2048]{1,0:T(8,128)(2,1)}, bf16[384,2048]{1,0:T(8,128)(2,1)}, u32[]{:S(2)}, u32[]{:S(2)}) collective-permute-start(bf16[384,2048]{1,0:T(8,128)(2,1)} %add_convert_fusion.4), channel_id=1, source_target_pairs={{0,8},{4,12},{8,0},{12,4},{16,24},{20,28},{24,16},{28,20},{1,9},{5... | collective-permute-start | bytes 4718600 | tf_op jit(solution)/shard_map/ppermute | solution.py:37
  568.2 37.2 %collective-permute-start.42 = (bf16[2,64,2048]{2,1,0:T(8,128)(2,1)S(1)}, bf16[2,64,2048]{2,1,0:T(8,128)(2,1)S(1)}, u32[]{:S(2)}, u32[]{:S(2)}) collective-permute-start(bf16[2,64,2048]{2,1,0:T(8,128)(2,1)S(1)} %bitcast.442), channel_id=1, source_target_pairs={{0,2},{1,3},{2,0},{3,1},{4,6},{5,7},{6,4},{7,5},{8,10},{9,11},{10,... | collective-permute-start | bytes 1572872 | tf_op jit(solution)/shard_map/ppermute | solution.py:37
  570.6 45.1 %collective-permute-start.43 = (bf16[2,64,2048]{2,1,0:T(8,128)(2,1)S(1)}, bf16[2,64,2048]{2,1,0:T(8,128)(2,1)S(1)}, u32[]{:S(2)}, u32[]{:S(2)}) collective-permute-start(bf16[2,64,2048]{2,1,0:T(8,128)(2,1)S(1)} %bitcast.443), channel_id=1, source_target_pairs={{0,3},{1,2},{2,1},{3,0},{4,7},{5,6},{6,5},{7,4},{8,11},{9,10},{10,... | collective-permute-start | bytes 1572872 | tf_op jit(solution)/shard_map/ppermute | solution.py:37
  649.4 154.0 %collective-permute-start.52 = (bf16[512,4224]{1,0:T(8,128)(2,1)}, bf16[512,4224]{1,0:T(8,128)(2,1)}, u32[]{:S(2)}, u32[]{:S(2)}) collective-permute-start(bf16[512,4224]{1,0:T(8,128)(2,1)} %add_convert_fusion.1), channel_id=1, source_target_pairs={{0,8},{4,12},{8,0},{12,4},{16,24},{20,28},{24,16},{28,20},{1,9},{5... | collective-permute-start | bytes 12976136 | tf_op jit(solution)/shard_map/ppermute | solution.py:37
  650.9 152.5 %collective-permute-start.53 = (bf16[512,4224]{1,0:T(8,128)(2,1)}, bf16[512,4224]{1,0:T(8,128)(2,1)}, u32[]{:S(2)}, u32[]{:S(2)}) collective-permute-start(bf16[512,4224]{1,0:T(8,128)(2,1)} %get-tuple-element.168), channel_id=1, source_target_pairs={{0,16},{4,20},{8,24},{12,28},{16,0},{20,4},{24,8},{28,12},{1,17},{... | collective-permute-start | bytes 12976136 | tf_op jit(solution)/shard_map/ppermute | solution.py:37
  696.3 38.6 %collective-permute-start.50 = (bf16[2,64,2176]{2,1,0:T(8,128)(2,1)}, bf16[2,64,2176]{2,1,0:T(8,128)(2,1)}, u32[]{:S(2)}, u32[]{:S(2)}) collective-permute-start(bf16[2,64,2176]{2,1,0:T(8,128)(2,1)} %get-tuple-element.222), channel_id=1, source_target_pairs={{0,2},{1,3},{2,0},{3,1},{4,6},{5,7},{6,4},{7,5},{8,10},{9,11},{10,... | collective-permute-start | bytes 1671176 | tf_op jit(solution)/shard_map/ppermute | solution.py:37
  696.3 38.6 %collective-permute-start.49 = (bf16[2,64,2176]{2,1,0:T(8,128)(2,1)}, bf16[2,64,2176]{2,1,0:T(8,128)(2,1)}, u32[]{:S(2)}, u32[]{:S(2)}) collective-permute-start(bf16[2,64,2176]{2,1,0:T(8,128)(2,1)} %get-tuple-element.220), channel_id=1, source_target_pairs={{0,1},{1,0},{2,3},{3,2},{4,5},{5,4},{6,7},{7,6},{8,9},{9,8},{10,11... | collective-permute-start | bytes 1671176 | tf_op jit(solution)/shard_map/ppermute | solution.py:37
  744.1 59.4 %all-to-all-start.1 = ((bf16[8,48,2048]{2,1,0:T(8,128)(2,1)}), bf16[8,48,2048]{2,1,0:T(8,128)(2,1)S(1)}, u32[]{:S(2)}, u32[]{:S(2)}) async-start(bf16[8,48,2048]{2,1,0:T(8,128)(2,1)} %pad_maximum_fusion.11), calls=%async_computation.1 | async-start | bytes 3145728 | tf_op jit(solution)/shard_map/all_to_all | solution.py:800
  747.7 139.2 %reduce-scatter.3.cloned.1.call-start = ((), (), s32[]{:S(2)}) async-start(), calls=%async_computation.6 | async-start | bytes 14155776 | tf_op jit(solution)/shard_map/reduce_scatter | solution.py:776
  895.1 34.0 %collective-permute-start.63 = (bf16[256,512]{1,0:T(8,128)(2,1)S(1)}, bf16[256,512]{1,0:T(8,128)(2,1)S(1)}, u32[]{:S(2)}, u32[]{:S(2)}) collective-permute-start(bf16[256,512]{1,0:T(8,128)(2,1)S(1)} %get-tuple-element.236), channel_id=1, source_target_pairs={{0,0},{2,1},{1,2},{3,3},{4,4},{6,5},{5,6},{7,7},{8,8},{10,9},{9,10... | collective-permute-start | bytes 786440 | tf_op jit(solution)/shard_map/ppermute | solution.py:835
  (135 other events, 1804.0 us)
Sparse Core Ops, SparseCore 0:
  92.6 78.5 all-gather.2
  173.6 81.1 all-gather.4
  626.9 103.8 reduce-scatter.4
  752.1 101.5 reduce-scatter.2

commit v15 on v14

--- a/solution.py
+++ b/solution.py
@@ -799,6 +799,7 @@
     results = jnp.concatenate([results, small], axis=1)
     results = lax.all_to_all(results, "dp", split_axis=0, concat_axis=0, tiled=True)
     query_own, kv_own = joint_own[:, :query_width], joint_own[:, query_width:]
+    results, out_grad = lax.optimization_barrier((results, out_grad))
     results, other_sum, keep_got = lax.optimization_barrier((results, other_sum, keep_got))
     small = results[:, sent_back:].astype(f32)
     results = results[:, :sent_back].reshape(dp_count, 2 * micro, piece_rows, width)
@@ -807,14 +808,11 @@
     peak_row = jnp.max((peak_row[:, 0] + peak_row[:, 1]) + peak_row[:, 2], axis=0)
     small = jnp.sum(small, axis=0)
     small = lax.dynamic_update_slice(small, peak_row[None], (sum_rows, 0))
-    smalls = [swap(small, "expert", k) if k else small for k in range(slots)]
-    peaks_all = jnp.zeros((slots, HEADS), f32)
-    for k, part in enumerate(smalls):
-        part = part[sum_rows, :peak_count].reshape(own_heads, slots).T
-        peaks_all = lax.dynamic_update_slice(peaks_all, part, (0, (col ^ k) * own_heads))
-    while len(smalls) > 1:
-        smalls = [left + right for left, right in zip(smalls[::2], smalls[1::2])]
-    sums = smalls[0][:sum_rows]
+    smalls = jnp.broadcast_to(small[None], (slots,) + small.shape)
+    smalls = lax.all_to_all(smalls, "expert", split_axis=0, concat_axis=0, tiled=True)
+    peaks_all = smalls[:, sum_rows, :peak_count].reshape(slots, own_heads, slots)
+    peaks_all = peaks_all.transpose(2, 0, 1).reshape(slots, HEADS)
+    sums = functools.reduce(jnp.add, [smalls[k, :sum_rows] for k in range(slots)])
 
     keep_sums = total(own_grads[1], keep_got).reshape(2, shard_rows, 3 * quarter)
     other_sums = other_sum.reshape(2, shard_rows, 3 * quarter)

time: 949 us -> 911 us (0.960)
  waiting for transfers between devices: 422 us -> 392 us
    all_to_all x1, waiting for transfers between devices: 55 us -> 17.3 us  [local(): lax.all_to_all(results, 'dp', split_axis=0, concat_axis=0, tiled=True)]
    ppermute x62 -> x59, starting transfers between devices: 57.6 us -> 54.7 us  [swap(): return lax.ppermute(value, axis, [(i, i ^ step) for i in range(count)])]
    unnamed x210 -> x213, local copies, waits for them, and re-layouts: 22.5 us -> 20.7 us
    ppermute x62 -> x59, waiting for transfers between devices: 325 us -> 325 us  [swap(): return lax.ppermute(value, axis, [(i, i ^ step) for i in range(count)])]
  transfers between devices with their start and end apart: 72 -> 70, of which waited for: 36 -> 38; matrix products, arithmetic and copies ran while one was open for 23% -> 23% of each run, Pallas kernels for 13% -> 14%
where the time goes in v15:
time: 911 us; the launch traced here: 904 us
  waiting for transfers between devices  392 us (43%)
  Pallas kernels  166 us (18%)
  other arithmetic  96.3 us (11%)
  matrix products  80.4 us (9%)
  starting transfers between devices  77.6 us (9%)
  local copies, waits for them, and re-layouts  74.1 us (8%)
  between operations  17.1 us (2%)
    ppermute x59, waiting for transfers between devices, swap(): return lax.ppermute(value, axis, [(i, i ^ step) for i in range(count)])  325 us
    pallas_call x2, Pallas kernels, expert_rows(): pl.pallas_call(expert_kernel, grid_spec=pltpu.PrefetchScalarGridSpec(num_...  81.8 us
    ppermute x59, starting transfers between devices, swap(): return lax.ppermute(value, axis, [(i, i ^ step) for i in range(count)])  54.7 us
    pallas_call x2, Pallas kernels, expert_grads(): pl.pallas_call(functools.partial(expert_grad_kernel, cuts), grid_spec=plt...  49.7 us
    dot_general x5, matrix products, dot(): return jnp.dot(left, right, preferred_element_type=f32)  25 us
    dot_general x5, matrix products, dot_t(): lax.dot_general(left, right, (((1,), (1,)), ((), ())), preferred_element_...  23.1 us
    unnamed x213, local copies, waits for them, and re-layouts  20.7 us
    pallas_call x1, Pallas kernels, attention_backward(): pl.pallas_call(backward_kernel, grid_spec=pltpu.PrefetchScalarGridSpec(nu...  20.1 us
  transfers between devices with their start and end apart: 70, of which 38 were waited for; matrix products, arithmetic and copies ran while one was open for 23% of the time, Pallas kernels for 14%

profile of v15, /device:TPU:8, one launch (start us, length us, event | category | flops | bytes accessed | tf_op | source)
XLA Modules:
  0.0 903.6 jit_solution(11815055506240351895)
XLA Ops:
  51.3 26.2 %collective-permute-done.12 = bf16[256,1024]{1,0:T(8,128)(2,1)S(1)} collective-permute-done((bf16[256,1024]{1,0:T(8,128)(2,1)}, bf16[256,1024]{1,0:T(8,128)(2,1)S(1)}, u32[]{:S(2)}, u32[]{:S(2)}) %collective-permute-start.12) | collective-permute-done | bytes 524320 | tf_op jit(solution)/shard_map/ppermute | solution.py:37
  77.6 12.2 %collective-permute-done.13 = bf16[256,1024]{1,0:T(8,128)(2,1)S(1)} collective-permute-done((bf16[256,1024]{1,0:T(8,128)(2,1)}, bf16[256,1024]{1,0:T(8,128)(2,1)S(1)}, u32[]{:S(2)}, u32[]{:S(2)}) %collective-permute-start.13) | collective-permute-done | bytes 524320 | tf_op jit(solution)/shard_map/ppermute | solution.py:37
  106.1 18.4 %all-to-all-done = bf16[8,4,8,2048]{3,2,1,0:T(8,128)(2,1)S(1)} async-done(((bf16[8,4,8,2048]{3,2,1,0:T(8,128)(2,1)}), bf16[8,4,8,2048]{3,2,1,0:T(8,128)(2,1)S(1)}, u32[]{:S(2)}, u32[]{:S(2)}) %all-to-all-start) | async-done | bytes 1048608 | tf_op jit(solution)/shard_map/all_to_all | solution.py:476
  136.8 12.2 %collective-permute-done.10 = bf16[2,48,2048]{2,1,0:T(8,128)(2,1)S(1)} collective-permute-done((bf16[2,48,2048]{2,1,0:T(8,128)(2,1)}, bf16[2,48,2048]{2,1,0:T(8,128)(2,1)S(1)}, u32[]{:S(2)}, u32[]{:S(2)}) %collective-permute-start.10) | collective-permute-done | bytes 393248 | tf_op jit(solution)/shard_map/ppermute | solution.py:37
  167.8 20.8 %collective-permute-done.6 = bf16[2,64,2048]{2,1,0:T(8,128)(2,1)S(1)} collective-permute-done((bf16[2,64,2048]{2,1,0:T(8,128)(2,1)S(1)}, bf16[2,64,2048]{2,1,0:T(8,128)(2,1)S(1)}, u32[]{:S(2)}, u32[]{:S(2)}) %collective-permute-start.6) | collective-permute-done | bytes 524320 | tf_op jit(solution)/shard_map/ppermute | solution.py:37
  188.7 12.8 %collective-permute-done.7 = bf16[2,64,2048]{2,1,0:T(8,128)(2,1)S(1)} collective-permute-done((bf16[2,64,2048]{2,1,0:T(8,128)(2,1)S(1)}, bf16[2,64,2048]{2,1,0:T(8,128)(2,1)S(1)}, u32[]{:S(2)}, u32[]{:S(2)}) %collective-permute-start.7) | collective-permute-done | bytes 524320 | tf_op jit(solution)/shard_map/ppermute | solution.py:37
  218.6 14.8 %attention_forward.1 = (bf16[512,2048]{1,0:T(8,128)(2,1)S(1)}, bf16[512,2048]{1,0:T(8,128)(2,1)}, bf16[512,2048]{1,0:T(8,128)(2,1)}, bf16[512,512]{1,0:T(8,128)(...) custom-call(s32[2]{0:T(128)S(1)} %fusion.136.lens, f32[512,2048]{1,0:T(8,128)} %fusion.2.query, ...), custom_call_target="tpu_custom_call" | custom-call | flops 1073741824 | bytes 14680064 | tf_op jit(solution)/shard_map/attention_forward/pallas_call | solution.py:181
  234.8 20.0 %all-gather.5.cloned.1.call-done = bf16[2048,2048]{1,0:T(8,128)(2,1)} async-done(((bf16[256,2048]{1,0:T(8,128)(2,1)}), bf16[2048,2048]{1,0:T(8,128)(2,1)}) %all-gather.5.cloned.1.call-update) | async-done | bytes 8388624 | tf_op jit(solution)/shard_map/all_gather | solution.py:553
  254.8 7.6 fusion.178
  262.5 13.5 %collective-permute-done.16.refs_2_ = bf16[256,4224]{1,0:T(8,128)(2,1)} collective-permute-done((bf16[256,4224]{1,0:T(8,128)(2,1)}, bf16[256,4224]{1,0:T(8,128)(2,1)}, u32[]{:S(2)}, u32[]{:S(2)}) %collective-permute-start.16) | collective-permute-done | bytes 2162720 | tf_op jit(solution)/shard_map/ppermute | solution.py:37
  281.3 22.3 %collective-permute-done.20 = bf16[2,64,2048]{2,1,0:T(8,128)(2,1)} collective-permute-done((bf16[2,64,2048]{2,1,0:T(8,128)(2,1)}, bf16[2,64,2048]{2,1,0:T(8,128)(2,1)}, u32[]{:S(2)}, u32[]{:S(2)}) %collective-permute-start.20) | collective-permute-done | bytes 524320 | tf_op jit(solution)/shard_map/ppermute | solution.py:37
  303.6 11.1 %collective-permute-done.19 = bf16[2,64,2048]{2,1,0:T(8,128)(2,1)} collective-permute-done((bf16[2,64,2048]{2,1,0:T(8,128)(2,1)}, bf16[2,64,2048]{2,1,0:T(8,128)(2,1)}, u32[]{:S(2)}, u32[]{:S(2)}) %collective-permute-start.19) | collective-permute-done | bytes 524320 | tf_op jit(solution)/shard_map/ppermute | solution.py:37
  331.5 23.6 %collective-permute-done.24 = bf16[2,48,2176]{2,1,0:T(8,128)(2,1)S(1)} collective-permute-done((bf16[2,48,2176]{2,1,0:T(8,128)(2,1)S(1)}, bf16[2,48,2176]{2,1,0:T(8,128)(2,1)S(1)}, u32[]{:S(2)}, u32[]{:S(2)}) %collective-permute-start.24) | collective-permute-done | bytes 417824 | tf_op jit(solution)/shard_map/ppermute | solution.py:37
  374.5 41.1 %expert_rows.2 = (bf16[768,2048]{1,0:T(8,128)(2,1)}, bf16[768,2176]{1,0:T(8,128)(2,1)}, bf16[768,1408]{1,0:T(8,128)(2,1)}, bf16[768,2816]{1,0:T(8,128)(2,1)}) custom-call(s32[2]{0:T(128)} %pad_add_fusion.1.place_ref, bf16[768,2176]{1,0:T(8,128)(2,1)} %pad_maximum_fusion.2.hidden.refs_0_.refs_4_, bf16[768,2048]{1,0:T(8,128)(2,1)} %copy-done.49, ...), custom_call_target="tpu_custom_call" | custom-call | flops 26575110144 | bytes 36175872 | tf_op jit(solution)/shard_map/expert_rows/pallas_call | solution.py:332
  420.6 40.7 %expert_rows.3 = (bf16[768,2048]{1,0:T(8,128)(2,1)}, bf16[768,2176]{1,0:T(8,128)(2,1)}, bf16[768,1408]{1,0:T(8,128)(2,1)}, bf16[768,2816]{1,0:T(8,128)(2,1)}) custom-call(s32[2]{0:T(128)} %pad_add_fusion.1.place_ref, bf16[768,2176]{1,0:T(8,128)(2,1)} %constant_dynamic-update-slice_fusion.4.hidden.refs_1_.refs_5_, bf16[768,2048]{1,0:T(8,128)(2,1)} %copy-done.48, ...), custom_call_target="tpu_custom_call" | custom-call | flops 26575110144 | bytes 36175872 | tf_op jit(solution)/shard_map/expert_rows/pallas_call | solution.py:332
  477.7 24.8 %expert_grads.2 = (bf16[512,4224]{1,0:T(8,128)(2,1)}, bf16[512,4224]{1,0:T(8,128)(2,1)}) custom-call(s32[4]{0:T(128)} %get-tuple-element.296.order, bf16[768,2176]{1,0:T(8,128)(2,1)} %pad_maximum_fusion.2.hidden.refs_0_.refs_4_, bf16[768,2176]{1,0:T(8,128)(2,1)} %constant_dynamic-update-slice_fusion.4.hidden.refs_1_.refs_5_, bf16[768,2048]{1,0:T(8,128)(2,1)} %copy-done.49, ...), custom_call_target="tpu_custom_call" | custom-call | flops 13287555072 | bytes 27918336 | tf_op jit(solution)/shard_map/expert_grads/pallas_call | solution.py:405
  524.0 25.0 %expert_grads.3 = (bf16[512,4224]{1,0:T(8,128)(2,1)}, bf16[512,4224]{1,0:T(8,128)(2,1)}) custom-call(s32[4]{0:T(128)} %get-tuple-element.297.order, bf16[768,2176]{1,0:T(8,128)(2,1)} %pad_maximum_fusion.2.hidden.refs_0_.refs_4_, bf16[768,2176]{1,0:T(8,128)(2,1)} %constant_dynamic-update-slice_fusion.4.hidden.refs_1_.refs_5_, bf16[768,2048]{1,0:T(8,128)(2,1)} %copy-done.49, ...), custom_call_target="tpu_custom_call" | custom-call | flops 13287555072 | bytes 27918336 | tf_op jit(solution)/shard_map/expert_grads/pallas_call | solution.py:405
  549.4 9.1 %collective-permute-done.40 = bf16[2,48,2176]{2,1,0:T(8,128)(2,1)S(1)} collective-permute-done((bf16[2,48,2176]{2,1,0:T(8,128)(2,1)S(1)}, bf16[2,48,2176]{2,1,0:T(8,128)(2,1)S(1)}, u32[]{:S(2)}, u32[]{:S(2)}) %collective-permute-start.40) | collective-permute-done | bytes 417824 | tf_op jit(solution)/shard_map/ppermute | solution.py:37
  572.0 16.1 %collective-permute-done.41 = bf16[2,64,2048]{2,1,0:T(8,128)(2,1)S(1)} collective-permute-done((bf16[2,64,2048]{2,1,0:T(8,128)(2,1)S(1)}, bf16[2,64,2048]{2,1,0:T(8,128)(2,1)S(1)}, u32[]{:S(2)}, u32[]{:S(2)}) %collective-permute-start.41) | collective-permute-done | bytes 524320 | tf_op jit(solution)/shard_map/ppermute | solution.py:37
  588.2 17.2 %collective-permute-done.42 = bf16[2,64,2048]{2,1,0:T(8,128)(2,1)S(1)} collective-permute-done((bf16[2,64,2048]{2,1,0:T(8,128)(2,1)S(1)}, bf16[2,64,2048]{2,1,0:T(8,128)(2,1)S(1)}, u32[]{:S(2)}, u32[]{:S(2)}) %collective-permute-start.42) | collective-permute-done | bytes 524320 | tf_op jit(solution)/shard_map/ppermute | solution.py:37
  605.4 10.3 %collective-permute-done.43 = bf16[2,64,2048]{2,1,0:T(8,128)(2,1)S(1)} collective-permute-done((bf16[2,64,2048]{2,1,0:T(8,128)(2,1)S(1)}, bf16[2,64,2048]{2,1,0:T(8,128)(2,1)S(1)}, u32[]{:S(2)}, u32[]{:S(2)}) %collective-permute-start.43) | collective-permute-done | bytes 524320 | tf_op jit(solution)/shard_map/ppermute | solution.py:37
  626.7 10.8 %fusion.180.vals_grad = f32[512,2048]{1,0:T(8,128)} fusion(bf16[512,2048]{1,0:T(8,128)(2,1)} %bitcast.432, bf16[2048,2048]{1,0:T(8,128)(2,1)} %all-gather.5.cloned.1.call-done), kind=kOutput, calls=%fused_computation.454 | convolution fusion | flops 4294967296 | bytes 14680064 | tf_op jit(solution)/shard_map/dot_general | solution.py:24
  637.5 8.0 add_convert_fusion.1
  651.9 20.1 %attention_backward.1 = (bf16[512,2048]{1,0:T(8,128)(2,1)S(1)}, bf16[512,512]{1,0:T(8,128)(2,1)S(1)}, bf16[512,512]{1,0:T(8,128)(2,1)S(1)}, f32[512,128]{1,0:T(8,128)S(1)}) custom-call(s32[2]{0:T(128)S(1)} %fusion.136.lens, bf16[512,2048]{1,0:T(8,128)(2,1)} %get-tuple-element.154.query, bf16[512,512]{1,0:T(8,128)(2,1)S(1)} %get-tuple-element.155.key, ...), custom_call_target="tpu_custom_call" | custom-call | flops 2684354560 | bytes 14680064 | tf_op jit(solution)/shard_map/attention_backward/pallas_call | solution.py:212
  685.8 8.5 add_convert_fusion.2
  704.9 9.9 %convolution_convert_fusion = bf16[2048,3072]{1,0:T(8,128)(2,1)} fusion(bf16[512,2048]{1,0:T(8,128)(2,1)S(1)} %bitcast.414, bf16[512,512]{1,0:T(8,128)(2,1)S(1)} %get-tuple-element.164, bf16[512,512]{1,0:T(8,128)(2,1)S(1)} %get-tuple-element.163, bf16[512,2048]{1,0:T(8,128)(2,1)S(1)} %get-tuple-element.162), kind=kOutput, calls=%fused_computation | convolution fusion | flops 6458179584 | bytes 17825792 | tf_op jit(solution)/shard_map/dot_general | solution.py:32
  718.2 8.0 collective-permute-done.51
  726.2 8.8 collective-permute-done.50
  766.0 10.3 %collective-permute-done.53 = bf16[256,512]{1,0:T(8,128)(2,1)S(1)} collective-permute-done((bf16[256,512]{1,0:T(8,128)(2,1)S(1)}, bf16[256,512]{1,0:T(8,128)(2,1)S(1)}, u32[]{:S(2)}, u32[]{:S(2)}) %collective-permute-start.53) | collective-permute-done | bytes 262176 | tf_op jit(solution)/shard_map/ppermute | solution.py:37
  783.3 17.3 %all-to-all-done.1 = bf16[8,48,2048]{2,1,0:T(8,128)(2,1)S(1)} async-done(((bf16[8,48,2048]{2,1,0:T(8,128)(2,1)}), bf16[8,48,2048]{2,1,0:T(8,128)(2,1)S(1)}, u32[]{:S(2)}, u32[]{:S(2)}) %all-to-all-start.1) | async-done | bytes 1572896 | tf_op jit(solution)/shard_map/all_to_all | solution.py:800
  845.8 7.9 reduce-scatter.5.cloned.1.call-done
  870.0 14.7 %collective-permute-done.58 = bf16[256,512]{1,0:T(8,128)(2,1)S(1)} collective-permute-done((bf16[256,512]{1,0:T(8,128)(2,1)S(1)}, bf16[256,512]{1,0:T(8,128)(2,1)S(1)}, u32[]{:S(2)}, u32[]{:S(2)}) %collective-permute-start.58) | collective-permute-done | bytes 262176 | tf_op jit(solution)/shard_map/ppermute | solution.py:37
  (585 shorter events, 362.6 us)
Async XLA Ops:
  7.2 195.9 %all-gather.3.cloned.1.call-start = ((), (), s32[]{:S(2)}) async-start(), calls=%async_computation.5 | async-start | bytes 14155776 | tf_op jit(solution)/shard_map/all_gather | solution.py:552
  14.3 78.1 %collective-permute-start.1 = (bf16[256,4224]{1,0:T(8,128)(2,1)}, bf16[256,4224]{1,0:T(8,128)(2,1)}, u32[]{:S(2)}, u32[]{:S(2)}) collective-permute-start(bf16[256,4224]{1,0:T(8,128)(2,1)} %pad_maximum_fusion.5), channel_id=1, source_target_pairs={{0,8},{4,12},{8,0},{12,4},{16,24},{20,28},{24,16},{28,20},{1,9},{5... | collective-permute-start | bytes 6488072 | tf_op jit(solution)/shard_map/ppermute | solution.py:37
  17.2 75.1 %collective-permute-start.3 = (bf16[256,4224]{1,0:T(8,128)(2,1)}, bf16[256,4224]{1,0:T(8,128)(2,1)}, u32[]{:S(2)}, u32[]{:S(2)}) collective-permute-start(bf16[256,4224]{1,0:T(8,128)(2,1)} %pad_maximum_fusion.4), channel_id=1, source_target_pairs={{0,16},{4,20},{8,24},{12,28},{16,0},{20,4},{24,8},{28,12},{1,17},{... | collective-permute-start | bytes 6488072 | tf_op jit(solution)/shard_map/ppermute | solution.py:37
  41.9 35.6 %collective-permute-start.12 = (bf16[256,1024]{1,0:T(8,128)(2,1)}, bf16[256,1024]{1,0:T(8,128)(2,1)S(1)}, u32[]{:S(2)}, u32[]{:S(2)}) collective-permute-start(bf16[256,1024]{1,0:T(8,128)(2,1)} %pad_maximum_fusion.14), channel_id=1, source_target_pairs={{0,2},{1,3},{2,0},{3,1},{4,6},{5,7},{6,4},{7,5},{8,10},{9,11},{10,... | collective-permute-start | bytes 1572872 | tf_op jit(solution)/shard_map/ppermute | solution.py:37
  42.7 47.1 %collective-permute-start.13 = (bf16[256,1024]{1,0:T(8,128)(2,1)}, bf16[256,1024]{1,0:T(8,128)(2,1)S(1)}, u32[]{:S(2)}, u32[]{:S(2)}) collective-permute-start(bf16[256,1024]{1,0:T(8,128)(2,1)} %pad_maximum_fusion.15), channel_id=1, source_target_pairs={{0,3},{1,2},{2,1},{3,0},{4,7},{5,6},{6,5},{7,4},{8,11},{9,10},{10,... | collective-permute-start | bytes 1572872 | tf_op jit(solution)/shard_map/ppermute | solution.py:37
  92.4 162.4 %all-gather.5.cloned.1.call-start = ((), (), s32[]{:S(2)}) async-start(), calls=%async_computation.6 | async-start | bytes 9437184 | tf_op jit(solution)/shard_map/all_gather | solution.py:553
  93.1 38.3 %collective-permute-start = (bf16[256,4224]{1,0:T(8,128)(2,1)}, bf16[256,4224]{1,0:T(8,128)(2,1)}, u32[]{:S(2)}, u32[]{:S(2)}) collective-permute-start(bf16[256,4224]{1,0:T(8,128)(2,1)} %pad_maximum_fusion.4), channel_id=1, source_target_pairs={{0,4},{4,0},{8,12},{12,8},{16,20},{20,16},{24,28},{28,24},{1,5},{5... | collective-permute-start | bytes 6488072 | tf_op jit(solution)/shard_map/ppermute | solution.py:37
  98.0 649.7 %reduce-scatter.3.cloned.1.call-start = ((), (), s32[]{:S(2)}) async-start(), calls=%async_computation.7 | async-start | bytes 9437184 | tf_op jit(solution)/shard_map/reduce_scatter | solution.py:758
  135.2 53.4 %collective-permute-start.6 = (bf16[2,64,2048]{2,1,0:T(8,128)(2,1)S(1)}, bf16[2,64,2048]{2,1,0:T(8,128)(2,1)S(1)}, u32[]{:S(2)}, u32[]{:S(2)}) collective-permute-start(bf16[2,64,2048]{2,1,0:T(8,128)(2,1)S(1)} %bitcast.434), channel_id=1, source_target_pairs={{0,2},{1,3},{2,0},{3,1},{4,6},{5,7},{6,4},{7,5},{8,10},{9,11},{10,... | collective-permute-start | bytes 1572872 | tf_op jit(solution)/shard_map/ppermute | solution.py:37
  157.5 44.0 %collective-permute-start.7 = (bf16[2,64,2048]{2,1,0:T(8,128)(2,1)S(1)}, bf16[2,64,2048]{2,1,0:T(8,128)(2,1)S(1)}, u32[]{:S(2)}, u32[]{:S(2)}) collective-permute-start(bf16[2,64,2048]{2,1,0:T(8,128)(2,1)S(1)} %bitcast.435), channel_id=1, source_target_pairs={{0,3},{1,2},{2,1},{3,0},{4,7},{5,6},{6,5},{7,4},{8,11},{9,10},{10,... | collective-permute-start | bytes 1572872 | tf_op jit(solution)/shard_map/ppermute | solution.py:37
  203.1 72.8 %collective-permute-start.16 = (bf16[256,4224]{1,0:T(8,128)(2,1)}, bf16[256,4224]{1,0:T(8,128)(2,1)}, u32[]{:S(2)}, u32[]{:S(2)}) collective-permute-start(bf16[256,4224]{1,0:T(8,128)(2,1)} %get-tuple-element.103.refs_0_), channel_id=1, source_target_pairs={{0,16},{4,20},{8,24},{12,28},{16,0},{20,4},{24,8},{28,12},{1,17},{... | collective-permute-start | bytes 6488072 | tf_op jit(solution)/shard_map/ppermute | solution.py:37
  203.7 72.2 %collective-permute-start.17 = (bf16[256,4224]{1,0:T(8,128)(2,1)}, bf16[256,4224]{1,0:T(8,128)(2,1)}, u32[]{:S(2)}, u32[]{:S(2)}) collective-permute-start(bf16[256,4224]{1,0:T(8,128)(2,1)} %get-tuple-element.104), channel_id=1, source_target_pairs={{0,8},{4,12},{8,0},{12,4},{16,24},{20,28},{24,16},{28,20},{1,9},{5... | collective-permute-start | bytes 6488072 | tf_op jit(solution)/shard_map/ppermute | solution.py:37
  204.3 118.0 %collective-permute-start.21 = (bf16[256,4224]{1,0:T(8,128)(2,1)}, bf16[256,4224]{1,0:T(8,128)(2,1)}, u32[]{:S(2)}, u32[]{:S(2)}) collective-permute-start(bf16[256,4224]{1,0:T(8,128)(2,1)} %collective-permute-done.1), channel_id=1, source_target_pairs={{0,16},{4,20},{8,24},{12,28},{16,0},{20,4},{24,8},{28,12},{1,17},{... | collective-permute-start | bytes 6488072 | tf_op jit(solution)/shard_map/ppermute | solution.py:37
  277.4 37.3 %collective-permute-start.19 = (bf16[2,64,2048]{2,1,0:T(8,128)(2,1)}, bf16[2,64,2048]{2,1,0:T(8,128)(2,1)}, u32[]{:S(2)}, u32[]{:S(2)}) collective-permute-start(bf16[2,64,2048]{2,1,0:T(8,128)(2,1)} %get-tuple-element.217), channel_id=1, source_target_pairs={{0,2},{1,3},{2,0},{3,1},{4,6},{5,7},{6,4},{7,5},{8,10},{9,11},{10,... | collective-permute-start | bytes 1572872 | tf_op jit(solution)/shard_map/ppermute | solution.py:37
  277.4 37.3 %collective-permute-start.18 = (bf16[2,64,2048]{2,1,0:T(8,128)(2,1)S(1)}, bf16[2,64,2048]{2,1,0:T(8,128)(2,1)}, u32[]{:S(2)}, u32[]{:S(2)}) collective-permute-start(bf16[2,64,2048]{2,1,0:T(8,128)(2,1)S(1)} %get-tuple-element.215), channel_id=1, source_target_pairs={{0,1},{1,0},{2,3},{3,2},{4,5},{5,4},{6,7},{7,6},{8,9},{9,8},{10,11... | collective-permute-start | bytes 1572872 | tf_op jit(solution)/shard_map/ppermute | solution.py:37
  280.8 86.1 %collective-permute-start.25 = (bf16[256,4224]{1,0:T(8,128)(2,1)}, bf16[256,4224]{1,0:T(8,128)(2,1)}, u32[]{:S(2)}, u32[]{:S(2)}) collective-permute-start(bf16[256,4224]{1,0:T(8,128)(2,1)} %collective-permute-done.17.refs_1_), channel_id=1, source_target_pairs={{0,16},{4,20},{8,24},{12,28},{16,0},{20,4},{24,8},{28,12},{1,17},{... | collective-permute-start | bytes 6488072 | tf_op jit(solution)/shard_map/ppermute | solution.py:37
  325.8 35.6 %collective-permute-start.29 = (bf16[384,2048]{1,0:T(8,128)(2,1)}, bf16[384,2048]{1,0:T(8,128)(2,1)}, u32[]{:S(2)}, u32[]{:S(2)}) collective-permute-start(bf16[384,2048]{1,0:T(8,128)(2,1)} %bitcast.419), channel_id=1, source_target_pairs={{0,8},{4,12},{8,0},{12,4},{16,24},{20,28},{24,16},{28,20},{1,9},{5... | collective-permute-start | bytes 4718600 | tf_op jit(solution)/shard_map/ppermute | solution.py:37
  369.3 46.3 %collective-permute-start.32 = (bf16[384,2176]{1,0:T(8,128)(2,1)S(1)}, bf16[384,2176]{1,0:T(8,128)(2,1)S(1)}, u32[]{:S(2)}, u32[]{:S(2)}) collective-permute-start(bf16[384,2176]{1,0:T(8,128)(2,1)S(1)} %bitcast.417), channel_id=1, source_target_pairs={{0,8},{4,12},{8,0},{12,4},{16,24},{20,28},{24,16},{28,20},{1,9},{5... | collective-permute-start | bytes 5013512 | tf_op jit(solution)/shard_map/ppermute | solution.py:37
  476.8 39.2 %collective-permute-start.31 = (bf16[384,2176]{1,0:T(8,128)(2,1)}, bf16[384,2176]{1,0:T(8,128)(2,1)}, u32[]{:S(2)}, u32[]{:S(2)}) collective-permute-start(bf16[384,2176]{1,0:T(8,128)(2,1)} %split.25), channel_id=1, source_target_pairs={{0,4},{4,0},{8,12},{12,8},{16,20},{20,16},{24,28},{28,24},{1,5},{5... | collective-permute-start | bytes 5013512 | tf_op jit(solution)/shard_map/ppermute | solution.py:37
  476.9 39.1 %collective-permute-start.35 = (bf16[384,2176]{1,0:T(8,128)(2,1)}, bf16[384,2176]{1,0:T(8,128)(2,1)}, u32[]{:S(2)}, u32[]{:S(2)}) collective-permute-start(bf16[384,2176]{1,0:T(8,128)(2,1)} %add_convert_fusion.3), channel_id=1, source_target_pairs={{0,8},{4,12},{8,0},{12,4},{16,24},{20,28},{24,16},{28,20},{1,9},{5... | collective-permute-start | bytes 5013512 | tf_op jit(solution)/shard_map/ppermute | solution.py:37
  502.5 117.2 %collective-permute-start.45 = (bf16[512,4224]{1,0:T(8,128)(2,1)}, bf16[512,4224]{1,0:T(8,128)(2,1)}, u32[]{:S(2)}, u32[]{:S(2)}) collective-permute-start(bf16[512,4224]{1,0:T(8,128)(2,1)} %get-tuple-element.127), channel_id=1, source_target_pairs={{0,16},{4,20},{8,24},{12,28},{16,0},{20,4},{24,8},{28,12},{1,17},{... | collective-permute-start | bytes 12976136 | tf_op jit(solution)/shard_map/ppermute | solution.py:37
  521.4 37.1 %collective-permute-start.40 = (bf16[2,48,2176]{2,1,0:T(8,128)(2,1)S(1)}, bf16[2,48,2176]{2,1,0:T(8,128)(2,1)S(1)}, u32[]{:S(2)}, u32[]{:S(2)}) collective-permute-start(bf16[2,48,2176]{2,1,0:T(8,128)(2,1)S(1)} %bitcast.459), channel_id=1, source_target_pairs={{0,3},{1,2},{2,1},{3,0},{4,7},{5,6},{6,5},{7,4},{8,11},{9,10},{10,... | collective-permute-start | bytes 1253384 | tf_op jit(solution)/shard_map/ppermute | solution.py:37
  522.5 93.3 %collective-permute-start.44 = (bf16[384,2048]{1,0:T(8,128)(2,1)}, bf16[384,2048]{1,0:T(8,128)(2,1)}, u32[]{:S(2)}, u32[]{:S(2)}) collective-permute-start(bf16[384,2048]{1,0:T(8,128)(2,1)} %add_convert_fusion.4), channel_id=1, source_target_pairs={{0,8},{4,12},{8,0},{12,4},{16,24},{20,28},{24,16},{28,20},{1,9},{5... | collective-permute-start | bytes 4718600 | tf_op jit(solution)/shard_map/ppermute | solution.py:37
  568.1 37.2 %collective-permute-start.42 = (bf16[2,64,2048]{2,1,0:T(8,128)(2,1)S(1)}, bf16[2,64,2048]{2,1,0:T(8,128)(2,1)S(1)}, u32[]{:S(2)}, u32[]{:S(2)}) collective-permute-start(bf16[2,64,2048]{2,1,0:T(8,128)(2,1)S(1)} %bitcast.441), channel_id=1, source_target_pairs={{0,2},{1,3},{2,0},{3,1},{4,6},{5,7},{6,4},{7,5},{8,10},{9,11},{10,... | collective-permute-start | bytes 1572872 | tf_op jit(solution)/shard_map/ppermute | solution.py:37
  570.6 45.1 %collective-permute-start.43 = (bf16[2,64,2048]{2,1,0:T(8,128)(2,1)S(1)}, bf16[2,64,2048]{2,1,0:T(8,128)(2,1)S(1)}, u32[]{:S(2)}, u32[]{:S(2)}) collective-permute-start(bf16[2,64,2048]{2,1,0:T(8,128)(2,1)S(1)} %bitcast.442), channel_id=1, source_target_pairs={{0,3},{1,2},{2,1},{3,0},{4,7},{5,6},{6,5},{7,4},{8,11},{9,10},{10,... | collective-permute-start | bytes 1572872 | tf_op jit(solution)/shard_map/ppermute | solution.py:37
  649.4 151.2 %collective-permute-start.55 = (bf16[512,4224]{1,0:T(8,128)(2,1)}, bf16[512,4224]{1,0:T(8,128)(2,1)}, u32[]{:S(2)}, u32[]{:S(2)}) collective-permute-start(bf16[512,4224]{1,0:T(8,128)(2,1)} %add_convert_fusion.1), channel_id=1, source_target_pairs={{0,8},{4,12},{8,0},{12,4},{16,24},{20,28},{24,16},{28,20},{1,9},{5... | collective-permute-start | bytes 12976136 | tf_op jit(solution)/shard_map/ppermute | solution.py:37
  650.9 149.7 %collective-permute-start.56 = (bf16[512,4224]{1,0:T(8,128)(2,1)}, bf16[512,4224]{1,0:T(8,128)(2,1)}, u32[]{:S(2)}, u32[]{:S(2)}) collective-permute-start(bf16[512,4224]{1,0:T(8,128)(2,1)} %get-tuple-element.172), channel_id=1, source_target_pairs={{0,16},{4,20},{8,24},{12,28},{16,0},{20,4},{24,8},{28,12},{1,17},{... | collective-permute-start | bytes 12976136 | tf_op jit(solution)/shard_map/ppermute | solution.py:37
  696.3 38.7 %collective-permute-start.50 = (bf16[2,64,2176]{2,1,0:T(8,128)(2,1)}, bf16[2,64,2176]{2,1,0:T(8,128)(2,1)}, u32[]{:S(2)}, u32[]{:S(2)}) collective-permute-start(bf16[2,64,2176]{2,1,0:T(8,128)(2,1)} %get-tuple-element.224), channel_id=1, source_target_pairs={{0,2},{1,3},{2,0},{3,1},{4,6},{5,7},{6,4},{7,5},{8,10},{9,11},{10,... | collective-permute-start | bytes 1671176 | tf_op jit(solution)/shard_map/ppermute | solution.py:37
  696.3 38.7 %collective-permute-start.49 = (bf16[2,64,2176]{2,1,0:T(8,128)(2,1)}, bf16[2,64,2176]{2,1,0:T(8,128)(2,1)}, u32[]{:S(2)}, u32[]{:S(2)}) collective-permute-start(bf16[2,64,2176]{2,1,0:T(8,128)(2,1)} %get-tuple-element.222), channel_id=1, source_target_pairs={{0,1},{1,0},{2,3},{3,2},{4,5},{5,4},{6,7},{7,6},{8,9},{9,8},{10,11... | collective-permute-start | bytes 1671176 | tf_op jit(solution)/shard_map/ppermute | solution.py:37
  744.1 56.5 %all-to-all-start.1 = ((bf16[8,48,2048]{2,1,0:T(8,128)(2,1)}), bf16[8,48,2048]{2,1,0:T(8,128)(2,1)S(1)}, u32[]{:S(2)}, u32[]{:S(2)}) async-start(bf16[8,48,2048]{2,1,0:T(8,128)(2,1)} %pad_maximum_fusion.11), calls=%async_computation.1 | async-start | bytes 3145728 | tf_op jit(solution)/shard_map/all_to_all | solution.py:800
  747.7 106.0 %reduce-scatter.5.cloned.1.call-start = ((), (), s32[]{:S(2)}) async-start(), calls=%async_computation.8 | async-start | bytes 14155776 | tf_op jit(solution)/shard_map/reduce_scatter | solution.py:776
  861.7 33.8 %collective-permute-start.60 = (bf16[256,512]{1,0:T(8,128)(2,1)S(1)}, bf16[256,512]{1,0:T(8,128)(2,1)S(1)}, u32[]{:S(2)}, u32[]{:S(2)}) collective-permute-start(bf16[256,512]{1,0:T(8,128)(2,1)S(1)} %get-tuple-element.238), channel_id=1, source_target_pairs={{0,0},{2,1},{1,2},{3,3},{4,4},{6,5},{5,6},{7,7},{8,8},{10,9},{9,10... | collective-permute-start | bytes 786440 | tf_op jit(solution)/shard_map/ppermute | solution.py:833
  (134 other events, 1755.2 us)
Sparse Core Ops, SparseCore 0:
  92.5 78.5 all-gather.2
  173.6 81.1 all-gather.4
  626.9 103.8 reduce-scatter.2
  757.3 96.3 reduce-scatter.4

commit v16 on v15

--- a/solution.py
+++ b/solution.py
@@ -277,27 +277,38 @@
     units = columns // 3
     width = grad.shape[1]
 
-    @pl.when(pl.program_id(0) == 0)
+    first = pl.program_id(0) == 0
+    blocks = unit_blocks(units)
+    copies = [[] for _ in blocks]
+    for k in range(piece_count):
+        base = (chip ^ k) * (2 * rows)
+        for piece, part in ((own_pieces[k], core), (near_pieces[k], 1 - core)):
+            held = weights.at[pl.ds(pl.multiple_of(base + part * rows, 16), rows)]
+            for group, (start, size) in zip(copies, blocks):
+                for offset in range(start, 3 * units, units):
+                    number = len(blocks) * len(group) + blocks.index((start, size))
+                    group.append(
+                        pltpu.make_async_copy(
+                            piece.at[:, pl.ds(offset, size)],
+                            held.at[:, pl.ds(offset, size)],
+                            sems.at[number],
+                        )
+                    )
+
+    @pl.when(first)
     def _():
-        copies = []
-        for k in range(piece_count):
-            base = (chip ^ k) * (2 * rows)
-            for number, (piece, part) in enumerate(
-                ((own_pieces[k], core), (near_pieces[k], 1 - core))
-            ):
-                start = pl.multiple_of(base + part * rows, 16)
-                copies.append(
-                    pltpu.make_async_copy(
-                        piece, weights.at[pl.ds(start, rows)], sems.at[2 * k + number]
-                    )
-                )
-        for copy in copies:
-            copy.start()
-        for copy in copies:
-            copy.wait()
+        for group in copies:
+            for copy in group:
+                copy.start()
 
     slot_sum = jnp.zeros((hidden.shape[0], 1), f32)
-    for start, size in unit_blocks(units):
+    for group, (start, size) in zip(copies, blocks):
+
+        @pl.when(first)
+        def _():
+            for copy in group:
+                copy.wait()
+
         gate_pre = dot(hidden[:, :width], weights[:, start : start + size])
         up_pre = dot(hidden[:, :width], weights[:, units + start : units + start + size])
         act_grad = dot(grad[...], weights[:, 2 * units + start : 2 * units + start + size])
@@ -339,7 +350,7 @@
             out_specs=[tiled(width), tiled(width + HDIM), tiled(units), tiled(2 * units)],
             scratch_shapes=[
                 pltpu.VMEM((width, columns), bf16),
-                pltpu.SemaphoreType.DMA((2 * count,)),
+                pltpu.SemaphoreType.DMA((6 * count * len(unit_blocks(units)),)),
             ],
         ),
         out_shape=[

time: 911 us -> 907 us (level)
  transfers between devices with their start and end apart: 70 -> 70, of which waited for: 38 -> 38; matrix products, arithmetic and copies ran while one was open for 23% -> 24% of each run, Pallas kernels for 14% -> 14%
where the time goes in v16:
time: 907 us; the launch traced here: 900 us
  waiting for transfers between devices  391 us (43%)
  Pallas kernels  163 us (18%)
  other arithmetic  96.6 us (11%)
  matrix products  80.9 us (9%)
  starting transfers between devices  77.7 us (9%)
  local copies, waits for them, and re-layouts  74.2 us (8%)
  between operations  17.1 us (2%)
    ppermute x59, waiting for transfers between devices, swap(): return lax.ppermute(value, axis, [(i, i ^ step) for i in range(count)])  324 us
    pallas_call x2, Pallas kernels, expert_rows(): pl.pallas_call(expert_kernel, grid_spec=pltpu.PrefetchScalarGridSpec(num_...  78.4 us
    ppermute x59, starting transfers between devices, swap(): return lax.ppermute(value, axis, [(i, i ^ step) for i in range(count)])  54.9 us
    pallas_call x2, Pallas kernels, expert_grads(): pl.pallas_call(functools.partial(expert_grad_kernel, cuts), grid_spec=plt...  49.7 us
    dot_general x5, matrix products, dot(): return jnp.dot(left, right, preferred_element_type=f32)  25 us
    dot_general x5, matrix products, dot_t(): lax.dot_general(left, right, (((1,), (1,)), ((), ())), preferred_element_...  23.6 us
    unnamed x213, local copies, waits for them, and re-layouts  20.7 us
    pallas_call x1, Pallas kernels, attention_backward(): pl.pallas_call(backward_kernel, grid_spec=pltpu.PrefetchScalarGridSpec(nu...  20.1 us
  transfers between devices with their start and end apart: 70, of which 38 were waited for; matrix products, arithmetic and copies ran while one was open for 24% of the time, Pallas kernels for 14%

profile of v16, /device:TPU:8, one launch (start us, length us, event | category | flops | bytes accessed | tf_op | source)
XLA Modules:
  0.0 900.3 jit_solution(1888413465889469632)
XLA Ops:
  51.3 26.2 %collective-permute-done.12 = bf16[256,1024]{1,0:T(8,128)(2,1)S(1)} collective-permute-done((bf16[256,1024]{1,0:T(8,128)(2,1)}, bf16[256,1024]{1,0:T(8,128)(2,1)S(1)}, u32[]{:S(2)}, u32[]{:S(2)}) %collective-permute-start.12) | collective-permute-done | bytes 524320 | tf_op jit(solution)/shard_map/ppermute | solution.py:37
  77.6 12.2 %collective-permute-done.13 = bf16[256,1024]{1,0:T(8,128)(2,1)S(1)} collective-permute-done((bf16[256,1024]{1,0:T(8,128)(2,1)}, bf16[256,1024]{1,0:T(8,128)(2,1)S(1)}, u32[]{:S(2)}, u32[]{:S(2)}) %collective-permute-start.13) | collective-permute-done | bytes 524320 | tf_op jit(solution)/shard_map/ppermute | solution.py:37
  106.1 18.4 %all-to-all-done = bf16[8,4,8,2048]{3,2,1,0:T(8,128)(2,1)S(1)} async-done(((bf16[8,4,8,2048]{3,2,1,0:T(8,128)(2,1)}), bf16[8,4,8,2048]{3,2,1,0:T(8,128)(2,1)S(1)}, u32[]{:S(2)}, u32[]{:S(2)}) %all-to-all-start) | async-done | bytes 1048608 | tf_op jit(solution)/shard_map/all_to_all | solution.py:487
  136.8 12.2 %collective-permute-done.10 = bf16[2,48,2048]{2,1,0:T(8,128)(2,1)S(1)} collective-permute-done((bf16[2,48,2048]{2,1,0:T(8,128)(2,1)}, bf16[2,48,2048]{2,1,0:T(8,128)(2,1)S(1)}, u32[]{:S(2)}, u32[]{:S(2)}) %collective-permute-start.10) | collective-permute-done | bytes 393248 | tf_op jit(solution)/shard_map/ppermute | solution.py:37
  167.8 20.8 %collective-permute-done.6 = bf16[2,64,2048]{2,1,0:T(8,128)(2,1)S(1)} collective-permute-done((bf16[2,64,2048]{2,1,0:T(8,128)(2,1)S(1)}, bf16[2,64,2048]{2,1,0:T(8,128)(2,1)S(1)}, u32[]{:S(2)}, u32[]{:S(2)}) %collective-permute-start.6) | collective-permute-done | bytes 524320 | tf_op jit(solution)/shard_map/ppermute | solution.py:37
  188.7 12.8 %collective-permute-done.7 = bf16[2,64,2048]{2,1,0:T(8,128)(2,1)S(1)} collective-permute-done((bf16[2,64,2048]{2,1,0:T(8,128)(2,1)S(1)}, bf16[2,64,2048]{2,1,0:T(8,128)(2,1)S(1)}, u32[]{:S(2)}, u32[]{:S(2)}) %collective-permute-start.7) | collective-permute-done | bytes 524320 | tf_op jit(solution)/shard_map/ppermute | solution.py:37
  218.6 14.8 %attention_forward.1 = (bf16[512,2048]{1,0:T(8,128)(2,1)S(1)}, bf16[512,2048]{1,0:T(8,128)(2,1)}, bf16[512,2048]{1,0:T(8,128)(2,1)}, bf16[512,512]{1,0:T(8,128)(...) custom-call(s32[2]{0:T(128)S(1)} %fusion.136.lens, f32[512,2048]{1,0:T(8,128)} %fusion.2.query, ...), custom_call_target="tpu_custom_call" | custom-call | flops 1073741824 | bytes 14680064 | tf_op jit(solution)/shard_map/attention_forward/pallas_call | solution.py:181
  234.8 20.0 %all-gather.5.cloned.1.call-done = bf16[2048,2048]{1,0:T(8,128)(2,1)} async-done(((bf16[256,2048]{1,0:T(8,128)(2,1)}), bf16[2048,2048]{1,0:T(8,128)(2,1)}) %all-gather.5.cloned.1.call-update) | async-done | bytes 8388624 | tf_op jit(solution)/shard_map/all_gather | solution.py:564
  254.8 8.1 fusion.178
  262.9 13.0 %collective-permute-done.16.refs_2_ = bf16[256,4224]{1,0:T(8,128)(2,1)} collective-permute-done((bf16[256,4224]{1,0:T(8,128)(2,1)}, bf16[256,4224]{1,0:T(8,128)(2,1)}, u32[]{:S(2)}, u32[]{:S(2)}) %collective-permute-start.16) | collective-permute-done | bytes 2162720 | tf_op jit(solution)/shard_map/ppermute | solution.py:37
  281.3 22.7 %collective-permute-done.20 = bf16[2,64,2048]{2,1,0:T(8,128)(2,1)} collective-permute-done((bf16[2,64,2048]{2,1,0:T(8,128)(2,1)}, bf16[2,64,2048]{2,1,0:T(8,128)(2,1)}, u32[]{:S(2)}, u32[]{:S(2)}) %collective-permute-start.20) | collective-permute-done | bytes 524320 | tf_op jit(solution)/shard_map/ppermute | solution.py:37
  304.1 11.1 %collective-permute-done.19 = bf16[2,64,2048]{2,1,0:T(8,128)(2,1)} collective-permute-done((bf16[2,64,2048]{2,1,0:T(8,128)(2,1)}, bf16[2,64,2048]{2,1,0:T(8,128)(2,1)}, u32[]{:S(2)}, u32[]{:S(2)}) %collective-permute-start.19) | collective-permute-done | bytes 524320 | tf_op jit(solution)/shard_map/ppermute | solution.py:37
  331.5 24.0 %collective-permute-done.24 = bf16[2,48,2176]{2,1,0:T(8,128)(2,1)S(1)} collective-permute-done((bf16[2,48,2176]{2,1,0:T(8,128)(2,1)S(1)}, bf16[2,48,2176]{2,1,0:T(8,128)(2,1)S(1)}, u32[]{:S(2)}, u32[]{:S(2)}) %collective-permute-start.24) | collective-permute-done | bytes 417824 | tf_op jit(solution)/shard_map/ppermute | solution.py:37
  374.5 39.1 %expert_rows.2 = (bf16[768,2048]{1,0:T(8,128)(2,1)}, bf16[768,2176]{1,0:T(8,128)(2,1)}, bf16[768,1408]{1,0:T(8,128)(2,1)}, bf16[768,2816]{1,0:T(8,128)(2,1)}) custom-call(s32[2]{0:T(128)} %pad_add_fusion.1.place_ref, bf16[768,2176]{1,0:T(8,128)(2,1)} %pad_maximum_fusion.2.hidden.refs_0_.refs_4_, bf16[768,2048]{1,0:T(8,128)(2,1)} %copy-done.49, ...), custom_call_target="tpu_custom_call" | custom-call | flops 26575110144 | bytes 36175872 | tf_op jit(solution)/shard_map/expert_rows/pallas_call | solution.py:343
  418.7 39.3 %expert_rows.3 = (bf16[768,2048]{1,0:T(8,128)(2,1)}, bf16[768,2176]{1,0:T(8,128)(2,1)}, bf16[768,1408]{1,0:T(8,128)(2,1)}, bf16[768,2816]{1,0:T(8,128)(2,1)}) custom-call(s32[2]{0:T(128)} %pad_add_fusion.1.place_ref, bf16[768,2176]{1,0:T(8,128)(2,1)} %constant_dynamic-update-slice_fusion.4.hidden.refs_1_.refs_5_, bf16[768,2048]{1,0:T(8,128)(2,1)} %copy-done.48, ...), custom_call_target="tpu_custom_call" | custom-call | flops 26575110144 | bytes 36175872 | tf_op jit(solution)/shard_map/expert_rows/pallas_call | solution.py:343
  474.4 24.8 %expert_grads.2 = (bf16[512,4224]{1,0:T(8,128)(2,1)}, bf16[512,4224]{1,0:T(8,128)(2,1)}) custom-call(s32[4]{0:T(128)} %get-tuple-element.296.order, bf16[768,2176]{1,0:T(8,128)(2,1)} %pad_maximum_fusion.2.hidden.refs_0_.refs_4_, bf16[768,2176]{1,0:T(8,128)(2,1)} %constant_dynamic-update-slice_fusion.4.hidden.refs_1_.refs_5_, bf16[768,2048]{1,0:T(8,128)(2,1)} %copy-done.49, ...), custom_call_target="tpu_custom_call" | custom-call | flops 13287555072 | bytes 27918336 | tf_op jit(solution)/shard_map/expert_grads/pallas_call | solution.py:416
  520.9 25.0 %expert_grads.3 = (bf16[512,4224]{1,0:T(8,128)(2,1)}, bf16[512,4224]{1,0:T(8,128)(2,1)}) custom-call(s32[4]{0:T(128)} %get-tuple-element.297.order, bf16[768,2176]{1,0:T(8,128)(2,1)} %pad_maximum_fusion.2.hidden.refs_0_.refs_4_, bf16[768,2176]{1,0:T(8,128)(2,1)} %constant_dynamic-update-slice_fusion.4.hidden.refs_1_.refs_5_, bf16[768,2048]{1,0:T(8,128)(2,1)} %copy-done.49, ...), custom_call_target="tpu_custom_call" | custom-call | flops 13287555072 | bytes 27918336 | tf_op jit(solution)/shard_map/expert_grads/pallas_call | solution.py:416
  546.1 9.1 %collective-permute-done.40 = bf16[2,48,2176]{2,1,0:T(8,128)(2,1)S(1)} collective-permute-done((bf16[2,48,2176]{2,1,0:T(8,128)(2,1)S(1)}, bf16[2,48,2176]{2,1,0:T(8,128)(2,1)S(1)}, u32[]{:S(2)}, u32[]{:S(2)}) %collective-permute-start.40) | collective-permute-done | bytes 417824 | tf_op jit(solution)/shard_map/ppermute | solution.py:37
  568.7 16.1 %collective-permute-done.41 = bf16[2,64,2048]{2,1,0:T(8,128)(2,1)S(1)} collective-permute-done((bf16[2,64,2048]{2,1,0:T(8,128)(2,1)S(1)}, bf16[2,64,2048]{2,1,0:T(8,128)(2,1)S(1)}, u32[]{:S(2)}, u32[]{:S(2)}) %collective-permute-start.41) | collective-permute-done | bytes 524320 | tf_op jit(solution)/shard_map/ppermute | solution.py:37
  584.9 17.2 %collective-permute-done.42 = bf16[2,64,2048]{2,1,0:T(8,128)(2,1)S(1)} collective-permute-done((bf16[2,64,2048]{2,1,0:T(8,128)(2,1)S(1)}, bf16[2,64,2048]{2,1,0:T(8,128)(2,1)S(1)}, u32[]{:S(2)}, u32[]{:S(2)}) %collective-permute-start.42) | collective-permute-done | bytes 524320 | tf_op jit(solution)/shard_map/ppermute | solution.py:37
  602.1 10.3 %collective-permute-done.43 = bf16[2,64,2048]{2,1,0:T(8,128)(2,1)S(1)} collective-permute-done((bf16[2,64,2048]{2,1,0:T(8,128)(2,1)S(1)}, bf16[2,64,2048]{2,1,0:T(8,128)(2,1)S(1)}, u32[]{:S(2)}, u32[]{:S(2)}) %collective-permute-start.43) | collective-permute-done | bytes 524320 | tf_op jit(solution)/shard_map/ppermute | solution.py:37
  623.4 10.8 %fusion.180.vals_grad = f32[512,2048]{1,0:T(8,128)} fusion(bf16[512,2048]{1,0:T(8,128)(2,1)} %bitcast.432, bf16[2048,2048]{1,0:T(8,128)(2,1)} %all-gather.5.cloned.1.call-done), kind=kOutput, calls=%fused_computation.454 | convolution fusion | flops 4294967296 | bytes 14680064 | tf_op jit(solution)/shard_map/dot_general | solution.py:24
  634.1 8.0 add_convert_fusion.1
  648.5 20.1 %attention_backward.1 = (bf16[512,2048]{1,0:T(8,128)(2,1)S(1)}, bf16[512,512]{1,0:T(8,128)(2,1)S(1)}, bf16[512,512]{1,0:T(8,128)(2,1)S(1)}, f32[512,128]{1,0:T(8,128)S(1)}) custom-call(s32[2]{0:T(128)S(1)} %fusion.136.lens, bf16[512,2048]{1,0:T(8,128)(2,1)} %get-tuple-element.154.query, bf16[512,512]{1,0:T(8,128)(2,1)S(1)} %get-tuple-element.155.key, ...), custom_call_target="tpu_custom_call" | custom-call | flops 2684354560 | bytes 14680064 | tf_op jit(solution)/shard_map/attention_backward/pallas_call | solution.py:212
  682.5 8.5 add_convert_fusion.2
  701.6 9.9 %convolution_convert_fusion = bf16[2048,3072]{1,0:T(8,128)(2,1)} fusion(bf16[512,2048]{1,0:T(8,128)(2,1)S(1)} %bitcast.414, bf16[512,512]{1,0:T(8,128)(2,1)S(1)} %get-tuple-element.164, bf16[512,512]{1,0:T(8,128)(2,1)S(1)} %get-tuple-element.163, bf16[512,2048]{1,0:T(8,128)(2,1)S(1)} %get-tuple-element.162), kind=kOutput, calls=%fused_computation | convolution fusion | flops 6458179584 | bytes 17825792 | tf_op jit(solution)/shard_map/dot_general | solution.py:32
  714.9 8.0 collective-permute-done.51
  722.9 8.7 collective-permute-done.50
  762.6 10.3 %collective-permute-done.53 = bf16[256,512]{1,0:T(8,128)(2,1)S(1)} collective-permute-done((bf16[256,512]{1,0:T(8,128)(2,1)S(1)}, bf16[256,512]{1,0:T(8,128)(2,1)S(1)}, u32[]{:S(2)}, u32[]{:S(2)}) %collective-permute-start.53) | collective-permute-done | bytes 262176 | tf_op jit(solution)/shard_map/ppermute | solution.py:37
  779.9 17.7 %all-to-all-done.1 = bf16[8,48,2048]{2,1,0:T(8,128)(2,1)S(1)} async-done(((bf16[8,48,2048]{2,1,0:T(8,128)(2,1)}), bf16[8,48,2048]{2,1,0:T(8,128)(2,1)S(1)}, u32[]{:S(2)}, u32[]{:S(2)}) %all-to-all-start.1) | async-done | bytes 1572896 | tf_op jit(solution)/shard_map/all_to_all | solution.py:811
  843.0 7.3 reduce-scatter.5.cloned.1.call-done
  866.7 14.7 %collective-permute-done.58 = bf16[256,512]{1,0:T(8,128)(2,1)S(1)} collective-permute-done((bf16[256,512]{1,0:T(8,128)(2,1)S(1)}, bf16[256,512]{1,0:T(8,128)(2,1)S(1)}, u32[]{:S(2)}, u32[]{:S(2)}) %collective-permute-start.58) | collective-permute-done | bytes 262176 | tf_op jit(solution)/shard_map/ppermute | solution.py:37
  (585 shorter events, 361.9 us)
Async XLA Ops:
  7.2 195.9 %all-gather.3.cloned.1.call-start = ((), (), s32[]{:S(2)}) async-start(), calls=%async_computation.5 | async-start | bytes 14155776 | tf_op jit(solution)/shard_map/all_gather | solution.py:563
  14.3 78.1 %collective-permute-start.1 = (bf16[256,4224]{1,0:T(8,128)(2,1)}, bf16[256,4224]{1,0:T(8,128)(2,1)}, u32[]{:S(2)}, u32[]{:S(2)}) collective-permute-start(bf16[256,4224]{1,0:T(8,128)(2,1)} %pad_maximum_fusion.5), channel_id=1, source_target_pairs={{0,8},{4,12},{8,0},{12,4},{16,24},{20,28},{24,16},{28,20},{1,9},{5... | collective-permute-start | bytes 6488072 | tf_op jit(solution)/shard_map/ppermute | solution.py:37
  17.2 75.1 %collective-permute-start.3 = (bf16[256,4224]{1,0:T(8,128)(2,1)}, bf16[256,4224]{1,0:T(8,128)(2,1)}, u32[]{:S(2)}, u32[]{:S(2)}) collective-permute-start(bf16[256,4224]{1,0:T(8,128)(2,1)} %pad_maximum_fusion.4), channel_id=1, source_target_pairs={{0,16},{4,20},{8,24},{12,28},{16,0},{20,4},{24,8},{28,12},{1,17},{... | collective-permute-start | bytes 6488072 | tf_op jit(solution)/shard_map/ppermute | solution.py:37
  41.9 35.6 %collective-permute-start.12 = (bf16[256,1024]{1,0:T(8,128)(2,1)}, bf16[256,1024]{1,0:T(8,128)(2,1)S(1)}, u32[]{:S(2)}, u32[]{:S(2)}) collective-permute-start(bf16[256,1024]{1,0:T(8,128)(2,1)} %pad_maximum_fusion.14), channel_id=1, source_target_pairs={{0,2},{1,3},{2,0},{3,1},{4,6},{5,7},{6,4},{7,5},{8,10},{9,11},{10,... | collective-permute-start | bytes 1572872 | tf_op jit(solution)/shard_map/ppermute | solution.py:37
  42.7 47.1 %collective-permute-start.13 = (bf16[256,1024]{1,0:T(8,128)(2,1)}, bf16[256,1024]{1,0:T(8,128)(2,1)S(1)}, u32[]{:S(2)}, u32[]{:S(2)}) collective-permute-start(bf16[256,1024]{1,0:T(8,128)(2,1)} %pad_maximum_fusion.15), channel_id=1, source_target_pairs={{0,3},{1,2},{2,1},{3,0},{4,7},{5,6},{6,5},{7,4},{8,11},{9,10},{10,... | collective-permute-start | bytes 1572872 | tf_op jit(solution)/shard_map/ppermute | solution.py:37
  92.4 162.4 %all-gather.5.cloned.1.call-start = ((), (), s32[]{:S(2)}) async-start(), calls=%async_computation.6 | async-start | bytes 9437184 | tf_op jit(solution)/shard_map/all_gather | solution.py:564
  93.1 38.3 %collective-permute-start = (bf16[256,4224]{1,0:T(8,128)(2,1)}, bf16[256,4224]{1,0:T(8,128)(2,1)}, u32[]{:S(2)}, u32[]{:S(2)}) collective-permute-start(bf16[256,4224]{1,0:T(8,128)(2,1)} %pad_maximum_fusion.4), channel_id=1, source_target_pairs={{0,4},{4,0},{8,12},{12,8},{16,20},{20,16},{24,28},{28,24},{1,5},{5... | collective-permute-start | bytes 6488072 | tf_op jit(solution)/shard_map/ppermute | solution.py:37
  98.0 646.3 %reduce-scatter.3.cloned.1.call-start = ((), (), s32[]{:S(2)}) async-start(), calls=%async_computation.7 | async-start | bytes 9437184 | tf_op jit(solution)/shard_map/reduce_scatter | solution.py:769
  135.2 53.4 %collective-permute-start.6 = (bf16[2,64,2048]{2,1,0:T(8,128)(2,1)S(1)}, bf16[2,64,2048]{2,1,0:T(8,128)(2,1)S(1)}, u32[]{:S(2)}, u32[]{:S(2)}) collective-permute-start(bf16[2,64,2048]{2,1,0:T(8,128)(2,1)S(1)} %bitcast.434), channel_id=1, source_target_pairs={{0,2},{1,3},{2,0},{3,1},{4,6},{5,7},{6,4},{7,5},{8,10},{9,11},{10,... | collective-permute-start | bytes 1572872 | tf_op jit(solution)/shard_map/ppermute | solution.py:37
  157.5 44.0 %collective-permute-start.7 = (bf16[2,64,2048]{2,1,0:T(8,128)(2,1)S(1)}, bf16[2,64,2048]{2,1,0:T(8,128)(2,1)S(1)}, u32[]{:S(2)}, u32[]{:S(2)}) collective-permute-start(bf16[2,64,2048]{2,1,0:T(8,128)(2,1)S(1)} %bitcast.435), channel_id=1, source_target_pairs={{0,3},{1,2},{2,1},{3,0},{4,7},{5,6},{6,5},{7,4},{8,11},{9,10},{10,... | collective-permute-start | bytes 1572872 | tf_op jit(solution)/shard_map/ppermute | solution.py:37
  203.1 72.8 %collective-permute-start.16 = (bf16[256,4224]{1,0:T(8,128)(2,1)}, bf16[256,4224]{1,0:T(8,128)(2,1)}, u32[]{:S(2)}, u32[]{:S(2)}) collective-permute-start(bf16[256,4224]{1,0:T(8,128)(2,1)} %get-tuple-element.103.refs_0_), channel_id=1, source_target_pairs={{0,16},{4,20},{8,24},{12,28},{16,0},{20,4},{24,8},{28,12},{1,17},{... | collective-permute-start | bytes 6488072 | tf_op jit(solution)/shard_map/ppermute | solution.py:37
  203.7 72.2 %collective-permute-start.17 = (bf16[256,4224]{1,0:T(8,128)(2,1)}, bf16[256,4224]{1,0:T(8,128)(2,1)}, u32[]{:S(2)}, u32[]{:S(2)}) collective-permute-start(bf16[256,4224]{1,0:T(8,128)(2,1)} %get-tuple-element.104), channel_id=1, source_target_pairs={{0,8},{4,12},{8,0},{12,4},{16,24},{20,28},{24,16},{28,20},{1,9},{5... | collective-permute-start | bytes 6488072 | tf_op jit(solution)/shard_map/ppermute | solution.py:37
  204.3 118.0 %collective-permute-start.21 = (bf16[256,4224]{1,0:T(8,128)(2,1)}, bf16[256,4224]{1,0:T(8,128)(2,1)}, u32[]{:S(2)}, u32[]{:S(2)}) collective-permute-start(bf16[256,4224]{1,0:T(8,128)(2,1)} %collective-permute-done.1), channel_id=1, source_target_pairs={{0,16},{4,20},{8,24},{12,28},{16,0},{20,4},{24,8},{28,12},{1,17},{... | collective-permute-start | bytes 6488072 | tf_op jit(solution)/shard_map/ppermute | solution.py:37
  277.4 37.8 %collective-permute-start.19 = (bf16[2,64,2048]{2,1,0:T(8,128)(2,1)}, bf16[2,64,2048]{2,1,0:T(8,128)(2,1)}, u32[]{:S(2)}, u32[]{:S(2)}) collective-permute-start(bf16[2,64,2048]{2,1,0:T(8,128)(2,1)} %get-tuple-element.217), channel_id=1, source_target_pairs={{0,2},{1,3},{2,0},{3,1},{4,6},{5,7},{6,4},{7,5},{8,10},{9,11},{10,... | collective-permute-start | bytes 1572872 | tf_op jit(solution)/shard_map/ppermute | solution.py:37
  277.4 37.8 %collective-permute-start.18 = (bf16[2,64,2048]{2,1,0:T(8,128)(2,1)S(1)}, bf16[2,64,2048]{2,1,0:T(8,128)(2,1)}, u32[]{:S(2)}, u32[]{:S(2)}) collective-permute-start(bf16[2,64,2048]{2,1,0:T(8,128)(2,1)S(1)} %get-tuple-element.215), channel_id=1, source_target_pairs={{0,1},{1,0},{2,3},{3,2},{4,5},{5,4},{6,7},{7,6},{8,9},{9,8},{10,11... | collective-permute-start | bytes 1572872 | tf_op jit(solution)/shard_map/ppermute | solution.py:37
  280.8 86.1 %collective-permute-start.25 = (bf16[256,4224]{1,0:T(8,128)(2,1)}, bf16[256,4224]{1,0:T(8,128)(2,1)}, u32[]{:S(2)}, u32[]{:S(2)}) collective-permute-start(bf16[256,4224]{1,0:T(8,128)(2,1)} %collective-permute-done.17.refs_1_), channel_id=1, source_target_pairs={{0,16},{4,20},{8,24},{12,28},{16,0},{20,4},{24,8},{28,12},{1,17},{... | collective-permute-start | bytes 6488072 | tf_op jit(solution)/shard_map/ppermute | solution.py:37
  325.8 35.6 %collective-permute-start.29 = (bf16[384,2048]{1,0:T(8,128)(2,1)}, bf16[384,2048]{1,0:T(8,128)(2,1)}, u32[]{:S(2)}, u32[]{:S(2)}) collective-permute-start(bf16[384,2048]{1,0:T(8,128)(2,1)} %bitcast.419), channel_id=1, source_target_pairs={{0,8},{4,12},{8,0},{12,4},{16,24},{20,28},{24,16},{28,20},{1,9},{5... | collective-permute-start | bytes 4718600 | tf_op jit(solution)/shard_map/ppermute | solution.py:37
  369.3 44.4 %collective-permute-start.32 = (bf16[384,2176]{1,0:T(8,128)(2,1)S(1)}, bf16[384,2176]{1,0:T(8,128)(2,1)S(1)}, u32[]{:S(2)}, u32[]{:S(2)}) collective-permute-start(bf16[384,2176]{1,0:T(8,128)(2,1)S(1)} %bitcast.417), channel_id=1, source_target_pairs={{0,8},{4,12},{8,0},{12,4},{16,24},{20,28},{24,16},{28,20},{1,9},{5... | collective-permute-start | bytes 5013512 | tf_op jit(solution)/shard_map/ppermute | solution.py:37
  473.4 39.2 %collective-permute-start.31 = (bf16[384,2176]{1,0:T(8,128)(2,1)}, bf16[384,2176]{1,0:T(8,128)(2,1)}, u32[]{:S(2)}, u32[]{:S(2)}) collective-permute-start(bf16[384,2176]{1,0:T(8,128)(2,1)} %split.25), channel_id=1, source_target_pairs={{0,4},{4,0},{8,12},{12,8},{16,20},{20,16},{24,28},{28,24},{1,5},{5... | collective-permute-start | bytes 5013512 | tf_op jit(solution)/shard_map/ppermute | solution.py:37
  473.6 39.1 %collective-permute-start.35 = (bf16[384,2176]{1,0:T(8,128)(2,1)}, bf16[384,2176]{1,0:T(8,128)(2,1)}, u32[]{:S(2)}, u32[]{:S(2)}) collective-permute-start(bf16[384,2176]{1,0:T(8,128)(2,1)} %add_convert_fusion.3), channel_id=1, source_target_pairs={{0,8},{4,12},{8,0},{12,4},{16,24},{20,28},{24,16},{28,20},{1,9},{5... | collective-permute-start | bytes 5013512 | tf_op jit(solution)/shard_map/ppermute | solution.py:37
  499.2 117.2 %collective-permute-start.45 = (bf16[512,4224]{1,0:T(8,128)(2,1)}, bf16[512,4224]{1,0:T(8,128)(2,1)}, u32[]{:S(2)}, u32[]{:S(2)}) collective-permute-start(bf16[512,4224]{1,0:T(8,128)(2,1)} %get-tuple-element.127), channel_id=1, source_target_pairs={{0,16},{4,20},{8,24},{12,28},{16,0},{20,4},{24,8},{28,12},{1,17},{... | collective-permute-start | bytes 12976136 | tf_op jit(solution)/shard_map/ppermute | solution.py:37
  518.1 37.1 %collective-permute-start.40 = (bf16[2,48,2176]{2,1,0:T(8,128)(2,1)S(1)}, bf16[2,48,2176]{2,1,0:T(8,128)(2,1)S(1)}, u32[]{:S(2)}, u32[]{:S(2)}) collective-permute-start(bf16[2,48,2176]{2,1,0:T(8,128)(2,1)S(1)} %bitcast.459), channel_id=1, source_target_pairs={{0,3},{1,2},{2,1},{3,0},{4,7},{5,6},{6,5},{7,4},{8,11},{9,10},{10,... | collective-permute-start | bytes 1253384 | tf_op jit(solution)/shard_map/ppermute | solution.py:37
  519.2 93.3 %collective-permute-start.44 = (bf16[384,2048]{1,0:T(8,128)(2,1)}, bf16[384,2048]{1,0:T(8,128)(2,1)}, u32[]{:S(2)}, u32[]{:S(2)}) collective-permute-start(bf16[384,2048]{1,0:T(8,128)(2,1)} %add_convert_fusion.4), channel_id=1, source_target_pairs={{0,8},{4,12},{8,0},{12,4},{16,24},{20,28},{24,16},{28,20},{1,9},{5... | collective-permute-start | bytes 4718600 | tf_op jit(solution)/shard_map/ppermute | solution.py:37
  564.8 37.2 %collective-permute-start.42 = (bf16[2,64,2048]{2,1,0:T(8,128)(2,1)S(1)}, bf16[2,64,2048]{2,1,0:T(8,128)(2,1)S(1)}, u32[]{:S(2)}, u32[]{:S(2)}) collective-permute-start(bf16[2,64,2048]{2,1,0:T(8,128)(2,1)S(1)} %bitcast.441), channel_id=1, source_target_pairs={{0,2},{1,3},{2,0},{3,1},{4,6},{5,7},{6,4},{7,5},{8,10},{9,11},{10,... | collective-permute-start | bytes 1572872 | tf_op jit(solution)/shard_map/ppermute | solution.py:37
  567.2 45.1 %collective-permute-start.43 = (bf16[2,64,2048]{2,1,0:T(8,128)(2,1)S(1)}, bf16[2,64,2048]{2,1,0:T(8,128)(2,1)S(1)}, u32[]{:S(2)}, u32[]{:S(2)}) collective-permute-start(bf16[2,64,2048]{2,1,0:T(8,128)(2,1)S(1)} %bitcast.442), channel_id=1, source_target_pairs={{0,3},{1,2},{2,1},{3,0},{4,7},{5,6},{6,5},{7,4},{8,11},{9,10},{10,... | collective-permute-start | bytes 1572872 | tf_op jit(solution)/shard_map/ppermute | solution.py:37
  646.0 151.6 %collective-permute-start.55 = (bf16[512,4224]{1,0:T(8,128)(2,1)}, bf16[512,4224]{1,0:T(8,128)(2,1)}, u32[]{:S(2)}, u32[]{:S(2)}) collective-permute-start(bf16[512,4224]{1,0:T(8,128)(2,1)} %add_convert_fusion.1), channel_id=1, source_target_pairs={{0,8},{4,12},{8,0},{12,4},{16,24},{20,28},{24,16},{28,20},{1,9},{5... | collective-permute-start | bytes 12976136 | tf_op jit(solution)/shard_map/ppermute | solution.py:37
  647.7 149.9 %collective-permute-start.56 = (bf16[512,4224]{1,0:T(8,128)(2,1)}, bf16[512,4224]{1,0:T(8,128)(2,1)}, u32[]{:S(2)}, u32[]{:S(2)}) collective-permute-start(bf16[512,4224]{1,0:T(8,128)(2,1)} %get-tuple-element.172), channel_id=1, source_target_pairs={{0,16},{4,20},{8,24},{12,28},{16,0},{20,4},{24,8},{28,12},{1,17},{... | collective-permute-start | bytes 12976136 | tf_op jit(solution)/shard_map/ppermute | solution.py:37
  693.0 38.7 %collective-permute-start.50 = (bf16[2,64,2176]{2,1,0:T(8,128)(2,1)}, bf16[2,64,2176]{2,1,0:T(8,128)(2,1)}, u32[]{:S(2)}, u32[]{:S(2)}) collective-permute-start(bf16[2,64,2176]{2,1,0:T(8,128)(2,1)} %get-tuple-element.224), channel_id=1, source_target_pairs={{0,2},{1,3},{2,0},{3,1},{4,6},{5,7},{6,4},{7,5},{8,10},{9,11},{10,... | collective-permute-start | bytes 1671176 | tf_op jit(solution)/shard_map/ppermute | solution.py:37
  693.0 38.7 %collective-permute-start.49 = (bf16[2,64,2176]{2,1,0:T(8,128)(2,1)}, bf16[2,64,2176]{2,1,0:T(8,128)(2,1)}, u32[]{:S(2)}, u32[]{:S(2)}) collective-permute-start(bf16[2,64,2176]{2,1,0:T(8,128)(2,1)} %get-tuple-element.222), channel_id=1, source_target_pairs={{0,1},{1,0},{2,3},{3,2},{4,5},{5,4},{6,7},{7,6},{8,9},{9,8},{10,11... | collective-permute-start | bytes 1671176 | tf_op jit(solution)/shard_map/ppermute | solution.py:37
  740.7 56.9 %all-to-all-start.1 = ((bf16[8,48,2048]{2,1,0:T(8,128)(2,1)}), bf16[8,48,2048]{2,1,0:T(8,128)(2,1)S(1)}, u32[]{:S(2)}, u32[]{:S(2)}) async-start(bf16[8,48,2048]{2,1,0:T(8,128)(2,1)} %pad_maximum_fusion.11), calls=%async_computation.1 | async-start | bytes 3145728 | tf_op jit(solution)/shard_map/all_to_all | solution.py:811
  744.3 106.0 %reduce-scatter.5.cloned.1.call-start = ((), (), s32[]{:S(2)}) async-start(), calls=%async_computation.8 | async-start | bytes 14155776 | tf_op jit(solution)/shard_map/reduce_scatter | solution.py:787
  858.4 33.8 %collective-permute-start.60 = (bf16[256,512]{1,0:T(8,128)(2,1)S(1)}, bf16[256,512]{1,0:T(8,128)(2,1)S(1)}, u32[]{:S(2)}, u32[]{:S(2)}) collective-permute-start(bf16[256,512]{1,0:T(8,128)(2,1)S(1)} %get-tuple-element.238), channel_id=1, source_target_pairs={{0,0},{2,1},{1,2},{3,3},{4,4},{6,5},{5,6},{7,7},{8,8},{10,9},{9,10... | collective-permute-start | bytes 786440 | tf_op jit(solution)/shard_map/ppermute | solution.py:844
  (134 other events, 1754.2 us)
Sparse Core Ops, SparseCore 0:
  92.5 78.5 all-gather.2
  173.6 81.1 all-gather.4
  623.5 103.8 reduce-scatter.2
  753.9 96.3 reduce-scatter.4
